TPU v7x, 32 devices: a whole 2x2x4 slice. The times are simulated.
32 devices in a mesh: wide: 8 (over z, x), narrow: 4 (over y, core).
Axes of the slice: x: 2, y: 2, z: 4, core: 2. Of those that a mesh axis runs over, the one named last changes fastest.
Arguments:
- frames: bfloat16 [26624, 1024], P(('wide', 'narrow')), may hold values from -6 to 6
- text_states: bfloat16 [16, 64, 1024], P('wide'), may hold values from -6 to 6
- lengths: int32 [16], P('wide'), may hold values from 1457 to 1664, as said below
- loss_mask: int32 [26624], P(('wide', 'narrow')), may hold values 0 or 1
- norm_gain: float32 [3, 1024], replicated, may hold values from 0.25 to 1.75
- norm_bias: float32 [3, 1024], replicated, may hold values from -2 to 2
- w_qkv: bfloat16 [3, 1024, 1024], P(None, None, 'narrow'), may hold values from -0.1875 to 0.1875
- w_out: bfloat16 [1024, 1024], P('narrow'), may hold values from -1.5 to 1.5
- w_cross_q: bfloat16 [1024, 1024], P(None, 'narrow'), may hold values from -0.1875 to 0.1875
- w_cross_kv: bfloat16 [2, 1024, 1024], P(None, None, 'narrow'), may hold values from -0.1875 to 0.1875
- w_cross_out: bfloat16 [1024, 1024], P('narrow'), may hold values from -0.75 to 0.75
- w_up: bfloat16 [1024, 4096], P(None, 'narrow'), may hold values from -0.1875 to 0.1875
- w_down: bfloat16 [4096, 1024], P('narrow'), may hold values from -0.09375 to 0.09375
- cotangent: bfloat16 [26624, 1024], P(('wide', 'narrow')), may hold values from -6 to 6
Outputs:
- out: bfloat16 [26624, 1024], P(('wide', 'narrow'))
- grad_frames: bfloat16 [26624, 1024], P(('wide', 'narrow'))
- grad_text: bfloat16 [16, 64, 1024], P('wide')
- grad_norm_gain: float32 [3, 1024], replicated
- grad_norm_bias: float32 [3, 1024], replicated
- grad_qkv: float32 [3, 1024, 1024], P(None, None, 'narrow')
- grad_out: float32 [1024, 1024], P('narrow')
- grad_cross_q: float32 [1024, 1024], P(None, 'narrow')
- grad_cross_kv: float32 [2, 1024, 1024], P(None, None, 'narrow')
- grad_cross_out: float32 [1024, 1024], P('narrow')
- grad_up: float32 [1024, 4096], P(None, 'narrow')
- grad_down: float32 [4096, 1024], P('narrow')
Inputs may be any that keep to these rules, and one draw needn't show every extreme that they name: `lengths`: in every draw one item has all 1664 frames real.
All inputs are finite; a program needn't handle non-finite values. No bound on the sum of `loss_mask` on one device may be relied on, other than what follows from the above.
Results may differ from a plain program's by a relative error of at most 0.019.
The roundings to bfloat16 on the way count: a program that leaves them out, or rounds other values in their place, can miss the bound.
Values may be sent and summed in bfloat16 or wider, within the bound.
No kernel may reach another device: no remote copies, remote signals or barrier semaphores. Data moves between devices by JAX's collectives and lax.ppermute only.
A program may use at most 320 MiB of HBM per device.

v0:
```python
import jax
import jax.numpy as jnp
from jax import lax
from jax.sharding import PartitionSpec as P

HEAD = 64


EPS = 1e-05
NEG = -1e30


def lower(values_in):
    return values_in.astype(jnp.bfloat16)


def product(left_side, right_side, transposed):
    if transposed:
        return lax.dot_general(
            left_side, right_side, (((1,), (1,)), ((), ())), preferred_element_type=jnp.float32
        )
    return jnp.dot(left_side, right_side, preferred_element_type=jnp.float32)


def outer_sum(left_side, right_side):
    return lax.dot_general(
        left_side, right_side, (((0,), (0,)), ((), ())), preferred_element_type=jnp.float32
    )


def normalize(values_in, gain_row, bias_row):
    row_mean = jnp.mean(values_in, axis=-1, keepdims=True)
    centered = values_in - row_mean
    inverse = lax.rsqrt(jnp.mean(centered * centered, axis=-1, keepdims=True) + EPS)
    scaled = centered * inverse
    return (scaled * gain_row + bias_row, scaled, inverse)


def normalize_back(upstream, scaled, inverse, gain_row):
    weighted = upstream * gain_row
    inner_mean = jnp.mean(weighted, axis=-1, keepdims=True)
    along_mean = jnp.mean(weighted * scaled, axis=-1, keepdims=True)
    grad_input = inverse * (weighted - inner_mean - scaled * along_mean)
    return (grad_input, jnp.sum(upstream * scaled, axis=0), jnp.sum(upstream, axis=0))


def gelu_parts(values_in):
    normal_cdf = 0.5 * (1.0 + jax.scipy.special.erf(values_in * 0.7071067811865476))
    normal_pdf = jnp.exp(-0.5 * values_in * values_in) * 0.3989422804014327
    return (values_in * normal_cdf, normal_cdf + values_in * normal_pdf)


def scores_of(query_part, key_part, valid):
    scores = jnp.einsum(
        "bhe,khe->hbk", query_part, key_part, preferred_element_type=jnp.float32
    ) * HEAD ** (-0.5)
    return jnp.where(valid, scores, NEG)


def attend(query_part, key_part, value_part, valid):
    scores = scores_of(query_part, key_part, valid)
    row_top = jnp.max(scores, axis=-1, keepdims=True)
    weights_exp = jnp.exp(scores - row_top)
    denominator = jnp.sum(weights_exp, axis=-1, keepdims=True)
    probability = weights_exp / denominator
    mixed = jnp.einsum(
        "hbk,khe->bhe", lower(probability), value_part, preferred_element_type=jnp.float32
    )
    return (lower(mixed), (row_top + jnp.log(denominator))[..., 0])


def attend_back(query_part, key_part, value_part, valid, summary, upstream):
    scores = scores_of(query_part, key_part, valid)
    probability = jnp.exp(scores - summary[..., None])
    pressure = jnp.einsum("bhe,khe->hbk", upstream, value_part, preferred_element_type=jnp.float32)
    grad_scores = lower(
        probability * (pressure - jnp.sum(probability * pressure, axis=-1, keepdims=True))
    )
    factor = HEAD ** (-0.5)
    grad_query = (
        jnp.einsum("hbk,khe->bhe", grad_scores, key_part, preferred_element_type=jnp.float32)
        * factor
    )
    grad_key = (
        jnp.einsum("hbk,bhe->khe", grad_scores, query_part, preferred_element_type=jnp.float32)
        * factor
    )
    grad_value = jnp.einsum(
        "hbk,bhe->khe", lower(probability), upstream, preferred_element_type=jnp.float32
    )
    return (grad_query, grad_key, grad_value)


def local(
    frames,
    text_states,
    lengths,
    loss_mask,
    norm_gain,
    norm_bias,
    w_qkv,
    w_out,
    w_cross_q,
    w_cross_kv,
    w_cross_out,
    w_up,
    w_down,
    cotangent,
):
    row_count = frames.shape[0]
    width = frames.shape[1]
    item_count = lengths.shape[0]
    span = row_count * lax.axis_size("narrow") // item_count
    half_span = span // 2
    inner_width = w_qkv.shape[2]
    head_count = inner_width // HEAD
    text_count = text_states.shape[1]
    full_rows = item_count * span
    places = jnp.arange(span, dtype=jnp.int32)

    def spread(shard_rows):
        return lax.all_gather(shard_rows, "narrow", axis=0, tiled=True)

    def collect(left_side, right_side, transposed):
        return lax.psum_scatter(
            product(
                lax.slice_in_dim(left_side, 0, lax.axis_size("narrow") * row_count, axis=0),
                right_side,
                transposed,
            ),
            "narrow",
            scatter_dimension=0,
            tiled=True,
        )

    def causal(block_index, item_limit):
        query_place = block_index * half_span + jnp.arange(half_span, dtype=jnp.int32)
        return (places[None, :] <= query_place[:, None]) & (places[None, :] < item_limit)

    frame_rows = frames.astype(jnp.float32)
    normed_one, scaled_one, inverse_one = normalize(frame_rows, norm_gain[0], norm_bias[0])
    first_input = spread(lower(normed_one))
    triple = lower(
        jnp.einsum("rd,cde->cre", first_input, w_qkv, preferred_element_type=jnp.float32)
    )
    triple = triple.reshape(3, item_count, span, head_count, HEAD)

    def self_item(packed):
        query_part, key_part, value_part, item_limit = packed
        mixed_list = []
        summary_list = []
        for block_index in range(2):
            mixed, summary = attend(
                query_part[block_index * half_span : (block_index + 1) * half_span],
                key_part,
                value_part,
                causal(block_index, item_limit),
            )
            mixed_list.append(mixed)
            summary_list.append(summary)
        return (jnp.concatenate(mixed_list, axis=0), jnp.stack(summary_list, axis=0))

    attended, self_summary = lax.map(self_item, (triple[0], triple[1], triple[2], lengths))
    attended_flat = attended.reshape(full_rows, inner_width)
    first_rows = frame_rows + collect(attended_flat, w_out, False)
    normed_two, scaled_two, inverse_two = normalize(first_rows, norm_gain[1], norm_bias[1])
    second_input = spread(lower(normed_two))
    cross_query = lower(product(second_input, w_cross_q, False)).reshape(
        item_count, span, head_count, HEAD
    )
    cross_pair = lower(
        jnp.einsum("ntd,cde->cnte", text_states, w_cross_kv, preferred_element_type=jnp.float32)
    )
    cross_pair = cross_pair.reshape(2, item_count, text_count, head_count, HEAD)

    def cross_item(packed):
        query_part, key_part, value_part = packed
        return attend(query_part, key_part, value_part, True)

    cross_mixed, cross_summary = lax.map(cross_item, (cross_query, cross_pair[0], cross_pair[1]))
    cross_flat = cross_mixed.reshape(full_rows, inner_width)
    second_rows = first_rows + collect(cross_flat, w_cross_out, False)
    normed_three, scaled_three, inverse_three = normalize(second_rows, norm_gain[2], norm_bias[2])
    upstream = cotangent.astype(jnp.float32) * loss_mask.astype(jnp.float32)[:, None]
    ffn_grad = lower(upstream)
    ffn_input = spread(lower(normed_three))
    hidden_pre = product(ffn_input, w_up, False)
    active, slope = gelu_parts(hidden_pre)
    active = lower(active)
    out_rows = second_rows + collect(active, w_down, False)
    ffn_full = spread(ffn_grad)
    grad_down = outer_sum(active, ffn_full)
    grad_hidden = lower(product(ffn_full, w_down, True) * slope)
    grad_up = outer_sum(ffn_input, grad_hidden)
    back_three = collect(grad_hidden, w_up, True)
    grad_up, grad_down = (grad_up, grad_down)
    grad_in_three, gain_three, bias_three = normalize_back(
        back_three, scaled_three, inverse_three, norm_gain[2]
    )
    grad_second = upstream + grad_in_three
    cross_full = spread(lower(grad_second))
    grad_cross_out = outer_sum(cross_flat, cross_full)
    cross_upstream = lower(product(cross_full, w_cross_out, True)).reshape(
        item_count, span, head_count, HEAD
    )

    def cross_back(packed):
        query_part, key_part, value_part, summary, upstream_item = packed
        return attend_back(query_part, key_part, value_part, True, summary, upstream_item)

    grad_cq, grad_ck, grad_cv = lax.map(
        cross_back, (cross_query, cross_pair[0], cross_pair[1], cross_summary, cross_upstream)
    )
    grad_cq = lower(grad_cq).reshape(full_rows, inner_width)
    grad_pair = lower(jnp.stack((grad_ck, grad_cv), axis=0)).reshape(
        2, item_count, text_count, inner_width
    )
    grad_cross_q = outer_sum(second_input, grad_cq)
    grad_cross_kv = jnp.einsum(
        "ntd,cnte->cde", text_states, grad_pair, preferred_element_type=jnp.float32
    )
    grad_cross_q, grad_cross_kv, grad_cross_out = (grad_cross_q, grad_cross_kv, grad_cross_out)
    text_partial = jnp.einsum(
        "cnte,cde->ntd", grad_pair, w_cross_kv, preferred_element_type=jnp.float32
    )
    grad_text = lower(lax.psum(text_partial, "narrow"))
    back_two = collect(grad_cq, w_cross_q, True)
    grad_in_two, gain_two, bias_two = normalize_back(
        back_two, scaled_two, inverse_two, norm_gain[1]
    )
    grad_first = grad_second + grad_in_two
    self_full = spread(lower(grad_first))
    grad_out = outer_sum(attended_flat, self_full)
    self_upstream = lower(product(self_full, w_out, True)).reshape(
        item_count, span, head_count, HEAD
    )

    def self_back(packed):
        query_part, key_part, value_part, item_limit, summary, upstream_item = packed
        query_list = []
        key_list = []
        value_list = []
        for block_index in range(2):
            lower_row = block_index * half_span
            grad_query, grad_key, grad_value = attend_back(
                query_part[lower_row : lower_row + half_span],
                key_part,
                value_part,
                causal(block_index, item_limit),
                summary[block_index],
                upstream_item[lower_row : lower_row + half_span],
            )
            query_list.append(grad_query)
            key_list.append(grad_key)
            value_list.append(grad_value)
        return (
            jnp.concatenate(query_list, axis=0),
            key_list[0] + key_list[1],
            value_list[0] + value_list[1],
        )

    grad_q, grad_k, grad_v = lax.map(
        self_back, (triple[0], triple[1], triple[2], lengths, self_summary, self_upstream)
    )
    grad_triple = lower(jnp.stack((grad_q, grad_k, grad_v), axis=0)).reshape(
        3, full_rows, inner_width
    )
    grad_qkv = jnp.einsum(
        "rd,cre->cde", first_input, grad_triple, preferred_element_type=jnp.float32
    )
    grad_qkv, grad_out = (grad_qkv, grad_out)
    merged = grad_triple.transpose(1, 0, 2).reshape(full_rows, 3 * inner_width)
    stacked_weights = w_qkv.transpose(0, 2, 1).reshape(3 * inner_width, width)
    back_one = collect(merged, stacked_weights, False)
    grad_in_one, gain_one, bias_one = normalize_back(
        back_one, scaled_one, inverse_one, norm_gain[0]
    )
    grad_frames = lower(grad_first + grad_in_one)
    gain_terms = jnp.stack((gain_one, gain_two, gain_three), axis=0)
    bias_terms = jnp.stack((bias_one, bias_two, bias_three), axis=0)
    grad_norm_gain, grad_norm_bias = lax.psum((gain_terms, bias_terms), ("wide", "narrow"))
    grad_qkv, grad_out, grad_cross_q, grad_cross_kv, grad_cross_out, grad_up, grad_down = lax.psum(
        (grad_qkv, grad_out, grad_cross_q, grad_cross_kv, grad_cross_out, grad_up, grad_down),
        "wide",
    )
    return (
        lower(out_rows),
        grad_frames,
        grad_text,
        grad_norm_gain,
        grad_norm_bias,
        grad_qkv,
        grad_out,
        grad_cross_q,
        grad_cross_kv,
        grad_cross_out,
        grad_up,
        grad_down,
    )


def solution(mesh):
    return jax.shard_map(
        local,
        mesh=mesh,
        in_specs=(
            P(("wide", "narrow"), None),
            P("wide", None, None),
            P("wide"),
            P(("wide", "narrow")),
            P(),
            P(),
            P(None, None, "narrow"),
            P("narrow", None),
            P(None, "narrow"),
            P(None, None, "narrow"),
            P("narrow", None),
            P(None, "narrow"),
            P("narrow", None),
            P(("wide", "narrow"), None),
        ),
        out_specs=(
            P(("wide", "narrow"), None),
            P(("wide", "narrow"), None),
            P("wide", None, None),
            P(),
            P(),
            P(None, None, "narrow"),
            P("narrow", None),
            P(None, "narrow"),
            P(None, None, "narrow"),
            P("narrow", None),
            P(None, "narrow"),
            P("narrow", None),
        ),
        check_vma=False,
    )
```

profile of v0, /device:TPU:0, one launch (start us, length us, event | category | flops | bytes accessed | tf_op | source)
XLA Modules:
  0.0 2264.1 jit_solution(37616242407162394)
XLA Ops:
  14.5 52.2 %all-gather.7.cloned.1.call-done = bf16[3328,1024]{1,0:T(8,128)(2,1)} async-done(((bf16[832,1024]{1,0:T(8,128)(2,1)}), bf16[3328,1024]{1,0:T(8,128)(2,1)}) %all-gather.7.cloned.1.call-update) | async-done | bytes 6815760 | tf_op jit(solution)/shard_map/all_gather | solution.py:122
  66.6 8.1 fusion.132
  115.1 156.7 %while.58 = (s32[]{:T(128)}, bf16[2,1664,4,64]{1,3,2,0:T(8,128)(2,1)}, f32[2,2,4,832]{3,2,1,0:T(4,128)S(1)}, bf16[2,1664,4,64]{1,3,2,0:T(8,128)(2,1)}, s32[2]{0:...) while((s32[]{:T(128)}, ...), condition=%wide.region_7.8_spmd.clone.clone, body=%wide.region_2.7_spmd.clone.clone.sunk | while | flops 2975926784 | bytes 178479616 | solution.py:163
  131.5 13.7 fusion.283
  145.2 11.3 fusion.284
  156.5 18.9 fusion.285
  175.4 11.2 fusion.287
  186.7 11.4 fusion.286
  203.4 13.7 fusion.283
  217.1 11.3 fusion.284
  228.4 18.9 fusion.285
  247.3 11.3 fusion.287
  258.6 11.4 fusion.286
  276.5 6.8 fusion.172
  283.5 106.1 %reduce-scatter.7.cloned.1.call-done = f32[832,1024]{1,0:T(8,128)} async-done(((f32[3328,1024]{1,0:T(8,128)}), f32[832,1024]{1,0:T(8,128)}) %reduce-scatter.7.cloned.1.call-update) | async-done | bytes 3407888 | tf_op jit(solution)/shard_map/reduce_scatter | solution.py:125
  396.7 48.8 %all-gather.9.cloned.1.call-done = bf16[3328,1024]{1,0:T(8,128)(2,1)} async-done(((bf16[832,1024]{1,0:T(8,128)(2,1)}), bf16[3328,1024]{1,0:T(8,128)(2,1)}) %all-gather.9.cloned.1.call-update) | async-done | bytes 6815760 | tf_op jit(solution)/shard_map/all_gather | solution.py:122
  465.2 7.5 while.56
  477.3 6.8 fusion.173
  484.3 106.0 %reduce-scatter.9.cloned.1.call-done = f32[832,1024]{1,0:T(8,128)} async-done(((f32[3328,1024]{1,0:T(8,128)}), f32[832,1024]{1,0:T(8,128)}) %reduce-scatter.9.cloned.1.call-update) | async-done | bytes 3407888 | tf_op jit(solution)/shard_map/reduce_scatter | solution.py:125
  600.4 46.4 %all-gather.11.cloned.1.call-done = bf16[3328,1024]{1,0:T(8,128)(2,1)} async-done(((bf16[832,1024]{1,0:T(8,128)(2,1)}), bf16[3328,1024]{1,0:T(8,128)(2,1)}) %all-gather.11.cloned.1.call-update) | async-done | bytes 6815760 | tf_op jit(solution)/shard_map/all_gather | solution.py:122
  646.8 14.3 multiply_convert_fusion.3
  661.1 37.1 %all-gather.13.cloned.1.call-done = bf16[3328,1024]{1,0:T(8,128)(2,1)} async-done(((bf16[832,1024]{1,0:T(8,128)(2,1)}), bf16[3328,1024]{1,0:T(8,128)(2,1)}) %all-gather.13.cloned.1.call-update) | async-done | bytes 6815760 | tf_op jit(solution)/shard_map/all_gather | solution.py:122
  698.2 14.2 fusion.124
  715.1 9.9 fusion.175
  726.6 14.9 fusion.174
  742.0 89.2 %reduce-scatter.13.cloned.1.call-done = f32[832,1024]{1,0:T(8,128)} async-done(((f32[3328,1024]{1,0:T(8,128)}), f32[832,1024]{1,0:T(8,128)}) %reduce-scatter.13.cloned.1.call-update) | async-done | bytes 3407888 | tf_op jit(solution)/shard_map/reduce_scatter | solution.py:125
  836.1 103.7 %reduce-scatter.11.cloned.1.call-done = f32[832,1024]{1,0:T(8,128)} async-done(((f32[3328,1024]{1,0:T(8,128)}), f32[832,1024]{1,0:T(8,128)}) %reduce-scatter.11.cloned.1.call-update) | async-done | bytes 3407888 | tf_op jit(solution)/shard_map/reduce_scatter | solution.py:125
  939.9 6.5 fusion.164
  946.5 49.4 %all-gather.15.cloned.1.call-done = bf16[3328,1024]{1,0:T(8,128)(2,1)} async-done(((bf16[832,1024]{1,0:T(8,128)(2,1)}), bf16[3328,1024]{1,0:T(8,128)(2,1)}) %all-gather.15.cloned.1.call-update) | async-done | bytes 6815760 | tf_op jit(solution)/shard_map/all_gather | solution.py:122
  1011.1 11.3 while.57
  1025.9 6.9 fusion.176
  1032.9 106.1 %reduce-scatter.15.cloned.1.call-done = f32[832,1024]{1,0:T(8,128)} async-done(((f32[3328,1024]{1,0:T(8,128)}), f32[832,1024]{1,0:T(8,128)}) %reduce-scatter.15.cloned.1.call-update) | async-done | bytes 3407888 | tf_op jit(solution)/shard_map/reduce_scatter | solution.py:125
  1149.4 12.7 fusion.181
  1162.2 12.9 fusion.180
  1189.1 9.6 all-gather.17.cloned.1.call-done
  1216.5 306.6 %while.59 = (s32[]{:T(128)}, bf16[2,1664,4,64]{1,3,2,0:T(8,128)(2,1)}, bf16[2,1664,4,64]{1,3,2,0:T(8,128)(2,1)}, bf16[2,1664,4,64]{1,3,2,0:T(8,128)(2,1)}, bf16[...) while((s32[]{:T(128)}, ...), condition=%wide.region_31.32_spmd.clone.clone, body=%wide.region_28.31_spmd.clone.clone.sunk | while | flops 7197421568 | bytes 513789888 | solution.py:262
  1237.9 11.6 fusion.300
  1249.5 16.8 multiply_reduce_fusion.16
  1266.2 14.5 multiply_convert_fusion.8
  1280.8 13.6 fusion.308
  1298.4 11.6 fusion.303
  1310.0 16.3 multiply_reduce_fusion.17
  1326.3 19.0 multiply_convert_fusion.9
  1345.3 9.8 fusion.309
  1355.2 8.0 fusion.304
  1363.2 6.5 fusion.306
  1378.5 11.6 fusion.300
  1390.1 16.8 multiply_reduce_fusion.16
  1406.9 14.5 multiply_convert_fusion.8
  1421.4 13.6 fusion.308
  1439.0 11.6 fusion.303
  1450.6 16.3 multiply_reduce_fusion.17
  1467.0 19.0 multiply_convert_fusion.9
  1486.0 9.8 fusion.309
  1495.8 8.0 fusion.304
  1503.9 6.5 fusion.306
  1529.2 6.2 reshape.252
  1563.3 6.4 fusion.177
  1569.7 7.2 fusion.152
  1578.3 11.2 convolution_bitcast_fusion.1
  1591.2 17.1 all-reduce.6
  1608.3 484.4 %all-reduce.5.cloned.1.call-done = (f32[3,1024,256]{1,2,0:T(8,128)}, f32[256,1024]{1,0:T(8,128)}, f32[1024,256]{1,0:T(8,128)}, f32[2,1024,256]{1,2,0:T(8,128)}, ...) async-done(((f32[3,1024,256]{1,2,0:T(8,128)}, f32[256,1024]{1,0:T(8,128)}, f32[1024,256]{1,0:T(8,128)}, f32[2,1024,256]{1,2,0:T(8,128)}, ...) | async-done | bytes 16777232 | tf_op jit(solution)/shard_map/psum | solution.py:282
  2099.3 100.9 %reduce-scatter.17.cloned.1.call-done = f32[832,1024]{1,0:T(8,128)} async-done(((f32[3328,1024]{1,0:T(8,128)}), f32[832,1024]{1,0:T(8,128)}) %reduce-scatter.17.cloned.1.call-update) | async-done | bytes 3407888 | tf_op jit(solution)/shard_map/reduce_scatter | solution.py:125
  2203.8 40.1 %all-reduce = (f32[3,1024]{1,0:T(4,128)}, f32[3,1024]{1,0:T(4,128)}) all-reduce(f32[3,1024]{1,0:T(4,128)S(1)} %pad_maximum_fusion.3, f32[3,1024]{1,0:T(4,128)S(1)} %pad_maximum_fusion.4), channel_id=1, replica_groups=mesh['wide'=8,'narrow'=4] {'wide','narrow'}, use_global_device_ids=true, to_apply=%region_39.40 | all-reduce | flops 6144 | bytes 49152 | tf_op jit(solution)/shard_map/psum | solution.py:281
  (414 shorter events, 279.5 us)
Async XLA Ops:
  7.2 639.6 %copy-start = (bf16[1024,1024]{1,0:T(8,128)(2,1)S(1)}, bf16[1024,1024]{1,0:T(8,128)(2,1)}, u32[]{:S(2)}) copy-start(bf16[1024,1024]{1,0:T(8,128)(2,1)} %param.33) | copy-start | bytes 6291460
  7.2 59.4 %all-gather.7.cloned.1.call-start = ((), (), s32[]{:S(2)}) async-start(), calls=%async_computation.6 | async-start | bytes 8519680 | tf_op jit(solution)/shard_map/all_gather | solution.py:122
  14.4 375.1 %reduce-scatter.7.cloned.1.call-start = ((), (), s32[]{:S(2)}) async-start(), calls=%async_computation.7 | async-start | bytes 17039360 | tf_op jit(solution)/shard_map/reduce_scatter | solution.py:125
  107.8 7.4 copy-start.84
  131.5 13.7 copy-start.3
  156.5 18.9 copy-start.14
  186.7 11.5 copy-start.36
  203.4 13.7 copy-start.3
  228.4 18.9 copy-start.14
  258.6 11.5 copy-start.36
  283.4 162.1 %all-gather.9.cloned.1.call-start = ((), (), s32[]{:S(2)}) async-start(), calls=%async_computation.8 | async-start | bytes 8519680 | tf_op jit(solution)/shard_map/all_gather | solution.py:122
  396.0 194.3 %reduce-scatter.9.cloned.1.call-start = ((), (), s32[]{:S(2)}) async-start(), calls=%async_computation.9 | async-start | bytes 17039360 | tf_op jit(solution)/shard_map/reduce_scatter | solution.py:125
  484.2 162.6 %all-gather.11.cloned.1.call-start = ((), (), s32[]{:S(2)}) async-start(), calls=%async_computation.10 | async-start | bytes 8519680 | tf_op jit(solution)/shard_map/all_gather | solution.py:122
  597.3 100.9 %all-gather.13.cloned.1.call-start = ((), (), s32[]{:S(2)}) async-start(), calls=%async_computation.12 | async-start | bytes 8519680 | tf_op jit(solution)/shard_map/all_gather | solution.py:122
  600.4 230.8 %reduce-scatter.13.cloned.1.call-start = ((), (), s32[]{:S(2)}) async-start(), calls=%async_computation.13 | async-start | bytes 17039360 | tf_op jit(solution)/shard_map/reduce_scatter | solution.py:125
  725.0 214.9 %reduce-scatter.11.cloned.1.call-start = ((), (), s32[]{:S(2)}) async-start(), calls=%async_computation.11 | async-start | bytes 17039360 | tf_op jit(solution)/shard_map/reduce_scatter | solution.py:125
  741.5 198.4 %copy-start.24 = (bf16[832,1024]{1,0:T(8,128)(2,1)S(1)}, bf16[832,1024]{1,0:T(8,128)(2,1)}, u32[]{:S(2)}) copy-start(bf16[832,1024]{1,0:T(8,128)(2,1)} %param.35) | copy-start | bytes 5111812
  741.5 254.4 %all-gather.15.cloned.1.call-start = ((), (), s32[]{:S(2)}) async-start(), calls=%async_computation.14 | async-start | bytes 8519680 | tf_op jit(solution)/shard_map/all_gather | solution.py:122
  946.4 192.5 %reduce-scatter.15.cloned.1.call-start = ((), (), s32[]{:S(2)}) async-start(), calls=%async_computation.15 | async-start | bytes 17039360 | tf_op jit(solution)/shard_map/reduce_scatter | solution.py:125
  1025.9 6.9 copy-start.22
  1032.8 106.1 %copy-start.61 = (f32[832]{0:T(1024)S(1)}, f32[832]{0:T(1024)}, u32[]{:S(2)}) copy-start(f32[832]{0:T(1024)} %copy-done.60) | copy-start | bytes 9988
  1032.8 106.1 %copy-start.65 = (f32[832]{0:T(1024)S(1)}, f32[832]{0:T(1024)}, u32[]{:S(2)}) copy-start(f32[832]{0:T(1024)} %copy-done.64) | copy-start | bytes 9988
  1032.8 106.1 %copy-start.67 = (f32[1,1024]{1,0:T(1,128)S(1)}, f32[1,1024]{1,0:T(1,128)}, u32[]{:S(2)}) copy-start(f32[1,1024]{1,0:T(1,128)} %get-tuple-element.513) | copy-start | bytes 12292
  1032.8 165.8 %all-gather.17.cloned.1.call-start = ((), (), s32[]{:S(2)}) async-start(), calls=%async_computation.16 | async-start | bytes 8519680 | tf_op jit(solution)/shard_map/all_gather | solution.py:122
  1149.2 943.6 %all-reduce.5.cloned.1.call-start = ((), (), s32[]{:S(2)}) async-start(), calls=%async_computation.18 | async-start | bytes 33554432 | tf_op jit(solution)/shard_map/psum | solution.py:282
  1162.2 13.1 copy-start.48
  1162.2 14.9 copy-start.21
  1175.1 7.9 copy-start.49
  1175.2 7.8 copy-start.51
  1183.0 15.7 copy-start.57
  1266.2 14.5 copy-start.9
  1280.7 13.6 copy-start.2
  1280.8 13.6 copy-start.4
  1326.3 19.0 copy-start.25
  1345.3 9.8 copy-start.5
  1355.1 8.1 copy-start.26
  1355.1 8.1 copy-start.10
  1355.1 14.6 slice-start
  1355.2 14.6 slice-start.1
  1363.2 6.6 slice-start.2
  1363.2 6.6 copy-start.27
  1406.9 14.5 copy-start.9
  1421.4 13.6 copy-start.2
  1421.4 13.6 copy-start.4
  1467.0 19.0 copy-start.25
  1486.0 9.8 copy-start.5
  1495.8 8.1 copy-start.26
  1495.8 8.1 copy-start.10
  1495.8 14.6 slice-start
  1495.8 14.6 slice-start.1
  1503.9 6.6 slice-start.2
  1503.9 6.6 copy-start.27
  1539.7 9.0 copy-start.29
  1562.0 7.7 slice-start.3
  1576.9 623.4 %reduce-scatter.17.cloned.1.call-start = ((), (), s32[]{:S(2)}) async-start(), calls=%async_computation.17 | async-start | bytes 17039360 | tf_op jit(solution)/shard_map/reduce_scatter | solution.py:125
  2096.3 104.0 %copy-start.12 = (bf16[832,1024]{1,0:T(8,128)(2,1)S(1)}, bf16[832,1024]{1,0:T(8,128)(2,1)}, u32[]{:S(2)}) copy-start(bf16[832,1024]{1,0:T(8,128)(2,1)} %param.22) | copy-start | bytes 5111812
  2096.3 104.0 %copy-start.63 = (f32[832]{0:T(1024)S(1)}, f32[832]{0:T(1024)}, u32[]{:S(2)}) copy-start(f32[832]{0:T(1024)} %copy-done.62) | copy-start | bytes 9988
  2096.3 104.0 %copy-start.70 = (f32[832]{0:T(1024)S(1)}, f32[832]{0:T(1024)}, u32[]{:S(2)}) copy-start(f32[832]{0:T(1024)} %copy-done.69) | copy-start | bytes 9988
  2096.3 104.0 %copy-start.72 = (f32[1,1024]{1,0:T(1,128)S(1)}, f32[1,1024]{1,0:T(1,128)}, u32[]{:S(2)}) copy-start(f32[1,1024]{1,0:T(1,128)} %copy-done.71) | copy-start | bytes 12292
  2099.3 104.4 %copy-start.74 = (f32[1024]{0:T(1024)S(1)}, f32[1024]{0:T(1024)}, u32[]{:S(2)}) copy-start(f32[1024]{0:T(1024)} %get-tuple-element.394) | copy-start | bytes 12292
  2099.3 104.4 %copy-start.76 = (f32[1024]{0:T(1024)S(1)}, f32[1024]{0:T(1024)}, u32[]{:S(2)}) copy-start(f32[1024]{0:T(1024)} %get-tuple-element.392) | copy-start | bytes 12292
  2099.3 104.4 %copy-start.73 = (f32[1024]{0:T(1024)S(1)}, f32[1024]{0:T(1024)}, u32[]{:S(2)}) copy-start(f32[1024]{0:T(1024)} %get-tuple-element.403) | copy-start | bytes 12292
  2099.3 104.4 %copy-start.75 = (f32[1024]{0:T(1024)S(1)}, f32[1024]{0:T(1024)}, u32[]{:S(2)}) copy-start(f32[1024]{0:T(1024)} %get-tuple-element.402) | copy-start | bytes 12292
  2243.9 6.6 copy-start.44
  (67 other events, 177.3 us)
Sparse Core Ops, SparseCore 0:
  14.5 52.0 all-gather.6
  283.5 105.9 reduce-scatter.6
  396.1 49.3 all-gather.8
  484.3 105.9 reduce-scatter.8
  597.4 49.3 all-gather.10
  648.8 49.3 all-gather.12
  725.1 105.9 reduce-scatter.12
  833.8 106.0 reduce-scatter.10
  946.6 49.3 all-gather.14
  1032.9 105.9 reduce-scatter.14
  1149.3 49.3 all-gather.16
  1577.0 515.6 all-reduce.4
  2095.4 104.8 reduce-scatter.16
where the time goes:
time: 2270 us; the launch traced here: 2260 us
  waiting for transfers between devices  1340 us (59%)
  matrix products  470 us (21%)
  local copies, waits for them, and re-layouts  172 us (8%)
  other arithmetic  169 us (7%)
  blocking collectives  57.2 us (3%)
  loops' own time  39.1 us (2%)
    reduce_scatter x6, waiting for transfers between devices, collect(): lax.psum_scatter(product(lax.slice_in_dim(left_side, 0, lax.axis_size('na...  612 us
    psum x1, waiting for transfers between devices, local(): lax.psum((grad_qkv, grad_out, grad_cross_q, grad_cross_kv, grad_cross_out...  484 us
    all_gather x6, waiting for transfers between devices, spread(): return lax.all_gather(shard_rows, 'narrow', axis=0, tiled=True)  244 us
    dot_general x12, matrix products, scores_of(): jnp.einsum('bhe,khe->hbk', query_part, key_part, preferred_element_type=j...  121 us
    convert_element_type x13, other arithmetic, lower(): return values_in.astype(jnp.bfloat16)  92.2 us
    dot_general x6, matrix products, product(): return jnp.dot(left_side, right_side, preferred_element_type=jnp.float32)  60.2 us
    unnamed x148, local copies, waits for them, and re-layouts  57.5 us
    dot_general x6, matrix products, attend_back(): jnp.einsum('bhe,khe->hbk', upstream, value_part, preferred_element_type=j...  49.7 us
  transfers between devices with their start and end apart: 13, of which 13 were waited for; matrix products, arithmetic and copies ran while one was open for 4% of the time, Pallas kernels for 0%

commit v1 on v0

--- a/solution.py
+++ b/solution.py
@@ -1,6 +1,10 @@
+import functools
+
 import jax
 import jax.numpy as jnp
 from jax import lax
+from jax.experimental import pallas as pl
+from jax.experimental.pallas import tpu as pltpu
 from jax.sharding import PartitionSpec as P
 
 HEAD = 64
@@ -91,7 +95,7 @@
     return (grad_query, grad_key, grad_value)
 
 
-def local(
+def general_local(
     frames,
     text_states,
     lengths,
@@ -299,9 +303,702 @@
     )
 
 
+ROUND = jnp.bfloat16
+FULL = jnp.float32
+CORE_PAIRS = ((0, 1), (1, 0), (2, 3), (3, 2))
+Y_PAIRS = ((0, 2), (2, 0), (1, 3), (3, 1))
+X_PAIRS = tuple((i, i ^ 1) for i in range(8))
+Z_INWARD = ((0, 2), (1, 3), (6, 4), (7, 5))
+Z_MIDDLE = ((2, 4), (4, 2), (3, 5), (5, 3))
+Z_OUTWARD = ((2, 0), (3, 1), (4, 6), (5, 7))
+Z_NEAR = tuple((i, i ^ 2) for i in range(8))
+Z_FAR = tuple((i, i ^ 4) for i in range(8))
+MIB = 1 << 20
+
+
+def nt(a, b):
+    return lax.dot_general(a, b, (((1,), (1,)), ((), ())), preferred_element_type=FULL)
+
+
+def nn(a, b):
+    return lax.dot_general(a, b, (((1,), (0,)), ((), ())), preferred_element_type=FULL)
+
+
+def tn(a, b):
+    return lax.dot_general(a, b, (((0,), (0,)), ((), ())), preferred_element_type=FULL)
+
+
+def shape(dims, kind):
+    return jax.ShapeDtypeStruct(dims, kind)
+
+
+def resident(dims):
+    zeros = (0,) * len(dims)
+    return pl.BlockSpec(dims, lambda i, s: zeros, pipeline_mode=pl.Buffered(1))
+
+
+def rows_of(block, width):
+    return pl.BlockSpec((block, width), lambda i, s: (i, 0))
+
+
+def cost(flops, moved):
+    return pl.CostEstimate(flops=int(flops), bytes_accessed=int(moved), transcendentals=0)
+
+
+def params(mib):
+    return pltpu.CompilerParams(vmem_limit_bytes=mib * MIB)
+
+
+def norm_parts(v):
+    centered = v - jnp.mean(v, axis=-1, keepdims=True)
+    inverse = lax.rsqrt(jnp.mean(centered * centered, axis=-1, keepdims=True) + EPS)
+    return centered * inverse, inverse
+
+
+def norm_pull(y, scaled, inverse, gain_row):
+    weighted = y * gain_row
+    inner = jnp.mean(weighted, axis=-1, keepdims=True)
+    along = jnp.mean(weighted * scaled, axis=-1, keepdims=True)
+    return inverse * (weighted - inner - scaled * along)
+
+
+def project_kernel(where_ref, mine_ref, other_ref, weight_ref, *out_refs, transposed, count):
+    half = pl.program_id(0)
+
+    def run(source):
+        for c in range(count):
+            if transposed:
+                result = nt(source[...], weight_ref[c])
+            else:
+                result = nn(source[...], weight_ref[c])
+            out_refs[c][...] = lower(result)
+
+    @pl.when(half == 0)
+    def _():
+        run(mine_ref)
+
+    @pl.when(half == 1)
+    def _():
+        run(other_ref)
+
+
+def project(where, mine, other, weights, transposed):
+    rows, depth = mine.shape
+    count = weights.shape[0]
+    wide = weights.shape[1] if transposed else weights.shape[2]
+    whole = pl.BlockSpec((rows, depth), lambda i, s: (0, 0), pipeline_mode=pl.Buffered(1))
+    out = pl.BlockSpec((rows, wide), lambda i, s: ((i + s[0]) % 2, 0))
+    return pl.pallas_call(
+        functools.partial(project_kernel, transposed=transposed, count=count),
+        grid_spec=pltpu.PrefetchScalarGridSpec(
+            num_scalar_prefetch=1,
+            grid=(2,),
+            in_specs=[whole, whole, resident(weights.shape)],
+            out_specs=[out] * count,
+        ),
+        out_shape=[shape((2 * rows, wide), ROUND)] * count,
+        compiler_params=params(32),
+        cost_estimate=cost(4 * rows * depth * wide * count, 8e6),
+        name="project",
+    )(where, mine, other, weights)
+
+
+def blocks_of(span, block):
+    return [(start, min(block, span - start)) for start in range(0, span, block)]
+
+
+def self_forward_kernel(limit_ref, q_ref, k_ref, v_ref, o_ref, lse_ref, *, span, floor, block):
+    limit = limit_ref[0]
+    lane = lax.broadcasted_iota(jnp.int32, (1, 128), 1)
+    zero = jnp.zeros((), ROUND)
+    for start, size in blocks_of(span, block):
+        end = start + size
+        mixed_list = []
+        for h in range(2):
+            own_lanes = (lane < HEAD) if h == 0 else (lane >= HEAD)
+            query = jnp.where(own_lanes, q_ref[start:end, :] * HEAD ** (-0.5), zero)
+            cuts = [(0, start)] if start <= floor else [(0, floor), (floor, start)]
+            parts = []
+            for low, high in cuts + [(start, end)]:
+                if low == high:
+                    continue
+                scores = nt(query, k_ref[low:high, :])
+                key = lax.broadcasted_iota(jnp.int32, (size, high - low), 1)
+                if low == start:
+                    valid = key <= lax.broadcasted_iota(jnp.int32, (size, high - low), 0)
+                    if high > floor:
+                        valid = valid & (key + low < limit)
+                    scores = jnp.where(valid, scores, NEG)
+                elif high > floor:
+                    scores = jnp.where(key + low < limit, scores, NEG)
+                parts.append((low, high, scores))
+            top = functools.reduce(
+                jnp.maximum, [jnp.max(s, axis=1, keepdims=True) for _, _, s in parts]
+            )
+            total = 0.0
+            mixed = 0.0
+            for low, high, scores in parts:
+                weights_exp = jnp.exp(scores - top)
+                total = total + jnp.sum(weights_exp, axis=1, keepdims=True)
+                mixed = mixed + nn(lower(weights_exp), v_ref[low:high, :])
+            mixed_list.append(mixed / total)
+            summary = jnp.broadcast_to(top + jnp.log(total), (size, 128))
+            lse_ref[0, h : h + 1, start:end] = summary.T[0:1, :]
+        o_ref[start:end, :] = lower(jnp.where(lane < HEAD, mixed_list[0], mixed_list[1]))
+
+
+def self_forward(limit, q, k, v):
+    span, wide = q.shape
+    pairs = wide // 128
+    floor = (span - span // 8 + 1) // 128 * 128
+    pair = pl.BlockSpec((span, 128), lambda p, s: (0, p))
+    return pl.pallas_call(
+        functools.partial(self_forward_kernel, span=span, floor=floor, block=256),
+        grid_spec=pltpu.PrefetchScalarGridSpec(
+            num_scalar_prefetch=1,
+            grid=(pairs,),
+            in_specs=[pair] * 3,
+            out_specs=[pair, pl.BlockSpec((1, 8, span), lambda p, s: (p, 0, 0))],
+        ),
+        out_shape=[shape((span, wide), ROUND), shape((pairs, 8, span), FULL)],
+        compiler_params=params(40),
+        cost_estimate=cost(16e9, 4e6),
+        name="self_forward",
+    )(limit, q, k, v)
+
+
+def self_back_kernel(
+    limit_ref, q_ref, k_ref, v_ref, o_ref, do_ref, lse_ref, dq_ref, dk_ref, dv_ref, dqt,
+    *, span, floor, block
+):
+    limit = limit_ref[0]
+    lane = lax.broadcasted_iota(jnp.int32, (1, 128), 1)
+    row = lax.broadcasted_iota(jnp.int32, (128, 1), 0)
+    zero = jnp.zeros((), ROUND)
+    factor = HEAD ** (-0.5)
+    product_rows = do_ref[...].astype(FULL) * o_ref[...].astype(FULL)
+    high = lower(product_rows)
+    rest = lower(product_rows - high.astype(FULL))
+    pick = lower(
+        jnp.concatenate(
+            [
+                jnp.where(lane < HEAD, 1.0, 0.0),
+                jnp.where(lane >= HEAD, 1.0, 0.0),
+                jnp.zeros((6, 128), FULL),
+            ],
+            axis=0,
+        )
+    )
+    delta = nt(pick, high) + nt(pick, rest)
+    for start, size in blocks_of(span, block):
+        end = start + size
+        key = k_ref[start:end, :]
+        value = v_ref[start:end, :]
+        key_turned = key.T
+        dk = 0.0
+        dv = 0.0
+        dq_add = 0.0
+        for h in range(2):
+            own_lanes = (lane < HEAD) if h == 0 else (lane >= HEAD)
+            own_rows = (row < HEAD) if h == 0 else (row >= HEAD)
+            query = jnp.where(own_lanes, q_ref[start:, :] * factor, zero)
+            pulled = jnp.where(own_lanes, do_ref[start:, :], zero)
+            probability = jnp.exp(nt(key, query) - lse_ref[0, h : h + 1, start:])
+            pressure = nt(value, pulled)
+            below = lax.broadcasted_iota(jnp.int32, (size, size), 0)
+            across = lax.broadcasted_iota(jnp.int32, (size, size), 1)
+            corner = jnp.where(below <= across, probability[:, :size], 0.0)
+            if end < span:
+                probability = jnp.concatenate([corner, probability[:, size:]], axis=1)
+            else:
+                probability = corner
+            if end > floor:
+                place = lax.broadcasted_iota(jnp.int32, (size, 1), 0) + start
+                probability = jnp.where(place < limit, probability, 0.0)
+            grad_scores = lower(probability * (pressure - delta[h : h + 1, start:]))
+            dv = dv + nn(lower(probability), pulled)
+            dk = dk + nn(grad_scores, query)
+            dq_add = dq_add + nn(jnp.where(own_rows, key_turned, zero), grad_scores)
+        dk_ref[start:end, :] = lower(dk)
+        dv_ref[start:end, :] = lower(dv)
+        if start == 0:
+            dqt[...] = dq_add
+        else:
+            dqt[:, start:] += dq_add
+    dq_ref[...] = lower(dqt[...].T * factor)
+
+
+def self_back(limit, q, k, v, o, do, lse):
+    span, wide = q.shape
+    pairs = wide // 128
+    floor = (span - span // 8 + 1) // 128 * 128
+    pair = pl.BlockSpec((span, 128), lambda p, s: (0, p))
+    return pl.pallas_call(
+        functools.partial(self_back_kernel, span=span, floor=floor, block=256),
+        grid_spec=pltpu.PrefetchScalarGridSpec(
+            num_scalar_prefetch=1,
+            grid=(pairs,),
+            in_specs=[pair] * 5 + [pl.BlockSpec((1, 8, span), lambda p, s: (p, 0, 0))],
+            out_specs=[pair] * 3,
+            scratch_shapes=[pltpu.VMEM((128, span), FULL)],
+        ),
+        out_shape=[shape((span, wide), ROUND)] * 3,
+        compiler_params=params(48),
+        cost_estimate=cost(20e9, 6e6),
+        name="self_back",
+    )(limit, q, k, v, o, do, lse)
+
+
+def by_head(values_in, reduce, empty):
+    lane = lax.broadcasted_iota(jnp.int32, (1, 128), 1)
+    pieces = []
+    for start in range(0, values_in.shape[1], 128):
+        part = values_in[:, start : start + 128]
+        first = reduce(jnp.where(lane < HEAD, part, empty), axis=1, keepdims=True)
+        second = reduce(jnp.where(lane >= HEAD, part, empty), axis=1, keepdims=True)
+        pieces.append(jnp.where(lane < HEAD, first, second))
+    return jnp.concatenate(pieces, axis=1)
+
+
+def cross_probability(query, keys):
+    scores = nt(query * HEAD ** (-0.5), keys)
+    weights_exp = jnp.exp(scores - by_head(scores, jnp.max, NEG))
+    return weights_exp / by_head(weights_exp, jnp.sum, 0.0)
+
+
+def middle_forward_kernel(
+    where_ref, frame_ref, a0_ref, a1_ref, a2_ref, a3_ref, gain_ref, bias_ref, wo0_ref, wo1_ref,
+    wq0_ref, wq1_ref, ck0_ref, ck1_ref, cv0_ref, cv1_ref, wc0_ref, wc1_ref,
+    x1_ref, x2_ref, h2_ref, cq_ref, ca_ref, h3_ref
+):
+    mixed = (a0_ref, a1_ref, a2_ref, a3_ref)
+    x1 = frame_ref[...].astype(FULL)
+    for g in range(4):
+        part = (wo0_ref, wo1_ref)[g // 2][(g % 2) * 256 : (g % 2 + 1) * 256, :]
+        x1 = x1 + nn(mixed[g][...], part)
+    x1_ref[...] = x1
+    scaled, _ = norm_parts(x1)
+    h2 = lower(scaled * gain_ref[1:2, :] + bias_ref[1:2, :])
+    h2_ref[...] = h2
+    for g in range(4):
+        lanes = slice(g * 256, (g + 1) * 256)
+        cq = lower(nn(h2, (wq0_ref, wq1_ref)[g // 2][g % 2]))
+        cq_ref[:, lanes] = cq
+        probability = cross_probability(cq, (ck0_ref, ck1_ref)[g // 2][g % 2])
+        ca_ref[:, lanes] = lower(nn(lower(probability), (cv0_ref, cv1_ref)[g // 2][g % 2]))
+    crossed = nn(ca_ref[:, :512], wc0_ref[...]) + nn(ca_ref[:, 512:], wc1_ref[...])
+    x2 = x1_ref[...] + crossed
+    x2_ref[...] = x2
+    scaled, _ = norm_parts(x2)
+    h3_ref[...] = lower(scaled * gain_ref[2:3, :] + bias_ref[2:3, :])
+
+
+def middle_forward(where, frames, attended, received, gains, biases, wo, wq, ck, cv, wc):
+    rows, width = frames.shape
+    block = 208
+    steps = rows // block
+    piece = pl.BlockSpec((block, 256), lambda i, s: (s[0] * steps + i, 0))
+    wide = rows_of(block, width)
+    return pl.pallas_call(
+        middle_forward_kernel,
+        grid_spec=pltpu.PrefetchScalarGridSpec(
+            num_scalar_prefetch=1,
+            grid=(steps,),
+            in_specs=[wide, piece, piece, rows_of(block, 256), rows_of(block, 256)]
+            + [resident(a.shape) for a in (gains, biases, *wo, *wq, *ck, *cv, *wc)],
+            out_specs=[wide] * 6,
+        ),
+        out_shape=[shape((rows, width), FULL)] * 2 + [shape((rows, width), ROUND)] * 4,
+        compiler_params=params(40),
+        cost_estimate=cost(7e9, 25e6),
+        name="middle_forward",
+    )(where, frames, *attended, *received, gains, biases, *wo, *wq, *ck, *cv, *wc)
+
+
+def feed_kernel(
+    where_ref, h_ref, d_ref, up0_ref, up1_ref, down0_ref, down1_ref,
+    g0_ref, g1_ref, du0_ref, du1_ref, out_ref, y_ref
+):
+    h = h_ref[...]
+    d = d_ref[...]
+    out = 0.0
+    y = 0.0
+    for up, down, g_ref, du_ref in (
+        (up0_ref, down0_ref, g0_ref, du0_ref),
+        (up1_ref, down1_ref, g1_ref, du1_ref),
+    ):
+        u = nn(h, up[...])
+        active, slope = gelu_parts(u)
+        g = lower(active)
+        g_ref[...] = g
+        du = lower(nt(d, down[...]) * slope)
+        du_ref[...] = du
+        out = out + nn(g, down[...])
+        y = y + nt(du, up[...])
+    out_ref[...] = out.astype(out_ref.dtype)
+    y_ref[...] = y.astype(y_ref.dtype)
+
+
+def feed(where, h, d, up, down, kind):
+    rows, width = h.shape
+    block = 208
+    hidden = up[0].shape[1]
+    wide = rows_of(block, width)
+    return pl.pallas_call(
+        feed_kernel,
+        grid_spec=pltpu.PrefetchScalarGridSpec(
+            num_scalar_prefetch=1,
+            grid=(rows // block,),
+            in_specs=[wide, wide] + [resident(a.shape) for a in (*up, *down)],
+            out_specs=[rows_of(block, hidden)] * 4 + [wide] * 2,
+        ),
+        out_shape=[shape((rows, hidden), ROUND)] * 4 + [shape((rows, width), kind)] * 2,
+        compiler_params=params(48),
+        cost_estimate=cost(16 * rows * width * hidden, 30e6),
+        name="feed",
+    )(where, h, d, *up, *down)
+
+
+def middle_back_kernel(
+    where_ref, ym_ref, yr_ref, x1_ref, x2_ref, d_ref, cq_ref, gain_ref,
+    wq0_ref, wq1_ref, ck0_ref, ck1_ref, cv0_ref, cv1_ref, wc0_ref, wc1_ref,
+    dx1_ref, dself_ref, dcross_ref, dcq_ref, dck_ref, dcv_ref, sums_ref, dck_all, dcv_all
+):
+    step = pl.program_id(0)
+
+    @pl.when(step == 0)
+    def _():
+        dck_all[...] = jnp.zeros_like(dck_all)
+        dcv_all[...] = jnp.zeros_like(dcv_all)
+        sums_ref[...] = jnp.zeros_like(sums_ref)
+
+    y3 = ym_ref[...] + yr_ref[...].astype(FULL)
+    scaled, inverse = norm_parts(x2_ref[...])
+    sums_ref[4:5, :] += jnp.sum(y3 * scaled, axis=0, keepdims=True)
+    sums_ref[5:6, :] += jnp.sum(y3, axis=0, keepdims=True)
+    dx2 = d_ref[...].astype(FULL) + norm_pull(y3, scaled, inverse, gain_ref[2:3, :])
+    dx1_ref[...] = dx2
+    dcross = lower(dx2)
+    dcross_ref[...] = dcross
+    y2 = 0.0
+    for g in range(4):
+        lanes = slice(g * 256, (g + 1) * 256)
+        part = (wc0_ref, wc1_ref)[g // 2][(g % 2) * 256 : (g % 2 + 1) * 256, :]
+        keys = (ck0_ref, ck1_ref)[g // 2][g % 2]
+        values = (cv0_ref, cv1_ref)[g // 2][g % 2]
+        dcatt = lower(nt(dcross, part))
+        cq = cq_ref[:, lanes]
+        probability = cross_probability(cq, keys)
+        weighed = nt(dcatt, values)
+        inner = by_head(probability * weighed, jnp.sum, 0.0)
+        dcs = lower(probability * (weighed - inner))
+        dcq = lower(nn(dcs, keys) * HEAD ** (-0.5))
+        dcq_ref[:, lanes] = dcq
+        dck_all[g] += tn(dcs, cq * HEAD ** (-0.5))
+        dcv_all[g] += tn(lower(probability), dcatt)
+        y2 = y2 + nt(dcq, (wq0_ref, wq1_ref)[g // 2][g % 2])
+    scaled, inverse = norm_parts(x1_ref[...])
+    sums_ref[2:3, :] += jnp.sum(y2 * scaled, axis=0, keepdims=True)
+    sums_ref[3:4, :] += jnp.sum(y2, axis=0, keepdims=True)
+    dx1 = dx1_ref[...] + norm_pull(y2, scaled, inverse, gain_ref[1:2, :])
+    dx1_ref[...] = dx1
+    dself_ref[...] = lower(dx1)
+
+    @pl.when(step == pl.num_programs(0) - 1)
+    def _():
+        for every, result in ((dck_all, dck_ref), (dcv_all, dcv_ref)):
+            for g in range(4):
+                total = 0.0
+                for h in range(4):
+                    lane = lax.broadcasted_iota(jnp.int32, (1, 256), 1) // HEAD
+                    total = total + jnp.where(lane == h, every[g, h * 64 : (h + 1) * 64, :], 0.0)
+                result[g] = total
+
+
+def middle_back(where, ym, yr, x1, x2, d, cq, gains, wq, ck, cv, wc):
+    rows, width = x1.shape
+    block = 208
+    wide = rows_of(block, width)
+    small = pl.BlockSpec((4, 64, 256), lambda i, s: (0, 0, 0))
+    return pl.pallas_call(
+        middle_back_kernel,
+        grid_spec=pltpu.PrefetchScalarGridSpec(
+            num_scalar_prefetch=1,
+            grid=(rows // block,),
+            in_specs=[wide] * 6 + [resident(a.shape) for a in (gains, *wq, *ck, *cv, *wc)],
+            out_specs=[wide] * 4 + [small, small, pl.BlockSpec((8, width), lambda i, s: (0, 0))],
+            scratch_shapes=[pltpu.VMEM((4, 256, 256), FULL)] * 2,
+        ),
+        out_shape=[shape((rows, width), FULL)]
+        + [shape((rows, width), ROUND)] * 3
+        + [shape((4, 64, 256), FULL)] * 2
+        + [shape((8, width), FULL)],
+        compiler_params=params(40),
+        cost_estimate=cost(7e9, 25e6),
+        name="middle_back",
+    )(where, ym, yr, x1, x2, d, cq, gains, *wq, *ck, *cv, *wc)
+
+
+def first_back_kernel(where_ref, *refs):
+    grads = refs[:6]
+    w0_ref, w1_ref, y_ref = refs[6:]
+    y = 0.0
+    for g in range(2):
+        for c in range(3):
+            y = y + nt(grads[3 * g + c][...], (w0_ref, w1_ref)[g][c])
+    y_ref[...] = y.astype(y_ref.dtype)
+
+
+def first_back(half, grads, weights, kind):
+    span = grads[0].shape[0]
+    rows = span // 2
+    width = weights[0].shape[1]
+    block = 208
+    steps = rows // block
+    piece = pl.BlockSpec((block, 256), lambda i, s: (s[0] * steps + i, 0))
+    return pl.pallas_call(
+        first_back_kernel,
+        grid_spec=pltpu.PrefetchScalarGridSpec(
+            num_scalar_prefetch=1,
+            grid=(steps,),
+            in_specs=[piece] * 6 + [resident(a.shape) for a in weights],
+            out_specs=rows_of(block, width),
+        ),
+        out_shape=shape((rows, width), kind),
+        compiler_params=params(24),
+        cost_estimate=cost(2 * rows * width * 1536, 8e6),
+        name="first_back",
+    )(half, *grads, *weights)
+
+
+def frames_back_kernel(where_ref, ym_ref, yr_ref, dx1_ref, frame_ref, gain_ref, out_ref, sums_ref):
+    @pl.when(pl.program_id(0) == 0)
+    def _():
+        sums_ref[...] = jnp.zeros_like(sums_ref)
+
+    y = ym_ref[...] + yr_ref[...].astype(FULL)
+    scaled, inverse = norm_parts(frame_ref[...].astype(FULL))
+    sums_ref[0:1, :] += jnp.sum(y * scaled, axis=0, keepdims=True)
+    sums_ref[1:2, :] += jnp.sum(y, axis=0, keepdims=True)
+    out_ref[...] = lower(dx1_ref[...] + norm_pull(y, scaled, inverse, gain_ref[0:1, :]))
+
+
+def frames_back(where, ym, yr, dx1, frames, gains):
+    rows, width = dx1.shape
+    block = 208
+    wide = rows_of(block, width)
+    return pl.pallas_call(
+        frames_back_kernel,
+        grid_spec=pltpu.PrefetchScalarGridSpec(
+            num_scalar_prefetch=1,
+            grid=(rows // block,),
+            in_specs=[wide] * 4 + [resident(gains.shape)],
+            out_specs=[wide, pl.BlockSpec((8, width), lambda i, s: (0, 0))],
+        ),
+        out_shape=[shape((rows, width), ROUND), shape((8, width), FULL)],
+        compiler_params=params(24),
+        cost_estimate=cost(1e7, 12e6),
+        name="frames_back",
+    )(where, ym, yr, dx1, frames, gains)
+
+
+def chip_local(
+    frames, text_states, lengths, loss_mask, norm_gain, norm_bias, w_qkv, w_out, w_cross_q,
+    w_cross_kv, w_cross_out, w_up, w_down, cotangent,
+):
+    at = lax.axis_index("narrow")
+    core = at % 2
+    side = at // 2
+    layer = lax.axis_index("wide") // 2
+    where = core.reshape(1).astype(jnp.int32)
+    away = (1 - core).reshape(1).astype(jnp.int32)
+    limit = lax.dynamic_slice(lengths, (side,), (1,))
+
+    def over_core(v):
+        return lax.ppermute(v, "narrow", CORE_PAIRS)
+
+    def over_y(v):
+        return lax.ppermute(v, "narrow", Y_PAIRS)
+
+    def along_wide(v, pairs):
+        return lax.ppermute(v, "wide", pairs)
+
+    def in_order(mine, other):
+        return jnp.where(
+            core == 0,
+            jnp.concatenate([mine, other], axis=0),
+            jnp.concatenate([other, mine], axis=0),
+        )
+
+    def over_chips(partial):
+        def plus(a, b):
+            return lower(a.astype(FULL) + b.astype(FULL))
+
+        total = plus(partial, along_wide(partial, X_PAIRS))
+        total = plus(total, along_wide(total, Z_INWARD))
+        total = plus(total, along_wide(total, Z_MIDDLE))
+        outer = along_wide(total, Z_OUTWARD)
+        return jnp.where((layer == 1) | (layer == 2), total, outer).astype(FULL)
+
+    def reduced(own, partner):
+        return over_chips(lower(own + over_y(lower(partner)).astype(FULL)))
+
+    qkv_y = over_y(w_qkv)
+    out_y = over_y(w_out)
+    cross_q_y = over_y(w_cross_q)
+    cross_kv_y = over_y(w_cross_kv)
+    cross_out_y = over_y(w_cross_out)
+    up_y = over_y(w_up)
+    down_y = over_y(w_down)
+
+    scaled, _ = norm_parts(frames.astype(FULL))
+    h1 = lower(scaled * norm_gain[0] + norm_bias[0])
+    h1_other = over_core(h1)
+    dout = jnp.where(loss_mask[:, None] != 0, cotangent, jnp.zeros((), ROUND))
+    dout_other = over_core(dout)
+
+    q0, k0, v0 = project(where, h1, h1_other, w_qkv, False)
+    o0, lse0 = self_forward(limit, q0, k0, v0)
+    q1, k1, v1 = project(where, h1, h1_other, qkv_y, False)
+    o1, lse1 = self_forward(limit, q1, k1, v1)
+    rows = frames.shape[0]
+
+    def away_rows(v):
+        return lax.dynamic_slice(v, ((1 - core) * rows, 0), (rows, v.shape[1]))
+
+    o0_other = over_core(away_rows(o0))
+    o1_other = over_core(away_rows(o1))
+
+    wo = jnp.concatenate([w_out, out_y], axis=0)
+    wo = (wo, over_core(wo))
+    wq = jnp.stack([w_cross_q, cross_q_y], axis=0)
+    wq = (wq, over_core(wq))
+    wc = jnp.concatenate([w_cross_out, cross_out_y], axis=0)
+    wc = (wc, over_core(wc))
+    text = lax.dynamic_slice(text_states, (side, 0, 0), (1, *text_states.shape[1:]))[0]
+    pair = lower(
+        jnp.einsum(
+            "td,gcde->gcte", text, jnp.stack([w_cross_kv, cross_kv_y]), preferred_element_type=FULL
+        )
+    )
+    pair_other = over_core(pair)
+    head_of = jnp.arange(256) // HEAD
+    same = head_of[:, None] == head_of[None, :]
+
+    def spread_heads(v):
+        return jnp.where(same, jnp.tile(v, (1, 4, 1)), jnp.zeros((), ROUND))
+
+    ck = (spread_heads(pair[:, 0]), spread_heads(pair_other[:, 0]))
+    cv = (spread_heads(pair[:, 1]), spread_heads(pair_other[:, 1]))
+
+    x1, x2, h2, cq, ca, h3 = middle_forward(
+        where, frames, (o0, o1), (o0_other, o1_other), norm_gain, norm_bias, wo, wq, ck, cv, wc
+    )
+    h3_other = over_core(h3)
+    h2_other = over_core(h2)
+    ca_other = over_core(ca[:, 512:])
+
+    up = (w_up, up_y)
+    down = (w_down, down_y)
+    g0m, g1m, du0m, du1m, outm, ym = feed(where, h3, dout, up, down, FULL)
+    g0o, g1o, du0o, du1o, outo, yo = feed(where, h3_other, dout_other, up, down, ROUND)
+    y_received = over_core(yo)
+    out_received = over_core(outo)
+
+    def rows_sum(left_mine, right_mine, left_other, right_other):
+        return tn(left_mine, right_mine) + tn(left_other, right_other)
+
+    grad_up = reduced(
+        rows_sum(h3, du0m, h3_other, du0o), rows_sum(h3, du1m, h3_other, du1o)
+    )
+    grad_down = reduced(
+        rows_sum(g0m, dout, g0o, dout_other), rows_sum(g1m, dout, g1o, dout_other)
+    )
+
+    dx1, dself, dcross, dcq, dck, dcv, sums = middle_back(
+        where, ym, y_received, x1, x2, dout, cq, norm_gain, wq, ck, cv, wc
+    )
+    out_rows = lower(x2 + outm + out_received.astype(FULL))
+    dself_other = over_core(dself)
+    dcross_other = over_core(dcross)
+    dcq_other = over_core(dcq[:, 512:])
+    d_pair = jnp.stack([dck, dcv], axis=1)
+    d_pair = lower(d_pair[:2] + over_core(d_pair[2:]))
+
+    do0, do1 = project(where, dself, dself_other, jnp.stack([w_out, out_y]), True)
+    dself_rows = in_order(dself, dself_other)
+    h1_rows = in_order(h1, h1_other)
+
+    def cross_term(g):
+        lanes = slice(g * 256, (g + 1) * 256)
+        return (
+            rows_sum(ca[:, lanes], dcross, ca_other[:, lanes], dcross_other),
+            jnp.concatenate(
+                [
+                    rows_sum(h2, dcq[:, lanes], h2_other, dcq_other[:, lanes]),
+                    tn(text, d_pair[g, 0]),
+                    tn(text, d_pair[g, 1]),
+                ],
+                axis=0,
+            ),
+        )
+
+    term0 = cross_term(0)
+    term1 = cross_term(1)
+    grad_cross_out = reduced(term0[0], term1[0])
+    grad_cross_in = reduced(term0[1], term1[1])
+    width = frames.shape[1]
+    grad_cross_q = grad_cross_in[:width]
+    grad_cross_kv = grad_cross_in[width:].reshape(2, width, 256)
+    grad_out = reduced(tn(o0, dself_rows), tn(o1, dself_rows))
+
+    text_part = 0.0
+    for g, weights in ((0, w_cross_kv), (1, cross_kv_y)):
+        for c in range(2):
+            text_part = text_part + nt(d_pair[g, c], weights[c])
+    text_grad = lower(text_part + over_core(text_part))
+    text_away = over_y(text_grad)
+    grad_text = jnp.where(
+        side == 0, jnp.stack([text_grad, text_away]), jnp.stack([text_away, text_grad])
+    )
+
+    grads1 = self_back(limit, q1, k1, v1, o1, do1, lse1)
+    term1 = jnp.concatenate([tn(h1_rows, g) for g in grads1], axis=0)
+    grads0 = self_back(limit, q0, k0, v0, o0, do0, lse0)
+    term0 = jnp.concatenate([tn(h1_rows, g) for g in grads0], axis=0)
+    grad_qkv = reduced(term0, term1).reshape(3, width, 256)
+
+    yo = first_back(away, (*grads0, *grads1), (w_qkv, qkv_y), ROUND)
+    y_received = over_core(yo)
+    ym = first_back(where, (*grads0, *grads1), (w_qkv, qkv_y), FULL)
+    grad_frames, first_sums = frames_back(where, ym, y_received, dx1, frames, norm_gain)
+
+    sums = sums + first_sums
+    sums = sums + over_core(sums)
+    sums = sums + over_y(sums)
+    sums = sums + along_wide(sums, X_PAIRS)
+    sums = sums + along_wide(sums, Z_NEAR)
+    sums = sums + along_wide(sums, Z_FAR)
+    return (
+        out_rows,
+        grad_frames,
+        grad_text,
+        sums[0:6:2],
+        sums[1:6:2],
+        grad_qkv,
+        grad_out,
+        grad_cross_q,
+        grad_cross_kv,
+        grad_cross_out,
+        grad_up,
+        grad_down,
+    )
+
+
 def solution(mesh):
+    chips = dict(mesh.shape) == {"wide": 8, "narrow": 4}
     return jax.shard_map(
-        local,
+        chip_local if chips else general_local,
         mesh=mesh,
         in_specs=(
             P(("wide", "narrow"), None),

time: 2270 us -> 889 us (0.39)
  waiting for transfers between devices: 1340 us -> 466 us
  matrix products: 470 us -> 80 us
  Pallas kernels: 0 us -> 186 us
  local copies, waits for them, and re-layouts: 172 us -> 10.7 us
  other arithmetic: 169 us -> 67.3 us
  starting transfers between devices: 1.14 us -> 71.6 us
  blocking collectives: 57.2 us -> 0 us
  loops' own time: 39.1 us -> 0 us
    reduce_scatter x6 -> x0, waiting for transfers between devices: 612 us -> none  [collect(): lax.psum_scatter(product(lax.slice_in_dim(left_side, 0, lax.axis_size('na...]
    psum x1 -> x0, waiting for transfers between devices: 484 us -> none  [local(): lax.psum((grad_qkv, grad_out, grad_cross_q, grad_cross_kv, grad_cross_out...]
    ppermute x0 -> x62, waiting for transfers between devices: none -> 466 us  [the longest x27 329 us: along_wide(): return lax.ppermute(v, 'wide', pairs)]
    dot_general x63 -> x33, matrix products: 470 us -> 80 us  [the longest x28 72.4 us: tn(): lax.dot_general(a, b, (((0,), (0,)), ((), ())), preferred_element_type=FULL)]
    all_gather x6 -> x0, waiting for transfers between devices: 244 us -> none  [spread(): return lax.all_gather(shard_rows, 'narrow', axis=0, tiled=True)]
    pallas_call x0 -> x14, Pallas kernels: none -> 186 us  [the longest x2 47.1 us: feed(): pl.pallas_call(feed_kernel, grid_spec=pltpu.PrefetchScalarGridSpec(num_sc...]
    ppermute x0 -> x62, starting transfers between devices: none -> 71.6 us  [the longest x27 47.6 us: along_wide(): return lax.ppermute(v, 'wide', pairs)]
    reduce_sum x13 -> x2, other arithmetic: 63 us -> 2.5 us  [the longest x1 1.9 us: norm_parts(): centered = v - jnp.mean(v, axis=-1, keepdims=True)]
  transfers between devices with their start and end apart: 13 -> 62, of which waited for: 13 -> 24; matrix products, arithmetic and copies ran while one was open for 4% -> 17% of each run, Pallas kernels for 0% -> 21%
where the time goes in v1:
time: 889 us; the launch traced here: 884 us
  waiting for transfers between devices  466 us (52%)
  Pallas kernels  186 us (21%)
  matrix products  80 us (9%)
  starting transfers between devices  71.6 us (8%)
  other arithmetic  67.3 us (8%)
  local copies, waits for them, and re-layouts  10.7 us (1%)
    ppermute x27, waiting for transfers between devices, along_wide(): return lax.ppermute(v, 'wide', pairs)  329 us
    ppermute x15, waiting for transfers between devices, over_y(): return lax.ppermute(v, 'narrow', Y_PAIRS)  135 us
    dot_general x28, matrix products, tn(): lax.dot_general(a, b, (((0,), (0,)), ((), ())), preferred_element_type=FULL)  72.4 us
    ppermute x27, starting transfers between devices, along_wide(): return lax.ppermute(v, 'wide', pairs)  47.6 us
    pallas_call x2, Pallas kernels, feed(): pl.pallas_call(feed_kernel, grid_spec=pltpu.PrefetchScalarGridSpec(num_sc...  47.1 us
    convert_element_type x26, other arithmetic, lower(): return values_in.astype(jnp.bfloat16)  46 us
    pallas_call x2, Pallas kernels, self_back(): pl.pallas_call(functools.partial(self_back_kernel, span=span, floor=floor...  40.3 us
    pallas_call x2, Pallas kernels, self_forward(): pl.pallas_call(functools.partial(self_forward_kernel, span=span, floor=fl...  31.8 us
  transfers between devices with their start and end apart: 62, of which 24 were waited for; matrix products, arithmetic and copies ran while one was open for 17% of the time, Pallas kernels for 21%

profile of v1, /device:TPU:0, one launch (start us, length us, event | category | flops | bytes accessed | tf_op | source)
XLA Modules:
  0.0 884.3 jit_solution(15614718626108295254)
XLA Ops:
  5.7 2.5 collective-permute-start.4
  14.6 6.4 collective-permute-done.4
  23.0 43.0 %collective-permute-done.10 = bf16[256,1024]{1,0:T(8,128)(2,1)S(1)} collective-permute-done((bf16[256,1024]{1,0:T(8,128)(2,1)}, bf16[256,1024]{1,0:T(8,128)(2,1)S(1)}, u32[]{:S(2)}, u32[]{:S(2)}) %collective-permute-start.10) | collective-permute-done | bytes 524320 | tf_op jit(solution)/shard_map/ppermute | solution.py:821
  73.6 4.8 project.3
  78.4 15.6 %self_forward.2 = (bf16[1664,256]{1,0:T(8,128)(2,1)S(1)}, f32[2,8,1664]{2,1,0:T(8,128)S(1)}) custom-call(s32[1]{0:T(128)} %dynamic_slice.12.limit_ref, bf16[1664,256]{1,0:T(8,128)(2,1)S(1)} %get-tuple-element.57.q_ref, bf16[1664,256]{1,0:T(8,128)(2,1)S(1)} %get-tuple-element.58.k_ref, bf16[1664,256]{1,0:T(8,128)(2,1)S(1)} %get-tuple-element.59.v_ref), custom_call_target="tpu_custom_call" | custom-call | flops 16000000000 | bytes 4000000 | tf_op jit(solution)/shard_map/self_forward/pallas_call | solution.py:455
  94.1 5.5 collective-permute-done.1.weight_ref.refs_7_
  99.6 5.1 project.4
  104.7 16.1 %self_forward.3 = (bf16[1664,256]{1,0:T(8,128)(2,1)S(1)}, f32[2,8,1664]{2,1,0:T(8,128)S(1)}) custom-call(s32[1]{0:T(128)} %dynamic_slice.12.limit_ref, bf16[1664,256]{1,0:T(8,128)(2,1)S(1)} %get-tuple-element.61.q_ref, bf16[1664,256]{1,0:T(8,128)(2,1)S(1)} %get-tuple-element.62.k_ref, bf16[1664,256]{1,0:T(8,128)(2,1)S(1)} %get-tuple-element.63.v_ref), custom_call_target="tpu_custom_call" | custom-call | flops 16000000000 | bytes 4000000 | tf_op jit(solution)/shard_map/self_forward/pallas_call | solution.py:455
  121.6 4.2 maximum_select_fusion
  126.2 20.3 %middle_forward.1 = (f32[832,1024]{1,0:T(8,128)}, f32[832,1024]{1,0:T(8,128)}, bf16[832,1024]{1,0:T(8,128)(2,1)S(1)}, bf16[832,1024]{1,0:T(8,128)(2,1)S(1)}, bf1...) custom-call(s32[1]{0:T(128)} %bitcast.where_ref, bf16[832,1024]{1,0:T(8,128)(2,1)} %frame_ref.3, ...), custom_call_target="tpu_custom_call" | custom-call | flops 7000000000 | bytes 25000000 | tf_op jit(solution)/shard_map/middle_forward/pallas_call | solution.py:602
  149.5 39.9 %collective-permute-done.13.down1_ref = bf16[1024,1024]{1,0:T(8,128)(2,1)} collective-permute-done((bf16[1024,1024]{1,0:T(8,128)(2,1)}, bf16[1024,1024]{1,0:T(8,128)(2,1)}, u32[]{:S(2)}, u32[]{:S(2)}) %collective-permute-start.13) | collective-permute-done | bytes 2097184 | tf_op jit(solution)/shard_map/ppermute | solution.py:821
  189.4 23.5 %feed.2 = (bf16[832,1024]{1,0:T(8,128)(2,1)S(1)}, bf16[832,1024]{1,0:T(8,128)(2,1)S(1)}, bf16[832,1024]{1,0:T(8,128)(2,1)S(1)}, bf16[832,1024]{1,0:T(8,128)(2,1)...) custom-call(s32[1]{0:T(128)} %bitcast.where_ref, bf16[832,1024]{1,0:T(8,128)(2,1)} %get-tuple-element.66.h_ref, ...), custom_call_target="tpu_custom_call" | custom-call | flops 13958643712 | bytes 30000000 | tf_op jit(solution)/shard_map/feed/pallas_call | solution.py:647
  212.9 4.4 fusion.68
  217.3 5.9 fusion.71
  223.3 23.6 %feed.3 = (bf16[832,1024]{1,0:T(8,128)(2,1)S(1)}, bf16[832,1024]{1,0:T(8,128)(2,1)S(1)}, bf16[832,1024]{1,0:T(8,128)(2,1)S(1)}, bf16[832,1024]{1,0:T(8,128)(2,1)...) custom-call(s32[1]{0:T(128)} %bitcast.where_ref, bf16[832,1024]{1,0:T(8,128)(2,1)} %collective-permute-done.14.h_ref, ...), custom_call_target="tpu_custom_call" | custom-call | flops 13958643712 | bytes 30000000 | tf_op jit(solution)/shard_map/feed/pallas_call | solution.py:647
  247.4 4.5 fusion.70
  252.0 3.9 add_convert_fusion.9
  257.6 5.9 fusion.69
  263.4 3.9 fusion.73
  267.3 5.9 fusion.72
  273.3 5.7 add_convert_fusion.4
  279.2 22.0 %middle_back.1 = (f32[832,1024]{1,0:T(8,128)}, bf16[832,1024]{1,0:T(8,128)(2,1)S(1)}, bf16[832,1024]{1,0:T(8,128)(2,1)S(1)}, bf16[832,1024]{1,0:T(8,128)(2,1)S(1...) custom-call(s32[1]{0:T(128)} %bitcast.where_ref, ...), custom_call_target="tpu_custom_call" | custom-call | flops 7000000000 | bytes 25000000 | tf_op jit(solution)/shard_map/middle_back/pallas_call | solution.py:723
  301.4 5.7 add_convert_fusion.10
  316.7 5.6 add_convert_fusion.8
  322.4 26.3 %collective-permute-done.57 = bf16[1024,1024]{1,0:T(8,128)(2,1)} collective-permute-done((bf16[1024,1024]{1,0:T(8,128)(2,1)}, bf16[1024,1024]{1,0:T(8,128)(2,1)}, u32[]{:S(2)}, u32[]{:S(2)}) %collective-permute-start.57) | collective-permute-done | bytes 2097184 | tf_op jit(solution)/shard_map/ppermute | solution.py:821
  350.4 5.4 add_convert_fusion.3
  358.6 2.2 fusion.36
  360.8 2.2 fusion.34
  367.2 2.2 project.5
  370.4 20.2 %self_back.3 = (bf16[1664,256]{1,0:T(8,128)(2,1)S(1)}, bf16[1664,256]{1,0:T(8,128)(2,1)S(1)}, bf16[1664,256]{1,0:T(8,128)(2,1)S(1)}) custom-call(s32[1]{0:T(128)} %dynamic_slice.12.limit_ref, bf16[1664,256]{1,0:T(8,128)(2,1)S(1)} %copy-done.29, bf16[1664,256]{1,0:T(8,128)(2,1)S(1)} %copy-done.31, bf16[1664,256]{1,0:T(8,128)(2,1)S(1)} %copy-done.33, ...), custom_call_target="tpu_custom_call" | custom-call | flops 20000000000 | bytes 6000000 | tf_op jit(solution)/shard_map/self_back/pallas_call | solution.py:536
  390.6 4.1 convolution_convert_fusion.1
  396.7 20.1 %self_back.2 = (bf16[1664,256]{1,0:T(8,128)(2,1)S(1)}, bf16[1664,256]{1,0:T(8,128)(2,1)S(1)}, bf16[1664,256]{1,0:T(8,128)(2,1)S(1)}) custom-call(s32[1]{0:T(128)} %dynamic_slice.12.limit_ref, bf16[1664,256]{1,0:T(8,128)(2,1)S(1)} %copy-done.23, bf16[1664,256]{1,0:T(8,128)(2,1)S(1)} %copy-done.25, bf16[1664,256]{1,0:T(8,128)(2,1)S(1)} %copy-done.27, ...), custom_call_target="tpu_custom_call" | custom-call | flops 20000000000 | bytes 6000000 | tf_op jit(solution)/shard_map/self_back/pallas_call | solution.py:536
  416.8 3.3 fusion.67
  423.1 4.4 first_back.3
  431.1 2.3 fusion.30
  434.7 2.3 fusion.32
  437.1 4.4 first_back.2.ym_ref
  447.0 10.2 %collective-permute-done.47 = bf16[256,1024]{1,0:T(8,128)(2,1)S(1)} collective-permute-done((bf16[256,1024]{1,0:T(8,128)(2,1)S(1)}, bf16[256,1024]{1,0:T(8,128)(2,1)S(1)}, u32[]{:S(2)}, u32[]{:S(2)}) %collective-permute-start.47) | collective-permute-done | bytes 524320 | tf_op jit(solution)/shard_map/ppermute | solution.py:821
  463.7 3.4 add_convert_fusion.7
  467.1 7.5 collective-permute-done.34
  476.3 3.5 collective-permute-start.35
  479.9 4.1 frames_back.1
  487.1 3.5 collective-permute-start.49
  498.6 52.9 %collective-permute-done.25 = f32[8,1024]{1,0:T(8,128)S(1)} collective-permute-done((f32[8,1024]{1,0:T(8,128)S(1)}, f32[8,1024]{1,0:T(8,128)S(1)}, u32[]{:S(2)}, u32[]{:S(2)}) %collective-permute-start.25) | collective-permute-done | bytes 32800 | tf_op jit(solution)/shard_map/ppermute | solution.py:824
  553.0 3.7 collective-permute-start.26
  560.1 4.0 collective-permute-start.27
  565.6 2.5 collective-permute-start.42
  568.1 4.5 add_convert_fusion.2
  572.6 6.1 collective-permute-done.27
  578.7 2.9 collective-permute-start.54
  589.3 2.3 add_convert_fusion.16
  591.6 10.5 %collective-permute-done.42 = bf16[3072,256]{1,0:T(8,128)(2,1)} collective-permute-done((bf16[3072,256]{1,0:T(8,128)(2,1)}, bf16[3072,256]{1,0:T(8,128)(2,1)}, u32[]{:S(2)}, u32[]{:S(2)}) %collective-permute-start.42) | collective-permute-done | bytes 1572896 | tf_op jit(solution)/shard_map/ppermute | solution.py:824
  602.1 4.5 collective-permute-start.30
  606.6 2.3 add_convert_fusion.12
  608.9 38.1 %collective-permute-done.54 = bf16[1024,1024]{1,0:T(8,128)(2,1)} collective-permute-done((bf16[1024,1024]{1,0:T(8,128)(2,1)S(1)}, bf16[1024,1024]{1,0:T(8,128)(2,1)}, u32[]{:S(2)}, u32[]{:S(2)}) %collective-permute-start.54) | collective-permute-done | bytes 2097184 | tf_op jit(solution)/shard_map/ppermute | solution.py:824
  647.7 2.5 add_convert_fusion.6
  650.2 41.7 %collective-permute-done.59 = bf16[1024,1024]{1,0:T(8,128)(2,1)S(1)} collective-permute-done((bf16[1024,1024]{1,0:T(8,128)(2,1)}, bf16[1024,1024]{1,0:T(8,128)(2,1)S(1)}, u32[]{:S(2)}, u32[]{:S(2)}) %collective-permute-start.59) | collective-permute-done | bytes 2097184 | tf_op jit(solution)/shard_map/ppermute | solution.py:824
  695.6 25.4 %collective-permute-done.30 = bf16[3072,256]{1,0:T(8,128)(2,1)S(1)} collective-permute-done((bf16[3072,256]{1,0:T(8,128)(2,1)S(1)}, bf16[3072,256]{1,0:T(8,128)(2,1)S(1)}, u32[]{:S(2)}, u32[]{:S(2)}) %collective-permute-start.30) | collective-permute-done | bytes 1572896 | tf_op jit(solution)/shard_map/ppermute | solution.py:824
  731.3 32.6 %collective-permute-done.44 = bf16[3072,256]{1,0:T(8,128)(2,1)S(1)} collective-permute-done((bf16[3072,256]{1,0:T(8,128)(2,1)S(1)}, bf16[3072,256]{1,0:T(8,128)(2,1)S(1)}, u32[]{:S(2)}, u32[]{:S(2)}) %collective-permute-start.44) | collective-permute-done | bytes 1572896 | tf_op jit(solution)/shard_map/ppermute | solution.py:824
  766.6 42.2 %collective-permute-done.56 = bf16[1024,1024]{1,0:T(8,128)(2,1)S(1)} collective-permute-done((bf16[1024,1024]{1,0:T(8,128)(2,1)S(1)}, bf16[1024,1024]{1,0:T(8,128)(2,1)S(1)}, u32[]{:S(2)}, u32[]{:S(2)}) %collective-permute-start.56) | collective-permute-done | bytes 2097184 | tf_op jit(solution)/shard_map/ppermute | solution.py:824
  808.9 2.3 select_convert_fusion.1
  811.2 42.7 %collective-permute-done.61 = bf16[1024,1024]{1,0:T(8,128)(2,1)S(1)} collective-permute-done((bf16[1024,1024]{1,0:T(8,128)(2,1)S(1)}, bf16[1024,1024]{1,0:T(8,128)(2,1)S(1)}, u32[]{:S(2)}, u32[]{:S(2)}) %collective-permute-start.61) | collective-permute-done | bytes 2097184 | tf_op jit(solution)/shard_map/ppermute | solution.py:824
  853.8 2.3 select_convert_fusion
  856.1 25.9 %collective-permute-done.32 = bf16[3072,256]{1,0:T(8,128)(2,1)S(1)} collective-permute-done((bf16[3072,256]{1,0:T(8,128)(2,1)S(1)}, bf16[3072,256]{1,0:T(8,128)(2,1)S(1)}, u32[]{:S(2)}, u32[]{:S(2)}) %collective-permute-start.32) | collective-permute-done | bytes 1572896 | tf_op jit(solution)/shard_map/ppermute | solution.py:824
  (289 shorter events, 114.9 us)
Async XLA Ops:
  0.6 68.9 %copy-start = (bf16[2,64,1024]{2,1,0:T(8,128)(2,1)S(1)}, bf16[2,64,1024]{2,1,0:T(8,128)(2,1)}, u32[]{:S(2)}) copy-start(bf16[2,64,1024]{2,1,0:T(8,128)(2,1)} %param.15) | copy-start | bytes 786436
  5.2 68.0 %collective-permute-start = (bf16[832,1024]{1,0:T(8,128)(2,1)}, bf16[832,1024]{1,0:T(8,128)(2,1)S(1)}, u32[]{:S(2)}, u32[]{:S(2)}) collective-permute-start(bf16[832,1024]{1,0:T(8,128)(2,1)} %fusion.5.mine_ref), channel_id=1, source_target_pairs={{0,1},{1,0},{2,3},{3,2},{4,5},{5,4},{6,7},{7,6},{8,9},{9,8},{10,11... | collective-permute-start | bytes 5111816 | tf_op jit(solution)/shard_map/ppermute | solution.py:818
  5.7 15.3 %collective-permute-start.4 = (bf16[256,1024]{1,0:T(8,128)(2,1)S(1)}, bf16[256,1024]{1,0:T(8,128)(2,1)S(1)}, u32[]{:S(2)}, u32[]{:S(2)}) collective-permute-start(bf16[256,1024]{1,0:T(8,128)(2,1)S(1)} %copy-done.42), channel_id=1, source_target_pairs={{0,2},{2,0},{1,3},{3,1},{4,6},{6,4},{5,7},{7,5},{8,10},{10,8},{9,1... | collective-permute-start | bytes 1572872 | tf_op jit(solution)/shard_map/ppermute | solution.py:821
  8.2 59.7 %collective-permute-start.6 = (bf16[1024,256]{1,0:T(8,128)(2,1)}, bf16[1024,256]{1,0:T(8,128)(2,1)}, u32[]{:S(2)}, u32[]{:S(2)}) collective-permute-start(bf16[1024,256]{1,0:T(8,128)(2,1)} %param.22), channel_id=1, source_target_pairs={{0,2},{2,0},{1,3},{3,1},{4,6},{6,4},{5,7},{7,5},{8,10},{10,8},{9,1... | collective-permute-start | bytes 1572872 | tf_op jit(solution)/shard_map/ppermute | solution.py:821
  8.3 61.2 %collective-permute-start.8 = (bf16[2,1024,256]{2,1,0:T(8,128)(2,1)}, bf16[2,1024,256]{2,1,0:T(8,128)(2,1)}, u32[]{:S(2)}, u32[]{:S(2)}) collective-permute-start(bf16[2,1024,256]{2,1,0:T(8,128)(2,1)} %param.23), channel_id=1, source_target_pairs={{0,2},{2,0},{1,3},{3,1},{4,6},{6,4},{5,7},{7,5},{8,10},{10,8},{9,1... | collective-permute-start | bytes 3145736 | tf_op jit(solution)/shard_map/ppermute | solution.py:821
  10.2 55.7 %collective-permute-start.10 = (bf16[256,1024]{1,0:T(8,128)(2,1)}, bf16[256,1024]{1,0:T(8,128)(2,1)S(1)}, u32[]{:S(2)}, u32[]{:S(2)}) collective-permute-start(bf16[256,1024]{1,0:T(8,128)(2,1)} %param.24), channel_id=1, source_target_pairs={{0,2},{2,0},{1,3},{3,1},{4,6},{6,4},{5,7},{7,5},{8,10},{10,8},{9,1... | collective-permute-start | bytes 1572872 | tf_op jit(solution)/shard_map/ppermute | solution.py:821
  21.0 78.6 %collective-permute-start.1 = (bf16[3,1024,256]{2,1,0:T(8,128)(2,1)S(1)}, bf16[3,1024,256]{2,1,0:T(8,128)(2,1)S(1)}, u32[]{:S(2)}, u32[]{:S(2)}) collective-permute-start(bf16[3,1024,256]{2,1,0:T(8,128)(2,1)S(1)} %copy-done.4), channel_id=1, source_target_pairs={{0,2},{2,0},{1,3},{3,1},{4,6},{6,4},{5,7},{7,5},{8,10},{10,8},{9,1... | collective-permute-start | bytes 4718600 | tf_op jit(solution)/shard_map/ppermute | solution.py:821
  65.9 83.3 %collective-permute-start.12 = (bf16[1024,1024]{1,0:T(8,128)(2,1)S(1)}, bf16[1024,1024]{1,0:T(8,128)(2,1)}, u32[]{:S(2)}, u32[]{:S(2)}) collective-permute-start(bf16[1024,1024]{1,0:T(8,128)(2,1)S(1)} %copy-done.49), channel_id=1, source_target_pairs={{0,2},{2,0},{1,3},{3,1},{4,6},{6,4},{5,7},{7,5},{8,10},{10,8},{9,1... | collective-permute-start | bytes 6291464 | tf_op jit(solution)/shard_map/ppermute | solution.py:821
  67.9 121.5 %collective-permute-start.13 = (bf16[1024,1024]{1,0:T(8,128)(2,1)}, bf16[1024,1024]{1,0:T(8,128)(2,1)}, u32[]{:S(2)}, u32[]{:S(2)}) collective-permute-start(bf16[1024,1024]{1,0:T(8,128)(2,1)} %down0_ref.3), channel_id=1, source_target_pairs={{0,2},{2,0},{1,3},{3,1},{4,6},{6,4},{5,7},{7,5},{8,10},{10,8},{9,1... | collective-permute-start | bytes 6291464 | tf_op jit(solution)/shard_map/ppermute | solution.py:821
  71.5 1.4 collective-permute-start.9
  72.9 48.1 %collective-permute-start.5 = (bf16[512,1024]{1,0:T(8,128)(2,1)S(1)}, bf16[512,1024]{1,0:T(8,128)(2,1)S(1)}, u32[]{:S(2)}, u32[]{:S(2)}) collective-permute-start(bf16[512,1024]{1,0:T(8,128)(2,1)S(1)} %constant_dynamic-update-slice_fusion.wo0_ref), channel_id=1, source_target_pairs={{0,1},{1,0},{2,3},{3,2},{4,5},{5,4},{6,7},{7,6},{8,9},{9,8},{10,11... | collective-permute-start | bytes 3145736 | tf_op jit(solution)/shard_map/ppermute | solution.py:818
  73.2 47.9 %collective-permute-start.7 = (bf16[2,1024,256]{2,1,0:T(8,128)(2,1)S(1)}, bf16[2,1024,256]{2,1,0:T(8,128)(2,1)S(1)}, u32[]{:S(2)}, u32[]{:S(2)}) collective-permute-start(bf16[2,1024,256]{2,1,0:T(8,128)(2,1)S(1)} %pad_maximum_fusion.2.wq0_ref), channel_id=1, source_target_pairs={{0,1},{1,0},{2,3},{3,2},{4,5},{5,4},{6,7},{7,6},{8,9},{9,8},{10,11... | collective-permute-start | bytes 3145736 | tf_op jit(solution)/shard_map/ppermute | solution.py:818
  99.6 26.2 %collective-permute-start.11 = (bf16[512,1024]{1,0:T(8,128)(2,1)S(1)}, bf16[512,1024]{1,0:T(8,128)(2,1)S(1)}, u32[]{:S(2)}, u32[]{:S(2)}) collective-permute-start(bf16[512,1024]{1,0:T(8,128)(2,1)S(1)} %constant_dynamic-update-slice_fusion.2.wc0_ref), channel_id=1, source_target_pairs={{0,1},{1,0},{2,3},{3,2},{4,5},{5,4},{6,7},{7,6},{8,9},{9,8},{10,11... | collective-permute-start | bytes 3145736 | tf_op jit(solution)/shard_map/ppermute | solution.py:818
  121.1 5.1 collective-permute-start.2
  121.2 5.0 collective-permute-start.3
  125.8 97.4 %collective-permute-start.15 = (bf16[832,1024]{1,0:T(8,128)(2,1)}, bf16[832,1024]{1,0:T(8,128)(2,1)}, u32[]{:S(2)}, u32[]{:S(2)}) collective-permute-start(bf16[832,1024]{1,0:T(8,128)(2,1)} %broadcast_select_fusion.d_ref), channel_id=1, source_target_pairs={{0,1},{1,0},{2,3},{3,2},{4,5},{5,4},{6,7},{7,6},{8,9},{9,8},{10,11... | collective-permute-start | bytes 5111816 | tf_op jit(solution)/shard_map/ppermute | solution.py:818
  146.5 76.7 %collective-permute-start.14 = (bf16[832,1024]{1,0:T(8,128)(2,1)}, bf16[832,1024]{1,0:T(8,128)(2,1)}, u32[]{:S(2)}, u32[]{:S(2)}) collective-permute-start(bf16[832,1024]{1,0:T(8,128)(2,1)} %get-tuple-element.66.h_ref), channel_id=1, source_target_pairs={{0,1},{1,0},{2,3},{3,2},{4,5},{5,4},{6,7},{7,6},{8,9},{9,8},{10,11... | collective-permute-start | bytes 5111816 | tf_op jit(solution)/shard_map/ppermute | solution.py:818
  146.8 209.7 %collective-permute-start.38 = (bf16[832,1024]{1,0:T(8,128)(2,1)S(1)}, bf16[832,1024]{1,0:T(8,128)(2,1)}, u32[]{:S(2)}, u32[]{:S(2)}) collective-permute-start(bf16[832,1024]{1,0:T(8,128)(2,1)S(1)} %get-tuple-element.90), channel_id=1, source_target_pairs={{0,1},{1,0},{2,3},{3,2},{4,5},{5,4},{6,7},{7,6},{8,9},{9,8},{10,11... | collective-permute-start | bytes 5111816 | tf_op jit(solution)/shard_map/ppermute | solution.py:818
  149.3 279.9 %collective-permute-start.45 = (bf16[832,512]{1,0:T(8,128)(2,1)}, bf16[832,512]{1,0:T(8,128)(2,1)}, u32[]{:S(2)}, u32[]{:S(2)}) collective-permute-start(bf16[832,512]{1,0:T(8,128)(2,1)} %slice.120), channel_id=1, source_target_pairs={{0,1},{1,0},{2,3},{3,2},{4,5},{5,4},{6,7},{7,6},{8,9},{9,8},{10,11... | collective-permute-start | bytes 2555912 | tf_op jit(solution)/shard_map/ppermute | solution.py:818
  246.8 54.5 %collective-permute-start.16 = (bf16[832,1024]{1,0:T(8,128)(2,1)}, bf16[832,1024]{1,0:T(8,128)(2,1)S(1)}, u32[]{:S(2)}, u32[]{:S(2)}) collective-permute-start(bf16[832,1024]{1,0:T(8,128)(2,1)} %get-tuple-element.68), channel_id=1, source_target_pairs={{0,1},{1,0},{2,3},{3,2},{4,5},{5,4},{6,7},{7,6},{8,9},{9,8},{10,11... | collective-permute-start | bytes 5111816 | tf_op jit(solution)/shard_map/ppermute | solution.py:818
  246.9 32.0 %collective-permute-start.17 = (bf16[832,1024]{1,0:T(8,128)(2,1)}, bf16[832,1024]{1,0:T(8,128)(2,1)S(1)}, u32[]{:S(2)}, u32[]{:S(2)}) collective-permute-start(bf16[832,1024]{1,0:T(8,128)(2,1)} %get-tuple-element.70), channel_id=1, source_target_pairs={{0,1},{1,0},{2,3},{3,2},{4,5},{5,4},{6,7},{7,6},{8,9},{9,8},{10,11... | collective-permute-start | bytes 5111816 | tf_op jit(solution)/shard_map/ppermute | solution.py:818
  255.8 60.4 %collective-permute-start.52 = (bf16[1024,1024]{1,0:T(8,128)(2,1)}, bf16[1024,1024]{1,0:T(8,128)(2,1)}, u32[]{:S(2)}, u32[]{:S(2)}) collective-permute-start(bf16[1024,1024]{1,0:T(8,128)(2,1)} %add_convert_fusion.9), channel_id=1, source_target_pairs={{0,2},{2,0},{1,3},{3,1},{4,6},{6,4},{5,7},{7,5},{8,10},{10,8},{9,1... | collective-permute-start | bytes 6291464 | tf_op jit(solution)/shard_map/ppermute | solution.py:821
  278.9 69.8 %collective-permute-start.57 = (bf16[1024,1024]{1,0:T(8,128)(2,1)}, bf16[1024,1024]{1,0:T(8,128)(2,1)}, u32[]{:S(2)}, u32[]{:S(2)}) collective-permute-start(bf16[1024,1024]{1,0:T(8,128)(2,1)} %add_convert_fusion.4), channel_id=1, source_target_pairs={{0,2},{2,0},{1,3},{3,1},{4,6},{6,4},{5,7},{7,5},{8,10},{10,8},{9,1... | collective-permute-start | bytes 6291464 | tf_op jit(solution)/shard_map/ppermute | solution.py:821
  301.4 5.8 collective-permute-start.20
  307.1 59.7 %collective-permute-start.18 = (bf16[832,1024]{1,0:T(8,128)(2,1)S(1)}, bf16[832,1024]{1,0:T(8,128)(2,1)S(1)}, u32[]{:S(2)}, u32[]{:S(2)}) collective-permute-start(bf16[832,1024]{1,0:T(8,128)(2,1)S(1)} %get-tuple-element.73.mine_ref), channel_id=1, source_target_pairs={{0,1},{1,0},{2,3},{3,2},{4,5},{5,4},{6,7},{7,6},{8,9},{9,8},{10,11... | collective-permute-start | bytes 5111816 | tf_op jit(solution)/shard_map/ppermute | solution.py:818
  316.2 6.1 collective-permute-start.21
  322.3 35.8 %collective-permute-start.39 = (bf16[832,512]{1,0:T(8,128)(2,1)S(1)}, bf16[832,512]{1,0:T(8,128)(2,1)S(1)}, u32[]{:S(2)}, u32[]{:S(2)}) collective-permute-start(bf16[832,512]{1,0:T(8,128)(2,1)S(1)} %slice.113), channel_id=1, source_target_pairs={{0,1},{1,0},{2,3},{3,2},{4,5},{5,4},{6,7},{7,6},{8,9},{9,8},{10,11... | collective-permute-start | bytes 2555912 | tf_op jit(solution)/shard_map/ppermute | solution.py:818
  348.7 7.1 collective-permute-start.22
  355.9 73.4 %collective-permute-start.46 = (bf16[832,1024]{1,0:T(8,128)(2,1)S(1)}, bf16[832,1024]{1,0:T(8,128)(2,1)}, u32[]{:S(2)}, u32[]{:S(2)}) collective-permute-start(bf16[832,1024]{1,0:T(8,128)(2,1)S(1)} %get-tuple-element.93), channel_id=1, source_target_pairs={{0,1},{1,0},{2,3},{3,2},{4,5},{5,4},{6,7},{7,6},{8,9},{9,8},{10,11... | collective-permute-start | bytes 5111816 | tf_op jit(solution)/shard_map/ppermute | solution.py:818
  356.6 106.5 %collective-permute-start.53 = (bf16[1024,1024]{1,0:T(8,128)(2,1)}, bf16[1024,1024]{1,0:T(8,128)(2,1)}, u32[]{:S(2)}, u32[]{:S(2)}) collective-permute-start(bf16[1024,1024]{1,0:T(8,128)(2,1)} %add_convert_fusion.8), channel_id=1, source_target_pairs={{0,4},{4,0},{8,12},{12,8},{16,20},{20,16},{24,28},{28,24},{1,5},{5... | collective-permute-start | bytes 6291464 | tf_op jit(solution)/shard_map/ppermute | solution.py:824
  358.1 207.5 %collective-permute-start.58 = (bf16[1024,1024]{1,0:T(8,128)(2,1)}, bf16[1024,1024]{1,0:T(8,128)(2,1)}, u32[]{:S(2)}, u32[]{:S(2)}) collective-permute-start(bf16[1024,1024]{1,0:T(8,128)(2,1)} %add_convert_fusion.3), channel_id=1, source_target_pairs={{0,4},{4,0},{8,12},{12,8},{16,20},{20,16},{24,28},{28,24},{1,5},{5... | collective-permute-start | bytes 6291464 | tf_op jit(solution)/shard_map/ppermute | solution.py:824
  366.9 92.8 %collective-permute-start.40 = (bf16[3072,256]{1,0:T(8,128)(2,1)}, bf16[3072,256]{1,0:T(8,128)(2,1)}, u32[]{:S(2)}, u32[]{:S(2)}) collective-permute-start(bf16[3072,256]{1,0:T(8,128)(2,1)} %pad_maximum_fusion.1), channel_id=1, source_target_pairs={{0,2},{2,0},{1,3},{3,1},{4,6},{6,4},{5,7},{7,5},{8,10},{10,8},{9,1... | collective-permute-start | bytes 4718600 | tf_op jit(solution)/shard_map/ppermute | solution.py:821
  429.2 47.1 %collective-permute-start.19 = (bf16[832,1024]{1,0:T(8,128)(2,1)S(1)}, bf16[832,1024]{1,0:T(8,128)(2,1)S(1)}, u32[]{:S(2)}, u32[]{:S(2)}) collective-permute-start(bf16[832,1024]{1,0:T(8,128)(2,1)S(1)} %first_back.3), channel_id=1, source_target_pairs={{0,1},{1,0},{2,3},{3,2},{4,5},{5,4},{6,7},{7,6},{8,9},{9,8},{10,11... | collective-permute-start | bytes 5111816 | tf_op jit(solution)/shard_map/ppermute | solution.py:818
  429.3 14.3 %collective-permute-start.33 = (bf16[256,1024]{1,0:T(8,128)(2,1)S(1)}, bf16[256,1024]{1,0:T(8,128)(2,1)S(1)}, u32[]{:S(2)}, u32[]{:S(2)}) collective-permute-start(bf16[256,1024]{1,0:T(8,128)(2,1)S(1)} %convolution_convert_fusion), channel_id=1, source_target_pairs={{0,2},{2,0},{1,3},{3,1},{4,6},{6,4},{5,7},{7,5},{8,10},{10,8},{9,1... | collective-permute-start | bytes 1572872 | tf_op jit(solution)/shard_map/ppermute | solution.py:821
  443.6 13.6 %collective-permute-start.47 = (bf16[256,1024]{1,0:T(8,128)(2,1)S(1)}, bf16[256,1024]{1,0:T(8,128)(2,1)S(1)}, u32[]{:S(2)}, u32[]{:S(2)}) collective-permute-start(bf16[256,1024]{1,0:T(8,128)(2,1)S(1)} %fusion.14), channel_id=1, source_target_pairs={{0,2},{2,0},{1,3},{3,1},{4,6},{6,4},{5,7},{7,5},{8,10},{10,8},{9,1... | collective-permute-start | bytes 1572872 | tf_op jit(solution)/shard_map/ppermute | solution.py:821
  457.2 35.2 %collective-permute-start.28 = (bf16[3072,256]{1,0:T(8,128)(2,1)S(1)}, bf16[3072,256]{1,0:T(8,128)(2,1)S(1)}, u32[]{:S(2)}, u32[]{:S(2)}) collective-permute-start(bf16[3072,256]{1,0:T(8,128)(2,1)S(1)} %pad_maximum_fusion), channel_id=1, source_target_pairs={{0,2},{2,0},{1,3},{3,1},{4,6},{6,4},{5,7},{7,5},{8,10},{10,8},{9,1... | collective-permute-start | bytes 4718600 | tf_op jit(solution)/shard_map/ppermute | solution.py:821
  459.7 14.9 %collective-permute-start.34 = (bf16[256,1024]{1,0:T(8,128)(2,1)S(1)}, bf16[256,1024]{1,0:T(8,128)(2,1)S(1)}, u32[]{:S(2)}, u32[]{:S(2)}) collective-permute-start(bf16[256,1024]{1,0:T(8,128)(2,1)S(1)} %fusion.15), channel_id=1, source_target_pairs={{0,4},{4,0},{8,12},{12,8},{16,20},{20,16},{24,28},{28,24},{1,5},{5... | collective-permute-start | bytes 1572872 | tf_op jit(solution)/shard_map/ppermute | solution.py:824
  463.1 22.8 %collective-permute-start.48 = (bf16[256,1024]{1,0:T(8,128)(2,1)S(1)}, bf16[256,1024]{1,0:T(8,128)(2,1)S(1)}, u32[]{:S(2)}, u32[]{:S(2)}) collective-permute-start(bf16[256,1024]{1,0:T(8,128)(2,1)S(1)} %fusion.16), channel_id=1, source_target_pairs={{0,4},{4,0},{8,12},{12,8},{16,20},{20,16},{24,28},{28,24},{1,5},{5... | collective-permute-start | bytes 1572872 | tf_op jit(solution)/shard_map/ppermute | solution.py:824
  474.6 85.4 %collective-permute-start.41 = (bf16[3072,256]{1,0:T(8,128)(2,1)S(1)}, bf16[3072,256]{1,0:T(8,128)(2,1)S(1)}, u32[]{:S(2)}, u32[]{:S(2)}) collective-permute-start(bf16[3072,256]{1,0:T(8,128)(2,1)S(1)} %fusion.7), channel_id=1, source_target_pairs={{0,4},{4,0},{8,12},{12,8},{16,20},{20,16},{24,28},{28,24},{1,5},{5... | collective-permute-start | bytes 4718600 | tf_op jit(solution)/shard_map/ppermute | solution.py:824
  476.3 21.7 %collective-permute-start.35 = (bf16[256,1024]{1,0:T(8,128)(2,1)S(1)}, bf16[256,1024]{1,0:T(8,128)(2,1)S(1)}, u32[]{:S(2)}, u32[]{:S(2)}) collective-permute-start(bf16[256,1024]{1,0:T(8,128)(2,1)S(1)} %add_convert_fusion.22), channel_id=1, source_target_pairs={{0,8},{4,12},{24,16},{28,20},{1,9},{5,13},{25,17},{29,21},{2,10},{... | collective-permute-start | bytes 1572872 | tf_op jit(solution)/shard_map/ppermute | solution.py:824
  485.9 1.2 collective-permute-start.23
  487.1 65.9 %collective-permute-start.49 = (bf16[256,1024]{1,0:T(8,128)(2,1)S(1)}, bf16[256,1024]{1,0:T(8,128)(2,1)S(1)}, u32[]{:S(2)}, u32[]{:S(2)}) collective-permute-start(bf16[256,1024]{1,0:T(8,128)(2,1)S(1)} %add_convert_fusion.19), channel_id=1, source_target_pairs={{0,8},{4,12},{24,16},{28,20},{1,9},{5,13},{25,17},{29,21},{2,10},{... | collective-permute-start | bytes 1572872 | tf_op jit(solution)/shard_map/ppermute | solution.py:824
  492.4 3.9 collective-permute-start.24
  496.3 91.7 %collective-permute-start.29 = (bf16[3072,256]{1,0:T(8,128)(2,1)}, bf16[3072,256]{1,0:T(8,128)(2,1)}, u32[]{:S(2)}, u32[]{:S(2)}) collective-permute-start(bf16[3072,256]{1,0:T(8,128)(2,1)} %fusion.6), channel_id=1, source_target_pairs={{0,4},{4,0},{8,12},{12,8},{16,20},{20,16},{24,28},{28,24},{1,5},{5... | collective-permute-start | bytes 4718600 | tf_op jit(solution)/shard_map/ppermute | solution.py:824
  498.0 53.5 %collective-permute-start.25 = (f32[8,1024]{1,0:T(8,128)S(1)}, f32[8,1024]{1,0:T(8,128)S(1)}, u32[]{:S(2)}, u32[]{:S(2)}) collective-permute-start(f32[8,1024]{1,0:T(8,128)S(1)} %add.196), channel_id=1, source_target_pairs={{0,4},{4,0},{8,12},{12,8},{16,20},{20,16},{24,28},{28,24},{1,5},{5... | collective-permute-start | bytes 98312 | tf_op jit(solution)/shard_map/ppermute | solution.py:824
  551.5 31.3 %collective-permute-start.36 = (bf16[256,1024]{1,0:T(8,128)(2,1)S(1)}, bf16[256,1024]{1,0:T(8,128)(2,1)}, u32[]{:S(2)}, u32[]{:S(2)}) collective-permute-start(bf16[256,1024]{1,0:T(8,128)(2,1)S(1)} %add_convert_fusion.21), channel_id=1, source_target_pairs={{8,16},{16,8},{12,20},{20,12},{9,17},{17,9},{13,21},{21,13},{10,18... | collective-permute-start | bytes 1572872 | tf_op jit(solution)/shard_map/ppermute | solution.py:824
  553.0 5.6 collective-permute-start.26
  558.6 26.9 %collective-permute-start.50 = (bf16[256,1024]{1,0:T(8,128)(2,1)S(1)}, bf16[256,1024]{1,0:T(8,128)(2,1)}, u32[]{:S(2)}, u32[]{:S(2)}) collective-permute-start(bf16[256,1024]{1,0:T(8,128)(2,1)S(1)} %add_convert_fusion.18), channel_id=1, source_target_pairs={{8,16},{16,8},{12,20},{20,12},{9,17},{17,9},{13,21},{21,13},{10,18... | collective-permute-start | bytes 1572872 | tf_op jit(solution)/shard_map/ppermute | solution.py:824
  560.1 18.6 %collective-permute-start.27 = (f32[8,1024]{1,0:T(8,128)S(1)}, f32[8,1024]{1,0:T(8,128)S(1)}, u32[]{:S(2)}, u32[]{:S(2)}) collective-permute-start(f32[8,1024]{1,0:T(8,128)S(1)} %add.198), channel_id=1, source_target_pairs={{0,16},{4,20},{8,24},{12,28},{16,0},{20,4},{24,8},{28,12},{1,17},{... | collective-permute-start | bytes 98312 | tf_op jit(solution)/shard_map/ppermute | solution.py:824
  565.6 36.4 %collective-permute-start.42 = (bf16[3072,256]{1,0:T(8,128)(2,1)}, bf16[3072,256]{1,0:T(8,128)(2,1)}, u32[]{:S(2)}, u32[]{:S(2)}) collective-permute-start(bf16[3072,256]{1,0:T(8,128)(2,1)} %add_convert_fusion.13), channel_id=1, source_target_pairs={{0,8},{4,12},{24,16},{28,20},{1,9},{5,13},{25,17},{29,21},{2,10},{... | collective-permute-start | bytes 4718600 | tf_op jit(solution)/shard_map/ppermute | solution.py:824
  578.7 68.2 %collective-permute-start.54 = (bf16[1024,1024]{1,0:T(8,128)(2,1)S(1)}, bf16[1024,1024]{1,0:T(8,128)(2,1)}, u32[]{:S(2)}, u32[]{:S(2)}) collective-permute-start(bf16[1024,1024]{1,0:T(8,128)(2,1)S(1)} %add_convert_fusion.7), channel_id=1, source_target_pairs={{0,8},{4,12},{24,16},{28,20},{1,9},{5,13},{25,17},{29,21},{2,10},{... | collective-permute-start | bytes 6291464 | tf_op jit(solution)/shard_map/ppermute | solution.py:824
  582.8 109.2 %collective-permute-start.59 = (bf16[1024,1024]{1,0:T(8,128)(2,1)}, bf16[1024,1024]{1,0:T(8,128)(2,1)S(1)}, u32[]{:S(2)}, u32[]{:S(2)}) collective-permute-start(bf16[1024,1024]{1,0:T(8,128)(2,1)} %add_convert_fusion.2), channel_id=1, source_target_pairs={{0,8},{4,12},{24,16},{28,20},{1,9},{5,13},{25,17},{29,21},{2,10},{... | collective-permute-start | bytes 6291464 | tf_op jit(solution)/shard_map/ppermute | solution.py:824
  585.5 108.3 %collective-permute-start.37 = (bf16[256,1024]{1,0:T(8,128)(2,1)S(1)}, bf16[256,1024]{1,0:T(8,128)(2,1)S(1)}, u32[]{:S(2)}, u32[]{:S(2)}) collective-permute-start(bf16[256,1024]{1,0:T(8,128)(2,1)S(1)} %add_convert_fusion.20), channel_id=1, source_target_pairs={{8,0},{12,4},{16,24},{20,28},{9,1},{13,5},{17,25},{21,29},{10,2},{... | collective-permute-start | bytes 1572872 | tf_op jit(solution)/shard_map/ppermute | solution.py:824
  588.0 140.6 %collective-permute-start.51 = (bf16[256,1024]{1,0:T(8,128)(2,1)S(1)}, bf16[256,1024]{1,0:T(8,128)(2,1)S(1)}, u32[]{:S(2)}, u32[]{:S(2)}) collective-permute-start(bf16[256,1024]{1,0:T(8,128)(2,1)S(1)} %add_convert_fusion.17), channel_id=1, source_target_pairs={{8,0},{12,4},{16,24},{20,28},{9,1},{13,5},{17,25},{21,29},{10,2},{... | collective-permute-start | bytes 1572872 | tf_op jit(solution)/shard_map/ppermute | solution.py:824
  602.1 118.9 %collective-permute-start.30 = (bf16[3072,256]{1,0:T(8,128)(2,1)S(1)}, bf16[3072,256]{1,0:T(8,128)(2,1)S(1)}, u32[]{:S(2)}, u32[]{:S(2)}) collective-permute-start(bf16[3072,256]{1,0:T(8,128)(2,1)S(1)} %add_convert_fusion.16), channel_id=1, source_target_pairs={{0,8},{4,12},{24,16},{28,20},{1,9},{5,13},{25,17},{29,21},{2,10},{... | collective-permute-start | bytes 4718600 | tf_op jit(solution)/shard_map/ppermute | solution.py:824
  608.8 83.9 %copy-start.34 = (bf16[1024,1024]{1,0:T(8,128)(2,1)S(1)}, bf16[1024,1024]{1,0:T(8,128)(2,1)}, u32[]{:S(2)}) copy-start(bf16[1024,1024]{1,0:T(8,128)(2,1)} %add_convert_fusion.2) | copy-start | bytes 6291460
  646.9 75.2 %collective-permute-start.43 = (bf16[3072,256]{1,0:T(8,128)(2,1)S(1)}, bf16[3072,256]{1,0:T(8,128)(2,1)S(1)}, u32[]{:S(2)}, u32[]{:S(2)}) collective-permute-start(bf16[3072,256]{1,0:T(8,128)(2,1)S(1)} %add_convert_fusion.12), channel_id=1, source_target_pairs={{8,16},{16,8},{12,20},{20,12},{9,17},{17,9},{13,21},{21,13},{10,18... | collective-permute-start | bytes 4718600 | tf_op jit(solution)/shard_map/ppermute | solution.py:824
  692.0 31.9 %collective-permute-start.55 = (bf16[1024,1024]{1,0:T(8,128)(2,1)S(1)}, bf16[1024,1024]{1,0:T(8,128)(2,1)S(1)}, u32[]{:S(2)}, u32[]{:S(2)}) collective-permute-start(bf16[1024,1024]{1,0:T(8,128)(2,1)S(1)} %add_convert_fusion.6), channel_id=1, source_target_pairs={{8,16},{16,8},{12,20},{20,12},{9,17},{17,9},{13,21},{21,13},{10,18... | collective-permute-start | bytes 6291464 | tf_op jit(solution)/shard_map/ppermute | solution.py:824
  693.7 32.5 %collective-permute-start.60 = (bf16[1024,1024]{1,0:T(8,128)(2,1)S(1)}, bf16[1024,1024]{1,0:T(8,128)(2,1)S(1)}, u32[]{:S(2)}, u32[]{:S(2)}) collective-permute-start(bf16[1024,1024]{1,0:T(8,128)(2,1)S(1)} %add_convert_fusion.1), channel_id=1, source_target_pairs={{8,16},{16,8},{12,20},{20,12},{9,17},{17,9},{13,21},{21,13},{10,18... | collective-permute-start | bytes 6291464 | tf_op jit(solution)/shard_map/ppermute | solution.py:824
  721.3 8.3 collective-permute-start.31
  722.5 41.4 %collective-permute-start.44 = (bf16[3072,256]{1,0:T(8,128)(2,1)S(1)}, bf16[3072,256]{1,0:T(8,128)(2,1)S(1)}, u32[]{:S(2)}, u32[]{:S(2)}) collective-permute-start(bf16[3072,256]{1,0:T(8,128)(2,1)S(1)} %add_convert_fusion.11), channel_id=1, source_target_pairs={{8,0},{12,4},{16,24},{20,28},{9,1},{13,5},{17,25},{21,29},{10,2},{... | collective-permute-start | bytes 4718600 | tf_op jit(solution)/shard_map/ppermute | solution.py:824
  724.8 84.1 %collective-permute-start.56 = (bf16[1024,1024]{1,0:T(8,128)(2,1)S(1)}, bf16[1024,1024]{1,0:T(8,128)(2,1)S(1)}, u32[]{:S(2)}, u32[]{:S(2)}) collective-permute-start(bf16[1024,1024]{1,0:T(8,128)(2,1)S(1)} %add_convert_fusion.5), channel_id=1, source_target_pairs={{8,0},{12,4},{16,24},{20,28},{9,1},{13,5},{17,25},{21,29},{10,2},{... | collective-permute-start | bytes 6291464 | tf_op jit(solution)/shard_map/ppermute | solution.py:824
  727.3 126.6 %collective-permute-start.61 = (bf16[1024,1024]{1,0:T(8,128)(2,1)S(1)}, bf16[1024,1024]{1,0:T(8,128)(2,1)S(1)}, u32[]{:S(2)}, u32[]{:S(2)}) collective-permute-start(bf16[1024,1024]{1,0:T(8,128)(2,1)S(1)} %add_convert_fusion), channel_id=1, source_target_pairs={{8,0},{12,4},{16,24},{20,28},{9,1},{13,5},{17,25},{21,29},{10,2},{... | collective-permute-start | bytes 6291464 | tf_op jit(solution)/shard_map/ppermute | solution.py:824
  730.0 152.0 %collective-permute-start.32 = (bf16[3072,256]{1,0:T(8,128)(2,1)S(1)}, bf16[3072,256]{1,0:T(8,128)(2,1)S(1)}, u32[]{:S(2)}, u32[]{:S(2)}) collective-permute-start(bf16[3072,256]{1,0:T(8,128)(2,1)S(1)} %add_convert_fusion.14), channel_id=1, source_target_pairs={{8,0},{12,4},{16,24},{20,28},{9,1},{13,5},{17,25},{21,29},{10,2},{... | collective-permute-start | bytes 4718600 | tf_op jit(solution)/shard_map/ppermute | solution.py:824
  (54 other events, 630.2 us)

commit v2 on v1

--- a/solution.py
+++ b/solution.py
@@ -567,26 +567,28 @@
 
 
 def middle_forward_kernel(
-    where_ref, frame_ref, a0_ref, a1_ref, a2_ref, a3_ref, gain_ref, bias_ref, wo0_ref, wo1_ref,
-    wq0_ref, wq1_ref, ck0_ref, ck1_ref, cv0_ref, cv1_ref, wc0_ref, wc1_ref,
-    x1_ref, x2_ref, h2_ref, cq_ref, ca_ref, h3_ref
+    where_ref, frame_ref, a0_ref, a1_ref, a2_ref, a3_ref, gain_ref, bias_ref, *refs
 ):
     mixed = (a0_ref, a1_ref, a2_ref, a3_ref)
+    wo, wq, wc = refs[0:4], refs[4:8], refs[12:16]
+    ck0_ref, ck1_ref, cv0_ref, cv1_ref = refs[8:12]
+    x1_ref, x2_ref, h2_ref, cq_ref, ca_ref, h3_ref = refs[16:]
     x1 = frame_ref[...].astype(FULL)
     for g in range(4):
-        part = (wo0_ref, wo1_ref)[g // 2][(g % 2) * 256 : (g % 2 + 1) * 256, :]
-        x1 = x1 + nn(mixed[g][...], part)
+        x1 = x1 + nn(mixed[g][...], wo[g][...])
     x1_ref[...] = x1
     scaled, _ = norm_parts(x1)
     h2 = lower(scaled * gain_ref[1:2, :] + bias_ref[1:2, :])
     h2_ref[...] = h2
     for g in range(4):
         lanes = slice(g * 256, (g + 1) * 256)
-        cq = lower(nn(h2, (wq0_ref, wq1_ref)[g // 2][g % 2]))
+        cq = lower(nn(h2, wq[g][...]))
         cq_ref[:, lanes] = cq
         probability = cross_probability(cq, (ck0_ref, ck1_ref)[g // 2][g % 2])
         ca_ref[:, lanes] = lower(nn(lower(probability), (cv0_ref, cv1_ref)[g // 2][g % 2]))
-    crossed = nn(ca_ref[:, :512], wc0_ref[...]) + nn(ca_ref[:, 512:], wc1_ref[...])
+    crossed = 0.0
+    for g in range(4):
+        crossed = crossed + nn(ca_ref[:, g * 256 : (g + 1) * 256], wc[g][...])
     x2 = x1_ref[...] + crossed
     x2_ref[...] = x2
     scaled, _ = norm_parts(x2)
@@ -615,55 +617,60 @@
     )(where, frames, *attended, *received, gains, biases, *wo, *wq, *ck, *cv, *wc)
 
 
-def feed_kernel(
-    where_ref, h_ref, d_ref, up0_ref, up1_ref, down0_ref, down1_ref,
-    g0_ref, g1_ref, du0_ref, du1_ref, out_ref, y_ref
-):
-    h = h_ref[...]
-    d = d_ref[...]
-    out = 0.0
-    y = 0.0
-    for up, down, g_ref, du_ref in (
-        (up0_ref, down0_ref, g0_ref, du0_ref),
-        (up1_ref, down1_ref, g1_ref, du1_ref),
-    ):
-        u = nn(h, up[...])
-        active, slope = gelu_parts(u)
-        g = lower(active)
-        g_ref[...] = g
-        du = lower(nt(d, down[...]) * slope)
-        du_ref[...] = du
-        out = out + nn(g, down[...])
-        y = y + nt(du, up[...])
+def feed_kernel(where_ref, h_ref, d_ref, up_ref, down_ref, *refs, carried, shared):
+    before = refs[: 2 * carried]
+    g_ref, du_ref, out_ref, y_ref = refs[2 * carried + 2 * shared :]
+    u = nn(h_ref[...], up_ref[...])
+    active, slope = gelu_parts(u)
+    g = lower(active)
+    g_ref[...] = g
+    du = lower(nt(d_ref[...], down_ref[...]) * slope)
+    du_ref[...] = du
+    out = nn(g, down_ref[...])
+    y = nt(du, up_ref[...])
+    if carried:
+        out = before[0][...] + out
+        y = before[1][...] + y
     out_ref[...] = out.astype(out_ref.dtype)
     y_ref[...] = y.astype(y_ref.dtype)
 
 
-def feed(where, h, d, up, down, kind):
+def feed(where, h, d, up, down, kind, before=(), shared=()):
     rows, width = h.shape
     block = 208
-    hidden = up[0].shape[1]
+    steps = rows // block
+    hidden = up.shape[1]
     wide = rows_of(block, width)
+    first = steps if shared else 0
+    kept = pl.BlockSpec((block, hidden), lambda i, s: (i + first, 0))
+    there = pl.BlockSpec(memory_space=pl.ANY)
+    carried = 1 if before else 0
+    at = 5 + len(before)
     return pl.pallas_call(
-        feed_kernel,
+        functools.partial(feed_kernel, carried=carried, shared=1 if shared else 0),
         grid_spec=pltpu.PrefetchScalarGridSpec(
             num_scalar_prefetch=1,
-            grid=(rows // block,),
-            in_specs=[wide, wide] + [resident(a.shape) for a in (*up, *down)],
-            out_specs=[rows_of(block, hidden)] * 4 + [wide] * 2,
+            grid=(steps,),
+            in_specs=[wide, wide, resident(up.shape), resident(down.shape)]
+            + [wide] * len(before)
+            + [there] * len(shared),
+            out_specs=[kept, kept, wide, wide],
         ),
-        out_shape=[shape((rows, hidden), ROUND)] * 4 + [shape((rows, width), kind)] * 2,
-        compiler_params=params(48),
-        cost_estimate=cost(16 * rows * width * hidden, 30e6),
+        out_shape=[shape((2 * rows, hidden), ROUND)] * 2 + [shape((rows, width), kind)] * 2,
+        input_output_aliases={at: 0, at + 1: 1} if shared else {},
+        compiler_params=params(56),
+        cost_estimate=cost(8 * rows * width * hidden, 20e6),
         name="feed",
-    )(where, h, d, *up, *down)
+    )(where, h, d, up, down, *before, *shared)
 
 
 def middle_back_kernel(
-    where_ref, ym_ref, yr_ref, x1_ref, x2_ref, d_ref, cq_ref, gain_ref,
-    wq0_ref, wq1_ref, ck0_ref, ck1_ref, cv0_ref, cv1_ref, wc0_ref, wc1_ref,
-    dx1_ref, dself_ref, dcross_ref, dcq_ref, dck_ref, dcv_ref, sums_ref, dck_all, dcv_all
+    where_ref, ym_ref, yr_ref, x1_ref, x2_ref, d_ref, cq_ref, gain_ref, *refs
 ):
+    wq, wc = refs[0:4], refs[8:12]
+    ck0_ref, ck1_ref, cv0_ref, cv1_ref = refs[4:8]
+    dx1_ref, dself_ref, dcross_ref, dcq_ref, dck_ref, dcv_ref, sums_ref = refs[12:19]
+    dck_all, dcv_all = refs[19:]
     step = pl.program_id(0)
 
     @pl.when(step == 0)
@@ -683,10 +690,9 @@
     y2 = 0.0
     for g in range(4):
         lanes = slice(g * 256, (g + 1) * 256)
-        part = (wc0_ref, wc1_ref)[g // 2][(g % 2) * 256 : (g % 2 + 1) * 256, :]
         keys = (ck0_ref, ck1_ref)[g // 2][g % 2]
         values = (cv0_ref, cv1_ref)[g // 2][g % 2]
-        dcatt = lower(nt(dcross, part))
+        dcatt = lower(nt(dcross, wc[g][...]))
         cq = cq_ref[:, lanes]
         probability = cross_probability(cq, keys)
         weighed = nt(dcatt, values)
@@ -696,7 +702,7 @@
         dcq_ref[:, lanes] = dcq
         dck_all[g] += tn(dcs, cq * HEAD ** (-0.5))
         dcv_all[g] += tn(lower(probability), dcatt)
-        y2 = y2 + nt(dcq, (wq0_ref, wq1_ref)[g // 2][g % 2])
+        y2 = y2 + nt(dcq, wq[g][...])
     scaled, inverse = norm_parts(x1_ref[...])
     sums_ref[2:3, :] += jnp.sum(y2 * scaled, axis=0, keepdims=True)
     sums_ref[3:4, :] += jnp.sum(y2, axis=0, keepdims=True)
@@ -809,10 +815,13 @@
     at = lax.axis_index("narrow")
     core = at % 2
     side = at // 2
+    column = lax.axis_index("wide") % 2
     layer = lax.axis_index("wide") // 2
     where = core.reshape(1).astype(jnp.int32)
     away = (1 - core).reshape(1).astype(jnp.int32)
     limit = lax.dynamic_slice(lengths, (side,), (1,))
+    rows, width = frames.shape
+    join = lax.optimization_barrier
 
     def over_core(v):
         return lax.ppermute(v, "narrow", CORE_PAIRS)
@@ -823,58 +832,67 @@
     def along_wide(v, pairs):
         return lax.ppermute(v, "wide", pairs)
 
-    def in_order(mine, other):
+    def half_of(v, which):
+        half = v.shape[0] // 2
+        return lax.dynamic_slice_in_dim(v, which * half, half, axis=0)
+
+    def ordered(first, second, which):
         return jnp.where(
-            core == 0,
-            jnp.concatenate([mine, other], axis=0),
-            jnp.concatenate([other, mine], axis=0),
+            which == 0,
+            jnp.concatenate([first, second], axis=0),
+            jnp.concatenate([second, first], axis=0),
         )
 
-    def over_chips(partial):
-        def plus(a, b):
-            return lower(a.astype(FULL) + b.astype(FULL))
-
-        total = plus(partial, along_wide(partial, X_PAIRS))
-        total = plus(total, along_wide(total, Z_INWARD))
-        total = plus(total, along_wide(total, Z_MIDDLE))
-        outer = along_wide(total, Z_OUTWARD)
-        return jnp.where((layer == 1) | (layer == 2), total, outer).astype(FULL)
-
-    def reduced(own, partner):
-        return over_chips(lower(own + over_y(lower(partner)).astype(FULL)))
-
-    qkv_y = over_y(w_qkv)
-    out_y = over_y(w_out)
-    cross_q_y = over_y(w_cross_q)
-    cross_kv_y = over_y(w_cross_kv)
-    cross_out_y = over_y(w_cross_out)
-    up_y = over_y(w_up)
-    down_y = over_y(w_down)
-
+    near = layer % 2
+
+    def ask(v, which):
+        return over_y(half_of(v, which))
+
+    bundle = jnp.concatenate(
+        [w_out, w_cross_out, w_cross_q.reshape(256, 1024), w_cross_kv.reshape(512, 1024)], axis=0
+    )
+    qkv_first = ask(w_qkv.reshape(3 * width, 256), near)
     scaled, _ = norm_parts(frames.astype(FULL))
     h1 = lower(scaled * norm_gain[0] + norm_bias[0])
     h1_other = over_core(h1)
     dout = jnp.where(loss_mask[:, None] != 0, cotangent, jnp.zeros((), ROUND))
+    q0, k0, v0 = project(where, h1, h1_other, w_qkv, False)
+
+    q0, qkv_first, bundle, dout = join((q0, qkv_first, bundle, dout))
+    qkv_second = along_wide(qkv_first, Z_NEAR)
+    bundle_first = ask(bundle, column)
     dout_other = over_core(dout)
-
-    q0, k0, v0 = project(where, h1, h1_other, w_qkv, False)
     o0, lse0 = self_forward(limit, q0, k0, v0)
+
+    o0, qkv_second, w_up_sent = join((o0, qkv_second, w_up))
+    qkv_y = ordered(qkv_first, qkv_second, near).reshape(3, width, 256)
     q1, k1, v1 = project(where, h1, h1_other, qkv_y, False)
+
+    def away_rows(v):
+        return half_of(v, 1 - core)
+
+    o0_other = over_core(away_rows(o0))
+    q1, bundle_first, w_up_sent, o0_other = join((q1, bundle_first, w_up_sent, o0_other))
+    bundle_second = along_wide(bundle_first, X_PAIRS)
+    up_first = ask(w_up_sent, column)
+    own_wo = over_core(jnp.concatenate([w_out, w_cross_out], axis=0))
+    own_wq = over_core(w_cross_q)
     o1, lse1 = self_forward(limit, q1, k1, v1)
-    rows = frames.shape[0]
-
-    def away_rows(v):
-        return lax.dynamic_slice(v, ((1 - core) * rows, 0), (rows, v.shape[1]))
-
-    o0_other = over_core(away_rows(o0))
     o1_other = over_core(away_rows(o1))
 
-    wo = jnp.concatenate([w_out, out_y], axis=0)
-    wo = (wo, over_core(wo))
-    wq = jnp.stack([w_cross_q, cross_q_y], axis=0)
-    wq = (wq, over_core(wq))
-    wc = jnp.concatenate([w_cross_out, cross_out_y], axis=0)
-    wc = (wc, over_core(wc))
+    o1, bundle_second, up_first, w_down_sent = join((o1, bundle_second, up_first, w_down))
+    up_second = along_wide(up_first, X_PAIRS)
+    down_first = ask(w_down_sent, near)
+    bundle_y = ordered(bundle_first, bundle_second, column)
+    out_y = bundle_y[:256]
+    cross_out_y = bundle_y[256:512]
+    cross_q_y = bundle_y[512:768].reshape(width, 256)
+    cross_kv_y = bundle_y[768:].reshape(2, width, 256)
+    y_wo = over_core(bundle_y[:512])
+    y_wq = over_core(cross_q_y)
+    wo = (w_out, out_y, own_wo[:256], y_wo[:256])
+    wc = (w_cross_out, cross_out_y, own_wo[256:], y_wo[256:])
+    wq = (w_cross_q, cross_q_y, own_wq, y_wq)
     text = lax.dynamic_slice(text_states, (side, 0, 0), (1, *text_states.shape[1:]))[0]
     pair = lower(
         jnp.einsum(
@@ -890,7 +908,6 @@
 
     ck = (spread_heads(pair[:, 0]), spread_heads(pair_other[:, 0]))
     cv = (spread_heads(pair[:, 1]), spread_heads(pair_other[:, 1]))
-
     x1, x2, h2, cq, ca, h3 = middle_forward(
         where, frames, (o0, o1), (o0_other, o1_other), norm_gain, norm_bias, wo, wq, ck, cv, wc
     )
@@ -898,87 +915,183 @@
     h2_other = over_core(h2)
     ca_other = over_core(ca[:, 512:])
 
-    up = (w_up, up_y)
-    down = (w_down, down_y)
-    g0m, g1m, du0m, du1m, outm, ym = feed(where, h3, dout, up, down, FULL)
-    g0o, g1o, du0o, du1o, outo, yo = feed(where, h3_other, dout_other, up, down, ROUND)
-    y_received = over_core(yo)
-    out_received = over_core(outo)
-
-    def rows_sum(left_mine, right_mine, left_other, right_other):
-        return tn(left_mine, right_mine) + tn(left_other, right_other)
-
-    grad_up = reduced(
-        rows_sum(h3, du0m, h3_other, du0o), rows_sum(h3, du1m, h3_other, du1o)
-    )
-    grad_down = reduced(
-        rows_sum(g0m, dout, g0o, dout_other), rows_sum(g1m, dout, g1o, dout_other)
-    )
-
+    h3, up_second, down_first = join((h3, up_second, down_first))
+    down_second = along_wide(down_first, Z_NEAR)
+    up_y = ordered(up_first, up_second, column)
+    g0, du0, out_m, y_m = feed(where, h3, dout, w_up, w_down, FULL)
+    g0, du0, out_o, y_o = feed(
+        where, h3_other, dout_other, w_up, w_down, FULL, shared=(g0, du0)
+    )
+    y_o, down_second = join((y_o, down_second))
+    down_y = ordered(down_first, down_second, near)
+    h3_rows = jnp.concatenate([h3, h3_other], axis=0)
+    dout_rows = jnp.concatenate([dout, dout_other], axis=0)
+    g1, du1, out_m, y_m = feed(where, h3, dout, up_y, down_y, FULL, before=(out_m, y_m))
+    g1, du1, out_o, y_o = feed(
+        where, h3_other, dout_other, up_y, down_y, ROUND, before=(out_o, y_o), shared=(g1, du1)
+    )
+    y_received = over_core(y_o)
+
+    def plus(a, b):
+        return lower(a.astype(FULL) + b.astype(FULL))
+
+    def x_send(own, received):
+        away_half = lower(half_of(own, 1 - column) + half_of(received, 1 - column).astype(FULL))
+        return along_wide(away_half, X_PAIRS)
+
+    def x_sum(own, received, over_x):
+        return plus(half_of(own, column) + half_of(received, column).astype(FULL), over_x)
+
+    def z_first(total):
+        return along_wide(total, Z_INWARD)
+
+    def z_second(total):
+        return along_wide(total, Z_MIDDLE)
+
+    def z_third(total):
+        return along_wide(total, Z_OUTWARD)
+
+    def z_pick(total, outer):
+        return jnp.where((layer == 1) | (layer == 2), total, outer)
+
+    def finish(mine, over_x):
+        return ordered(mine, over_x, column).astype(FULL)
+
+    up1 = lower(tn(h3_rows, du1))
+    up1, g1 = join((up1, g1))
+    up_y_got = over_y(up1)
+    down1 = lower(tn(g1, dout_rows))
+    up0 = tn(h3_rows, du0)
+    down0 = tn(g0, dout_rows)
     dx1, dself, dcross, dcq, dck, dcv, sums = middle_back(
-        where, ym, y_received, x1, x2, dout, cq, norm_gain, wq, ck, cv, wc
-    )
-    out_rows = lower(x2 + outm + out_received.astype(FULL))
+        where, y_m, y_received, x1, x2, dout, cq, norm_gain, wq, ck, cv, wc
+    )
+    dself, up_y_got, down1, up0, down0 = join((dself, up_y_got, down1, up0, down0))
+
+    down_y_got = over_y(down1)
+    up_x = x_send(up0, up_y_got)
     dself_other = over_core(dself)
     dcross_other = over_core(dcross)
     dcq_other = over_core(dcq[:, 512:])
     d_pair = jnp.stack([dck, dcv], axis=1)
     d_pair = lower(d_pair[:2] + over_core(d_pair[2:]))
-
     do0, do1 = project(where, dself, dself_other, jnp.stack([w_out, out_y]), True)
-    dself_rows = in_order(dself, dself_other)
-    h1_rows = in_order(h1, h1_other)
-
-    def cross_term(g):
+    grads1 = self_back(limit, q1, k1, v1, o1, do1, lse1)
+    h1_rows = ordered(h1, h1_other, core)
+    qkv1 = lower(jnp.concatenate([tn(h1_rows, g) for g in grads1], axis=0))
+    dself_rows = ordered(dself, dself_other, core)
+    dcross_rows = jnp.concatenate([dcross, dcross_other], axis=0)
+    h2_rows = jnp.concatenate([h2, h2_other], axis=0)
+
+    def both(mine, other, g):
         lanes = slice(g * 256, (g + 1) * 256)
-        return (
-            rows_sum(ca[:, lanes], dcross, ca_other[:, lanes], dcross_other),
-            jnp.concatenate(
-                [
-                    rows_sum(h2, dcq[:, lanes], h2_other, dcq_other[:, lanes]),
-                    tn(text, d_pair[g, 0]),
-                    tn(text, d_pair[g, 1]),
-                ],
-                axis=0,
-            ),
+        return jnp.concatenate([mine[:, lanes], other[:, lanes]], axis=0)
+
+    def into(g):
+        return jnp.concatenate(
+            [tn(h2_rows, both(dcq, dcq_other, g)), tn(text, d_pair[g, 0]), tn(text, d_pair[g, 1])],
+            axis=0,
         )
 
-    term0 = cross_term(0)
-    term1 = cross_term(1)
-    grad_cross_out = reduced(term0[0], term1[0])
-    grad_cross_in = reduced(term0[1], term1[1])
-    width = frames.shape[1]
-    grad_cross_q = grad_cross_in[:width]
-    grad_cross_kv = grad_cross_in[width:].reshape(2, width, 256)
-    grad_out = reduced(tn(o0, dself_rows), tn(o1, dself_rows))
-
+    def outof(g, o):
+        return jnp.concatenate(
+            [tn(o, dself_rows), tn(both(ca, ca_other, g), dcross_rows)], axis=0
+        )
+
+    into1 = lower(into(1))
+    outof1 = lower(outof(1, o1))
+    qkv1, into1, outof1, down_y_got, up_x, do0 = join((qkv1, into1, outof1, down_y_got, up_x, do0))
+
+    qkv_y_got = over_y(qkv1)
+    down_x = x_send(down0, down_y_got)
+    up_sum = x_sum(up0, up_y_got, up_x)
+    up_z = z_first(up_sum)
+    grads0 = self_back(limit, q0, k0, v0, o0, do0, lse0)
+    yo = first_back(away, (*grads0, *grads1), (w_qkv, qkv_y), ROUND)
+    y_received = over_core(yo)
+    qkv0 = jnp.concatenate([tn(h1_rows, g) for g in grads0], axis=0)
+    qkv0, yo, qkv_y_got, down_x, up_z, into1 = join((qkv0, yo, qkv_y_got, down_x, up_z, into1))
+
+    into_y_got = over_y(into1)
+    qkv_x = x_send(qkv0, qkv_y_got)
+    down_sum = x_sum(down0, down_y_got, down_x)
+    down_z = z_first(down_sum)
+    up_sum = plus(up_sum, up_z)
+    up_z = z_second(up_sum)
+    ym = first_back(where, (*grads0, *grads1), (w_qkv, qkv_y), FULL)
+    grad_frames, first_sums = frames_back(where, ym, y_received, dx1, frames, norm_gain)
+    out_rows = lower(x2 + out_m + over_core(out_o).astype(FULL))
+    into0 = into(0)
+    outof0 = outof(0, o0)
     text_part = 0.0
     for g, weights in ((0, w_cross_kv), (1, cross_kv_y)):
         for c in range(2):
             text_part = text_part + nt(d_pair[g, c], weights[c])
     text_grad = lower(text_part + over_core(text_part))
     text_away = over_y(text_grad)
-    grad_text = jnp.where(
-        side == 0, jnp.stack([text_grad, text_away]), jnp.stack([text_away, text_grad])
-    )
-
-    grads1 = self_back(limit, q1, k1, v1, o1, do1, lse1)
-    term1 = jnp.concatenate([tn(h1_rows, g) for g in grads1], axis=0)
-    grads0 = self_back(limit, q0, k0, v0, o0, do0, lse0)
-    term0 = jnp.concatenate([tn(h1_rows, g) for g in grads0], axis=0)
-    grad_qkv = reduced(term0, term1).reshape(3, width, 256)
-
-    yo = first_back(away, (*grads0, *grads1), (w_qkv, qkv_y), ROUND)
-    y_received = over_core(yo)
-    ym = first_back(where, (*grads0, *grads1), (w_qkv, qkv_y), FULL)
-    grad_frames, first_sums = frames_back(where, ym, y_received, dx1, frames, norm_gain)
-
+    grad_text = ordered(text_grad[None], text_away[None], side)
     sums = sums + first_sums
     sums = sums + over_core(sums)
     sums = sums + over_y(sums)
+    into_y_got, qkv_x, down_z, up_z, outof1, into0, outof0, grad_frames = join(
+        (into_y_got, qkv_x, down_z, up_z, outof1, into0, outof0, grad_frames)
+    )
+
+    outof_y_got = over_y(outof1)
+    into_x = x_send(into0, into_y_got)
+    qkv_sum = x_sum(qkv0, qkv_y_got, qkv_x)
+    qkv_z = z_first(qkv_sum)
+    down_sum = plus(down_sum, down_z)
+    down_z = z_second(down_sum)
+    up_sum = plus(up_sum, up_z)
+    up_z = z_third(up_sum)
     sums = sums + along_wide(sums, X_PAIRS)
     sums = sums + along_wide(sums, Z_NEAR)
     sums = sums + along_wide(sums, Z_FAR)
+    outof_y_got, into_x, qkv_z, down_z, up_z = join((outof_y_got, into_x, qkv_z, down_z, up_z))
+
+    outof_x = x_send(outof0, outof_y_got)
+    into_sum = x_sum(into0, into_y_got, into_x)
+    into_z = z_first(into_sum)
+    qkv_sum = plus(qkv_sum, qkv_z)
+    qkv_z = z_second(qkv_sum)
+    down_sum = plus(down_sum, down_z)
+    down_z = z_third(down_sum)
+    up_sum = z_pick(up_sum, up_z)
+    up_x = along_wide(up_sum, X_PAIRS)
+    outof_x, into_z, qkv_z, down_z, up_x = join((outof_x, into_z, qkv_z, down_z, up_x))
+
+    outof_sum = x_sum(outof0, outof_y_got, outof_x)
+    outof_z = z_first(outof_sum)
+    into_sum = plus(into_sum, into_z)
+    into_z = z_second(into_sum)
+    qkv_sum = plus(qkv_sum, qkv_z)
+    qkv_z = z_third(qkv_sum)
+    down_sum = z_pick(down_sum, down_z)
+    down_x = along_wide(down_sum, X_PAIRS)
+    outof_z, into_z, qkv_z, down_x = join((outof_z, into_z, qkv_z, down_x))
+
+    outof_sum = plus(outof_sum, outof_z)
+    outof_z = z_second(outof_sum)
+    into_sum = plus(into_sum, into_z)
+    into_z = z_third(into_sum)
+    qkv_sum = z_pick(qkv_sum, qkv_z)
+    qkv_x = along_wide(qkv_sum, X_PAIRS)
+    grad_up = finish(up_sum, up_x)
+    outof_z, into_z, qkv_x, grad_up = join((outof_z, into_z, qkv_x, grad_up))
+
+    outof_sum = plus(outof_sum, outof_z)
+    outof_z = z_third(outof_sum)
+    into_sum = z_pick(into_sum, into_z)
+    into_x = along_wide(into_sum, X_PAIRS)
+    grad_down = finish(down_sum, down_x)
+    outof_z, into_x, grad_down = join((outof_z, into_x, grad_down))
+
+    outof_sum = z_pick(outof_sum, outof_z)
+    outof_x = along_wide(outof_sum, X_PAIRS)
+    grad_qkv = finish(qkv_sum, qkv_x).reshape(3, width, 256)
+    grad_cross_in = finish(into_sum, into_x)
+    grad_outs = finish(outof_sum, outof_x)
     return (
         out_rows,
         grad_frames,
@@ -986,10 +1099,10 @@
         sums[0:6:2],
         sums[1:6:2],
         grad_qkv,
-        grad_out,
-        grad_cross_q,
-        grad_cross_kv,
-        grad_cross_out,
+        grad_outs[:256],
+        grad_cross_in[:width],
+        grad_cross_in[width:].reshape(2, width, 256),
+        grad_outs[256:],
         grad_up,
         grad_down,
     )

time: 889 us -> 564 us (0.63)
  waiting for transfers between devices: 466 us -> 102 us
  local copies, waits for them, and re-layouts: 10.7 us -> 49.8 us
  matrix products: 80 us -> 48.2 us
  other arithmetic: 67.3 us -> 89.3 us
  Pallas kernels: 186 us -> 195 us
    ppermute x27 -> x32, waiting for transfers between devices: 329 us -> 78.7 us  [along_wide(): return lax.ppermute(v, 'wide', pairs)]
    ppermute x15 -> x11, waiting for transfers between devices: 135 us -> 20.5 us  [over_y(): return lax.ppermute(v, 'narrow', Y_PAIRS)]
    dot_general x28 -> x20, matrix products: 72.4 us -> 43.8 us  [tn(): lax.dot_general(a, b, (((0,), (0,)), ((), ())), preferred_element_type=FULL)]
    select_n x3 -> x12, other arithmetic: 5.07 us -> 23.6 us  [the longest x7 17.5 us: ordered(): jnp.where(which == 0, jnp.concatenate([first, second], axis=0), jnp.conca...]
    slice x2 -> x11, local copies, waits for them, and re-layouts: 2.49 us -> 14.6 us  [the longest x2 4.11 us: chip_local(): wc = (w_cross_out, cross_out_y, own_wo[256:], y_wo[256:])]
    unnamed x110 -> x228, local copies, waits for them, and re-layouts: 3.96 us -> 15.3 us
    ppermute x27 -> x32, starting transfers between devices: 47.6 us -> 57 us  [along_wide(): return lax.ppermute(v, 'wide', pairs)]
    ppermute x15 -> x11, starting transfers between devices: 19.8 us -> 12 us  [over_y(): return lax.ppermute(v, 'narrow', Y_PAIRS)]
  transfers between devices with their start and end apart: 62 -> 64, of which waited for: 24 -> 21; matrix products, arithmetic and copies ran while one was open for 17% -> 29% of each run, Pallas kernels for 21% -> 35%
where the time goes in v2:
time: 564 us; the launch traced here: 559 us
  Pallas kernels  195 us (35%)
  waiting for transfers between devices  102 us (18%)
  other arithmetic  89.3 us (16%)
  starting transfers between devices  73.1 us (13%)
  local copies, waits for them, and re-layouts  49.8 us (9%)
  matrix products  48.2 us (9%)
    ppermute x32, waiting for transfers between devices, along_wide(): return lax.ppermute(v, 'wide', pairs)  78.7 us
    ppermute x32, starting transfers between devices, along_wide(): return lax.ppermute(v, 'wide', pairs)  57 us
    pallas_call x4, Pallas kernels, feed(): pl.pallas_call(functools.partial(feed_kernel, carried=carried, shared=1 i...  54.3 us
    dot_general x20, matrix products, tn(): lax.dot_general(a, b, (((0,), (0,)), ((), ())), preferred_element_type=FULL)  43.8 us
    pallas_call x2, Pallas kernels, self_back(): pl.pallas_call(functools.partial(self_back_kernel, span=span, floor=floor...  40.1 us
    convert_element_type x24, other arithmetic, lower(): return values_in.astype(jnp.bfloat16)  38.2 us
    pallas_call x2, Pallas kernels, self_forward(): pl.pallas_call(functools.partial(self_forward_kernel, span=span, floor=fl...  31.1 us
    pallas_call x1, Pallas kernels, middle_back(): pl.pallas_call(middle_back_kernel, grid_spec=pltpu.PrefetchScalarGridSpec...  22.1 us
  transfers between devices with their start and end apart: 64, of which 21 were waited for; matrix products, arithmetic and copies ran while one was open for 29% of the time, Pallas kernels for 35%

profile of v2, /device:TPU:0, one launch (start us, length us, event | category | flops | bytes accessed | tf_op | source)
XLA Modules:
  0.0 559.4 jit_solution(15989524414550792071)
XLA Ops:
  6.6 2.5 collective-permute-start.1
  11.8 2.7 reshape.121
  18.0 2.8 fusion.73
  20.8 5.0 project.3
  31.1 15.6 %self_forward.2 = (bf16[1664,256]{1,0:T(8,128)(2,1)S(1)}, f32[2,8,1664]{2,1,0:T(8,128)S(1)}) custom-call(s32[1]{0:T(128)} %dynamic_slice.84.limit_ref, bf16[1664,256]{1,0:T(8,128)(2,1)S(1)} %get-tuple-element.129.q_ref, bf16[1664,256]{1,0:T(8,128)(2,1)S(1)} %get-tuple-element.130.k_ref, bf16[1664,256]{1,0:T(8,128)(2,1)S(1)} %get-tuple-element.131.v_ref), custom_call_target="tpu_custom_call" | custom-call | flops 16000000000 | bytes 4000000 | tf_op jit(solution)/shard_map/self_forward/pallas_call | solution.py:455
  46.9 4.9 maximum_select_fusion
  54.3 6.2 %project.4 = (bf16[1664,256]{1,0:T(8,128)(2,1)S(1)}, bf16[1664,256]{1,0:T(8,128)(2,1)S(1)}, bf16[1664,256]{1,0:T(8,128)(2,1)S(1)}) custom-call(s32[1]{0:T(128)} %bitcast.where_ref, bf16[832,1024]{1,0:T(8,128)(2,1)} %fusion.5.mine_ref, bf16[832,1024]{1,0:T(8,128)(2,1)} %collective-permute-done.other_ref, bf16[3,1024,256]{2,1,0:T(8,128)(2,1)S(1)} %bitcast.100), custom_call_target="tpu_custom_call" | custom-call | flops 2617245696 | bytes 8000000 | tf_op jit(solution)/shard_map/project/pallas_call | solution.py:391
  62.9 15.6 %self_forward.3 = (bf16[1664,256]{1,0:T(8,128)(2,1)S(1)}, f32[2,8,1664]{2,1,0:T(8,128)S(1)}) custom-call(s32[1]{0:T(128)} %dynamic_slice.84.limit_ref, bf16[1664,256]{1,0:T(8,128)(2,1)S(1)} %get-tuple-element.139.q_ref, bf16[1664,256]{1,0:T(8,128)(2,1)S(1)} %get-tuple-element.140.k_ref, bf16[1664,256]{1,0:T(8,128)(2,1)S(1)} %get-tuple-element.141.v_ref), custom_call_target="tpu_custom_call" | custom-call | flops 16000000000 | bytes 4000000 | tf_op jit(solution)/shard_map/self_forward/pallas_call | solution.py:455
  81.2 5.8 %collective-permute-done.6 = bf16[512,1024]{1,0:T(8,128)(2,1)S(1)} collective-permute-done((bf16[512,1024]{1,0:T(8,128)(2,1)S(1)}, bf16[512,1024]{1,0:T(8,128)(2,1)S(1)}, u32[]{:S(2)}, u32[]{:S(2)}) %collective-permute-start.6) | collective-permute-done | bytes 1048608 | tf_op jit(solution)/shard_map/ppermute | solution.py:830
  88.0 3.3 collective-permute-done.5
  97.5 2.2 reshape.122.refs_5_.refs_1_
  100.1 2.6 stack_reshape.3
  102.8 2.2 fusion.16
  110.1 20.7 %middle_forward.1 = (f32[832,1024]{1,0:T(8,128)}, f32[832,1024]{1,0:T(8,128)}, bf16[832,1024]{1,0:T(8,128)(2,1)S(1)}, bf16[832,1024]{1,0:T(8,128)(2,1)S(1)}, bf1...) custom-call(s32[1]{0:T(128)} %bitcast.where_ref, bf16[832,1024]{1,0:T(8,128)(2,1)} %frame_ref.3, ...), custom_call_target="tpu_custom_call" | custom-call | flops 7000000000 | bytes 25000000 | tf_op jit(solution)/shard_map/middle_forward/pallas_call | solution.py:604
  134.6 2.3 maximum_select_fusion.3.up_ref
  139.6 13.1 %feed.4 = (bf16[1664,1024]{1,0:T(8,128)(2,1)}, bf16[1664,1024]{1,0:T(8,128)(2,1)}, f32[832,1024]{1,0:T(8,128)}, f32[832,1024]{1,0:T(8,128)}) custom-call(s32[1]{0:T(128)} %bitcast.where_ref, bf16[832,1024]{1,0:T(8,128)(2,1)} %get-tuple-element.152.h_ref, bf16[832,1024]{1,0:T(8,128)(2,1)} %copy-done.7, bf16[1024,1024]{1,0:T(8,128)(2,1)} %up_ref.3, ...), custom_call_target="tpu_custom_call" | custom-call | flops 6979321856 | bytes 20000000 | tf_op jit(solution)/shard_map/feed/pallas_call | solution.py:649
  154.1 2.1 fusion.74
  156.1 13.2 %feed.5 = (bf16[1664,1024]{1,0:T(8,128)(2,1)}, bf16[1664,1024]{1,0:T(8,128)(2,1)}, f32[832,1024]{1,0:T(8,128)}, f32[832,1024]{1,0:T(8,128)}) custom-call(s32[1]{0:T(128)} %bitcast.where_ref, bf16[832,1024]{1,0:T(8,128)(2,1)} %collective-permute-done.15.h_ref, bf16[832,1024]{1,0:T(8,128)(2,1)} %copy-done.83, ...), custom_call_target="tpu_custom_call", output_to_operand_aliasing={{0}: (5, {}), {1}: (6, {})} | custom-call | flops 6979321856 | bytes 20000000 | tf_op jit(solution)/shard_map/feed/pallas_call | solution.py:649
  169.3 4.6 maximum_select_fusion.4.down_ref
  173.9 14.4 %feed.6 = (bf16[1664,1024]{1,0:T(8,128)(2,1)}, bf16[1664,1024]{1,0:T(8,128)(2,1)}, f32[832,1024]{1,0:T(8,128)}, f32[832,1024]{1,0:T(8,128)}) custom-call(s32[1]{0:T(128)} %bitcast.where_ref, bf16[832,1024]{1,0:T(8,128)(2,1)} %get-tuple-element.152.h_ref, bf16[832,1024]{1,0:T(8,128)(2,1)} %copy-done.7, bf16[1024,1024]{1,0:T(8,128)(2,1)} %maximum_select_fusion.3.up_ref, ...), custom_call_target="tpu_custom_call" | custom-call | flops 6979321856 | bytes 20000000 | tf_op jit(solution)/shard_map/feed/pallas_call | solution.py:649
  188.2 13.7 %feed.7 = (bf16[1664,1024]{1,0:T(8,128)(2,1)}, bf16[1664,1024]{1,0:T(8,128)(2,1)}, bf16[832,1024]{1,0:T(8,128)(2,1)}, bf16[832,1024]{1,0:T(8,128)(2,1)}) custom-call(s32[1]{0:T(128)} %bitcast.where_ref, bf16[832,1024]{1,0:T(8,128)(2,1)} %collective-permute-done.15.h_ref, bf16[832,1024]{1,0:T(8,128)(2,1)} %copy-done.83, ...), custom_call_target="tpu_custom_call", output_to_operand_aliasing={{0}: (7, {}), {1}: (8, {})} | custom-call | flops 6979321856 | bytes 20000000 | tf_op jit(solution)/shard_map/feed/pallas_call | solution.py:649
  202.0 3.0 constant_dynamic-update-slice_fusion
  205.0 7.3 %convolution_convert_fusion.1 = bf16[1024,1024]{1,0:T(8,128)(2,1)} fusion(bf16[1664,1024]{1,0:T(8,128)(2,1)} %constant_dynamic-update-slice_fusion, bf16[1664,1024]{1,0:T(8,128)(2,1)S(1)} %copy-done.111), kind=kOutput, calls=%fused_computation.35 | convolution fusion | flops 3490709504 | bytes 8912896 | tf_op jit(solution)/shard_map/dot_general | solution.py:328
  213.1 4.2 fusion.76
  218.7 2.6 copy-done.96
  221.4 5.2 convolution_convert_fusion
  226.6 5.7 %fusion.77 = f32[1024,1024]{1,0:T(8,128)} fusion(bf16[1664,1024]{1,0:T(8,128)(2,1)S(1)} %copy-done.108, bf16[1664,1024]{1,0:T(8,128)(2,1)S(1)} %copy-done.96), kind=kOutput, calls=%fused_computation.175 | convolution fusion | flops 3489660928 | bytes 11010048 | tf_op jit(solution)/shard_map/dot_general | solution.py:328
  232.4 22.1 %middle_back.1 = (f32[832,1024]{1,0:T(8,128)}, bf16[832,1024]{1,0:T(8,128)(2,1)S(1)}, bf16[832,1024]{1,0:T(8,128)(2,1)S(1)}, bf16[832,1024]{1,0:T(8,128)(2,1)S(1...) custom-call(s32[1]{0:T(128)} %bitcast.where_ref, ...), custom_call_target="tpu_custom_call" | custom-call | flops 7000000000 | bytes 25000000 | tf_op jit(solution)/shard_map/middle_back/pallas_call | solution.py:729
  257.6 3.2 collective-permute-done.20
  261.6 2.5 add_convert_fusion.8
  264.8 3.1 convolution_convert_fusion.4
  269.2 3.1 fusion.26
  275.3 2.1 fusion.30
  278.6 2.2 project.5
  282.7 20.3 %self_back.2 = (bf16[1664,256]{1,0:T(8,128)(2,1)S(1)}, bf16[1664,256]{1,0:T(8,128)(2,1)S(1)}, bf16[1664,256]{1,0:T(8,128)(2,1)S(1)}) custom-call(s32[1]{0:T(128)} %dynamic_slice.84.limit_ref, bf16[1664,256]{1,0:T(8,128)(2,1)S(1)} %copy-done.56, bf16[1664,256]{1,0:T(8,128)(2,1)S(1)} %copy-done.58, bf16[1664,256]{1,0:T(8,128)(2,1)S(1)} %copy-done.60, ...), custom_call_target="tpu_custom_call" | custom-call | flops 20000000000 | bytes 6000000 | tf_op jit(solution)/shard_map/self_back/pallas_call | solution.py:536
  312.0 2.5 add_convert_fusion.7
  316.1 2.1 add_convert_fusion.6
  318.3 3.5 collective-permute-start.31
  321.8 19.8 %self_back.3 = (bf16[1664,256]{1,0:T(8,128)(2,1)S(1)}, bf16[1664,256]{1,0:T(8,128)(2,1)S(1)}, bf16[1664,256]{1,0:T(8,128)(2,1)S(1)}) custom-call(s32[1]{0:T(128)} %dynamic_slice.84.limit_ref, bf16[1664,256]{1,0:T(8,128)(2,1)S(1)} %copy-done.50, bf16[1664,256]{1,0:T(8,128)(2,1)S(1)} %copy-done.52, bf16[1664,256]{1,0:T(8,128)(2,1)S(1)} %copy-done.54, ...), custom_call_target="tpu_custom_call" | custom-call | flops 20000000000 | bytes 6000000 | tf_op jit(solution)/shard_map/self_back/pallas_call | solution.py:536
  341.7 4.7 first_back.2
  361.4 2.1 fusion.34
  365.1 4.4 first_back.3.ym_ref
  369.6 3.7 frames_back.1
  373.3 7.1 %collective-permute-done.33 = bf16[1536,256]{1,0:T(8,128)(2,1)S(1)} collective-permute-done((bf16[1536,256]{1,0:T(8,128)(2,1)S(1)}, bf16[1536,256]{1,0:T(8,128)(2,1)S(1)}, u32[]{:S(2)}, u32[]{:S(2)}) %collective-permute-start.33) | collective-permute-done | bytes 786464 | tf_op jit(solution)/shard_map/ppermute | solution.py:833
  380.4 8.1 %collective-permute-done.32 = bf16[3072,256]{1,0:T(8,128)(2,1)S(1)} collective-permute-done((bf16[3072,256]{1,0:T(8,128)(2,1)S(1)}, bf16[3072,256]{1,0:T(8,128)(2,1)S(1)}, u32[]{:S(2)}, u32[]{:S(2)}) %collective-permute-start.32) | collective-permute-done | bytes 1572896 | tf_op jit(solution)/shard_map/ppermute | solution.py:830
  397.3 5.6 %collective-permute-start.46 = (bf16[1536,256]{1,0:T(8,128)(2,1)S(1)}, bf16[1536,256]{1,0:T(8,128)(2,1)S(1)}, u32[]{:S(2)}, u32[]{:S(2)}) collective-permute-start(bf16[1536,256]{1,0:T(8,128)(2,1)S(1)} %add_convert_fusion.15), channel_id=1, source_target_pairs={{0,8},{4,12},{24,16},{28,20},{1,9},{5,13},{25,17},{29,21},{2,10},{... | collective-permute-start | bytes 2359304 | tf_op jit(solution)/shard_map/ppermute | solution.py:833
  403.0 6.6 %collective-permute-done.45 = bf16[1536,256]{1,0:T(8,128)(2,1)} collective-permute-done((bf16[1536,256]{1,0:T(8,128)(2,1)}, bf16[1536,256]{1,0:T(8,128)(2,1)}, u32[]{:S(2)}, u32[]{:S(2)}) %collective-permute-start.45) | collective-permute-done | bytes 786464 | tf_op jit(solution)/shard_map/ppermute | solution.py:833
  409.6 9.2 %collective-permute-done.46 = bf16[1536,256]{1,0:T(8,128)(2,1)S(1)} collective-permute-done((bf16[1536,256]{1,0:T(8,128)(2,1)S(1)}, bf16[1536,256]{1,0:T(8,128)(2,1)S(1)}, u32[]{:S(2)}, u32[]{:S(2)}) %collective-permute-start.46) | collective-permute-done | bytes 786464 | tf_op jit(solution)/shard_map/ppermute | solution.py:833
  418.7 2.3 collective-permute-done.48
  421.0 3.0 add_convert_fusion.12
  424.0 3.3 collective-permute-start.50
  427.3 2.6 add_convert_fusion.1
  431.5 2.3 broadcast_select_fusion.2
  435.1 2.2 add_convert_fusion.13
  444.7 23.3 %collective-permute-done.49 = bf16[256,1024]{1,0:T(8,128)(2,1)} collective-permute-done((bf16[256,1024]{1,0:T(8,128)(2,1)}, bf16[256,1024]{1,0:T(8,128)(2,1)}, u32[]{:S(2)}, u32[]{:S(2)}) %collective-permute-start.49) | collective-permute-done | bytes 524320 | tf_op jit(solution)/shard_map/ppermute | solution.py:833
  477.7 8.5 %collective-permute-start.54 = (bf16[256,1024]{1,0:T(8,128)(2,1)S(1)}, bf16[256,1024]{1,0:T(8,128)(2,1)S(1)}, u32[]{:S(2)}, u32[]{:S(2)}) collective-permute-start(bf16[256,1024]{1,0:T(8,128)(2,1)S(1)} %add_convert_fusion.19), channel_id=1, source_target_pairs={{0,8},{4,12},{24,16},{28,20},{1,9},{5,13},{25,17},{29,21},{2,10},{... | collective-permute-start | bytes 1572872 | tf_op jit(solution)/shard_map/ppermute | solution.py:833
  488.2 5.2 collective-permute-done.54
  501.0 15.2 %collective-permute-done.41 = f32[8,1024]{1,0:T(8,128)S(1)} collective-permute-done((f32[8,1024]{1,0:T(8,128)S(1)}, f32[8,1024]{1,0:T(8,128)S(1)}, u32[]{:S(2)}, u32[]{:S(2)}) %collective-permute-start.41) | collective-permute-done | bytes 32800 | tf_op jit(solution)/shard_map/ppermute | solution.py:833
  517.4 5.4 fusion.10
  522.8 3.5 collective-permute-start.42
  531.1 3.9 add_convert_fusion
  534.9 2.1 collective-permute-start.43
  537.8 2.1 collective-permute-done.43
  541.2 4.4 fusion.11
  (437 shorter events, 145.6 us)
Async XLA Ops:
  5.2 15.6 %collective-permute-start = (bf16[832,1024]{1,0:T(8,128)(2,1)}, bf16[832,1024]{1,0:T(8,128)(2,1)}, u32[]{:S(2)}, u32[]{:S(2)}) collective-permute-start(bf16[832,1024]{1,0:T(8,128)(2,1)} %fusion.5.mine_ref), channel_id=1, source_target_pairs={{0,1},{1,0},{2,3},{3,2},{4,5},{5,4},{6,7},{7,6},{8,9},{9,8},{10,11... | collective-permute-start | bytes 5111816 | tf_op jit(solution)/shard_map/ppermute | solution.py:827
  6.6 21.0 %collective-permute-start.1 = (bf16[1536,256]{1,0:T(8,128)(2,1)}, bf16[1536,256]{1,0:T(8,128)(2,1)}, u32[]{:S(2)}, u32[]{:S(2)}) collective-permute-start(bf16[1536,256]{1,0:T(8,128)(2,1)} %constant_dynamic-slice_fusion.5), channel_id=1, source_target_pairs={{0,2},{2,0},{1,3},{3,1},{4,6},{6,4},{5,7},{7,5},{8,10},{10,8},{9,1... | collective-permute-start | bytes 2359304 | tf_op jit(solution)/shard_map/ppermute | solution.py:830
  10.2 7.8 %collective-permute-start.8 = (bf16[512,1024]{1,0:T(8,128)(2,1)}, bf16[512,1024]{1,0:T(8,128)(2,1)}, u32[]{:S(2)}, u32[]{:S(2)}) collective-permute-start(bf16[512,1024]{1,0:T(8,128)(2,1)} %pad_maximum_fusion.6), channel_id=1, source_target_pairs={{0,1},{1,0},{2,3},{3,2},{4,5},{5,4},{6,7},{7,6},{8,9},{9,8},{10,11... | collective-permute-start | bytes 3145736 | tf_op jit(solution)/shard_map/ppermute | solution.py:827
  10.4 99.5 %collective-permute-start.10 = (bf16[1024,256]{1,0:T(8,128)(2,1)S(1)}, bf16[1024,256]{1,0:T(8,128)(2,1)}, u32[]{:S(2)}, u32[]{:S(2)}) collective-permute-start(bf16[1024,256]{1,0:T(8,128)(2,1)S(1)} %copy-done.12), channel_id=1, source_target_pairs={{0,1},{1,0},{2,3},{3,2},{4,5},{5,4},{6,7},{7,6},{8,9},{9,8},{10,11... | collective-permute-start | bytes 1572872 | tf_op jit(solution)/shard_map/ppermute | solution.py:827
  27.7 24.1 %collective-permute-start.2 = (bf16[1536,256]{1,0:T(8,128)(2,1)}, bf16[1536,256]{1,0:T(8,128)(2,1)S(1)}, u32[]{:S(2)}, u32[]{:S(2)}) collective-permute-start(bf16[1536,256]{1,0:T(8,128)(2,1)} %collective-permute-done.1), channel_id=1, source_target_pairs={{0,8},{4,12},{8,0},{12,4},{16,24},{20,28},{24,16},{28,20},{1,9},{5... | collective-permute-start | bytes 2359304 | tf_op jit(solution)/shard_map/ppermute | solution.py:833
  29.6 31.0 %collective-permute-start.3 = (bf16[640,1024]{1,0:T(8,128)(2,1)S(1)}, bf16[640,1024]{1,0:T(8,128)(2,1)S(1)}, u32[]{:S(2)}, u32[]{:S(2)}) collective-permute-start(bf16[640,1024]{1,0:T(8,128)(2,1)S(1)} %constant_dynamic-slice_fusion.4), channel_id=1, source_target_pairs={{0,2},{2,0},{1,3},{3,1},{4,6},{6,4},{5,7},{7,5},{8,10},{10,8},{9,1... | collective-permute-start | bytes 3932168 | tf_op jit(solution)/shard_map/ppermute | solution.py:830
  31.1 63.1 %collective-permute-start.16 = (bf16[832,1024]{1,0:T(8,128)(2,1)S(1)}, bf16[832,1024]{1,0:T(8,128)(2,1)S(1)}, u32[]{:S(2)}, u32[]{:S(2)}) collective-permute-start(bf16[832,1024]{1,0:T(8,128)(2,1)S(1)} %broadcast_select_fusion.d_ref), channel_id=1, source_target_pairs={{0,1},{1,0},{2,3},{3,2},{4,5},{5,4},{6,7},{7,6},{8,9},{9,8},{10,11... | collective-permute-start | bytes 5111816 | tf_op jit(solution)/shard_map/ppermute | solution.py:827
  51.8 8.7 %collective-permute-start.4 = (bf16[832,256]{1,0:T(8,128)(2,1)S(1)}, bf16[832,256]{1,0:T(8,128)(2,1)S(1)}, u32[]{:S(2)}, u32[]{:S(2)}) collective-permute-start(bf16[832,256]{1,0:T(8,128)(2,1)S(1)} %constant_dynamic-slice_fusion.3), channel_id=1, source_target_pairs={{0,1},{1,0},{2,3},{3,2},{4,5},{5,4},{6,7},{7,6},{8,9},{9,8},{10,11... | collective-permute-start | bytes 1277960 | tf_op jit(solution)/shard_map/ppermute | solution.py:827
  60.5 30.8 %collective-permute-start.5 = (bf16[640,1024]{1,0:T(8,128)(2,1)S(1)}, bf16[640,1024]{1,0:T(8,128)(2,1)S(1)}, u32[]{:S(2)}, u32[]{:S(2)}) collective-permute-start(bf16[640,1024]{1,0:T(8,128)(2,1)S(1)} %collective-permute-done.3), channel_id=1, source_target_pairs={{0,4},{4,0},{8,12},{12,8},{16,20},{20,16},{24,28},{28,24},{1,5},{5... | collective-permute-start | bytes 3932168 | tf_op jit(solution)/shard_map/ppermute | solution.py:833
  62.1 24.9 %collective-permute-start.6 = (bf16[512,1024]{1,0:T(8,128)(2,1)S(1)}, bf16[512,1024]{1,0:T(8,128)(2,1)S(1)}, u32[]{:S(2)}, u32[]{:S(2)}) collective-permute-start(bf16[512,1024]{1,0:T(8,128)(2,1)S(1)} %constant_dynamic-slice_fusion.2), channel_id=1, source_target_pairs={{0,2},{2,0},{1,3},{3,1},{4,6},{6,4},{5,7},{7,5},{8,10},{10,8},{9,1... | collective-permute-start | bytes 3145736 | tf_op jit(solution)/shard_map/ppermute | solution.py:830
  81.2 28.8 %collective-permute-start.7 = (bf16[832,256]{1,0:T(8,128)(2,1)}, bf16[832,256]{1,0:T(8,128)(2,1)}, u32[]{:S(2)}, u32[]{:S(2)}) collective-permute-start(bf16[832,256]{1,0:T(8,128)(2,1)} %constant_dynamic-slice_fusion.1), channel_id=1, source_target_pairs={{0,1},{1,0},{2,3},{3,2},{4,5},{5,4},{6,7},{7,6},{8,9},{9,8},{10,11... | collective-permute-start | bytes 1277960 | tf_op jit(solution)/shard_map/ppermute | solution.py:827
  94.2 13.8 %collective-permute-start.9 = (bf16[512,1024]{1,0:T(8,128)(2,1)}, bf16[512,1024]{1,0:T(8,128)(2,1)}, u32[]{:S(2)}, u32[]{:S(2)}) collective-permute-start(bf16[512,1024]{1,0:T(8,128)(2,1)} %get-tuple-element.251), channel_id=1, source_target_pairs={{0,1},{1,0},{2,3},{3,2},{4,5},{5,4},{6,7},{7,6},{8,9},{9,8},{10,11... | collective-permute-start | bytes 3145736 | tf_op jit(solution)/shard_map/ppermute | solution.py:827
  99.6 10.3 %collective-permute-start.11 = (bf16[1024,256]{1,0:T(8,128)(2,1)}, bf16[1024,256]{1,0:T(8,128)(2,1)}, u32[]{:S(2)}, u32[]{:S(2)}) collective-permute-start(bf16[1024,256]{1,0:T(8,128)(2,1)} %reshape.122.refs_5_.refs_1_), channel_id=1, source_target_pairs={{0,1},{1,0},{2,3},{3,2},{4,5},{5,4},{6,7},{7,6},{8,9},{9,8},{10,11... | collective-permute-start | bytes 1572872 | tf_op jit(solution)/shard_map/ppermute | solution.py:827
  105.0 1.4 collective-permute-start.12
  106.4 25.2 %collective-permute-start.13 = (bf16[512,1024]{1,0:T(8,128)(2,1)S(1)}, bf16[512,1024]{1,0:T(8,128)(2,1)S(1)}, u32[]{:S(2)}, u32[]{:S(2)}) collective-permute-start(bf16[512,1024]{1,0:T(8,128)(2,1)S(1)} %copy-done.92), channel_id=1, source_target_pairs={{0,4},{4,0},{8,12},{12,8},{16,20},{20,16},{24,28},{28,24},{1,5},{5... | collective-permute-start | bytes 3145736 | tf_op jit(solution)/shard_map/ppermute | solution.py:833
  108.1 25.1 %collective-permute-start.14 = (bf16[512,1024]{1,0:T(8,128)(2,1)S(1)}, bf16[512,1024]{1,0:T(8,128)(2,1)}, u32[]{:S(2)}, u32[]{:S(2)}) collective-permute-start(bf16[512,1024]{1,0:T(8,128)(2,1)S(1)} %constant_dynamic-slice_fusion), channel_id=1, source_target_pairs={{0,2},{2,0},{1,3},{3,1},{4,6},{6,4},{5,7},{7,5},{8,10},{10,8},{9,1... | collective-permute-start | bytes 3145736 | tf_op jit(solution)/shard_map/ppermute | solution.py:830
  130.9 25.3 %collective-permute-start.15 = (bf16[832,1024]{1,0:T(8,128)(2,1)}, bf16[832,1024]{1,0:T(8,128)(2,1)}, u32[]{:S(2)}, u32[]{:S(2)}) collective-permute-start(bf16[832,1024]{1,0:T(8,128)(2,1)} %get-tuple-element.152.h_ref), channel_id=1, source_target_pairs={{0,1},{1,0},{2,3},{3,2},{4,5},{5,4},{6,7},{7,6},{8,9},{9,8},{10,11... | collective-permute-start | bytes 5111816 | tf_op jit(solution)/shard_map/ppermute | solution.py:827
  133.2 36.1 %collective-permute-start.17 = (bf16[512,1024]{1,0:T(8,128)(2,1)}, bf16[512,1024]{1,0:T(8,128)(2,1)}, u32[]{:S(2)}, u32[]{:S(2)}) collective-permute-start(bf16[512,1024]{1,0:T(8,128)(2,1)} %collective-permute-done.14), channel_id=1, source_target_pairs={{0,8},{4,12},{8,0},{12,4},{16,24},{20,28},{24,16},{28,20},{1,9},{5... | collective-permute-start | bytes 3145736 | tf_op jit(solution)/shard_map/ppermute | solution.py:833
  134.6 19.4 %collective-permute-start.25 = (bf16[832,512]{1,0:T(8,128)(2,1)}, bf16[832,512]{1,0:T(8,128)(2,1)}, u32[]{:S(2)}, u32[]{:S(2)}) collective-permute-start(bf16[832,512]{1,0:T(8,128)(2,1)} %slice.154), channel_id=1, source_target_pairs={{0,1},{1,0},{2,3},{3,2},{4,5},{5,4},{6,7},{7,6},{8,9},{9,8},{10,11... | collective-permute-start | bytes 2555912 | tf_op jit(solution)/shard_map/ppermute | solution.py:827
  139.1 78.2 %collective-permute-start.22 = (bf16[832,1024]{1,0:T(8,128)(2,1)S(1)}, bf16[832,1024]{1,0:T(8,128)(2,1)S(1)}, u32[]{:S(2)}, u32[]{:S(2)}) collective-permute-start(bf16[832,1024]{1,0:T(8,128)(2,1)S(1)} %get-tuple-element.185), channel_id=1, source_target_pairs={{0,1},{1,0},{2,3},{3,2},{4,5},{5,4},{6,7},{7,6},{8,9},{9,8},{10,11... | collective-permute-start | bytes 5111816 | tf_op jit(solution)/shard_map/ppermute | solution.py:827
  201.9 30.5 %collective-permute-start.19 = (bf16[832,1024]{1,0:T(8,128)(2,1)}, bf16[832,1024]{1,0:T(8,128)(2,1)S(1)}, u32[]{:S(2)}, u32[]{:S(2)}) collective-permute-start(bf16[832,1024]{1,0:T(8,128)(2,1)} %get-tuple-element.169), channel_id=1, source_target_pairs={{0,1},{1,0},{2,3},{3,2},{4,5},{5,4},{6,7},{7,6},{8,9},{9,8},{10,11... | collective-permute-start | bytes 5111816 | tf_op jit(solution)/shard_map/ppermute | solution.py:827
  212.3 48.5 %collective-permute-start.20 = (bf16[1024,1024]{1,0:T(8,128)(2,1)}, bf16[1024,1024]{1,0:T(8,128)(2,1)}, u32[]{:S(2)}, u32[]{:S(2)}) collective-permute-start(bf16[1024,1024]{1,0:T(8,128)(2,1)} %convolution_convert_fusion.1), channel_id=1, source_target_pairs={{0,2},{2,0},{1,3},{3,1},{4,6},{6,4},{5,7},{7,5},{8,10},{10,8},{9,1... | collective-permute-start | bytes 6291464 | tf_op jit(solution)/shard_map/ppermute | solution.py:830
  254.6 1.6 collective-permute-start.24
  255.2 19.1 %collective-permute-start.26 = (bf16[832,1024]{1,0:T(8,128)(2,1)S(1)}, bf16[832,1024]{1,0:T(8,128)(2,1)S(1)}, u32[]{:S(2)}, u32[]{:S(2)}) collective-permute-start(bf16[832,1024]{1,0:T(8,128)(2,1)S(1)} %get-tuple-element.190), channel_id=1, source_target_pairs={{0,1},{1,0},{2,3},{3,2},{4,5},{5,4},{6,7},{7,6},{8,9},{9,8},{10,11... | collective-permute-start | bytes 5111816 | tf_op jit(solution)/shard_map/ppermute | solution.py:827
  255.5 9.3 %collective-permute-start.23 = (bf16[832,512]{1,0:T(8,128)(2,1)S(1)}, bf16[832,512]{1,0:T(8,128)(2,1)S(1)}, u32[]{:S(2)}, u32[]{:S(2)}) collective-permute-start(bf16[832,512]{1,0:T(8,128)(2,1)S(1)} %slice.147), channel_id=1, source_target_pairs={{0,1},{1,0},{2,3},{3,2},{4,5},{5,4},{6,7},{7,6},{8,9},{9,8},{10,11... | collective-permute-start | bytes 2555912 | tf_op jit(solution)/shard_map/ppermute | solution.py:827
  260.8 17.8 %collective-permute-start.21 = (bf16[832,1024]{1,0:T(8,128)(2,1)S(1)}, bf16[832,1024]{1,0:T(8,128)(2,1)S(1)}, u32[]{:S(2)}, u32[]{:S(2)}) collective-permute-start(bf16[832,1024]{1,0:T(8,128)(2,1)S(1)} %get-tuple-element.179.mine_ref), channel_id=1, source_target_pairs={{0,1},{1,0},{2,3},{3,2},{4,5},{5,4},{6,7},{7,6},{8,9},{9,8},{10,11... | collective-permute-start | bytes 5111816 | tf_op jit(solution)/shard_map/ppermute | solution.py:827
  260.8 49.9 %collective-permute-start.27 = (bf16[1024,1024]{1,0:T(8,128)(2,1)}, bf16[1024,1024]{1,0:T(8,128)(2,1)}, u32[]{:S(2)}, u32[]{:S(2)}) collective-permute-start(bf16[1024,1024]{1,0:T(8,128)(2,1)} %convolution_convert_fusion), channel_id=1, source_target_pairs={{0,2},{2,0},{1,3},{3,1},{4,6},{6,4},{5,7},{7,5},{8,10},{10,8},{9,1... | collective-permute-start | bytes 6291464 | tf_op jit(solution)/shard_map/ppermute | solution.py:830
  264.2 46.5 %collective-permute-start.28 = (bf16[512,1024]{1,0:T(8,128)(2,1)}, bf16[512,1024]{1,0:T(8,128)(2,1)}, u32[]{:S(2)}, u32[]{:S(2)}) collective-permute-start(bf16[512,1024]{1,0:T(8,128)(2,1)} %add_convert_fusion.8), channel_id=1, source_target_pairs={{0,4},{4,0},{8,12},{12,8},{16,20},{20,16},{24,28},{28,24},{1,5},{5... | collective-permute-start | bytes 3145736 | tf_op jit(solution)/shard_map/ppermute | solution.py:833
  310.7 39.5 %collective-permute-start.29 = (bf16[3072,256]{1,0:T(8,128)(2,1)}, bf16[3072,256]{1,0:T(8,128)(2,1)}, u32[]{:S(2)}, u32[]{:S(2)}) collective-permute-start(bf16[3072,256]{1,0:T(8,128)(2,1)} %pad_maximum_fusion.4), channel_id=1, source_target_pairs={{0,2},{2,0},{1,3},{3,1},{4,6},{6,4},{5,7},{7,5},{8,10},{10,8},{9,1... | collective-permute-start | bytes 4718600 | tf_op jit(solution)/shard_map/ppermute | solution.py:830
  314.5 35.6 %collective-permute-start.30 = (bf16[512,1024]{1,0:T(8,128)(2,1)}, bf16[512,1024]{1,0:T(8,128)(2,1)}, u32[]{:S(2)}, u32[]{:S(2)}) collective-permute-start(bf16[512,1024]{1,0:T(8,128)(2,1)} %add_convert_fusion.7), channel_id=1, source_target_pairs={{0,4},{4,0},{8,12},{12,8},{16,20},{20,16},{24,28},{28,24},{1,5},{5... | collective-permute-start | bytes 3145736 | tf_op jit(solution)/shard_map/ppermute | solution.py:833
  318.3 31.9 %collective-permute-start.31 = (bf16[512,1024]{1,0:T(8,128)(2,1)S(1)}, bf16[512,1024]{1,0:T(8,128)(2,1)S(1)}, u32[]{:S(2)}, u32[]{:S(2)}) collective-permute-start(bf16[512,1024]{1,0:T(8,128)(2,1)S(1)} %add_convert_fusion.6), channel_id=1, source_target_pairs={{0,8},{4,12},{24,16},{28,20},{1,9},{5,13},{25,17},{29,21},{2,10},{... | collective-permute-start | bytes 3145736 | tf_op jit(solution)/shard_map/ppermute | solution.py:833
  346.4 23.2 %collective-permute-start.36 = (bf16[832,1024]{1,0:T(8,128)(2,1)S(1)}, bf16[832,1024]{1,0:T(8,128)(2,1)S(1)}, u32[]{:S(2)}, u32[]{:S(2)}) collective-permute-start(bf16[832,1024]{1,0:T(8,128)(2,1)S(1)} %first_back.2), channel_id=1, source_target_pairs={{0,1},{1,0},{2,3},{3,2},{4,5},{5,4},{6,7},{7,6},{8,9},{9,8},{10,11... | collective-permute-start | bytes 5111816 | tf_op jit(solution)/shard_map/ppermute | solution.py:827
  351.7 36.8 %collective-permute-start.32 = (bf16[3072,256]{1,0:T(8,128)(2,1)S(1)}, bf16[3072,256]{1,0:T(8,128)(2,1)S(1)}, u32[]{:S(2)}, u32[]{:S(2)}) collective-permute-start(bf16[3072,256]{1,0:T(8,128)(2,1)S(1)} %copy-done.86), channel_id=1, source_target_pairs={{0,2},{2,0},{1,3},{3,1},{4,6},{6,4},{5,7},{7,5},{8,10},{10,8},{9,1... | collective-permute-start | bytes 4718600 | tf_op jit(solution)/shard_map/ppermute | solution.py:830
  355.1 25.4 %collective-permute-start.34 = (bf16[512,1024]{1,0:T(8,128)(2,1)S(1)}, bf16[512,1024]{1,0:T(8,128)(2,1)S(1)}, u32[]{:S(2)}, u32[]{:S(2)}) collective-permute-start(bf16[512,1024]{1,0:T(8,128)(2,1)S(1)} %add_convert_fusion.5), channel_id=1, source_target_pairs={{0,8},{4,12},{24,16},{28,20},{1,9},{5,13},{25,17},{29,21},{2,10},{... | collective-permute-start | bytes 3145736 | tf_op jit(solution)/shard_map/ppermute | solution.py:833
  358.4 22.0 %collective-permute-start.35 = (bf16[512,1024]{1,0:T(8,128)(2,1)S(1)}, bf16[512,1024]{1,0:T(8,128)(2,1)S(1)}, u32[]{:S(2)}, u32[]{:S(2)}) collective-permute-start(bf16[512,1024]{1,0:T(8,128)(2,1)S(1)} %add_convert_fusion.4), channel_id=1, source_target_pairs={{8,16},{16,8},{12,20},{20,12},{9,17},{17,9},{13,21},{21,13},{10,18... | collective-permute-start | bytes 3145736 | tf_op jit(solution)/shard_map/ppermute | solution.py:833
  360.5 19.9 %collective-permute-start.33 = (bf16[1536,256]{1,0:T(8,128)(2,1)S(1)}, bf16[1536,256]{1,0:T(8,128)(2,1)S(1)}, u32[]{:S(2)}, u32[]{:S(2)}) collective-permute-start(bf16[1536,256]{1,0:T(8,128)(2,1)S(1)} %add_convert_fusion.16), channel_id=1, source_target_pairs={{0,4},{4,0},{8,12},{12,8},{16,20},{20,16},{24,28},{28,24},{1,5},{5... | collective-permute-start | bytes 2359304 | tf_op jit(solution)/shard_map/ppermute | solution.py:833
  388.5 30.2 %collective-permute-start.44 = (bf16[512,1024]{1,0:T(8,128)(2,1)}, bf16[512,1024]{1,0:T(8,128)(2,1)}, u32[]{:S(2)}, u32[]{:S(2)}) collective-permute-start(bf16[512,1024]{1,0:T(8,128)(2,1)} %pad_maximum_fusion.8), channel_id=1, source_target_pairs={{0,2},{2,0},{1,3},{3,1},{4,6},{6,4},{5,7},{7,5},{8,10},{10,8},{9,1... | collective-permute-start | bytes 3145736 | tf_op jit(solution)/shard_map/ppermute | solution.py:830
  390.4 19.2 %collective-permute-start.45 = (bf16[1536,256]{1,0:T(8,128)(2,1)}, bf16[1536,256]{1,0:T(8,128)(2,1)}, u32[]{:S(2)}, u32[]{:S(2)}) collective-permute-start(bf16[1536,256]{1,0:T(8,128)(2,1)} %add_convert_fusion.14), channel_id=1, source_target_pairs={{0,4},{4,0},{8,12},{12,8},{16,20},{20,16},{24,28},{28,24},{1,5},{5... | collective-permute-start | bytes 2359304 | tf_op jit(solution)/shard_map/ppermute | solution.py:833
  391.5 27.2 %collective-permute-start.47 = (bf16[512,1024]{1,0:T(8,128)(2,1)S(1)}, bf16[512,1024]{1,0:T(8,128)(2,1)}, u32[]{:S(2)}, u32[]{:S(2)}) collective-permute-start(bf16[512,1024]{1,0:T(8,128)(2,1)S(1)} %add_convert_fusion.3), channel_id=1, source_target_pairs={{8,16},{16,8},{12,20},{20,12},{9,17},{17,9},{13,21},{21,13},{10,18... | collective-permute-start | bytes 3145736 | tf_op jit(solution)/shard_map/ppermute | solution.py:833
  394.6 26.4 %collective-permute-start.48 = (bf16[512,1024]{1,0:T(8,128)(2,1)}, bf16[512,1024]{1,0:T(8,128)(2,1)}, u32[]{:S(2)}, u32[]{:S(2)}) collective-permute-start(bf16[512,1024]{1,0:T(8,128)(2,1)} %add_convert_fusion.2), channel_id=1, source_target_pairs={{8,0},{12,4},{16,24},{20,28},{9,1},{13,5},{17,25},{21,29},{10,2},{... | collective-permute-start | bytes 3145736 | tf_op jit(solution)/shard_map/ppermute | solution.py:833
  397.3 21.4 %collective-permute-start.46 = (bf16[1536,256]{1,0:T(8,128)(2,1)S(1)}, bf16[1536,256]{1,0:T(8,128)(2,1)S(1)}, u32[]{:S(2)}, u32[]{:S(2)}) collective-permute-start(bf16[1536,256]{1,0:T(8,128)(2,1)S(1)} %add_convert_fusion.15), channel_id=1, source_target_pairs={{0,8},{4,12},{24,16},{28,20},{1,9},{5,13},{25,17},{29,21},{2,10},{... | collective-permute-start | bytes 2359304 | tf_op jit(solution)/shard_map/ppermute | solution.py:833
  424.0 44.0 %collective-permute-start.50 = (bf16[1536,256]{1,0:T(8,128)(2,1)}, bf16[1536,256]{1,0:T(8,128)(2,1)}, u32[]{:S(2)}, u32[]{:S(2)}) collective-permute-start(bf16[1536,256]{1,0:T(8,128)(2,1)} %add_convert_fusion.12), channel_id=1, source_target_pairs={{0,8},{4,12},{24,16},{28,20},{1,9},{5,13},{25,17},{29,21},{2,10},{... | collective-permute-start | bytes 2359304 | tf_op jit(solution)/shard_map/ppermute | solution.py:833
  429.9 38.2 %collective-permute-start.52 = (bf16[512,1024]{1,0:T(8,128)(2,1)}, bf16[512,1024]{1,0:T(8,128)(2,1)}, u32[]{:S(2)}, u32[]{:S(2)}) collective-permute-start(bf16[512,1024]{1,0:T(8,128)(2,1)} %add_convert_fusion.1), channel_id=1, source_target_pairs={{8,0},{12,4},{16,24},{20,28},{9,1},{13,5},{17,25},{21,29},{10,2},{... | collective-permute-start | bytes 3145736 | tf_op jit(solution)/shard_map/ppermute | solution.py:833
  433.8 34.3 %collective-permute-start.53 = (bf16[512,1024]{1,0:T(8,128)(2,1)}, bf16[512,1024]{1,0:T(8,128)(2,1)}, u32[]{:S(2)}, u32[]{:S(2)}) collective-permute-start(bf16[512,1024]{1,0:T(8,128)(2,1)} %broadcast_select_fusion.2), channel_id=1, source_target_pairs={{0,4},{4,0},{8,12},{12,8},{16,20},{20,16},{24,28},{28,24},{1,5},{5... | collective-permute-start | bytes 3145736 | tf_op jit(solution)/shard_map/ppermute | solution.py:833
  437.3 30.8 %collective-permute-start.51 = (bf16[1536,256]{1,0:T(8,128)(2,1)}, bf16[1536,256]{1,0:T(8,128)(2,1)}, u32[]{:S(2)}, u32[]{:S(2)}) collective-permute-start(bf16[1536,256]{1,0:T(8,128)(2,1)} %add_convert_fusion.13), channel_id=1, source_target_pairs={{8,16},{16,8},{12,20},{20,12},{9,17},{17,9},{13,21},{21,13},{10,18... | collective-permute-start | bytes 2359304 | tf_op jit(solution)/shard_map/ppermute | solution.py:833
  441.0 27.1 %collective-permute-start.49 = (bf16[256,1024]{1,0:T(8,128)(2,1)}, bf16[256,1024]{1,0:T(8,128)(2,1)}, u32[]{:S(2)}, u32[]{:S(2)}) collective-permute-start(bf16[256,1024]{1,0:T(8,128)(2,1)} %add_convert_fusion.20), channel_id=1, source_target_pairs={{0,4},{4,0},{8,12},{12,8},{16,20},{20,16},{24,28},{28,24},{1,5},{5... | collective-permute-start | bytes 1572872 | tf_op jit(solution)/shard_map/ppermute | solution.py:833
  469.7 23.7 %collective-permute-start.55 = (bf16[1536,256]{1,0:T(8,128)(2,1)S(1)}, bf16[1536,256]{1,0:T(8,128)(2,1)S(1)}, u32[]{:S(2)}, u32[]{:S(2)}) collective-permute-start(bf16[1536,256]{1,0:T(8,128)(2,1)S(1)} %add_convert_fusion.10), channel_id=1, source_target_pairs={{8,16},{16,8},{12,20},{20,12},{9,17},{17,9},{13,21},{21,13},{10,18... | collective-permute-start | bytes 2359304 | tf_op jit(solution)/shard_map/ppermute | solution.py:833
  472.0 24.3 %collective-permute-start.57 = (bf16[512,1024]{1,0:T(8,128)(2,1)S(1)}, bf16[512,1024]{1,0:T(8,128)(2,1)S(1)}, u32[]{:S(2)}, u32[]{:S(2)}) collective-permute-start(bf16[512,1024]{1,0:T(8,128)(2,1)S(1)} %broadcast_select_fusion.1), channel_id=1, source_target_pairs={{0,4},{4,0},{8,12},{12,8},{16,20},{20,16},{24,28},{28,24},{1,5},{5... | collective-permute-start | bytes 3145736 | tf_op jit(solution)/shard_map/ppermute | solution.py:833
  474.9 21.4 %collective-permute-start.56 = (bf16[1536,256]{1,0:T(8,128)(2,1)S(1)}, bf16[1536,256]{1,0:T(8,128)(2,1)S(1)}, u32[]{:S(2)}, u32[]{:S(2)}) collective-permute-start(bf16[1536,256]{1,0:T(8,128)(2,1)S(1)} %add_convert_fusion.11), channel_id=1, source_target_pairs={{8,0},{12,4},{16,24},{20,28},{9,1},{13,5},{17,25},{21,29},{10,2},{... | collective-permute-start | bytes 2359304 | tf_op jit(solution)/shard_map/ppermute | solution.py:833
  477.7 15.7 %collective-permute-start.54 = (bf16[256,1024]{1,0:T(8,128)(2,1)S(1)}, bf16[256,1024]{1,0:T(8,128)(2,1)S(1)}, u32[]{:S(2)}, u32[]{:S(2)}) collective-permute-start(bf16[256,1024]{1,0:T(8,128)(2,1)S(1)} %add_convert_fusion.19), channel_id=1, source_target_pairs={{0,8},{4,12},{24,16},{28,20},{1,9},{5,13},{25,17},{29,21},{2,10},{... | collective-permute-start | bytes 1572872 | tf_op jit(solution)/shard_map/ppermute | solution.py:833
  486.7 1.3 collective-permute-start.39
  488.0 43.0 %collective-permute-start.18 = (bf16[832,1024]{1,0:T(8,128)(2,1)}, bf16[832,1024]{1,0:T(8,128)(2,1)}, u32[]{:S(2)}, u32[]{:S(2)}) collective-permute-start(bf16[832,1024]{1,0:T(8,128)(2,1)} %get-tuple-element.167), channel_id=1, source_target_pairs={{0,1},{1,0},{2,3},{3,2},{4,5},{5,4},{6,7},{7,6},{8,9},{9,8},{10,11... | collective-permute-start | bytes 5111816 | tf_op jit(solution)/shard_map/ppermute | solution.py:827
  493.4 6.5 %collective-permute-start.37 = (f32[64,1024]{1,0:T(8,128)S(1)}, f32[64,1024]{1,0:T(8,128)S(1)}, u32[]{:S(2)}, u32[]{:S(2)}) collective-permute-start(f32[64,1024]{1,0:T(8,128)S(1)} %convolution_add_fusion), channel_id=1, source_target_pairs={{0,1},{1,0},{2,3},{3,2},{4,5},{5,4},{6,7},{7,6},{8,9},{9,8},{10,11... | collective-permute-start | bytes 786440 | tf_op jit(solution)/shard_map/ppermute | solution.py:827
  493.4 5.7 %collective-permute-start.40 = (f32[8,1024]{1,0:T(8,128)S(1)}, f32[8,1024]{1,0:T(8,128)S(1)}, u32[]{:S(2)}, u32[]{:S(2)}) collective-permute-start(f32[8,1024]{1,0:T(8,128)S(1)} %add.238), channel_id=1, source_target_pairs={{0,2},{2,0},{1,3},{3,1},{4,6},{6,4},{5,7},{7,5},{8,10},{10,8},{9,1... | collective-permute-start | bytes 98312 | tf_op jit(solution)/shard_map/ppermute | solution.py:830
  496.5 29.8 %collective-permute-start.59 = (bf16[1536,256]{1,0:T(8,128)(2,1)S(1)}, bf16[1536,256]{1,0:T(8,128)(2,1)}, u32[]{:S(2)}, u32[]{:S(2)}) collective-permute-start(bf16[1536,256]{1,0:T(8,128)(2,1)S(1)} %add_convert_fusion.9), channel_id=1, source_target_pairs={{8,0},{12,4},{16,24},{20,28},{9,1},{13,5},{17,25},{21,29},{10,2},{... | collective-permute-start | bytes 2359304 | tf_op jit(solution)/shard_map/ppermute | solution.py:833
  497.9 28.4 %collective-permute-start.60 = (bf16[1536,256]{1,0:T(8,128)(2,1)S(1)}, bf16[1536,256]{1,0:T(8,128)(2,1)}, u32[]{:S(2)}, u32[]{:S(2)}) collective-permute-start(bf16[1536,256]{1,0:T(8,128)(2,1)S(1)} %broadcast_select_fusion.4), channel_id=1, source_target_pairs={{0,4},{4,0},{8,12},{12,8},{16,20},{20,16},{24,28},{28,24},{1,5},{5... | collective-permute-start | bytes 2359304 | tf_op jit(solution)/shard_map/ppermute | solution.py:833
  499.1 23.7 %collective-permute-start.58 = (bf16[256,1024]{1,0:T(8,128)(2,1)S(1)}, bf16[256,1024]{1,0:T(8,128)(2,1)S(1)}, u32[]{:S(2)}, u32[]{:S(2)}) collective-permute-start(bf16[256,1024]{1,0:T(8,128)(2,1)S(1)} %add_convert_fusion.18), channel_id=1, source_target_pairs={{8,16},{16,8},{12,20},{20,12},{9,17},{17,9},{13,21},{21,13},{10,18... | collective-permute-start | bytes 1572872 | tf_op jit(solution)/shard_map/ppermute | solution.py:833
  499.8 16.4 %collective-permute-start.41 = (f32[8,1024]{1,0:T(8,128)S(1)}, f32[8,1024]{1,0:T(8,128)S(1)}, u32[]{:S(2)}, u32[]{:S(2)}) collective-permute-start(f32[8,1024]{1,0:T(8,128)S(1)} %add.239), channel_id=1, source_target_pairs={{0,4},{4,0},{8,12},{12,8},{16,20},{20,16},{24,28},{28,24},{1,5},{5... | collective-permute-start | bytes 98312 | tf_op jit(solution)/shard_map/ppermute | solution.py:833
  516.3 20.8 %collective-permute-start.38 = (bf16[64,1024]{1,0:T(8,128)(2,1)S(1)}, bf16[64,1024]{1,0:T(8,128)(2,1)S(1)}, u32[]{:S(2)}, u32[]{:S(2)}) collective-permute-start(bf16[64,1024]{1,0:T(8,128)(2,1)S(1)} %add_convert_fusion.21), channel_id=1, source_target_pairs={{0,2},{2,0},{1,3},{3,1},{4,6},{6,4},{5,7},{7,5},{8,10},{10,8},{9,1... | collective-permute-start | bytes 393224 | tf_op jit(solution)/shard_map/ppermute | solution.py:830
  522.8 12.1 %collective-permute-start.42 = (f32[8,1024]{1,0:T(8,128)S(1)}, f32[8,1024]{1,0:T(8,128)S(1)}, u32[]{:S(2)}, u32[]{:S(2)}) collective-permute-start(f32[8,1024]{1,0:T(8,128)S(1)} %add.240), channel_id=1, source_target_pairs={{0,8},{4,12},{8,0},{12,4},{16,24},{20,28},{24,16},{28,20},{1,9},{5... | collective-permute-start | bytes 98312 | tf_op jit(solution)/shard_map/ppermute | solution.py:833
  527.5 18.0 %collective-permute-start.61 = (bf16[256,1024]{1,0:T(8,128)(2,1)S(1)}, bf16[256,1024]{1,0:T(8,128)(2,1)}, u32[]{:S(2)}, u32[]{:S(2)}) collective-permute-start(bf16[256,1024]{1,0:T(8,128)(2,1)S(1)} %add_convert_fusion.17), channel_id=1, source_target_pairs={{8,0},{12,4},{16,24},{20,28},{9,1},{13,5},{17,25},{21,29},{10,2},{... | collective-permute-start | bytes 1572872 | tf_op jit(solution)/shard_map/ppermute | solution.py:833
  530.1 16.6 %collective-permute-start.62 = (bf16[1536,256]{1,0:T(8,128)(2,1)S(1)}, bf16[1536,256]{1,0:T(8,128)(2,1)}, u32[]{:S(2)}, u32[]{:S(2)}) collective-permute-start(bf16[1536,256]{1,0:T(8,128)(2,1)S(1)} %broadcast_select_fusion.3), channel_id=1, source_target_pairs={{0,4},{4,0},{8,12},{12,8},{16,20},{20,16},{24,28},{28,24},{1,5},{5... | collective-permute-start | bytes 2359304 | tf_op jit(solution)/shard_map/ppermute | solution.py:833
  534.9 5.0 collective-permute-start.43
  547.8 9.2 %collective-permute-start.63 = (bf16[256,1024]{1,0:T(8,128)(2,1)S(1)}, bf16[256,1024]{1,0:T(8,128)(2,1)S(1)}, u32[]{:S(2)}, u32[]{:S(2)}) collective-permute-start(bf16[256,1024]{1,0:T(8,128)(2,1)S(1)} %broadcast_select_fusion.5), channel_id=1, source_target_pairs={{0,4},{4,0},{8,12},{12,8},{16,20},{20,16},{24,28},{28,24},{1,5},{5... | collective-permute-start | bytes 1572872 | tf_op jit(solution)/shard_map/ppermute | solution.py:833
  (114 other events, 1035.2 us)

commit v3 on v2

--- a/solution.py
+++ b/solution.py
@@ -848,9 +848,8 @@
     def ask(v, which):
         return over_y(half_of(v, which))
 
-    bundle = jnp.concatenate(
-        [w_out, w_cross_out, w_cross_q.reshape(256, 1024), w_cross_kv.reshape(512, 1024)], axis=0
-    )
+    inward = jnp.concatenate([w_cross_q, w_cross_kv.reshape(2 * width, 256)], axis=0)
+    outward = jnp.concatenate([w_out, w_cross_out], axis=0)
     qkv_first = ask(w_qkv.reshape(3 * width, 256), near)
     scaled, _ = norm_parts(frames.astype(FULL))
     h1 = lower(scaled * norm_gain[0] + norm_bias[0])
@@ -858,9 +857,12 @@
     dout = jnp.where(loss_mask[:, None] != 0, cotangent, jnp.zeros((), ROUND))
     q0, k0, v0 = project(where, h1, h1_other, w_qkv, False)
 
-    q0, qkv_first, bundle, dout = join((q0, qkv_first, bundle, dout))
+    q0, qkv_first, inward, outward, dout = join((q0, qkv_first, inward, outward, dout))
     qkv_second = along_wide(qkv_first, Z_NEAR)
-    bundle_first = ask(bundle, column)
+    outward_first = ask(outward, column)
+    inward_first = ask(inward, column)
+    own_wo = over_core(outward)
+    own_wq = over_core(w_cross_q)
     dout_other = over_core(dout)
     o0, lse0 = self_forward(limit, q0, k0, v0)
 
@@ -872,32 +874,34 @@
         return half_of(v, 1 - core)
 
     o0_other = over_core(away_rows(o0))
-    q1, bundle_first, w_up_sent, o0_other = join((q1, bundle_first, w_up_sent, o0_other))
-    bundle_second = along_wide(bundle_first, X_PAIRS)
+    q1, outward_first, inward_first, w_up_sent, o0_other, own_wo, own_wq = join(
+        (q1, outward_first, inward_first, w_up_sent, o0_other, own_wo, own_wq)
+    )
+    outward_second = along_wide(outward_first, X_PAIRS)
+    inward_second = along_wide(inward_first, X_PAIRS)
     up_first = ask(w_up_sent, column)
-    own_wo = over_core(jnp.concatenate([w_out, w_cross_out], axis=0))
-    own_wq = over_core(w_cross_q)
     o1, lse1 = self_forward(limit, q1, k1, v1)
     o1_other = over_core(away_rows(o1))
 
-    o1, bundle_second, up_first, w_down_sent = join((o1, bundle_second, up_first, w_down))
+    o1, outward_second, inward_second, up_first, w_down_sent = join(
+        (o1, outward_second, inward_second, up_first, w_down)
+    )
     up_second = along_wide(up_first, X_PAIRS)
     down_first = ask(w_down_sent, near)
-    bundle_y = ordered(bundle_first, bundle_second, column)
-    out_y = bundle_y[:256]
-    cross_out_y = bundle_y[256:512]
-    cross_q_y = bundle_y[512:768].reshape(width, 256)
-    cross_kv_y = bundle_y[768:].reshape(2, width, 256)
-    y_wo = over_core(bundle_y[:512])
+    outward_y = ordered(outward_first, outward_second, column)
+    inward_y = ordered(inward_first, inward_second, column)
+    out_y = outward_y[:256]
+    cross_out_y = outward_y[256:]
+    cross_q_y = inward_y[:width]
+    cross_kv_y = inward_y[width:].reshape(2, width, 256)
+    y_wo = over_core(outward_y)
     y_wq = over_core(cross_q_y)
     wo = (w_out, out_y, own_wo[:256], y_wo[:256])
     wc = (w_cross_out, cross_out_y, own_wo[256:], y_wo[256:])
     wq = (w_cross_q, cross_q_y, own_wq, y_wq)
     text = lax.dynamic_slice(text_states, (side, 0, 0), (1, *text_states.shape[1:]))[0]
-    pair = lower(
-        jnp.einsum(
-            "td,gcde->gcte", text, jnp.stack([w_cross_kv, cross_kv_y]), preferred_element_type=FULL
-        )
+    pair = jnp.stack(
+        [jnp.stack([lower(nn(text, w[c])) for c in range(2)]) for w in (w_cross_kv, cross_kv_y)]
     )
     pair_other = over_core(pair)
     head_of = jnp.arange(256) // HEAD
@@ -935,50 +939,67 @@
     def plus(a, b):
         return lower(a.astype(FULL) + b.astype(FULL))
 
-    def x_send(own, received):
-        away_half = lower(half_of(own, 1 - column) + half_of(received, 1 - column).astype(FULL))
-        return along_wide(away_half, X_PAIRS)
-
-    def x_sum(own, received, over_x):
-        return plus(half_of(own, column) + half_of(received, column).astype(FULL), over_x)
-
-    def z_first(total):
-        return along_wide(total, Z_INWARD)
-
-    def z_second(total):
-        return along_wide(total, Z_MIDDLE)
-
-    def z_third(total):
-        return along_wide(total, Z_OUTWARD)
-
-    def z_pick(total, outer):
-        return jnp.where((layer == 1) | (layer == 2), total, outer)
-
-    def finish(mine, over_x):
-        return ordered(mine, over_x, column).astype(FULL)
+    class Sum:
+        def __init__(self, partner):
+            self.fly = over_y(partner)
+
+        def x(self, own):
+            away_half = lower(half_of(own, 1 - column) + half_of(self.fly, 1 - column).astype(FULL))
+            self.kept = half_of(own, column) + half_of(self.fly, column).astype(FULL)
+            self.fly = along_wide(away_half, X_PAIRS)
+
+        def near(self):
+            total = self.kept + self.fly.astype(FULL)
+            self.kept = half_of(total, near)
+            self.fly = along_wide(lower(half_of(total, 1 - near)), Z_NEAR)
+
+        def far(self):
+            self.kept = plus(self.kept, self.fly)
+            self.fly = along_wide(self.kept, Z_FAR)
+
+        def back(self):
+            self.kept = plus(self.kept, self.fly)
+            self.fly = along_wide(self.kept, Z_NEAR)
+
+        def along(self):
+            self.kept = ordered(self.kept, self.fly, near)
+            self.fly = along_wide(self.kept, X_PAIRS)
+
+        def end(self):
+            return ordered(self.kept, self.fly, column).astype(FULL)
+
+    def sync(sums_in_flight, *values):
+        done = join((*[each.fly for each in sums_in_flight], *values))
+        for each, fly in zip(sums_in_flight, done):
+            each.fly = fly
+        return done[len(sums_in_flight) :]
 
     up1 = lower(tn(h3_rows, du1))
     up1, g1 = join((up1, g1))
-    up_y_got = over_y(up1)
+    up = Sum(up1)
     down1 = lower(tn(g1, dout_rows))
     up0 = tn(h3_rows, du0)
     down0 = tn(g0, dout_rows)
     dx1, dself, dcross, dcq, dck, dcv, sums = middle_back(
         where, y_m, y_received, x1, x2, dout, cq, norm_gain, wq, ck, cv, wc
     )
-    dself, up_y_got, down1, up0, down0 = join((dself, up_y_got, down1, up0, down0))
-
-    down_y_got = over_y(down1)
-    up_x = x_send(up0, up_y_got)
+    dself, down1, up0, down0 = sync([up], dself, down1, up0, down0)
+
+    down = Sum(down1)
+    up.x(up0)
     dself_other = over_core(dself)
     dcross_other = over_core(dcross)
     dcq_other = over_core(dcq[:, 512:])
     d_pair = jnp.stack([dck, dcv], axis=1)
     d_pair = lower(d_pair[:2] + over_core(d_pair[2:]))
     do0, do1 = project(where, dself, dself_other, jnp.stack([w_out, out_y]), True)
-    grads1 = self_back(limit, q1, k1, v1, o1, do1, lse1)
+    do1, dcross_other, dcq_other = join((do1, dcross_other, dcq_other))
+    dq1, dk1, dv1 = self_back(limit, q1, k1, v1, o1, do1, lse1)
+    dq1, dcross_other = sync([up], dq1, dcross_other)
+
+    up.near()
     h1_rows = ordered(h1, h1_other, core)
-    qkv1 = lower(jnp.concatenate([tn(h1_rows, g) for g in grads1], axis=0))
+    qkv1 = lower(jnp.concatenate([tn(h1_rows, g) for g in (dq1, dk1, dv1)], axis=0))
     dself_rows = ordered(dself, dself_other, core)
     dcross_rows = jnp.concatenate([dcross, dcross_other], axis=0)
     h2_rows = jnp.concatenate([h2, h2_other], axis=0)
@@ -999,99 +1020,94 @@
         )
 
     into1 = lower(into(1))
+    qkv1, into1, do0 = sync([down, up], qkv1, into1, do0)
+
+    qkv = Sum(qkv1)
+    down.x(down0)
+    up.far()
+    dq0, dk0, dv0 = self_back(limit, q0, k0, v0, o0, do0, lse0)
+    dq0, dself_rows, dcross_rows = sync([down, up], dq0, dself_rows, dcross_rows)
+
+    down.near()
+    up.back()
+    grads = (dq0, dk0, dv0, dq1, dk1, dv1)
+    yo = first_back(away, grads, (w_qkv, qkv_y), ROUND)
+    y_received = over_core(yo)
+    qkv0 = jnp.concatenate([tn(h1_rows, g) for g in (dq0, dk0, dv0)], axis=0)
     outof1 = lower(outof(1, o1))
-    qkv1, into1, outof1, down_y_got, up_x, do0 = join((qkv1, into1, outof1, down_y_got, up_x, do0))
-
-    qkv_y_got = over_y(qkv1)
-    down_x = x_send(down0, down_y_got)
-    up_sum = x_sum(up0, up_y_got, up_x)
-    up_z = z_first(up_sum)
-    grads0 = self_back(limit, q0, k0, v0, o0, do0, lse0)
-    yo = first_back(away, (*grads0, *grads1), (w_qkv, qkv_y), ROUND)
-    y_received = over_core(yo)
-    qkv0 = jnp.concatenate([tn(h1_rows, g) for g in grads0], axis=0)
-    qkv0, yo, qkv_y_got, down_x, up_z, into1 = join((qkv0, yo, qkv_y_got, down_x, up_z, into1))
-
-    into_y_got = over_y(into1)
-    qkv_x = x_send(qkv0, qkv_y_got)
-    down_sum = x_sum(down0, down_y_got, down_x)
-    down_z = z_first(down_sum)
-    up_sum = plus(up_sum, up_z)
-    up_z = z_second(up_sum)
-    ym = first_back(where, (*grads0, *grads1), (w_qkv, qkv_y), FULL)
+    ym = first_back(where, grads, (w_qkv, qkv_y), FULL)
+    qkv0, ym, y_received, outof1 = sync([qkv, down, up], qkv0, ym, y_received, outof1)
+
+    cross_in = Sum(into1)
+    qkv.x(qkv0)
+    down.far()
+    up.along()
     grad_frames, first_sums = frames_back(where, ym, y_received, dx1, frames, norm_gain)
-    out_rows = lower(x2 + out_m + over_core(out_o).astype(FULL))
+    sums = sums + first_sums
+    sums_other = over_core(sums)
     into0 = into(0)
     outof0 = outof(0, o0)
     text_part = 0.0
     for g, weights in ((0, w_cross_kv), (1, cross_kv_y)):
         for c in range(2):
             text_part = text_part + nt(d_pair[g, c], weights[c])
-    text_grad = lower(text_part + over_core(text_part))
+    text_other = over_core(text_part)
+    sums_other, text_other, into0, outof0, grad_frames = sync(
+        [qkv, down], sums_other, text_other, into0, outof0, grad_frames
+    )
+
+    qkv.near()
+    down.back()
+    sums = sums + sums_other
+    sums_other = over_y(sums)
+    text_grad = lower(text_part + text_other)
     text_away = over_y(text_grad)
+    out_rows = lower(x2 + out_m + over_core(out_o).astype(FULL))
+    sums_other, text_away, out_rows = sync(
+        [cross_in, qkv, down, up], sums_other, text_away, out_rows
+    )
+
+    outs = Sum(outof1)
+    cross_in.x(into0)
+    qkv.far()
+    down.along()
+    sums = sums + sums_other
+    sums_other = along_wide(sums, X_PAIRS)
+    grad_up = up.end()
+    sums_other, grad_up = sync([cross_in, qkv], sums_other, grad_up)
+
+    cross_in.near()
+    qkv.back()
+    sums = sums + sums_other
+    sums_other = along_wide(sums, Z_NEAR)
     grad_text = ordered(text_grad[None], text_away[None], side)
-    sums = sums + first_sums
-    sums = sums + over_core(sums)
-    sums = sums + over_y(sums)
-    into_y_got, qkv_x, down_z, up_z, outof1, into0, outof0, grad_frames = join(
-        (into_y_got, qkv_x, down_z, up_z, outof1, into0, outof0, grad_frames)
-    )
-
-    outof_y_got = over_y(outof1)
-    into_x = x_send(into0, into_y_got)
-    qkv_sum = x_sum(qkv0, qkv_y_got, qkv_x)
-    qkv_z = z_first(qkv_sum)
-    down_sum = plus(down_sum, down_z)
-    down_z = z_second(down_sum)
-    up_sum = plus(up_sum, up_z)
-    up_z = z_third(up_sum)
-    sums = sums + along_wide(sums, X_PAIRS)
-    sums = sums + along_wide(sums, Z_NEAR)
-    sums = sums + along_wide(sums, Z_FAR)
-    outof_y_got, into_x, qkv_z, down_z, up_z = join((outof_y_got, into_x, qkv_z, down_z, up_z))
-
-    outof_x = x_send(outof0, outof_y_got)
-    into_sum = x_sum(into0, into_y_got, into_x)
-    into_z = z_first(into_sum)
-    qkv_sum = plus(qkv_sum, qkv_z)
-    qkv_z = z_second(qkv_sum)
-    down_sum = plus(down_sum, down_z)
-    down_z = z_third(down_sum)
-    up_sum = z_pick(up_sum, up_z)
-    up_x = along_wide(up_sum, X_PAIRS)
-    outof_x, into_z, qkv_z, down_z, up_x = join((outof_x, into_z, qkv_z, down_z, up_x))
-
-    outof_sum = x_sum(outof0, outof_y_got, outof_x)
-    outof_z = z_first(outof_sum)
-    into_sum = plus(into_sum, into_z)
-    into_z = z_second(into_sum)
-    qkv_sum = plus(qkv_sum, qkv_z)
-    qkv_z = z_third(qkv_sum)
-    down_sum = z_pick(down_sum, down_z)
-    down_x = along_wide(down_sum, X_PAIRS)
-    outof_z, into_z, qkv_z, down_x = join((outof_z, into_z, qkv_z, down_x))
-
-    outof_sum = plus(outof_sum, outof_z)
-    outof_z = z_second(outof_sum)
-    into_sum = plus(into_sum, into_z)
-    into_z = z_third(into_sum)
-    qkv_sum = z_pick(qkv_sum, qkv_z)
-    qkv_x = along_wide(qkv_sum, X_PAIRS)
-    grad_up = finish(up_sum, up_x)
-    outof_z, into_z, qkv_x, grad_up = join((outof_z, into_z, qkv_x, grad_up))
-
-    outof_sum = plus(outof_sum, outof_z)
-    outof_z = z_third(outof_sum)
-    into_sum = z_pick(into_sum, into_z)
-    into_x = along_wide(into_sum, X_PAIRS)
-    grad_down = finish(down_sum, down_x)
-    outof_z, into_x, grad_down = join((outof_z, into_x, grad_down))
-
-    outof_sum = z_pick(outof_sum, outof_z)
-    outof_x = along_wide(outof_sum, X_PAIRS)
-    grad_qkv = finish(qkv_sum, qkv_x).reshape(3, width, 256)
-    grad_cross_in = finish(into_sum, into_x)
-    grad_outs = finish(outof_sum, outof_x)
+    sums_other, grad_text = sync([outs, cross_in, qkv], sums_other, grad_text)
+
+    outs.x(outof0)
+    cross_in.far()
+    qkv.along()
+    sums = sums + sums_other
+    sums_other = along_wide(sums, Z_FAR)
+    (down.fly,) = join((down.fly,))
+    grad_down = down.end()
+    sums_other, grad_down = sync([outs, cross_in], sums_other, grad_down)
+
+    outs.near()
+    cross_in.back()
+    sums = sums + sums_other
+    sync([outs, cross_in])
+
+    outs.far()
+    cross_in.along()
+    grad_qkv = qkv.end().reshape(3, width, 256)
+    (grad_qkv,) = sync([outs], grad_qkv)
+
+    outs.back()
+    sync([outs])
+
+    outs.along()
+    grad_cross_in = cross_in.end()
+    grad_outs = outs.end()
     return (
         out_rows,
         grad_frames,

time: 564 us -> 567 us (level)
  waiting for transfers between devices: 102 us -> 145 us
  starting transfers between devices: 73.1 us -> 55.1 us
  other arithmetic: 89.3 us -> 78.1 us
  local copies, waits for them, and re-layouts: 49.8 us -> 38.9 us
    ppermute x32 -> x33, waiting for transfers between devices: 78.7 us -> 131 us  [along_wide(): return lax.ppermute(v, 'wide', pairs)]
    ppermute x32 -> x33, starting transfers between devices: 57 us -> 37.7 us  [along_wide(): return lax.ppermute(v, 'wide', pairs)]
    convert_element_type x24 -> x19, other arithmetic: 38.2 us -> 19 us  [lower(): return values_in.astype(jnp.bfloat16)]
    select_n x7 -> x14, other arithmetic: 17.5 us -> 27 us  [ordered(): jnp.where(which == 0, jnp.concatenate([first, second], axis=0), jnp.conca...]
    ppermute x11 -> x12, waiting for transfers between devices: 20.5 us -> 12.6 us  [over_y(): return lax.ppermute(v, 'narrow', Y_PAIRS)]
    add x5 -> x10, other arithmetic: 0.03 us -> 7.76 us  [the longest x5 6.96 us: near(): total = self.kept + self.fly.astype(FULL)]
    select_n x5 -> x0, other arithmetic: 6.08 us -> none  [z_pick(): return jnp.where((layer == 1) | (layer == 2), total, outer)]
    reshape x3 -> x0, local copies, waits for them, and re-layouts: 5.94 us -> none  [the longest x1 2.67 us: chip_local(): w_cross_kv.reshape(512, 1024)]
  transfers between devices with their start and end apart: 64 -> 66, of which waited for: 21 -> 22; matrix products, arithmetic and copies ran while one was open for 29% -> 25% of each run, Pallas kernels for 35% -> 35%
where the time goes in v3:
time: 567 us; the launch traced here: 563 us
  Pallas kernels  196 us (35%)
  waiting for transfers between devices  145 us (26%)
  other arithmetic  78.1 us (14%)
  starting transfers between devices  55.1 us (10%)
  matrix products  46.6 us (8%)
  local copies, waits for them, and re-layouts  38.9 us (7%)
    ppermute x33, waiting for transfers between devices, along_wide(): return lax.ppermute(v, 'wide', pairs)  131 us
    pallas_call x4, Pallas kernels, feed(): pl.pallas_call(functools.partial(feed_kernel, carried=carried, shared=1 i...  54.4 us
    dot_general x20, matrix products, tn(): lax.dot_general(a, b, (((0,), (0,)), ((), ())), preferred_element_type=FULL)  42.8 us
    pallas_call x2, Pallas kernels, self_back(): pl.pallas_call(functools.partial(self_back_kernel, span=span, floor=floor...  40.8 us
    ppermute x33, starting transfers between devices, along_wide(): return lax.ppermute(v, 'wide', pairs)  37.7 us
    pallas_call x2, Pallas kernels, self_forward(): pl.pallas_call(functools.partial(self_forward_kernel, span=span, floor=fl...  31.2 us
    select_n x14, other arithmetic, ordered(): jnp.where(which == 0, jnp.concatenate([first, second], axis=0), jnp.conca...  27 us
    pallas_call x1, Pallas kernels, middle_back(): pl.pallas_call(middle_back_kernel, grid_spec=pltpu.PrefetchScalarGridSpec...  22.7 us
  transfers between devices with their start and end apart: 66, of which 22 were waited for; matrix products, arithmetic and copies ran while one was open for 25% of the time, Pallas kernels for 35%

profile of v3, /device:TPU:0, one launch (start us, length us, event | category | flops | bytes accessed | tf_op | source)
XLA Modules:
  0.0 563.4 jit_solution(10698152491529004685)
XLA Ops:
  0.7 2.2 constant_dynamic-slice_fusion.6
  2.9 3.0 collective-permute-start.1
  5.9 1.8 convert_reduce_fusion
  8.3 1.9 fusion.5.mine_ref
  13.1 1.6 broadcast_select_fusion.d_ref
  17.8 5.5 project.3
  23.7 1.8 collective-permute-start.2
  25.6 1.6 collective-permute-start.4
  27.8 15.6 %self_forward.2 = (bf16[1664,256]{1,0:T(8,128)(2,1)S(1)}, f32[2,8,1664]{2,1,0:T(8,128)S(1)}) custom-call(s32[1]{0:T(128)} %dynamic_slice.117.limit_ref, bf16[1664,256]{1,0:T(8,128)(2,1)S(1)} %get-tuple-element.148.q_ref, bf16[1664,256]{1,0:T(8,128)(2,1)S(1)} %get-tuple-element.149.k_ref, bf16[1664,256]{1,0:T(8,128)(2,1)S(1)} %get-tuple-element.150.v_ref), custom_call_target="tpu_custom_call" | custom-call | flops 16000000000 | bytes 4000000 | tf_op jit(solution)/shard_map/self_forward/pallas_call | solution.py:455
  43.4 5.1 maximum_select_fusion
  49.0 1.9 maximum_select_fusion.6
  50.9 5.9 %project.4 = (bf16[1664,256]{1,0:T(8,128)(2,1)S(1)}, bf16[1664,256]{1,0:T(8,128)(2,1)S(1)}, bf16[1664,256]{1,0:T(8,128)(2,1)S(1)}) custom-call(s32[1]{0:T(128)} %bitcast.where_ref, bf16[832,1024]{1,0:T(8,128)(2,1)} %fusion.5.mine_ref, bf16[832,1024]{1,0:T(8,128)(2,1)} %collective-permute-done.other_ref, bf16[3,1024,256]{2,1,0:T(8,128)(2,1)S(1)} %bitcast.116), custom_call_target="tpu_custom_call" | custom-call | flops 2617245696 | bytes 8000000 | tf_op jit(solution)/shard_map/project/pallas_call | solution.py:391
  60.9 15.6 %self_forward.3 = (bf16[1664,256]{1,0:T(8,128)(2,1)S(1)}, f32[2,8,1664]{2,1,0:T(8,128)S(1)}) custom-call(s32[1]{0:T(128)} %dynamic_slice.117.limit_ref, bf16[1664,256]{1,0:T(8,128)(2,1)S(1)} %get-tuple-element.159.q_ref, bf16[1664,256]{1,0:T(8,128)(2,1)S(1)} %get-tuple-element.160.k_ref, bf16[1664,256]{1,0:T(8,128)(2,1)S(1)} %get-tuple-element.161.v_ref), custom_call_target="tpu_custom_call" | custom-call | flops 16000000000 | bytes 4000000 | tf_op jit(solution)/shard_map/self_forward/pallas_call | solution.py:455
  77.2 12.3 %collective-permute-done.8 = bf16[256,1024]{1,0:T(8,128)(2,1)S(1)} collective-permute-done((bf16[256,1024]{1,0:T(8,128)(2,1)S(1)}, bf16[256,1024]{1,0:T(8,128)(2,1)S(1)}, u32[]{:S(2)}, u32[]{:S(2)}) %collective-permute-start.8) | collective-permute-done | bytes 524320 | tf_op jit(solution)/shard_map/ppermute | solution.py:833
  95.5 20.9 %middle_forward.1 = (f32[832,1024]{1,0:T(8,128)}, f32[832,1024]{1,0:T(8,128)}, bf16[832,1024]{1,0:T(8,128)(2,1)S(1)}, bf16[832,1024]{1,0:T(8,128)(2,1)S(1)}, bf1...) custom-call(s32[1]{0:T(128)} %bitcast.where_ref, bf16[832,1024]{1,0:T(8,128)(2,1)} %frame_ref.3, ...), custom_call_target="tpu_custom_call" | custom-call | flops 7000000000 | bytes 25000000 | tf_op jit(solution)/shard_map/middle_forward/pallas_call | solution.py:604
  120.3 2.3 maximum_select_fusion.2.up_ref
  125.4 13.1 %feed.4 = (bf16[1664,1024]{1,0:T(8,128)(2,1)}, bf16[1664,1024]{1,0:T(8,128)(2,1)}, f32[832,1024]{1,0:T(8,128)}, f32[832,1024]{1,0:T(8,128)}) custom-call(s32[1]{0:T(128)} %bitcast.where_ref, bf16[832,1024]{1,0:T(8,128)(2,1)} %get-tuple-element.175.h_ref, bf16[832,1024]{1,0:T(8,128)(2,1)} %copy-done.8, bf16[1024,1024]{1,0:T(8,128)(2,1)} %up_ref.3, ...), custom_call_target="tpu_custom_call" | custom-call | flops 6979321856 | bytes 20000000 | tf_op jit(solution)/shard_map/feed/pallas_call | solution.py:649
  139.9 2.1 fusion.83
  143.2 13.1 %feed.5 = (bf16[1664,1024]{1,0:T(8,128)(2,1)}, bf16[1664,1024]{1,0:T(8,128)(2,1)}, f32[832,1024]{1,0:T(8,128)}, f32[832,1024]{1,0:T(8,128)}) custom-call(s32[1]{0:T(128)} %bitcast.where_ref, bf16[832,1024]{1,0:T(8,128)(2,1)} %copy-done.85, bf16[832,1024]{1,0:T(8,128)(2,1)} %copy-done.84, ...), custom_call_target="tpu_custom_call", output_to_operand_aliasing={{0}: (5, {}), {1}: (6, {})} | custom-call | flops 6979321856 | bytes 20000000 | tf_op jit(solution)/shard_map/feed/pallas_call | solution.py:649
  156.4 4.7 maximum_select_fusion.3.down_ref
  161.0 14.3 %feed.6 = (bf16[1664,1024]{1,0:T(8,128)(2,1)}, bf16[1664,1024]{1,0:T(8,128)(2,1)}, f32[832,1024]{1,0:T(8,128)}, f32[832,1024]{1,0:T(8,128)}) custom-call(s32[1]{0:T(128)} %bitcast.where_ref, bf16[832,1024]{1,0:T(8,128)(2,1)} %get-tuple-element.175.h_ref, bf16[832,1024]{1,0:T(8,128)(2,1)} %copy-done.8, bf16[1024,1024]{1,0:T(8,128)(2,1)} %maximum_select_fusion.2.up_ref, ...), custom_call_target="tpu_custom_call" | custom-call | flops 6979321856 | bytes 20000000 | tf_op jit(solution)/shard_map/feed/pallas_call | solution.py:649
  175.4 13.8 %feed.7 = (bf16[1664,1024]{1,0:T(8,128)(2,1)}, bf16[1664,1024]{1,0:T(8,128)(2,1)}, bf16[832,1024]{1,0:T(8,128)(2,1)}, bf16[832,1024]{1,0:T(8,128)(2,1)}) custom-call(s32[1]{0:T(128)} %bitcast.where_ref, bf16[832,1024]{1,0:T(8,128)(2,1)} %copy-done.85, bf16[832,1024]{1,0:T(8,128)(2,1)} %copy-done.84, ...), custom_call_target="tpu_custom_call", output_to_operand_aliasing={{0}: (7, {}), {1}: (8, {})} | custom-call | flops 6979321856 | bytes 20000000 | tf_op jit(solution)/shard_map/feed/pallas_call | solution.py:649
  191.7 7.7 %fusion.85 = f32[1024,1024]{1,0:T(8,128)} fusion(bf16[1664,1024]{1,0:T(8,128)(2,1)} %constant_dynamic-update-slice_fusion, bf16[1664,1024]{1,0:T(8,128)(2,1)S(1)} %copy-done.132), kind=kOutput, calls=%fused_computation.202 | convolution fusion | flops 3489660928 | bytes 11010048 | tf_op jit(solution)/shard_map/dot_general | solution.py:328
  199.5 5.2 convolution_convert_fusion.1
  205.2 5.2 convolution_convert_fusion
  210.5 5.5 fusion.86
  216.2 22.7 %middle_back.1 = (f32[832,1024]{1,0:T(8,128)}, bf16[832,1024]{1,0:T(8,128)(2,1)S(1)}, bf16[832,1024]{1,0:T(8,128)(2,1)S(1)}, bf16[832,1024]{1,0:T(8,128)(2,1)S(1...) custom-call(s32[1]{0:T(128)} %bitcast.where_ref, ...), custom_call_target="tpu_custom_call" | custom-call | flops 7000000000 | bytes 25000000 | tf_op jit(solution)/shard_map/middle_back/pallas_call | solution.py:729
  239.2 2.8 constant_dynamic-update-slice_fusion.4
  245.0 7.9 %collective-permute-done.20 = bf16[1024,1024]{1,0:T(8,128)(2,1)S(1)} collective-permute-done((bf16[1024,1024]{1,0:T(8,128)(2,1)}, bf16[1024,1024]{1,0:T(8,128)(2,1)S(1)}, u32[]{:S(2)}, u32[]{:S(2)}) %collective-permute-start.20) | collective-permute-done | bytes 2097184 | tf_op jit(solution)/shard_map/ppermute | solution.py:830
  260.3 2.2 project.5
  264.9 20.3 %self_back.2 = (bf16[1664,256]{1,0:T(8,128)(2,1)S(1)}, bf16[1664,256]{1,0:T(8,128)(2,1)S(1)}, bf16[1664,256]{1,0:T(8,128)(2,1)S(1)}) custom-call(s32[1]{0:T(128)} %dynamic_slice.117.limit_ref, bf16[1664,256]{1,0:T(8,128)(2,1)S(1)} %copy-done.48, bf16[1664,256]{1,0:T(8,128)(2,1)S(1)} %copy-done.50, bf16[1664,256]{1,0:T(8,128)(2,1)S(1)} %copy-done.52, ...), custom_call_target="tpu_custom_call" | custom-call | flops 20000000000 | bytes 6000000 | tf_op jit(solution)/shard_map/self_back/pallas_call | solution.py:536
  285.3 3.3 convolution_convert_fusion.7
  293.2 1.6 collective-permute-start.27
  301.5 2.1 pad_maximum_fusion
  303.6 3.1 maximum_select_fusion.1
  308.8 2.7 collective-permute-start.33
  311.5 2.5 add_convert_fusion.1
  314.6 20.5 %self_back.3 = (bf16[1664,256]{1,0:T(8,128)(2,1)S(1)}, bf16[1664,256]{1,0:T(8,128)(2,1)S(1)}, bf16[1664,256]{1,0:T(8,128)(2,1)S(1)}) custom-call(s32[1]{0:T(128)} %dynamic_slice.117.limit_ref, bf16[1664,256]{1,0:T(8,128)(2,1)S(1)} %copy-done.42, bf16[1664,256]{1,0:T(8,128)(2,1)S(1)} %copy-done.44, bf16[1664,256]{1,0:T(8,128)(2,1)S(1)} %copy-done.46, ...), custom_call_target="tpu_custom_call" | custom-call | flops 20000000000 | bytes 6000000 | tf_op jit(solution)/shard_map/self_back/pallas_call | solution.py:536
  341.1 4.4 first_back.3
  347.1 1.6 collective-permute-start.35
  348.7 2.0 convert_add_fusion
  352.7 4.4 first_back.2.ym_ref
  362.3 10.4 %collective-permute-done.34 = bf16[256,1024]{1,0:T(8,128)(2,1)S(1)} collective-permute-done((bf16[256,1024]{1,0:T(8,128)(2,1)S(1)}, bf16[256,1024]{1,0:T(8,128)(2,1)S(1)}, u32[]{:S(2)}, u32[]{:S(2)}) %collective-permute-start.34) | collective-permute-done | bytes 524320 | tf_op jit(solution)/shard_map/ppermute | solution.py:833
  381.2 4.0 frames_back.1
  387.0 15.2 %collective-permute-done.39 = bf16[256,1024]{1,0:T(8,128)(2,1)S(1)} collective-permute-done((bf16[256,1024]{1,0:T(8,128)(2,1)S(1)}, bf16[256,1024]{1,0:T(8,128)(2,1)S(1)}, u32[]{:S(2)}, u32[]{:S(2)}) %collective-permute-start.39) | collective-permute-done | bytes 524320 | tf_op jit(solution)/shard_map/ppermute | solution.py:833
  403.4 1.8 convert_add_fusion.3
  407.8 2.2 collective-permute-done.30
  411.6 3.8 add_convert_fusion
  416.7 7.6 %collective-permute-done.42 = bf16[768,256]{1,0:T(8,128)(2,1)S(1)} collective-permute-done((bf16[768,256]{1,0:T(8,128)(2,1)S(1)}, bf16[768,256]{1,0:T(8,128)(2,1)S(1)}, u32[]{:S(2)}, u32[]{:S(2)}) %collective-permute-start.42) | collective-permute-done | bytes 393248 | tf_op jit(solution)/shard_map/ppermute | solution.py:833
  430.1 3.0 maximum_select_fusion.12
  435.3 2.9 fusion.6
  438.2 28.0 %collective-permute-done.51 = f32[8,1024]{1,0:T(8,128)S(1)} collective-permute-done((f32[8,1024]{1,0:T(8,128)S(1)}, f32[8,1024]{1,0:T(8,128)S(1)}, u32[]{:S(2)}, u32[]{:S(2)}) %collective-permute-start.51) | collective-permute-done | bytes 32800 | tf_op jit(solution)/shard_map/ppermute | solution.py:833
  472.4 1.8 maximum_select_fusion.17
  474.2 9.2 %collective-permute-done.54 = f32[8,1024]{1,0:T(8,128)S(1)} collective-permute-done((f32[8,1024]{1,0:T(8,128)S(1)}, f32[8,1024]{1,0:T(8,128)S(1)}, u32[]{:S(2)}, u32[]{:S(2)}) %collective-permute-start.54) | collective-permute-done | bytes 32800 | tf_op jit(solution)/shard_map/ppermute | solution.py:833
  485.6 4.3 collective-permute-start.56
  489.8 5.3 fusion.7
  498.2 7.9 %collective-permute-done.57 = f32[8,1024]{1,0:T(8,128)S(1)} collective-permute-done((f32[8,1024]{1,0:T(8,128)S(1)}, f32[8,1024]{1,0:T(8,128)S(1)}, u32[]{:S(2)}, u32[]{:S(2)}) %collective-permute-start.57) | collective-permute-done | bytes 32800 | tf_op jit(solution)/shard_map/ppermute | solution.py:833
  507.6 2.1 collective-permute-start.59
  509.7 13.0 %collective-permute-done.59 = bf16[128,1024]{1,0:T(8,128)(2,1)S(1)} collective-permute-done((bf16[128,1024]{1,0:T(8,128)(2,1)S(1)}, bf16[128,1024]{1,0:T(8,128)(2,1)S(1)}, u32[]{:S(2)}, u32[]{:S(2)}) %collective-permute-start.59) | collective-permute-done | bytes 262176 | tf_op jit(solution)/shard_map/ppermute | solution.py:833
  527.5 1.8 maximum_select_fusion.8
  529.3 1.9 convert.33
  531.2 8.5 %collective-permute-done.61 = bf16[128,1024]{1,0:T(8,128)(2,1)S(1)} collective-permute-done((bf16[128,1024]{1,0:T(8,128)(2,1)S(1)}, bf16[128,1024]{1,0:T(8,128)(2,1)S(1)}, u32[]{:S(2)}, u32[]{:S(2)}) %collective-permute-start.61) | collective-permute-done | bytes 262176 | tf_op jit(solution)/shard_map/ppermute | solution.py:833
  539.9 8.2 %collective-permute-done.63 = bf16[128,1024]{1,0:T(8,128)(2,1)S(1)} collective-permute-done((bf16[128,1024]{1,0:T(8,128)(2,1)S(1)}, bf16[128,1024]{1,0:T(8,128)(2,1)S(1)}, u32[]{:S(2)}, u32[]{:S(2)}) %collective-permute-start.63) | collective-permute-done | bytes 262176 | tf_op jit(solution)/shard_map/ppermute | solution.py:833
  552.9 8.3 %collective-permute-done.64 = bf16[256,1024]{1,0:T(8,128)(2,1)S(1)} collective-permute-done((bf16[256,1024]{1,0:T(8,128)(2,1)S(1)}, bf16[256,1024]{1,0:T(8,128)(2,1)S(1)}, u32[]{:S(2)}, u32[]{:S(2)}) %collective-permute-start.64) | collective-permute-done | bytes 524320 | tf_op jit(solution)/shard_map/ppermute | solution.py:833
  (494 shorter events, 121.4 us)
Async XLA Ops:
  2.9 20.8 %collective-permute-start.1 = (bf16[1536,256]{1,0:T(8,128)(2,1)}, bf16[1536,256]{1,0:T(8,128)(2,1)}, u32[]{:S(2)}, u32[]{:S(2)}) collective-permute-start(bf16[1536,256]{1,0:T(8,128)(2,1)} %constant_dynamic-slice_fusion.6), channel_id=1, source_target_pairs={{0,2},{2,0},{1,3},{3,1},{4,6},{6,4},{5,7},{7,5},{8,10},{10,8},{9,1... | collective-permute-start | bytes 2359304 | tf_op jit(solution)/shard_map/ppermute | solution.py:830
  10.2 7.2 %collective-permute-start = (bf16[832,1024]{1,0:T(8,128)(2,1)}, bf16[832,1024]{1,0:T(8,128)(2,1)}, u32[]{:S(2)}, u32[]{:S(2)}) collective-permute-start(bf16[832,1024]{1,0:T(8,128)(2,1)} %fusion.5.mine_ref), channel_id=1, source_target_pairs={{0,1},{1,0},{2,3},{3,2},{4,5},{5,4},{6,7},{7,6},{8,9},{9,8},{10,11... | collective-permute-start | bytes 5111816 | tf_op jit(solution)/shard_map/ppermute | solution.py:827
  10.2 46.6 %collective-permute-start.7 = (bf16[1024,256]{1,0:T(8,128)(2,1)S(1)}, bf16[1024,256]{1,0:T(8,128)(2,1)}, u32[]{:S(2)}, u32[]{:S(2)}) collective-permute-start(bf16[1024,256]{1,0:T(8,128)(2,1)S(1)} %copy-done.16), channel_id=1, source_target_pairs={{0,1},{1,0},{2,3},{3,2},{4,5},{5,4},{6,7},{7,6},{8,9},{9,8},{10,11... | collective-permute-start | bytes 1572872 | tf_op jit(solution)/shard_map/ppermute | solution.py:827
  23.7 24.9 %collective-permute-start.2 = (bf16[1536,256]{1,0:T(8,128)(2,1)}, bf16[1536,256]{1,0:T(8,128)(2,1)S(1)}, u32[]{:S(2)}, u32[]{:S(2)}) collective-permute-start(bf16[1536,256]{1,0:T(8,128)(2,1)} %collective-permute-done.1), channel_id=1, source_target_pairs={{0,8},{4,12},{8,0},{12,4},{16,24},{20,28},{24,16},{28,20},{1,9},{5... | collective-permute-start | bytes 2359304 | tf_op jit(solution)/shard_map/ppermute | solution.py:833
  25.6 31.6 %collective-permute-start.4 = (bf16[1536,256]{1,0:T(8,128)(2,1)S(1)}, bf16[1536,256]{1,0:T(8,128)(2,1)S(1)}, u32[]{:S(2)}, u32[]{:S(2)}) collective-permute-start(bf16[1536,256]{1,0:T(8,128)(2,1)S(1)} %constant_dynamic-slice_fusion.4), channel_id=1, source_target_pairs={{0,2},{2,0},{1,3},{3,1},{4,6},{6,4},{5,7},{7,5},{8,10},{10,8},{9,1... | collective-permute-start | bytes 2359304 | tf_op jit(solution)/shard_map/ppermute | solution.py:830
  27.2 30.0 %collective-permute-start.6 = (bf16[512,1024]{1,0:T(8,128)(2,1)S(1)}, bf16[512,1024]{1,0:T(8,128)(2,1)S(1)}, u32[]{:S(2)}, u32[]{:S(2)}) collective-permute-start(bf16[512,1024]{1,0:T(8,128)(2,1)S(1)} %pad_maximum_fusion.7), channel_id=1, source_target_pairs={{0,1},{1,0},{2,3},{3,2},{4,5},{5,4},{6,7},{7,6},{8,9},{9,8},{10,11... | collective-permute-start | bytes 3145736 | tf_op jit(solution)/shard_map/ppermute | solution.py:827
  27.2 30.0 %collective-permute-start.3 = (bf16[256,1024]{1,0:T(8,128)(2,1)S(1)}, bf16[256,1024]{1,0:T(8,128)(2,1)S(1)}, u32[]{:S(2)}, u32[]{:S(2)}) collective-permute-start(bf16[256,1024]{1,0:T(8,128)(2,1)S(1)} %constant_dynamic-slice_fusion.5), channel_id=1, source_target_pairs={{0,2},{2,0},{1,3},{3,1},{4,6},{6,4},{5,7},{7,5},{8,10},{10,8},{9,1... | collective-permute-start | bytes 1572872 | tf_op jit(solution)/shard_map/ppermute | solution.py:830
  48.7 8.5 %collective-permute-start.5 = (bf16[832,256]{1,0:T(8,128)(2,1)S(1)}, bf16[832,256]{1,0:T(8,128)(2,1)S(1)}, u32[]{:S(2)}, u32[]{:S(2)}) collective-permute-start(bf16[832,256]{1,0:T(8,128)(2,1)S(1)} %constant_dynamic-slice_fusion.3), channel_id=1, source_target_pairs={{0,1},{1,0},{2,3},{3,2},{4,5},{5,4},{6,7},{7,6},{8,9},{9,8},{10,11... | collective-permute-start | bytes 1277960 | tf_op jit(solution)/shard_map/ppermute | solution.py:827
  56.8 19.9 %collective-permute-start.18 = (bf16[832,1024]{1,0:T(8,128)(2,1)S(1)}, bf16[832,1024]{1,0:T(8,128)(2,1)S(1)}, u32[]{:S(2)}, u32[]{:S(2)}) collective-permute-start(bf16[832,1024]{1,0:T(8,128)(2,1)S(1)} %broadcast_select_fusion.d_ref), channel_id=1, source_target_pairs={{0,1},{1,0},{2,3},{3,2},{4,5},{5,4},{6,7},{7,6},{8,9},{9,8},{10,11... | collective-permute-start | bytes 5111816 | tf_op jit(solution)/shard_map/ppermute | solution.py:827
  57.3 32.2 %collective-permute-start.10 = (bf16[512,1024]{1,0:T(8,128)(2,1)S(1)}, bf16[512,1024]{1,0:T(8,128)(2,1)S(1)}, u32[]{:S(2)}, u32[]{:S(2)}) collective-permute-start(bf16[512,1024]{1,0:T(8,128)(2,1)S(1)} %constant_dynamic-slice_fusion.2), channel_id=1, source_target_pairs={{0,2},{2,0},{1,3},{3,1},{4,6},{6,4},{5,7},{7,5},{8,10},{10,8},{9,1... | collective-permute-start | bytes 3145736 | tf_op jit(solution)/shard_map/ppermute | solution.py:830
  58.9 30.6 %collective-permute-start.9 = (bf16[1536,256]{1,0:T(8,128)(2,1)S(1)}, bf16[1536,256]{1,0:T(8,128)(2,1)S(1)}, u32[]{:S(2)}, u32[]{:S(2)}) collective-permute-start(bf16[1536,256]{1,0:T(8,128)(2,1)S(1)} %collective-permute-done.4), channel_id=1, source_target_pairs={{0,4},{4,0},{8,12},{12,8},{16,20},{20,16},{24,28},{28,24},{1,5},{5... | collective-permute-start | bytes 2359304 | tf_op jit(solution)/shard_map/ppermute | solution.py:833
  60.4 29.1 %collective-permute-start.8 = (bf16[256,1024]{1,0:T(8,128)(2,1)S(1)}, bf16[256,1024]{1,0:T(8,128)(2,1)S(1)}, u32[]{:S(2)}, u32[]{:S(2)}) collective-permute-start(bf16[256,1024]{1,0:T(8,128)(2,1)S(1)} %collective-permute-done.3), channel_id=1, source_target_pairs={{0,4},{4,0},{8,12},{12,8},{16,20},{20,16},{24,28},{28,24},{1,5},{5... | collective-permute-start | bytes 1572872 | tf_op jit(solution)/shard_map/ppermute | solution.py:833
  76.6 18.8 %collective-permute-start.11 = (bf16[832,256]{1,0:T(8,128)(2,1)S(1)}, bf16[832,256]{1,0:T(8,128)(2,1)S(1)}, u32[]{:S(2)}, u32[]{:S(2)}) collective-permute-start(bf16[832,256]{1,0:T(8,128)(2,1)S(1)} %constant_dynamic-slice_fusion.1), channel_id=1, source_target_pairs={{0,1},{1,0},{2,3},{3,2},{4,5},{5,4},{6,7},{7,6},{8,9},{9,8},{10,11... | collective-permute-start | bytes 1277960 | tf_op jit(solution)/shard_map/ppermute | solution.py:827
  90.7 4.6 collective-permute-start.12
  91.6 3.8 collective-permute-start.13
  92.4 25.2 %collective-permute-start.16 = (bf16[512,1024]{1,0:T(8,128)(2,1)S(1)}, bf16[512,1024]{1,0:T(8,128)(2,1)}, u32[]{:S(2)}, u32[]{:S(2)}) collective-permute-start(bf16[512,1024]{1,0:T(8,128)(2,1)S(1)} %constant_dynamic-slice_fusion), channel_id=1, source_target_pairs={{0,2},{2,0},{1,3},{3,1},{4,6},{6,4},{5,7},{7,5},{8,10},{10,8},{9,1... | collective-permute-start | bytes 3145736 | tf_op jit(solution)/shard_map/ppermute | solution.py:830
  93.6 25.2 %collective-permute-start.15 = (bf16[512,1024]{1,0:T(8,128)(2,1)S(1)}, bf16[512,1024]{1,0:T(8,128)(2,1)S(1)}, u32[]{:S(2)}, u32[]{:S(2)}) collective-permute-start(bf16[512,1024]{1,0:T(8,128)(2,1)S(1)} %collective-permute-done.10), channel_id=1, source_target_pairs={{0,4},{4,0},{8,12},{12,8},{16,20},{20,16},{24,28},{28,24},{1,5},{5... | collective-permute-start | bytes 3145736 | tf_op jit(solution)/shard_map/ppermute | solution.py:833
  116.5 25.6 %collective-permute-start.17 = (bf16[832,1024]{1,0:T(8,128)(2,1)}, bf16[832,1024]{1,0:T(8,128)(2,1)S(1)}, u32[]{:S(2)}, u32[]{:S(2)}) collective-permute-start(bf16[832,1024]{1,0:T(8,128)(2,1)} %get-tuple-element.175.h_ref), channel_id=1, source_target_pairs={{0,1},{1,0},{2,3},{3,2},{4,5},{5,4},{6,7},{7,6},{8,9},{9,8},{10,11... | collective-permute-start | bytes 5111816 | tf_op jit(solution)/shard_map/ppermute | solution.py:827
  118.8 37.5 %collective-permute-start.19 = (bf16[512,1024]{1,0:T(8,128)(2,1)}, bf16[512,1024]{1,0:T(8,128)(2,1)}, u32[]{:S(2)}, u32[]{:S(2)}) collective-permute-start(bf16[512,1024]{1,0:T(8,128)(2,1)} %collective-permute-done.16), channel_id=1, source_target_pairs={{0,8},{4,12},{8,0},{12,4},{16,24},{20,28},{24,16},{28,20},{1,9},{5... | collective-permute-start | bytes 3145736 | tf_op jit(solution)/shard_map/ppermute | solution.py:833
  120.3 19.6 %collective-permute-start.37 = (bf16[832,512]{1,0:T(8,128)(2,1)}, bf16[832,512]{1,0:T(8,128)(2,1)}, u32[]{:S(2)}, u32[]{:S(2)}) collective-permute-start(bf16[832,512]{1,0:T(8,128)(2,1)} %slice.155), channel_id=1, source_target_pairs={{0,1},{1,0},{2,3},{3,2},{4,5},{5,4},{6,7},{7,6},{8,9},{9,8},{10,11... | collective-permute-start | bytes 2555912 | tf_op jit(solution)/shard_map/ppermute | solution.py:827
  124.9 114.3 %collective-permute-start.28 = (bf16[832,1024]{1,0:T(8,128)(2,1)S(1)}, bf16[832,1024]{1,0:T(8,128)(2,1)}, u32[]{:S(2)}, u32[]{:S(2)}) collective-permute-start(bf16[832,1024]{1,0:T(8,128)(2,1)S(1)} %get-tuple-element.216), channel_id=1, source_target_pairs={{0,1},{1,0},{2,3},{3,2},{4,5},{5,4},{6,7},{7,6},{8,9},{9,8},{10,11... | collective-permute-start | bytes 5111816 | tf_op jit(solution)/shard_map/ppermute | solution.py:827
  189.2 217.2 %collective-permute-start.47 = (bf16[832,1024]{1,0:T(8,128)(2,1)}, bf16[832,1024]{1,0:T(8,128)(2,1)}, u32[]{:S(2)}, u32[]{:S(2)}) collective-permute-start(bf16[832,1024]{1,0:T(8,128)(2,1)} %get-tuple-element.253), channel_id=1, source_target_pairs={{0,1},{1,0},{2,3},{3,2},{4,5},{5,4},{6,7},{7,6},{8,9},{9,8},{10,11... | collective-permute-start | bytes 5111816 | tf_op jit(solution)/shard_map/ppermute | solution.py:827
  204.7 11.4 %collective-permute-start.21 = (bf16[832,1024]{1,0:T(8,128)(2,1)S(1)}, bf16[832,1024]{1,0:T(8,128)(2,1)S(1)}, u32[]{:S(2)}, u32[]{:S(2)}) collective-permute-start(bf16[832,1024]{1,0:T(8,128)(2,1)S(1)} %copy-done.129), channel_id=1, source_target_pairs={{0,1},{1,0},{2,3},{3,2},{4,5},{5,4},{6,7},{7,6},{8,9},{9,8},{10,11... | collective-permute-start | bytes 5111816 | tf_op jit(solution)/shard_map/ppermute | solution.py:827
  204.7 48.2 %collective-permute-start.20 = (bf16[1024,1024]{1,0:T(8,128)(2,1)}, bf16[1024,1024]{1,0:T(8,128)(2,1)S(1)}, u32[]{:S(2)}, u32[]{:S(2)}) collective-permute-start(bf16[1024,1024]{1,0:T(8,128)(2,1)} %convolution_convert_fusion.1), channel_id=1, source_target_pairs={{0,2},{2,0},{1,3},{3,1},{4,6},{6,4},{5,7},{7,5},{8,10},{10,8},{9,1... | collective-permute-start | bytes 6291464 | tf_op jit(solution)/shard_map/ppermute | solution.py:830
  238.9 4.7 collective-permute-start.29
  242.0 21.4 %collective-permute-start.25 = (bf16[832,1024]{1,0:T(8,128)(2,1)S(1)}, bf16[832,1024]{1,0:T(8,128)(2,1)S(1)}, u32[]{:S(2)}, u32[]{:S(2)}) collective-permute-start(bf16[832,1024]{1,0:T(8,128)(2,1)S(1)} %get-tuple-element.206), channel_id=1, source_target_pairs={{0,1},{1,0},{2,3},{3,2},{4,5},{5,4},{6,7},{7,6},{8,9},{9,8},{10,11... | collective-permute-start | bytes 5111816 | tf_op jit(solution)/shard_map/ppermute | solution.py:827
  242.4 21.0 %collective-permute-start.26 = (bf16[832,512]{1,0:T(8,128)(2,1)S(1)}, bf16[832,512]{1,0:T(8,128)(2,1)S(1)}, u32[]{:S(2)}, u32[]{:S(2)}) collective-permute-start(bf16[832,512]{1,0:T(8,128)(2,1)S(1)} %slice.147), channel_id=1, source_target_pairs={{0,1},{1,0},{2,3},{3,2},{4,5},{5,4},{6,7},{7,6},{8,9},{9,8},{10,11... | collective-permute-start | bytes 2555912 | tf_op jit(solution)/shard_map/ppermute | solution.py:827
  252.9 6.8 %collective-permute-start.24 = (bf16[832,1024]{1,0:T(8,128)(2,1)S(1)}, bf16[832,1024]{1,0:T(8,128)(2,1)S(1)}, u32[]{:S(2)}, u32[]{:S(2)}) collective-permute-start(bf16[832,1024]{1,0:T(8,128)(2,1)S(1)} %get-tuple-element.204.mine_ref), channel_id=1, source_target_pairs={{0,1},{1,0},{2,3},{3,2},{4,5},{5,4},{6,7},{7,6},{8,9},{9,8},{10,11... | collective-permute-start | bytes 5111816 | tf_op jit(solution)/shard_map/ppermute | solution.py:827
  258.2 27.0 %collective-permute-start.23 = (bf16[512,1024]{1,0:T(8,128)(2,1)}, bf16[512,1024]{1,0:T(8,128)(2,1)S(1)}, u32[]{:S(2)}, u32[]{:S(2)}) collective-permute-start(bf16[512,1024]{1,0:T(8,128)(2,1)} %add_convert_fusion.2), channel_id=1, source_target_pairs={{0,4},{4,0},{8,12},{12,8},{16,20},{20,16},{24,28},{28,24},{1,5},{5... | collective-permute-start | bytes 3145736 | tf_op jit(solution)/shard_map/ppermute | solution.py:833
  259.7 48.1 %collective-permute-start.22 = (bf16[1024,1024]{1,0:T(8,128)(2,1)}, bf16[1024,1024]{1,0:T(8,128)(2,1)}, u32[]{:S(2)}, u32[]{:S(2)}) collective-permute-start(bf16[1024,1024]{1,0:T(8,128)(2,1)} %convolution_convert_fusion), channel_id=1, source_target_pairs={{0,2},{2,0},{1,3},{3,1},{4,6},{6,4},{5,7},{7,5},{8,10},{10,8},{9,1... | collective-permute-start | bytes 6291464 | tf_op jit(solution)/shard_map/ppermute | solution.py:830
  293.2 14.6 %collective-permute-start.27 = (bf16[256,1024]{1,0:T(8,128)(2,1)S(1)}, bf16[256,1024]{1,0:T(8,128)(2,1)S(1)}, u32[]{:S(2)}, u32[]{:S(2)}) collective-permute-start(bf16[256,1024]{1,0:T(8,128)(2,1)S(1)} %dynamic-slice_convert_fusion.1), channel_id=1, source_target_pairs={{0,8},{4,12},{8,0},{12,4},{16,24},{20,28},{24,16},{28,20},{1,9},{5... | collective-permute-start | bytes 1572872 | tf_op jit(solution)/shard_map/ppermute | solution.py:833
  308.8 29.6 %collective-permute-start.33 = (bf16[256,1024]{1,0:T(8,128)(2,1)}, bf16[256,1024]{1,0:T(8,128)(2,1)}, u32[]{:S(2)}, u32[]{:S(2)}) collective-permute-start(bf16[256,1024]{1,0:T(8,128)(2,1)} %add_convert_fusion.9), channel_id=1, source_target_pairs={{0,16},{4,20},{8,24},{12,28},{16,0},{20,4},{24,8},{28,12},{1,17},{... | collective-permute-start | bytes 1572872 | tf_op jit(solution)/shard_map/ppermute | solution.py:833
  314.0 24.5 %collective-permute-start.32 = (bf16[512,1024]{1,0:T(8,128)(2,1)}, bf16[512,1024]{1,0:T(8,128)(2,1)}, u32[]{:S(2)}, u32[]{:S(2)}) collective-permute-start(bf16[512,1024]{1,0:T(8,128)(2,1)} %add_convert_fusion.1), channel_id=1, source_target_pairs={{0,4},{4,0},{8,12},{12,8},{16,20},{20,16},{24,28},{28,24},{1,5},{5... | collective-permute-start | bytes 3145736 | tf_op jit(solution)/shard_map/ppermute | solution.py:833
  336.5 37.4 %collective-permute-start.31 = (bf16[3072,256]{1,0:T(8,128)(2,1)S(1)}, bf16[3072,256]{1,0:T(8,128)(2,1)}, u32[]{:S(2)}, u32[]{:S(2)}) collective-permute-start(bf16[3072,256]{1,0:T(8,128)(2,1)S(1)} %copy-done.92), channel_id=1, source_target_pairs={{0,2},{2,0},{1,3},{3,1},{4,6},{6,4},{5,7},{7,5},{8,10},{10,8},{9,1... | collective-permute-start | bytes 4718600 | tf_op jit(solution)/shard_map/ppermute | solution.py:830
  345.6 28.4 %collective-permute-start.36 = (bf16[832,1024]{1,0:T(8,128)(2,1)S(1)}, bf16[832,1024]{1,0:T(8,128)(2,1)S(1)}, u32[]{:S(2)}, u32[]{:S(2)}) collective-permute-start(bf16[832,1024]{1,0:T(8,128)(2,1)S(1)} %first_back.3), channel_id=1, source_target_pairs={{0,1},{1,0},{2,3},{3,2},{4,5},{5,4},{6,7},{7,6},{8,9},{9,8},{10,11... | collective-permute-start | bytes 5111816 | tf_op jit(solution)/shard_map/ppermute | solution.py:827
  347.1 14.8 %collective-permute-start.35 = (bf16[256,1024]{1,0:T(8,128)(2,1)S(1)}, bf16[256,1024]{1,0:T(8,128)(2,1)S(1)}, u32[]{:S(2)}, u32[]{:S(2)}) collective-permute-start(bf16[256,1024]{1,0:T(8,128)(2,1)S(1)} %add_convert_fusion.8), channel_id=1, source_target_pairs={{0,8},{4,12},{8,0},{12,4},{16,24},{20,28},{24,16},{28,20},{1,9},{5... | collective-permute-start | bytes 1572872 | tf_op jit(solution)/shard_map/ppermute | solution.py:833
  350.8 21.9 %collective-permute-start.34 = (bf16[256,1024]{1,0:T(8,128)(2,1)S(1)}, bf16[256,1024]{1,0:T(8,128)(2,1)S(1)}, u32[]{:S(2)}, u32[]{:S(2)}) collective-permute-start(bf16[256,1024]{1,0:T(8,128)(2,1)S(1)} %dynamic-slice_convert_fusion), channel_id=1, source_target_pairs={{0,8},{4,12},{8,0},{12,4},{16,24},{20,28},{24,16},{28,20},{1,9},{5... | collective-permute-start | bytes 1572872 | tf_op jit(solution)/shard_map/ppermute | solution.py:833
  362.3 22.9 %collective-permute-start.41 = (f32[64,1024]{1,0:T(8,128)S(1)}, f32[64,1024]{1,0:T(8,128)S(1)}, u32[]{:S(2)}, u32[]{:S(2)}) collective-permute-start(f32[64,1024]{1,0:T(8,128)S(1)} %copy-done.97), channel_id=1, source_target_pairs={{0,1},{1,0},{2,3},{3,2},{4,5},{5,4},{6,7},{7,6},{8,9},{9,8},{10,11... | collective-permute-start | bytes 786440 | tf_op jit(solution)/shard_map/ppermute | solution.py:827
  372.7 37.3 %collective-permute-start.30 = (bf16[3072,256]{1,0:T(8,128)(2,1)S(1)}, bf16[3072,256]{1,0:T(8,128)(2,1)S(1)}, u32[]{:S(2)}, u32[]{:S(2)}) collective-permute-start(bf16[3072,256]{1,0:T(8,128)(2,1)S(1)} %copy-done.91), channel_id=1, source_target_pairs={{0,2},{2,0},{1,3},{3,1},{4,6},{6,4},{5,7},{7,5},{8,10},{10,8},{9,1... | collective-permute-start | bytes 4718600 | tf_op jit(solution)/shard_map/ppermute | solution.py:830
  375.3 26.9 %collective-permute-start.38 = (bf16[1536,256]{1,0:T(8,128)(2,1)S(1)}, bf16[1536,256]{1,0:T(8,128)(2,1)S(1)}, u32[]{:S(2)}, u32[]{:S(2)}) collective-permute-start(bf16[1536,256]{1,0:T(8,128)(2,1)S(1)} %add_convert_fusion.4), channel_id=1, source_target_pairs={{0,4},{4,0},{8,12},{12,8},{16,20},{20,16},{24,28},{28,24},{1,5},{5... | collective-permute-start | bytes 2359304 | tf_op jit(solution)/shard_map/ppermute | solution.py:833
  377.0 25.2 %collective-permute-start.39 = (bf16[256,1024]{1,0:T(8,128)(2,1)S(1)}, bf16[256,1024]{1,0:T(8,128)(2,1)S(1)}, u32[]{:S(2)}, u32[]{:S(2)}) collective-permute-start(bf16[256,1024]{1,0:T(8,128)(2,1)S(1)} %add_convert_fusion.7), channel_id=1, source_target_pairs={{0,16},{4,20},{8,24},{12,28},{16,0},{20,4},{24,8},{28,12},{1,17},{... | collective-permute-start | bytes 1572872 | tf_op jit(solution)/shard_map/ppermute | solution.py:833
  386.5 30.3 %collective-permute-start.44 = (bf16[512,1024]{1,0:T(8,128)(2,1)S(1)}, bf16[512,1024]{1,0:T(8,128)(2,1)S(1)}, u32[]{:S(2)}, u32[]{:S(2)}) collective-permute-start(bf16[512,1024]{1,0:T(8,128)(2,1)S(1)} %maximum_select_fusion.11), channel_id=1, source_target_pairs={{0,4},{4,0},{8,12},{12,8},{16,20},{20,16},{24,28},{28,24},{1,5},{5... | collective-permute-start | bytes 3145736 | tf_op jit(solution)/shard_map/ppermute | solution.py:833
  402.3 13.1 %collective-permute-start.46 = (bf16[64,1024]{1,0:T(8,128)(2,1)S(1)}, bf16[64,1024]{1,0:T(8,128)(2,1)S(1)}, u32[]{:S(2)}, u32[]{:S(2)}) collective-permute-start(bf16[64,1024]{1,0:T(8,128)(2,1)S(1)} %add_convert_fusion.16), channel_id=1, source_target_pairs={{0,2},{2,0},{1,3},{3,1},{4,6},{6,4},{5,7},{7,5},{8,10},{10,8},{9,1... | collective-permute-start | bytes 393224 | tf_op jit(solution)/shard_map/ppermute | solution.py:830
  403.3 21.0 %collective-permute-start.43 = (bf16[256,1024]{1,0:T(8,128)(2,1)S(1)}, bf16[256,1024]{1,0:T(8,128)(2,1)S(1)}, u32[]{:S(2)}, u32[]{:S(2)}) collective-permute-start(bf16[256,1024]{1,0:T(8,128)(2,1)S(1)} %add_convert_fusion.6), channel_id=1, source_target_pairs={{0,8},{4,12},{8,0},{12,4},{16,24},{20,28},{24,16},{28,20},{1,9},{5... | collective-permute-start | bytes 1572872 | tf_op jit(solution)/shard_map/ppermute | solution.py:833
  406.4 8.9 %collective-permute-start.45 = (f32[8,1024]{1,0:T(8,128)S(1)}, f32[8,1024]{1,0:T(8,128)S(1)}, u32[]{:S(2)}, u32[]{:S(2)}) collective-permute-start(f32[8,1024]{1,0:T(8,128)S(1)} %add.265), channel_id=1, source_target_pairs={{0,2},{2,0},{1,3},{3,1},{4,6},{6,4},{5,7},{7,5},{8,10},{10,8},{9,1... | collective-permute-start | bytes 98312 | tf_op jit(solution)/shard_map/ppermute | solution.py:830
  410.0 14.3 %collective-permute-start.42 = (bf16[768,256]{1,0:T(8,128)(2,1)S(1)}, bf16[768,256]{1,0:T(8,128)(2,1)S(1)}, u32[]{:S(2)}, u32[]{:S(2)}) collective-permute-start(bf16[768,256]{1,0:T(8,128)(2,1)S(1)} %dynamic-slice_convert_fusion.3), channel_id=1, source_target_pairs={{0,8},{4,12},{8,0},{12,4},{16,24},{20,28},{24,16},{28,20},{1,9},{5... | collective-permute-start | bytes 1179656 | tf_op jit(solution)/shard_map/ppermute | solution.py:833
  425.5 40.7 %collective-permute-start.49 = (bf16[1536,256]{1,0:T(8,128)(2,1)}, bf16[1536,256]{1,0:T(8,128)(2,1)}, u32[]{:S(2)}, u32[]{:S(2)}) collective-permute-start(bf16[1536,256]{1,0:T(8,128)(2,1)} %add_convert_fusion.3), channel_id=1, source_target_pairs={{0,4},{4,0},{8,12},{12,8},{16,20},{20,16},{24,28},{28,24},{1,5},{5... | collective-permute-start | bytes 2359304 | tf_op jit(solution)/shard_map/ppermute | solution.py:833
  427.4 38.7 %collective-permute-start.50 = (bf16[768,256]{1,0:T(8,128)(2,1)S(1)}, bf16[768,256]{1,0:T(8,128)(2,1)S(1)}, u32[]{:S(2)}, u32[]{:S(2)}) collective-permute-start(bf16[768,256]{1,0:T(8,128)(2,1)S(1)} %add_convert_fusion.13), channel_id=1, source_target_pairs={{0,16},{4,20},{8,24},{12,28},{16,0},{20,4},{24,8},{28,12},{1,17},{... | collective-permute-start | bytes 1179656 | tf_op jit(solution)/shard_map/ppermute | solution.py:833
  428.8 45.4 %collective-permute-start.48 = (bf16[512,1024]{1,0:T(8,128)(2,1)}, bf16[512,1024]{1,0:T(8,128)(2,1)}, u32[]{:S(2)}, u32[]{:S(2)}) collective-permute-start(bf16[512,1024]{1,0:T(8,128)(2,1)} %pad_maximum_fusion.9), channel_id=1, source_target_pairs={{0,2},{2,0},{1,3},{3,1},{4,6},{6,4},{5,7},{7,5},{8,10},{10,8},{9,1... | collective-permute-start | bytes 3145736 | tf_op jit(solution)/shard_map/ppermute | solution.py:830
  433.2 41.1 %collective-permute-start.58 = (bf16[512,1024]{1,0:T(8,128)(2,1)}, bf16[512,1024]{1,0:T(8,128)(2,1)}, u32[]{:S(2)}, u32[]{:S(2)}) collective-permute-start(bf16[512,1024]{1,0:T(8,128)(2,1)} %maximum_select_fusion.12), channel_id=1, source_target_pairs={{0,4},{4,0},{8,12},{12,8},{16,20},{20,16},{24,28},{28,24},{1,5},{5... | collective-permute-start | bytes 3145736 | tf_op jit(solution)/shard_map/ppermute | solution.py:833
  434.7 31.5 %collective-permute-start.51 = (f32[8,1024]{1,0:T(8,128)S(1)}, f32[8,1024]{1,0:T(8,128)S(1)}, u32[]{:S(2)}, u32[]{:S(2)}) collective-permute-start(f32[8,1024]{1,0:T(8,128)S(1)} %add.273), channel_id=1, source_target_pairs={{0,4},{4,0},{8,12},{12,8},{16,20},{20,16},{24,28},{28,24},{1,5},{5... | collective-permute-start | bytes 98312 | tf_op jit(solution)/shard_map/ppermute | solution.py:833
  466.3 17.2 %collective-permute-start.53 = (bf16[768,256]{1,0:T(8,128)(2,1)S(1)}, bf16[768,256]{1,0:T(8,128)(2,1)}, u32[]{:S(2)}, u32[]{:S(2)}) collective-permute-start(bf16[768,256]{1,0:T(8,128)(2,1)S(1)} %add_convert_fusion.12), channel_id=1, source_target_pairs={{0,8},{4,12},{8,0},{12,4},{16,24},{20,28},{24,16},{28,20},{1,9},{5... | collective-permute-start | bytes 1179656 | tf_op jit(solution)/shard_map/ppermute | solution.py:833
  469.5 13.9 %collective-permute-start.52 = (bf16[768,256]{1,0:T(8,128)(2,1)S(1)}, bf16[768,256]{1,0:T(8,128)(2,1)S(1)}, u32[]{:S(2)}, u32[]{:S(2)}) collective-permute-start(bf16[768,256]{1,0:T(8,128)(2,1)S(1)} %dynamic-slice_convert_fusion.2), channel_id=1, source_target_pairs={{0,8},{4,12},{8,0},{12,4},{16,24},{20,28},{24,16},{28,20},{1,9},{5... | collective-permute-start | bytes 1179656 | tf_op jit(solution)/shard_map/ppermute | solution.py:833
  471.8 11.6 %collective-permute-start.54 = (f32[8,1024]{1,0:T(8,128)S(1)}, f32[8,1024]{1,0:T(8,128)S(1)}, u32[]{:S(2)}, u32[]{:S(2)}) collective-permute-start(f32[8,1024]{1,0:T(8,128)S(1)} %add.276), channel_id=1, source_target_pairs={{0,8},{4,12},{8,0},{12,4},{16,24},{20,28},{24,16},{28,20},{1,9},{5... | collective-permute-start | bytes 98312 | tf_op jit(solution)/shard_map/ppermute | solution.py:833
  484.9 21.2 %collective-permute-start.55 = (bf16[256,1024]{1,0:T(8,128)(2,1)S(1)}, bf16[256,1024]{1,0:T(8,128)(2,1)S(1)}, u32[]{:S(2)}, u32[]{:S(2)}) collective-permute-start(bf16[256,1024]{1,0:T(8,128)(2,1)S(1)} %add_convert_fusion.5), channel_id=1, source_target_pairs={{0,4},{4,0},{8,12},{12,8},{16,20},{20,16},{24,28},{28,24},{1,5},{5... | collective-permute-start | bytes 1572872 | tf_op jit(solution)/shard_map/ppermute | solution.py:833
  485.6 20.5 %collective-permute-start.56 = (bf16[768,256]{1,0:T(8,128)(2,1)S(1)}, bf16[768,256]{1,0:T(8,128)(2,1)S(1)}, u32[]{:S(2)}, u32[]{:S(2)}) collective-permute-start(bf16[768,256]{1,0:T(8,128)(2,1)S(1)} %add_convert_fusion.11), channel_id=1, source_target_pairs={{0,16},{4,20},{8,24},{12,28},{16,0},{20,4},{24,8},{28,12},{1,17},{... | collective-permute-start | bytes 1179656 | tf_op jit(solution)/shard_map/ppermute | solution.py:833
  495.1 11.0 %collective-permute-start.57 = (f32[8,1024]{1,0:T(8,128)S(1)}, f32[8,1024]{1,0:T(8,128)S(1)}, u32[]{:S(2)}, u32[]{:S(2)}) collective-permute-start(f32[8,1024]{1,0:T(8,128)S(1)} %add.277), channel_id=1, source_target_pairs={{0,16},{4,20},{8,24},{12,28},{16,0},{20,4},{24,8},{28,12},{1,17},{... | collective-permute-start | bytes 98312 | tf_op jit(solution)/shard_map/ppermute | solution.py:833
  496.7 30.8 %collective-permute-start.62 = (bf16[1536,256]{1,0:T(8,128)(2,1)S(1)}, bf16[1536,256]{1,0:T(8,128)(2,1)}, u32[]{:S(2)}, u32[]{:S(2)}) collective-permute-start(bf16[1536,256]{1,0:T(8,128)(2,1)S(1)} %maximum_select_fusion.14), channel_id=1, source_target_pairs={{0,4},{4,0},{8,12},{12,8},{16,20},{20,16},{24,28},{28,24},{1,5},{5... | collective-permute-start | bytes 2359304 | tf_op jit(solution)/shard_map/ppermute | solution.py:833
  506.2 17.2 %collective-permute-start.60 = (bf16[768,256]{1,0:T(8,128)(2,1)S(1)}, bf16[768,256]{1,0:T(8,128)(2,1)S(1)}, u32[]{:S(2)}, u32[]{:S(2)}) collective-permute-start(bf16[768,256]{1,0:T(8,128)(2,1)S(1)} %add_convert_fusion.10), channel_id=1, source_target_pairs={{0,8},{4,12},{8,0},{12,4},{16,24},{20,28},{24,16},{28,20},{1,9},{5... | collective-permute-start | bytes 1179656 | tf_op jit(solution)/shard_map/ppermute | solution.py:833
  507.6 15.1 %collective-permute-start.59 = (bf16[128,1024]{1,0:T(8,128)(2,1)S(1)}, bf16[128,1024]{1,0:T(8,128)(2,1)S(1)}, u32[]{:S(2)}, u32[]{:S(2)}) collective-permute-start(bf16[128,1024]{1,0:T(8,128)(2,1)S(1)} %dynamic-slice_convert_fusion.4), channel_id=1, source_target_pairs={{0,8},{4,12},{8,0},{12,4},{16,24},{20,28},{24,16},{28,20},{1,9},{5... | collective-permute-start | bytes 786440 | tf_op jit(solution)/shard_map/ppermute | solution.py:833
  523.7 26.3 %collective-permute-start.65 = (bf16[1536,256]{1,0:T(8,128)(2,1)S(1)}, bf16[1536,256]{1,0:T(8,128)(2,1)S(1)}, u32[]{:S(2)}, u32[]{:S(2)}) collective-permute-start(bf16[1536,256]{1,0:T(8,128)(2,1)S(1)} %maximum_select_fusion.15), channel_id=1, source_target_pairs={{0,4},{4,0},{8,12},{12,8},{16,20},{20,16},{24,28},{28,24},{1,5},{5... | collective-permute-start | bytes 2359304 | tf_op jit(solution)/shard_map/ppermute | solution.py:833
  526.3 13.4 %collective-permute-start.61 = (bf16[128,1024]{1,0:T(8,128)(2,1)S(1)}, bf16[128,1024]{1,0:T(8,128)(2,1)S(1)}, u32[]{:S(2)}, u32[]{:S(2)}) collective-permute-start(bf16[128,1024]{1,0:T(8,128)(2,1)S(1)} %add_convert_fusion.15), channel_id=1, source_target_pairs={{0,16},{4,20},{8,24},{12,28},{16,0},{20,4},{24,8},{28,12},{1,17},{... | collective-permute-start | bytes 786440 | tf_op jit(solution)/shard_map/ppermute | solution.py:833
  539.8 8.3 %collective-permute-start.63 = (bf16[128,1024]{1,0:T(8,128)(2,1)S(1)}, bf16[128,1024]{1,0:T(8,128)(2,1)S(1)}, u32[]{:S(2)}, u32[]{:S(2)}) collective-permute-start(bf16[128,1024]{1,0:T(8,128)(2,1)S(1)} %add_convert_fusion.14), channel_id=1, source_target_pairs={{0,8},{4,12},{8,0},{12,4},{16,24},{20,28},{24,16},{28,20},{1,9},{5... | collective-permute-start | bytes 786440 | tf_op jit(solution)/shard_map/ppermute | solution.py:833
  548.2 13.0 %collective-permute-start.64 = (bf16[256,1024]{1,0:T(8,128)(2,1)S(1)}, bf16[256,1024]{1,0:T(8,128)(2,1)S(1)}, u32[]{:S(2)}, u32[]{:S(2)}) collective-permute-start(bf16[256,1024]{1,0:T(8,128)(2,1)S(1)} %maximum_select_fusion.16), channel_id=1, source_target_pairs={{0,4},{4,0},{8,12},{12,8},{16,20},{20,16},{24,28},{28,24},{1,5},{5... | collective-permute-start | bytes 1572872 | tf_op jit(solution)/shard_map/ppermute | solution.py:833
  (139 other events, 1135.9 us)

commit v4 on v3

--- a/solution.py
+++ b/solution.py
@@ -341,8 +341,8 @@
     return pl.BlockSpec((block, width), lambda i, s: (i, 0))
 
 
-def cost(flops, moved):
-    return pl.CostEstimate(flops=int(flops), bytes_accessed=int(moved), transcendentals=0)
+def brief():
+    return pl.CostEstimate(flops=1000, bytes_accessed=1000, transcendentals=0)
 
 
 def params(mib):
@@ -398,7 +398,7 @@
         ),
         out_shape=[shape((2 * rows, wide), ROUND)] * count,
         compiler_params=params(32),
-        cost_estimate=cost(4 * rows * depth * wide * count, 8e6),
+        cost_estimate=brief(),
         name="project",
     )(where, mine, other, weights)
 
@@ -462,7 +462,7 @@
         ),
         out_shape=[shape((span, wide), ROUND), shape((pairs, 8, span), FULL)],
         compiler_params=params(40),
-        cost_estimate=cost(16e9, 4e6),
+        cost_estimate=brief(),
         name="self_forward",
     )(limit, q, k, v)
 
@@ -544,7 +544,7 @@
         ),
         out_shape=[shape((span, wide), ROUND)] * 3,
         compiler_params=params(48),
-        cost_estimate=cost(20e9, 6e6),
+        cost_estimate=brief(),
         name="self_back",
     )(limit, q, k, v, o, do, lse)
 
@@ -612,7 +612,7 @@
         ),
         out_shape=[shape((rows, width), FULL)] * 2 + [shape((rows, width), ROUND)] * 4,
         compiler_params=params(40),
-        cost_estimate=cost(7e9, 25e6),
+        cost_estimate=brief(),
         name="middle_forward",
     )(where, frames, *attended, *received, gains, biases, *wo, *wq, *ck, *cv, *wc)
 
@@ -659,7 +659,7 @@
         out_shape=[shape((2 * rows, hidden), ROUND)] * 2 + [shape((rows, width), kind)] * 2,
         input_output_aliases={at: 0, at + 1: 1} if shared else {},
         compiler_params=params(56),
-        cost_estimate=cost(8 * rows * width * hidden, 20e6),
+        cost_estimate=brief(),
         name="feed",
     )(where, h, d, up, down, *before, *shared)
 
@@ -740,7 +740,7 @@
         + [shape((4, 64, 256), FULL)] * 2
         + [shape((8, width), FULL)],
         compiler_params=params(40),
-        cost_estimate=cost(7e9, 25e6),
+        cost_estimate=brief(),
         name="middle_back",
     )(where, ym, yr, x1, x2, d, cq, gains, *wq, *ck, *cv, *wc)
 
@@ -772,7 +772,7 @@
         ),
         out_shape=shape((rows, width), kind),
         compiler_params=params(24),
-        cost_estimate=cost(2 * rows * width * 1536, 8e6),
+        cost_estimate=brief(),
         name="first_back",
     )(half, *grads, *weights)
 
@@ -803,7 +803,7 @@
         ),
         out_shape=[shape((rows, width), ROUND), shape((8, width), FULL)],
         compiler_params=params(24),
-        cost_estimate=cost(1e7, 12e6),
+        cost_estimate=brief(),
         name="frames_back",
     )(where, ym, yr, dx1, frames, gains)
 
@@ -939,19 +939,25 @@
     def plus(a, b):
         return lower(a.astype(FULL) + b.astype(FULL))
 
+    across = (column, X_PAIRS)
+    down_z = (near, Z_NEAR)
+
     class Sum:
-        def __init__(self, partner):
+        def __init__(self, partner, order=(across, down_z)):
+            self.order = order
             self.fly = over_y(partner)
 
-        def x(self, own):
-            away_half = lower(half_of(own, 1 - column) + half_of(self.fly, 1 - column).astype(FULL))
-            self.kept = half_of(own, column) + half_of(self.fly, column).astype(FULL)
-            self.fly = along_wide(away_half, X_PAIRS)
-
-        def near(self):
+        def first(self, own):
+            which, pairs = self.order[0]
+            away_half = lower(half_of(own, 1 - which) + half_of(self.fly, 1 - which).astype(FULL))
+            self.kept = half_of(own, which) + half_of(self.fly, which).astype(FULL)
+            self.fly = along_wide(away_half, pairs)
+
+        def second(self):
+            which, pairs = self.order[1]
             total = self.kept + self.fly.astype(FULL)
-            self.kept = half_of(total, near)
-            self.fly = along_wide(lower(half_of(total, 1 - near)), Z_NEAR)
+            self.kept = half_of(total, which)
+            self.fly = along_wide(lower(half_of(total, 1 - which)), pairs)
 
         def far(self):
             self.kept = plus(self.kept, self.fly)
@@ -959,23 +965,32 @@
 
         def back(self):
             self.kept = plus(self.kept, self.fly)
-            self.fly = along_wide(self.kept, Z_NEAR)
+            self.fly = along_wide(self.kept, self.order[1][1])
 
         def along(self):
-            self.kept = ordered(self.kept, self.fly, near)
-            self.fly = along_wide(self.kept, X_PAIRS)
+            self.kept = ordered(self.kept, self.fly, self.order[1][0])
+            self.fly = along_wide(self.kept, self.order[0][1])
 
         def end(self):
-            return ordered(self.kept, self.fly, column).astype(FULL)
-
-    def sync(sums_in_flight, *values):
-        done = join((*[each.fly for each in sums_in_flight], *values))
-        for each, fly in zip(sums_in_flight, done):
+            return ordered(self.kept, self.fly, self.order[0][0]).astype(FULL)
+
+    def sync(in_flight, *values):
+        done = join((*[each.fly for each in in_flight], *values))
+        for each, fly in zip(in_flight, done):
             each.fly = fly
-        return done[len(sums_in_flight) :]
+        return done[len(in_flight) :]
+
+    class Row:
+        def __init__(self, value, step):
+            self.kept = value
+            self.fly = step(value)
+
+        def then(self, step):
+            self.kept = self.kept + self.fly
+            self.fly = step(self.kept)
 
     up1 = lower(tn(h3_rows, du1))
-    up1, g1 = join((up1, g1))
+    up1, g1, du0, g0 = join((up1, g1, du0, g0))
     up = Sum(up1)
     down1 = lower(tn(g1, dout_rows))
     up0 = tn(h3_rows, du0)
@@ -983,25 +998,25 @@
     dx1, dself, dcross, dcq, dck, dcv, sums = middle_back(
         where, y_m, y_received, x1, x2, dout, cq, norm_gain, wq, ck, cv, wc
     )
-    dself, down1, up0, down0 = sync([up], dself, down1, up0, down0)
-
-    down = Sum(down1)
-    up.x(up0)
+    dself, dcross, dcq, down1, up0, down0 = sync([up], dself, dcross, dcq, down1, up0, down0)
+
+    down = Sum(down1, (down_z, across))
+    up.first(up0)
     dself_other = over_core(dself)
+    do0, do1 = project(where, dself, dself_other, jnp.stack([w_out, out_y]), True)
     dcross_other = over_core(dcross)
     dcq_other = over_core(dcq[:, 512:])
     d_pair = jnp.stack([dck, dcv], axis=1)
-    d_pair = lower(d_pair[:2] + over_core(d_pair[2:]))
-    do0, do1 = project(where, dself, dself_other, jnp.stack([w_out, out_y]), True)
-    do1, dcross_other, dcq_other = join((do1, dcross_other, dcq_other))
+    d_pair_other = over_core(d_pair[2:])
     dq1, dk1, dv1 = self_back(limit, q1, k1, v1, o1, do1, lse1)
-    dq1, dcross_other = sync([up], dq1, dcross_other)
-
-    up.near()
+    dq1, dcross_other, dcq_other, d_pair_other = sync(
+        [up], dq1, dcross_other, dcq_other, d_pair_other
+    )
+
+    up.second()
+    d_pair = lower(d_pair[:2] + d_pair_other)
     h1_rows = ordered(h1, h1_other, core)
     qkv1 = lower(jnp.concatenate([tn(h1_rows, g) for g in (dq1, dk1, dv1)], axis=0))
-    dself_rows = ordered(dself, dself_other, core)
-    dcross_rows = jnp.concatenate([dcross, dcross_other], axis=0)
     h2_rows = jnp.concatenate([h2, h2_other], axis=0)
 
     def both(mine, other, g):
@@ -1020,91 +1035,93 @@
         )
 
     into1 = lower(into(1))
-    qkv1, into1, do0 = sync([down, up], qkv1, into1, do0)
+    qkv1, into1, do0, dself, dcross = sync([down, up], qkv1, into1, do0, dself, dcross)
 
     qkv = Sum(qkv1)
-    down.x(down0)
+    down.first(down0)
     up.far()
     dq0, dk0, dv0 = self_back(limit, q0, k0, v0, o0, do0, lse0)
-    dq0, dself_rows, dcross_rows = sync([down, up], dq0, dself_rows, dcross_rows)
-
-    down.near()
-    up.back()
+    dself_rows = ordered(dself, dself_other, core)
+    dcross_rows = jnp.concatenate([dcross, dcross_other], axis=0)
     grads = (dq0, dk0, dv0, dq1, dk1, dv1)
     yo = first_back(away, grads, (w_qkv, qkv_y), ROUND)
+    dq0, dself_rows, dcross_rows, yo = sync([down, up], dq0, dself_rows, dcross_rows, yo)
+
+    down.second()
+    up.back()
     y_received = over_core(yo)
     qkv0 = jnp.concatenate([tn(h1_rows, g) for g in (dq0, dk0, dv0)], axis=0)
+    grads = (dq0, dk0, dv0, dq1, dk1, dv1)
+    ym = first_back(where, grads, (w_qkv, qkv_y), FULL)
     outof1 = lower(outof(1, o1))
-    ym = first_back(where, grads, (w_qkv, qkv_y), FULL)
-    qkv0, ym, y_received, outof1 = sync([qkv, down, up], qkv0, ym, y_received, outof1)
+    qkv0, ym, y_received, outof1, x2 = sync(
+        [qkv, down, up], qkv0, ym, y_received, outof1, x2
+    )
 
     cross_in = Sum(into1)
-    qkv.x(qkv0)
+    qkv.first(qkv0)
     down.far()
     up.along()
     grad_frames, first_sums = frames_back(where, ym, y_received, dx1, frames, norm_gain)
-    sums = sums + first_sums
-    sums_other = over_core(sums)
+    norms = Row(sums + first_sums, over_core)
     into0 = into(0)
     outof0 = outof(0, o0)
     text_part = 0.0
     for g, weights in ((0, w_cross_kv), (1, cross_kv_y)):
         for c in range(2):
             text_part = text_part + nt(d_pair[g, c], weights[c])
-    text_other = over_core(text_part)
-    sums_other, text_other, into0, outof0, grad_frames = sync(
-        [qkv, down], sums_other, text_other, into0, outof0, grad_frames
-    )
-
-    qkv.near()
+    texts = Row(text_part, over_core)
+    out_rows = lower(x2 + out_m + over_core(out_o).astype(FULL))
+    into0, outof0, grad_frames, out_rows = sync(
+        [qkv, down, norms, texts], into0, outof0, grad_frames, out_rows
+    )
+
+    qkv.second()
     down.back()
-    sums = sums + sums_other
-    sums_other = over_y(sums)
-    text_grad = lower(text_part + text_other)
+    norms.then(over_y)
+    text_grad = lower(texts.kept + texts.fly)
+    (outof1,) = sync([cross_in, norms], outof1)
+
+    outs = Sum(outof1)
+    cross_in.first(into0)
+    norms.then(lambda v: along_wide(v, X_PAIRS))
     text_away = over_y(text_grad)
-    out_rows = lower(x2 + out_m + over_core(out_o).astype(FULL))
-    sums_other, text_away, out_rows = sync(
-        [cross_in, qkv, down, up], sums_other, text_away, out_rows
-    )
-
-    outs = Sum(outof1)
-    cross_in.x(into0)
+    (text_away,) = sync([qkv, down, up], text_away)
+
     qkv.far()
     down.along()
-    sums = sums + sums_other
-    sums_other = along_wide(sums, X_PAIRS)
     grad_up = up.end()
-    sums_other, grad_up = sync([cross_in, qkv], sums_other, grad_up)
-
-    cross_in.near()
+    grad_text = ordered(text_grad[None], text_away[None], side)
+    grad_up, grad_text = sync([outs, cross_in, norms], grad_up, grad_text)
+
+    outs.first(outof0)
+    cross_in.second()
+    norms.then(lambda v: along_wide(v, Z_NEAR))
+    sync([qkv, down])
+
     qkv.back()
-    sums = sums + sums_other
-    sums_other = along_wide(sums, Z_NEAR)
-    grad_text = ordered(text_grad[None], text_away[None], side)
-    sums_other, grad_text = sync([outs, cross_in, qkv], sums_other, grad_text)
-
-    outs.x(outof0)
+    grad_down = down.end()
+    (grad_down,) = sync([outs, cross_in, norms], grad_down)
+
+    outs.second()
     cross_in.far()
+    norms.then(lambda v: along_wide(v, Z_FAR))
+    sync([qkv, outs])
+
     qkv.along()
-    sums = sums + sums_other
-    sums_other = along_wide(sums, Z_FAR)
-    (down.fly,) = join((down.fly,))
-    grad_down = down.end()
-    sums_other, grad_down = sync([outs, cross_in], sums_other, grad_down)
-
-    outs.near()
+    outs.far()
+    sync([cross_in, norms])
+
     cross_in.back()
-    sums = sums + sums_other
-    sync([outs, cross_in])
-
-    outs.far()
+    sums = norms.kept + norms.fly
+    sync([outs])
+
+    outs.back()
+    sync([cross_in, qkv])
+
     cross_in.along()
     grad_qkv = qkv.end().reshape(3, width, 256)
-    (grad_qkv,) = sync([outs], grad_qkv)
-
-    outs.back()
     sync([outs])
-
     outs.along()
     grad_cross_in = cross_in.end()
     grad_outs = outs.end()

time: 567 us -> 614 us (1.083)
  waiting for transfers between devices: 145 us -> 166 us
  local copies, waits for them, and re-layouts: 38.9 us -> 57.6 us
    ppermute x12, waiting for transfers between devices: 12.6 us -> 60 us  [over_y(): return lax.ppermute(v, 'narrow', Y_PAIRS)]
    ppermute x33, waiting for transfers between devices: 131 us -> 106 us  [along_wide(): return lax.ppermute(v, 'wide', pairs)]
    unnamed x273 -> x249, local copies, waits for them, and re-layouts: 20.5 us -> 28 us
  transfers between devices with their start and end apart: 66 -> 66, of which waited for: 22 -> 20; matrix products, arithmetic and copies ran while one was open for 25% -> 26% of each run, Pallas kernels for 35% -> 32%
where the time goes in v4:
time: 614 us; the launch traced here: 610 us
  Pallas kernels  195 us (32%)
  waiting for transfers between devices  166 us (27%)
  other arithmetic  83 us (14%)
  local copies, waits for them, and re-layouts  57.6 us (9%)
  starting transfers between devices  55.4 us (9%)
  matrix products  50.4 us (8%)
    ppermute x33, waiting for transfers between devices, along_wide(): return lax.ppermute(v, 'wide', pairs)  106 us
    ppermute x12, waiting for transfers between devices, over_y(): return lax.ppermute(v, 'narrow', Y_PAIRS)  60 us
    pallas_call x4, Pallas kernels, feed(): pl.pallas_call(functools.partial(feed_kernel, carried=carried, shared=1 i...  54.4 us
    dot_general x20, matrix products, tn(): lax.dot_general(a, b, (((0,), (0,)), ((), ())), preferred_element_type=FULL)  47.2 us
    pallas_call x2, Pallas kernels, self_back(): pl.pallas_call(functools.partial(self_back_kernel, span=span, floor=floor...  40.6 us
    ppermute x33, starting transfers between devices, along_wide(): return lax.ppermute(v, 'wide', pairs)  35.3 us
    pallas_call x2, Pallas kernels, self_forward(): pl.pallas_call(functools.partial(self_forward_kernel, span=span, floor=fl...  31.2 us
    select_n x14, other arithmetic, ordered(): jnp.where(which == 0, jnp.concatenate([first, second], axis=0), jnp.conca...  29 us
  transfers between devices with their start and end apart: 66, of which 20 were waited for; matrix products, arithmetic and copies ran while one was open for 26% of the time, Pallas kernels for 32%

profile of v4, /device:TPU:0, one launch (start us, length us, event | category | flops | bytes accessed | tf_op | source)
XLA Modules:
  0.0 610.0 jit_solution(14967757336953839514)
XLA Ops:
  0.7 1.9 convert_reduce_fusion
  3.4 1.9 fusion.5.mine_ref
  6.6 2.5 collective-permute-start.1
  14.2 5.5 project.3
  22.5 5.2 collective-permute-done.1
  29.5 2.1 constant_dynamic-slice_fusion.4
  33.9 1.9 constant_dynamic-slice_fusion.5
  38.6 15.6 %self_forward.2 = (bf16[1664,256]{1,0:T(8,128)(2,1)S(1)}, f32[2,8,1664]{2,1,0:T(8,128)S(1)}) custom-call(s32[1]{0:T(128)} %dynamic_slice.117.limit_ref, bf16[1664,256]{1,0:T(8,128)(2,1)S(1)} %copy-done.32, bf16[1664,256]{1,0:T(8,128)(2,1)S(1)} %copy-done.35, bf16[1664,256]{1,0:T(8,128)(2,1)S(1)} %copy-done.38), custom_call_target="tpu_custom_call" | custom-call | flops 1000 | bytes 1000 | tf_op jit(solution)/shard_map/self_forward/pallas_call | solution.py:455
  55.9 2.3 maximum_select_fusion.6
  58.2 5.3 project.4
  77.6 15.6 %self_forward.3 = (bf16[1664,256]{1,0:T(8,128)(2,1)S(1)}, f32[2,8,1664]{2,1,0:T(8,128)S(1)}) custom-call(s32[1]{0:T(128)} %dynamic_slice.117.limit_ref, bf16[1664,256]{1,0:T(8,128)(2,1)S(1)} %copy-done.41, bf16[1664,256]{1,0:T(8,128)(2,1)S(1)} %copy-done.44, bf16[1664,256]{1,0:T(8,128)(2,1)S(1)} %copy-done.47), custom_call_target="tpu_custom_call" | custom-call | flops 1000 | bytes 1000 | tf_op jit(solution)/shard_map/self_forward/pallas_call | solution.py:455
  95.1 5.7 collective-permute-done.8
  100.8 2.0 maximum_select_fusion.10
  102.9 2.3 maximum_select_fusion.7
  110.5 20.9 %middle_forward.1 = (f32[832,1024]{1,0:T(8,128)}, f32[832,1024]{1,0:T(8,128)}, bf16[832,1024]{1,0:T(8,128)(2,1)S(1)}, bf16[832,1024]{1,0:T(8,128)(2,1)S(1)}, bf1...) custom-call(s32[1]{0:T(128)} %bitcast.where_ref, bf16[832,1024]{1,0:T(8,128)(2,1)} %frame_ref.3, ...), custom_call_target="tpu_custom_call" | custom-call | flops 1000 | bytes 1000 | tf_op jit(solution)/shard_map/middle_forward/pallas_call | solution.py:604
  135.7 2.8 constant_dynamic-update-slice_fusion.2
  138.5 13.2 %feed.4 = (bf16[1664,1024]{1,0:T(8,128)(2,1)}, bf16[1664,1024]{1,0:T(8,128)(2,1)}, f32[832,1024]{1,0:T(8,128)}, f32[832,1024]{1,0:T(8,128)}) custom-call(s32[1]{0:T(128)} %bitcast.where_ref, bf16[832,1024]{1,0:T(8,128)(2,1)} %get-tuple-element.183.h_ref, bf16[832,1024]{1,0:T(8,128)(2,1)} %copy-done.4, bf16[1024,1024]{1,0:T(8,128)(2,1)} %up_ref.3, ...), custom_call_target="tpu_custom_call" | custom-call | flops 1000 | bytes 1000 | tf_op jit(solution)/shard_map/feed/pallas_call | solution.py:649
  154.8 4.6 maximum_select_fusion.2.up_ref
  159.5 13.2 %feed.5 = (bf16[1664,1024]{1,0:T(8,128)(2,1)}, bf16[1664,1024]{1,0:T(8,128)(2,1)}, f32[832,1024]{1,0:T(8,128)}, f32[832,1024]{1,0:T(8,128)}) custom-call(s32[1]{0:T(128)} %bitcast.where_ref, bf16[832,1024]{1,0:T(8,128)(2,1)} %collective-permute-done.17.h_ref, ...), custom_call_target="tpu_custom_call", output_to_operand_aliasing={{0}: (5, {}), {1}: (6, {})} | custom-call | flops 1000 | bytes 1000 | tf_op jit(solution)/shard_map/feed/pallas_call | solution.py:649
  172.6 4.7 maximum_select_fusion.3.down_ref
  177.4 14.3 %feed.6 = (bf16[1664,1024]{1,0:T(8,128)(2,1)}, bf16[1664,1024]{1,0:T(8,128)(2,1)}, f32[832,1024]{1,0:T(8,128)}, f32[832,1024]{1,0:T(8,128)}) custom-call(s32[1]{0:T(128)} %bitcast.where_ref, bf16[832,1024]{1,0:T(8,128)(2,1)} %get-tuple-element.183.h_ref, bf16[832,1024]{1,0:T(8,128)(2,1)} %copy-done.4, bf16[1024,1024]{1,0:T(8,128)(2,1)} %maximum_select_fusion.2.up_ref, ...), custom_call_target="tpu_custom_call" | custom-call | flops 1000 | bytes 1000 | tf_op jit(solution)/shard_map/feed/pallas_call | solution.py:649
  191.7 13.7 %feed.7 = (bf16[1664,1024]{1,0:T(8,128)(2,1)}, bf16[1664,1024]{1,0:T(8,128)(2,1)}, bf16[832,1024]{1,0:T(8,128)(2,1)}, bf16[832,1024]{1,0:T(8,128)(2,1)}) custom-call(s32[1]{0:T(128)} %bitcast.where_ref, bf16[832,1024]{1,0:T(8,128)(2,1)} %collective-permute-done.17.h_ref, ...), custom_call_target="tpu_custom_call", output_to_operand_aliasing={{0}: (7, {}), {1}: (8, {})} | custom-call | flops 1000 | bytes 1000 | tf_op jit(solution)/shard_map/feed/pallas_call | solution.py:649
  205.4 2.9 constant_dynamic-update-slice_fusion
  208.4 7.4 %convolution_convert_fusion.1 = bf16[1024,1024]{1,0:T(8,128)(2,1)} fusion(bf16[1664,1024]{1,0:T(8,128)(2,1)} %constant_dynamic-update-slice_fusion, bf16[1664,1024]{1,0:T(8,128)(2,1)S(1)} %copy-done.95), kind=kOutput, calls=%fused_computation.26 | convolution fusion | flops 3490709504 | bytes 8912896 | tf_op jit(solution)/shard_map/dot_general | solution.py:328
  217.3 5.5 fusion.85
  222.8 7.7 %fusion.86 = f32[1024,1024]{1,0:T(8,128)} fusion(bf16[1664,1024]{1,0:T(8,128)(2,1)S(1)} %copy-done.92, bf16[1664,1024]{1,0:T(8,128)(2,1)} %constant_dynamic-update-slice_fusion.2), kind=kOutput, calls=%fused_computation.203 | convolution fusion | flops 3489660928 | bytes 11010048 | tf_op jit(solution)/shard_map/dot_general | solution.py:328
  230.7 7.4 %convolution_convert_fusion = bf16[1024,1024]{1,0:T(8,128)(2,1)} fusion(bf16[1664,1024]{1,0:T(8,128)(2,1)S(1)} %copy-done.94, bf16[1664,1024]{1,0:T(8,128)(2,1)} %constant_dynamic-update-slice_fusion.2), kind=kOutput, calls=%fused_computation.25 | convolution fusion | flops 3490709504 | bytes 8912896 | tf_op jit(solution)/shard_map/dot_general | solution.py:328
  238.1 22.6 %middle_back.1 = (f32[832,1024]{1,0:T(8,128)}, bf16[832,1024]{1,0:T(8,128)(2,1)S(1)}, bf16[832,1024]{1,0:T(8,128)(2,1)}, bf16[832,1024]{1,0:T(8,128)(2,1)S(1)}, ...) custom-call(s32[1]{0:T(128)} %bitcast.where_ref, ...), custom_call_target="tpu_custom_call" | custom-call | flops 1000 | bytes 1000 | tf_op jit(solution)/shard_map/middle_back/pallas_call | solution.py:729
  260.7 3.5 collective-permute-done.20
  264.7 4.8 maximum_select_fusion
  270.2 2.5 add_convert_fusion.2
  276.4 2.1 fusion.83
  282.5 2.2 project.5
  285.7 20.2 %self_back.2 = (bf16[1664,256]{1,0:T(8,128)(2,1)S(1)}, bf16[1664,256]{1,0:T(8,128)(2,1)S(1)}, bf16[1664,256]{1,0:T(8,128)(2,1)S(1)}) custom-call(s32[1]{0:T(128)} %dynamic_slice.117.limit_ref, bf16[1664,256]{1,0:T(8,128)(2,1)S(1)} %copy-done.42, bf16[1664,256]{1,0:T(8,128)(2,1)S(1)} %copy-done.45, bf16[1664,256]{1,0:T(8,128)(2,1)S(1)} %copy-done.48, ...), custom_call_target="tpu_custom_call" | custom-call | flops 1000 | bytes 1000 | tf_op jit(solution)/shard_map/self_back/pallas_call | solution.py:536
  315.0 2.3 convert_add_fusion.1
  326.6 1.9 pad_maximum_fusion.2
  328.5 25.7 %collective-permute-done.22 = bf16[1024,1024]{1,0:T(8,128)(2,1)S(1)} collective-permute-done((bf16[1024,1024]{1,0:T(8,128)(2,1)}, bf16[1024,1024]{1,0:T(8,128)(2,1)S(1)}, u32[]{:S(2)}, u32[]{:S(2)}) %collective-permute-start.22) | collective-permute-done | bytes 2097184 | tf_op jit(solution)/shard_map/ppermute | solution.py:830
  354.4 2.7 collective-permute-start.32
  360.0 20.4 %self_back.3 = (bf16[1664,256]{1,0:T(8,128)(2,1)S(1)}, bf16[1664,256]{1,0:T(8,128)(2,1)S(1)}, bf16[1664,256]{1,0:T(8,128)(2,1)S(1)}) custom-call(s32[1]{0:T(128)} %dynamic_slice.117.limit_ref, bf16[1664,256]{1,0:T(8,128)(2,1)S(1)} %copy-done.33, bf16[1664,256]{1,0:T(8,128)(2,1)S(1)} %copy-done.36, bf16[1664,256]{1,0:T(8,128)(2,1)S(1)} %copy-done.39, ...), custom_call_target="tpu_custom_call" | custom-call | flops 1000 | bytes 1000 | tf_op jit(solution)/shard_map/self_back/pallas_call | solution.py:536
  380.4 4.2 fusion.88
  386.1 2.1 fusion.89
  388.3 2.4 pad_maximum_fusion
  390.7 4.4 first_back.2
  395.2 1.9 maximum_select_fusion.1
  399.4 4.4 first_back.3.ym_ref
  413.1 4.7 collective-permute-done.34
  420.4 3.9 frames_back.1
  427.1 3.7 add_convert_fusion
  433.8 18.8 %collective-permute-done.38 = bf16[256,1024]{1,0:T(8,128)(2,1)S(1)} collective-permute-done((bf16[256,1024]{1,0:T(8,128)(2,1)S(1)}, bf16[256,1024]{1,0:T(8,128)(2,1)S(1)}, u32[]{:S(2)}, u32[]{:S(2)}) %collective-permute-start.38) | collective-permute-done | bytes 524320 | tf_op jit(solution)/shard_map/ppermute | solution.py:833
  462.6 24.4 %collective-permute-done.50 = bf16[64,1024]{1,0:T(8,128)(2,1)S(1)} collective-permute-done((bf16[64,1024]{1,0:T(8,128)(2,1)S(1)}, bf16[64,1024]{1,0:T(8,128)(2,1)S(1)}, u32[]{:S(2)}, u32[]{:S(2)}) %collective-permute-start.50) | collective-permute-done | bytes 131104 | tf_op jit(solution)/shard_map/ppermute | solution.py:830
  489.1 2.0 maximum_select_fusion.12
  494.4 5.4 fusion.6
  500.5 5.5 collective-permute-done.46
  512.7 12.2 %collective-permute-done.54 = bf16[768,256]{1,0:T(8,128)(2,1)S(1)} collective-permute-done((bf16[768,256]{1,0:T(8,128)(2,1)S(1)}, bf16[768,256]{1,0:T(8,128)(2,1)S(1)}, u32[]{:S(2)}, u32[]{:S(2)}) %collective-permute-start.54) | collective-permute-done | bytes 393248 | tf_op jit(solution)/shard_map/ppermute | solution.py:833
  525.8 2.9 fusion.7
  530.4 4.4 collective-permute-done.53
  540.9 2.7 collective-permute-start.57
  543.6 9.9 %collective-permute-done.59 = bf16[128,1024]{1,0:T(8,128)(2,1)S(1)} collective-permute-done((bf16[128,1024]{1,0:T(8,128)(2,1)S(1)}, bf16[128,1024]{1,0:T(8,128)(2,1)S(1)}, u32[]{:S(2)}, u32[]{:S(2)}) %collective-permute-start.59) | collective-permute-done | bytes 262176 | tf_op jit(solution)/shard_map/ppermute | solution.py:833
  555.8 9.0 %collective-permute-done.57 = f32[8,1024]{1,0:T(8,128)S(1)} collective-permute-done((f32[8,1024]{1,0:T(8,128)S(1)}, f32[8,1024]{1,0:T(8,128)S(1)}, u32[]{:S(2)}, u32[]{:S(2)}) %collective-permute-start.57) | collective-permute-done | bytes 32800 | tf_op jit(solution)/shard_map/ppermute | solution.py:833
  565.0 3.9 collective-permute-done.62
  570.3 8.4 %collective-permute-done.63 = bf16[128,1024]{1,0:T(8,128)(2,1)S(1)} collective-permute-done((bf16[128,1024]{1,0:T(8,128)(2,1)S(1)}, bf16[128,1024]{1,0:T(8,128)(2,1)S(1)}, u32[]{:S(2)}, u32[]{:S(2)}) %collective-permute-start.63) | collective-permute-done | bytes 262176 | tf_op jit(solution)/shard_map/ppermute | solution.py:833
  581.7 1.9 convert.33
  583.6 10.2 %collective-permute-done.64 = bf16[256,1024]{1,0:T(8,128)(2,1)S(1)} collective-permute-done((bf16[256,1024]{1,0:T(8,128)(2,1)S(1)}, bf16[256,1024]{1,0:T(8,128)(2,1)S(1)}, u32[]{:S(2)}, u32[]{:S(2)}) %collective-permute-start.64) | collective-permute-done | bytes 524320 | tf_op jit(solution)/shard_map/ppermute | solution.py:833
  595.7 11.2 %collective-permute-done.65 = bf16[1536,256]{1,0:T(8,128)(2,1)S(1)} collective-permute-done((bf16[1536,256]{1,0:T(8,128)(2,1)S(1)}, bf16[1536,256]{1,0:T(8,128)(2,1)S(1)}, u32[]{:S(2)}, u32[]{:S(2)}) %collective-permute-start.65) | collective-permute-done | bytes 786464 | tf_op jit(solution)/shard_map/ppermute | solution.py:833
  (470 shorter events, 144.0 us)
Async XLA Ops:
  5.2 9.0 %collective-permute-start = (bf16[832,1024]{1,0:T(8,128)(2,1)}, bf16[832,1024]{1,0:T(8,128)(2,1)}, u32[]{:S(2)}, u32[]{:S(2)}) collective-permute-start(bf16[832,1024]{1,0:T(8,128)(2,1)} %fusion.5.mine_ref), channel_id=1, source_target_pairs={{0,1},{1,0},{2,3},{3,2},{4,5},{5,4},{6,7},{7,6},{8,9},{9,8},{10,11... | collective-permute-start | bytes 5111816 | tf_op jit(solution)/shard_map/ppermute | solution.py:827
  6.6 21.0 %collective-permute-start.1 = (bf16[1536,256]{1,0:T(8,128)(2,1)}, bf16[1536,256]{1,0:T(8,128)(2,1)}, u32[]{:S(2)}, u32[]{:S(2)}) collective-permute-start(bf16[1536,256]{1,0:T(8,128)(2,1)} %constant_dynamic-slice_fusion.6), channel_id=1, source_target_pairs={{0,2},{2,0},{1,3},{3,1},{4,6},{6,4},{5,7},{7,5},{8,10},{10,8},{9,1... | collective-permute-start | bytes 2359304 | tf_op jit(solution)/shard_map/ppermute | solution.py:830
  27.7 26.5 %collective-permute-start.2 = (bf16[1536,256]{1,0:T(8,128)(2,1)}, bf16[1536,256]{1,0:T(8,128)(2,1)}, u32[]{:S(2)}, u32[]{:S(2)}) collective-permute-start(bf16[1536,256]{1,0:T(8,128)(2,1)} %collective-permute-done.1), channel_id=1, source_target_pairs={{0,8},{4,12},{8,0},{12,4},{16,24},{20,28},{24,16},{28,20},{1,9},{5... | collective-permute-start | bytes 2359304 | tf_op jit(solution)/shard_map/ppermute | solution.py:833
  29.5 36.8 %collective-permute-start.6 = (bf16[512,1024]{1,0:T(8,128)(2,1)}, bf16[512,1024]{1,0:T(8,128)(2,1)}, u32[]{:S(2)}, u32[]{:S(2)}) collective-permute-start(bf16[512,1024]{1,0:T(8,128)(2,1)} %pad_maximum_fusion.7), channel_id=1, source_target_pairs={{0,1},{1,0},{2,3},{3,2},{4,5},{5,4},{6,7},{7,6},{8,9},{9,8},{10,11... | collective-permute-start | bytes 3145736 | tf_op jit(solution)/shard_map/ppermute | solution.py:827
  31.5 34.7 %collective-permute-start.4 = (bf16[1536,256]{1,0:T(8,128)(2,1)}, bf16[1536,256]{1,0:T(8,128)(2,1)}, u32[]{:S(2)}, u32[]{:S(2)}) collective-permute-start(bf16[1536,256]{1,0:T(8,128)(2,1)} %constant_dynamic-slice_fusion.4), channel_id=1, source_target_pairs={{0,2},{2,0},{1,3},{3,1},{4,6},{6,4},{5,7},{7,5},{8,10},{10,8},{9,1... | collective-permute-start | bytes 2359304 | tf_op jit(solution)/shard_map/ppermute | solution.py:830
  33.0 33.2 %collective-permute-start.7 = (bf16[1024,256]{1,0:T(8,128)(2,1)}, bf16[1024,256]{1,0:T(8,128)(2,1)}, u32[]{:S(2)}, u32[]{:S(2)}) collective-permute-start(bf16[1024,256]{1,0:T(8,128)(2,1)} %refs_0_.3), channel_id=1, source_target_pairs={{0,1},{1,0},{2,3},{3,2},{4,5},{5,4},{6,7},{7,6},{8,9},{9,8},{10,11... | collective-permute-start | bytes 1572872 | tf_op jit(solution)/shard_map/ppermute | solution.py:827
  35.7 30.5 %collective-permute-start.3 = (bf16[256,1024]{1,0:T(8,128)(2,1)}, bf16[256,1024]{1,0:T(8,128)(2,1)}, u32[]{:S(2)}, u32[]{:S(2)}) collective-permute-start(bf16[256,1024]{1,0:T(8,128)(2,1)} %constant_dynamic-slice_fusion.5), channel_id=1, source_target_pairs={{0,2},{2,0},{1,3},{3,1},{4,6},{6,4},{5,7},{7,5},{8,10},{10,8},{9,1... | collective-permute-start | bytes 1572872 | tf_op jit(solution)/shard_map/ppermute | solution.py:830
  55.9 10.4 %collective-permute-start.5 = (bf16[832,256]{1,0:T(8,128)(2,1)}, bf16[832,256]{1,0:T(8,128)(2,1)}, u32[]{:S(2)}, u32[]{:S(2)}) collective-permute-start(bf16[832,256]{1,0:T(8,128)(2,1)} %constant_dynamic-slice_fusion.3), channel_id=1, source_target_pairs={{0,1},{1,0},{2,3},{3,2},{4,5},{5,4},{6,7},{7,6},{8,9},{9,8},{10,11... | collective-permute-start | bytes 1277960 | tf_op jit(solution)/shard_map/ppermute | solution.py:827
  67.3 33.5 %collective-permute-start.10 = (bf16[512,1024]{1,0:T(8,128)(2,1)}, bf16[512,1024]{1,0:T(8,128)(2,1)}, u32[]{:S(2)}, u32[]{:S(2)}) collective-permute-start(bf16[512,1024]{1,0:T(8,128)(2,1)} %constant_dynamic-slice_fusion.2), channel_id=1, source_target_pairs={{0,2},{2,0},{1,3},{3,1},{4,6},{6,4},{5,7},{7,5},{8,10},{10,8},{9,1... | collective-permute-start | bytes 3145736 | tf_op jit(solution)/shard_map/ppermute | solution.py:830
  69.6 31.2 %collective-permute-start.9 = (bf16[1536,256]{1,0:T(8,128)(2,1)}, bf16[1536,256]{1,0:T(8,128)(2,1)}, u32[]{:S(2)}, u32[]{:S(2)}) collective-permute-start(bf16[1536,256]{1,0:T(8,128)(2,1)} %collective-permute-done.4), channel_id=1, source_target_pairs={{0,4},{4,0},{8,12},{12,8},{16,20},{20,16},{24,28},{28,24},{1,5},{5... | collective-permute-start | bytes 2359304 | tf_op jit(solution)/shard_map/ppermute | solution.py:833
  71.9 28.9 %collective-permute-start.8 = (bf16[256,1024]{1,0:T(8,128)(2,1)}, bf16[256,1024]{1,0:T(8,128)(2,1)}, u32[]{:S(2)}, u32[]{:S(2)}) collective-permute-start(bf16[256,1024]{1,0:T(8,128)(2,1)} %collective-permute-done.3), channel_id=1, source_target_pairs={{0,4},{4,0},{8,12},{12,8},{16,20},{20,16},{24,28},{28,24},{1,5},{5... | collective-permute-start | bytes 1572872 | tf_op jit(solution)/shard_map/ppermute | solution.py:833
  74.1 61.6 %collective-permute-start.18 = (bf16[832,1024]{1,0:T(8,128)(2,1)S(1)}, bf16[832,1024]{1,0:T(8,128)(2,1)}, u32[]{:S(2)}, u32[]{:S(2)}) collective-permute-start(bf16[832,1024]{1,0:T(8,128)(2,1)S(1)} %broadcast_select_fusion.d_ref), channel_id=1, source_target_pairs={{0,1},{1,0},{2,3},{3,2},{4,5},{5,4},{6,7},{7,6},{8,9},{9,8},{10,11... | collective-permute-start | bytes 5111816 | tf_op jit(solution)/shard_map/ppermute | solution.py:827
  93.3 17.1 %collective-permute-start.11 = (bf16[832,256]{1,0:T(8,128)(2,1)S(1)}, bf16[832,256]{1,0:T(8,128)(2,1)S(1)}, u32[]{:S(2)}, u32[]{:S(2)}) collective-permute-start(bf16[832,256]{1,0:T(8,128)(2,1)S(1)} %constant_dynamic-slice_fusion.1), channel_id=1, source_target_pairs={{0,1},{1,0},{2,3},{3,2},{4,5},{5,4},{6,7},{7,6},{8,9},{9,8},{10,11... | collective-permute-start | bytes 1277960 | tf_op jit(solution)/shard_map/ppermute | solution.py:827
  102.8 5.8 collective-permute-start.12
  108.0 25.8 %collective-permute-start.16 = (bf16[512,1024]{1,0:T(8,128)(2,1)S(1)}, bf16[512,1024]{1,0:T(8,128)(2,1)}, u32[]{:S(2)}, u32[]{:S(2)}) collective-permute-start(bf16[512,1024]{1,0:T(8,128)(2,1)S(1)} %constant_dynamic-slice_fusion), channel_id=1, source_target_pairs={{0,2},{2,0},{1,3},{3,1},{4,6},{6,4},{5,7},{7,5},{8,10},{10,8},{9,1... | collective-permute-start | bytes 3145736 | tf_op jit(solution)/shard_map/ppermute | solution.py:830
  108.6 25.3 %collective-permute-start.15 = (bf16[512,1024]{1,0:T(8,128)(2,1)}, bf16[512,1024]{1,0:T(8,128)(2,1)}, u32[]{:S(2)}, u32[]{:S(2)}) collective-permute-start(bf16[512,1024]{1,0:T(8,128)(2,1)} %collective-permute-done.10), channel_id=1, source_target_pairs={{0,4},{4,0},{8,12},{12,8},{16,20},{20,16},{24,28},{28,24},{1,5},{5... | collective-permute-start | bytes 3145736 | tf_op jit(solution)/shard_map/ppermute | solution.py:833
  133.8 25.7 %collective-permute-start.17 = (bf16[832,1024]{1,0:T(8,128)(2,1)}, bf16[832,1024]{1,0:T(8,128)(2,1)}, u32[]{:S(2)}, u32[]{:S(2)}) collective-permute-start(bf16[832,1024]{1,0:T(8,128)(2,1)} %get-tuple-element.183.h_ref), channel_id=1, source_target_pairs={{0,1},{1,0},{2,3},{3,2},{4,5},{5,4},{6,7},{7,6},{8,9},{9,8},{10,11... | collective-permute-start | bytes 5111816 | tf_op jit(solution)/shard_map/ppermute | solution.py:827
  133.9 38.7 %collective-permute-start.19 = (bf16[512,1024]{1,0:T(8,128)(2,1)}, bf16[512,1024]{1,0:T(8,128)(2,1)}, u32[]{:S(2)}, u32[]{:S(2)}) collective-permute-start(bf16[512,1024]{1,0:T(8,128)(2,1)} %collective-permute-done.16), channel_id=1, source_target_pairs={{0,8},{4,12},{8,0},{12,4},{16,24},{20,28},{24,16},{28,20},{1,9},{5... | collective-permute-start | bytes 3145736 | tf_op jit(solution)/shard_map/ppermute | solution.py:833
  151.8 127.5 %collective-permute-start.29 = (bf16[832,1024]{1,0:T(8,128)(2,1)S(1)}, bf16[832,1024]{1,0:T(8,128)(2,1)}, u32[]{:S(2)}, u32[]{:S(2)}) collective-permute-start(bf16[832,1024]{1,0:T(8,128)(2,1)S(1)} %copy-done.61), channel_id=1, source_target_pairs={{0,1},{1,0},{2,3},{3,2},{4,5},{5,4},{6,7},{7,6},{8,9},{9,8},{10,11... | collective-permute-start | bytes 5111816 | tf_op jit(solution)/shard_map/ppermute | solution.py:827
  153.0 123.3 %collective-permute-start.36 = (bf16[832,512]{1,0:T(8,128)(2,1)}, bf16[832,512]{1,0:T(8,128)(2,1)}, u32[]{:S(2)}, u32[]{:S(2)}) collective-permute-start(bf16[832,512]{1,0:T(8,128)(2,1)} %slice.155), channel_id=1, source_target_pairs={{0,1},{1,0},{2,3},{3,2},{4,5},{5,4},{6,7},{7,6},{8,9},{9,8},{10,11... | collective-permute-start | bytes 2555912 | tf_op jit(solution)/shard_map/ppermute | solution.py:827
  205.4 32.7 %collective-permute-start.21 = (bf16[832,1024]{1,0:T(8,128)(2,1)}, bf16[832,1024]{1,0:T(8,128)(2,1)S(1)}, u32[]{:S(2)}, u32[]{:S(2)}) collective-permute-start(bf16[832,1024]{1,0:T(8,128)(2,1)} %get-tuple-element.203), channel_id=1, source_target_pairs={{0,1},{1,0},{2,3},{3,2},{4,5},{5,4},{6,7},{7,6},{8,9},{9,8},{10,11... | collective-permute-start | bytes 5111816 | tf_op jit(solution)/shard_map/ppermute | solution.py:827
  215.7 48.5 %collective-permute-start.20 = (bf16[1024,1024]{1,0:T(8,128)(2,1)}, bf16[1024,1024]{1,0:T(8,128)(2,1)}, u32[]{:S(2)}, u32[]{:S(2)}) collective-permute-start(bf16[1024,1024]{1,0:T(8,128)(2,1)} %convolution_convert_fusion.1), channel_id=1, source_target_pairs={{0,2},{2,0},{1,3},{3,1},{4,6},{6,4},{5,7},{7,5},{8,10},{10,8},{9,1... | collective-permute-start | bytes 6291464 | tf_op jit(solution)/shard_map/ppermute | solution.py:830
  264.2 18.2 %collective-permute-start.24 = (bf16[832,1024]{1,0:T(8,128)(2,1)S(1)}, bf16[832,1024]{1,0:T(8,128)(2,1)S(1)}, u32[]{:S(2)}, u32[]{:S(2)}) collective-permute-start(bf16[832,1024]{1,0:T(8,128)(2,1)S(1)} %get-tuple-element.239.mine_ref), channel_id=1, source_target_pairs={{0,1},{1,0},{2,3},{3,2},{4,5},{5,4},{6,7},{7,6},{8,9},{9,8},{10,11... | collective-permute-start | bytes 5111816 | tf_op jit(solution)/shard_map/ppermute | solution.py:827
  264.2 43.3 %collective-permute-start.25 = (bf16[832,1024]{1,0:T(8,128)(2,1)}, bf16[832,1024]{1,0:T(8,128)(2,1)}, u32[]{:S(2)}, u32[]{:S(2)}) collective-permute-start(bf16[832,1024]{1,0:T(8,128)(2,1)} %get-tuple-element.240), channel_id=1, source_target_pairs={{0,1},{1,0},{2,3},{3,2},{4,5},{5,4},{6,7},{7,6},{8,9},{9,8},{10,11... | collective-permute-start | bytes 5111816 | tf_op jit(solution)/shard_map/ppermute | solution.py:827
  272.8 34.7 %collective-permute-start.23 = (bf16[512,1024]{1,0:T(8,128)(2,1)}, bf16[512,1024]{1,0:T(8,128)(2,1)}, u32[]{:S(2)}, u32[]{:S(2)}) collective-permute-start(bf16[512,1024]{1,0:T(8,128)(2,1)} %add_convert_fusion.2), channel_id=1, source_target_pairs={{0,4},{4,0},{8,12},{12,8},{16,20},{20,16},{24,28},{28,24},{1,5},{5... | collective-permute-start | bytes 3145736 | tf_op jit(solution)/shard_map/ppermute | solution.py:833
  276.3 31.2 %collective-permute-start.26 = (bf16[832,512]{1,0:T(8,128)(2,1)}, bf16[832,512]{1,0:T(8,128)(2,1)S(1)}, u32[]{:S(2)}, u32[]{:S(2)}) collective-permute-start(bf16[832,512]{1,0:T(8,128)(2,1)} %slice.147), channel_id=1, source_target_pairs={{0,1},{1,0},{2,3},{3,2},{4,5},{5,4},{6,7},{7,6},{8,9},{9,8},{10,11... | collective-permute-start | bytes 2555912 | tf_op jit(solution)/shard_map/ppermute | solution.py:827
  279.2 26.7 %collective-permute-start.27 = (f32[2,2,64,256]{3,2,0,1:T(8,128)}, f32[2,2,64,256]{3,2,0,1:T(8,128)S(1)}, u32[]{:S(2)}, u32[]{:S(2)}) collective-permute-start(f32[2,2,64,256]{3,2,0,1:T(8,128)} %fusion.41), channel_id=1, source_target_pairs={{0,1},{1,0},{2,3},{3,2},{4,5},{5,4},{6,7},{7,6},{8,9},{9,8},{10,11... | collective-permute-start | bytes 786440 | tf_op jit(solution)/shard_map/ppermute | solution.py:827
  282.4 144.2 %collective-permute-start.41 = (bf16[832,1024]{1,0:T(8,128)(2,1)}, bf16[832,1024]{1,0:T(8,128)(2,1)}, u32[]{:S(2)}, u32[]{:S(2)}) collective-permute-start(bf16[832,1024]{1,0:T(8,128)(2,1)} %get-tuple-element.262), channel_id=1, source_target_pairs={{0,1},{1,0},{2,3},{3,2},{4,5},{5,4},{6,7},{7,6},{8,9},{9,8},{10,11... | collective-permute-start | bytes 5111816 | tf_op jit(solution)/shard_map/ppermute | solution.py:827
  305.9 48.3 %collective-permute-start.22 = (bf16[1024,1024]{1,0:T(8,128)(2,1)}, bf16[1024,1024]{1,0:T(8,128)(2,1)S(1)}, u32[]{:S(2)}, u32[]{:S(2)}) collective-permute-start(bf16[1024,1024]{1,0:T(8,128)(2,1)} %convolution_convert_fusion), channel_id=1, source_target_pairs={{0,2},{2,0},{1,3},{3,1},{4,6},{6,4},{5,7},{7,5},{8,10},{10,8},{9,1... | collective-permute-start | bytes 6291464 | tf_op jit(solution)/shard_map/ppermute | solution.py:830
  317.3 36.9 %collective-permute-start.28 = (bf16[256,1024]{1,0:T(8,128)(2,1)S(1)}, bf16[256,1024]{1,0:T(8,128)(2,1)S(1)}, u32[]{:S(2)}, u32[]{:S(2)}) collective-permute-start(bf16[256,1024]{1,0:T(8,128)(2,1)S(1)} %dynamic-slice_convert_fusion.1), channel_id=1, source_target_pairs={{0,8},{4,12},{8,0},{12,4},{16,24},{20,28},{24,16},{28,20},{1,9},{5... | collective-permute-start | bytes 1572872 | tf_op jit(solution)/shard_map/ppermute | solution.py:833
  354.4 42.6 %collective-permute-start.32 = (bf16[256,1024]{1,0:T(8,128)(2,1)S(1)}, bf16[256,1024]{1,0:T(8,128)(2,1)}, u32[]{:S(2)}, u32[]{:S(2)}) collective-permute-start(bf16[256,1024]{1,0:T(8,128)(2,1)S(1)} %add_convert_fusion.9), channel_id=1, source_target_pairs={{0,16},{4,20},{8,24},{12,28},{16,0},{20,4},{24,8},{28,12},{1,17},{... | collective-permute-start | bytes 1572872 | tf_op jit(solution)/shard_map/ppermute | solution.py:833
  358.4 38.7 %collective-permute-start.31 = (bf16[512,1024]{1,0:T(8,128)(2,1)}, bf16[512,1024]{1,0:T(8,128)(2,1)S(1)}, u32[]{:S(2)}, u32[]{:S(2)}) collective-permute-start(bf16[512,1024]{1,0:T(8,128)(2,1)} %add_convert_fusion.1), channel_id=1, source_target_pairs={{0,8},{4,12},{8,0},{12,4},{16,24},{20,28},{24,16},{28,20},{1,9},{5... | collective-permute-start | bytes 3145736 | tf_op jit(solution)/shard_map/ppermute | solution.py:833
  384.6 35.7 %collective-permute-start.30 = (bf16[3072,256]{1,0:T(8,128)(2,1)}, bf16[3072,256]{1,0:T(8,128)(2,1)}, u32[]{:S(2)}, u32[]{:S(2)}) collective-permute-start(bf16[3072,256]{1,0:T(8,128)(2,1)} %pad_maximum_fusion.5), channel_id=1, source_target_pairs={{0,2},{2,0},{1,3},{3,1},{4,6},{6,4},{5,7},{7,5},{8,10},{10,8},{9,1... | collective-permute-start | bytes 4718600 | tf_op jit(solution)/shard_map/ppermute | solution.py:830
  405.0 12.7 %collective-permute-start.34 = (bf16[256,1024]{1,0:T(8,128)(2,1)S(1)}, bf16[256,1024]{1,0:T(8,128)(2,1)S(1)}, u32[]{:S(2)}, u32[]{:S(2)}) collective-permute-start(bf16[256,1024]{1,0:T(8,128)(2,1)S(1)} %add_convert_fusion.8), channel_id=1, source_target_pairs={{0,8},{4,12},{8,0},{12,4},{16,24},{20,28},{24,16},{28,20},{1,9},{5... | collective-permute-start | bytes 1572872 | tf_op jit(solution)/shard_map/ppermute | solution.py:833
  406.1 12.5 %collective-permute-start.33 = (bf16[256,1024]{1,0:T(8,128)(2,1)S(1)}, bf16[256,1024]{1,0:T(8,128)(2,1)S(1)}, u32[]{:S(2)}, u32[]{:S(2)}) collective-permute-start(bf16[256,1024]{1,0:T(8,128)(2,1)S(1)} %dynamic-slice_convert_fusion), channel_id=1, source_target_pairs={{0,4},{4,0},{8,12},{12,8},{16,20},{20,16},{24,28},{28,24},{1,5},{5... | collective-permute-start | bytes 1572872 | tf_op jit(solution)/shard_map/ppermute | solution.py:833
  406.8 13.6 %collective-permute-start.35 = (bf16[832,1024]{1,0:T(8,128)(2,1)S(1)}, bf16[832,1024]{1,0:T(8,128)(2,1)S(1)}, u32[]{:S(2)}, u32[]{:S(2)}) collective-permute-start(bf16[832,1024]{1,0:T(8,128)(2,1)S(1)} %first_back.2), channel_id=1, source_target_pairs={{0,1},{1,0},{2,3},{3,2},{4,5},{5,4},{6,7},{7,6},{8,9},{9,8},{10,11... | collective-permute-start | bytes 5111816 | tf_op jit(solution)/shard_map/ppermute | solution.py:827
  417.8 14.5 %collective-permute-start.40 = (f32[64,1024]{1,0:T(8,128)S(1)}, f32[64,1024]{1,0:T(8,128)S(1)}, u32[]{:S(2)}, u32[]{:S(2)}) collective-permute-start(f32[64,1024]{1,0:T(8,128)S(1)} %convolution_add_fusion), channel_id=1, source_target_pairs={{0,1},{1,0},{2,3},{3,2},{4,5},{5,4},{6,7},{7,6},{8,9},{9,8},{10,11... | collective-permute-start | bytes 786440 | tf_op jit(solution)/shard_map/ppermute | solution.py:827
  418.6 40.7 %collective-permute-start.42 = (bf16[3072,256]{1,0:T(8,128)(2,1)S(1)}, bf16[3072,256]{1,0:T(8,128)(2,1)S(1)}, u32[]{:S(2)}, u32[]{:S(2)}) collective-permute-start(bf16[3072,256]{1,0:T(8,128)(2,1)S(1)} %copy-done.101), channel_id=1, source_target_pairs={{0,2},{2,0},{1,3},{3,1},{4,6},{6,4},{5,7},{7,5},{8,10},{10,8},{9,1... | collective-permute-start | bytes 4718600 | tf_op jit(solution)/shard_map/ppermute | solution.py:830
  424.3 9.5 %collective-permute-start.39 = (f32[8,1024]{1,0:T(8,128)S(1)}, f32[8,1024]{1,0:T(8,128)S(1)}, u32[]{:S(2)}, u32[]{:S(2)}) collective-permute-start(f32[8,1024]{1,0:T(8,128)S(1)} %add.261), channel_id=1, source_target_pairs={{0,1},{1,0},{2,3},{3,2},{4,5},{5,4},{6,7},{7,6},{8,9},{9,8},{10,11... | collective-permute-start | bytes 98312 | tf_op jit(solution)/shard_map/ppermute | solution.py:827
  425.9 26.8 %collective-permute-start.37 = (bf16[1536,256]{1,0:T(8,128)(2,1)S(1)}, bf16[1536,256]{1,0:T(8,128)(2,1)S(1)}, u32[]{:S(2)}, u32[]{:S(2)}) collective-permute-start(bf16[1536,256]{1,0:T(8,128)(2,1)S(1)} %add_convert_fusion.4), channel_id=1, source_target_pairs={{0,4},{4,0},{8,12},{12,8},{16,20},{20,16},{24,28},{28,24},{1,5},{5... | collective-permute-start | bytes 2359304 | tf_op jit(solution)/shard_map/ppermute | solution.py:833
  426.6 26.0 %collective-permute-start.38 = (bf16[256,1024]{1,0:T(8,128)(2,1)S(1)}, bf16[256,1024]{1,0:T(8,128)(2,1)S(1)}, u32[]{:S(2)}, u32[]{:S(2)}) collective-permute-start(bf16[256,1024]{1,0:T(8,128)(2,1)S(1)} %add_convert_fusion.7), channel_id=1, source_target_pairs={{0,16},{4,20},{8,24},{12,28},{16,0},{20,4},{24,8},{28,12},{1,17},{... | collective-permute-start | bytes 1572872 | tf_op jit(solution)/shard_map/ppermute | solution.py:833
  432.3 55.3 %collective-permute-start.49 = (bf16[512,1024]{1,0:T(8,128)(2,1)}, bf16[512,1024]{1,0:T(8,128)(2,1)}, u32[]{:S(2)}, u32[]{:S(2)}) collective-permute-start(bf16[512,1024]{1,0:T(8,128)(2,1)} %maximum_select_fusion.11), channel_id=1, source_target_pairs={{0,4},{4,0},{8,12},{12,8},{16,20},{20,16},{24,28},{28,24},{1,5},{5... | collective-permute-start | bytes 3145736 | tf_op jit(solution)/shard_map/ppermute | solution.py:833
  453.6 35.5 %collective-permute-start.48 = (bf16[256,1024]{1,0:T(8,128)(2,1)}, bf16[256,1024]{1,0:T(8,128)(2,1)}, u32[]{:S(2)}, u32[]{:S(2)}) collective-permute-start(bf16[256,1024]{1,0:T(8,128)(2,1)} %add_convert_fusion.6), channel_id=1, source_target_pairs={{0,4},{4,0},{8,12},{12,8},{16,20},{20,16},{24,28},{28,24},{1,5},{5... | collective-permute-start | bytes 1572872 | tf_op jit(solution)/shard_map/ppermute | solution.py:833
  455.1 4.2 collective-permute-start.43
  459.3 29.8 %collective-permute-start.47 = (bf16[768,256]{1,0:T(8,128)(2,1)}, bf16[768,256]{1,0:T(8,128)(2,1)}, u32[]{:S(2)}, u32[]{:S(2)}) collective-permute-start(bf16[768,256]{1,0:T(8,128)(2,1)} %dynamic-slice_convert_fusion.3), channel_id=1, source_target_pairs={{0,8},{4,12},{8,0},{12,4},{16,24},{20,28},{24,16},{28,20},{1,9},{5... | collective-permute-start | bytes 1179656 | tf_op jit(solution)/shard_map/ppermute | solution.py:833
  459.3 46.6 %collective-permute-start.44 = (bf16[512,1024]{1,0:T(8,128)(2,1)}, bf16[512,1024]{1,0:T(8,128)(2,1)}, u32[]{:S(2)}, u32[]{:S(2)}) collective-permute-start(bf16[512,1024]{1,0:T(8,128)(2,1)} %pad_maximum_fusion.9), channel_id=1, source_target_pairs={{0,2},{2,0},{1,3},{3,1},{4,6},{6,4},{5,7},{7,5},{8,10},{10,8},{9,1... | collective-permute-start | bytes 3145736 | tf_op jit(solution)/shard_map/ppermute | solution.py:830
  460.9 26.1 %collective-permute-start.50 = (bf16[64,1024]{1,0:T(8,128)(2,1)S(1)}, bf16[64,1024]{1,0:T(8,128)(2,1)S(1)}, u32[]{:S(2)}, u32[]{:S(2)}) collective-permute-start(bf16[64,1024]{1,0:T(8,128)(2,1)S(1)} %add_convert_fusion.16), channel_id=1, source_target_pairs={{0,2},{2,0},{1,3},{3,1},{4,6},{6,4},{5,7},{7,5},{8,10},{10,8},{9,1... | collective-permute-start | bytes 393224 | tf_op jit(solution)/shard_map/ppermute | solution.py:830
  487.0 19.0 %collective-permute-start.45 = (bf16[1536,256]{1,0:T(8,128)(2,1)}, bf16[1536,256]{1,0:T(8,128)(2,1)}, u32[]{:S(2)}, u32[]{:S(2)}) collective-permute-start(bf16[1536,256]{1,0:T(8,128)(2,1)} %add_convert_fusion.3), channel_id=1, source_target_pairs={{0,4},{4,0},{8,12},{12,8},{16,20},{20,16},{24,28},{28,24},{1,5},{5... | collective-permute-start | bytes 2359304 | tf_op jit(solution)/shard_map/ppermute | solution.py:833
  487.7 18.3 %collective-permute-start.46 = (f32[8,1024]{1,0:T(8,128)S(1)}, f32[8,1024]{1,0:T(8,128)S(1)}, u32[]{:S(2)}, u32[]{:S(2)}) collective-permute-start(f32[8,1024]{1,0:T(8,128)S(1)} %add.269), channel_id=1, source_target_pairs={{0,4},{4,0},{8,12},{12,8},{16,20},{20,16},{24,28},{28,24},{1,5},{5... | collective-permute-start | bytes 98312 | tf_op jit(solution)/shard_map/ppermute | solution.py:833
  491.1 34.6 %collective-permute-start.55 = (bf16[512,1024]{1,0:T(8,128)(2,1)S(1)}, bf16[512,1024]{1,0:T(8,128)(2,1)S(1)}, u32[]{:S(2)}, u32[]{:S(2)}) collective-permute-start(bf16[512,1024]{1,0:T(8,128)(2,1)S(1)} %maximum_select_fusion.12), channel_id=1, source_target_pairs={{0,8},{4,12},{8,0},{12,4},{16,24},{20,28},{24,16},{28,20},{1,9},{5... | collective-permute-start | bytes 3145736 | tf_op jit(solution)/shard_map/ppermute | solution.py:833
  494.1 30.9 %collective-permute-start.54 = (bf16[768,256]{1,0:T(8,128)(2,1)S(1)}, bf16[768,256]{1,0:T(8,128)(2,1)S(1)}, u32[]{:S(2)}, u32[]{:S(2)}) collective-permute-start(bf16[768,256]{1,0:T(8,128)(2,1)S(1)} %add_convert_fusion.13), channel_id=1, source_target_pairs={{0,16},{4,20},{8,24},{12,28},{16,0},{20,4},{24,8},{28,12},{1,17},{... | collective-permute-start | bytes 1179656 | tf_op jit(solution)/shard_map/ppermute | solution.py:833
  507.2 28.4 %collective-permute-start.51 = (bf16[256,1024]{1,0:T(8,128)(2,1)S(1)}, bf16[256,1024]{1,0:T(8,128)(2,1)S(1)}, u32[]{:S(2)}, u32[]{:S(2)}) collective-permute-start(bf16[256,1024]{1,0:T(8,128)(2,1)S(1)} %add_convert_fusion.5), channel_id=1, source_target_pairs={{0,4},{4,0},{8,12},{12,8},{16,20},{20,16},{24,28},{28,24},{1,5},{5... | collective-permute-start | bytes 1572872 | tf_op jit(solution)/shard_map/ppermute | solution.py:833
  510.6 24.3 %collective-permute-start.52 = (bf16[768,256]{1,0:T(8,128)(2,1)S(1)}, bf16[768,256]{1,0:T(8,128)(2,1)S(1)}, u32[]{:S(2)}, u32[]{:S(2)}) collective-permute-start(bf16[768,256]{1,0:T(8,128)(2,1)S(1)} %dynamic-slice_convert_fusion.2), channel_id=1, source_target_pairs={{0,8},{4,12},{8,0},{12,4},{16,24},{20,28},{24,16},{28,20},{1,9},{5... | collective-permute-start | bytes 1179656 | tf_op jit(solution)/shard_map/ppermute | solution.py:833
  512.1 22.7 %collective-permute-start.53 = (f32[8,1024]{1,0:T(8,128)S(1)}, f32[8,1024]{1,0:T(8,128)S(1)}, u32[]{:S(2)}, u32[]{:S(2)}) collective-permute-start(f32[8,1024]{1,0:T(8,128)S(1)} %add.275), channel_id=1, source_target_pairs={{0,8},{4,12},{8,0},{12,4},{16,24},{20,28},{24,16},{28,20},{1,9},{5... | collective-permute-start | bytes 98312 | tf_op jit(solution)/shard_map/ppermute | solution.py:833
  528.7 24.8 %collective-permute-start.58 = (bf16[768,256]{1,0:T(8,128)(2,1)S(1)}, bf16[768,256]{1,0:T(8,128)(2,1)}, u32[]{:S(2)}, u32[]{:S(2)}) collective-permute-start(bf16[768,256]{1,0:T(8,128)(2,1)S(1)} %add_convert_fusion.11), channel_id=1, source_target_pairs={{0,8},{4,12},{8,0},{12,4},{16,24},{20,28},{24,16},{28,20},{1,9},{5... | collective-permute-start | bytes 1179656 | tf_op jit(solution)/shard_map/ppermute | solution.py:833
  536.9 16.5 %collective-permute-start.59 = (bf16[128,1024]{1,0:T(8,128)(2,1)S(1)}, bf16[128,1024]{1,0:T(8,128)(2,1)S(1)}, u32[]{:S(2)}, u32[]{:S(2)}) collective-permute-start(bf16[128,1024]{1,0:T(8,128)(2,1)S(1)} %dynamic-slice_convert_fusion.4), channel_id=1, source_target_pairs={{0,8},{4,12},{8,0},{12,4},{16,24},{20,28},{24,16},{28,20},{1,9},{5... | collective-permute-start | bytes 786440 | tf_op jit(solution)/shard_map/ppermute | solution.py:833
  539.8 25.0 %collective-permute-start.56 = (bf16[768,256]{1,0:T(8,128)(2,1)S(1)}, bf16[768,256]{1,0:T(8,128)(2,1)S(1)}, u32[]{:S(2)}, u32[]{:S(2)}) collective-permute-start(bf16[768,256]{1,0:T(8,128)(2,1)S(1)} %add_convert_fusion.12), channel_id=1, source_target_pairs={{0,16},{4,20},{8,24},{12,28},{16,0},{20,4},{24,8},{28,12},{1,17},{... | collective-permute-start | bytes 1179656 | tf_op jit(solution)/shard_map/ppermute | solution.py:833
  540.9 23.9 %collective-permute-start.57 = (f32[8,1024]{1,0:T(8,128)S(1)}, f32[8,1024]{1,0:T(8,128)S(1)}, u32[]{:S(2)}, u32[]{:S(2)}) collective-permute-start(f32[8,1024]{1,0:T(8,128)S(1)} %add.281), channel_id=1, source_target_pairs={{0,16},{4,20},{8,24},{12,28},{16,0},{20,4},{24,8},{28,12},{1,17},{... | collective-permute-start | bytes 98312 | tf_op jit(solution)/shard_map/ppermute | solution.py:833
  553.5 15.4 %collective-permute-start.62 = (bf16[128,1024]{1,0:T(8,128)(2,1)S(1)}, bf16[128,1024]{1,0:T(8,128)(2,1)S(1)}, u32[]{:S(2)}, u32[]{:S(2)}) collective-permute-start(bf16[128,1024]{1,0:T(8,128)(2,1)S(1)} %add_convert_fusion.15), channel_id=1, source_target_pairs={{0,16},{4,20},{8,24},{12,28},{16,0},{20,4},{24,8},{28,12},{1,17},{... | collective-permute-start | bytes 786440 | tf_op jit(solution)/shard_map/ppermute | solution.py:833
  555.0 24.6 %collective-permute-start.61 = (bf16[1536,256]{1,0:T(8,128)(2,1)S(1)}, bf16[1536,256]{1,0:T(8,128)(2,1)S(1)}, u32[]{:S(2)}, u32[]{:S(2)}) collective-permute-start(bf16[1536,256]{1,0:T(8,128)(2,1)S(1)} %maximum_select_fusion.14), channel_id=1, source_target_pairs={{0,4},{4,0},{8,12},{12,8},{16,20},{20,16},{24,28},{28,24},{1,5},{5... | collective-permute-start | bytes 2359304 | tf_op jit(solution)/shard_map/ppermute | solution.py:833
  564.9 14.7 %collective-permute-start.60 = (bf16[768,256]{1,0:T(8,128)(2,1)S(1)}, bf16[768,256]{1,0:T(8,128)(2,1)S(1)}, u32[]{:S(2)}, u32[]{:S(2)}) collective-permute-start(bf16[768,256]{1,0:T(8,128)(2,1)S(1)} %add_convert_fusion.10), channel_id=1, source_target_pairs={{0,8},{4,12},{8,0},{12,4},{16,24},{20,28},{24,16},{28,20},{1,9},{5... | collective-permute-start | bytes 1179656 | tf_op jit(solution)/shard_map/ppermute | solution.py:833
  569.0 9.7 %collective-permute-start.63 = (bf16[128,1024]{1,0:T(8,128)(2,1)S(1)}, bf16[128,1024]{1,0:T(8,128)(2,1)S(1)}, u32[]{:S(2)}, u32[]{:S(2)}) collective-permute-start(bf16[128,1024]{1,0:T(8,128)(2,1)S(1)} %add_convert_fusion.14), channel_id=1, source_target_pairs={{0,8},{4,12},{8,0},{12,4},{16,24},{20,28},{24,16},{28,20},{1,9},{5... | collective-permute-start | bytes 786440 | tf_op jit(solution)/shard_map/ppermute | solution.py:833
  578.9 14.9 %collective-permute-start.64 = (bf16[256,1024]{1,0:T(8,128)(2,1)S(1)}, bf16[256,1024]{1,0:T(8,128)(2,1)S(1)}, u32[]{:S(2)}, u32[]{:S(2)}) collective-permute-start(bf16[256,1024]{1,0:T(8,128)(2,1)S(1)} %maximum_select_fusion.16), channel_id=1, source_target_pairs={{0,4},{4,0},{8,12},{12,8},{16,20},{20,16},{24,28},{28,24},{1,5},{5... | collective-permute-start | bytes 1572872 | tf_op jit(solution)/shard_map/ppermute | solution.py:833
  579.9 26.9 %collective-permute-start.65 = (bf16[1536,256]{1,0:T(8,128)(2,1)S(1)}, bf16[1536,256]{1,0:T(8,128)(2,1)S(1)}, u32[]{:S(2)}, u32[]{:S(2)}) collective-permute-start(bf16[1536,256]{1,0:T(8,128)(2,1)S(1)} %maximum_select_fusion.15), channel_id=1, source_target_pairs={{0,4},{4,0},{8,12},{12,8},{16,20},{20,16},{24,28},{28,24},{1,5},{5... | collective-permute-start | bytes 2359304 | tf_op jit(solution)/shard_map/ppermute | solution.py:833
  (127 other events, 937.0 us)

commit v5 on v4

--- a/solution.py
+++ b/solution.py
@@ -362,16 +362,19 @@
     return inverse * (weighted - inner - scaled * along)
 
 
-def project_kernel(where_ref, mine_ref, other_ref, weight_ref, *out_refs, transposed, count):
+def first_project_kernel(
+    place_ref, mine_ref, other_ref, gain_ref, bias_ref, weight_ref, h_ref, *out_refs
+):
     half = pl.program_id(0)
 
     def run(source):
-        for c in range(count):
-            if transposed:
-                result = nt(source[...], weight_ref[c])
-            else:
-                result = nn(source[...], weight_ref[c])
-            out_refs[c][...] = lower(result)
+        for start in range(0, source.shape[0], 208):
+            part = slice(start, start + 208)
+            scaled, _ = norm_parts(source[part, :].astype(FULL))
+            h = lower(scaled * gain_ref[0:1, :] + bias_ref[0:1, :])
+            h_ref[part, :] = h
+            for c, out_ref in enumerate(out_refs):
+                out_ref[part, :] = lower(nn(h, weight_ref[c]))
 
     @pl.when(half == 0)
     def _():
@@ -382,69 +385,133 @@
         run(other_ref)
 
 
-def project(where, mine, other, weights, transposed):
+def first_project(place, mine, other, gains, biases, weights):
     rows, depth = mine.shape
-    count = weights.shape[0]
-    wide = weights.shape[1] if transposed else weights.shape[2]
-    whole = pl.BlockSpec((rows, depth), lambda i, s: (0, 0), pipeline_mode=pl.Buffered(1))
+    count, _, wide = weights.shape
     out = pl.BlockSpec((rows, wide), lambda i, s: ((i + s[0]) % 2, 0))
     return pl.pallas_call(
-        functools.partial(project_kernel, transposed=transposed, count=count),
+        first_project_kernel,
         grid_spec=pltpu.PrefetchScalarGridSpec(
             num_scalar_prefetch=1,
             grid=(2,),
-            in_specs=[whole, whole, resident(weights.shape)],
+            in_specs=[resident(a.shape) for a in (mine, other, gains, biases, weights)],
+            out_specs=[rows_of(rows, depth)] + [out] * count,
+        ),
+        out_shape=[shape((2 * rows, depth), ROUND)] + [shape((2 * rows, wide), ROUND)] * count,
+        compiler_params=params(40),
+        cost_estimate=brief(),
+        name="first_project",
+    )(place, mine, other, gains, biases, weights)
+
+
+def project_kernel(place_ref, h_ref, first_ref, second_ref, *out_refs):
+    depth = first_ref.shape[1]
+    near = place_ref[1]
+    left = h_ref[:, pl.ds(pl.multiple_of(near * depth, 128), depth)]
+    right = h_ref[:, pl.ds(pl.multiple_of((1 - near) * depth, 128), depth)]
+    for c, out_ref in enumerate(out_refs):
+        out_ref[...] = lower(nn(left, first_ref[c]) + nn(right, second_ref[c]))
+
+
+def project(place, h, first, second):
+    rows, depth = h.shape[0] // 2, h.shape[1]
+    count, _, wide = first.shape
+    out = pl.BlockSpec((rows, wide), lambda i, s: ((i + s[0]) % 2, 0))
+    return pl.pallas_call(
+        project_kernel,
+        grid_spec=pltpu.PrefetchScalarGridSpec(
+            num_scalar_prefetch=1,
+            grid=(2,),
+            in_specs=[rows_of(rows, depth), resident(first.shape), resident(second.shape)],
             out_specs=[out] * count,
         ),
         out_shape=[shape((2 * rows, wide), ROUND)] * count,
         compiler_params=params(32),
         cost_estimate=brief(),
         name="project",
-    )(where, mine, other, weights)
+    )(place, h, first, second)
+
+
+def pull_kernel(place_ref, mine_ref, other_ref, *refs):
+    half = pl.program_id(0)
+    count = len(refs) // 2
+
+    def run(source):
+        for weight_ref, out_ref in zip(refs[:count], refs[count:]):
+            out_ref[...] = lower(nt(source[...], weight_ref[...]))
+
+    @pl.when(half == 0)
+    def _():
+        run(mine_ref)
+
+    @pl.when(half == 1)
+    def _():
+        run(other_ref)
+
+
+def pull(place, mine, other, weights):
+    rows = mine.shape[0]
+    wide = weights[0].shape[0]
+    out = pl.BlockSpec((rows, wide), lambda i, s: ((i + s[0]) % 2, 0))
+    return pl.pallas_call(
+        pull_kernel,
+        grid_spec=pltpu.PrefetchScalarGridSpec(
+            num_scalar_prefetch=1,
+            grid=(2,),
+            in_specs=[resident(a.shape) for a in (mine, other, *weights)],
+            out_specs=[out] * len(weights),
+        ),
+        out_shape=[shape((2 * rows, wide), ROUND)] * len(weights),
+        compiler_params=params(32),
+        cost_estimate=brief(),
+        name="pull",
+    )(place, mine, other, *weights)
 
 
 def blocks_of(span, block):
     return [(start, min(block, span - start)) for start in range(0, span, block)]
 
 
-def self_forward_kernel(limit_ref, q_ref, k_ref, v_ref, o_ref, lse_ref, *, span, floor, block):
+def self_forward_kernel(
+    limit_ref, q_ref, k_ref, v_ref, o_ref, lse_ref, *, span, floor, block
+):
     limit = limit_ref[0]
     lane = lax.broadcasted_iota(jnp.int32, (1, 128), 1)
+    row = lax.broadcasted_iota(jnp.int32, (128, 1), 0)
     zero = jnp.zeros((), ROUND)
+    value_turned = v_ref[...].T
     for start, size in blocks_of(span, block):
         end = start + size
         mixed_list = []
         for h in range(2):
             own_lanes = (lane < HEAD) if h == 0 else (lane >= HEAD)
             query = jnp.where(own_lanes, q_ref[start:end, :] * HEAD ** (-0.5), zero)
-            cuts = [(0, start)] if start <= floor else [(0, floor), (floor, start)]
             parts = []
-            for low, high in cuts + [(start, end)]:
-                if low == high:
-                    continue
-                scores = nt(query, k_ref[low:high, :])
-                key = lax.broadcasted_iota(jnp.int32, (size, high - low), 1)
+            for low in range(0, end, block):
+                high = min(low + block, end)
+                scores = nt(k_ref[low:high, :], query)
                 if low == start:
-                    valid = key <= lax.broadcasted_iota(jnp.int32, (size, high - low), 0)
+                    key = lax.broadcasted_iota(jnp.int32, (size, size), 0)
+                    valid = key <= lax.broadcasted_iota(jnp.int32, (size, size), 1)
                     if high > floor:
                         valid = valid & (key + low < limit)
                     scores = jnp.where(valid, scores, NEG)
                 elif high > floor:
+                    key = lax.broadcasted_iota(jnp.int32, (high - low, 1), 0)
                     scores = jnp.where(key + low < limit, scores, NEG)
                 parts.append((low, high, scores))
             top = functools.reduce(
-                jnp.maximum, [jnp.max(s, axis=1, keepdims=True) for _, _, s in parts]
+                jnp.maximum, [jnp.max(s, axis=0, keepdims=True) for _, _, s in parts]
             )
             total = 0.0
             mixed = 0.0
             for low, high, scores in parts:
                 weights_exp = jnp.exp(scores - top)
-                total = total + jnp.sum(weights_exp, axis=1, keepdims=True)
-                mixed = mixed + nn(lower(weights_exp), v_ref[low:high, :])
+                total = total + jnp.sum(weights_exp, axis=0, keepdims=True)
+                mixed = mixed + nn(value_turned[:, low:high], lower(weights_exp))
             mixed_list.append(mixed / total)
-            summary = jnp.broadcast_to(top + jnp.log(total), (size, 128))
-            lse_ref[0, h : h + 1, start:end] = summary.T[0:1, :]
-        o_ref[start:end, :] = lower(jnp.where(lane < HEAD, mixed_list[0], mixed_list[1]))
+            lse_ref[0, h : h + 1, start:end] = top + jnp.log(total)
+        o_ref[start:end, :] = lower(jnp.where(row < HEAD, mixed_list[0], mixed_list[1]).T)
 
 
 def self_forward(limit, q, k, v):
@@ -453,7 +520,7 @@
     floor = (span - span // 8 + 1) // 128 * 128
     pair = pl.BlockSpec((span, 128), lambda p, s: (0, p))
     return pl.pallas_call(
-        functools.partial(self_forward_kernel, span=span, floor=floor, block=256),
+        functools.partial(self_forward_kernel, span=span, floor=floor, block=512),
         grid_spec=pltpu.PrefetchScalarGridSpec(
             num_scalar_prefetch=1,
             grid=(pairs,),
@@ -461,7 +528,7 @@
             out_specs=[pair, pl.BlockSpec((1, 8, span), lambda p, s: (p, 0, 0))],
         ),
         out_shape=[shape((span, wide), ROUND), shape((pairs, 8, span), FULL)],
-        compiler_params=params(40),
+        compiler_params=params(56),
         cost_estimate=brief(),
         name="self_forward",
     )(limit, q, k, v)
@@ -567,7 +634,7 @@
 
 
 def middle_forward_kernel(
-    where_ref, frame_ref, a0_ref, a1_ref, a2_ref, a3_ref, gain_ref, bias_ref, *refs
+    place_ref, frame_ref, a0_ref, a1_ref, a2_ref, a3_ref, gain_ref, bias_ref, *refs
 ):
     mixed = (a0_ref, a1_ref, a2_ref, a3_ref)
     wo, wq, wc = refs[0:4], refs[4:8], refs[12:16]
@@ -595,9 +662,9 @@
     h3_ref[...] = lower(scaled * gain_ref[2:3, :] + bias_ref[2:3, :])
 
 
-def middle_forward(where, frames, attended, received, gains, biases, wo, wq, ck, cv, wc):
+def middle_forward(place, frames, attended, received, gains, biases, wo, wq, ck, cv, wc):
     rows, width = frames.shape
-    block = 208
+    block = 416
     steps = rows // block
     piece = pl.BlockSpec((block, 256), lambda i, s: (s[0] * steps + i, 0))
     wide = rows_of(block, width)
@@ -611,23 +678,36 @@
             out_specs=[wide] * 6,
         ),
         out_shape=[shape((rows, width), FULL)] * 2 + [shape((rows, width), ROUND)] * 4,
-        compiler_params=params(40),
+        compiler_params=params(56),
         cost_estimate=brief(),
         name="middle_forward",
-    )(where, frames, *attended, *received, gains, biases, *wo, *wq, *ck, *cv, *wc)
-
-
-def feed_kernel(where_ref, h_ref, d_ref, up_ref, down_ref, *refs, carried, shared):
-    before = refs[: 2 * carried]
-    g_ref, du_ref, out_ref, y_ref = refs[2 * carried + 2 * shared :]
-    u = nn(h_ref[...], up_ref[...])
-    active, slope = gelu_parts(u)
-    g = lower(active)
-    g_ref[...] = g
-    du = lower(nt(d_ref[...], down_ref[...]) * slope)
-    du_ref[...] = du
-    out = nn(g, down_ref[...])
-    y = nt(du, up_ref[...])
+    )(place, frames, *attended, *received, gains, biases, *wo, *wq, *ck, *cv, *wc)
+
+
+def feed_kernel(place_ref, h_ref, d_ref, *refs, parts, carried):
+    ups, downs = refs[:parts], refs[parts : 2 * parts]
+    before = refs[2 * parts : 2 * parts + carried]
+    g_ref, du_ref, out_ref, y_ref = refs[-4:]
+    h = h_ref[...]
+    d = d_ref[...]
+    out = 0.0
+    y = 0.0
+    for n, (up_ref, down_ref) in enumerate(zip(ups, downs)):
+        size = down_ref.shape[0]
+        if parts == 1:
+            lanes = slice(0, size)
+        else:
+            near = place_ref[1]
+            which = near if n == 0 else 1 - near
+            lanes = pl.ds(pl.multiple_of(which * size, 128), size)
+        u = nn(h, up_ref[...])
+        active, slope = gelu_parts(u)
+        g = lower(active)
+        g_ref[:, lanes] = g
+        du = lower(nt(d, down_ref[...]) * slope)
+        du_ref[:, lanes] = du
+        out = out + nn(g, down_ref[...])
+        y = y + nt(du, up_ref[...])
     if carried:
         out = before[0][...] + out
         y = before[1][...] + y
@@ -635,37 +715,176 @@
     y_ref[...] = y.astype(y_ref.dtype)
 
 
-def feed(where, h, d, up, down, kind, before=(), shared=()):
+def feed(place, h, d, ups, downs, kind, half, before=(), shared=()):
     rows, width = h.shape
-    block = 208
+    block = 416
     steps = rows // block
-    hidden = up.shape[1]
+    hidden = sum(a.shape[0] for a in downs)
     wide = rows_of(block, width)
-    first = steps if shared else 0
-    kept = pl.BlockSpec((block, hidden), lambda i, s: (i + first, 0))
+    kept = pl.BlockSpec((block, hidden), lambda i, s: (i + half * steps, 0))
     there = pl.BlockSpec(memory_space=pl.ANY)
-    carried = 1 if before else 0
-    at = 5 + len(before)
-    return pl.pallas_call(
-        functools.partial(feed_kernel, carried=carried, shared=1 if shared else 0),
+    parts = len(ups)
+    at = 3 + 2 * parts + len(before)
+    return pl.pallas_call(
+        functools.partial(feed_kernel, parts=parts, carried=len(before)),
         grid_spec=pltpu.PrefetchScalarGridSpec(
             num_scalar_prefetch=1,
             grid=(steps,),
-            in_specs=[wide, wide, resident(up.shape), resident(down.shape)]
+            in_specs=[wide, wide]
+            + [resident(a.shape) for a in (*ups, *downs)]
             + [wide] * len(before)
             + [there] * len(shared),
             out_specs=[kept, kept, wide, wide],
         ),
         out_shape=[shape((2 * rows, hidden), ROUND)] * 2 + [shape((rows, width), kind)] * 2,
         input_output_aliases={at: 0, at + 1: 1} if shared else {},
-        compiler_params=params(56),
+        compiler_params=params(58),
         cost_estimate=brief(),
         name="feed",
-    )(where, h, d, up, down, *before, *shared)
+    )(place, h, d, *ups, *downs, *before, *shared)
+
+
+def up_grad_kernel(mine_ref, other_ref, du_ref, out_ref):
+    rows = mine_ref.shape[0]
+    total = tn(mine_ref[...], du_ref[:rows, :]) + tn(other_ref[...], du_ref[rows:, :])
+    out_ref[...] = total.astype(out_ref.dtype)
+
+
+def up_grad(mine, other, du, kind):
+    rows, width = mine.shape
+    hidden = du.shape[1]
+    tile = 512
+    whole = pl.BlockSpec((rows, width), lambda i: (0, 0), pipeline_mode=pl.Buffered(1))
+    return pl.pallas_call(
+        up_grad_kernel,
+        grid=(hidden // tile,),
+        in_specs=[whole, whole, pl.BlockSpec((2 * rows, tile), lambda i: (0, i))],
+        out_specs=pl.BlockSpec((width, tile), lambda i: (0, i)),
+        out_shape=shape((width, hidden), kind),
+        compiler_params=params(48),
+        cost_estimate=brief(),
+        name="up_grad",
+    )(mine, other, du)
+
+
+def down_grad_kernel(g_ref, mine_ref, other_ref, out_ref):
+    rows = mine_ref.shape[0]
+    total = tn(g_ref[:rows, :], mine_ref[...]) + tn(g_ref[rows:, :], other_ref[...])
+    out_ref[...] = total.astype(out_ref.dtype)
+
+
+def down_grad(g, mine, other, kind):
+    rows, width = mine.shape
+    hidden = g.shape[1]
+    tile = 512
+    whole = pl.BlockSpec((rows, width), lambda i: (0, 0), pipeline_mode=pl.Buffered(1))
+    return pl.pallas_call(
+        down_grad_kernel,
+        grid=(hidden // tile,),
+        in_specs=[pl.BlockSpec((2 * rows, tile), lambda i: (0, i)), whole, whole],
+        out_specs=pl.BlockSpec((tile, width), lambda i: (i, 0)),
+        out_shape=shape((hidden, width), kind),
+        compiler_params=params(48),
+        cost_estimate=brief(),
+        name="down_grad",
+    )(g, mine, other)
+
+
+def qkv_grad_kernel(place_ref, h_ref, *refs):
+    out_ref = refs[-1]
+    rows, width = h_ref.shape[0] // 2, h_ref.shape[1]
+    core = place_ref[0]
+    total = [0.0] * 3
+    for half in range(2):
+        turned = h_ref[half * rows : (half + 1) * rows, :].T
+        at = pl.multiple_of((core if half == 0 else 1 - core) * rows, 16)
+        for c in range(3):
+            total[c] = total[c] + nn(turned, refs[c][pl.ds(at, rows), :])
+    for c in range(3):
+        out_ref[c * width : (c + 1) * width, :] = total[c].astype(out_ref.dtype)
+
+
+def qkv_grad(place, h, grads, kind):
+    width = h.shape[1]
+    wide = grads[0].shape[1]
+    return pl.pallas_call(
+        qkv_grad_kernel,
+        grid_spec=pltpu.PrefetchScalarGridSpec(
+            num_scalar_prefetch=1,
+            grid=(1,),
+            in_specs=[resident(a.shape) for a in (h, *grads)],
+            out_specs=resident((3 * width, wide)),
+        ),
+        out_shape=shape((3 * width, wide), kind),
+        compiler_params=params(48),
+        cost_estimate=brief(),
+        name="qkv_grad",
+    )(place, h, *grads)
+
+
+def cross_in_grad_kernel(mine_ref, other_ref, dm_ref, do_ref, text_ref, pair_ref, out_ref):
+    width = mine_ref.shape[1]
+    total = tn(mine_ref[...], dm_ref[...]) + tn(other_ref[...], do_ref[...])
+    out_ref[:width, :] = total.astype(out_ref.dtype)
+    turned = text_ref[...].T
+    for c in range(2):
+        part = nn(turned, pair_ref[c]).astype(out_ref.dtype)
+        out_ref[(1 + c) * width : (2 + c) * width, :] = part
+
+
+def cross_in_grad(group, mine, other, d_mine, d_other, text, pair, kind):
+    rows, width = mine.shape
+    lanes = pl.BlockSpec((rows, 256), lambda i: (0, group))
+
+    def whole(a):
+        zeros = (0,) * a.ndim
+        return pl.BlockSpec(a.shape, lambda i: zeros)
+
+    return pl.pallas_call(
+        cross_in_grad_kernel,
+        grid=(1,),
+        in_specs=[whole(mine), whole(other), lanes, lanes, whole(text), whole(pair)],
+        out_specs=pl.BlockSpec((3 * width, 256), lambda i: (0, 0)),
+        out_shape=shape((3 * width, 256), kind),
+        compiler_params=params(48),
+        cost_estimate=brief(),
+        name="cross_in_grad",
+    )(mine, other, d_mine, d_other, text, pair)
+
+
+def outputs_grad_kernel(
+    place_ref, o_ref, sm_ref, so_ref, am_ref, ao_ref, cm_ref, co_ref, out_ref
+):
+    rows = sm_ref.shape[0]
+    core = place_ref[0]
+    mine = o_ref[pl.ds(pl.multiple_of(core * rows, 16), rows), :]
+    other = o_ref[pl.ds(pl.multiple_of((1 - core) * rows, 16), rows), :]
+    out_ref[:256, :] = (tn(mine, sm_ref[...]) + tn(other, so_ref[...])).astype(out_ref.dtype)
+    total = tn(am_ref[...], cm_ref[...]) + tn(ao_ref[...], co_ref[...])
+    out_ref[256:, :] = total.astype(out_ref.dtype)
+
+
+def outputs_grad(place, group, o, dself, dself_other, ca, ca_other, dcross, dcross_other, kind):
+    rows, width = dself.shape
+    lanes = pl.BlockSpec((rows, 256), lambda i, s: (0, group))
+    whole = resident((rows, width))
+    return pl.pallas_call(
+        outputs_grad_kernel,
+        grid_spec=pltpu.PrefetchScalarGridSpec(
+            num_scalar_prefetch=1,
+            grid=(1,),
+            in_specs=[resident(o.shape), whole, whole, lanes, lanes, whole, whole],
+            out_specs=resident((512, width)),
+        ),
+        out_shape=shape((512, width), kind),
+        compiler_params=params(48),
+        cost_estimate=brief(),
+        name="outputs_grad",
+    )(place, o, dself, dself_other, ca, ca_other, dcross, dcross_other)
 
 
 def middle_back_kernel(
-    where_ref, ym_ref, yr_ref, x1_ref, x2_ref, d_ref, cq_ref, gain_ref, *refs
+    place_ref, ym_ref, yr_ref, x1_ref, x2_ref, d_ref, cq_ref, gain_ref, *refs
 ):
     wq, wc = refs[0:4], refs[8:12]
     ck0_ref, ck1_ref, cv0_ref, cv1_ref = refs[4:8]
@@ -721,9 +940,9 @@
                 result[g] = total
 
 
-def middle_back(where, ym, yr, x1, x2, d, cq, gains, wq, ck, cv, wc):
+def middle_back(place, ym, yr, x1, x2, d, cq, gains, wq, ck, cv, wc):
     rows, width = x1.shape
-    block = 208
+    block = 416
     wide = rows_of(block, width)
     small = pl.BlockSpec((4, 64, 256), lambda i, s: (0, 0, 0))
     return pl.pallas_call(
@@ -739,27 +958,35 @@
         + [shape((rows, width), ROUND)] * 3
         + [shape((4, 64, 256), FULL)] * 2
         + [shape((8, width), FULL)],
-        compiler_params=params(40),
+        compiler_params=params(56),
         cost_estimate=brief(),
         name="middle_back",
-    )(where, ym, yr, x1, x2, d, cq, gains, *wq, *ck, *cv, *wc)
-
-
-def first_back_kernel(where_ref, *refs):
+    )(place, ym, yr, x1, x2, d, cq, gains, *wq, *ck, *cv, *wc)
+
+
+def first_back_kernel(place_ref, *refs):
     grads = refs[:6]
-    w0_ref, w1_ref, y_ref = refs[6:]
+    own_ref, first_ref, second_ref, y_ref, total = refs[6:]
+    depth = first_ref.shape[1]
     y = 0.0
-    for g in range(2):
-        for c in range(3):
-            y = y + nt(grads[3 * g + c][...], (w0_ref, w1_ref)[g][c])
-    y_ref[...] = y.astype(y_ref.dtype)
-
-
-def first_back(half, grads, weights, kind):
+    left = 0.0
+    right = 0.0
+    for c in range(3):
+        y = y + nt(grads[c][...], own_ref[c])
+        left = left + nt(grads[3 + c][...], first_ref[c])
+        right = right + nt(grads[3 + c][...], second_ref[c])
+    near = place_ref[1]
+    total[...] = y
+    total[:, pl.ds(pl.multiple_of(near * depth, 128), depth)] += left
+    total[:, pl.ds(pl.multiple_of((1 - near) * depth, 128), depth)] += right
+    y_ref[...] = total[...].astype(y_ref.dtype)
+
+
+def first_back(place, grads, own, first, second, kind):
     span = grads[0].shape[0]
     rows = span // 2
-    width = weights[0].shape[1]
-    block = 208
+    width = own.shape[1]
+    block = 416
     steps = rows // block
     piece = pl.BlockSpec((block, 256), lambda i, s: (s[0] * steps + i, 0))
     return pl.pallas_call(
@@ -767,17 +994,18 @@
         grid_spec=pltpu.PrefetchScalarGridSpec(
             num_scalar_prefetch=1,
             grid=(steps,),
-            in_specs=[piece] * 6 + [resident(a.shape) for a in weights],
+            in_specs=[piece] * 6 + [resident(a.shape) for a in (own, first, second)],
             out_specs=rows_of(block, width),
+            scratch_shapes=[pltpu.VMEM((block, width), FULL)],
         ),
         out_shape=shape((rows, width), kind),
-        compiler_params=params(24),
+        compiler_params=params(40),
         cost_estimate=brief(),
         name="first_back",
-    )(half, *grads, *weights)
-
-
-def frames_back_kernel(where_ref, ym_ref, yr_ref, dx1_ref, frame_ref, gain_ref, out_ref, sums_ref):
+    )(place, *grads, own, first, second)
+
+
+def frames_back_kernel(place_ref, ym_ref, yr_ref, dx1_ref, frame_ref, gain_ref, out_ref, sums_ref):
     @pl.when(pl.program_id(0) == 0)
     def _():
         sums_ref[...] = jnp.zeros_like(sums_ref)
@@ -789,7 +1017,7 @@
     out_ref[...] = lower(dx1_ref[...] + norm_pull(y, scaled, inverse, gain_ref[0:1, :]))
 
 
-def frames_back(where, ym, yr, dx1, frames, gains):
+def frames_back(place, ym, yr, dx1, frames, gains):
     rows, width = dx1.shape
     block = 208
     wide = rows_of(block, width)
@@ -805,7 +1033,7 @@
         compiler_params=params(24),
         cost_estimate=brief(),
         name="frames_back",
-    )(where, ym, yr, dx1, frames, gains)
+    )(place, ym, yr, dx1, frames, gains)
 
 
 def chip_local(
@@ -817,8 +1045,9 @@
     side = at // 2
     column = lax.axis_index("wide") % 2
     layer = lax.axis_index("wide") // 2
-    where = core.reshape(1).astype(jnp.int32)
-    away = (1 - core).reshape(1).astype(jnp.int32)
+    near = layer % 2
+    place = jnp.stack([core, near]).astype(jnp.int32)
+    away = jnp.stack([1 - core, near]).astype(jnp.int32)
     limit = lax.dynamic_slice(lengths, (side,), (1,))
     rows, width = frames.shape
     join = lax.optimization_barrier
@@ -832,9 +1061,9 @@
     def along_wide(v, pairs):
         return lax.ppermute(v, "wide", pairs)
 
-    def half_of(v, which):
-        half = v.shape[0] // 2
-        return lax.dynamic_slice_in_dim(v, which * half, half, axis=0)
+    def half_of(v, which, axis=0):
+        half = v.shape[axis] // 2
+        return lax.dynamic_slice_in_dim(v, which * half, half, axis=axis)
 
     def ordered(first, second, which):
         return jnp.where(
@@ -843,53 +1072,46 @@
             jnp.concatenate([second, first], axis=0),
         )
 
-    near = layer % 2
-
-    def ask(v, which):
-        return over_y(half_of(v, which))
-
+    frames_other = over_core(frames)
+    qkv_first = over_y(half_of(w_qkv, near, 1))
+    dout = jnp.where(loss_mask[:, None] != 0, cotangent, jnp.zeros((), ROUND))
     inward = jnp.concatenate([w_cross_q, w_cross_kv.reshape(2 * width, 256)], axis=0)
     outward = jnp.concatenate([w_out, w_cross_out], axis=0)
-    qkv_first = ask(w_qkv.reshape(3 * width, 256), near)
-    scaled, _ = norm_parts(frames.astype(FULL))
-    h1 = lower(scaled * norm_gain[0] + norm_bias[0])
-    h1_other = over_core(h1)
-    dout = jnp.where(loss_mask[:, None] != 0, cotangent, jnp.zeros((), ROUND))
-    q0, k0, v0 = project(where, h1, h1_other, w_qkv, False)
+    h1, q0, k0, v0 = first_project(place, frames, frames_other, norm_gain, norm_bias, w_qkv)
 
     q0, qkv_first, inward, outward, dout = join((q0, qkv_first, inward, outward, dout))
     qkv_second = along_wide(qkv_first, Z_NEAR)
-    outward_first = ask(outward, column)
-    inward_first = ask(inward, column)
+    outward_first = over_y(half_of(outward, column))
+    inward_first = over_y(half_of(inward, near))
+    dout_other = over_core(dout)
     own_wo = over_core(outward)
     own_wq = over_core(w_cross_q)
-    dout_other = over_core(dout)
     o0, lse0 = self_forward(limit, q0, k0, v0)
 
-    o0, qkv_second, w_up_sent = join((o0, qkv_second, w_up))
-    qkv_y = ordered(qkv_first, qkv_second, near).reshape(3, width, 256)
-    q1, k1, v1 = project(where, h1, h1_other, qkv_y, False)
+    o0, qkv_second, w_up, w_down = join((o0, qkv_second, w_up, w_down))
+    q1, k1, v1 = project(place, h1, qkv_first, qkv_second)
 
     def away_rows(v):
         return half_of(v, 1 - core)
 
     o0_other = over_core(away_rows(o0))
-    q1, outward_first, inward_first, w_up_sent, o0_other, own_wo, own_wq = join(
-        (q1, outward_first, inward_first, w_up_sent, o0_other, own_wo, own_wq)
+    up_sent = half_of(w_up, near, 1)
+    down_sent = half_of(w_down, near)
+    q1, outward_first, inward_first, up_sent, down_sent, o0_other, own_wo, own_wq = join(
+        (q1, outward_first, inward_first, up_sent, down_sent, o0_other, own_wo, own_wq)
     )
     outward_second = along_wide(outward_first, X_PAIRS)
-    inward_second = along_wide(inward_first, X_PAIRS)
-    up_first = ask(w_up_sent, column)
+    inward_second = along_wide(inward_first, Z_NEAR)
+    up_first = over_y(up_sent)
     o1, lse1 = self_forward(limit, q1, k1, v1)
     o1_other = over_core(away_rows(o1))
-
-    o1, outward_second, inward_second, up_first, w_down_sent = join(
-        (o1, outward_second, inward_second, up_first, w_down)
-    )
-    up_second = along_wide(up_first, X_PAIRS)
-    down_first = ask(w_down_sent, near)
+    o1, outward_second, inward_second, down_sent, dout_other = join(
+        (o1, outward_second, inward_second, down_sent, dout_other)
+    )
+
+    down_first = over_y(down_sent)
     outward_y = ordered(outward_first, outward_second, column)
-    inward_y = ordered(inward_first, inward_second, column)
+    inward_y = ordered(inward_first, inward_second, near)
     out_y = outward_y[:256]
     cross_out_y = outward_y[256:]
     cross_q_y = inward_y[:width]
@@ -913,28 +1135,30 @@
     ck = (spread_heads(pair[:, 0]), spread_heads(pair_other[:, 0]))
     cv = (spread_heads(pair[:, 1]), spread_heads(pair_other[:, 1]))
     x1, x2, h2, cq, ca, h3 = middle_forward(
-        where, frames, (o0, o1), (o0_other, o1_other), norm_gain, norm_bias, wo, wq, ck, cv, wc
-    )
+        place, frames, (o0, o1), (o0_other, o1_other), norm_gain, norm_bias, wo, wq, ck, cv, wc
+    )
+    h3, ca, h2, up_first, down_first = join((h3, ca, h2, up_first, down_first))
+
     h3_other = over_core(h3)
+    up_second = along_wide(up_first, Z_NEAR)
+    down_second = along_wide(down_first, Z_NEAR)
+    g0, du0, out_m, y_m = feed(place, h3, dout, (w_up,), (w_down,), FULL, 0)
+    g0, du0, out_o, y_o = feed(
+        place, h3_other, dout_other, (w_up,), (w_down,), FULL, 1, shared=(g0, du0)
+    )
+    y_o, up_second, down_second, ca, h2 = join((y_o, up_second, down_second, ca, h2))
+
+    ups = (up_first, up_second)
+    downs = (down_first, down_second)
+    g1, du1, out_o, y_o = feed(
+        place, h3_other, dout_other, ups, downs, ROUND, 1, before=(out_o, y_o)
+    )
+    y_received = over_core(y_o)
     h2_other = over_core(h2)
     ca_other = over_core(ca[:, 512:])
-
-    h3, up_second, down_first = join((h3, up_second, down_first))
-    down_second = along_wide(down_first, Z_NEAR)
-    up_y = ordered(up_first, up_second, column)
-    g0, du0, out_m, y_m = feed(where, h3, dout, w_up, w_down, FULL)
-    g0, du0, out_o, y_o = feed(
-        where, h3_other, dout_other, w_up, w_down, FULL, shared=(g0, du0)
-    )
-    y_o, down_second = join((y_o, down_second))
-    down_y = ordered(down_first, down_second, near)
-    h3_rows = jnp.concatenate([h3, h3_other], axis=0)
-    dout_rows = jnp.concatenate([dout, dout_other], axis=0)
-    g1, du1, out_m, y_m = feed(where, h3, dout, up_y, down_y, FULL, before=(out_m, y_m))
-    g1, du1, out_o, y_o = feed(
-        where, h3_other, dout_other, up_y, down_y, ROUND, before=(out_o, y_o), shared=(g1, du1)
-    )
-    y_received = over_core(y_o)
+    g1, du1, out_m, y_m = feed(
+        place, h3, dout, ups, downs, FULL, 0, before=(out_m, y_m), shared=(g1, du1)
+    )
 
     def plus(a, b):
         return lower(a.astype(FULL) + b.astype(FULL))
@@ -989,21 +1213,24 @@
             self.kept = self.kept + self.fly
             self.fly = step(self.kept)
 
-    up1 = lower(tn(h3_rows, du1))
+    up1 = up_grad(h3, h3_other, du1, ROUND)
     up1, g1, du0, g0 = join((up1, g1, du0, g0))
     up = Sum(up1)
-    down1 = lower(tn(g1, dout_rows))
-    up0 = tn(h3_rows, du0)
-    down0 = tn(g0, dout_rows)
+    down1 = down_grad(g1, dout, dout_other, ROUND)
+    (y_received, down1) = join((y_received, down1))
     dx1, dself, dcross, dcq, dck, dcv, sums = middle_back(
-        where, y_m, y_received, x1, x2, dout, cq, norm_gain, wq, ck, cv, wc
-    )
-    dself, dcross, dcq, down1, up0, down0 = sync([up], dself, dcross, dcq, down1, up0, down0)
+        place, y_m, y_received, x1, x2, dout, cq, norm_gain, wq, ck, cv, wc
+    )
+    du0, dself = join((du0, dself))
+    up0 = up_grad(h3, h3_other, du0, FULL)
+    dself_other = over_core(dself)
+    dself, dself_other, dcross, dcq, down1, up0, g0 = sync(
+        [up], dself, dself_other, dcross, dcq, down1, up0, g0
+    )
 
     down = Sum(down1, (down_z, across))
     up.first(up0)
-    dself_other = over_core(dself)
-    do0, do1 = project(where, dself, dself_other, jnp.stack([w_out, out_y]), True)
+    do0, do1 = pull(place, dself, dself_other, (w_out, out_y))
     dcross_other = over_core(dcross)
     dcq_other = over_core(dcq[:, 512:])
     d_pair = jnp.stack([dck, dcv], axis=1)
@@ -1015,45 +1242,28 @@
 
     up.second()
     d_pair = lower(d_pair[:2] + d_pair_other)
-    h1_rows = ordered(h1, h1_other, core)
-    qkv1 = lower(jnp.concatenate([tn(h1_rows, g) for g in (dq1, dk1, dv1)], axis=0))
-    h2_rows = jnp.concatenate([h2, h2_other], axis=0)
-
-    def both(mine, other, g):
-        lanes = slice(g * 256, (g + 1) * 256)
-        return jnp.concatenate([mine[:, lanes], other[:, lanes]], axis=0)
-
-    def into(g):
-        return jnp.concatenate(
-            [tn(h2_rows, both(dcq, dcq_other, g)), tn(text, d_pair[g, 0]), tn(text, d_pair[g, 1])],
-            axis=0,
-        )
-
-    def outof(g, o):
-        return jnp.concatenate(
-            [tn(o, dself_rows), tn(both(ca, ca_other, g), dcross_rows)], axis=0
-        )
-
-    into1 = lower(into(1))
-    qkv1, into1, do0, dself, dcross = sync([down, up], qkv1, into1, do0, dself, dcross)
+    qkv1 = qkv_grad(place, h1, (dq1, dk1, dv1), ROUND)
+    down0 = down_grad(g0, dout, dout_other, FULL)
+    cross = (h2, h2_other, dcq, dcq_other, text)
+    outer = (dself, dself_other, ca, ca_other, dcross, dcross_other)
+    into1 = cross_in_grad(1, *cross, d_pair[1], ROUND)
+    qkv1, into1, do0, down0 = sync([down, up], qkv1, into1, do0, down0)
 
     qkv = Sum(qkv1)
     down.first(down0)
     up.far()
     dq0, dk0, dv0 = self_back(limit, q0, k0, v0, o0, do0, lse0)
-    dself_rows = ordered(dself, dself_other, core)
-    dcross_rows = jnp.concatenate([dcross, dcross_other], axis=0)
     grads = (dq0, dk0, dv0, dq1, dk1, dv1)
-    yo = first_back(away, grads, (w_qkv, qkv_y), ROUND)
-    dq0, dself_rows, dcross_rows, yo = sync([down, up], dq0, dself_rows, dcross_rows, yo)
+    yo = first_back(away, grads, w_qkv, qkv_first, qkv_second, ROUND)
+    dq0, yo = sync([down, up], dq0, yo)
 
     down.second()
     up.back()
     y_received = over_core(yo)
-    qkv0 = jnp.concatenate([tn(h1_rows, g) for g in (dq0, dk0, dv0)], axis=0)
+    qkv0 = qkv_grad(place, h1, (dq0, dk0, dv0), FULL)
     grads = (dq0, dk0, dv0, dq1, dk1, dv1)
-    ym = first_back(where, grads, (w_qkv, qkv_y), FULL)
-    outof1 = lower(outof(1, o1))
+    ym = first_back(place, grads, w_qkv, qkv_first, qkv_second, FULL)
+    outof1 = outputs_grad(place, 1, o1, *outer, ROUND)
     qkv0, ym, y_received, outof1, x2 = sync(
         [qkv, down, up], qkv0, ym, y_received, outof1, x2
     )
@@ -1062,10 +1272,10 @@
     qkv.first(qkv0)
     down.far()
     up.along()
-    grad_frames, first_sums = frames_back(where, ym, y_received, dx1, frames, norm_gain)
+    grad_frames, first_sums = frames_back(place, ym, y_received, dx1, frames, norm_gain)
     norms = Row(sums + first_sums, over_core)
-    into0 = into(0)
-    outof0 = outof(0, o0)
+    into0 = cross_in_grad(0, *cross, d_pair[0], FULL)
+    outof0 = outputs_grad(place, 0, o0, *outer, FULL)
     text_part = 0.0
     for g, weights in ((0, w_cross_kv), (1, cross_kv_y)):
         for c in range(2):

time: 614 us -> 590 us (0.961)
  Pallas kernels: 195 us -> 255 us
  matrix products: 50.4 us -> 3.01 us
  other arithmetic: 83 us -> 61.9 us
  waiting for transfers between devices: 166 us -> 151 us
    pallas_call x7 -> x17, Pallas kernels: 67.4 us -> 126 us  [the longest x4 51.6 us: feed(): pl.pallas_call(functools.partial(feed_kernel, parts=parts, carried=len(be...]
    dot_general x20 -> x0, matrix products: 47.2 us -> none  [tn(): lax.dot_general(a, b, (((0,), (0,)), ((), ())), preferred_element_type=FULL)]
    ppermute x12, waiting for transfers between devices: 60 us -> 37.7 us  [over_y(): return lax.ppermute(v, 'narrow', Y_PAIRS)]
    select_n x14 -> x9, other arithmetic: 29 us -> 10.3 us  [ordered(): jnp.where(which == 0, jnp.concatenate([first, second], axis=0), jnp.conca...]
    concatenate x7 -> x0, other arithmetic: 9.6 us -> none  [the longest x2 3.11 us: into(): jnp.concatenate([tn(h2_rows, both(dcq, dcq_other, g)), tn(text, d_pair[g,...]
    ppermute x33, waiting for transfers between devices: 106 us -> 113 us  [along_wide(): return lax.ppermute(v, 'wide', pairs)]
    concatenate x3 -> x0, local copies, waits for them, and re-layouts: 7.35 us -> none  [the longest x1 2.93 us: chip_local(): h3_rows = jnp.concatenate([h3, h3_other], axis=0)]
    convert_element_type x19 -> x18, other arithmetic: 18.3 us -> 22.9 us  [lower(): return values_in.astype(jnp.bfloat16)]
  transfers between devices with their start and end apart: 66 -> 66, of which waited for: 20 -> 19; matrix products, arithmetic and copies ran while one was open for 26% -> 15% of each run, Pallas kernels for 32% -> 42%
where the time goes in v5:
time: 590 us; the launch traced here: 580 us
  Pallas kernels  255 us (43%)
  waiting for transfers between devices  151 us (26%)
  other arithmetic  61.9 us (10%)
  starting transfers between devices  54.4 us (9%)
  local copies, waits for them, and re-layouts  52.2 us (9%)
    ppermute x33, waiting for transfers between devices, along_wide(): return lax.ppermute(v, 'wide', pairs)  113 us
    pallas_call x4, Pallas kernels, feed(): pl.pallas_call(functools.partial(feed_kernel, parts=parts, carried=len(be...  51.6 us
    pallas_call x2, Pallas kernels, self_back(): pl.pallas_call(functools.partial(self_back_kernel, span=span, floor=floor...  40.3 us
    ppermute x12, waiting for transfers between devices, over_y(): return lax.ppermute(v, 'narrow', Y_PAIRS)  37.7 us
    ppermute x33, starting transfers between devices, along_wide(): return lax.ppermute(v, 'wide', pairs)  36.4 us
    pallas_call x2, Pallas kernels, self_forward(): pl.pallas_call(functools.partial(self_forward_kernel, span=span, floor=fl...  28.6 us
    unnamed x254, local copies, waits for them, and re-layouts  25.7 us
    pallas_call x1, Pallas kernels, middle_back(): pl.pallas_call(middle_back_kernel, grid_spec=pltpu.PrefetchScalarGridSpec...  23.2 us
  transfers between devices with their start and end apart: 66, of which 19 were waited for; matrix products, arithmetic and copies ran while one was open for 15% of the time, Pallas kernels for 42%

profile of v5, /device:TPU:0, one launch (start us, length us, event | category | flops | bytes accessed | tf_op | source)
XLA Modules:
  0.0 579.9 jit_solution(340098396661562773)
XLA Ops:
  2.4 2.6 collective-permute-start.1
  5.0 2.4 pad_maximum_fusion.1
  8.6 3.0 pad_maximum_fusion
  11.7 6.2 %first_project.1 = (bf16[1664,1024]{1,0:T(8,128)(2,1)S(1)}, bf16[1664,256]{1,0:T(8,128)(2,1)S(1)}, bf16[1664,256]{1,0:T(8,128)(2,1)S(1)}, bf16[1664,256]{1,0:T(8,128)(2,1)S(1)}) custom-call(s32[2]{0:T(128)S(1)} %pad_add_fusion.place_ref, bf16[832,1024]{1,0:T(8,128)(2,1)S(1)} %copy-done.15, bf16[832,1024]{1,0:T(8,128)(2,1)} %collective-permute-done.other_ref, ...), custom_call_target="tpu_custom_call" | custom-call | flops 1000 | bytes 1000 | tf_op jit(solution)/shard_map/first_project/pallas_call | solution.py:392
  23.2 1.8 collective-permute-start.2
  26.7 2.1 constant_dynamic-slice_fusion.4
  30.3 1.9 constant_dynamic-slice_fusion.5
  32.2 14.4 %self_forward.2 = (bf16[1664,256]{1,0:T(8,128)(2,1)}, f32[2,8,1664]{2,1,0:T(8,128)}) custom-call(s32[1]{0:T(128)} %dynamic_slice.117.limit_ref, bf16[1664,256]{1,0:T(8,128)(2,1)} %copy-done.50, bf16[1664,256]{1,0:T(8,128)(2,1)} %copy-done.52, bf16[1664,256]{1,0:T(8,128)(2,1)} %copy-done.54), custom_call_target="tpu_custom_call" | custom-call | flops 1000 | bytes 1000 | tf_op jit(solution)/shard_map/self_forward/pallas_call | solution.py:522
  49.1 3.6 project.1
  53.8 1.8 copy-done.84
  56.7 4.4 collective-permute-done.3
  64.7 14.2 %self_forward.3 = (bf16[1664,256]{1,0:T(8,128)(2,1)}, f32[2,8,1664]{2,1,0:T(8,128)}) custom-call(s32[1]{0:T(128)} %dynamic_slice.117.limit_ref, bf16[1664,256]{1,0:T(8,128)(2,1)} %copy-done.56, bf16[1664,256]{1,0:T(8,128)(2,1)} %copy-done.58, bf16[1664,256]{1,0:T(8,128)(2,1)} %copy-done.60), custom_call_target="tpu_custom_call" | custom-call | flops 1000 | bytes 1000 | tf_op jit(solution)/shard_map/self_forward/pallas_call | solution.py:522
  79.9 2.2 fusion.30
  84.8 2.3 maximum_select_fusion.2
  94.0 21.2 %middle_forward.1 = (f32[832,1024]{1,0:T(8,128)}, f32[832,1024]{1,0:T(8,128)}, bf16[832,1024]{1,0:T(8,128)(2,1)}, bf16[832,1024]{1,0:T(8,128)(2,1)}, bf16[832,10...) custom-call(s32[2]{0:T(128)} %copy-done.75, bf16[832,1024]{1,0:T(8,128)(2,1)} %frame_ref.3, ...), custom_call_target="tpu_custom_call" | custom-call | flops 1000 | bytes 1000 | tf_op jit(solution)/shard_map/middle_forward/pallas_call | solution.py:671
  117.6 12.1 %feed.4 = (bf16[1664,1024]{1,0:T(8,128)(2,1)}, bf16[1664,1024]{1,0:T(8,128)(2,1)}, f32[832,1024]{1,0:T(8,128)}, f32[832,1024]{1,0:T(8,128)}) custom-call(s32[2]{0:T(128)} %copy-done.75, bf16[832,1024]{1,0:T(8,128)(2,1)} %get-tuple-element.198.h_ref.mine_ref, bf16[832,1024]{1,0:T(8,128)(2,1)} %copy-done.2, bf16[1024,1024]{1,0:T(8,128)(2,1)} %refs_0_.5, ...), custom_call_target="tpu_custom_call" | custom-call | flops 1000 | bytes 1000 | tf_op jit(solution)/shard_map/feed/pallas_call | solution.py:728
  131.0 12.1 %feed.5 = (bf16[1664,1024]{1,0:T(8,128)(2,1)}, bf16[1664,1024]{1,0:T(8,128)(2,1)}, f32[832,1024]{1,0:T(8,128)}, f32[832,1024]{1,0:T(8,128)}) custom-call(s32[2]{0:T(128)} %copy-done.75, bf16[832,1024]{1,0:T(8,128)(2,1)} %copy-done.8, bf16[832,1024]{1,0:T(8,128)(2,1)} %collective-permute-done.10.d_ref.other_ref, ...), custom_call_target="tpu_custom_call", output_to_operand_aliasing={{0}: (5, {}), {1}: (6, {})} | custom-call | flops 1000 | bytes 1000 | tf_op jit(solution)/shard_map/feed/pallas_call | solution.py:728
  143.2 20.2 %collective-permute-done.19.refs_3_ = bf16[512,1024]{1,0:T(8,128)(2,1)S(1)} collective-permute-done((bf16[512,1024]{1,0:T(8,128)(2,1)S(1)}, bf16[512,1024]{1,0:T(8,128)(2,1)S(1)}, u32[]{:S(2)}, u32[]{:S(2)}) %collective-permute-start.19) | collective-permute-done | bytes 1048608 | tf_op jit(solution)/shard_map/ppermute | solution.py:1062
  164.3 13.6 %feed.6 = (bf16[1664,1024]{1,0:T(8,128)(2,1)}, bf16[1664,1024]{1,0:T(8,128)(2,1)}, bf16[832,1024]{1,0:T(8,128)(2,1)}, bf16[832,1024]{1,0:T(8,128)(2,1)}) custom-call(s32[2]{0:T(128)} %copy-done.75, bf16[832,1024]{1,0:T(8,128)(2,1)} %copy-done.8, bf16[832,1024]{1,0:T(8,128)(2,1)} %collective-permute-done.10.d_ref.other_ref, bf16[1024,512]{1,0:T(8,128)(2,1)} %copy-done.95, ...), custom_call_target="tpu_custom_call" | custom-call | flops 1000 | bytes 1000 | tf_op jit(solution)/shard_map/feed/pallas_call | solution.py:728
  178.0 13.7 %feed.7 = (bf16[1664,1024]{1,0:T(8,128)(2,1)}, bf16[1664,1024]{1,0:T(8,128)(2,1)}, f32[832,1024]{1,0:T(8,128)}, f32[832,1024]{1,0:T(8,128)}) custom-call(s32[2]{0:T(128)} %copy-done.75, bf16[832,1024]{1,0:T(8,128)(2,1)} %get-tuple-element.198.h_ref.mine_ref, bf16[832,1024]{1,0:T(8,128)(2,1)} %copy-done.2, ...), custom_call_target="tpu_custom_call", output_to_operand_aliasing={{0}: (9, {}), {1}: (10, {})} | custom-call | flops 1000 | bytes 1000 | tf_op jit(solution)/shard_map/feed/pallas_call | solution.py:728
  191.7 6.5 %up_grad.2 = bf16[1024,1024]{1,0:T(8,128)(2,1)S(1)} custom-call(bf16[832,1024]{1,0:T(8,128)(2,1)S(1)} %copy-done.7, bf16[832,1024]{1,0:T(8,128)(2,1)S(1)} %copy-done.9, bf16[1664,1024]{1,0:T(8,128)(2,1)} %get-tuple-element.215.du_ref), custom_call_target="tpu_custom_call" | custom-call | flops 1000 | bytes 1000 | tf_op jit(solution)/shard_map/up_grad/pallas_call | solution.py:758
  199.0 6.7 %down_grad.2 = bf16[1024,1024]{1,0:T(8,128)(2,1)S(1)} custom-call(bf16[1664,1024]{1,0:T(8,128)(2,1)} %get-tuple-element.223.g_ref, bf16[832,1024]{1,0:T(8,128)(2,1)S(1)} %copy-done.3, bf16[832,1024]{1,0:T(8,128)(2,1)} %collective-permute-done.10.d_ref.other_ref), custom_call_target="tpu_custom_call" | custom-call | flops 1000 | bytes 1000 | tf_op jit(solution)/shard_map/down_grad/pallas_call | solution.py:781
  207.1 23.2 %middle_back.1 = (f32[832,1024]{1,0:T(8,128)}, bf16[832,1024]{1,0:T(8,128)(2,1)}, bf16[832,1024]{1,0:T(8,128)(2,1)}, bf16[832,1024]{1,0:T(8,128)(2,1)}, f32[4,64...) custom-call(s32[2]{0:T(128)} %copy-done.75, f32[832,1024]{1,0:T(8,128)} %get-tuple-element.221.ym_ref, ...), custom_call_target="tpu_custom_call" | custom-call | flops 1000 | bytes 1000 | tf_op jit(solution)/shard_map/middle_back/pallas_call | solution.py:948
  230.6 7.5 %up_grad.3 = f32[1024,1024]{1,0:T(8,128)} custom-call(bf16[832,1024]{1,0:T(8,128)(2,1)S(1)} %copy-done.7, bf16[832,1024]{1,0:T(8,128)(2,1)S(1)} %copy-done.9, bf16[1664,1024]{1,0:T(8,128)(2,1)} %get-tuple-element.233.du_ref), custom_call_target="tpu_custom_call" | custom-call | flops 1000 | bytes 1000 | tf_op jit(solution)/shard_map/up_grad/pallas_call | solution.py:758
  238.1 8.3 %collective-permute-done.20 = bf16[1024,1024]{1,0:T(8,128)(2,1)} collective-permute-done((bf16[1024,1024]{1,0:T(8,128)(2,1)S(1)}, bf16[1024,1024]{1,0:T(8,128)(2,1)}, u32[]{:S(2)}, u32[]{:S(2)}) %collective-permute-start.20) | collective-permute-done | bytes 2097184 | tf_op jit(solution)/shard_map/ppermute | solution.py:1059
  247.3 3.6 add_convert_fusion.2
  255.5 2.8 pull.1
  260.1 20.3 %self_back.2 = (bf16[1664,256]{1,0:T(8,128)(2,1)S(1)}, bf16[1664,256]{1,0:T(8,128)(2,1)S(1)}, bf16[1664,256]{1,0:T(8,128)(2,1)S(1)}) custom-call(s32[1]{0:T(128)} %dynamic_slice.117.limit_ref, bf16[1664,256]{1,0:T(8,128)(2,1)S(1)} %copy-done.57, bf16[1664,256]{1,0:T(8,128)(2,1)S(1)} %copy-done.59, bf16[1664,256]{1,0:T(8,128)(2,1)S(1)} %copy-done.61, ...), custom_call_target="tpu_custom_call" | custom-call | flops 1000 | bytes 1000 | tf_op jit(solution)/shard_map/self_back/pallas_call | solution.py:603
  280.4 3.0 convert_add_fusion.1
  286.4 8.3 %down_grad.3 = f32[1024,1024]{1,0:T(8,128)} custom-call(bf16[1664,1024]{1,0:T(8,128)(2,1)} %get-tuple-element.255.g_ref, bf16[832,1024]{1,0:T(8,128)(2,1)S(1)} %copy-done.4, bf16[832,1024]{1,0:T(8,128)(2,1)} %collective-permute-done.10.d_ref.other_ref), custom_call_target="tpu_custom_call" | custom-call | flops 1000 | bytes 1000 | tf_op jit(solution)/shard_map/down_grad/pallas_call | solution.py:781
  294.8 6.0 %qkv_grad.2 = bf16[3072,256]{1,0:T(8,128)(2,1)S(1)} custom-call(s32[2]{0:T(128)S(1)} %copy-done.77, bf16[1664,1024]{1,0:T(8,128)(2,1)} %copy-done.5, bf16[1664,256]{1,0:T(8,128)(2,1)S(1)} %copy-done.30, bf16[1664,256]{1,0:T(8,128)(2,1)S(1)} %copy-done.34, bf16[1664,256]{1,0:T(8,128)(2,1)S(1)} %copy-done.38), custom_call_target="tpu_custom_call" | custom-call | flops 1000 | bytes 1000 | tf_op jit(solution)/shard_map/qkv_grad/pallas_call | solution.py:810
  302.6 3.9 cross_in_grad.2
  306.6 3.1 add_convert_fusion.1
  312.0 2.6 collective-permute-start.32
  319.4 20.0 %self_back.3 = (bf16[1664,256]{1,0:T(8,128)(2,1)S(1)}, bf16[1664,256]{1,0:T(8,128)(2,1)S(1)}, bf16[1664,256]{1,0:T(8,128)(2,1)S(1)}) custom-call(s32[1]{0:T(128)} %dynamic_slice.117.limit_ref, bf16[1664,256]{1,0:T(8,128)(2,1)S(1)} %copy-done.51, bf16[1664,256]{1,0:T(8,128)(2,1)S(1)} %copy-done.53, bf16[1664,256]{1,0:T(8,128)(2,1)S(1)} %copy-done.55, ...), custom_call_target="tpu_custom_call" | custom-call | flops 1000 | bytes 1000 | tf_op jit(solution)/shard_map/self_back/pallas_call | solution.py:603
  339.5 5.1 first_back.2
  351.5 3.3 collective-permute-start.34
  354.8 2.7 convert_add_fusion
  360.3 5.0 outputs_grad.2
  365.3 6.7 %outputs_grad.3 = f32[512,1024]{1,0:T(8,128)} custom-call(s32[2]{0:T(128)S(1)} %copy-done.77, bf16[1664,256]{1,0:T(8,128)(2,1)S(1)} %copy-done.20, bf16[832,1024]{1,0:T(8,128)(2,1)S(1)} %copy-done.12, bf16[832,1024]{1,0:T(8,128)(2,1)S(1)} %copy-done.14, bf16[832,1024]{1,0:T(8,128)(2,1)} %get-tuple-element.269.am_ref, ...), custom_call_target="tpu_custom_call" | custom-call | flops 1000 | bytes 1000 | tf_op jit(solution)/shard_map/outputs_grad/pallas_call | solution.py:871
  372.1 5.4 cross_in_grad.3
  380.0 3.8 first_back.3.ym_ref
  383.9 6.3 %qkv_grad.3 = f32[3072,256]{1,0:T(8,128)S(1)} custom-call(s32[2]{0:T(128)S(1)} %copy-done.77, bf16[1664,1024]{1,0:T(8,128)(2,1)} %copy-done.5, bf16[1664,256]{1,0:T(8,128)(2,1)S(1)} %copy-done.24, bf16[1664,256]{1,0:T(8,128)(2,1)S(1)} %copy-done.26, bf16[1664,256]{1,0:T(8,128)(2,1)S(1)} %copy-done.28), custom_call_target="tpu_custom_call" | custom-call | flops 1000 | bytes 1000 | tf_op jit(solution)/shard_map/qkv_grad/pallas_call | solution.py:810
  391.6 6.2 %frames_back.1 = (bf16[832,1024]{1,0:T(8,128)(2,1)}, f32[8,1024]{1,0:T(8,128)S(1)}) custom-call(s32[2]{0:T(128)S(1)} %copy-done.77, f32[832,1024]{1,0:T(8,128)S(1)} %first_back.3.ym_ref, bf16[832,1024]{1,0:T(8,128)(2,1)} %collective-permute-done.35.yr_ref, f32[832,1024]{1,0:T(8,128)S(1)} %copy-done.49, bf16[832,1024]{1,0:T(8,128)(2,1)S(1)} %copy-done.16, ...), custom_call_target="tpu_custom_call" | custom-call | flops 1000 | bytes 1000 | tf_op jit(solution)/shard_map/frames_back/pallas_call | solution.py:1024
  402.1 3.8 add_convert_fusion
  405.9 2.9 maximum_select_fusion.6
  409.7 18.1 %collective-permute-done.38 = bf16[256,1024]{1,0:T(8,128)(2,1)S(1)} collective-permute-done((bf16[256,1024]{1,0:T(8,128)(2,1)S(1)}, bf16[256,1024]{1,0:T(8,128)(2,1)S(1)}, u32[]{:S(2)}, u32[]{:S(2)}) %collective-permute-start.38) | collective-permute-done | bytes 524320 | tf_op jit(solution)/shard_map/ppermute | solution.py:1062
  429.8 1.8 convert_add_fusion.3
  436.1 23.7 %collective-permute-done.50 = bf16[64,1024]{1,0:T(8,128)(2,1)S(1)} collective-permute-done((bf16[64,1024]{1,0:T(8,128)(2,1)S(1)}, bf16[64,1024]{1,0:T(8,128)(2,1)S(1)}, u32[]{:S(2)}, u32[]{:S(2)}) %collective-permute-start.50) | collective-permute-done | bytes 131104 | tf_op jit(solution)/shard_map/ppermute | solution.py:1059
  463.5 1.8 collective-permute-start.55
  466.5 5.4 fusion
  472.6 5.7 collective-permute-done.46
  482.4 1.9 collective-permute-start.52
  484.5 12.9 %collective-permute-done.54 = bf16[768,256]{1,0:T(8,128)(2,1)S(1)} collective-permute-done((bf16[768,256]{1,0:T(8,128)(2,1)S(1)}, bf16[768,256]{1,0:T(8,128)(2,1)S(1)}, u32[]{:S(2)}, u32[]{:S(2)}) %collective-permute-start.54) | collective-permute-done | bytes 393248 | tf_op jit(solution)/shard_map/ppermute | solution.py:1062
  498.2 2.9 fusion.1
  501.6 5.7 collective-permute-done.53
  512.9 2.9 collective-permute-start.57
  515.8 8.8 %collective-permute-done.59 = bf16[128,1024]{1,0:T(8,128)(2,1)} collective-permute-done((bf16[128,1024]{1,0:T(8,128)(2,1)}, bf16[128,1024]{1,0:T(8,128)(2,1)}, u32[]{:S(2)}, u32[]{:S(2)}) %collective-permute-start.59) | collective-permute-done | bytes 262176 | tf_op jit(solution)/shard_map/ppermute | solution.py:1062
  528.6 8.8 %collective-permute-done.57 = f32[8,1024]{1,0:T(8,128)S(1)} collective-permute-done((f32[8,1024]{1,0:T(8,128)S(1)}, f32[8,1024]{1,0:T(8,128)S(1)}, u32[]{:S(2)}, u32[]{:S(2)}) %collective-permute-start.57) | collective-permute-done | bytes 32800 | tf_op jit(solution)/shard_map/ppermute | solution.py:1062
  537.5 2.8 collective-permute-done.62
  541.8 8.7 %collective-permute-done.63 = bf16[128,1024]{1,0:T(8,128)(2,1)S(1)} collective-permute-done((bf16[128,1024]{1,0:T(8,128)(2,1)S(1)}, bf16[128,1024]{1,0:T(8,128)(2,1)S(1)}, u32[]{:S(2)}, u32[]{:S(2)}) %collective-permute-start.63) | collective-permute-done | bytes 262176 | tf_op jit(solution)/shard_map/ppermute | solution.py:1062
  553.4 1.9 convert.1
  555.3 10.2 %collective-permute-done.64 = bf16[256,1024]{1,0:T(8,128)(2,1)S(1)} collective-permute-done((bf16[256,1024]{1,0:T(8,128)(2,1)S(1)}, bf16[256,1024]{1,0:T(8,128)(2,1)S(1)}, u32[]{:S(2)}, u32[]{:S(2)}) %collective-permute-start.64) | collective-permute-done | bytes 524320 | tf_op jit(solution)/shard_map/ppermute | solution.py:1062
  567.4 9.4 %collective-permute-done.65 = bf16[1536,256]{1,0:T(8,128)(2,1)S(1)} collective-permute-done((bf16[1536,256]{1,0:T(8,128)(2,1)S(1)}, bf16[1536,256]{1,0:T(8,128)(2,1)S(1)}, u32[]{:S(2)}, u32[]{:S(2)}) %collective-permute-start.65) | collective-permute-done | bytes 786464 | tf_op jit(solution)/shard_map/ppermute | solution.py:1062
  (440 shorter events, 111.1 us)
Async XLA Ops:
  0.7 11.0 %collective-permute-start = (bf16[832,1024]{1,0:T(8,128)(2,1)}, bf16[832,1024]{1,0:T(8,128)(2,1)}, u32[]{:S(2)}, u32[]{:S(2)}) collective-permute-start(bf16[832,1024]{1,0:T(8,128)(2,1)} %frame_ref.3), channel_id=1, source_target_pairs={{0,1},{1,0},{2,3},{3,2},{4,5},{5,4},{6,7},{7,6},{8,9},{9,8},{10,11... | collective-permute-start | bytes 5111816 | tf_op jit(solution)/shard_map/ppermute | solution.py:1056
  2.4 20.8 %collective-permute-start.1 = (bf16[3,512,256]{2,1,0:T(8,128)(2,1)S(1)}, bf16[3,512,256]{2,1,0:T(8,128)(2,1)S(1)}, u32[]{:S(2)}, u32[]{:S(2)}) collective-permute-start(bf16[3,512,256]{2,1,0:T(8,128)(2,1)S(1)} %constant_dynamic-slice_fusion.6), channel_id=1, source_target_pairs={{0,2},{2,0},{1,3},{3,1},{4,6},{6,4},{5,7},{7,5},{8,10},{10,8},{9,1... | collective-permute-start | bytes 2359304 | tf_op jit(solution)/shard_map/ppermute | solution.py:1059
  23.2 23.4 %collective-permute-start.2 = (bf16[3,512,256]{2,1,0:T(8,128)(2,1)S(1)}, bf16[3,512,256]{2,1,0:T(8,128)(2,1)S(1)}, u32[]{:S(2)}, u32[]{:S(2)}) collective-permute-start(bf16[3,512,256]{2,1,0:T(8,128)(2,1)S(1)} %collective-permute-done.1.first_ref.refs_7_), channel_id=1, source_target_pairs={{0,8},{4,12},{8,0},{12,4},{16,24},{20,28},{24,16},{28,20},{1,9},{5... | collective-permute-start | bytes 2359304 | tf_op jit(solution)/shard_map/ppermute | solution.py:1062
  25.0 23.3 %collective-permute-start.7 = (bf16[1024,256]{1,0:T(8,128)(2,1)}, bf16[1024,256]{1,0:T(8,128)(2,1)}, u32[]{:S(2)}, u32[]{:S(2)}) collective-permute-start(bf16[1024,256]{1,0:T(8,128)(2,1)} %refs_0_.6), channel_id=1, source_target_pairs={{0,1},{1,0},{2,3},{3,2},{4,5},{5,4},{6,7},{7,6},{8,9},{9,8},{10,11... | collective-permute-start | bytes 1572872 | tf_op jit(solution)/shard_map/ppermute | solution.py:1056
  26.2 34.8 %collective-permute-start.6 = (bf16[512,1024]{1,0:T(8,128)(2,1)}, bf16[512,1024]{1,0:T(8,128)(2,1)}, u32[]{:S(2)}, u32[]{:S(2)}) collective-permute-start(bf16[512,1024]{1,0:T(8,128)(2,1)} %pad_maximum_fusion.1), channel_id=1, source_target_pairs={{0,1},{1,0},{2,3},{3,2},{4,5},{5,4},{6,7},{7,6},{8,9},{9,8},{10,11... | collective-permute-start | bytes 3145736 | tf_op jit(solution)/shard_map/ppermute | solution.py:1056
  26.7 55.4 %collective-permute-start.10 = (bf16[832,1024]{1,0:T(8,128)(2,1)S(1)}, bf16[832,1024]{1,0:T(8,128)(2,1)}, u32[]{:S(2)}, u32[]{:S(2)}) collective-permute-start(bf16[832,1024]{1,0:T(8,128)(2,1)S(1)} %broadcast_select_fusion.d_ref.mine_ref), channel_id=1, source_target_pairs={{0,1},{1,0},{2,3},{3,2},{4,5},{5,4},{6,7},{7,6},{8,9},{9,8},{10,11... | collective-permute-start | bytes 5111816 | tf_op jit(solution)/shard_map/ppermute | solution.py:1056
  28.8 32.3 %collective-permute-start.4 = (bf16[1536,256]{1,0:T(8,128)(2,1)}, bf16[1536,256]{1,0:T(8,128)(2,1)}, u32[]{:S(2)}, u32[]{:S(2)}) collective-permute-start(bf16[1536,256]{1,0:T(8,128)(2,1)} %constant_dynamic-slice_fusion.4), channel_id=1, source_target_pairs={{0,2},{2,0},{1,3},{3,1},{4,6},{6,4},{5,7},{7,5},{8,10},{10,8},{9,1... | collective-permute-start | bytes 2359304 | tf_op jit(solution)/shard_map/ppermute | solution.py:1059
  46.6 14.4 %collective-permute-start.3 = (bf16[256,1024]{1,0:T(8,128)(2,1)}, bf16[256,1024]{1,0:T(8,128)(2,1)}, u32[]{:S(2)}, u32[]{:S(2)}) collective-permute-start(bf16[256,1024]{1,0:T(8,128)(2,1)} %constant_dynamic-slice_fusion.5), channel_id=1, source_target_pairs={{0,2},{2,0},{1,3},{3,1},{4,6},{6,4},{5,7},{7,5},{8,10},{10,8},{9,1... | collective-permute-start | bytes 1572872 | tf_op jit(solution)/shard_map/ppermute | solution.py:1059
  48.2 12.8 %collective-permute-start.5 = (bf16[832,256]{1,0:T(8,128)(2,1)S(1)}, bf16[832,256]{1,0:T(8,128)(2,1)S(1)}, u32[]{:S(2)}, u32[]{:S(2)}) collective-permute-start(bf16[832,256]{1,0:T(8,128)(2,1)S(1)} %constant_dynamic-slice_fusion.1), channel_id=1, source_target_pairs={{0,1},{1,0},{2,3},{3,2},{4,5},{5,4},{6,7},{7,6},{8,9},{9,8},{10,11... | collective-permute-start | bytes 1277960 | tf_op jit(solution)/shard_map/ppermute | solution.py:1056
  61.1 21.1 %collective-permute-start.9 = (bf16[1536,256]{1,0:T(8,128)(2,1)}, bf16[1536,256]{1,0:T(8,128)(2,1)S(1)}, u32[]{:S(2)}, u32[]{:S(2)}) collective-permute-start(bf16[1536,256]{1,0:T(8,128)(2,1)} %collective-permute-done.4), channel_id=1, source_target_pairs={{0,8},{4,12},{8,0},{12,4},{16,24},{20,28},{24,16},{28,20},{1,9},{5... | collective-permute-start | bytes 2359304 | tf_op jit(solution)/shard_map/ppermute | solution.py:1062
  62.0 20.1 %collective-permute-start.8 = (bf16[256,1024]{1,0:T(8,128)(2,1)}, bf16[256,1024]{1,0:T(8,128)(2,1)S(1)}, u32[]{:S(2)}, u32[]{:S(2)}) collective-permute-start(bf16[256,1024]{1,0:T(8,128)(2,1)} %collective-permute-done.3), channel_id=1, source_target_pairs={{0,4},{4,0},{8,12},{12,8},{16,20},{20,16},{24,28},{28,24},{1,5},{5... | collective-permute-start | bytes 1572872 | tf_op jit(solution)/shard_map/ppermute | solution.py:1062
  63.8 51.4 %collective-permute-start.15 = (bf16[1024,512]{1,0:T(8,128)(2,1)}, bf16[1024,512]{1,0:T(8,128)(2,1)S(1)}, u32[]{:S(2)}, u32[]{:S(2)}) collective-permute-start(bf16[1024,512]{1,0:T(8,128)(2,1)} %constant_dynamic-slice_fusion.3), channel_id=1, source_target_pairs={{0,2},{2,0},{1,3},{3,1},{4,6},{6,4},{5,7},{7,5},{8,10},{10,8},{9,1... | collective-permute-start | bytes 3145736 | tf_op jit(solution)/shard_map/ppermute | solution.py:1059
  84.7 7.3 %collective-permute-start.12 = (bf16[512,1024]{1,0:T(8,128)(2,1)S(1)}, bf16[512,1024]{1,0:T(8,128)(2,1)S(1)}, u32[]{:S(2)}, u32[]{:S(2)}) collective-permute-start(bf16[512,1024]{1,0:T(8,128)(2,1)S(1)} %maximum_select_fusion.5), channel_id=1, source_target_pairs={{0,1},{1,0},{2,3},{3,2},{4,5},{5,4},{6,7},{7,6},{8,9},{9,8},{10,11... | collective-permute-start | bytes 3145736 | tf_op jit(solution)/shard_map/ppermute | solution.py:1056
  87.3 27.9 %collective-permute-start.16 = (bf16[512,1024]{1,0:T(8,128)(2,1)S(1)}, bf16[512,1024]{1,0:T(8,128)(2,1)S(1)}, u32[]{:S(2)}, u32[]{:S(2)}) collective-permute-start(bf16[512,1024]{1,0:T(8,128)(2,1)S(1)} %copy-done.115), channel_id=1, source_target_pairs={{0,2},{2,0},{1,3},{3,1},{4,6},{6,4},{5,7},{7,5},{8,10},{10,8},{9,1... | collective-permute-start | bytes 3145736 | tf_op jit(solution)/shard_map/ppermute | solution.py:1059
  90.3 2.8 collective-permute-start.13
  90.7 2.4 collective-permute-start.11
  115.2 14.6 %collective-permute-start.17 = (bf16[832,1024]{1,0:T(8,128)(2,1)}, bf16[832,1024]{1,0:T(8,128)(2,1)S(1)}, u32[]{:S(2)}, u32[]{:S(2)}) collective-permute-start(bf16[832,1024]{1,0:T(8,128)(2,1)} %get-tuple-element.198.h_ref.mine_ref), channel_id=1, source_target_pairs={{0,1},{1,0},{2,3},{3,2},{4,5},{5,4},{6,7},{7,6},{8,9},{9,8},{10,11... | collective-permute-start | bytes 5111816 | tf_op jit(solution)/shard_map/ppermute | solution.py:1056
  115.6 27.5 %collective-permute-start.18 = (bf16[1024,512]{1,0:T(8,128)(2,1)S(1)}, bf16[1024,512]{1,0:T(8,128)(2,1)S(1)}, u32[]{:S(2)}, u32[]{:S(2)}) collective-permute-start(bf16[1024,512]{1,0:T(8,128)(2,1)S(1)} %collective-permute-done.15.refs_0_), channel_id=1, source_target_pairs={{0,8},{4,12},{8,0},{12,4},{16,24},{20,28},{24,16},{28,20},{1,9},{5... | collective-permute-start | bytes 3145736 | tf_op jit(solution)/shard_map/ppermute | solution.py:1062
  117.0 46.4 %collective-permute-start.19 = (bf16[512,1024]{1,0:T(8,128)(2,1)S(1)}, bf16[512,1024]{1,0:T(8,128)(2,1)S(1)}, u32[]{:S(2)}, u32[]{:S(2)}) collective-permute-start(bf16[512,1024]{1,0:T(8,128)(2,1)S(1)} %collective-permute-done.16.refs_2_), channel_id=1, source_target_pairs={{0,8},{4,12},{8,0},{12,4},{16,24},{20,28},{24,16},{28,20},{1,9},{5... | collective-permute-start | bytes 3145736 | tf_op jit(solution)/shard_map/ppermute | solution.py:1062
  177.9 29.1 %collective-permute-start.21 = (bf16[832,1024]{1,0:T(8,128)(2,1)}, bf16[832,1024]{1,0:T(8,128)(2,1)}, u32[]{:S(2)}, u32[]{:S(2)}) collective-permute-start(bf16[832,1024]{1,0:T(8,128)(2,1)} %get-tuple-element.222), channel_id=1, source_target_pairs={{0,1},{1,0},{2,3},{3,2},{4,5},{5,4},{6,7},{7,6},{8,9},{9,8},{10,11... | collective-permute-start | bytes 5111816 | tf_op jit(solution)/shard_map/ppermute | solution.py:1056
  198.2 48.2 %collective-permute-start.20 = (bf16[1024,1024]{1,0:T(8,128)(2,1)S(1)}, bf16[1024,1024]{1,0:T(8,128)(2,1)}, u32[]{:S(2)}, u32[]{:S(2)}) collective-permute-start(bf16[1024,1024]{1,0:T(8,128)(2,1)S(1)} %up_grad.2), channel_id=1, source_target_pairs={{0,2},{2,0},{1,3},{3,1},{4,6},{6,4},{5,7},{7,5},{8,10},{10,8},{9,1... | collective-permute-start | bytes 6291464 | tf_op jit(solution)/shard_map/ppermute | solution.py:1059
  230.3 16.1 %collective-permute-start.22 = (bf16[832,1024]{1,0:T(8,128)(2,1)}, bf16[832,1024]{1,0:T(8,128)(2,1)S(1)}, u32[]{:S(2)}, u32[]{:S(2)}) collective-permute-start(bf16[832,1024]{1,0:T(8,128)(2,1)} %get-tuple-element.238.mine_ref.sm_ref), channel_id=1, source_target_pairs={{0,1},{1,0},{2,3},{3,2},{4,5},{5,4},{6,7},{7,6},{8,9},{9,8},{10,11... | collective-permute-start | bytes 5111816 | tf_op jit(solution)/shard_map/ppermute | solution.py:1056
  246.4 34.0 %collective-permute-start.25 = (bf16[832,1024]{1,0:T(8,128)(2,1)}, bf16[832,1024]{1,0:T(8,128)(2,1)}, u32[]{:S(2)}, u32[]{:S(2)}) collective-permute-start(bf16[832,1024]{1,0:T(8,128)(2,1)} %get-tuple-element.243.cm_ref), channel_id=1, source_target_pairs={{0,1},{1,0},{2,3},{3,2},{4,5},{5,4},{6,7},{7,6},{8,9},{9,8},{10,11... | collective-permute-start | bytes 5111816 | tf_op jit(solution)/shard_map/ppermute | solution.py:1056
  246.5 60.1 %collective-permute-start.23 = (bf16[1024,1024]{1,0:T(8,128)(2,1)}, bf16[1024,1024]{1,0:T(8,128)(2,1)}, u32[]{:S(2)}, u32[]{:S(2)}) collective-permute-start(bf16[1024,1024]{1,0:T(8,128)(2,1)} %copy-done.62), channel_id=1, source_target_pairs={{0,2},{2,0},{1,3},{3,1},{4,6},{6,4},{5,7},{7,5},{8,10},{10,8},{9,1... | collective-permute-start | bytes 6291464 | tf_op jit(solution)/shard_map/ppermute | solution.py:1059
  250.9 29.5 %collective-permute-start.24 = (bf16[512,1024]{1,0:T(8,128)(2,1)}, bf16[512,1024]{1,0:T(8,128)(2,1)}, u32[]{:S(2)}, u32[]{:S(2)}) collective-permute-start(bf16[512,1024]{1,0:T(8,128)(2,1)} %add_convert_fusion.2), channel_id=1, source_target_pairs={{0,4},{4,0},{8,12},{12,8},{16,20},{20,16},{24,28},{28,24},{1,5},{5... | collective-permute-start | bytes 3145736 | tf_op jit(solution)/shard_map/ppermute | solution.py:1062
  252.5 27.8 %collective-permute-start.26 = (bf16[832,512]{1,0:T(8,128)(2,1)}, bf16[832,512]{1,0:T(8,128)(2,1)}, u32[]{:S(2)}, u32[]{:S(2)}) collective-permute-start(bf16[832,512]{1,0:T(8,128)(2,1)} %slice.117), channel_id=1, source_target_pairs={{0,1},{1,0},{2,3},{3,2},{4,5},{5,4},{6,7},{7,6},{8,9},{9,8},{10,11... | collective-permute-start | bytes 2555912 | tf_op jit(solution)/shard_map/ppermute | solution.py:1056
  253.2 49.4 %collective-permute-start.29 = (bf16[832,1024]{1,0:T(8,128)(2,1)}, bf16[832,1024]{1,0:T(8,128)(2,1)}, u32[]{:S(2)}, u32[]{:S(2)}) collective-permute-start(bf16[832,1024]{1,0:T(8,128)(2,1)} %get-tuple-element.251.mine_ref), channel_id=1, source_target_pairs={{0,1},{1,0},{2,3},{3,2},{4,5},{5,4},{6,7},{7,6},{8,9},{9,8},{10,11... | collective-permute-start | bytes 5111816 | tf_op jit(solution)/shard_map/ppermute | solution.py:1056
  285.0 21.5 %collective-permute-start.28 = (bf16[256,1024]{1,0:T(8,128)(2,1)}, bf16[256,1024]{1,0:T(8,128)(2,1)}, u32[]{:S(2)}, u32[]{:S(2)}) collective-permute-start(bf16[256,1024]{1,0:T(8,128)(2,1)} %dynamic-slice_convert_fusion.1), channel_id=1, source_target_pairs={{0,8},{4,12},{8,0},{12,4},{16,24},{20,28},{24,16},{28,20},{1,9},{5... | collective-permute-start | bytes 1572872 | tf_op jit(solution)/shard_map/ppermute | solution.py:1062
  309.7 36.7 %collective-permute-start.31 = (bf16[512,1024]{1,0:T(8,128)(2,1)}, bf16[512,1024]{1,0:T(8,128)(2,1)}, u32[]{:S(2)}, u32[]{:S(2)}) collective-permute-start(bf16[512,1024]{1,0:T(8,128)(2,1)} %add_convert_fusion.1), channel_id=1, source_target_pairs={{0,8},{4,12},{8,0},{12,4},{16,24},{20,28},{24,16},{28,20},{1,9},{5... | collective-permute-start | bytes 3145736 | tf_op jit(solution)/shard_map/ppermute | solution.py:1062
  312.0 32.6 %collective-permute-start.32 = (bf16[256,1024]{1,0:T(8,128)(2,1)S(1)}, bf16[256,1024]{1,0:T(8,128)(2,1)S(1)}, u32[]{:S(2)}, u32[]{:S(2)}) collective-permute-start(bf16[256,1024]{1,0:T(8,128)(2,1)S(1)} %add_convert_fusion.9), channel_id=1, source_target_pairs={{0,16},{4,20},{8,24},{12,28},{16,0},{20,4},{24,8},{28,12},{1,17},{... | collective-permute-start | bytes 1572872 | tf_op jit(solution)/shard_map/ppermute | solution.py:1062
  346.3 45.2 %collective-permute-start.35 = (bf16[832,1024]{1,0:T(8,128)(2,1)}, bf16[832,1024]{1,0:T(8,128)(2,1)}, u32[]{:S(2)}, u32[]{:S(2)}) collective-permute-start(bf16[832,1024]{1,0:T(8,128)(2,1)} %first_back.2), channel_id=1, source_target_pairs={{0,1},{1,0},{2,3},{3,2},{4,5},{5,4},{6,7},{7,6},{8,9},{9,8},{10,11... | collective-permute-start | bytes 5111816 | tf_op jit(solution)/shard_map/ppermute | solution.py:1056
  347.7 10.8 %collective-permute-start.36 = (bf16[832,512]{1,0:T(8,128)(2,1)S(1)}, bf16[832,512]{1,0:T(8,128)(2,1)S(1)}, u32[]{:S(2)}, u32[]{:S(2)}) collective-permute-start(bf16[832,512]{1,0:T(8,128)(2,1)S(1)} %slice.121), channel_id=1, source_target_pairs={{0,1},{1,0},{2,3},{3,2},{4,5},{5,4},{6,7},{7,6},{8,9},{9,8},{10,11... | collective-permute-start | bytes 2555912 | tf_op jit(solution)/shard_map/ppermute | solution.py:1056
  348.2 53.8 %collective-permute-start.41 = (bf16[832,1024]{1,0:T(8,128)(2,1)}, bf16[832,1024]{1,0:T(8,128)(2,1)}, u32[]{:S(2)}, u32[]{:S(2)}) collective-permute-start(bf16[832,1024]{1,0:T(8,128)(2,1)} %get-tuple-element.282), channel_id=1, source_target_pairs={{0,1},{1,0},{2,3},{3,2},{4,5},{5,4},{6,7},{7,6},{8,9},{9,8},{10,11... | collective-permute-start | bytes 5111816 | tf_op jit(solution)/shard_map/ppermute | solution.py:1056
  348.3 43.2 %collective-permute-start.30 = (bf16[3072,256]{1,0:T(8,128)(2,1)}, bf16[3072,256]{1,0:T(8,128)(2,1)}, u32[]{:S(2)}, u32[]{:S(2)}) collective-permute-start(bf16[3072,256]{1,0:T(8,128)(2,1)} %copy-done.65), channel_id=1, source_target_pairs={{0,2},{2,0},{1,3},{3,1},{4,6},{6,4},{5,7},{7,5},{8,10},{10,8},{9,1... | collective-permute-start | bytes 4718600 | tf_op jit(solution)/shard_map/ppermute | solution.py:1059
  351.5 38.7 %collective-permute-start.34 = (bf16[256,1024]{1,0:T(8,128)(2,1)}, bf16[256,1024]{1,0:T(8,128)(2,1)}, u32[]{:S(2)}, u32[]{:S(2)}) collective-permute-start(bf16[256,1024]{1,0:T(8,128)(2,1)} %add_convert_fusion.8), channel_id=1, source_target_pairs={{0,8},{4,12},{8,0},{12,4},{16,24},{20,28},{24,16},{28,20},{1,9},{5... | collective-permute-start | bytes 1572872 | tf_op jit(solution)/shard_map/ppermute | solution.py:1062
  358.4 31.9 %collective-permute-start.33 = (bf16[256,1024]{1,0:T(8,128)(2,1)}, bf16[256,1024]{1,0:T(8,128)(2,1)}, u32[]{:S(2)}, u32[]{:S(2)}) collective-permute-start(bf16[256,1024]{1,0:T(8,128)(2,1)} %dynamic-slice_convert_fusion), channel_id=1, source_target_pairs={{0,4},{4,0},{8,12},{12,8},{16,20},{20,16},{24,28},{28,24},{1,5},{5... | collective-permute-start | bytes 1572872 | tf_op jit(solution)/shard_map/ppermute | solution.py:1062
  390.2 18.7 %collective-permute-start.40 = (f32[64,1024]{1,0:T(8,128)S(1)}, f32[64,1024]{1,0:T(8,128)S(1)}, u32[]{:S(2)}, u32[]{:S(2)}) collective-permute-start(f32[64,1024]{1,0:T(8,128)S(1)} %convolution_add_fusion), channel_id=1, source_target_pairs={{0,1},{1,0},{2,3},{3,2},{4,5},{5,4},{6,7},{7,6},{8,9},{9,8},{10,11... | collective-permute-start | bytes 786440 | tf_op jit(solution)/shard_map/ppermute | solution.py:1056
  390.3 42.0 %collective-permute-start.42 = (bf16[3072,256]{1,0:T(8,128)(2,1)S(1)}, bf16[3072,256]{1,0:T(8,128)(2,1)S(1)}, u32[]{:S(2)}, u32[]{:S(2)}) collective-permute-start(bf16[3072,256]{1,0:T(8,128)(2,1)S(1)} %copy-done.64), channel_id=1, source_target_pairs={{0,2},{2,0},{1,3},{3,1},{4,6},{6,4},{5,7},{7,5},{8,10},{10,8},{9,1... | collective-permute-start | bytes 4718600 | tf_op jit(solution)/shard_map/ppermute | solution.py:1059
  397.9 11.8 %collective-permute-start.39 = (f32[8,1024]{1,0:T(8,128)S(1)}, f32[8,1024]{1,0:T(8,128)S(1)}, u32[]{:S(2)}, u32[]{:S(2)}) collective-permute-start(f32[8,1024]{1,0:T(8,128)S(1)} %add.234), channel_id=1, source_target_pairs={{0,1},{1,0},{2,3},{3,2},{4,5},{5,4},{6,7},{7,6},{8,9},{9,8},{10,11... | collective-permute-start | bytes 98312 | tf_op jit(solution)/shard_map/ppermute | solution.py:1056
  399.6 28.2 %collective-permute-start.37 = (bf16[1536,256]{1,0:T(8,128)(2,1)S(1)}, bf16[1536,256]{1,0:T(8,128)(2,1)S(1)}, u32[]{:S(2)}, u32[]{:S(2)}) collective-permute-start(bf16[1536,256]{1,0:T(8,128)(2,1)S(1)} %add_convert_fusion.4), channel_id=1, source_target_pairs={{0,4},{4,0},{8,12},{12,8},{16,20},{20,16},{24,28},{28,24},{1,5},{5... | collective-permute-start | bytes 2359304 | tf_op jit(solution)/shard_map/ppermute | solution.py:1062
  402.0 25.8 %collective-permute-start.38 = (bf16[256,1024]{1,0:T(8,128)(2,1)S(1)}, bf16[256,1024]{1,0:T(8,128)(2,1)S(1)}, u32[]{:S(2)}, u32[]{:S(2)}) collective-permute-start(bf16[256,1024]{1,0:T(8,128)(2,1)S(1)} %add_convert_fusion.7), channel_id=1, source_target_pairs={{0,16},{4,20},{8,24},{12,28},{16,0},{20,4},{24,8},{28,12},{1,17},{... | collective-permute-start | bytes 1572872 | tf_op jit(solution)/shard_map/ppermute | solution.py:1062
  408.9 52.2 %collective-permute-start.49 = (bf16[512,1024]{1,0:T(8,128)(2,1)}, bf16[512,1024]{1,0:T(8,128)(2,1)}, u32[]{:S(2)}, u32[]{:S(2)}) collective-permute-start(bf16[512,1024]{1,0:T(8,128)(2,1)} %maximum_select_fusion.6), channel_id=1, source_target_pairs={{0,4},{4,0},{8,12},{12,8},{16,20},{20,16},{24,28},{28,24},{1,5},{5... | collective-permute-start | bytes 3145736 | tf_op jit(solution)/shard_map/ppermute | solution.py:1062
  428.0 33.8 %collective-permute-start.48 = (bf16[256,1024]{1,0:T(8,128)(2,1)S(1)}, bf16[256,1024]{1,0:T(8,128)(2,1)}, u32[]{:S(2)}, u32[]{:S(2)}) collective-permute-start(bf16[256,1024]{1,0:T(8,128)(2,1)S(1)} %add_convert_fusion.6), channel_id=1, source_target_pairs={{0,4},{4,0},{8,12},{12,8},{16,20},{20,16},{24,28},{28,24},{1,5},{5... | collective-permute-start | bytes 1572872 | tf_op jit(solution)/shard_map/ppermute | solution.py:1062
  428.9 4.0 collective-permute-start.43
  432.3 29.5 %collective-permute-start.47 = (bf16[768,256]{1,0:T(8,128)(2,1)}, bf16[768,256]{1,0:T(8,128)(2,1)}, u32[]{:S(2)}, u32[]{:S(2)}) collective-permute-start(bf16[768,256]{1,0:T(8,128)(2,1)} %dynamic-slice_convert_fusion.3), channel_id=1, source_target_pairs={{0,8},{4,12},{8,0},{12,4},{16,24},{20,28},{24,16},{28,20},{1,9},{5... | collective-permute-start | bytes 1179656 | tf_op jit(solution)/shard_map/ppermute | solution.py:1062
  432.9 45.5 %collective-permute-start.44 = (bf16[512,1024]{1,0:T(8,128)(2,1)S(1)}, bf16[512,1024]{1,0:T(8,128)(2,1)}, u32[]{:S(2)}, u32[]{:S(2)}) collective-permute-start(bf16[512,1024]{1,0:T(8,128)(2,1)S(1)} %copy-done.69), channel_id=1, source_target_pairs={{0,2},{2,0},{1,3},{3,1},{4,6},{6,4},{5,7},{7,5},{8,10},{10,8},{9,1... | collective-permute-start | bytes 3145736 | tf_op jit(solution)/shard_map/ppermute | solution.py:1059
  433.7 26.0 %collective-permute-start.50 = (bf16[64,1024]{1,0:T(8,128)(2,1)S(1)}, bf16[64,1024]{1,0:T(8,128)(2,1)S(1)}, u32[]{:S(2)}, u32[]{:S(2)}) collective-permute-start(bf16[64,1024]{1,0:T(8,128)(2,1)S(1)} %add_convert_fusion.16), channel_id=1, source_target_pairs={{0,2},{2,0},{1,3},{3,1},{4,6},{6,4},{5,7},{7,5},{8,10},{10,8},{9,1... | collective-permute-start | bytes 393224 | tf_op jit(solution)/shard_map/ppermute | solution.py:1059
  459.8 18.6 %collective-permute-start.45 = (bf16[1536,256]{1,0:T(8,128)(2,1)}, bf16[1536,256]{1,0:T(8,128)(2,1)}, u32[]{:S(2)}, u32[]{:S(2)}) collective-permute-start(bf16[1536,256]{1,0:T(8,128)(2,1)} %add_convert_fusion.3), channel_id=1, source_target_pairs={{0,4},{4,0},{8,12},{12,8},{16,20},{20,16},{24,28},{28,24},{1,5},{5... | collective-permute-start | bytes 2359304 | tf_op jit(solution)/shard_map/ppermute | solution.py:1062
  461.1 17.3 %collective-permute-start.46 = (f32[8,1024]{1,0:T(8,128)S(1)}, f32[8,1024]{1,0:T(8,128)S(1)}, u32[]{:S(2)}, u32[]{:S(2)}) collective-permute-start(f32[8,1024]{1,0:T(8,128)S(1)} %add.242), channel_id=1, source_target_pairs={{0,4},{4,0},{8,12},{12,8},{16,20},{20,16},{24,28},{28,24},{1,5},{5... | collective-permute-start | bytes 98312 | tf_op jit(solution)/shard_map/ppermute | solution.py:1062
  463.5 34.6 %collective-permute-start.55 = (bf16[512,1024]{1,0:T(8,128)(2,1)S(1)}, bf16[512,1024]{1,0:T(8,128)(2,1)S(1)}, u32[]{:S(2)}, u32[]{:S(2)}) collective-permute-start(bf16[512,1024]{1,0:T(8,128)(2,1)S(1)} %maximum_select_fusion.7), channel_id=1, source_target_pairs={{0,8},{4,12},{8,0},{12,4},{16,24},{20,28},{24,16},{28,20},{1,9},{5... | collective-permute-start | bytes 3145736 | tf_op jit(solution)/shard_map/ppermute | solution.py:1062
  466.4 30.9 %collective-permute-start.54 = (bf16[768,256]{1,0:T(8,128)(2,1)S(1)}, bf16[768,256]{1,0:T(8,128)(2,1)S(1)}, u32[]{:S(2)}, u32[]{:S(2)}) collective-permute-start(bf16[768,256]{1,0:T(8,128)(2,1)S(1)} %add_convert_fusion.13), channel_id=1, source_target_pairs={{0,16},{4,20},{8,24},{12,28},{16,0},{20,4},{24,8},{28,12},{1,17},{... | collective-permute-start | bytes 1179656 | tf_op jit(solution)/shard_map/ppermute | solution.py:1062
  479.6 28.4 %collective-permute-start.51 = (bf16[256,1024]{1,0:T(8,128)(2,1)S(1)}, bf16[256,1024]{1,0:T(8,128)(2,1)S(1)}, u32[]{:S(2)}, u32[]{:S(2)}) collective-permute-start(bf16[256,1024]{1,0:T(8,128)(2,1)S(1)} %add_convert_fusion.5), channel_id=1, source_target_pairs={{0,4},{4,0},{8,12},{12,8},{16,20},{20,16},{24,28},{28,24},{1,5},{5... | collective-permute-start | bytes 1572872 | tf_op jit(solution)/shard_map/ppermute | solution.py:1062
  482.4 24.9 %collective-permute-start.52 = (bf16[768,256]{1,0:T(8,128)(2,1)S(1)}, bf16[768,256]{1,0:T(8,128)(2,1)S(1)}, u32[]{:S(2)}, u32[]{:S(2)}) collective-permute-start(bf16[768,256]{1,0:T(8,128)(2,1)S(1)} %dynamic-slice_convert_fusion.2), channel_id=1, source_target_pairs={{0,8},{4,12},{8,0},{12,4},{16,24},{20,28},{24,16},{28,20},{1,9},{5... | collective-permute-start | bytes 1179656 | tf_op jit(solution)/shard_map/ppermute | solution.py:1062
  484.3 22.9 %collective-permute-start.53 = (f32[8,1024]{1,0:T(8,128)S(1)}, f32[8,1024]{1,0:T(8,128)S(1)}, u32[]{:S(2)}, u32[]{:S(2)}) collective-permute-start(f32[8,1024]{1,0:T(8,128)S(1)} %add.249), channel_id=1, source_target_pairs={{0,8},{4,12},{8,0},{12,4},{16,24},{20,28},{24,16},{28,20},{1,9},{5... | collective-permute-start | bytes 98312 | tf_op jit(solution)/shard_map/ppermute | solution.py:1062
  501.1 23.5 %collective-permute-start.58 = (bf16[768,256]{1,0:T(8,128)(2,1)S(1)}, bf16[768,256]{1,0:T(8,128)(2,1)S(1)}, u32[]{:S(2)}, u32[]{:S(2)}) collective-permute-start(bf16[768,256]{1,0:T(8,128)(2,1)S(1)} %add_convert_fusion.11), channel_id=1, source_target_pairs={{0,8},{4,12},{8,0},{12,4},{16,24},{20,28},{24,16},{28,20},{1,9},{5... | collective-permute-start | bytes 1179656 | tf_op jit(solution)/shard_map/ppermute | solution.py:1062
  510.0 14.6 %collective-permute-start.59 = (bf16[128,1024]{1,0:T(8,128)(2,1)}, bf16[128,1024]{1,0:T(8,128)(2,1)}, u32[]{:S(2)}, u32[]{:S(2)}) collective-permute-start(bf16[128,1024]{1,0:T(8,128)(2,1)} %dynamic-slice_convert_fusion.4), channel_id=1, source_target_pairs={{0,8},{4,12},{8,0},{12,4},{16,24},{20,28},{24,16},{28,20},{1,9},{5... | collective-permute-start | bytes 786440 | tf_op jit(solution)/shard_map/ppermute | solution.py:1062
  512.8 24.5 %collective-permute-start.56 = (bf16[768,256]{1,0:T(8,128)(2,1)S(1)}, bf16[768,256]{1,0:T(8,128)(2,1)S(1)}, u32[]{:S(2)}, u32[]{:S(2)}) collective-permute-start(bf16[768,256]{1,0:T(8,128)(2,1)S(1)} %add_convert_fusion.12), channel_id=1, source_target_pairs={{0,16},{4,20},{8,24},{12,28},{16,0},{20,4},{24,8},{28,12},{1,17},{... | collective-permute-start | bytes 1179656 | tf_op jit(solution)/shard_map/ppermute | solution.py:1062
  512.9 24.4 %collective-permute-start.57 = (f32[8,1024]{1,0:T(8,128)S(1)}, f32[8,1024]{1,0:T(8,128)S(1)}, u32[]{:S(2)}, u32[]{:S(2)}) collective-permute-start(f32[8,1024]{1,0:T(8,128)S(1)} %add.255), channel_id=1, source_target_pairs={{0,16},{4,20},{8,24},{12,28},{16,0},{20,4},{24,8},{28,12},{1,17},{... | collective-permute-start | bytes 98312 | tf_op jit(solution)/shard_map/ppermute | solution.py:1062
  525.6 14.7 %collective-permute-start.62 = (bf16[128,1024]{1,0:T(8,128)(2,1)S(1)}, bf16[128,1024]{1,0:T(8,128)(2,1)S(1)}, u32[]{:S(2)}, u32[]{:S(2)}) collective-permute-start(bf16[128,1024]{1,0:T(8,128)(2,1)S(1)} %add_convert_fusion.15), channel_id=1, source_target_pairs={{0,16},{4,20},{8,24},{12,28},{16,0},{20,4},{24,8},{28,12},{1,17},{... | collective-permute-start | bytes 786440 | tf_op jit(solution)/shard_map/ppermute | solution.py:1062
  526.9 25.0 %collective-permute-start.61 = (bf16[1536,256]{1,0:T(8,128)(2,1)S(1)}, bf16[1536,256]{1,0:T(8,128)(2,1)S(1)}, u32[]{:S(2)}, u32[]{:S(2)}) collective-permute-start(bf16[1536,256]{1,0:T(8,128)(2,1)S(1)} %maximum_select_fusion.9), channel_id=1, source_target_pairs={{0,4},{4,0},{8,12},{12,8},{16,20},{20,16},{24,28},{28,24},{1,5},{5... | collective-permute-start | bytes 2359304 | tf_op jit(solution)/shard_map/ppermute | solution.py:1062
  537.5 14.4 %collective-permute-start.60 = (bf16[768,256]{1,0:T(8,128)(2,1)S(1)}, bf16[768,256]{1,0:T(8,128)(2,1)S(1)}, u32[]{:S(2)}, u32[]{:S(2)}) collective-permute-start(bf16[768,256]{1,0:T(8,128)(2,1)S(1)} %add_convert_fusion.10), channel_id=1, source_target_pairs={{0,8},{4,12},{8,0},{12,4},{16,24},{20,28},{24,16},{28,20},{1,9},{5... | collective-permute-start | bytes 1179656 | tf_op jit(solution)/shard_map/ppermute | solution.py:1062
  540.4 10.0 %collective-permute-start.63 = (bf16[128,1024]{1,0:T(8,128)(2,1)S(1)}, bf16[128,1024]{1,0:T(8,128)(2,1)S(1)}, u32[]{:S(2)}, u32[]{:S(2)}) collective-permute-start(bf16[128,1024]{1,0:T(8,128)(2,1)S(1)} %add_convert_fusion.14), channel_id=1, source_target_pairs={{0,8},{4,12},{8,0},{12,4},{16,24},{20,28},{24,16},{28,20},{1,9},{5... | collective-permute-start | bytes 786440 | tf_op jit(solution)/shard_map/ppermute | solution.py:1062
  550.6 14.9 %collective-permute-start.64 = (bf16[256,1024]{1,0:T(8,128)(2,1)S(1)}, bf16[256,1024]{1,0:T(8,128)(2,1)S(1)}, u32[]{:S(2)}, u32[]{:S(2)}) collective-permute-start(bf16[256,1024]{1,0:T(8,128)(2,1)S(1)} %maximum_select_fusion.11), channel_id=1, source_target_pairs={{0,4},{4,0},{8,12},{12,8},{16,20},{20,16},{24,28},{28,24},{1,5},{5... | collective-permute-start | bytes 1572872 | tf_op jit(solution)/shard_map/ppermute | solution.py:1062
  552.2 24.7 %collective-permute-start.65 = (bf16[1536,256]{1,0:T(8,128)(2,1)S(1)}, bf16[1536,256]{1,0:T(8,128)(2,1)S(1)}, u32[]{:S(2)}, u32[]{:S(2)}) collective-permute-start(bf16[1536,256]{1,0:T(8,128)(2,1)S(1)} %maximum_select_fusion.10), channel_id=1, source_target_pairs={{0,4},{4,0},{8,12},{12,8},{16,20},{20,16},{24,28},{28,24},{1,5},{5... | collective-permute-start | bytes 2359304 | tf_op jit(solution)/shard_map/ppermute | solution.py:1062
  (129 other events, 891.6 us)

commit v6 on v5

--- a/solution.py
+++ b/solution.py
@@ -773,17 +773,16 @@
     out_ref[...] = total.astype(out_ref.dtype)
 
 
-def down_grad(g, mine, other, kind):
+def down_grad(g, mine, other, kind, first=0, tiles=2):
     rows, width = mine.shape
-    hidden = g.shape[1]
     tile = 512
     whole = pl.BlockSpec((rows, width), lambda i: (0, 0), pipeline_mode=pl.Buffered(1))
     return pl.pallas_call(
         down_grad_kernel,
-        grid=(hidden // tile,),
-        in_specs=[pl.BlockSpec((2 * rows, tile), lambda i: (0, i)), whole, whole],
+        grid=(tiles,),
+        in_specs=[pl.BlockSpec((2 * rows, tile), lambda i: (0, i + first)), whole, whole],
         out_specs=pl.BlockSpec((tile, width), lambda i: (i, 0)),
-        out_shape=shape((hidden, width), kind),
+        out_shape=shape((tiles * tile, width), kind),
         compiler_params=params(48),
         cost_estimate=brief(),
         name="down_grad",
@@ -1216,123 +1215,105 @@
     up1 = up_grad(h3, h3_other, du1, ROUND)
     up1, g1, du0, g0 = join((up1, g1, du0, g0))
     up = Sum(up1)
-    down1 = down_grad(g1, dout, dout_other, ROUND)
-    (y_received, down1) = join((y_received, down1))
+    down1a = down_grad(g1, dout, dout_other, ROUND, 0, 1)
+    down1b = down_grad(g1, dout, dout_other, ROUND, 1, 1)
+    y_received, down1a, down1b = join((y_received, down1a, down1b))
     dx1, dself, dcross, dcq, dck, dcv, sums = middle_back(
         place, y_m, y_received, x1, x2, dout, cq, norm_gain, wq, ck, cv, wc
     )
     du0, dself = join((du0, dself))
     up0 = up_grad(h3, h3_other, du0, FULL)
     dself_other = over_core(dself)
-    dself, dself_other, dcross, dcq, down1, up0, g0 = sync(
-        [up], dself, dself_other, dcross, dcq, down1, up0, g0
-    )
-
-    down = Sum(down1, (down_z, across))
-    up.first(up0)
+    dself, dself_other, dcross, dcq, down1a, down1b, up0, g0 = sync(
+        [up], dself, dself_other, dcross, dcq, down1a, down1b, up0, g0
+    )
+
+    down_a = Sum(down1a)
+    up_total = lax.psum(lower(up0 + up.fly.astype(FULL)), "wide")
     do0, do1 = pull(place, dself, dself_other, (w_out, out_y))
     dcross_other = over_core(dcross)
     dcq_other = over_core(dcq[:, 512:])
     d_pair = jnp.stack([dck, dcv], axis=1)
     d_pair_other = over_core(d_pair[2:])
     dq1, dk1, dv1 = self_back(limit, q1, k1, v1, o1, do1, lse1)
-    dq1, dcross_other, dcq_other, d_pair_other = sync(
-        [up], dq1, dcross_other, dcq_other, d_pair_other
-    )
-
-    up.second()
+    dq1, dcross_other, dcq_other, d_pair_other, down1b = sync(
+        [down_a], dq1, dcross_other, dcq_other, d_pair_other, down1b
+    )
+
+    down_b = Sum(down1b)
     d_pair = lower(d_pair[:2] + d_pair_other)
     qkv1 = qkv_grad(place, h1, (dq1, dk1, dv1), ROUND)
     down0 = down_grad(g0, dout, dout_other, FULL)
     cross = (h2, h2_other, dcq, dcq_other, text)
     outer = (dself, dself_other, ca, ca_other, dcross, dcross_other)
     into1 = cross_in_grad(1, *cross, d_pair[1], ROUND)
-    qkv1, into1, do0, down0 = sync([down, up], qkv1, into1, do0, down0)
+    outof1 = outputs_grad(place, 1, o1, *outer, ROUND)
+    qkv1, into1, outof1, do0, down0 = sync([down_b], qkv1, into1, outof1, do0, down0)
 
     qkv = Sum(qkv1)
-    down.first(down0)
-    up.far()
     dq0, dk0, dv0 = self_back(limit, q0, k0, v0, o0, do0, lse0)
     grads = (dq0, dk0, dv0, dq1, dk1, dv1)
     yo = first_back(away, grads, w_qkv, qkv_first, qkv_second, ROUND)
-    dq0, yo = sync([down, up], dq0, yo)
-
-    down.second()
-    up.back()
+    dq0, yo, into1, outof1, d_pair = sync([qkv], dq0, yo, into1, outof1, d_pair)
+
+    cross_in = Sum(into1)
     y_received = over_core(yo)
     qkv0 = qkv_grad(place, h1, (dq0, dk0, dv0), FULL)
+    qkv.first(qkv0)
     grads = (dq0, dk0, dv0, dq1, dk1, dv1)
     ym = first_back(place, grads, w_qkv, qkv_first, qkv_second, FULL)
-    outof1 = outputs_grad(place, 1, o1, *outer, ROUND)
-    qkv0, ym, y_received, outof1, x2 = sync(
-        [qkv, down, up], qkv0, ym, y_received, outof1, x2
-    )
-
-    cross_in = Sum(into1)
-    qkv.first(qkv0)
-    down.far()
-    up.along()
-    grad_frames, first_sums = frames_back(place, ym, y_received, dx1, frames, norm_gain)
-    norms = Row(sums + first_sums, over_core)
     into0 = cross_in_grad(0, *cross, d_pair[0], FULL)
     outof0 = outputs_grad(place, 0, o0, *outer, FULL)
+    grad_frames, first_sums = frames_back(place, ym, y_received, dx1, frames, norm_gain)
+    outof1, into0, outof0, grad_frames, x2, down0, up_total = sync(
+        [cross_in, qkv], outof1, into0, outof0, grad_frames, x2, down0, up_total
+    )
+
+    outs = Sum(outof1)
+    received = jnp.concatenate([down_a.fly, down_b.fly], axis=0)
+    down_total = lax.psum(lower(down0 + received.astype(FULL)), "wide")
+    cross_in.first(into0)
+    qkv.second()
+    norms = Row(sums + first_sums, over_core)
     text_part = 0.0
     for g, weights in ((0, w_cross_kv), (1, cross_kv_y)):
         for c in range(2):
             text_part = text_part + nt(d_pair[g, c], weights[c])
     texts = Row(text_part, over_core)
     out_rows = lower(x2 + out_m + over_core(out_o).astype(FULL))
-    into0, outof0, grad_frames, out_rows = sync(
-        [qkv, down, norms, texts], into0, outof0, grad_frames, out_rows
-    )
-
-    qkv.second()
-    down.back()
+    (out_rows,) = sync([outs, cross_in, qkv, norms, texts], out_rows)
+
+    outs.first(outof0)
+    cross_in.second()
+    qkv.far()
     norms.then(over_y)
     text_grad = lower(texts.kept + texts.fly)
-    (outof1,) = sync([cross_in, norms], outof1)
-
-    outs = Sum(outof1)
-    cross_in.first(into0)
-    norms.then(lambda v: along_wide(v, X_PAIRS))
     text_away = over_y(text_grad)
-    (text_away,) = sync([qkv, down, up], text_away)
-
-    qkv.far()
-    down.along()
-    grad_up = up.end()
-    grad_text = ordered(text_grad[None], text_away[None], side)
-    grad_up, grad_text = sync([outs, cross_in, norms], grad_up, grad_text)
-
-    outs.first(outof0)
-    cross_in.second()
-    norms.then(lambda v: along_wide(v, Z_NEAR))
-    sync([qkv, down])
-
-    qkv.back()
-    grad_down = down.end()
-    (grad_down,) = sync([outs, cross_in, norms], grad_down)
+    grad_up = up_total.astype(FULL)
+    text_away, grad_up = sync([outs, cross_in, qkv, norms], text_away, grad_up)
 
     outs.second()
     cross_in.far()
+    qkv.back()
+    norms.then(lambda v: along_wide(v, X_PAIRS))
+    grad_text = ordered(text_grad[None], text_away[None], side)
+    (grad_text,) = sync([outs, cross_in, qkv, norms], grad_text)
+
+    outs.far()
+    cross_in.back()
+    qkv.along()
+    norms.then(lambda v: along_wide(v, Z_NEAR))
+    sync([outs, cross_in, norms])
+
+    outs.back()
+    cross_in.along()
     norms.then(lambda v: along_wide(v, Z_FAR))
-    sync([qkv, outs])
-
-    qkv.along()
-    outs.far()
-    sync([cross_in, norms])
-
-    cross_in.back()
+    sync([outs, qkv])
+
+    outs.along()
+    grad_qkv = qkv.end().reshape(3, width, 256)
+    (grad_qkv,) = sync([cross_in, norms], grad_qkv)
     sums = norms.kept + norms.fly
-    sync([outs])
-
-    outs.back()
-    sync([cross_in, qkv])
-
-    cross_in.along()
-    grad_qkv = qkv.end().reshape(3, width, 256)
-    sync([outs])
-    outs.along()
     grad_cross_in = cross_in.end()
     grad_outs = outs.end()
     return (
@@ -1347,7 +1328,7 @@
         grad_cross_in[width:].reshape(2, width, 256),
         grad_outs[256:],
         grad_up,
-        grad_down,
+        down_total.astype(FULL),
     )
 
 

time: 590 us -> 633 us (1.073)
  waiting for transfers between devices: 151 us -> 193 us
  between operations: 2.67 us -> 15.9 us
  starting transfers between devices: 54.4 us -> 44.4 us
  Pallas kernels: 255 us -> 264 us
    psum x0 -> x2, waiting for transfers between devices: none -> 81.7 us  [the longest x1 48.6 us: chip_local(): down_total = lax.psum(lower(down0 + received.astype(FULL)), 'wide')]
    ppermute x12 -> x13, waiting for transfers between devices: 37.7 us -> 16.9 us  [over_y(): return lax.ppermute(v, 'narrow', Y_PAIRS)]
    ppermute x33 -> x23, waiting for transfers between devices: 113 us -> 92.7 us  [along_wide(): return lax.ppermute(v, 'wide', pairs)]
    ppermute x33 -> x23, starting transfers between devices: 36.4 us -> 23.7 us  [along_wide(): return lax.ppermute(v, 'wide', pairs)]
    convert_element_type x0 -> x2, other arithmetic: none -> 8.26 us  [the longest x1 4.19 us: chip_local(): grad_up = up_total.astype(FULL)]
    convert_element_type x5 -> x3, other arithmetic: 10.9 us -> 3.85 us  [end(): return ordered(self.kept, self.fly, self.order[0][0]).astype(FULL)]
    pallas_call x2 -> x3, Pallas kernels: 15 us -> 18 us  [down_grad(): pl.pallas_call(down_grad_kernel, grid=(tiles,), in_specs=[pl.BlockSpec((2...]
    ppermute x12 -> x13, starting transfers between devices: 13.6 us -> 16.3 us  [over_y(): return lax.ppermute(v, 'narrow', Y_PAIRS)]
  transfers between devices with their start and end apart: 66 -> 59, of which waited for: 19 -> 16; matrix products, arithmetic and copies ran while one was open for 15% -> 13% of each run, Pallas kernels for 42% -> 40%
where the time goes in v6:
time: 633 us; the launch traced here: 622 us
  Pallas kernels  264 us (42%)
  waiting for transfers between devices  193 us (30%)
  other arithmetic  56.2 us (9%)
  local copies, waits for them, and re-layouts  46.1 us (7%)
  starting transfers between devices  44.4 us (7%)
  between operations  15.9 us (3%)
    ppermute x23, waiting for transfers between devices, along_wide(): return lax.ppermute(v, 'wide', pairs)  92.7 us
    pallas_call x4, Pallas kernels, feed(): pl.pallas_call(functools.partial(feed_kernel, parts=parts, carried=len(be...  51.4 us
    psum x1, waiting for transfers between devices, chip_local(): down_total = lax.psum(lower(down0 + received.astype(FULL)), 'wide')  48.6 us
    pallas_call x2, Pallas kernels, self_back(): pl.pallas_call(functools.partial(self_back_kernel, span=span, floor=floor...  40.4 us
    psum x1, waiting for transfers between devices, chip_local(): up_total = lax.psum(lower(up0 + up.fly.astype(FULL)), 'wide')  33.2 us
    pallas_call x2, Pallas kernels, self_forward(): pl.pallas_call(functools.partial(self_forward_kernel, span=span, floor=fl...  28.7 us
    unnamed x222, local copies, waits for them, and re-layouts  24 us
    ppermute x23, starting transfers between devices, along_wide(): return lax.ppermute(v, 'wide', pairs)  23.7 us
  transfers between devices with their start and end apart: 59, of which 16 were waited for; matrix products, arithmetic and copies ran while one was open for 13% of the time, Pallas kernels for 40%

profile of v6, /device:TPU:0, one launch (start us, length us, event | category | flops | bytes accessed | tf_op | source)
XLA Modules:
  0.0 622.3 jit_solution(18249141995280193066)
XLA Ops:
  7.8 2.1 constant_dynamic-slice_fusion.6
  9.9 2.7 collective-permute-start.1
  15.5 2.9 pad_maximum_fusion
  18.4 6.0 first_project.1
  29.0 1.9 collective-permute-done.1.first_ref.refs_7_
  30.9 1.8 collective-permute-start.2
  33.9 2.1 constant_dynamic-slice_fusion.4
  38.3 14.4 %self_forward.2 = (bf16[1664,256]{1,0:T(8,128)(2,1)}, f32[2,8,1664]{2,1,0:T(8,128)}) custom-call(s32[1]{0:T(128)} %dynamic_slice.81.limit_ref, bf16[1664,256]{1,0:T(8,128)(2,1)} %copy-done.44, bf16[1664,256]{1,0:T(8,128)(2,1)} %copy-done.46, bf16[1664,256]{1,0:T(8,128)(2,1)} %copy-done.48), custom_call_target="tpu_custom_call" | custom-call | flops 1000 | bytes 1000 | tf_op jit(solution)/shard_map/self_forward/pallas_call | solution.py:522
  55.2 5.0 project.1
  61.4 1.8 copy-done.74
  64.2 3.1 collective-permute-done.3
  72.2 14.2 %self_forward.3 = (bf16[1664,256]{1,0:T(8,128)(2,1)}, f32[2,8,1664]{2,1,0:T(8,128)}) custom-call(s32[1]{0:T(128)} %dynamic_slice.81.limit_ref, bf16[1664,256]{1,0:T(8,128)(2,1)} %copy-done.50, bf16[1664,256]{1,0:T(8,128)(2,1)} %copy-done.52, bf16[1664,256]{1,0:T(8,128)(2,1)} %copy-done.54), custom_call_target="tpu_custom_call" | custom-call | flops 1000 | bytes 1000 | tf_op jit(solution)/shard_map/self_forward/pallas_call | solution.py:522
  87.5 2.2 fusion.36
  89.7 2.0 maximum_select_fusion.3
  91.8 2.3 maximum_select_fusion
  100.2 21.4 %middle_forward.1 = (f32[832,1024]{1,0:T(8,128)}, f32[832,1024]{1,0:T(8,128)}, bf16[832,1024]{1,0:T(8,128)(2,1)}, bf16[832,1024]{1,0:T(8,128)(2,1)}, bf16[832,10...) custom-call(s32[2]{0:T(128)} %copy-done.65, bf16[832,1024]{1,0:T(8,128)(2,1)} %frame_ref.3, ...), custom_call_target="tpu_custom_call" | custom-call | flops 1000 | bytes 1000 | tf_op jit(solution)/shard_map/middle_forward/pallas_call | solution.py:671
  124.0 12.2 %feed.4 = (bf16[1664,1024]{1,0:T(8,128)(2,1)}, bf16[1664,1024]{1,0:T(8,128)(2,1)}, f32[832,1024]{1,0:T(8,128)}, f32[832,1024]{1,0:T(8,128)}) custom-call(s32[2]{0:T(128)} %copy-done.65, bf16[832,1024]{1,0:T(8,128)(2,1)} %get-tuple-element.197.h_ref.mine_ref, bf16[832,1024]{1,0:T(8,128)(2,1)} %copy-done.2, bf16[1024,1024]{1,0:T(8,128)(2,1)} %refs_0_.5, ...), custom_call_target="tpu_custom_call" | custom-call | flops 1000 | bytes 1000 | tf_op jit(solution)/shard_map/feed/pallas_call | solution.py:728
  137.5 12.1 %feed.5 = (bf16[1664,1024]{1,0:T(8,128)(2,1)}, bf16[1664,1024]{1,0:T(8,128)(2,1)}, f32[832,1024]{1,0:T(8,128)}, f32[832,1024]{1,0:T(8,128)}) custom-call(s32[2]{0:T(128)} %copy-done.65, bf16[832,1024]{1,0:T(8,128)(2,1)} %copy-done.8, bf16[832,1024]{1,0:T(8,128)(2,1)} %collective-permute-done.10.d_ref.other_ref, ...), custom_call_target="tpu_custom_call", output_to_operand_aliasing={{0}: (5, {}), {1}: (6, {})} | custom-call | flops 1000 | bytes 1000 | tf_op jit(solution)/shard_map/feed/pallas_call | solution.py:728
  149.6 20.5 %collective-permute-done.19.refs_3_ = bf16[512,1024]{1,0:T(8,128)(2,1)} collective-permute-done((bf16[512,1024]{1,0:T(8,128)(2,1)S(1)}, bf16[512,1024]{1,0:T(8,128)(2,1)}, u32[]{:S(2)}, u32[]{:S(2)}) %collective-permute-start.19) | collective-permute-done | bytes 1048608 | tf_op jit(solution)/shard_map/ppermute | solution.py:1061
  170.1 13.4 %feed.6 = (bf16[1664,1024]{1,0:T(8,128)(2,1)}, bf16[1664,1024]{1,0:T(8,128)(2,1)}, bf16[832,1024]{1,0:T(8,128)(2,1)}, bf16[832,1024]{1,0:T(8,128)(2,1)}) custom-call(s32[2]{0:T(128)} %copy-done.65, bf16[832,1024]{1,0:T(8,128)(2,1)} %copy-done.8, bf16[832,1024]{1,0:T(8,128)(2,1)} %collective-permute-done.10.d_ref.other_ref, ...), custom_call_target="tpu_custom_call" | custom-call | flops 1000 | bytes 1000 | tf_op jit(solution)/shard_map/feed/pallas_call | solution.py:728
  183.5 13.7 %feed.7 = (bf16[1664,1024]{1,0:T(8,128)(2,1)}, bf16[1664,1024]{1,0:T(8,128)(2,1)}, f32[832,1024]{1,0:T(8,128)}, f32[832,1024]{1,0:T(8,128)}) custom-call(s32[2]{0:T(128)} %copy-done.65, bf16[832,1024]{1,0:T(8,128)(2,1)} %get-tuple-element.197.h_ref.mine_ref, bf16[832,1024]{1,0:T(8,128)(2,1)} %copy-done.2, ...), custom_call_target="tpu_custom_call", output_to_operand_aliasing={{0}: (9, {}), {1}: (10, {})} | custom-call | flops 1000 | bytes 1000 | tf_op jit(solution)/shard_map/feed/pallas_call | solution.py:728
  197.2 7.3 %up_grad.2 = bf16[1024,1024]{1,0:T(8,128)(2,1)} custom-call(bf16[832,1024]{1,0:T(8,128)(2,1)S(1)} %copy-done.7, bf16[832,1024]{1,0:T(8,128)(2,1)S(1)} %copy-done.9, bf16[1664,1024]{1,0:T(8,128)(2,1)} %get-tuple-element.214.du_ref), custom_call_target="tpu_custom_call" | custom-call | flops 1000 | bytes 1000 | tf_op jit(solution)/shard_map/up_grad/pallas_call | solution.py:758
  206.1 4.3 down_grad.4
  211.4 5.3 down_grad.3
  216.7 23.4 %middle_back.1 = (f32[832,1024]{1,0:T(8,128)}, bf16[832,1024]{1,0:T(8,128)(2,1)}, bf16[832,1024]{1,0:T(8,128)(2,1)}, bf16[832,1024]{1,0:T(8,128)(2,1)}, f32[4,64...) custom-call(s32[2]{0:T(128)} %copy-done.65, f32[832,1024]{1,0:T(8,128)} %get-tuple-element.220.ym_ref, ...), custom_call_target="tpu_custom_call" | custom-call | flops 1000 | bytes 1000 | tf_op jit(solution)/shard_map/middle_back/pallas_call | solution.py:947
  240.3 7.7 %up_grad.3 = f32[1024,1024]{1,0:T(8,128)} custom-call(bf16[832,1024]{1,0:T(8,128)(2,1)S(1)} %copy-done.7, bf16[832,1024]{1,0:T(8,128)(2,1)S(1)} %copy-done.9, bf16[1664,1024]{1,0:T(8,128)(2,1)} %get-tuple-element.233.du_ref), custom_call_target="tpu_custom_call" | custom-call | flops 1000 | bytes 1000 | tf_op jit(solution)/shard_map/up_grad/pallas_call | solution.py:758
  248.0 4.8 collective-permute-done.20
  259.5 2.8 pull.1
  265.2 20.3 %self_back.2 = (bf16[1664,256]{1,0:T(8,128)(2,1)S(1)}, bf16[1664,256]{1,0:T(8,128)(2,1)S(1)}, bf16[1664,256]{1,0:T(8,128)(2,1)S(1)}) custom-call(s32[1]{0:T(128)} %dynamic_slice.81.limit_ref, bf16[1664,256]{1,0:T(8,128)(2,1)S(1)} %copy-done.51, bf16[1664,256]{1,0:T(8,128)(2,1)S(1)} %copy-done.53, bf16[1664,256]{1,0:T(8,128)(2,1)S(1)} %copy-done.55, ...), custom_call_target="tpu_custom_call" | custom-call | flops 1000 | bytes 1000 | tf_op jit(solution)/shard_map/self_back/pallas_call | solution.py:603
  286.2 8.4 %down_grad.5 = f32[1024,1024]{1,0:T(8,128)} custom-call(bf16[1664,1024]{1,0:T(8,128)(2,1)} %get-tuple-element.256.g_ref, bf16[832,1024]{1,0:T(8,128)(2,1)S(1)} %copy-done.4, bf16[832,1024]{1,0:T(8,128)(2,1)} %collective-permute-done.10.d_ref.other_ref), custom_call_target="tpu_custom_call" | custom-call | flops 1000 | bytes 1000 | tf_op jit(solution)/shard_map/down_grad/pallas_call | solution.py:780
  294.6 7.1 %qkv_grad.2 = bf16[3072,256]{1,0:T(8,128)(2,1)} custom-call(s32[2]{0:T(128)S(1)} %copy-done.67, bf16[1664,1024]{1,0:T(8,128)(2,1)} %copy-done.5, bf16[1664,256]{1,0:T(8,128)(2,1)S(1)} %get-tuple-element.247.refs_0_.refs_3_, bf16[1664,256]{1,0:T(8,128)(2,1)S(1)} %get-tuple-element.248.refs_1_.refs_4_, bf16[1664,256]{1,0:T(8,128)(2,1)S(1)} %get-tuple-element.249.refs_2_.refs_5_), custom_call_target="tpu_custom_call" | custom-call | flops 1000 | bytes 1000 | tf_op jit(solution)/shard_map/qkv_grad/pallas_call | solution.py:809
  301.8 5.1 outputs_grad.2
  308.6 4.5 cross_in_grad.2
  314.4 3.7 add_convert_fusion.1
  323.8 20.1 %self_back.3 = (bf16[1664,256]{1,0:T(8,128)(2,1)S(1)}, bf16[1664,256]{1,0:T(8,128)(2,1)S(1)}, bf16[1664,256]{1,0:T(8,128)(2,1)S(1)}) custom-call(s32[1]{0:T(128)} %dynamic_slice.81.limit_ref, bf16[1664,256]{1,0:T(8,128)(2,1)S(1)} %copy-done.45, bf16[1664,256]{1,0:T(8,128)(2,1)S(1)} %copy-done.47, bf16[1664,256]{1,0:T(8,128)(2,1)S(1)} %copy-done.49, ...), custom_call_target="tpu_custom_call" | custom-call | flops 1000 | bytes 1000 | tf_op jit(solution)/shard_map/self_back/pallas_call | solution.py:603
  343.9 6.6 %first_back.2 = bf16[832,1024]{1,0:T(8,128)(2,1)} custom-call(s32[2]{0:T(128)S(1)} %pad_add_fusion.1.place_ref, bf16[1664,256]{1,0:T(8,128)(2,1)S(1)} %get-tuple-element.266.refs_0_, bf16[1664,256]{1,0:T(8,128)(2,1)S(1)} %get-tuple-element.261.refs_1_, bf16[1664,256]{1,0:T(8,128)(2,1)S(1)} %get-tuple-element.262.refs_2_, bf16[1664,256]{1,0:T(8,128)(2,1)S(1)} %copy-done.30, ...), custom_call_target="tpu_custom_call" | custom-call | flops 1000 | bytes 1000 | tf_op jit(solution)/shard_map/first_back/pallas_call | solution.py:991
  354.3 6.7 %outputs_grad.3 = f32[512,1024]{1,0:T(8,128)} custom-call(s32[2]{0:T(128)S(1)} %copy-done.67, bf16[1664,256]{1,0:T(8,128)(2,1)S(1)} %copy-done.21, bf16[832,1024]{1,0:T(8,128)(2,1)S(1)} %copy-done.11, bf16[832,1024]{1,0:T(8,128)(2,1)S(1)} %copy-done.13, bf16[832,1024]{1,0:T(8,128)(2,1)} %get-tuple-element.253.am_ref, ...), custom_call_target="tpu_custom_call" | custom-call | flops 1000 | bytes 1000 | tf_op jit(solution)/shard_map/outputs_grad/pallas_call | solution.py:870
  361.0 6.0 qkv_grad.3
  367.0 3.1 add_convert_fusion.4
  371.1 5.5 first_back.3.ym_ref
  378.4 4.9 cross_in_grad.3
  383.3 6.0 frames_back.1
  389.3 33.2 %all-reduce.3.cloned.1.call-done = bf16[1024,1024]{1,0:T(8,128)(2,1)} async-done(((bf16[1024,1024]{1,0:T(8,128)(2,1)}), bf16[1024,1024]{1,0:T(8,128)(2,1)}) %all-reduce.3.cloned.1.call-update) | async-done | bytes 2097168 | tf_op jit(solution)/shard_map/psum | solution.py:1232
  422.6 1.8 add_convert_fusion.3
  430.6 4.9 add_convert_fusion.2
  435.5 4.6 collective-permute-done.36
  440.1 4.3 collective-permute-done.35
  444.4 7.0 %collective-permute-done.34 = bf16[512,1024]{1,0:T(8,128)(2,1)S(1)} collective-permute-done((bf16[512,1024]{1,0:T(8,128)(2,1)}, bf16[512,1024]{1,0:T(8,128)(2,1)S(1)}, u32[]{:S(2)}, u32[]{:S(2)}) %collective-permute-start.34) | collective-permute-done | bytes 1048608 | tf_op jit(solution)/shard_map/ppermute | solution.py:1058
  451.5 2.2 collective-permute-start.42
  460.6 3.4 add_convert_fusion
  464.0 4.2 convert_element_type.170
  468.2 3.3 collective-permute-done.42
  471.6 19.7 %collective-permute-done.41 = bf16[768,256]{1,0:T(8,128)(2,1)} collective-permute-done((bf16[768,256]{1,0:T(8,128)(2,1)}, bf16[768,256]{1,0:T(8,128)(2,1)}, u32[]{:S(2)}, u32[]{:S(2)}) %collective-permute-start.41) | collective-permute-done | bytes 393248 | tf_op jit(solution)/shard_map/ppermute | solution.py:1061
  491.2 1.8 add_convert_fusion.7
  493.1 1.9 add_convert_fusion.8
  499.1 3.2 collective-permute-done.48
  502.3 16.8 %collective-permute-done.45 = bf16[128,1024]{1,0:T(8,128)(2,1)S(1)} collective-permute-done((bf16[128,1024]{1,0:T(8,128)(2,1)S(1)}, bf16[128,1024]{1,0:T(8,128)(2,1)S(1)}, u32[]{:S(2)}, u32[]{:S(2)}) %collective-permute-start.45) | collective-permute-done | bytes 262176 | tf_op jit(solution)/shard_map/ppermute | solution.py:1061
  520.5 2.1 collective-permute-start.49
  524.9 16.0 %collective-permute-done.51 = f32[8,1024]{1,0:T(8,128)S(1)} collective-permute-done((f32[8,1024]{1,0:T(8,128)S(1)}, f32[8,1024]{1,0:T(8,128)S(1)}, u32[]{:S(2)}, u32[]{:S(2)}) %collective-permute-start.51) | collective-permute-done | bytes 32800 | tf_op jit(solution)/shard_map/ppermute | solution.py:1061
  543.5 48.6 %all-reduce.5.cloned.1.call-done = bf16[1024,1024]{1,0:T(8,128)(2,1)} async-done(((bf16[1024,1024]{1,0:T(8,128)(2,1)}), bf16[1024,1024]{1,0:T(8,128)(2,1)}) %all-reduce.5.cloned.1.call-update) | async-done | bytes 2097168 | tf_op jit(solution)/shard_map/psum | solution.py:1274
  592.0 4.1 convert_element_type.192
  596.1 2.1 collective-permute-start.53
  601.7 1.9 convert.1
  607.7 4.3 collective-permute-done.56
  (388 shorter events, 93.9 us)
Async XLA Ops:
  7.2 48.0 %copy-start = (bf16[2,64,1024]{2,1,0:T(8,128)(2,1)S(1)}, bf16[2,64,1024]{2,1,0:T(8,128)(2,1)}, u32[]{:S(2)}) copy-start(bf16[2,64,1024]{2,1,0:T(8,128)(2,1)} %param.15) | copy-start | bytes 786436
  7.2 415.3 %all-reduce.3.cloned.1.call-start = ((), (), s32[]{:S(2)}) async-start(), calls=%async_computation | async-start | bytes 4194304 | tf_op jit(solution)/shard_map/psum | solution.py:1232
  7.3 11.1 %collective-permute-start = (bf16[832,1024]{1,0:T(8,128)(2,1)}, bf16[832,1024]{1,0:T(8,128)(2,1)}, u32[]{:S(2)}, u32[]{:S(2)}) collective-permute-start(bf16[832,1024]{1,0:T(8,128)(2,1)} %frame_ref.3), channel_id=1, source_target_pairs={{0,1},{1,0},{2,3},{3,2},{4,5},{5,4},{6,7},{7,6},{8,9},{9,8},{10,11... | collective-permute-start | bytes 5111816 | tf_op jit(solution)/shard_map/ppermute | solution.py:1055
  9.9 21.0 %collective-permute-start.1 = (bf16[3,512,256]{2,1,0:T(8,128)(2,1)}, bf16[3,512,256]{2,1,0:T(8,128)(2,1)}, u32[]{:S(2)}, u32[]{:S(2)}) collective-permute-start(bf16[3,512,256]{2,1,0:T(8,128)(2,1)} %constant_dynamic-slice_fusion.6), channel_id=1, source_target_pairs={{0,2},{2,0},{1,3},{3,1},{4,6},{6,4},{5,7},{7,5},{8,10},{10,8},{9,1... | collective-permute-start | bytes 2359304 | tf_op jit(solution)/shard_map/ppermute | solution.py:1058
  30.9 21.8 %collective-permute-start.2 = (bf16[3,512,256]{2,1,0:T(8,128)(2,1)}, bf16[3,512,256]{2,1,0:T(8,128)(2,1)}, u32[]{:S(2)}, u32[]{:S(2)}) collective-permute-start(bf16[3,512,256]{2,1,0:T(8,128)(2,1)} %collective-permute-done.1.first_ref.refs_7_), channel_id=1, source_target_pairs={{0,8},{4,12},{8,0},{12,4},{16,24},{20,28},{24,16},{28,20},{1,9},{5... | collective-permute-start | bytes 2359304 | tf_op jit(solution)/shard_map/ppermute | solution.py:1061
  32.7 21.6 %collective-permute-start.7 = (bf16[1024,256]{1,0:T(8,128)(2,1)}, bf16[1024,256]{1,0:T(8,128)(2,1)}, u32[]{:S(2)}, u32[]{:S(2)}) collective-permute-start(bf16[1024,256]{1,0:T(8,128)(2,1)} %refs_0_.6), channel_id=1, source_target_pairs={{0,1},{1,0},{2,3},{3,2},{4,5},{5,4},{6,7},{7,6},{8,9},{9,8},{10,11... | collective-permute-start | bytes 1572872 | tf_op jit(solution)/shard_map/ppermute | solution.py:1055
  33.3 34.1 %collective-permute-start.6 = (bf16[512,1024]{1,0:T(8,128)(2,1)}, bf16[512,1024]{1,0:T(8,128)(2,1)}, u32[]{:S(2)}, u32[]{:S(2)}) collective-permute-start(bf16[512,1024]{1,0:T(8,128)(2,1)} %pad_maximum_fusion.1), channel_id=1, source_target_pairs={{0,1},{1,0},{2,3},{3,2},{4,5},{5,4},{6,7},{7,6},{8,9},{9,8},{10,11... | collective-permute-start | bytes 3145736 | tf_op jit(solution)/shard_map/ppermute | solution.py:1055
  33.8 55.9 %collective-permute-start.10 = (bf16[832,1024]{1,0:T(8,128)(2,1)S(1)}, bf16[832,1024]{1,0:T(8,128)(2,1)}, u32[]{:S(2)}, u32[]{:S(2)}) collective-permute-start(bf16[832,1024]{1,0:T(8,128)(2,1)S(1)} %broadcast_select_fusion.d_ref.mine_ref), channel_id=1, source_target_pairs={{0,1},{1,0},{2,3},{3,2},{4,5},{5,4},{6,7},{7,6},{8,9},{9,8},{10,11... | collective-permute-start | bytes 5111816 | tf_op jit(solution)/shard_map/ppermute | solution.py:1055
  35.9 31.4 %collective-permute-start.4 = (bf16[1536,256]{1,0:T(8,128)(2,1)}, bf16[1536,256]{1,0:T(8,128)(2,1)}, u32[]{:S(2)}, u32[]{:S(2)}) collective-permute-start(bf16[1536,256]{1,0:T(8,128)(2,1)} %constant_dynamic-slice_fusion.4), channel_id=1, source_target_pairs={{0,2},{2,0},{1,3},{3,1},{4,6},{6,4},{5,7},{7,5},{8,10},{10,8},{9,1... | collective-permute-start | bytes 2359304 | tf_op jit(solution)/shard_map/ppermute | solution.py:1058
  52.7 14.7 %collective-permute-start.3 = (bf16[256,1024]{1,0:T(8,128)(2,1)}, bf16[256,1024]{1,0:T(8,128)(2,1)}, u32[]{:S(2)}, u32[]{:S(2)}) collective-permute-start(bf16[256,1024]{1,0:T(8,128)(2,1)} %constant_dynamic-slice_fusion.5), channel_id=1, source_target_pairs={{0,2},{2,0},{1,3},{3,1},{4,6},{6,4},{5,7},{7,5},{8,10},{10,8},{9,1... | collective-permute-start | bytes 1572872 | tf_op jit(solution)/shard_map/ppermute | solution.py:1058
  54.3 13.1 %collective-permute-start.5 = (bf16[832,256]{1,0:T(8,128)(2,1)S(1)}, bf16[832,256]{1,0:T(8,128)(2,1)S(1)}, u32[]{:S(2)}, u32[]{:S(2)}) collective-permute-start(bf16[832,256]{1,0:T(8,128)(2,1)S(1)} %constant_dynamic-slice_fusion.1), channel_id=1, source_target_pairs={{0,1},{1,0},{2,3},{3,2},{4,5},{5,4},{6,7},{7,6},{8,9},{9,8},{10,11... | collective-permute-start | bytes 1277960 | tf_op jit(solution)/shard_map/ppermute | solution.py:1055
  68.2 21.6 %collective-permute-start.9 = (bf16[1536,256]{1,0:T(8,128)(2,1)}, bf16[1536,256]{1,0:T(8,128)(2,1)}, u32[]{:S(2)}, u32[]{:S(2)}) collective-permute-start(bf16[1536,256]{1,0:T(8,128)(2,1)} %collective-permute-done.4), channel_id=1, source_target_pairs={{0,8},{4,12},{8,0},{12,4},{16,24},{20,28},{24,16},{28,20},{1,9},{5... | collective-permute-start | bytes 2359304 | tf_op jit(solution)/shard_map/ppermute | solution.py:1061
  68.6 21.1 %collective-permute-start.8 = (bf16[256,1024]{1,0:T(8,128)(2,1)}, bf16[256,1024]{1,0:T(8,128)(2,1)}, u32[]{:S(2)}, u32[]{:S(2)}) collective-permute-start(bf16[256,1024]{1,0:T(8,128)(2,1)} %collective-permute-done.3), channel_id=1, source_target_pairs={{0,4},{4,0},{8,12},{12,8},{16,20},{20,16},{24,28},{28,24},{1,5},{5... | collective-permute-start | bytes 1572872 | tf_op jit(solution)/shard_map/ppermute | solution.py:1061
  70.6 51.0 %collective-permute-start.15 = (bf16[1024,512]{1,0:T(8,128)(2,1)}, bf16[1024,512]{1,0:T(8,128)(2,1)}, u32[]{:S(2)}, u32[]{:S(2)}) collective-permute-start(bf16[1024,512]{1,0:T(8,128)(2,1)} %constant_dynamic-slice_fusion.3), channel_id=1, source_target_pairs={{0,2},{2,0},{1,3},{3,1},{4,6},{6,4},{5,7},{7,5},{8,10},{10,8},{9,1... | collective-permute-start | bytes 3145736 | tf_op jit(solution)/shard_map/ppermute | solution.py:1058
  91.7 6.5 %collective-permute-start.12 = (bf16[512,1024]{1,0:T(8,128)(2,1)S(1)}, bf16[512,1024]{1,0:T(8,128)(2,1)S(1)}, u32[]{:S(2)}, u32[]{:S(2)}) collective-permute-start(bf16[512,1024]{1,0:T(8,128)(2,1)S(1)} %maximum_select_fusion.3), channel_id=1, source_target_pairs={{0,1},{1,0},{2,3},{3,2},{4,5},{5,4},{6,7},{7,6},{8,9},{9,8},{10,11... | collective-permute-start | bytes 3145736 | tf_op jit(solution)/shard_map/ppermute | solution.py:1055
  94.3 27.3 %collective-permute-start.16 = (bf16[512,1024]{1,0:T(8,128)(2,1)S(1)}, bf16[512,1024]{1,0:T(8,128)(2,1)S(1)}, u32[]{:S(2)}, u32[]{:S(2)}) collective-permute-start(bf16[512,1024]{1,0:T(8,128)(2,1)S(1)} %copy-done.98), channel_id=1, source_target_pairs={{0,2},{2,0},{1,3},{3,1},{4,6},{6,4},{5,7},{7,5},{8,10},{10,8},{9,1... | collective-permute-start | bytes 3145736 | tf_op jit(solution)/shard_map/ppermute | solution.py:1058
  95.2 1.7 collective-permute-start.14
  96.5 2.8 collective-permute-start.13
  96.9 2.4 collective-permute-start.11
  121.7 14.6 %collective-permute-start.17 = (bf16[832,1024]{1,0:T(8,128)(2,1)}, bf16[832,1024]{1,0:T(8,128)(2,1)S(1)}, u32[]{:S(2)}, u32[]{:S(2)}) collective-permute-start(bf16[832,1024]{1,0:T(8,128)(2,1)} %get-tuple-element.197.h_ref.mine_ref), channel_id=1, source_target_pairs={{0,1},{1,0},{2,3},{3,2},{4,5},{5,4},{6,7},{7,6},{8,9},{9,8},{10,11... | collective-permute-start | bytes 5111816 | tf_op jit(solution)/shard_map/ppermute | solution.py:1055
  122.0 27.6 %collective-permute-start.18 = (bf16[1024,512]{1,0:T(8,128)(2,1)}, bf16[1024,512]{1,0:T(8,128)(2,1)}, u32[]{:S(2)}, u32[]{:S(2)}) collective-permute-start(bf16[1024,512]{1,0:T(8,128)(2,1)} %collective-permute-done.15.refs_0_), channel_id=1, source_target_pairs={{0,8},{4,12},{8,0},{12,4},{16,24},{20,28},{24,16},{28,20},{1,9},{5... | collective-permute-start | bytes 3145736 | tf_op jit(solution)/shard_map/ppermute | solution.py:1061
  123.6 46.5 %collective-permute-start.19 = (bf16[512,1024]{1,0:T(8,128)(2,1)S(1)}, bf16[512,1024]{1,0:T(8,128)(2,1)}, u32[]{:S(2)}, u32[]{:S(2)}) collective-permute-start(bf16[512,1024]{1,0:T(8,128)(2,1)S(1)} %collective-permute-done.16.refs_2_), channel_id=1, source_target_pairs={{0,8},{4,12},{8,0},{12,4},{16,24},{20,28},{24,16},{28,20},{1,9},{5... | collective-permute-start | bytes 3145736 | tf_op jit(solution)/shard_map/ppermute | solution.py:1061
  183.5 33.2 %collective-permute-start.21 = (bf16[832,1024]{1,0:T(8,128)(2,1)}, bf16[832,1024]{1,0:T(8,128)(2,1)}, u32[]{:S(2)}, u32[]{:S(2)}) collective-permute-start(bf16[832,1024]{1,0:T(8,128)(2,1)} %get-tuple-element.221), channel_id=1, source_target_pairs={{0,1},{1,0},{2,3},{3,2},{4,5},{5,4},{6,7},{7,6},{8,9},{9,8},{10,11... | collective-permute-start | bytes 5111816 | tf_op jit(solution)/shard_map/ppermute | solution.py:1055
  204.5 48.2 %collective-permute-start.20 = (bf16[1024,1024]{1,0:T(8,128)(2,1)}, bf16[1024,1024]{1,0:T(8,128)(2,1)S(1)}, u32[]{:S(2)}, u32[]{:S(2)}) collective-permute-start(bf16[1024,1024]{1,0:T(8,128)(2,1)} %up_grad.2), channel_id=1, source_target_pairs={{0,2},{2,0},{1,3},{3,1},{4,6},{6,4},{5,7},{7,5},{8,10},{10,8},{9,1... | collective-permute-start | bytes 6291464 | tf_op jit(solution)/shard_map/ppermute | solution.py:1058
  240.0 12.8 %collective-permute-start.22 = (bf16[832,1024]{1,0:T(8,128)(2,1)}, bf16[832,1024]{1,0:T(8,128)(2,1)S(1)}, u32[]{:S(2)}, u32[]{:S(2)}) collective-permute-start(bf16[832,1024]{1,0:T(8,128)(2,1)} %get-tuple-element.236.mine_ref.sm_ref), channel_id=1, source_target_pairs={{0,1},{1,0},{2,3},{3,2},{4,5},{5,4},{6,7},{7,6},{8,9},{9,8},{10,11... | collective-permute-start | bytes 5111816 | tf_op jit(solution)/shard_map/ppermute | solution.py:1055
  252.8 49.0 %copy-start.12 = (bf16[832,1024]{1,0:T(8,128)(2,1)}, bf16[832,1024]{1,0:T(8,128)(2,1)S(1)}, u32[]{:S(2)}) copy-start(bf16[832,1024]{1,0:T(8,128)(2,1)S(1)} %collective-permute-done.22.other_ref.so_ref) | copy-start | bytes 5111812
  252.8 32.7 %collective-permute-start.24 = (bf16[832,1024]{1,0:T(8,128)(2,1)}, bf16[832,1024]{1,0:T(8,128)(2,1)}, u32[]{:S(2)}, u32[]{:S(2)}) collective-permute-start(bf16[832,1024]{1,0:T(8,128)(2,1)} %get-tuple-element.241.cm_ref), channel_id=1, source_target_pairs={{0,1},{1,0},{2,3},{3,2},{4,5},{5,4},{6,7},{7,6},{8,9},{9,8},{10,11... | collective-permute-start | bytes 5111816 | tf_op jit(solution)/shard_map/ppermute | solution.py:1055
  252.9 32.7 %collective-permute-start.23 = (bf16[512,1024]{1,0:T(8,128)(2,1)}, bf16[512,1024]{1,0:T(8,128)(2,1)}, u32[]{:S(2)}, u32[]{:S(2)}) collective-permute-start(bf16[512,1024]{1,0:T(8,128)(2,1)} %down_grad.3), channel_id=1, source_target_pairs={{0,2},{2,0},{1,3},{3,1},{4,6},{6,4},{5,7},{7,5},{8,10},{10,8},{9,1... | collective-permute-start | bytes 3145736 | tf_op jit(solution)/shard_map/ppermute | solution.py:1058
  255.5 30.1 %collective-permute-start.25 = (bf16[832,512]{1,0:T(8,128)(2,1)}, bf16[832,512]{1,0:T(8,128)(2,1)}, u32[]{:S(2)}, u32[]{:S(2)}) collective-permute-start(bf16[832,512]{1,0:T(8,128)(2,1)} %slice.117), channel_id=1, source_target_pairs={{0,1},{1,0},{2,3},{3,2},{4,5},{5,4},{6,7},{7,6},{8,9},{9,8},{10,11... | collective-permute-start | bytes 2555912 | tf_op jit(solution)/shard_map/ppermute | solution.py:1055
  255.6 52.9 %collective-permute-start.28 = (bf16[832,1024]{1,0:T(8,128)(2,1)S(1)}, bf16[832,1024]{1,0:T(8,128)(2,1)}, u32[]{:S(2)}, u32[]{:S(2)}) collective-permute-start(bf16[832,1024]{1,0:T(8,128)(2,1)S(1)} %copy-done.38), channel_id=1, source_target_pairs={{0,1},{1,0},{2,3},{3,2},{4,5},{5,4},{6,7},{7,6},{8,9},{9,8},{10,11... | collective-permute-start | bytes 5111816 | tf_op jit(solution)/shard_map/ppermute | solution.py:1055
  256.0 2.6 collective-permute-start.26
  259.3 42.4 %collective-permute-start.29 = (bf16[832,512]{1,0:T(8,128)(2,1)}, bf16[832,512]{1,0:T(8,128)(2,1)}, u32[]{:S(2)}, u32[]{:S(2)}) collective-permute-start(bf16[832,512]{1,0:T(8,128)(2,1)} %slice.121), channel_id=1, source_target_pairs={{0,1},{1,0},{2,3},{3,2},{4,5},{5,4},{6,7},{7,6},{8,9},{9,8},{10,11... | collective-permute-start | bytes 2555912 | tf_op jit(solution)/shard_map/ppermute | solution.py:1055
  285.6 27.5 %collective-permute-start.27 = (bf16[512,1024]{1,0:T(8,128)(2,1)S(1)}, bf16[512,1024]{1,0:T(8,128)(2,1)S(1)}, u32[]{:S(2)}, u32[]{:S(2)}) collective-permute-start(bf16[512,1024]{1,0:T(8,128)(2,1)S(1)} %copy-done.59), channel_id=1, source_target_pairs={{0,2},{2,0},{1,3},{3,1},{4,6},{6,4},{5,7},{7,5},{8,10},{10,8},{9,1... | collective-permute-start | bytes 3145736 | tf_op jit(solution)/shard_map/ppermute | solution.py:1058
  313.1 37.4 %collective-permute-start.30 = (bf16[3072,256]{1,0:T(8,128)(2,1)}, bf16[3072,256]{1,0:T(8,128)(2,1)}, u32[]{:S(2)}, u32[]{:S(2)}) collective-permute-start(bf16[3072,256]{1,0:T(8,128)(2,1)} %qkv_grad.2), channel_id=1, source_target_pairs={{0,2},{2,0},{1,3},{3,1},{4,6},{6,4},{5,7},{7,5},{8,10},{10,8},{9,1... | collective-permute-start | bytes 4718600 | tf_op jit(solution)/shard_map/ppermute | solution.py:1058
  318.1 273.9 %all-reduce.5.cloned.1.call-start = ((), (), s32[]{:S(2)}) async-start(), calls=%async_computation.1 | async-start | bytes 4194304 | tf_op jit(solution)/shard_map/psum | solution.py:1274
  350.5 32.8 %collective-permute-start.33 = (bf16[832,1024]{1,0:T(8,128)(2,1)}, bf16[832,1024]{1,0:T(8,128)(2,1)}, u32[]{:S(2)}, u32[]{:S(2)}) collective-permute-start(bf16[832,1024]{1,0:T(8,128)(2,1)} %first_back.2), channel_id=1, source_target_pairs={{0,1},{1,0},{2,3},{3,2},{4,5},{5,4},{6,7},{7,6},{8,9},{9,8},{10,11... | collective-permute-start | bytes 5111816 | tf_op jit(solution)/shard_map/ppermute | solution.py:1055
  350.6 71.9 %collective-permute-start.31 = (bf16[3072,256]{1,0:T(8,128)(2,1)}, bf16[3072,256]{1,0:T(8,128)(2,1)}, u32[]{:S(2)}, u32[]{:S(2)}) collective-permute-start(bf16[3072,256]{1,0:T(8,128)(2,1)} %cross_in_grad.2), channel_id=1, source_target_pairs={{0,2},{2,0},{1,3},{3,1},{4,6},{6,4},{5,7},{7,5},{8,10},{10,8},{9,1... | collective-permute-start | bytes 4718600 | tf_op jit(solution)/shard_map/ppermute | solution.py:1058
  351.5 77.6 %collective-permute-start.39 = (bf16[832,1024]{1,0:T(8,128)(2,1)}, bf16[832,1024]{1,0:T(8,128)(2,1)}, u32[]{:S(2)}, u32[]{:S(2)}) collective-permute-start(bf16[832,1024]{1,0:T(8,128)(2,1)} %get-tuple-element.284), channel_id=1, source_target_pairs={{0,1},{1,0},{2,3},{3,2},{4,5},{5,4},{6,7},{7,6},{8,9},{9,8},{10,11... | collective-permute-start | bytes 5111816 | tf_op jit(solution)/shard_map/ppermute | solution.py:1055
  370.1 52.4 %collective-permute-start.32 = (bf16[1536,256]{1,0:T(8,128)(2,1)}, bf16[1536,256]{1,0:T(8,128)(2,1)}, u32[]{:S(2)}, u32[]{:S(2)}) collective-permute-start(bf16[1536,256]{1,0:T(8,128)(2,1)} %add_convert_fusion.4), channel_id=1, source_target_pairs={{0,4},{4,0},{8,12},{12,8},{16,20},{20,16},{24,28},{28,24},{1,5},{5... | collective-permute-start | bytes 2359304 | tf_op jit(solution)/shard_map/ppermute | solution.py:1061
  378.2 57.2 %collective-permute-start.38 = (f32[64,1024]{1,0:T(8,128)}, f32[64,1024]{1,0:T(8,128)}, u32[]{:S(2)}, u32[]{:S(2)}) collective-permute-start(f32[64,1024]{1,0:T(8,128)} %convolution_add_fusion), channel_id=1, source_target_pairs={{0,1},{1,0},{2,3},{3,2},{4,5},{5,4},{6,7},{7,6},{8,9},{9,8},{10,11... | collective-permute-start | bytes 786440 | tf_op jit(solution)/shard_map/ppermute | solution.py:1055
  383.3 39.2 %copy-start.108 = (f32[8,1024]{1,0:T(8,128)S(1)}, f32[8,1024]{1,0:T(8,128)}, u32[]{:S(2)}) copy-start(f32[8,1024]{1,0:T(8,128)} %get-tuple-element.280) | copy-start | bytes 98308
  389.3 38.1 %copy-start.17 = (f32[3072,256]{1,0:T(8,128)S(1)}, f32[3072,256]{1,0:T(8,128)}, u32[]{:S(2)}) copy-start(f32[3072,256]{1,0:T(8,128)} %copy-done.16) | copy-start | bytes 9437188
  422.5 13.0 %collective-permute-start.37 = (f32[8,1024]{1,0:T(8,128)S(1)}, f32[8,1024]{1,0:T(8,128)S(1)}, u32[]{:S(2)}, u32[]{:S(2)}) collective-permute-start(f32[8,1024]{1,0:T(8,128)S(1)} %add.183), channel_id=1, source_target_pairs={{0,1},{1,0},{2,3},{3,2},{4,5},{5,4},{6,7},{7,6},{8,9},{9,8},{10,11... | collective-permute-start | bytes 98312 | tf_op jit(solution)/shard_map/ppermute | solution.py:1055
  424.4 20.0 %collective-permute-start.35 = (bf16[1536,256]{1,0:T(8,128)(2,1)S(1)}, bf16[1536,256]{1,0:T(8,128)(2,1)S(1)}, u32[]{:S(2)}, u32[]{:S(2)}) collective-permute-start(bf16[1536,256]{1,0:T(8,128)(2,1)S(1)} %add_convert_fusion.3), channel_id=1, source_target_pairs={{0,4},{4,0},{8,12},{12,8},{16,20},{20,16},{24,28},{28,24},{1,5},{5... | collective-permute-start | bytes 2359304 | tf_op jit(solution)/shard_map/ppermute | solution.py:1061
  425.9 25.5 %collective-permute-start.34 = (bf16[512,1024]{1,0:T(8,128)(2,1)}, bf16[512,1024]{1,0:T(8,128)(2,1)S(1)}, u32[]{:S(2)}, u32[]{:S(2)}) collective-permute-start(bf16[512,1024]{1,0:T(8,128)(2,1)} %copy-done.60), channel_id=1, source_target_pairs={{0,2},{2,0},{1,3},{3,1},{4,6},{6,4},{5,7},{7,5},{8,10},{10,8},{9,1... | collective-permute-start | bytes 3145736 | tf_op jit(solution)/shard_map/ppermute | solution.py:1058
  429.1 11.0 %collective-permute-start.36 = (bf16[768,256]{1,0:T(8,128)(2,1)S(1)}, bf16[768,256]{1,0:T(8,128)(2,1)S(1)}, u32[]{:S(2)}, u32[]{:S(2)}) collective-permute-start(bf16[768,256]{1,0:T(8,128)(2,1)S(1)} %dynamic-slice_convert_fusion.1), channel_id=1, source_target_pairs={{0,8},{4,12},{8,0},{12,4},{16,24},{20,28},{24,16},{28,20},{1,9},{5... | collective-permute-start | bytes 1179656 | tf_op jit(solution)/shard_map/ppermute | solution.py:1061
  451.5 20.0 %collective-permute-start.42 = (bf16[768,256]{1,0:T(8,128)(2,1)S(1)}, bf16[768,256]{1,0:T(8,128)(2,1)}, u32[]{:S(2)}, u32[]{:S(2)}) collective-permute-start(bf16[768,256]{1,0:T(8,128)(2,1)S(1)} %add_convert_fusion.9), channel_id=1, source_target_pairs={{0,16},{4,20},{8,24},{12,28},{16,0},{20,4},{24,8},{28,12},{1,17},{... | collective-permute-start | bytes 1179656 | tf_op jit(solution)/shard_map/ppermute | solution.py:1061
  456.2 35.0 %collective-permute-start.41 = (bf16[768,256]{1,0:T(8,128)(2,1)}, bf16[768,256]{1,0:T(8,128)(2,1)}, u32[]{:S(2)}, u32[]{:S(2)}) collective-permute-start(bf16[768,256]{1,0:T(8,128)(2,1)} %dynamic-slice_convert_fusion), channel_id=1, source_target_pairs={{0,8},{4,12},{8,0},{12,4},{16,24},{20,28},{24,16},{28,20},{1,9},{5... | collective-permute-start | bytes 1179656 | tf_op jit(solution)/shard_map/ppermute | solution.py:1061
  456.8 34.4 %collective-permute-start.40 = (bf16[256,1024]{1,0:T(8,128)(2,1)S(1)}, bf16[256,1024]{1,0:T(8,128)(2,1)}, u32[]{:S(2)}, u32[]{:S(2)}) collective-permute-start(bf16[256,1024]{1,0:T(8,128)(2,1)S(1)} %add_convert_fusion.5), channel_id=1, source_target_pairs={{0,4},{4,0},{8,12},{12,8},{16,20},{20,16},{24,28},{28,24},{1,5},{5... | collective-permute-start | bytes 1572872 | tf_op jit(solution)/shard_map/ppermute | solution.py:1061
  458.5 9.7 %collective-permute-start.44 = (bf16[64,1024]{1,0:T(8,128)(2,1)S(1)}, bf16[64,1024]{1,0:T(8,128)(2,1)S(1)}, u32[]{:S(2)}, u32[]{:S(2)}) collective-permute-start(bf16[64,1024]{1,0:T(8,128)(2,1)S(1)} %add_convert_fusion.12), channel_id=1, source_target_pairs={{0,2},{2,0},{1,3},{3,1},{4,6},{6,4},{5,7},{7,5},{8,10},{10,8},{9,1... | collective-permute-start | bytes 393224 | tf_op jit(solution)/shard_map/ppermute | solution.py:1058
  460.0 8.2 %collective-permute-start.43 = (f32[8,1024]{1,0:T(8,128)S(1)}, f32[8,1024]{1,0:T(8,128)S(1)}, u32[]{:S(2)}, u32[]{:S(2)}) collective-permute-start(f32[8,1024]{1,0:T(8,128)S(1)} %add.196), channel_id=1, source_target_pairs={{0,2},{2,0},{1,3},{3,1},{4,6},{6,4},{5,7},{7,5},{8,10},{10,8},{9,1... | collective-permute-start | bytes 98312 | tf_op jit(solution)/shard_map/ppermute | solution.py:1058
  464.0 29.1 %copy-start.82 = (f32[1536,256]{1,0:T(8,128)S(1)}, f32[1536,256]{1,0:T(8,128)}, u32[]{:S(2)}) copy-start(f32[1536,256]{1,0:T(8,128)} %copy-done.81) | copy-start | bytes 4718596
  493.0 26.0 %collective-permute-start.47 = (bf16[768,256]{1,0:T(8,128)(2,1)}, bf16[768,256]{1,0:T(8,128)(2,1)}, u32[]{:S(2)}, u32[]{:S(2)}) collective-permute-start(bf16[768,256]{1,0:T(8,128)(2,1)} %add_convert_fusion.7), channel_id=1, source_target_pairs={{0,8},{4,12},{8,0},{12,4},{16,24},{20,28},{24,16},{28,20},{1,9},{5... | collective-permute-start | bytes 1179656 | tf_op jit(solution)/shard_map/ppermute | solution.py:1061
  494.9 24.2 %collective-permute-start.46 = (bf16[768,256]{1,0:T(8,128)(2,1)}, bf16[768,256]{1,0:T(8,128)(2,1)}, u32[]{:S(2)}, u32[]{:S(2)}) collective-permute-start(bf16[768,256]{1,0:T(8,128)(2,1)} %add_convert_fusion.8), channel_id=1, source_target_pairs={{0,16},{4,20},{8,24},{12,28},{16,0},{20,4},{24,8},{28,12},{1,17},{... | collective-permute-start | bytes 1179656 | tf_op jit(solution)/shard_map/ppermute | solution.py:1061
  497.9 21.1 %collective-permute-start.45 = (bf16[128,1024]{1,0:T(8,128)(2,1)S(1)}, bf16[128,1024]{1,0:T(8,128)(2,1)S(1)}, u32[]{:S(2)}, u32[]{:S(2)}) collective-permute-start(bf16[128,1024]{1,0:T(8,128)(2,1)S(1)} %dynamic-slice_convert_fusion.2), channel_id=1, source_target_pairs={{0,8},{4,12},{8,0},{12,4},{16,24},{20,28},{24,16},{28,20},{1,9},{5... | collective-permute-start | bytes 786440 | tf_op jit(solution)/shard_map/ppermute | solution.py:1061
  498.4 3.9 collective-permute-start.48
  520.3 20.6 %collective-permute-start.50 = (bf16[768,256]{1,0:T(8,128)(2,1)S(1)}, bf16[768,256]{1,0:T(8,128)(2,1)S(1)}, u32[]{:S(2)}, u32[]{:S(2)}) collective-permute-start(bf16[768,256]{1,0:T(8,128)(2,1)S(1)} %add_convert_fusion.6), channel_id=1, source_target_pairs={{0,8},{4,12},{8,0},{12,4},{16,24},{20,28},{24,16},{28,20},{1,9},{5... | collective-permute-start | bytes 1179656 | tf_op jit(solution)/shard_map/ppermute | solution.py:1061
  520.5 20.5 %collective-permute-start.49 = (bf16[128,1024]{1,0:T(8,128)(2,1)S(1)}, bf16[128,1024]{1,0:T(8,128)(2,1)S(1)}, u32[]{:S(2)}, u32[]{:S(2)}) collective-permute-start(bf16[128,1024]{1,0:T(8,128)(2,1)S(1)} %add_convert_fusion.11), channel_id=1, source_target_pairs={{0,16},{4,20},{8,24},{12,28},{16,0},{20,4},{24,8},{28,12},{1,17},{... | collective-permute-start | bytes 786440 | tf_op jit(solution)/shard_map/ppermute | solution.py:1061
  522.6 18.4 %collective-permute-start.51 = (f32[8,1024]{1,0:T(8,128)S(1)}, f32[8,1024]{1,0:T(8,128)S(1)}, u32[]{:S(2)}, u32[]{:S(2)}) collective-permute-start(f32[8,1024]{1,0:T(8,128)S(1)} %add.203), channel_id=1, source_target_pairs={{0,8},{4,12},{8,0},{12,4},{16,24},{20,28},{24,16},{28,20},{1,9},{5... | collective-permute-start | bytes 98312 | tf_op jit(solution)/shard_map/ppermute | solution.py:1061
  524.2 74.1 %collective-permute-start.55 = (bf16[1536,256]{1,0:T(8,128)(2,1)S(1)}, bf16[1536,256]{1,0:T(8,128)(2,1)}, u32[]{:S(2)}, u32[]{:S(2)}) collective-permute-start(bf16[1536,256]{1,0:T(8,128)(2,1)S(1)} %maximum_select_fusion.6), channel_id=1, source_target_pairs={{0,4},{4,0},{8,12},{12,8},{16,20},{20,16},{24,28},{28,24},{1,5},{5... | collective-permute-start | bytes 2359304 | tf_op jit(solution)/shard_map/ppermute | solution.py:1061
  541.3 62.3 %collective-permute-start.52 = (bf16[1536,256]{1,0:T(8,128)(2,1)S(1)}, bf16[1536,256]{1,0:T(8,128)(2,1)S(1)}, u32[]{:S(2)}, u32[]{:S(2)}) collective-permute-start(bf16[1536,256]{1,0:T(8,128)(2,1)S(1)} %maximum_select_fusion.5), channel_id=1, source_target_pairs={{0,4},{4,0},{8,12},{12,8},{16,20},{20,16},{24,28},{28,24},{1,5},{5... | collective-permute-start | bytes 2359304 | tf_op jit(solution)/shard_map/ppermute | solution.py:1061
  542.2 56.0 %collective-permute-start.54 = (bf16[128,1024]{1,0:T(8,128)(2,1)S(1)}, bf16[128,1024]{1,0:T(8,128)(2,1)S(1)}, u32[]{:S(2)}, u32[]{:S(2)}) collective-permute-start(bf16[128,1024]{1,0:T(8,128)(2,1)S(1)} %add_convert_fusion.10), channel_id=1, source_target_pairs={{0,8},{4,12},{8,0},{12,4},{16,24},{20,28},{24,16},{28,20},{1,9},{5... | collective-permute-start | bytes 786440 | tf_op jit(solution)/shard_map/ppermute | solution.py:1061
  596.1 7.5 %collective-permute-start.53 = (f32[8,1024]{1,0:T(8,128)S(1)}, f32[8,1024]{1,0:T(8,128)S(1)}, u32[]{:S(2)}, u32[]{:S(2)}) collective-permute-start(f32[8,1024]{1,0:T(8,128)S(1)} %add.207), channel_id=1, source_target_pairs={{0,16},{4,20},{8,24},{12,28},{16,0},{20,4},{24,8},{28,12},{1,17},{... | collective-permute-start | bytes 98312 | tf_op jit(solution)/shard_map/ppermute | solution.py:1061
  598.4 13.6 %collective-permute-start.56 = (bf16[256,1024]{1,0:T(8,128)(2,1)S(1)}, bf16[256,1024]{1,0:T(8,128)(2,1)}, u32[]{:S(2)}, u32[]{:S(2)}) collective-permute-start(bf16[256,1024]{1,0:T(8,128)(2,1)S(1)} %maximum_select_fusion.7), channel_id=1, source_target_pairs={{0,4},{4,0},{8,12},{12,8},{16,20},{20,16},{24,28},{28,24},{1,5},{5... | collective-permute-start | bytes 1572872 | tf_op jit(solution)/shard_map/ppermute | solution.py:1061
  (106 other events, 716.2 us)
Sparse Core Ops, SparseCore 0:
  318.2 104.2 all-reduce.2
  464.1 127.8 all-reduce.4

commit v7 on v6

--- a/solution.py
+++ b/solution.py
@@ -773,16 +773,17 @@
     out_ref[...] = total.astype(out_ref.dtype)
 
 
-def down_grad(g, mine, other, kind, first=0, tiles=2):
+def down_grad(g, mine, other, kind):
     rows, width = mine.shape
+    hidden = g.shape[1]
     tile = 512
     whole = pl.BlockSpec((rows, width), lambda i: (0, 0), pipeline_mode=pl.Buffered(1))
     return pl.pallas_call(
         down_grad_kernel,
-        grid=(tiles,),
-        in_specs=[pl.BlockSpec((2 * rows, tile), lambda i: (0, i + first)), whole, whole],
+        grid=(hidden // tile,),
+        in_specs=[pl.BlockSpec((2 * rows, tile), lambda i: (0, i)), whole, whole],
         out_specs=pl.BlockSpec((tile, width), lambda i: (i, 0)),
-        out_shape=shape((tiles * tile, width), kind),
+        out_shape=shape((hidden, width), kind),
         compiler_params=params(48),
         cost_estimate=brief(),
         name="down_grad",
@@ -1164,171 +1165,237 @@
 
     across = (column, X_PAIRS)
     down_z = (near, Z_NEAR)
+    store = {}
+    last = []
+
+    def order(*names):
+        names = tuple(dict.fromkeys((*names, *last)))
+        for name, value in zip(names, join(tuple(store[name] for name in names))):
+            store[name] = value
+
+    def get(*names):
+        return tuple(store[name] for name in names)
+
+    def step(results, make, *needs):
+        order(*needs)
+        made = make()
+        made = made if isinstance(made, (tuple, list)) else (made,)
+        store.update(zip(results, made))
+        last[:] = results[:1]
 
     class Sum:
-        def __init__(self, partner, order=(across, down_z)):
-            self.order = order
-            self.fly = over_y(partner)
+        def __init__(self, name, axes=(across, down_z)):
+            self.fly, self.kept, self.axes = name + "_fly", name + "_kept", axes
+
+        def over_y(self, partner):
+            order(partner)
+            store[self.fly] = over_y(store[partner])
 
         def first(self, own):
-            which, pairs = self.order[0]
-            away_half = lower(half_of(own, 1 - which) + half_of(self.fly, 1 - which).astype(FULL))
-            self.kept = half_of(own, which) + half_of(self.fly, which).astype(FULL)
-            self.fly = along_wide(away_half, pairs)
+            which, pairs = self.axes[0]
+            order(self.fly, own)
+            mine, fly = get(own, self.fly)
+            away_half = plus(half_of(mine, 1 - which), half_of(fly, 1 - which))
+            store[self.kept] = half_of(mine, which).astype(FULL) + half_of(fly, which).astype(FULL)
+            store[self.fly] = along_wide(away_half, pairs)
+            last[:] = [self.kept]
 
         def second(self):
-            which, pairs = self.order[1]
-            total = self.kept + self.fly.astype(FULL)
-            self.kept = half_of(total, which)
-            self.fly = along_wide(lower(half_of(total, 1 - which)), pairs)
+            which, pairs = self.axes[1]
+            order(self.fly, self.kept)
+            total = store[self.kept] + store[self.fly].astype(FULL)
+            store[self.kept] = half_of(total, which)
+            store[self.fly] = along_wide(lower(half_of(total, 1 - which)), pairs)
+            last[:] = [self.kept]
+
+        def add(self, pairs):
+            order(self.fly, self.kept)
+            store[self.kept] = plus(*get(self.kept, self.fly))
+            store[self.fly] = along_wide(store[self.kept], pairs)
+            last[:] = [self.kept]
 
         def far(self):
-            self.kept = plus(self.kept, self.fly)
-            self.fly = along_wide(self.kept, Z_FAR)
+            self.add(Z_FAR)
 
         def back(self):
-            self.kept = plus(self.kept, self.fly)
-            self.fly = along_wide(self.kept, self.order[1][1])
+            self.add(self.axes[1][1])
 
         def along(self):
-            self.kept = ordered(self.kept, self.fly, self.order[1][0])
-            self.fly = along_wide(self.kept, self.order[0][1])
-
-        def end(self):
-            return ordered(self.kept, self.fly, self.order[0][0]).astype(FULL)
-
-    def sync(in_flight, *values):
-        done = join((*[each.fly for each in in_flight], *values))
-        for each, fly in zip(in_flight, done):
-            each.fly = fly
-        return done[len(in_flight) :]
+            order(self.fly, self.kept)
+            store[self.kept] = ordered(*get(self.kept, self.fly), self.axes[1][0])
+            store[self.fly] = along_wide(store[self.kept], self.axes[0][1])
+            last[:] = [self.kept]
+
+        def end(self, result):
+            order(self.fly, self.kept)
+            store[result] = ordered(*get(self.kept, self.fly), self.axes[0][0]).astype(FULL)
+            last[:] = [result]
 
     class Row:
-        def __init__(self, value, step):
-            self.kept = value
-            self.fly = step(value)
-
-        def then(self, step):
-            self.kept = self.kept + self.fly
-            self.fly = step(self.kept)
-
-    up1 = up_grad(h3, h3_other, du1, ROUND)
-    up1, g1, du0, g0 = join((up1, g1, du0, g0))
-    up = Sum(up1)
-    down1a = down_grad(g1, dout, dout_other, ROUND, 0, 1)
-    down1b = down_grad(g1, dout, dout_other, ROUND, 1, 1)
-    y_received, down1a, down1b = join((y_received, down1a, down1b))
-    dx1, dself, dcross, dcq, dck, dcv, sums = middle_back(
-        place, y_m, y_received, x1, x2, dout, cq, norm_gain, wq, ck, cv, wc
-    )
-    du0, dself = join((du0, dself))
-    up0 = up_grad(h3, h3_other, du0, FULL)
-    dself_other = over_core(dself)
-    dself, dself_other, dcross, dcq, down1a, down1b, up0, g0 = sync(
-        [up], dself, dself_other, dcross, dcq, down1a, down1b, up0, g0
-    )
-
-    down_a = Sum(down1a)
-    up_total = lax.psum(lower(up0 + up.fly.astype(FULL)), "wide")
-    do0, do1 = pull(place, dself, dself_other, (w_out, out_y))
-    dcross_other = over_core(dcross)
-    dcq_other = over_core(dcq[:, 512:])
-    d_pair = jnp.stack([dck, dcv], axis=1)
-    d_pair_other = over_core(d_pair[2:])
-    dq1, dk1, dv1 = self_back(limit, q1, k1, v1, o1, do1, lse1)
-    dq1, dcross_other, dcq_other, d_pair_other, down1b = sync(
-        [down_a], dq1, dcross_other, dcq_other, d_pair_other, down1b
-    )
-
-    down_b = Sum(down1b)
-    d_pair = lower(d_pair[:2] + d_pair_other)
-    qkv1 = qkv_grad(place, h1, (dq1, dk1, dv1), ROUND)
-    down0 = down_grad(g0, dout, dout_other, FULL)
-    cross = (h2, h2_other, dcq, dcq_other, text)
-    outer = (dself, dself_other, ca, ca_other, dcross, dcross_other)
-    into1 = cross_in_grad(1, *cross, d_pair[1], ROUND)
-    outof1 = outputs_grad(place, 1, o1, *outer, ROUND)
-    qkv1, into1, outof1, do0, down0 = sync([down_b], qkv1, into1, outof1, do0, down0)
-
-    qkv = Sum(qkv1)
-    dq0, dk0, dv0 = self_back(limit, q0, k0, v0, o0, do0, lse0)
-    grads = (dq0, dk0, dv0, dq1, dk1, dv1)
-    yo = first_back(away, grads, w_qkv, qkv_first, qkv_second, ROUND)
-    dq0, yo, into1, outof1, d_pair = sync([qkv], dq0, yo, into1, outof1, d_pair)
-
-    cross_in = Sum(into1)
-    y_received = over_core(yo)
-    qkv0 = qkv_grad(place, h1, (dq0, dk0, dv0), FULL)
-    qkv.first(qkv0)
-    grads = (dq0, dk0, dv0, dq1, dk1, dv1)
-    ym = first_back(place, grads, w_qkv, qkv_first, qkv_second, FULL)
-    into0 = cross_in_grad(0, *cross, d_pair[0], FULL)
-    outof0 = outputs_grad(place, 0, o0, *outer, FULL)
-    grad_frames, first_sums = frames_back(place, ym, y_received, dx1, frames, norm_gain)
-    outof1, into0, outof0, grad_frames, x2, down0, up_total = sync(
-        [cross_in, qkv], outof1, into0, outof0, grad_frames, x2, down0, up_total
-    )
-
-    outs = Sum(outof1)
-    received = jnp.concatenate([down_a.fly, down_b.fly], axis=0)
-    down_total = lax.psum(lower(down0 + received.astype(FULL)), "wide")
-    cross_in.first(into0)
+        def __init__(self, name, value, move):
+            self.fly, self.kept = name + "_fly", name + "_kept"
+            store[self.kept] = value
+            store[self.fly] = move(value)
+
+        def then(self, move):
+            order(self.fly, self.kept)
+            store[self.kept] = store[self.kept] + store[self.fly]
+            store[self.fly] = move(store[self.kept])
+            last[:] = [self.kept]
+
+        def total(self):
+            return store[self.kept] + store[self.fly]
+
+    up, down, outs, cross_in = Sum("up"), Sum("down"), Sum("outs"), Sum("cross_in")
+    qkv = Sum("qkv", (down_z, across))
+    store.update(h3_other=h3_other, du1=du1, g1=g1, du0=du0, g0=g0, y_m=y_m, y_fly=y_received)
+    store.update(o1=o1, o0=o0, x2=x2, h2_other=h2_other, ca_other=ca_other)
+
+    step(["up1"], lambda: up_grad(h3, *get("h3_other", "du1"), ROUND), "du1", "du0")
+    up.over_y("up1")
+    step(["down1"], lambda: down_grad(store["g1"], dout, dout_other, ROUND), "g1")
+    down.over_y("down1")
+    step(
+        ["dself", "dx1", "dcross", "dcq", "dck", "dcv", "sums"],
+        lambda: (
+            lambda r: (r[1], r[0], *r[2:])
+        )(
+            middle_back(
+                place, *get("y_m", "y_fly"), x1, store["x2"], dout, cq, norm_gain, wq, ck, cv, wc
+            )
+        ),
+        "y_fly",
+        "y_m",
+        "x2",
+    )
+    store["dself_other"] = over_core(store["dself"])
+    step(["up0"], lambda: up_grad(h3, *get("h3_other", "du0"), ROUND), "du0")
+    store["dcross_other"] = over_core(store["dcross"])
+    store["dcq_other"] = over_core(store["dcq"][:, 512:])
+    d_pair = jnp.stack(get("dck", "dcv"), axis=1)
+    store["pair_kept"] = d_pair[:2]
+    store["pair_fly"] = over_core(d_pair[2:])
+    step(
+        ["do1", "do0"],
+        lambda: pull(place, *get("dself", "dself_other"), (out_y, w_out)),
+        "dself",
+        "dself_other",
+    )
+    step(
+        ["dq1", "dk1", "dv1"],
+        lambda: self_back(limit, q1, k1, v1, store["o1"], store["do1"], lse1),
+        "do1",
+    )
+    up.first("up0")
+    step(["down0"], lambda: down_grad(store["g0"], dout, dout_other, ROUND), "g0")
+    step(["qkv1"], lambda: qkv_grad(place, h1, get("dq1", "dk1", "dv1"), ROUND), "dq1")
+    qkv.over_y("qkv1")
+    order("dcross_other", "dcq_other", "pair_fly", "pair_kept")
+    store["pair"] = lower(store["pair_kept"] + store["pair_fly"])
+
+    def into(g):
+        return cross_in_grad(
+            g, h2, *get("h2_other", "dcq", "dcq_other"), text, store["pair"][g], ROUND
+        )
+
+    def outof(g, o):
+        return outputs_grad(
+            place, g, o, *get("dself", "dself_other"), ca,
+            *get("ca_other", "dcross", "dcross_other"), ROUND,
+        )
+
+    step(["into1"], lambda: into(1), "pair", "dcq_other", "h2_other")
+    cross_in.over_y("into1")
+    down.first("down0")
+    up.second()
+    step(["outs1"], lambda: outof(1, store["o1"]), "dcross_other", "ca_other")
+    step(
+        ["dq0", "dk0", "dv0"],
+        lambda: self_back(limit, q0, k0, v0, store["o0"], store["do0"], lse0),
+        "do0",
+    )
+    outs.over_y("outs1")
+    up.far()
+    down.second()
+    six = ("dq0", "dk0", "dv0", "dq1", "dk1", "dv1")
+    step(
+        ["yo"],
+        lambda: first_back(away, get(*six), w_qkv, qkv_first, qkv_second, ROUND),
+        "dq0",
+    )
+    store["yo_fly"] = over_core(store["yo"])
+    step(["qkv0"], lambda: qkv_grad(place, h1, get("dq0", "dk0", "dv0"), ROUND), "dq0")
+    qkv.first("qkv0")
+    step(["into0"], lambda: into(0), "dcq")
+    cross_in.first("into0")
+    down.far()
+    up.back()
+    step(["outs0"], lambda: outof(0, store["o0"]), "dcross")
     qkv.second()
-    norms = Row(sums + first_sums, over_core)
+    outs.first("outs0")
+    cross_in.second()
+    step(
+        ["ym"],
+        lambda: first_back(place, get(*six), w_qkv, qkv_first, qkv_second, FULL),
+        "dq0",
+    )
+    down.back()
+    qkv.far()
+    up.along()
+    outs.second()
+    cross_in.far()
+    down.along()
+    step(
+        ["grad_frames", "first_sums"],
+        lambda: frames_back(place, *get("ym", "yo_fly", "dx1"), frames, norm_gain),
+        "ym",
+        "yo_fly",
+    )
+    norms = Row("norms", store["sums"] + store["first_sums"], over_core)
+    qkv.back()
+    outs.far()
+    norms.then(over_y)
+    up.end("grad_up")
+    norms.then(lambda v: along_wide(v, X_PAIRS))
+    cross_in.back()
+    order("pair")
     text_part = 0.0
     for g, weights in ((0, w_cross_kv), (1, cross_kv_y)):
         for c in range(2):
-            text_part = text_part + nt(d_pair[g, c], weights[c])
-    texts = Row(text_part, over_core)
-    out_rows = lower(x2 + out_m + over_core(out_o).astype(FULL))
-    (out_rows,) = sync([outs, cross_in, qkv, norms, texts], out_rows)
-
-    outs.first(outof0)
-    cross_in.second()
-    qkv.far()
-    norms.then(over_y)
-    text_grad = lower(texts.kept + texts.fly)
-    text_away = over_y(text_grad)
-    grad_up = up_total.astype(FULL)
-    text_away, grad_up = sync([outs, cross_in, qkv, norms], text_away, grad_up)
-
-    outs.second()
-    cross_in.far()
-    qkv.back()
-    norms.then(lambda v: along_wide(v, X_PAIRS))
-    grad_text = ordered(text_grad[None], text_away[None], side)
-    (grad_text,) = sync([outs, cross_in, qkv, norms], grad_text)
-
-    outs.far()
-    cross_in.back()
-    qkv.along()
+            text_part = text_part + nt(store["pair"][g, c], weights[c])
+    texts = Row("texts", text_part, over_core)
     norms.then(lambda v: along_wide(v, Z_NEAR))
-    sync([outs, cross_in, norms])
-
+    store["out_fly"] = over_core(out_o)
     outs.back()
     cross_in.along()
     norms.then(lambda v: along_wide(v, Z_FAR))
-    sync([outs, qkv])
-
+    order("texts_fly", "texts_kept")
+    text_grad = lower(texts.total())
+    text_away = over_y(text_grad)
+    down.end("grad_down")
+    order("out_fly", "x2")
+    out_rows = lower(store["x2"] + out_m + store["out_fly"].astype(FULL))
+    qkv.along()
     outs.along()
-    grad_qkv = qkv.end().reshape(3, width, 256)
-    (grad_qkv,) = sync([cross_in, norms], grad_qkv)
-    sums = norms.kept + norms.fly
-    grad_cross_in = cross_in.end()
-    grad_outs = outs.end()
+    grad_text = ordered(text_grad[None], text_away[None], side)
+    cross_in.end("grad_in")
+    sums = norms.total()
+    qkv.end("grad_qkv")
+    outs.end("grad_outs")
+    grad_in, grad_outs = get("grad_in", "grad_outs")
     return (
         out_rows,
-        grad_frames,
+        store["grad_frames"],
         grad_text,
         sums[0:6:2],
         sums[1:6:2],
-        grad_qkv,
+        store["grad_qkv"].reshape(3, width, 256),
         grad_outs[:256],
-        grad_cross_in[:width],
-        grad_cross_in[width:].reshape(2, width, 256),
+        grad_in[:width],
+        grad_in[width:].reshape(2, width, 256),
         grad_outs[256:],
-        grad_up,
-        down_total.astype(FULL),
+        store["grad_up"],
+        store["grad_down"],
     )
 
 

time: 633 us -> 554 us (0.88)
  waiting for transfers between devices: 193 us -> 123 us
  between operations: 15.9 us -> 2.69 us
  Pallas kernels: 264 us -> 253 us
  starting transfers between devices: 44.4 us -> 51.8 us
  other arithmetic: 56.2 us -> 62.7 us
    psum x2 -> x0, waiting for transfers between devices: 81.7 us -> none  [the longest x1 48.6 us: chip_local(): down_total = lax.psum(lower(down0 + received.astype(FULL)), 'wide')]
    ppermute x23 -> x33, waiting for transfers between devices: 92.7 us -> 104 us  [along_wide(): return lax.ppermute(v, 'wide', pairs)]
    ppermute x23 -> x33, starting transfers between devices: 23.7 us -> 34.6 us  [along_wide(): return lax.ppermute(v, 'wide', pairs)]
    add x9 -> x12, other arithmetic: 4.47 us -> 12 us  [the longest x5 7.69 us: second(): total = store[self.kept] + store[self.fly].astype(FULL)]
    unnamed x222 -> x198, local copies, waits for them, and re-layouts: 24 us -> 16.5 us
    pallas_call x3 -> x2, Pallas kernels: 18 us -> 14.8 us  [down_grad(): pl.pallas_call(down_grad_kernel, grid=(hidden // tile,), in_specs=[pl.Blo...]
    ppermute x13 -> x12, starting transfers between devices: 16.3 us -> 13.7 us  [over_y(): return lax.ppermute(v, 'narrow', Y_PAIRS)]
    ppermute x13 -> x12, waiting for transfers between devices: 16.9 us -> 18 us  [over_y(): return lax.ppermute(v, 'narrow', Y_PAIRS)]
  transfers between devices with their start and end apart: 59 -> 66, of which waited for: 16 -> 19; matrix products, arithmetic and copies ran while one was open for 13% -> 17% of each run, Pallas kernels for 40% -> 44%
where the time goes in v7:
time: 554 us; the launch traced here: 544 us
  Pallas kernels  253 us (46%)
  waiting for transfers between devices  123 us (22%)
  other arithmetic  62.7 us (11%)
  starting transfers between devices  51.8 us (9%)
  local copies, waits for them, and re-layouts  48.5 us (9%)
    ppermute x33, waiting for transfers between devices, along_wide(): return lax.ppermute(v, 'wide', pairs)  104 us
    pallas_call x4, Pallas kernels, feed(): pl.pallas_call(functools.partial(feed_kernel, parts=parts, carried=len(be...  51.6 us
    pallas_call x2, Pallas kernels, self_back(): pl.pallas_call(functools.partial(self_back_kernel, span=span, floor=floor...  40 us
    ppermute x33, starting transfers between devices, along_wide(): return lax.ppermute(v, 'wide', pairs)  34.6 us
    pallas_call x2, Pallas kernels, self_forward(): pl.pallas_call(functools.partial(self_forward_kernel, span=span, floor=fl...  28.7 us
    pallas_call x1, Pallas kernels, middle_back(): pl.pallas_call(middle_back_kernel, grid_spec=pltpu.PrefetchScalarGridSpec...  23.2 us
    convert_element_type x17, other arithmetic, lower(): return values_in.astype(jnp.bfloat16)  22.8 us
    pallas_call x1, Pallas kernels, middle_forward(): pl.pallas_call(middle_forward_kernel, grid_spec=pltpu.PrefetchScalarGridS...  21.2 us
  transfers between devices with their start and end apart: 66, of which 19 were waited for; matrix products, arithmetic and copies ran while one was open for 17% of the time, Pallas kernels for 44%

profile of v7, /device:TPU:0, one launch (start us, length us, event | category | flops | bytes accessed | tf_op | source)
XLA Modules:
  0.0 543.5 jit_solution(7712255291831412118)
XLA Ops:
  2.4 2.6 collective-permute-start.1
  5.0 2.4 pad_maximum_fusion.1
  8.6 3.0 pad_maximum_fusion
  11.7 6.2 %first_project.1 = (bf16[1664,1024]{1,0:T(8,128)(2,1)S(1)}, bf16[1664,256]{1,0:T(8,128)(2,1)S(1)}, bf16[1664,256]{1,0:T(8,128)(2,1)S(1)}, bf16[1664,256]{1,0:T(8,128)(2,1)S(1)}) custom-call(s32[2]{0:T(128)S(1)} %pad_add_fusion.place_ref, bf16[832,1024]{1,0:T(8,128)(2,1)S(1)} %copy-done.13, bf16[832,1024]{1,0:T(8,128)(2,1)} %collective-permute-done.other_ref, ...), custom_call_target="tpu_custom_call" | custom-call | flops 1000 | bytes 1000 | tf_op jit(solution)/shard_map/first_project/pallas_call | solution.py:392
  32.2 14.5 %self_forward.2 = (bf16[1664,256]{1,0:T(8,128)(2,1)}, f32[2,8,1664]{2,1,0:T(8,128)}) custom-call(s32[1]{0:T(128)} %dynamic_slice.117.limit_ref, bf16[1664,256]{1,0:T(8,128)(2,1)} %copy-done.41, bf16[1664,256]{1,0:T(8,128)(2,1)} %copy-done.43, bf16[1664,256]{1,0:T(8,128)(2,1)} %copy-done.45), custom_call_target="tpu_custom_call" | custom-call | flops 1000 | bytes 1000 | tf_op jit(solution)/shard_map/self_forward/pallas_call | solution.py:522
  49.2 3.6 project.1
  56.7 4.4 collective-permute-done.3
  65.1 14.2 %self_forward.3 = (bf16[1664,256]{1,0:T(8,128)(2,1)}, f32[2,8,1664]{2,1,0:T(8,128)}) custom-call(s32[1]{0:T(128)} %dynamic_slice.117.limit_ref, bf16[1664,256]{1,0:T(8,128)(2,1)} %copy-done.47, bf16[1664,256]{1,0:T(8,128)(2,1)} %copy-done.49, bf16[1664,256]{1,0:T(8,128)(2,1)} %copy-done.51), custom_call_target="tpu_custom_call" | custom-call | flops 1000 | bytes 1000 | tf_op jit(solution)/shard_map/self_forward/pallas_call | solution.py:522
  80.4 2.2 fusion.37
  84.7 2.3 maximum_select_fusion.2
  93.9 21.2 %middle_forward.1 = (f32[832,1024]{1,0:T(8,128)}, f32[832,1024]{1,0:T(8,128)}, bf16[832,1024]{1,0:T(8,128)(2,1)}, bf16[832,1024]{1,0:T(8,128)(2,1)}, bf16[832,10...) custom-call(s32[2]{0:T(128)} %copy-done.60, bf16[832,1024]{1,0:T(8,128)(2,1)} %frame_ref.3, ...), custom_call_target="tpu_custom_call" | custom-call | flops 1000 | bytes 1000 | tf_op jit(solution)/shard_map/middle_forward/pallas_call | solution.py:671
  117.6 12.1 %feed.4 = (bf16[1664,1024]{1,0:T(8,128)(2,1)}, bf16[1664,1024]{1,0:T(8,128)(2,1)}, f32[832,1024]{1,0:T(8,128)}, f32[832,1024]{1,0:T(8,128)}) custom-call(s32[2]{0:T(128)} %copy-done.60, bf16[832,1024]{1,0:T(8,128)(2,1)} %get-tuple-element.275.h_ref.mine_ref, bf16[832,1024]{1,0:T(8,128)(2,1)} %copy-done.2, bf16[1024,1024]{1,0:T(8,128)(2,1)} %refs_0_.4, ...), custom_call_target="tpu_custom_call" | custom-call | flops 1000 | bytes 1000 | tf_op jit(solution)/shard_map/feed/pallas_call | solution.py:728
  131.0 12.2 %feed.5 = (bf16[1664,1024]{1,0:T(8,128)(2,1)}, bf16[1664,1024]{1,0:T(8,128)(2,1)}, f32[832,1024]{1,0:T(8,128)}, f32[832,1024]{1,0:T(8,128)}) custom-call(s32[2]{0:T(128)} %copy-done.60, bf16[832,1024]{1,0:T(8,128)(2,1)} %copy-done.8, bf16[832,1024]{1,0:T(8,128)(2,1)} %collective-permute-done.10.d_ref.other_ref, ...), custom_call_target="tpu_custom_call", output_to_operand_aliasing={{0}: (5, {}), {1}: (6, {})} | custom-call | flops 1000 | bytes 1000 | tf_op jit(solution)/shard_map/feed/pallas_call | solution.py:728
  143.2 20.2 %collective-permute-done.19.refs_3_ = bf16[512,1024]{1,0:T(8,128)(2,1)} collective-permute-done((bf16[512,1024]{1,0:T(8,128)(2,1)S(1)}, bf16[512,1024]{1,0:T(8,128)(2,1)}, u32[]{:S(2)}, u32[]{:S(2)}) %collective-permute-start.19) | collective-permute-done | bytes 1048608 | tf_op jit(solution)/shard_map/ppermute | solution.py:1062
  163.4 13.6 %feed.6 = (bf16[1664,1024]{1,0:T(8,128)(2,1)}, bf16[1664,1024]{1,0:T(8,128)(2,1)}, bf16[832,1024]{1,0:T(8,128)(2,1)}, bf16[832,1024]{1,0:T(8,128)(2,1)}) custom-call(s32[2]{0:T(128)} %copy-done.60, bf16[832,1024]{1,0:T(8,128)(2,1)} %copy-done.8, bf16[832,1024]{1,0:T(8,128)(2,1)} %collective-permute-done.10.d_ref.other_ref, bf16[1024,512]{1,0:T(8,128)(2,1)} %copy-done.76, ...), custom_call_target="tpu_custom_call" | custom-call | flops 1000 | bytes 1000 | tf_op jit(solution)/shard_map/feed/pallas_call | solution.py:728
  177.0 13.8 %feed.7 = (bf16[1664,1024]{1,0:T(8,128)(2,1)}, bf16[1664,1024]{1,0:T(8,128)(2,1)}, f32[832,1024]{1,0:T(8,128)}, f32[832,1024]{1,0:T(8,128)}) custom-call(s32[2]{0:T(128)} %copy-done.60, bf16[832,1024]{1,0:T(8,128)(2,1)} %get-tuple-element.275.h_ref.mine_ref, bf16[832,1024]{1,0:T(8,128)(2,1)} %copy-done.2, ...), custom_call_target="tpu_custom_call", output_to_operand_aliasing={{0}: (9, {}), {1}: (10, {})} | custom-call | flops 1000 | bytes 1000 | tf_op jit(solution)/shard_map/feed/pallas_call | solution.py:728
  190.7 6.5 %up_grad.2 = bf16[1024,1024]{1,0:T(8,128)(2,1)S(1)} custom-call(bf16[832,1024]{1,0:T(8,128)(2,1)S(1)} %copy-done.7, bf16[832,1024]{1,0:T(8,128)(2,1)S(1)} %copy-done.9, bf16[1664,1024]{1,0:T(8,128)(2,1)} %get-tuple-element.299.du_ref), custom_call_target="tpu_custom_call" | custom-call | flops 1000 | bytes 1000 | tf_op jit(solution)/shard_map/up_grad/pallas_call | solution.py:758
  198.0 7.7 %down_grad.2 = bf16[1024,1024]{1,0:T(8,128)(2,1)} custom-call(bf16[1664,1024]{1,0:T(8,128)(2,1)} %get-tuple-element.300.g_ref, bf16[832,1024]{1,0:T(8,128)(2,1)S(1)} %copy-done.3, bf16[832,1024]{1,0:T(8,128)(2,1)} %collective-permute-done.10.d_ref.other_ref), custom_call_target="tpu_custom_call" | custom-call | flops 1000 | bytes 1000 | tf_op jit(solution)/shard_map/down_grad/pallas_call | solution.py:781
  205.7 23.2 %middle_back.1 = (f32[832,1024]{1,0:T(8,128)}, bf16[832,1024]{1,0:T(8,128)(2,1)}, bf16[832,1024]{1,0:T(8,128)(2,1)}, bf16[832,1024]{1,0:T(8,128)(2,1)}, f32[4,64...) custom-call(s32[2]{0:T(128)} %copy-done.60, f32[832,1024]{1,0:T(8,128)} %get-tuple-element.303.ym_ref, ...), custom_call_target="tpu_custom_call" | custom-call | flops 1000 | bytes 1000 | tf_op jit(solution)/shard_map/middle_back/pallas_call | solution.py:948
  230.8 2.1 slice.117
  232.9 12.8 %collective-permute-done.23 = bf16[1024,1024]{1,0:T(8,128)(2,1)S(1)} collective-permute-done((bf16[1024,1024]{1,0:T(8,128)(2,1)S(1)}, bf16[1024,1024]{1,0:T(8,128)(2,1)S(1)}, u32[]{:S(2)}, u32[]{:S(2)}) %collective-permute-start.23) | collective-permute-done | bytes 2097184 | tf_op jit(solution)/shard_map/ppermute | solution.py:1059
  245.7 2.5 pad_maximum_fusion.2
  249.5 6.5 %up_grad.3 = bf16[1024,1024]{1,0:T(8,128)(2,1)S(1)} custom-call(bf16[832,1024]{1,0:T(8,128)(2,1)S(1)} %copy-done.7, bf16[832,1024]{1,0:T(8,128)(2,1)S(1)} %copy-done.10, bf16[1664,1024]{1,0:T(8,128)(2,1)} %get-tuple-element.309.du_ref), custom_call_target="tpu_custom_call" | custom-call | flops 1000 | bytes 1000 | tf_op jit(solution)/shard_map/up_grad/pallas_call | solution.py:758
  256.1 2.8 pull.1
  260.7 20.1 %self_back.2 = (bf16[1664,256]{1,0:T(8,128)(2,1)S(1)}, bf16[1664,256]{1,0:T(8,128)(2,1)S(1)}, bf16[1664,256]{1,0:T(8,128)(2,1)S(1)}) custom-call(s32[1]{0:T(128)} %dynamic_slice.117.limit_ref, bf16[1664,256]{1,0:T(8,128)(2,1)S(1)} %copy-done.48, bf16[1664,256]{1,0:T(8,128)(2,1)S(1)} %copy-done.50, bf16[1664,256]{1,0:T(8,128)(2,1)S(1)} %copy-done.52, ...), custom_call_target="tpu_custom_call" | custom-call | flops 1000 | bytes 1000 | tf_op jit(solution)/shard_map/self_back/pallas_call | solution.py:603
  280.8 2.6 add_convert_fusion.1
  284.0 2.1 slice.121
  286.2 7.2 %down_grad.3 = bf16[1024,1024]{1,0:T(8,128)(2,1)S(1)} custom-call(bf16[1664,1024]{1,0:T(8,128)(2,1)} %get-tuple-element.320.g_ref, bf16[832,1024]{1,0:T(8,128)(2,1)S(1)} %copy-done.4, bf16[832,1024]{1,0:T(8,128)(2,1)} %collective-permute-done.10.d_ref.other_ref), custom_call_target="tpu_custom_call" | custom-call | flops 1000 | bytes 1000 | tf_op jit(solution)/shard_map/down_grad/pallas_call | solution.py:781
  293.4 7.1 %qkv_grad.2 = bf16[3072,256]{1,0:T(8,128)(2,1)} custom-call(s32[2]{0:T(128)S(1)} %copy-done.62, bf16[1664,1024]{1,0:T(8,128)(2,1)} %copy-done.5, bf16[1664,256]{1,0:T(8,128)(2,1)S(1)} %get-tuple-element.327.refs_0_.refs_3_, bf16[1664,256]{1,0:T(8,128)(2,1)S(1)} %get-tuple-element.328.refs_1_.refs_4_, bf16[1664,256]{1,0:T(8,128)(2,1)S(1)} %copy-done.28), custom_call_target="tpu_custom_call" | custom-call | flops 1000 | bytes 1000 | tf_op jit(solution)/shard_map/qkv_grad/pallas_call | solution.py:810
  303.3 4.9 cross_in_grad.2
  308.2 4.3 convert_add_fusion.2
  313.8 3.1 convert_add_fusion.1
  316.9 2.2 dynamic-slice_convert_fusion.1
  323.6 6.5 %outputs_grad.2 = bf16[512,1024]{1,0:T(8,128)(2,1)} custom-call(s32[2]{0:T(128)S(1)} %copy-done.62, bf16[1664,256]{1,0:T(8,128)(2,1)S(1)} %copy-done.22, bf16[832,1024]{1,0:T(8,128)(2,1)S(1)} %copy-done.16, bf16[832,1024]{1,0:T(8,128)(2,1)S(1)} %copy-done.19, bf16[832,1024]{1,0:T(8,128)(2,1)} %get-tuple-element.343.am_ref, ...), custom_call_target="tpu_custom_call" | custom-call | flops 1000 | bytes 1000 | tf_op jit(solution)/shard_map/outputs_grad/pallas_call | solution.py:871
  330.1 19.9 %self_back.3 = (bf16[1664,256]{1,0:T(8,128)(2,1)S(1)}, bf16[1664,256]{1,0:T(8,128)(2,1)S(1)}, bf16[1664,256]{1,0:T(8,128)(2,1)S(1)}) custom-call(s32[1]{0:T(128)} %dynamic_slice.117.limit_ref, bf16[1664,256]{1,0:T(8,128)(2,1)S(1)} %copy-done.42, bf16[1664,256]{1,0:T(8,128)(2,1)S(1)} %copy-done.44, bf16[1664,256]{1,0:T(8,128)(2,1)S(1)} %copy-done.46, ...), custom_call_target="tpu_custom_call" | custom-call | flops 1000 | bytes 1000 | tf_op jit(solution)/shard_map/self_back/pallas_call | solution.py:603
  350.9 2.2 add_convert_fusion.9
  353.0 2.6 collective-permute-start.37
  360.6 4.9 first_back.2
  365.5 6.0 %qkv_grad.3 = bf16[3072,256]{1,0:T(8,128)(2,1)S(1)} custom-call(s32[2]{0:T(128)S(1)} %copy-done.62, bf16[1664,1024]{1,0:T(8,128)(2,1)} %copy-done.5, bf16[1664,256]{1,0:T(8,128)(2,1)S(1)} %get-tuple-element.385.refs_0_, bf16[1664,256]{1,0:T(8,128)(2,1)S(1)} %get-tuple-element.360.refs_1_, bf16[1664,256]{1,0:T(8,128)(2,1)S(1)} %get-tuple-element.361.refs_2_), custom_call_target="tpu_custom_call" | custom-call | flops 1000 | bytes 1000 | tf_op jit(solution)/shard_map/qkv_grad/pallas_call | solution.py:810
  371.5 2.1 dynamic-slice_convert_fusion
  374.0 3.2 add_convert_fusion.3
  377.2 3.7 cross_in_grad.3
  382.6 2.6 add_convert_fusion.4
  385.2 5.5 %collective-permute-done.33 = bf16[256,1024]{1,0:T(8,128)(2,1)} collective-permute-done((bf16[256,1024]{1,0:T(8,128)(2,1)}, bf16[256,1024]{1,0:T(8,128)(2,1)}, u32[]{:S(2)}, u32[]{:S(2)}) %collective-permute-start.33) | collective-permute-done | bytes 524320 | tf_op jit(solution)/shard_map/ppermute | solution.py:1062
  393.4 2.2 add_convert_fusion.7
  395.5 5.2 outputs_grad.3
  400.7 6.6 %collective-permute-done.40 = bf16[1536,256]{1,0:T(8,128)(2,1)S(1)} collective-permute-done((bf16[1536,256]{1,0:T(8,128)(2,1)}, bf16[1536,256]{1,0:T(8,128)(2,1)S(1)}, u32[]{:S(2)}, u32[]{:S(2)}) %collective-permute-start.40) | collective-permute-done | bytes 786464 | tf_op jit(solution)/shard_map/ppermute | solution.py:1062
  410.4 2.4 collective-permute-start.45
  416.6 3.8 first_back.3.ym_ref
  420.5 14.0 %collective-permute-done.36 = bf16[256,1024]{1,0:T(8,128)(2,1)S(1)} collective-permute-done((bf16[256,1024]{1,0:T(8,128)(2,1)}, bf16[256,1024]{1,0:T(8,128)(2,1)S(1)}, u32[]{:S(2)}, u32[]{:S(2)}) %collective-permute-start.36) | collective-permute-done | bytes 524320 | tf_op jit(solution)/shard_map/ppermute | solution.py:1062
  439.3 9.1 %collective-permute-done.44 = bf16[256,1024]{1,0:T(8,128)(2,1)S(1)} collective-permute-done((bf16[256,1024]{1,0:T(8,128)(2,1)S(1)}, bf16[256,1024]{1,0:T(8,128)(2,1)S(1)}, u32[]{:S(2)}, u32[]{:S(2)}) %collective-permute-start.44) | collective-permute-done | bytes 524320 | tf_op jit(solution)/shard_map/ppermute | solution.py:1062
  449.6 15.7 %collective-permute-done.41 = bf16[256,1024]{1,0:T(8,128)(2,1)S(1)} collective-permute-done((bf16[256,1024]{1,0:T(8,128)(2,1)S(1)}, bf16[256,1024]{1,0:T(8,128)(2,1)S(1)}, u32[]{:S(2)}, u32[]{:S(2)}) %collective-permute-start.41) | collective-permute-done | bytes 524320 | tf_op jit(solution)/shard_map/ppermute | solution.py:1062
  465.8 2.8 collective-permute-start.48
  468.6 6.0 %frames_back.1 = (bf16[832,1024]{1,0:T(8,128)(2,1)}, f32[8,1024]{1,0:T(8,128)S(1)}) custom-call(s32[2]{0:T(128)S(1)} %copy-done.62, f32[832,1024]{1,0:T(8,128)S(1)} %first_back.3.ym_ref, bf16[832,1024]{1,0:T(8,128)(2,1)} %collective-permute-done.47.yr_ref, f32[832,1024]{1,0:T(8,128)S(1)} %copy-done.40, bf16[832,1024]{1,0:T(8,128)(2,1)S(1)} %copy-done.14, ...), custom_call_target="tpu_custom_call" | custom-call | flops 1000 | bytes 1000 | tf_op jit(solution)/shard_map/frames_back/pallas_call | solution.py:1024
  480.3 2.9 fusion
  484.7 8.2 %collective-permute-done.48 = bf16[768,256]{1,0:T(8,128)(2,1)S(1)} collective-permute-done((bf16[768,256]{1,0:T(8,128)(2,1)S(1)}, bf16[768,256]{1,0:T(8,128)(2,1)S(1)}, u32[]{:S(2)}, u32[]{:S(2)}) %collective-permute-start.48) | collective-permute-done | bytes 393248 | tf_op jit(solution)/shard_map/ppermute | solution.py:1062
  494.2 4.4 collective-permute-done.55
  500.2 5.0 collective-permute-done.58
  505.5 3.6 collective-permute-done.56
  509.1 2.2 collective-permute-start.60
  512.8 3.0 fusion.1
  518.9 3.8 add_convert_fusion
  524.7 7.2 %collective-permute-done.64 = bf16[1536,256]{1,0:T(8,128)(2,1)S(1)} collective-permute-done((bf16[1536,256]{1,0:T(8,128)(2,1)S(1)}, bf16[1536,256]{1,0:T(8,128)(2,1)S(1)}, u32[]{:S(2)}, u32[]{:S(2)}) %collective-permute-start.64) | collective-permute-done | bytes 786464 | tf_op jit(solution)/shard_map/ppermute | solution.py:1062
  536.4 3.4 fusion.3
  (388 shorter events, 104.2 us)
Async XLA Ops:
  0.7 11.0 %collective-permute-start = (bf16[832,1024]{1,0:T(8,128)(2,1)}, bf16[832,1024]{1,0:T(8,128)(2,1)}, u32[]{:S(2)}, u32[]{:S(2)}) collective-permute-start(bf16[832,1024]{1,0:T(8,128)(2,1)} %frame_ref.3), channel_id=1, source_target_pairs={{0,1},{1,0},{2,3},{3,2},{4,5},{5,4},{6,7},{7,6},{8,9},{9,8},{10,11... | collective-permute-start | bytes 5111816 | tf_op jit(solution)/shard_map/ppermute | solution.py:1056
  2.4 20.8 %collective-permute-start.1 = (bf16[3,512,256]{2,1,0:T(8,128)(2,1)S(1)}, bf16[3,512,256]{2,1,0:T(8,128)(2,1)S(1)}, u32[]{:S(2)}, u32[]{:S(2)}) collective-permute-start(bf16[3,512,256]{2,1,0:T(8,128)(2,1)S(1)} %constant_dynamic-slice_fusion.11), channel_id=1, source_target_pairs={{0,2},{2,0},{1,3},{3,1},{4,6},{6,4},{5,7},{7,5},{8,10},{10,8},{9,1... | collective-permute-start | bytes 2359304 | tf_op jit(solution)/shard_map/ppermute | solution.py:1059
  23.2 23.5 %collective-permute-start.2 = (bf16[3,512,256]{2,1,0:T(8,128)(2,1)S(1)}, bf16[3,512,256]{2,1,0:T(8,128)(2,1)S(1)}, u32[]{:S(2)}, u32[]{:S(2)}) collective-permute-start(bf16[3,512,256]{2,1,0:T(8,128)(2,1)S(1)} %collective-permute-done.1.first_ref.refs_7_), channel_id=1, source_target_pairs={{0,8},{4,12},{8,0},{12,4},{16,24},{20,28},{24,16},{28,20},{1,9},{5... | collective-permute-start | bytes 2359304 | tf_op jit(solution)/shard_map/ppermute | solution.py:1062
  25.0 23.3 %collective-permute-start.7 = (bf16[1024,256]{1,0:T(8,128)(2,1)}, bf16[1024,256]{1,0:T(8,128)(2,1)}, u32[]{:S(2)}, u32[]{:S(2)}) collective-permute-start(bf16[1024,256]{1,0:T(8,128)(2,1)} %refs_0_.5), channel_id=1, source_target_pairs={{0,1},{1,0},{2,3},{3,2},{4,5},{5,4},{6,7},{7,6},{8,9},{9,8},{10,11... | collective-permute-start | bytes 1572872 | tf_op jit(solution)/shard_map/ppermute | solution.py:1056
  26.2 34.9 %collective-permute-start.6 = (bf16[512,1024]{1,0:T(8,128)(2,1)}, bf16[512,1024]{1,0:T(8,128)(2,1)}, u32[]{:S(2)}, u32[]{:S(2)}) collective-permute-start(bf16[512,1024]{1,0:T(8,128)(2,1)} %pad_maximum_fusion.1), channel_id=1, source_target_pairs={{0,1},{1,0},{2,3},{3,2},{4,5},{5,4},{6,7},{7,6},{8,9},{9,8},{10,11... | collective-permute-start | bytes 3145736 | tf_op jit(solution)/shard_map/ppermute | solution.py:1056
  26.7 55.9 %collective-permute-start.10 = (bf16[832,1024]{1,0:T(8,128)(2,1)S(1)}, bf16[832,1024]{1,0:T(8,128)(2,1)}, u32[]{:S(2)}, u32[]{:S(2)}) collective-permute-start(bf16[832,1024]{1,0:T(8,128)(2,1)S(1)} %broadcast_select_fusion.d_ref.mine_ref), channel_id=1, source_target_pairs={{0,1},{1,0},{2,3},{3,2},{4,5},{5,4},{6,7},{7,6},{8,9},{9,8},{10,11... | collective-permute-start | bytes 5111816 | tf_op jit(solution)/shard_map/ppermute | solution.py:1056
  28.8 32.3 %collective-permute-start.4 = (bf16[1536,256]{1,0:T(8,128)(2,1)}, bf16[1536,256]{1,0:T(8,128)(2,1)}, u32[]{:S(2)}, u32[]{:S(2)}) collective-permute-start(bf16[1536,256]{1,0:T(8,128)(2,1)} %constant_dynamic-slice_fusion.9), channel_id=1, source_target_pairs={{0,2},{2,0},{1,3},{3,1},{4,6},{6,4},{5,7},{7,5},{8,10},{10,8},{9,1... | collective-permute-start | bytes 2359304 | tf_op jit(solution)/shard_map/ppermute | solution.py:1059
  46.7 14.4 %collective-permute-start.3 = (bf16[256,1024]{1,0:T(8,128)(2,1)}, bf16[256,1024]{1,0:T(8,128)(2,1)}, u32[]{:S(2)}, u32[]{:S(2)}) collective-permute-start(bf16[256,1024]{1,0:T(8,128)(2,1)} %constant_dynamic-slice_fusion.10), channel_id=1, source_target_pairs={{0,2},{2,0},{1,3},{3,1},{4,6},{6,4},{5,7},{7,5},{8,10},{10,8},{9,1... | collective-permute-start | bytes 1572872 | tf_op jit(solution)/shard_map/ppermute | solution.py:1059
  48.3 12.8 %collective-permute-start.5 = (bf16[832,256]{1,0:T(8,128)(2,1)S(1)}, bf16[832,256]{1,0:T(8,128)(2,1)S(1)}, u32[]{:S(2)}, u32[]{:S(2)}) collective-permute-start(bf16[832,256]{1,0:T(8,128)(2,1)S(1)} %constant_dynamic-slice_fusion.6), channel_id=1, source_target_pairs={{0,1},{1,0},{2,3},{3,2},{4,5},{5,4},{6,7},{7,6},{8,9},{9,8},{10,11... | collective-permute-start | bytes 1277960 | tf_op jit(solution)/shard_map/ppermute | solution.py:1056
  61.9 20.8 %collective-permute-start.9 = (bf16[1536,256]{1,0:T(8,128)(2,1)}, bf16[1536,256]{1,0:T(8,128)(2,1)}, u32[]{:S(2)}, u32[]{:S(2)}) collective-permute-start(bf16[1536,256]{1,0:T(8,128)(2,1)} %collective-permute-done.4), channel_id=1, source_target_pairs={{0,8},{4,12},{8,0},{12,4},{16,24},{20,28},{24,16},{28,20},{1,9},{5... | collective-permute-start | bytes 2359304 | tf_op jit(solution)/shard_map/ppermute | solution.py:1062
  62.5 20.1 %collective-permute-start.8 = (bf16[256,1024]{1,0:T(8,128)(2,1)}, bf16[256,1024]{1,0:T(8,128)(2,1)}, u32[]{:S(2)}, u32[]{:S(2)}) collective-permute-start(bf16[256,1024]{1,0:T(8,128)(2,1)} %collective-permute-done.3), channel_id=1, source_target_pairs={{0,4},{4,0},{8,12},{12,8},{16,20},{20,16},{24,28},{28,24},{1,5},{5... | collective-permute-start | bytes 1572872 | tf_op jit(solution)/shard_map/ppermute | solution.py:1062
  64.3 50.8 %collective-permute-start.15 = (bf16[1024,512]{1,0:T(8,128)(2,1)}, bf16[1024,512]{1,0:T(8,128)(2,1)S(1)}, u32[]{:S(2)}, u32[]{:S(2)}) collective-permute-start(bf16[1024,512]{1,0:T(8,128)(2,1)} %constant_dynamic-slice_fusion.8), channel_id=1, source_target_pairs={{0,2},{2,0},{1,3},{3,1},{4,6},{6,4},{5,7},{7,5},{8,10},{10,8},{9,1... | collective-permute-start | bytes 3145736 | tf_op jit(solution)/shard_map/ppermute | solution.py:1059
  84.6 7.3 %collective-permute-start.12 = (bf16[512,1024]{1,0:T(8,128)(2,1)S(1)}, bf16[512,1024]{1,0:T(8,128)(2,1)S(1)}, u32[]{:S(2)}, u32[]{:S(2)}) collective-permute-start(bf16[512,1024]{1,0:T(8,128)(2,1)S(1)} %maximum_select_fusion.5), channel_id=1, source_target_pairs={{0,1},{1,0},{2,3},{3,2},{4,5},{5,4},{6,7},{7,6},{8,9},{9,8},{10,11... | collective-permute-start | bytes 3145736 | tf_op jit(solution)/shard_map/ppermute | solution.py:1056
  87.3 27.9 %collective-permute-start.16 = (bf16[512,1024]{1,0:T(8,128)(2,1)S(1)}, bf16[512,1024]{1,0:T(8,128)(2,1)S(1)}, u32[]{:S(2)}, u32[]{:S(2)}) collective-permute-start(bf16[512,1024]{1,0:T(8,128)(2,1)S(1)} %copy-done.91), channel_id=1, source_target_pairs={{0,2},{2,0},{1,3},{3,1},{4,6},{6,4},{5,7},{7,5},{8,10},{10,8},{9,1... | collective-permute-start | bytes 3145736 | tf_op jit(solution)/shard_map/ppermute | solution.py:1059
  90.2 2.8 collective-permute-start.13
  90.6 2.3 collective-permute-start.11
  115.2 14.6 %collective-permute-start.17 = (bf16[832,1024]{1,0:T(8,128)(2,1)}, bf16[832,1024]{1,0:T(8,128)(2,1)S(1)}, u32[]{:S(2)}, u32[]{:S(2)}) collective-permute-start(bf16[832,1024]{1,0:T(8,128)(2,1)} %get-tuple-element.275.h_ref.mine_ref), channel_id=1, source_target_pairs={{0,1},{1,0},{2,3},{3,2},{4,5},{5,4},{6,7},{7,6},{8,9},{9,8},{10,11... | collective-permute-start | bytes 5111816 | tf_op jit(solution)/shard_map/ppermute | solution.py:1056
  115.6 27.6 %collective-permute-start.18 = (bf16[1024,512]{1,0:T(8,128)(2,1)S(1)}, bf16[1024,512]{1,0:T(8,128)(2,1)S(1)}, u32[]{:S(2)}, u32[]{:S(2)}) collective-permute-start(bf16[1024,512]{1,0:T(8,128)(2,1)S(1)} %collective-permute-done.15.refs_0_), channel_id=1, source_target_pairs={{0,8},{4,12},{8,0},{12,4},{16,24},{20,28},{24,16},{28,20},{1,9},{5... | collective-permute-start | bytes 3145736 | tf_op jit(solution)/shard_map/ppermute | solution.py:1062
  117.1 46.2 %collective-permute-start.19 = (bf16[512,1024]{1,0:T(8,128)(2,1)S(1)}, bf16[512,1024]{1,0:T(8,128)(2,1)}, u32[]{:S(2)}, u32[]{:S(2)}) collective-permute-start(bf16[512,1024]{1,0:T(8,128)(2,1)S(1)} %collective-permute-done.16.refs_2_), channel_id=1, source_target_pairs={{0,8},{4,12},{8,0},{12,4},{16,24},{20,28},{24,16},{28,20},{1,9},{5... | collective-permute-start | bytes 3145736 | tf_op jit(solution)/shard_map/ppermute | solution.py:1062
  176.9 28.8 %collective-permute-start.21 = (bf16[832,1024]{1,0:T(8,128)(2,1)}, bf16[832,1024]{1,0:T(8,128)(2,1)}, u32[]{:S(2)}, u32[]{:S(2)}) collective-permute-start(bf16[832,1024]{1,0:T(8,128)(2,1)} %get-tuple-element.289), channel_id=1, source_target_pairs={{0,1},{1,0},{2,3},{3,2},{4,5},{5,4},{6,7},{7,6},{8,9},{9,8},{10,11... | collective-permute-start | bytes 5111816 | tf_op jit(solution)/shard_map/ppermute | solution.py:1056
  197.2 48.5 %collective-permute-start.23 = (bf16[1024,1024]{1,0:T(8,128)(2,1)S(1)}, bf16[1024,1024]{1,0:T(8,128)(2,1)S(1)}, u32[]{:S(2)}, u32[]{:S(2)}) collective-permute-start(bf16[1024,1024]{1,0:T(8,128)(2,1)S(1)} %up_grad.2), channel_id=1, source_target_pairs={{0,2},{2,0},{1,3},{3,1},{4,6},{6,4},{5,7},{7,5},{8,10},{10,8},{9,1... | collective-permute-start | bytes 6291464 | tf_op jit(solution)/shard_map/ppermute | solution.py:1059
  228.9 19.3 %collective-permute-start.24 = (bf16[832,1024]{1,0:T(8,128)(2,1)}, bf16[832,1024]{1,0:T(8,128)(2,1)S(1)}, u32[]{:S(2)}, u32[]{:S(2)}) collective-permute-start(bf16[832,1024]{1,0:T(8,128)(2,1)} %get-tuple-element.311.mine_ref.sm_ref), channel_id=1, source_target_pairs={{0,1},{1,0},{2,3},{3,2},{4,5},{5,4},{6,7},{7,6},{8,9},{9,8},{10,11... | collective-permute-start | bytes 5111816 | tf_op jit(solution)/shard_map/ppermute | solution.py:1056
  229.2 71.7 %collective-permute-start.25 = (bf16[832,1024]{1,0:T(8,128)(2,1)}, bf16[832,1024]{1,0:T(8,128)(2,1)}, u32[]{:S(2)}, u32[]{:S(2)}) collective-permute-start(bf16[832,1024]{1,0:T(8,128)(2,1)} %get-tuple-element.377.cm_ref), channel_id=1, source_target_pairs={{0,1},{1,0},{2,3},{3,2},{4,5},{5,4},{6,7},{7,6},{8,9},{9,8},{10,11... | collective-permute-start | bytes 5111816 | tf_op jit(solution)/shard_map/ppermute | solution.py:1056
  229.5 78.7 %collective-permute-start.22 = (bf16[1024,1024]{1,0:T(8,128)(2,1)}, bf16[1024,1024]{1,0:T(8,128)(2,1)}, u32[]{:S(2)}, u32[]{:S(2)}) collective-permute-start(bf16[1024,1024]{1,0:T(8,128)(2,1)} %down_grad.2), channel_id=1, source_target_pairs={{0,2},{2,0},{1,3},{3,1},{4,6},{6,4},{5,7},{7,5},{8,10},{10,8},{9,1... | collective-permute-start | bytes 6291464 | tf_op jit(solution)/shard_map/ppermute | solution.py:1059
  230.8 71.8 %collective-permute-start.28 = (bf16[832,1024]{1,0:T(8,128)(2,1)}, bf16[832,1024]{1,0:T(8,128)(2,1)}, u32[]{:S(2)}, u32[]{:S(2)}) collective-permute-start(bf16[832,1024]{1,0:T(8,128)(2,1)} %get-tuple-element.322.mine_ref), channel_id=1, source_target_pairs={{0,1},{1,0},{2,3},{3,2},{4,5},{5,4},{6,7},{7,6},{8,9},{9,8},{10,11... | collective-permute-start | bytes 5111816 | tf_op jit(solution)/shard_map/ppermute | solution.py:1056
  245.7 54.8 %collective-permute-start.26 = (bf16[832,512]{1,0:T(8,128)(2,1)}, bf16[832,512]{1,0:T(8,128)(2,1)}, u32[]{:S(2)}, u32[]{:S(2)}) collective-permute-start(bf16[832,512]{1,0:T(8,128)(2,1)} %slice.117), channel_id=1, source_target_pairs={{0,1},{1,0},{2,3},{3,2},{4,5},{5,4},{6,7},{7,6},{8,9},{9,8},{10,11... | collective-permute-start | bytes 2555912 | tf_op jit(solution)/shard_map/ppermute | solution.py:1056
  249.4 34.0 %collective-permute-start.27 = (f32[2,2,64,256]{3,2,1,0:T(8,128)}, f32[2,2,64,256]{3,2,1,0:T(8,128)}, u32[]{:S(2)}, u32[]{:S(2)}) collective-permute-start(f32[2,2,64,256]{3,2,1,0:T(8,128)} %get-tuple-element.491), channel_id=1, source_target_pairs={{0,1},{1,0},{2,3},{3,2},{4,5},{5,4},{6,7},{7,6},{8,9},{9,8},{10,11... | collective-permute-start | bytes 786440 | tf_op jit(solution)/shard_map/ppermute | solution.py:1056
  283.4 30.4 %collective-permute-start.30 = (bf16[512,1024]{1,0:T(8,128)(2,1)}, bf16[512,1024]{1,0:T(8,128)(2,1)}, u32[]{:S(2)}, u32[]{:S(2)}) collective-permute-start(bf16[512,1024]{1,0:T(8,128)(2,1)} %get-tuple-element.474), channel_id=1, source_target_pairs={{0,4},{4,0},{8,12},{12,8},{16,20},{20,16},{24,28},{28,24},{1,5},{5... | collective-permute-start | bytes 3145736 | tf_op jit(solution)/shard_map/ppermute | solution.py:1062
  300.5 23.0 %collective-permute-start.32 = (bf16[832,512]{1,0:T(8,128)(2,1)}, bf16[832,512]{1,0:T(8,128)(2,1)}, u32[]{:S(2)}, u32[]{:S(2)}) collective-permute-start(bf16[832,512]{1,0:T(8,128)(2,1)} %slice.121), channel_id=1, source_target_pairs={{0,1},{1,0},{2,3},{3,2},{4,5},{5,4},{6,7},{7,6},{8,9},{9,8},{10,11... | collective-permute-start | bytes 2555912 | tf_op jit(solution)/shard_map/ppermute | solution.py:1056
  300.9 72.7 %collective-permute-start.35 = (bf16[3072,256]{1,0:T(8,128)(2,1)}, bf16[3072,256]{1,0:T(8,128)(2,1)}, u32[]{:S(2)}, u32[]{:S(2)}) collective-permute-start(bf16[3072,256]{1,0:T(8,128)(2,1)} %qkv_grad.2), channel_id=1, source_target_pairs={{0,2},{2,0},{1,3},{3,1},{4,6},{6,4},{5,7},{7,5},{8,10},{10,8},{9,1... | collective-permute-start | bytes 4718600 | tf_op jit(solution)/shard_map/ppermute | solution.py:1059
  312.5 40.6 %collective-permute-start.29 = (bf16[512,1024]{1,0:T(8,128)(2,1)}, bf16[512,1024]{1,0:T(8,128)(2,1)}, u32[]{:S(2)}, u32[]{:S(2)}) collective-permute-start(bf16[512,1024]{1,0:T(8,128)(2,1)} %get-tuple-element.473), channel_id=1, source_target_pairs={{0,4},{4,0},{8,12},{12,8},{16,20},{20,16},{24,28},{28,24},{1,5},{5... | collective-permute-start | bytes 3145736 | tf_op jit(solution)/shard_map/ppermute | solution.py:1062
  319.1 30.9 %collective-permute-start.31 = (bf16[256,1024]{1,0:T(8,128)(2,1)}, bf16[256,1024]{1,0:T(8,128)(2,1)}, u32[]{:S(2)}, u32[]{:S(2)}) collective-permute-start(bf16[256,1024]{1,0:T(8,128)(2,1)} %dynamic-slice_convert_fusion.1), channel_id=1, source_target_pairs={{0,8},{4,12},{8,0},{12,4},{16,24},{20,28},{24,16},{28,20},{1,9},{5... | collective-permute-start | bytes 1572872 | tf_op jit(solution)/shard_map/ppermute | solution.py:1062
  320.7 60.2 %collective-permute-start.34 = (bf16[3072,256]{1,0:T(8,128)(2,1)}, bf16[3072,256]{1,0:T(8,128)(2,1)}, u32[]{:S(2)}, u32[]{:S(2)}) collective-permute-start(bf16[3072,256]{1,0:T(8,128)(2,1)} %cross_in_grad.2), channel_id=1, source_target_pairs={{0,2},{2,0},{1,3},{3,1},{4,6},{6,4},{5,7},{7,5},{8,10},{10,8},{9,1... | collective-permute-start | bytes 4718600 | tf_op jit(solution)/shard_map/ppermute | solution.py:1059
  323.5 192.2 %collective-permute-start.20 = (bf16[832,1024]{1,0:T(8,128)(2,1)}, bf16[832,1024]{1,0:T(8,128)(2,1)}, u32[]{:S(2)}, u32[]{:S(2)}) collective-permute-start(bf16[832,1024]{1,0:T(8,128)(2,1)} %get-tuple-element.288), channel_id=1, source_target_pairs={{0,1},{1,0},{2,3},{3,2},{4,5},{5,4},{6,7},{7,6},{8,9},{9,8},{10,11... | collective-permute-start | bytes 5111816 | tf_op jit(solution)/shard_map/ppermute | solution.py:1056
  350.1 60.3 %collective-permute-start.39 = (bf16[512,1024]{1,0:T(8,128)(2,1)}, bf16[512,1024]{1,0:T(8,128)(2,1)}, u32[]{:S(2)}, u32[]{:S(2)}) collective-permute-start(bf16[512,1024]{1,0:T(8,128)(2,1)} %outputs_grad.2), channel_id=1, source_target_pairs={{0,2},{2,0},{1,3},{3,1},{4,6},{6,4},{5,7},{7,5},{8,10},{10,8},{9,1... | collective-permute-start | bytes 3145736 | tf_op jit(solution)/shard_map/ppermute | solution.py:1059
  353.0 39.6 %collective-permute-start.37 = (bf16[256,1024]{1,0:T(8,128)(2,1)}, bf16[256,1024]{1,0:T(8,128)(2,1)}, u32[]{:S(2)}, u32[]{:S(2)}) collective-permute-start(bf16[256,1024]{1,0:T(8,128)(2,1)} %add_convert_fusion.9), channel_id=1, source_target_pairs={{0,16},{4,20},{8,24},{12,28},{16,0},{20,4},{24,8},{28,12},{1,17},{... | collective-permute-start | bytes 1572872 | tf_op jit(solution)/shard_map/ppermute | solution.py:1062
  373.6 17.1 %collective-permute-start.33 = (bf16[256,1024]{1,0:T(8,128)(2,1)}, bf16[256,1024]{1,0:T(8,128)(2,1)}, u32[]{:S(2)}, u32[]{:S(2)}) collective-permute-start(bf16[256,1024]{1,0:T(8,128)(2,1)} %dynamic-slice_convert_fusion), channel_id=1, source_target_pairs={{0,8},{4,12},{8,0},{12,4},{16,24},{20,28},{24,16},{28,20},{1,9},{5... | collective-permute-start | bytes 1572872 | tf_op jit(solution)/shard_map/ppermute | solution.py:1062
  380.9 26.4 %collective-permute-start.40 = (bf16[1536,256]{1,0:T(8,128)(2,1)}, bf16[1536,256]{1,0:T(8,128)(2,1)S(1)}, u32[]{:S(2)}, u32[]{:S(2)}) collective-permute-start(bf16[1536,256]{1,0:T(8,128)(2,1)} %get-tuple-element.476), channel_id=1, source_target_pairs={{0,8},{4,12},{8,0},{12,4},{16,24},{20,28},{24,16},{28,20},{1,9},{5... | collective-permute-start | bytes 2359304 | tf_op jit(solution)/shard_map/ppermute | solution.py:1062
  390.7 75.1 %collective-permute-start.47 = (bf16[832,1024]{1,0:T(8,128)(2,1)}, bf16[832,1024]{1,0:T(8,128)(2,1)}, u32[]{:S(2)}, u32[]{:S(2)}) collective-permute-start(bf16[832,1024]{1,0:T(8,128)(2,1)} %first_back.2), channel_id=1, source_target_pairs={{0,1},{1,0},{2,3},{3,2},{4,5},{5,4},{6,7},{7,6},{8,9},{9,8},{10,11... | collective-permute-start | bytes 5111816 | tf_op jit(solution)/shard_map/ppermute | solution.py:1056
  392.7 21.7 %collective-permute-start.38 = (bf16[1536,256]{1,0:T(8,128)(2,1)}, bf16[1536,256]{1,0:T(8,128)(2,1)}, u32[]{:S(2)}, u32[]{:S(2)}) collective-permute-start(bf16[1536,256]{1,0:T(8,128)(2,1)} %get-tuple-element.478), channel_id=1, source_target_pairs={{0,4},{4,0},{8,12},{12,8},{16,20},{20,16},{24,28},{28,24},{1,5},{5... | collective-permute-start | bytes 2359304 | tf_op jit(solution)/shard_map/ppermute | solution.py:1062
  408.2 26.3 %collective-permute-start.36 = (bf16[256,1024]{1,0:T(8,128)(2,1)}, bf16[256,1024]{1,0:T(8,128)(2,1)S(1)}, u32[]{:S(2)}, u32[]{:S(2)}) collective-permute-start(bf16[256,1024]{1,0:T(8,128)(2,1)} %add_convert_fusion.8), channel_id=1, source_target_pairs={{0,16},{4,20},{8,24},{12,28},{16,0},{20,4},{24,8},{28,12},{1,17},{... | collective-permute-start | bytes 1572872 | tf_op jit(solution)/shard_map/ppermute | solution.py:1062
  410.4 26.3 %collective-permute-start.45 = (bf16[256,1024]{1,0:T(8,128)(2,1)S(1)}, bf16[256,1024]{1,0:T(8,128)(2,1)S(1)}, u32[]{:S(2)}, u32[]{:S(2)}) collective-permute-start(bf16[256,1024]{1,0:T(8,128)(2,1)S(1)} %copy-done.85), channel_id=1, source_target_pairs={{0,8},{4,12},{8,0},{12,4},{16,24},{20,28},{24,16},{28,20},{1,9},{5... | collective-permute-start | bytes 1572872 | tf_op jit(solution)/shard_map/ppermute | solution.py:1062
  414.5 22.0 %collective-permute-start.42 = (bf16[768,256]{1,0:T(8,128)(2,1)S(1)}, bf16[768,256]{1,0:T(8,128)(2,1)S(1)}, u32[]{:S(2)}, u32[]{:S(2)}) collective-permute-start(bf16[768,256]{1,0:T(8,128)(2,1)S(1)} %dynamic-slice_convert_fusion.3), channel_id=1, source_target_pairs={{0,4},{4,0},{8,12},{12,8},{16,20},{20,16},{24,28},{28,24},{1,5},{5... | collective-permute-start | bytes 1179656 | tf_op jit(solution)/shard_map/ppermute | solution.py:1062
  434.6 13.8 %collective-permute-start.44 = (bf16[256,1024]{1,0:T(8,128)(2,1)S(1)}, bf16[256,1024]{1,0:T(8,128)(2,1)S(1)}, u32[]{:S(2)}, u32[]{:S(2)}) collective-permute-start(bf16[256,1024]{1,0:T(8,128)(2,1)S(1)} %get-tuple-element.482), channel_id=1, source_target_pairs={{0,4},{4,0},{8,12},{12,8},{16,20},{20,16},{24,28},{28,24},{1,5},{5... | collective-permute-start | bytes 1572872 | tf_op jit(solution)/shard_map/ppermute | solution.py:1062
  436.5 12.8 %collective-permute-start.43 = (bf16[768,256]{1,0:T(8,128)(2,1)S(1)}, bf16[768,256]{1,0:T(8,128)(2,1)S(1)}, u32[]{:S(2)}, u32[]{:S(2)}) collective-permute-start(bf16[768,256]{1,0:T(8,128)(2,1)S(1)} %dynamic-slice_convert_fusion.2), channel_id=1, source_target_pairs={{0,8},{4,12},{8,0},{12,4},{16,24},{20,28},{24,16},{28,20},{1,9},{5... | collective-permute-start | bytes 1179656 | tf_op jit(solution)/shard_map/ppermute | solution.py:1062
  436.7 28.6 %collective-permute-start.41 = (bf16[256,1024]{1,0:T(8,128)(2,1)S(1)}, bf16[256,1024]{1,0:T(8,128)(2,1)S(1)}, u32[]{:S(2)}, u32[]{:S(2)}) collective-permute-start(bf16[256,1024]{1,0:T(8,128)(2,1)S(1)} %add_convert_fusion.6), channel_id=1, source_target_pairs={{0,8},{4,12},{8,0},{12,4},{16,24},{20,28},{24,16},{28,20},{1,9},{5... | collective-permute-start | bytes 1572872 | tf_op jit(solution)/shard_map/ppermute | solution.py:1062
  448.4 31.0 %collective-permute-start.53 = (bf16[512,1024]{1,0:T(8,128)(2,1)S(1)}, bf16[512,1024]{1,0:T(8,128)(2,1)S(1)}, u32[]{:S(2)}, u32[]{:S(2)}) collective-permute-start(bf16[512,1024]{1,0:T(8,128)(2,1)S(1)} %maximum_select_fusion.6), channel_id=1, source_target_pairs={{0,4},{4,0},{8,12},{12,8},{16,20},{20,16},{24,28},{28,24},{1,5},{5... | collective-permute-start | bytes 3145736 | tf_op jit(solution)/shard_map/ppermute | solution.py:1062
  449.3 25.3 %collective-permute-start.51 = (bf16[768,256]{1,0:T(8,128)(2,1)S(1)}, bf16[768,256]{1,0:T(8,128)(2,1)S(1)}, u32[]{:S(2)}, u32[]{:S(2)}) collective-permute-start(bf16[768,256]{1,0:T(8,128)(2,1)S(1)} %add_convert_fusion.13), channel_id=1, source_target_pairs={{0,16},{4,20},{8,24},{12,28},{16,0},{20,4},{24,8},{28,12},{1,17},{... | collective-permute-start | bytes 1179656 | tf_op jit(solution)/shard_map/ppermute | solution.py:1062
  465.3 12.8 %collective-permute-start.50 = (bf16[128,1024]{1,0:T(8,128)(2,1)S(1)}, bf16[128,1024]{1,0:T(8,128)(2,1)S(1)}, u32[]{:S(2)}, u32[]{:S(2)}) collective-permute-start(bf16[128,1024]{1,0:T(8,128)(2,1)S(1)} %dynamic-slice_convert_fusion.4), channel_id=1, source_target_pairs={{0,8},{4,12},{8,0},{12,4},{16,24},{20,28},{24,16},{28,20},{1,9},{5... | collective-permute-start | bytes 786440 | tf_op jit(solution)/shard_map/ppermute | solution.py:1062
  465.8 27.1 %collective-permute-start.48 = (bf16[768,256]{1,0:T(8,128)(2,1)S(1)}, bf16[768,256]{1,0:T(8,128)(2,1)S(1)}, u32[]{:S(2)}, u32[]{:S(2)}) collective-permute-start(bf16[768,256]{1,0:T(8,128)(2,1)S(1)} %add_convert_fusion.12), channel_id=1, source_target_pairs={{0,16},{4,20},{8,24},{12,28},{16,0},{20,4},{24,8},{28,12},{1,17},{... | collective-permute-start | bytes 1179656 | tf_op jit(solution)/shard_map/ppermute | solution.py:1062
  474.6 36.7 %collective-permute-start.46 = (bf16[512,1024]{1,0:T(8,128)(2,1)S(1)}, bf16[512,1024]{1,0:T(8,128)(2,1)S(1)}, u32[]{:S(2)}, u32[]{:S(2)}) collective-permute-start(bf16[512,1024]{1,0:T(8,128)(2,1)S(1)} %maximum_select_fusion.7), channel_id=1, source_target_pairs={{0,4},{4,0},{8,12},{12,8},{16,20},{20,16},{24,28},{28,24},{1,5},{5... | collective-permute-start | bytes 3145736 | tf_op jit(solution)/shard_map/ppermute | solution.py:1062
  479.3 20.7 %collective-permute-start.57 = (bf16[128,1024]{1,0:T(8,128)(2,1)S(1)}, bf16[128,1024]{1,0:T(8,128)(2,1)S(1)}, u32[]{:S(2)}, u32[]{:S(2)}) collective-permute-start(bf16[128,1024]{1,0:T(8,128)(2,1)S(1)} %add_convert_fusion.15), channel_id=1, source_target_pairs={{0,16},{4,20},{8,24},{12,28},{16,0},{20,4},{24,8},{28,12},{1,17},{... | collective-permute-start | bytes 786440 | tf_op jit(solution)/shard_map/ppermute | solution.py:1062
  479.4 4.0 collective-permute-start.52
  483.4 15.3 %collective-permute-start.55 = (f32[8,1024]{1,0:T(8,128)S(1)}, f32[8,1024]{1,0:T(8,128)S(1)}, u32[]{:S(2)}, u32[]{:S(2)}) collective-permute-start(f32[8,1024]{1,0:T(8,128)S(1)} %add.260), channel_id=1, source_target_pairs={{0,4},{4,0},{8,12},{12,8},{16,20},{20,16},{24,28},{28,24},{1,5},{5... | collective-permute-start | bytes 98312 | tf_op jit(solution)/shard_map/ppermute | solution.py:1062
  493.0 12.2 %collective-permute-start.58 = (bf16[768,256]{1,0:T(8,128)(2,1)S(1)}, bf16[768,256]{1,0:T(8,128)(2,1)S(1)}, u32[]{:S(2)}, u32[]{:S(2)}) collective-permute-start(bf16[768,256]{1,0:T(8,128)(2,1)S(1)} %add_convert_fusion.10), channel_id=1, source_target_pairs={{0,8},{4,12},{8,0},{12,4},{16,24},{20,28},{24,16},{28,20},{1,9},{5... | collective-permute-start | bytes 1179656 | tf_op jit(solution)/shard_map/ppermute | solution.py:1062
  498.7 18.0 %collective-permute-start.62 = (bf16[768,256]{1,0:T(8,128)(2,1)S(1)}, bf16[768,256]{1,0:T(8,128)(2,1)S(1)}, u32[]{:S(2)}, u32[]{:S(2)}) collective-permute-start(bf16[768,256]{1,0:T(8,128)(2,1)S(1)} %add_convert_fusion.11), channel_id=1, source_target_pairs={{0,4},{4,0},{8,12},{12,8},{16,20},{20,16},{24,28},{28,24},{1,5},{5... | collective-permute-start | bytes 1179656 | tf_op jit(solution)/shard_map/ppermute | solution.py:1062
  500.0 9.1 %collective-permute-start.54 = (f32[64,1024]{1,0:T(8,128)S(1)}, f32[64,1024]{1,0:T(8,128)S(1)}, u32[]{:S(2)}, u32[]{:S(2)}) collective-permute-start(f32[64,1024]{1,0:T(8,128)S(1)} %convolution_add_fusion), channel_id=1, source_target_pairs={{0,1},{1,0},{2,3},{3,2},{4,5},{5,4},{6,7},{7,6},{8,9},{9,8},{10,11... | collective-permute-start | bytes 786440 | tf_op jit(solution)/shard_map/ppermute | solution.py:1056
  505.2 3.9 collective-permute-start.56
  509.1 7.9 %collective-permute-start.61 = (bf16[128,1024]{1,0:T(8,128)(2,1)S(1)}, bf16[128,1024]{1,0:T(8,128)(2,1)S(1)}, u32[]{:S(2)}, u32[]{:S(2)}) collective-permute-start(bf16[128,1024]{1,0:T(8,128)(2,1)S(1)} %add_convert_fusion.14), channel_id=1, source_target_pairs={{0,8},{4,12},{8,0},{12,4},{16,24},{20,28},{24,16},{28,20},{1,9},{5... | collective-permute-start | bytes 786440 | tf_op jit(solution)/shard_map/ppermute | solution.py:1062
  509.1 13.6 %collective-permute-start.60 = (f32[8,1024]{1,0:T(8,128)S(1)}, f32[8,1024]{1,0:T(8,128)S(1)}, u32[]{:S(2)}, u32[]{:S(2)}) collective-permute-start(f32[8,1024]{1,0:T(8,128)S(1)} %add.267), channel_id=1, source_target_pairs={{0,16},{4,20},{8,24},{12,28},{16,0},{20,4},{24,8},{28,12},{1,17},{... | collective-permute-start | bytes 98312 | tf_op jit(solution)/shard_map/ppermute | solution.py:1062
  511.4 20.5 %collective-permute-start.64 = (bf16[1536,256]{1,0:T(8,128)(2,1)S(1)}, bf16[1536,256]{1,0:T(8,128)(2,1)S(1)}, u32[]{:S(2)}, u32[]{:S(2)}) collective-permute-start(bf16[1536,256]{1,0:T(8,128)(2,1)S(1)} %maximum_select_fusion.9), channel_id=1, source_target_pairs={{0,4},{4,0},{8,12},{12,8},{16,20},{20,16},{24,28},{28,24},{1,5},{5... | collective-permute-start | bytes 2359304 | tf_op jit(solution)/shard_map/ppermute | solution.py:1062
  515.8 8.2 %collective-permute-start.59 = (bf16[64,1024]{1,0:T(8,128)(2,1)S(1)}, bf16[64,1024]{1,0:T(8,128)(2,1)S(1)}, u32[]{:S(2)}, u32[]{:S(2)}) collective-permute-start(bf16[64,1024]{1,0:T(8,128)(2,1)S(1)} %add_convert_fusion.16), channel_id=1, source_target_pairs={{0,2},{2,0},{1,3},{3,1},{4,6},{6,4},{5,7},{7,5},{8,10},{10,8},{9,1... | collective-permute-start | bytes 393224 | tf_op jit(solution)/shard_map/ppermute | solution.py:1059
  517.0 16.9 %collective-permute-start.65 = (bf16[1536,256]{1,0:T(8,128)(2,1)S(1)}, bf16[1536,256]{1,0:T(8,128)(2,1)}, u32[]{:S(2)}, u32[]{:S(2)}) collective-permute-start(bf16[1536,256]{1,0:T(8,128)(2,1)S(1)} %maximum_select_fusion.10), channel_id=1, source_target_pairs={{0,8},{4,12},{8,0},{12,4},{16,24},{20,28},{24,16},{28,20},{1,9},{5... | collective-permute-start | bytes 2359304 | tf_op jit(solution)/shard_map/ppermute | solution.py:1062
  517.2 22.9 %collective-permute-start.63 = (bf16[256,1024]{1,0:T(8,128)(2,1)S(1)}, bf16[256,1024]{1,0:T(8,128)(2,1)}, u32[]{:S(2)}, u32[]{:S(2)}) collective-permute-start(bf16[256,1024]{1,0:T(8,128)(2,1)S(1)} %maximum_select_fusion.11), channel_id=1, source_target_pairs={{0,4},{4,0},{8,12},{12,8},{16,20},{20,16},{24,28},{28,24},{1,5},{5... | collective-permute-start | bytes 1572872 | tf_op jit(solution)/shard_map/ppermute | solution.py:1062
  (101 other events, 733.1 us)

commit v8 on v7

--- a/solution.py
+++ b/solution.py
@@ -404,32 +404,34 @@
     )(place, mine, other, gains, biases, weights)
 
 
-def project_kernel(place_ref, h_ref, first_ref, second_ref, *out_refs):
-    depth = first_ref.shape[1]
-    near = place_ref[1]
-    left = h_ref[:, pl.ds(pl.multiple_of(near * depth, 128), depth)]
-    right = h_ref[:, pl.ds(pl.multiple_of((1 - near) * depth, 128), depth)]
-    for c, out_ref in enumerate(out_refs):
-        out_ref[...] = lower(nn(left, first_ref[c]) + nn(right, second_ref[c]))
-
-
-def project(place, h, first, second):
+def project_kernel(place_ref, h_ref, weight_ref, *out_refs):
+    count = len(out_refs)
+    wide = weight_ref.shape[2]
+    weights = jnp.concatenate([weight_ref[c] for c in range(count)], axis=1)
+    for start in range(0, h_ref.shape[0], 416):
+        part = slice(start, start + 416)
+        result = lower(nn(h_ref[part, :], weights))
+        for c, out_ref in enumerate(out_refs):
+            out_ref[part, :] = result[:, c * wide : (c + 1) * wide]
+
+
+def project(place, h, weights):
     rows, depth = h.shape[0] // 2, h.shape[1]
-    count, _, wide = first.shape
+    count, _, wide = weights.shape
     out = pl.BlockSpec((rows, wide), lambda i, s: ((i + s[0]) % 2, 0))
     return pl.pallas_call(
         project_kernel,
         grid_spec=pltpu.PrefetchScalarGridSpec(
             num_scalar_prefetch=1,
             grid=(2,),
-            in_specs=[rows_of(rows, depth), resident(first.shape), resident(second.shape)],
+            in_specs=[rows_of(rows, depth), resident(weights.shape)],
             out_specs=[out] * count,
         ),
         out_shape=[shape((2 * rows, wide), ROUND)] * count,
-        compiler_params=params(32),
+        compiler_params=params(40),
         cost_estimate=brief(),
         name="project",
-    )(place, h, first, second)
+    )(place, h, weights)
 
 
 def pull_kernel(place_ref, mine_ref, other_ref, *refs):
@@ -451,17 +453,17 @@
 
 def pull(place, mine, other, weights):
     rows = mine.shape[0]
-    wide = weights[0].shape[0]
-    out = pl.BlockSpec((rows, wide), lambda i, s: ((i + s[0]) % 2, 0))
     return pl.pallas_call(
         pull_kernel,
         grid_spec=pltpu.PrefetchScalarGridSpec(
             num_scalar_prefetch=1,
             grid=(2,),
             in_specs=[resident(a.shape) for a in (mine, other, *weights)],
-            out_specs=[out] * len(weights),
+            out_specs=[
+                pl.BlockSpec((rows, a.shape[0]), lambda i, s: ((i + s[0]) % 2, 0)) for a in weights
+            ],
         ),
-        out_shape=[shape((2 * rows, wide), ROUND)] * len(weights),
+        out_shape=[shape((2 * rows, a.shape[0]), ROUND) for a in weights],
         compiler_params=params(32),
         cost_estimate=brief(),
         name="pull",
@@ -633,55 +635,77 @@
     return weights_exp / by_head(weights_exp, jnp.sum, 0.0)
 
 
-def middle_forward_kernel(
-    place_ref, frame_ref, a0_ref, a1_ref, a2_ref, a3_ref, gain_ref, bias_ref, *refs
-):
-    mixed = (a0_ref, a1_ref, a2_ref, a3_ref)
-    wo, wq, wc = refs[0:4], refs[4:8], refs[12:16]
-    ck0_ref, ck1_ref, cv0_ref, cv1_ref = refs[8:12]
-    x1_ref, x2_ref, h2_ref, cq_ref, ca_ref, h3_ref = refs[16:]
+PIECES = ((0, 256), (256, 128), (384, 128), (512, 256), (768, 128), (896, 128))
+
+
+def middle_forward_kernel(place_ref, frame_ref, *refs):
+    mixed, wo, wq, wc = refs[0:6], refs[6:12], refs[12:18], refs[18:24]
+    ck_ref, cv_ref, gain_ref, bias_ref = refs[24:28]
+    x1_ref, x2_ref, h2_ref, cq_ref, ca_ref, h3_ref = refs[28:]
     x1 = frame_ref[...].astype(FULL)
-    for g in range(4):
-        x1 = x1 + nn(mixed[g][...], wo[g][...])
+    for o_ref, weight_ref in zip(mixed, wo):
+        x1 = x1 + nn(o_ref[...], weight_ref[...])
     x1_ref[...] = x1
     scaled, _ = norm_parts(x1)
     h2 = lower(scaled * gain_ref[1:2, :] + bias_ref[1:2, :])
     h2_ref[...] = h2
+    for (start, size), weight_ref in zip(PIECES, wq):
+        cq_ref[:, start : start + size] = lower(nn(h2, weight_ref[...]))
     for g in range(4):
         lanes = slice(g * 256, (g + 1) * 256)
-        cq = lower(nn(h2, wq[g][...]))
-        cq_ref[:, lanes] = cq
-        probability = cross_probability(cq, (ck0_ref, ck1_ref)[g // 2][g % 2])
-        ca_ref[:, lanes] = lower(nn(lower(probability), (cv0_ref, cv1_ref)[g // 2][g % 2]))
+        probability = cross_probability(cq_ref[:, lanes], ck_ref[g])
+        ca_ref[:, lanes] = lower(nn(lower(probability), cv_ref[g]))
     crossed = 0.0
-    for g in range(4):
-        crossed = crossed + nn(ca_ref[:, g * 256 : (g + 1) * 256], wc[g][...])
+    for (start, size), weight_ref in zip(PIECES, wc):
+        crossed = crossed + nn(ca_ref[:, start : start + size], weight_ref[...])
     x2 = x1_ref[...] + crossed
     x2_ref[...] = x2
     scaled, _ = norm_parts(x2)
     h3_ref[...] = lower(scaled * gain_ref[2:3, :] + bias_ref[2:3, :])
 
 
-def middle_forward(place, frames, attended, received, gains, biases, wo, wq, ck, cv, wc):
+def middle_forward(place, frames, attended, received, wo, wq, wc, ck, cv, gains, biases):
     rows, width = frames.shape
     block = 416
     steps = rows // block
-    piece = pl.BlockSpec((block, 256), lambda i, s: (s[0] * steps + i, 0))
     wide = rows_of(block, width)
+    whole = (*wo, *wq, *wc, ck, cv, gains, biases)
     return pl.pallas_call(
         middle_forward_kernel,
         grid_spec=pltpu.PrefetchScalarGridSpec(
             num_scalar_prefetch=1,
             grid=(steps,),
-            in_specs=[wide, piece, piece, rows_of(block, 256), rows_of(block, 256)]
-            + [resident(a.shape) for a in (gains, biases, *wo, *wq, *ck, *cv, *wc)],
+            in_specs=[wide]
+            + [
+                pl.BlockSpec((block, a.shape[1]), lambda i, s: (s[0] * steps + i, 0))
+                for a in attended
+            ]
+            + [rows_of(block, a.shape[1]) for a in received]
+            + [resident(a.shape) for a in whole],
             out_specs=[wide] * 6,
         ),
         out_shape=[shape((rows, width), FULL)] * 2 + [shape((rows, width), ROUND)] * 4,
         compiler_params=params(56),
         cost_estimate=brief(),
         name="middle_forward",
-    )(place, frames, *attended, *received, gains, biases, *wo, *wq, *ck, *cv, *wc)
+    )(place, frames, *attended, *received, *whole)
+
+
+def keys_kernel(text_ref, weight_ref, out_ref):
+    for item in range(2):
+        for c in range(2):
+            out_ref[item, c] = lower(nn(text_ref[item], weight_ref[c]))
+
+
+def keys_of(text_states, weights):
+    items, states, _ = text_states.shape
+    return pl.pallas_call(
+        keys_kernel,
+        out_shape=shape((items, 2, states, weights.shape[2]), ROUND),
+        compiler_params=params(24),
+        cost_estimate=brief(),
+        name="keys_of",
+    )(text_states, weights)
 
 
 def feed_kernel(place_ref, h_ref, d_ref, *refs, parts, carried):
@@ -697,8 +721,8 @@
         if parts == 1:
             lanes = slice(0, size)
         else:
-            near = place_ref[1]
-            which = near if n == 0 else 1 - near
+            column = place_ref[2]
+            which = column if n == 0 else 1 - column
             lanes = pl.ds(pl.multiple_of(which * size, 128), size)
         u = nn(h, up_ref[...])
         active, slope = gelu_parts(u)
@@ -793,75 +817,93 @@
 def qkv_grad_kernel(place_ref, h_ref, *refs):
     out_ref = refs[-1]
     rows, width = h_ref.shape[0] // 2, h_ref.shape[1]
-    core = place_ref[0]
+    core, near = place_ref[0], place_ref[1]
+    halves = (len(refs) - 1) // 3
     total = [0.0] * 3
     for half in range(2):
         turned = h_ref[half * rows : (half + 1) * rows, :].T
         at = pl.multiple_of((core if half == 0 else 1 - core) * rows, 16)
         for c in range(3):
-            total[c] = total[c] + nn(turned, refs[c][pl.ds(at, rows), :])
+            parts = [refs[3 * n + c][pl.ds(at, rows), :] for n in range(halves)]
+            grads = parts[0] if halves == 1 else jnp.concatenate(parts, axis=1)
+            total[c] = total[c] + nn(turned, grads)
     for c in range(3):
-        out_ref[c * width : (c + 1) * width, :] = total[c].astype(out_ref.dtype)
+        part = slice(c * width, (c + 1) * width)
+        value = total[c].astype(out_ref.dtype)
+        if halves == 1:
+            out_ref[part, :] = value
+        else:
+            out_ref[part, pl.ds(pl.multiple_of(near * 128, 128), 128)] = value[:, :128]
+            out_ref[part, pl.ds(pl.multiple_of((1 - near) * 128, 128), 128)] = value[:, 128:]
 
 
 def qkv_grad(place, h, grads, kind):
     width = h.shape[1]
-    wide = grads[0].shape[1]
     return pl.pallas_call(
         qkv_grad_kernel,
         grid_spec=pltpu.PrefetchScalarGridSpec(
             num_scalar_prefetch=1,
             grid=(1,),
             in_specs=[resident(a.shape) for a in (h, *grads)],
-            out_specs=resident((3 * width, wide)),
+            out_specs=resident((3 * width, 256)),
         ),
-        out_shape=shape((3 * width, wide), kind),
+        out_shape=shape((3 * width, 256), kind),
         compiler_params=params(48),
         cost_estimate=brief(),
         name="qkv_grad",
     )(place, h, *grads)
 
 
-def cross_in_grad_kernel(mine_ref, other_ref, dm_ref, do_ref, text_ref, pair_ref, out_ref):
-    width = mine_ref.shape[1]
+def query_grad_kernel(place_ref, mine_ref, other_ref, dm_ref, do_ref, out_ref, *, split):
+    column = place_ref[2]
     total = tn(mine_ref[...], dm_ref[...]) + tn(other_ref[...], do_ref[...])
-    out_ref[:width, :] = total.astype(out_ref.dtype)
-    turned = text_ref[...].T
-    for c in range(2):
-        part = nn(turned, pair_ref[c]).astype(out_ref.dtype)
-        out_ref[(1 + c) * width : (2 + c) * width, :] = part
-
-
-def cross_in_grad(group, mine, other, d_mine, d_other, text, pair, kind):
+    value = total.astype(out_ref.dtype)
+    if split:
+        out_ref[:, pl.ds(pl.multiple_of(column * 128, 128), 128)] = value[:, :128]
+        out_ref[:, pl.ds(pl.multiple_of((1 - column) * 128, 128), 128)] = value[:, 128:]
+    else:
+        out_ref[...] = value
+
+
+def query_grad(place, group, mine, other, d_mine, d_other, kind):
     rows, width = mine.shape
-    lanes = pl.BlockSpec((rows, 256), lambda i: (0, group))
-
-    def whole(a):
-        zeros = (0,) * a.ndim
-        return pl.BlockSpec(a.shape, lambda i: zeros)
-
+    lanes = pl.BlockSpec((rows, 256), lambda i, s: (0, group))
     return pl.pallas_call(
-        cross_in_grad_kernel,
-        grid=(1,),
-        in_specs=[whole(mine), whole(other), lanes, lanes, whole(text), whole(pair)],
-        out_specs=pl.BlockSpec((3 * width, 256), lambda i: (0, 0)),
-        out_shape=shape((3 * width, 256), kind),
+        functools.partial(query_grad_kernel, split=group == 1),
+        grid_spec=pltpu.PrefetchScalarGridSpec(
+            num_scalar_prefetch=1,
+            grid=(1,),
+            in_specs=[resident(mine.shape), resident(other.shape), lanes, lanes],
+            out_specs=resident((width, 256)),
+        ),
+        out_shape=shape((width, 256), kind),
         compiler_params=params(48),
         cost_estimate=brief(),
-        name="cross_in_grad",
-    )(mine, other, d_mine, d_other, text, pair)
-
-
-def outputs_grad_kernel(
-    place_ref, o_ref, sm_ref, so_ref, am_ref, ao_ref, cm_ref, co_ref, out_ref
-):
+        name="query_grad",
+    )(place, mine, other, d_mine, d_other)
+
+
+def outputs_grad_kernel(place_ref, *refs, count):
+    o_refs = refs[:count]
+    sm_ref, so_ref, am_ref, ao_ref, cm_ref, co_ref, out_ref = refs[count:]
     rows = sm_ref.shape[0]
-    core = place_ref[0]
-    mine = o_ref[pl.ds(pl.multiple_of(core * rows, 16), rows), :]
-    other = o_ref[pl.ds(pl.multiple_of((1 - core) * rows, 16), rows), :]
-    out_ref[:256, :] = (tn(mine, sm_ref[...]) + tn(other, so_ref[...])).astype(out_ref.dtype)
+    core, near, column = place_ref[0], place_ref[1], place_ref[2]
+    mine_at = pl.ds(pl.multiple_of(core * rows, 16), rows)
+    other_at = pl.ds(pl.multiple_of((1 - core) * rows, 16), rows)
+    for n, o_ref in enumerate(o_refs):
+        total = tn(o_ref[mine_at, :], sm_ref[...]) + tn(o_ref[other_at, :], so_ref[...])
+        if count == 1:
+            at = slice(0, 256)
+        else:
+            at = pl.ds(pl.multiple_of((near if n == 0 else 1 - near) * 128, 128), 128)
+        out_ref[at, :] = total.astype(out_ref.dtype)
     total = tn(am_ref[...], cm_ref[...]) + tn(ao_ref[...], co_ref[...])
-    out_ref[256:, :] = total.astype(out_ref.dtype)
+    value = total.astype(out_ref.dtype)
+    if count == 1:
+        out_ref[256:, :] = value
+    else:
+        out_ref[pl.ds(pl.multiple_of(256 + column * 128, 128), 128), :] = value[:128, :]
+        out_ref[pl.ds(pl.multiple_of(384 - column * 128, 128), 128), :] = value[128:, :]
 
 
 def outputs_grad(place, group, o, dself, dself_other, ca, ca_other, dcross, dcross_other, kind):
@@ -869,27 +911,25 @@
     lanes = pl.BlockSpec((rows, 256), lambda i, s: (0, group))
     whole = resident((rows, width))
     return pl.pallas_call(
-        outputs_grad_kernel,
+        functools.partial(outputs_grad_kernel, count=len(o)),
         grid_spec=pltpu.PrefetchScalarGridSpec(
             num_scalar_prefetch=1,
             grid=(1,),
-            in_specs=[resident(o.shape), whole, whole, lanes, lanes, whole, whole],
+            in_specs=[resident(a.shape) for a in o] + [whole, whole, lanes, lanes, whole, whole],
             out_specs=resident((512, width)),
         ),
         out_shape=shape((512, width), kind),
         compiler_params=params(48),
         cost_estimate=brief(),
         name="outputs_grad",
-    )(place, o, dself, dself_other, ca, ca_other, dcross, dcross_other)
-
-
-def middle_back_kernel(
-    place_ref, ym_ref, yr_ref, x1_ref, x2_ref, d_ref, cq_ref, gain_ref, *refs
-):
-    wq, wc = refs[0:4], refs[8:12]
-    ck0_ref, ck1_ref, cv0_ref, cv1_ref = refs[4:8]
-    dx1_ref, dself_ref, dcross_ref, dcq_ref, dck_ref, dcv_ref, sums_ref = refs[12:19]
-    dck_all, dcv_all = refs[19:]
+    )(place, *o, dself, dself_other, ca, ca_other, dcross, dcross_other)
+
+
+def middle_back_kernel(place_ref, ym_ref, yr_ref, x1_ref, x2_ref, d_ref, cq_ref, *refs):
+    wq, wc = refs[0:6], refs[6:12]
+    ck_ref, cv_ref, gain_ref = refs[12:15]
+    dx1_ref, dself_ref, dcross_ref, dcq_ref, dck_ref, dcv_ref, sums_ref = refs[15:22]
+    dck_all, dcv_all = refs[22:]
     step = pl.program_id(0)
 
     @pl.when(step == 0)
@@ -906,22 +946,26 @@
     dx1_ref[...] = dx2
     dcross = lower(dx2)
     dcross_ref[...] = dcross
-    y2 = 0.0
+    pulled = [lower(nt(dcross, weight_ref[...])) for weight_ref in wc]
     for g in range(4):
         lanes = slice(g * 256, (g + 1) * 256)
-        keys = (ck0_ref, ck1_ref)[g // 2][g % 2]
-        values = (cv0_ref, cv1_ref)[g // 2][g % 2]
-        dcatt = lower(nt(dcross, wc[g][...]))
+        at = 3 * (g // 2)
+        if g % 2 == 0:
+            dcatt = pulled[at]
+        else:
+            dcatt = jnp.concatenate(pulled[at + 1 : at + 3], axis=1)
+        keys = ck_ref[g]
         cq = cq_ref[:, lanes]
         probability = cross_probability(cq, keys)
-        weighed = nt(dcatt, values)
+        weighed = nt(dcatt, cv_ref[g])
         inner = by_head(probability * weighed, jnp.sum, 0.0)
         dcs = lower(probability * (weighed - inner))
-        dcq = lower(nn(dcs, keys) * HEAD ** (-0.5))
-        dcq_ref[:, lanes] = dcq
+        dcq_ref[:, lanes] = lower(nn(dcs, keys) * HEAD ** (-0.5))
         dck_all[g] += tn(dcs, cq * HEAD ** (-0.5))
         dcv_all[g] += tn(lower(probability), dcatt)
-        y2 = y2 + nt(dcq, wq[g][...])
+    y2 = 0.0
+    for (start, size), weight_ref in zip(PIECES, wq):
+        y2 = y2 + nt(dcq_ref[:, start : start + size], weight_ref[...])
     scaled, inverse = norm_parts(x1_ref[...])
     sums_ref[2:3, :] += jnp.sum(y2 * scaled, axis=0, keepdims=True)
     sums_ref[3:4, :] += jnp.sum(y2, axis=0, keepdims=True)
@@ -940,17 +984,18 @@
                 result[g] = total
 
 
-def middle_back(place, ym, yr, x1, x2, d, cq, gains, wq, ck, cv, wc):
+def middle_back(place, ym, yr, x1, x2, d, cq, wq, wc, ck, cv, gains):
     rows, width = x1.shape
     block = 416
     wide = rows_of(block, width)
     small = pl.BlockSpec((4, 64, 256), lambda i, s: (0, 0, 0))
+    whole = (*wq, *wc, ck, cv, gains)
     return pl.pallas_call(
         middle_back_kernel,
         grid_spec=pltpu.PrefetchScalarGridSpec(
             num_scalar_prefetch=1,
             grid=(rows // block,),
-            in_specs=[wide] * 6 + [resident(a.shape) for a in (gains, *wq, *ck, *cv, *wc)],
+            in_specs=[wide] * 6 + [resident(a.shape) for a in whole],
             out_specs=[wide] * 4 + [small, small, pl.BlockSpec((8, width), lambda i, s: (0, 0))],
             scratch_shapes=[pltpu.VMEM((4, 256, 256), FULL)] * 2,
         ),
@@ -961,48 +1006,41 @@
         compiler_params=params(56),
         cost_estimate=brief(),
         name="middle_back",
-    )(place, ym, yr, x1, x2, d, cq, gains, *wq, *ck, *cv, *wc)
+    )(place, ym, yr, x1, x2, d, cq, *whole)
 
 
 def first_back_kernel(place_ref, *refs):
-    grads = refs[:6]
-    own_ref, first_ref, second_ref, y_ref, total = refs[6:]
-    depth = first_ref.shape[1]
+    y_ref = refs[-1]
     y = 0.0
-    left = 0.0
-    right = 0.0
-    for c in range(3):
-        y = y + nt(grads[c][...], own_ref[c])
-        left = left + nt(grads[3 + c][...], first_ref[c])
-        right = right + nt(grads[3 + c][...], second_ref[c])
-    near = place_ref[1]
-    total[...] = y
-    total[:, pl.ds(pl.multiple_of(near * depth, 128), depth)] += left
-    total[:, pl.ds(pl.multiple_of((1 - near) * depth, 128), depth)] += right
-    y_ref[...] = total[...].astype(y_ref.dtype)
-
-
-def first_back(place, grads, own, first, second, kind):
+    for n in range(3):
+        for c in range(3):
+            y = y + nt(refs[3 * n + c][...], refs[9 + n][c])
+    y_ref[...] = y.astype(y_ref.dtype)
+
+
+def first_back(place, grads, weights, kind):
     span = grads[0].shape[0]
     rows = span // 2
-    width = own.shape[1]
+    width = weights[0].shape[1]
     block = 416
     steps = rows // block
-    piece = pl.BlockSpec((block, 256), lambda i, s: (s[0] * steps + i, 0))
     return pl.pallas_call(
         first_back_kernel,
         grid_spec=pltpu.PrefetchScalarGridSpec(
             num_scalar_prefetch=1,
             grid=(steps,),
-            in_specs=[piece] * 6 + [resident(a.shape) for a in (own, first, second)],
+            in_specs=[
+                pl.BlockSpec((block, a.shape[1]), lambda i, s: (s[0] * steps + i, 0))
+                for a in grads
+            ]
+            + [resident(a.shape) for a in weights],
             out_specs=rows_of(block, width),
-            scratch_shapes=[pltpu.VMEM((block, width), FULL)],
         ),
         out_shape=shape((rows, width), kind),
         compiler_params=params(40),
         cost_estimate=brief(),
         name="first_back",
-    )(place, *grads, own, first, second)
+    )(place, *grads, *weights)
 
 
 def frames_back_kernel(place_ref, ym_ref, yr_ref, dx1_ref, frame_ref, gain_ref, out_ref, sums_ref):
@@ -1046,8 +1084,8 @@
     column = lax.axis_index("wide") % 2
     layer = lax.axis_index("wide") // 2
     near = layer % 2
-    place = jnp.stack([core, near]).astype(jnp.int32)
-    away = jnp.stack([1 - core, near]).astype(jnp.int32)
+    place = jnp.stack([core, near, column]).astype(jnp.int32)
+    away = jnp.stack([1 - core, near, column]).astype(jnp.int32)
     limit = lax.dynamic_slice(lengths, (side,), (1,))
     rows, width = frames.shape
     join = lax.optimization_barrier
@@ -1072,76 +1110,88 @@
             jnp.concatenate([second, first], axis=0),
         )
 
-    frames_other = over_core(frames)
-    qkv_first = over_y(half_of(w_qkv, near, 1))
-    dout = jnp.where(loss_mask[:, None] != 0, cotangent, jnp.zeros((), ROUND))
-    inward = jnp.concatenate([w_cross_q, w_cross_kv.reshape(2 * width, 256)], axis=0)
-    outward = jnp.concatenate([w_out, w_cross_out], axis=0)
-    h1, q0, k0, v0 = first_project(place, frames, frames_other, norm_gain, norm_bias, w_qkv)
-
-    q0, qkv_first, inward, outward, dout = join((q0, qkv_first, inward, outward, dout))
-    qkv_second = along_wide(qkv_first, Z_NEAR)
-    outward_first = over_y(half_of(outward, column))
-    inward_first = over_y(half_of(inward, near))
-    dout_other = over_core(dout)
-    own_wo = over_core(outward)
-    own_wq = over_core(w_cross_q)
-    o0, lse0 = self_forward(limit, q0, k0, v0)
-
-    o0, qkv_second, w_up, w_down = join((o0, qkv_second, w_up, w_down))
-    q1, k1, v1 = project(place, h1, qkv_first, qkv_second)
+    def over_z(v):
+        return along_wide(v, Z_NEAR)
+
+    def over_x(v):
+        return along_wide(v, X_PAIRS)
 
     def away_rows(v):
         return half_of(v, 1 - core)
 
+    def cross_order(v):
+        return jnp.where(column == 0, v, jnp.concatenate([v[..., 128:], v[..., :128]], axis=-1))
+
+    qkv_first = over_y(half_of(w_qkv, near, 2))
+    frames_other = over_core(frames)
+    h1, q0, k0, v0 = first_project(place, frames, frames_other, norm_gain, norm_bias, w_qkv)
+    q0, qkv_first, w_out, w_cross_q, w_cross_out, cotangent = join(
+        (q0, qkv_first, w_out, w_cross_q, w_cross_out, cotangent)
+    )
+
+    qkv_second = over_z(qkv_first)
+    out_first = over_y(half_of(w_out, near))
+    query_first = over_y(half_of(w_cross_q, column, 1))
+    cross_out_first = over_y(half_of(w_cross_out, column))
+    o0, lse0 = self_forward(limit, q0, k0, v0)
+    qf, kf, vf = project(place, h1, qkv_first)
+    out_other, query_other, cross_out_other = map(over_core, (w_out, w_cross_q, w_cross_out))
+    qf, o0, out_first, query_first, cross_out_first, w_up, w_down, *core_got = join(
+        (qf, o0, out_first, query_first, cross_out_first, w_up, w_down)
+        + (out_other, query_other, cross_out_other)
+    )
+
+    out_other, query_other, cross_out_other = core_got
+    out_second = over_z(out_first)
+    query_second = over_x(query_first)
+    cross_out_second = over_x(cross_out_first)
+    up_first = over_y(half_of(w_up, column, 1))
+    down_sent = half_of(w_down, column)
     o0_other = over_core(away_rows(o0))
-    up_sent = half_of(w_up, near, 1)
-    down_sent = half_of(w_down, near)
-    q1, outward_first, inward_first, up_sent, down_sent, o0_other, own_wo, own_wq = join(
-        (q1, outward_first, inward_first, up_sent, down_sent, o0_other, own_wo, own_wq)
-    )
-    outward_second = along_wide(outward_first, X_PAIRS)
-    inward_second = along_wide(inward_first, Z_NEAR)
-    up_first = over_y(up_sent)
-    o1, lse1 = self_forward(limit, q1, k1, v1)
-    o1_other = over_core(away_rows(o1))
-    o1, outward_second, inward_second, down_sent, dout_other = join(
-        (o1, outward_second, inward_second, down_sent, dout_other)
+    keys = keys_of(text_states, w_cross_kv)
+    own_keys = lax.dynamic_index_in_dim(keys, side, keepdims=False)
+    keys_y = over_y(lax.dynamic_index_in_dim(keys, 1 - side, keepdims=False))
+    of, lse_f = self_forward(limit, qf, kf, vf)
+    of, qkv_second, keys_y, o0_other = join((of, qkv_second, keys_y, o0_other))
+
+    qs, ks, vs = project(place, h1, qkv_second)
+    of_other = over_core(away_rows(of))
+    pair = jnp.stack([own_keys, cross_order(keys_y)])
+    pair_other = over_core(pair)
+    o_s, lse_s = self_forward(limit, qs, ks, vs)
+    o_s, out_second, query_second, cross_out_second, up_first, down_sent, pair_other, of_other = join(
+        (o_s, out_second, query_second, cross_out_second, up_first, down_sent, pair_other, of_other)
     )
 
     down_first = over_y(down_sent)
-    outward_y = ordered(outward_first, outward_second, column)
-    inward_y = ordered(inward_first, inward_second, near)
-    out_y = outward_y[:256]
-    cross_out_y = outward_y[256:]
-    cross_q_y = inward_y[:width]
-    cross_kv_y = inward_y[width:].reshape(2, width, 256)
-    y_wo = over_core(outward_y)
-    y_wq = over_core(cross_q_y)
-    wo = (w_out, out_y, own_wo[:256], y_wo[:256])
-    wc = (w_cross_out, cross_out_y, own_wo[256:], y_wo[256:])
-    wq = (w_cross_q, cross_q_y, own_wq, y_wq)
-    text = lax.dynamic_slice(text_states, (side, 0, 0), (1, *text_states.shape[1:]))[0]
-    pair = jnp.stack(
-        [jnp.stack([lower(nn(text, w[c])) for c in range(2)]) for w in (w_cross_kv, cross_kv_y)]
-    )
-    pair_other = over_core(pair)
+    up_second = over_x(up_first)
+    os_other = over_core(away_rows(o_s))
+    dout = jnp.where(loss_mask[:, None] != 0, cotangent, jnp.zeros((), ROUND))
+
+    def pieces(own, first, second, own_other):
+        return (own, first, second, own_other, over_core(first), over_core(second))
+
+    wo = pieces(w_out, out_first, out_second, out_other)
+    wq = pieces(w_cross_q, query_first, query_second, query_other)
+    wc = pieces(w_cross_out, cross_out_first, cross_out_second, cross_out_other)
+    text = lax.dynamic_index_in_dim(text_states, side, keepdims=False)
     head_of = jnp.arange(256) // HEAD
     same = head_of[:, None] == head_of[None, :]
 
     def spread_heads(v):
         return jnp.where(same, jnp.tile(v, (1, 4, 1)), jnp.zeros((), ROUND))
 
-    ck = (spread_heads(pair[:, 0]), spread_heads(pair_other[:, 0]))
-    cv = (spread_heads(pair[:, 1]), spread_heads(pair_other[:, 1]))
+    every = jnp.concatenate([pair, pair_other], axis=0)
+    ck, cv = spread_heads(every[:, 0]), spread_heads(every[:, 1])
     x1, x2, h2, cq, ca, h3 = middle_forward(
-        place, frames, (o0, o1), (o0_other, o1_other), norm_gain, norm_bias, wo, wq, ck, cv, wc
-    )
-    h3, ca, h2, up_first, down_first = join((h3, ca, h2, up_first, down_first))
+        place, frames, (o0, of, o_s), (o0_other, of_other, os_other), wo, wq, wc, ck, cv,
+        norm_gain, norm_bias,
+    )
+    h3, ca, h2, down_first, dout = join((h3, ca, h2, down_first, dout))
 
     h3_other = over_core(h3)
-    up_second = along_wide(up_first, Z_NEAR)
-    down_second = along_wide(down_first, Z_NEAR)
+    dout_other = over_core(dout)
+    down_second = over_x(down_first)
     g0, du0, out_m, y_m = feed(place, h3, dout, (w_up,), (w_down,), FULL, 0)
     g0, du0, out_o, y_o = feed(
         place, h3_other, dout_other, (w_up,), (w_down,), FULL, 1, shared=(g0, du0)
@@ -1200,6 +1250,12 @@
             store[self.fly] = along_wide(away_half, pairs)
             last[:] = [self.kept]
 
+        def first_alone(self, own):
+            which, pairs = self.axes[0]
+            store[self.kept] = half_of(store[own], which).astype(FULL)
+            store[self.fly] = along_wide(half_of(store[own], 1 - which), pairs)
+            last[:] = [self.kept]
+
         def second(self):
             which, pairs = self.axes[1]
             order(self.fly, self.kept)
@@ -1249,66 +1305,68 @@
     up, down, outs, cross_in = Sum("up"), Sum("down"), Sum("outs"), Sum("cross_in")
     qkv = Sum("qkv", (down_z, across))
     store.update(h3_other=h3_other, du1=du1, g1=g1, du0=du0, g0=g0, y_m=y_m, y_fly=y_received)
-    store.update(o1=o1, o0=o0, x2=x2, h2_other=h2_other, ca_other=ca_other)
+    store.update(of=of, o_s=o_s, o0=o0, x2=x2, h2_other=h2_other, ca_other=ca_other)
+
+    def middle():
+        dx1, *rest = middle_back(
+            place, *get("y_m", "y_fly"), x1, store["x2"], dout, cq, wq, wc, ck, cv, norm_gain
+        )
+        return (rest[0], dx1, *rest[1:])
 
     step(["up1"], lambda: up_grad(h3, *get("h3_other", "du1"), ROUND), "du1", "du0")
     up.over_y("up1")
     step(["down1"], lambda: down_grad(store["g1"], dout, dout_other, ROUND), "g1")
     down.over_y("down1")
-    step(
-        ["dself", "dx1", "dcross", "dcq", "dck", "dcv", "sums"],
-        lambda: (
-            lambda r: (r[1], r[0], *r[2:])
-        )(
-            middle_back(
-                place, *get("y_m", "y_fly"), x1, store["x2"], dout, cq, norm_gain, wq, ck, cv, wc
-            )
-        ),
-        "y_fly",
-        "y_m",
-        "x2",
-    )
+    step(["dself", "dx1", "dcross", "dcq", "dck", "dcv", "sums"], middle, "y_fly", "y_m", "x2")
     store["dself_other"] = over_core(store["dself"])
     step(["up0"], lambda: up_grad(h3, *get("h3_other", "du0"), ROUND), "du0")
+    step(
+        ["dof", "dos", "do0"],
+        lambda: pull(place, *get("dself", "dself_other"), (out_first, out_second, w_out)),
+        "dself",
+        "dself_other",
+        "dcross",
+        "dcq",
+    )
     store["dcross_other"] = over_core(store["dcross"])
     store["dcq_other"] = over_core(store["dcq"][:, 512:])
     d_pair = jnp.stack(get("dck", "dcv"), axis=1)
     store["pair_kept"] = d_pair[:2]
     store["pair_fly"] = over_core(d_pair[2:])
     step(
-        ["do1", "do0"],
-        lambda: pull(place, *get("dself", "dself_other"), (out_y, w_out)),
-        "dself",
-        "dself_other",
-    )
+        ["dqf", "dkf", "dvf"],
+        lambda: self_back(limit, qf, kf, vf, store["of"], store["dof"], lse_f),
+        "dof",
+    )
+    order("dcross_other", "dcq_other", "pair_fly", "pair_kept")
+    pair_sum = lower(store["pair_kept"] + store["pair_fly"])
+    store["pair"] = pair_sum[0]
+    store["pair_y"] = over_y(cross_order(pair_sum[1]))
     step(
-        ["dq1", "dk1", "dv1"],
-        lambda: self_back(limit, q1, k1, v1, store["o1"], store["do1"], lse1),
-        "do1",
+        ["dqs", "dks", "dvs"],
+        lambda: self_back(limit, qs, ks, vs, store["o_s"], store["dos"], lse_s),
+        "dos",
     )
     up.first("up0")
     step(["down0"], lambda: down_grad(store["g0"], dout, dout_other, ROUND), "g0")
-    step(["qkv1"], lambda: qkv_grad(place, h1, get("dq1", "dk1", "dv1"), ROUND), "dq1")
+    yp = ("dqf", "dkf", "dvf", "dqs", "dks", "dvs")
+    step(["qkv1"], lambda: qkv_grad(place, h1, get(*yp), ROUND), "dqs", "pair_y")
     qkv.over_y("qkv1")
-    order("dcross_other", "dcq_other", "pair_fly", "pair_kept")
-    store["pair"] = lower(store["pair_kept"] + store["pair_fly"])
-
-    def into(g):
-        return cross_in_grad(
-            g, h2, *get("h2_other", "dcq", "dcq_other"), text, store["pair"][g], ROUND
-        )
-
-    def outof(g, o):
+
+    def query(g):
+        return query_grad(place, g, h2, *get("h2_other", "dcq", "dcq_other"), ROUND)
+
+    def outof(g, *o):
         return outputs_grad(
-            place, g, o, *get("dself", "dself_other"), ca,
+            place, g, get(*o), *get("dself", "dself_other"), ca,
             *get("ca_other", "dcross", "dcross_other"), ROUND,
         )
 
-    step(["into1"], lambda: into(1), "pair", "dcq_other", "h2_other")
-    cross_in.over_y("into1")
+    step(["query1"], lambda: query(1), "dcq_other", "h2_other")
+    store["query_fly"] = over_y(store["query1"])
     down.first("down0")
     up.second()
-    step(["outs1"], lambda: outof(1, store["o1"]), "dcross_other", "ca_other")
+    step(["outs1"], lambda: outof(1, "of", "o_s"), "dcross_other", "ca_other")
     step(
         ["dq0", "dk0", "dv0"],
         lambda: self_back(limit, q0, k0, v0, store["o0"], store["do0"], lse0),
@@ -1317,34 +1375,36 @@
     outs.over_y("outs1")
     up.far()
     down.second()
-    six = ("dq0", "dk0", "dv0", "dq1", "dk1", "dv1")
-    step(
-        ["yo"],
-        lambda: first_back(away, get(*six), w_qkv, qkv_first, qkv_second, ROUND),
-        "dq0",
-    )
+    nine = ("dq0", "dk0", "dv0", *yp)
+    weights = (w_qkv, qkv_first, qkv_second)
+    step(["yo"], lambda: first_back(away, get(*nine), weights, ROUND), "dq0")
     store["yo_fly"] = over_core(store["yo"])
     step(["qkv0"], lambda: qkv_grad(place, h1, get("dq0", "dk0", "dv0"), ROUND), "dq0")
     qkv.first("qkv0")
-    step(["into0"], lambda: into(0), "dcq")
-    cross_in.first("into0")
+    up.back()
+    step(["query0"], lambda: query(0), "dcq", "query_fly")
+    other_text = lax.dynamic_index_in_dim(text_states, 1 - side, keepdims=False)
+    texts = jnp.concatenate([text, other_text], axis=0)
+    pairs = jnp.concatenate(get("pair", "pair_y"), axis=1)
+    store["into0"] = jnp.concatenate(
+        [
+            lower(store["query0"].astype(FULL) + store["query_fly"].astype(FULL)),
+            lower(tn(texts, pairs[0])),
+            lower(tn(texts, pairs[1])),
+        ],
+        axis=0,
+    )
+    cross_in.first_alone("into0")
     down.far()
-    up.back()
-    step(["outs0"], lambda: outof(0, store["o0"]), "dcross")
+    step(["outs0"], lambda: outof(0, "o0"), "dcross")
+    up.along()
+    outs.first("outs0")
     qkv.second()
-    outs.first("outs0")
+    step(["ym"], lambda: first_back(place, get(*nine), weights, FULL), "dq0")
     cross_in.second()
-    step(
-        ["ym"],
-        lambda: first_back(place, get(*six), w_qkv, qkv_first, qkv_second, FULL),
-        "dq0",
-    )
+    qkv.far()
+    outs.second()
     down.back()
-    qkv.far()
-    up.along()
-    outs.second()
-    cross_in.far()
-    down.along()
     step(
         ["grad_frames", "first_sums"],
         lambda: frames_back(place, *get("ym", "yo_fly", "dx1"), frames, norm_gain),
@@ -1352,35 +1412,37 @@
         "yo_fly",
     )
     norms = Row("norms", store["sums"] + store["first_sums"], over_core)
+    up.end("grad_up")
+    cross_in.far()
+    down.along()
+    norms.then(over_y)
     qkv.back()
     outs.far()
-    norms.then(over_y)
-    up.end("grad_up")
-    norms.then(lambda v: along_wide(v, X_PAIRS))
+    norms.then(over_x)
     cross_in.back()
-    order("pair")
     text_part = 0.0
-    for g, weights in ((0, w_cross_kv), (1, cross_kv_y)):
-        for c in range(2):
-            text_part = text_part + nt(store["pair"][g, c], weights[c])
-    texts = Row("texts", text_part, over_core)
-    norms.then(lambda v: along_wide(v, Z_NEAR))
+    for c in range(2):
+        text_part = text_part + nt(pairs[c], w_cross_kv[c])
+    text_mine, text_theirs = text_part[:64], text_part[64:]
+    text_rows = Row("texts", text_mine, lambda v: over_y(text_theirs))
+    qkv.along()
+    norms.then(over_z)
     store["out_fly"] = over_core(out_o)
     outs.back()
+    text_rows.then(over_core)
     cross_in.along()
     norms.then(lambda v: along_wide(v, Z_FAR))
+    down.end("grad_down")
     order("texts_fly", "texts_kept")
-    text_grad = lower(texts.total())
+    text_grad = lower(text_rows.total())
     text_away = over_y(text_grad)
-    down.end("grad_down")
+    outs.along()
     order("out_fly", "x2")
     out_rows = lower(store["x2"] + out_m + store["out_fly"].astype(FULL))
-    qkv.along()
-    outs.along()
+    qkv.end("grad_qkv")
     grad_text = ordered(text_grad[None], text_away[None], side)
     cross_in.end("grad_in")
     sums = norms.total()
-    qkv.end("grad_qkv")
     outs.end("grad_outs")
     grad_in, grad_outs = get("grad_in", "grad_outs")
     return (

time: 554 us -> 642 us (1.16)
  waiting for transfers between devices: 123 us -> 174 us
  Pallas kernels: 253 us -> 274 us
  starting transfers between devices: 51.8 us -> 64.4 us
    ppermute x12 -> x16, waiting for transfers between devices: 18 us -> 49.2 us  [over_y(): return lax.ppermute(v, 'narrow', Y_PAIRS)]
    ppermute x33 -> x34, waiting for transfers between devices: 104 us -> 123 us  [along_wide(): return lax.ppermute(v, 'wide', pairs)]
    unnamed x198 -> x224, local copies, waits for them, and re-layouts: 16.5 us -> 28.8 us
    pallas_call x1, Pallas kernels: 21.2 us -> 29.1 us  [middle_forward(): pl.pallas_call(middle_forward_kernel, grid_spec=pltpu.PrefetchScalarGridS...]
    ppermute x33 -> x34, starting transfers between devices: 34.6 us -> 40.1 us  [along_wide(): return lax.ppermute(v, 'wide', pairs)]
    ppermute x12 -> x16, starting transfers between devices: 13.7 us -> 18.9 us  [over_y(): return lax.ppermute(v, 'narrow', Y_PAIRS)]
    pallas_call x2 -> x3, Pallas kernels: 28.7 us -> 31 us  [self_forward(): pl.pallas_call(functools.partial(self_forward_kernel, span=span, floor=fl...]
    convert_element_type x17 -> x16, other arithmetic: 22.8 us -> 20.6 us  [lower(): return values_in.astype(jnp.bfloat16)]
  transfers between devices with their start and end apart: 66 -> 77, of which waited for: 19 -> 21; matrix products, arithmetic and copies ran while one was open for 17% -> 13% of each run, Pallas kernels for 44% -> 37%
where the time goes in v8:
time: 642 us; the launch traced here: 632 us
  Pallas kernels  274 us (43%)
  waiting for transfers between devices  174 us (27%)
  starting transfers between devices  64.4 us (10%)
  other arithmetic  59.8 us (9%)
  local copies, waits for them, and re-layouts  54.4 us (8%)
    ppermute x34, waiting for transfers between devices, along_wide(): return lax.ppermute(v, 'wide', pairs)  123 us
    pallas_call x4, Pallas kernels, feed(): pl.pallas_call(functools.partial(feed_kernel, parts=parts, carried=len(be...  51.3 us
    ppermute x16, waiting for transfers between devices, over_y(): return lax.ppermute(v, 'narrow', Y_PAIRS)  49.2 us
    ppermute x34, starting transfers between devices, along_wide(): return lax.ppermute(v, 'wide', pairs)  40.1 us
    pallas_call x3, Pallas kernels, self_back(): pl.pallas_call(functools.partial(self_back_kernel, span=span, floor=floor...  39.1 us
    pallas_call x3, Pallas kernels, self_forward(): pl.pallas_call(functools.partial(self_forward_kernel, span=span, floor=fl...  31 us
    pallas_call x1, Pallas kernels, middle_forward(): pl.pallas_call(middle_forward_kernel, grid_spec=pltpu.PrefetchScalarGridS...  29.1 us
    unnamed x224, local copies, waits for them, and re-layouts  28.8 us
  transfers between devices with their start and end apart: 77, of which 21 were waited for; matrix products, arithmetic and copies ran while one was open for 13% of the time, Pallas kernels for 37%

profile of v8, /device:TPU:0, one launch (start us, length us, event | category | flops | bytes accessed | tf_op | source)
XLA Modules:
  0.0 631.8 jit_solution(1546751099470306036)
XLA Ops:
  1.2 2.1 constant_dynamic-slice_fusion.15
  3.2 2.6 collective-permute-start.1
  12.8 4.5 first_project.1
  20.1 4.1 collective-permute-done.1.weight_ref.refs_10_
  30.6 4.0 collective-permute-done.2.refs_7_.refs_0_
  36.3 3.8 collective-permute-done.3.refs_13_.refs_1_
  43.8 3.8 project.2
  50.0 14.3 %self_forward.3 = (bf16[1664,256]{1,0:T(8,128)(2,1)}, f32[2,8,1664]{2,1,0:T(8,128)}) custom-call(s32[1]{0:T(128)} %dynamic_slice.129.limit_ref, bf16[1664,256]{1,0:T(8,128)(2,1)} %copy-done.43, bf16[1664,256]{1,0:T(8,128)(2,1)} %copy-done.45, bf16[1664,256]{1,0:T(8,128)(2,1)} %copy-done.47), custom_call_target="tpu_custom_call" | custom-call | flops 1000 | bytes 1000 | tf_op jit(solution)/shard_map/self_forward/pallas_call | solution.py:524
  68.3 2.3 constant_dynamic-slice_fusion.10
  72.5 8.4 %self_forward.4 = (bf16[1664,128]{1,0:T(8,128)(2,1)}, f32[1,8,1664]{2,1,0:T(8,128)}) custom-call(s32[1]{0:T(128)} %dynamic_slice.129.limit_ref, bf16[1664,128]{1,0:T(8,128)(2,1)} %copy-done.51, bf16[1664,128]{1,0:T(8,128)(2,1)} %copy-done.53, bf16[1664,128]{1,0:T(8,128)(2,1)} %copy-done.55), custom_call_target="tpu_custom_call" | custom-call | flops 1000 | bytes 1000 | tf_op jit(solution)/shard_map/self_forward/pallas_call | solution.py:524
  85.7 3.8 project.3
  92.4 8.3 %self_forward.5 = (bf16[1664,128]{1,0:T(8,128)(2,1)}, f32[1,8,1664]{2,1,0:T(8,128)}) custom-call(s32[1]{0:T(128)} %dynamic_slice.129.limit_ref, bf16[1664,128]{1,0:T(8,128)(2,1)} %copy-done.57, bf16[1664,128]{1,0:T(8,128)(2,1)} %copy-done.59, bf16[1664,128]{1,0:T(8,128)(2,1)} %copy-done.61), custom_call_target="tpu_custom_call" | custom-call | flops 1000 | bytes 1000 | tf_op jit(solution)/shard_map/self_forward/pallas_call | solution.py:524
  108.9 29.1 %middle_forward.1 = (f32[832,1024]{1,0:T(8,128)}, f32[832,1024]{1,0:T(8,128)}, bf16[832,1024]{1,0:T(8,128)(2,1)}, bf16[832,1024]{1,0:T(8,128)(2,1)}, bf16[832,10...) custom-call(s32[3]{0:T(128)} %copy-done.71, bf16[832,1024]{1,0:T(8,128)(2,1)} %frame_ref.3, ...), custom_call_target="tpu_custom_call" | custom-call | flops 1000 | bytes 1000 | tf_op jit(solution)/shard_map/middle_forward/pallas_call | solution.py:673
  140.7 12.2 %feed.4 = (bf16[1664,1024]{1,0:T(8,128)(2,1)}, bf16[1664,1024]{1,0:T(8,128)(2,1)}, f32[832,1024]{1,0:T(8,128)}, f32[832,1024]{1,0:T(8,128)}) custom-call(s32[3]{0:T(128)} %copy-done.71, bf16[832,1024]{1,0:T(8,128)(2,1)} %get-tuple-element.305.h_ref.mine_ref, bf16[832,1024]{1,0:T(8,128)(2,1)} %copy-done, bf16[1024,1024]{1,0:T(8,128)(2,1)} %refs_0_.1, ...), custom_call_target="tpu_custom_call" | custom-call | flops 1000 | bytes 1000 | tf_op jit(solution)/shard_map/feed/pallas_call | solution.py:752
  154.7 12.2 %feed.5 = (bf16[1664,1024]{1,0:T(8,128)(2,1)}, bf16[1664,1024]{1,0:T(8,128)(2,1)}, f32[832,1024]{1,0:T(8,128)}, f32[832,1024]{1,0:T(8,128)}) custom-call(s32[3]{0:T(128)} %copy-done.71, bf16[832,1024]{1,0:T(8,128)(2,1)} %copy-done.7, bf16[832,1024]{1,0:T(8,128)(2,1)} %copy-done.5, ...), custom_call_target="tpu_custom_call", output_to_operand_aliasing={{0}: (5, {}), {1}: (6, {})} | custom-call | flops 1000 | bytes 1000 | tf_op jit(solution)/shard_map/feed/pallas_call | solution.py:752
  166.8 19.9 %collective-permute-done.28.refs_3_ = bf16[512,1024]{1,0:T(8,128)(2,1)} collective-permute-done((bf16[512,1024]{1,0:T(8,128)(2,1)S(1)}, bf16[512,1024]{1,0:T(8,128)(2,1)}, u32[]{:S(2)}, u32[]{:S(2)}) %collective-permute-start.28) | collective-permute-done | bytes 1048608 | tf_op jit(solution)/shard_map/ppermute | solution.py:1100
  186.7 13.4 %feed.6 = (bf16[1664,1024]{1,0:T(8,128)(2,1)}, bf16[1664,1024]{1,0:T(8,128)(2,1)}, bf16[832,1024]{1,0:T(8,128)(2,1)}, bf16[832,1024]{1,0:T(8,128)(2,1)}) custom-call(s32[3]{0:T(128)} %copy-done.71, bf16[832,1024]{1,0:T(8,128)(2,1)} %copy-done.7, bf16[832,1024]{1,0:T(8,128)(2,1)} %copy-done.5, bf16[1024,512]{1,0:T(8,128)(2,1)} %collective-permute-done.14.refs_0_, ...), custom_call_target="tpu_custom_call" | custom-call | flops 1000 | bytes 1000 | tf_op jit(solution)/shard_map/feed/pallas_call | solution.py:752
  200.2 13.6 %feed.7 = (bf16[1664,1024]{1,0:T(8,128)(2,1)}, bf16[1664,1024]{1,0:T(8,128)(2,1)}, f32[832,1024]{1,0:T(8,128)}, f32[832,1024]{1,0:T(8,128)}) custom-call(s32[3]{0:T(128)} %copy-done.71, bf16[832,1024]{1,0:T(8,128)(2,1)} %get-tuple-element.305.h_ref.mine_ref, bf16[832,1024]{1,0:T(8,128)(2,1)} %copy-done, ...), custom_call_target="tpu_custom_call", output_to_operand_aliasing={{0}: (9, {}), {1}: (10, {})} | custom-call | flops 1000 | bytes 1000 | tf_op jit(solution)/shard_map/feed/pallas_call | solution.py:752
  215.2 7.3 %up_grad.2 = bf16[1024,1024]{1,0:T(8,128)(2,1)} custom-call(bf16[832,1024]{1,0:T(8,128)(2,1)S(1)} %copy-done.4, bf16[832,1024]{1,0:T(8,128)(2,1)S(1)} %copy-done.8, bf16[1664,1024]{1,0:T(8,128)(2,1)} %get-tuple-element.329.du_ref), custom_call_target="tpu_custom_call" | custom-call | flops 1000 | bytes 1000 | tf_op jit(solution)/shard_map/up_grad/pallas_call | solution.py:782
  222.5 7.2 %down_grad.2 = bf16[1024,1024]{1,0:T(8,128)(2,1)} custom-call(bf16[1664,1024]{1,0:T(8,128)(2,1)} %get-tuple-element.330.g_ref, bf16[832,1024]{1,0:T(8,128)(2,1)S(1)} %copy-done.1, bf16[832,1024]{1,0:T(8,128)(2,1)S(1)} %copy-done.6), custom_call_target="tpu_custom_call" | custom-call | flops 1000 | bytes 1000 | tf_op jit(solution)/shard_map/down_grad/pallas_call | solution.py:805
  229.8 27.4 %middle_back.1 = (f32[832,1024]{1,0:T(8,128)}, bf16[832,1024]{1,0:T(8,128)(2,1)}, bf16[832,1024]{1,0:T(8,128)(2,1)}, bf16[832,1024]{1,0:T(8,128)(2,1)}, f32[4,64...) custom-call(s32[3]{0:T(128)} %copy-done.71, f32[832,1024]{1,0:T(8,128)} %get-tuple-element.333.ym_ref, ...), custom_call_target="tpu_custom_call" | custom-call | flops 1000 | bytes 1000 | tf_op jit(solution)/shard_map/middle_back/pallas_call | solution.py:993
  258.0 6.3 %up_grad.3 = bf16[1024,1024]{1,0:T(8,128)(2,1)S(1)} custom-call(bf16[832,1024]{1,0:T(8,128)(2,1)S(1)} %copy-done.4, bf16[832,1024]{1,0:T(8,128)(2,1)S(1)} %copy-done.9, bf16[1664,1024]{1,0:T(8,128)(2,1)} %get-tuple-element.341.du_ref), custom_call_target="tpu_custom_call" | custom-call | flops 1000 | bytes 1000 | tf_op jit(solution)/shard_map/up_grad/pallas_call | solution.py:782
  276.1 4.9 pull.1
  282.0 9.6 %self_back.3 = (bf16[1664,128]{1,0:T(8,128)(2,1)S(1)}, bf16[1664,128]{1,0:T(8,128)(2,1)S(1)}, bf16[1664,128]{1,0:T(8,128)(2,1)S(1)}) custom-call(s32[1]{0:T(128)} %dynamic_slice.129.limit_ref, bf16[1664,128]{1,0:T(8,128)(2,1)S(1)} %copy-done.52, bf16[1664,128]{1,0:T(8,128)(2,1)S(1)} %copy-done.54, bf16[1664,128]{1,0:T(8,128)(2,1)S(1)} %copy-done.56, ...), custom_call_target="tpu_custom_call" | custom-call | flops 1000 | bytes 1000 | tf_op jit(solution)/shard_map/self_back/pallas_call | solution.py:605
  291.7 9.6 %self_back.4 = (bf16[1664,128]{1,0:T(8,128)(2,1)S(1)}, bf16[1664,128]{1,0:T(8,128)(2,1)S(1)}, bf16[1664,128]{1,0:T(8,128)(2,1)S(1)}) custom-call(s32[1]{0:T(128)} %dynamic_slice.129.limit_ref, bf16[1664,128]{1,0:T(8,128)(2,1)S(1)} %copy-done.58, bf16[1664,128]{1,0:T(8,128)(2,1)S(1)} %copy-done.60, bf16[1664,128]{1,0:T(8,128)(2,1)S(1)} %copy-done.62, ...), custom_call_target="tpu_custom_call" | custom-call | flops 1000 | bytes 1000 | tf_op jit(solution)/shard_map/self_back/pallas_call | solution.py:605
  301.4 5.2 collective-permute-done.36
  306.5 4.3 convert_add_fusion.3
  315.0 6.7 %down_grad.3 = bf16[1024,1024]{1,0:T(8,128)(2,1)S(1)} custom-call(bf16[1664,1024]{1,0:T(8,128)(2,1)} %get-tuple-element.367.g_ref, bf16[832,1024]{1,0:T(8,128)(2,1)S(1)} %copy-done.2, bf16[832,1024]{1,0:T(8,128)(2,1)S(1)} %copy-done.6), custom_call_target="tpu_custom_call" | custom-call | flops 1000 | bytes 1000 | tf_op jit(solution)/shard_map/down_grad/pallas_call | solution.py:805
  321.7 30.2 %collective-permute-done.39 = bf16[2,64,256]{2,1,0:T(8,128)(2,1)S(1)} collective-permute-done((bf16[2,64,256]{2,1,0:T(8,128)(2,1)S(1)}, bf16[2,64,256]{2,1,0:T(8,128)(2,1)S(1)}, u32[]{:S(2)}, u32[]{:S(2)}) %collective-permute-start.39) | collective-permute-done | bytes 65568 | tf_op jit(solution)/shard_map/ppermute | solution.py:1097
  351.9 7.3 %qkv_grad.2 = bf16[3072,256]{1,0:T(8,128)(2,1)} custom-call(s32[3]{0:T(128)S(1)} %copy-done.72, bf16[1664,1024]{1,0:T(8,128)(2,1)} %copy-done.3, bf16[1664,128]{1,0:T(8,128)(2,1)S(1)} %get-tuple-element.371.refs_0_.refs_3_, bf16[1664,128]{1,0:T(8,128)(2,1)S(1)} %get-tuple-element.372.refs_1_.refs_4_, ...), custom_call_target="tpu_custom_call" | custom-call | flops 1000 | bytes 1000 | tf_op jit(solution)/shard_map/qkv_grad/pallas_call | solution.py:842
  359.5 4.0 query_grad.2
  363.5 4.2 add_convert_fusion.1
  377.3 6.0 outputs_grad.2
  383.3 19.9 %self_back.5 = (bf16[1664,256]{1,0:T(8,128)(2,1)S(1)}, bf16[1664,256]{1,0:T(8,128)(2,1)S(1)}, bf16[1664,256]{1,0:T(8,128)(2,1)S(1)}) custom-call(s32[1]{0:T(128)} %dynamic_slice.129.limit_ref, bf16[1664,256]{1,0:T(8,128)(2,1)S(1)} %copy-done.44, bf16[1664,256]{1,0:T(8,128)(2,1)S(1)} %copy-done.46, bf16[1664,256]{1,0:T(8,128)(2,1)S(1)} %copy-done.48, ...), custom_call_target="tpu_custom_call" | custom-call | flops 1000 | bytes 1000 | tf_op jit(solution)/shard_map/self_back/pallas_call | solution.py:605
  404.1 2.7 collective-permute-start.43
  411.2 6.5 %first_back.2 = bf16[832,1024]{1,0:T(8,128)(2,1)S(1)} custom-call(s32[3]{0:T(128)S(1)} %add_add_fusion.1.place_ref, bf16[1664,256]{1,0:T(8,128)(2,1)S(1)} %get-tuple-element.426.refs_0_, bf16[1664,256]{1,0:T(8,128)(2,1)S(1)} %get-tuple-element.400.refs_1_, bf16[1664,256]{1,0:T(8,128)(2,1)S(1)} %get-tuple-element.401.refs_2_, ...), custom_call_target="tpu_custom_call" | custom-call | flops 1000 | bytes 1000 | tf_op jit(solution)/shard_map/first_back/pallas_call | solution.py:1027
  418.9 5.9 qkv_grad.3
  424.8 2.1 dynamic-slice_convert_fusion
  427.6 3.2 add_convert_fusion.3
  434.1 4.0 query_grad.3
  442.5 2.0 add_convert_fusion.6
  444.5 5.0 outputs_grad.3
  449.5 19.5 %collective-permute-done.46 = bf16[256,1024]{1,0:T(8,128)(2,1)} collective-permute-done((bf16[256,1024]{1,0:T(8,128)(2,1)S(1)}, bf16[256,1024]{1,0:T(8,128)(2,1)}, u32[]{:S(2)}, u32[]{:S(2)}) %collective-permute-start.46) | collective-permute-done | bytes 524320 | tf_op jit(solution)/shard_map/ppermute | solution.py:1100
  469.6 2.6 maximum_select_fusion.4
  477.5 6.3 first_back.3.ym_ref
  483.8 8.9 %collective-permute-done.52 = bf16[1536,256]{1,0:T(8,128)(2,1)S(1)} collective-permute-done((bf16[1536,256]{1,0:T(8,128)(2,1)S(1)}, bf16[1536,256]{1,0:T(8,128)(2,1)S(1)}, u32[]{:S(2)}, u32[]{:S(2)}) %collective-permute-start.52) | collective-permute-done | bytes 786464 | tf_op jit(solution)/shard_map/ppermute | solution.py:1100
  494.3 16.8 %collective-permute-done.51 = bf16[768,256]{1,0:T(8,128)(2,1)S(1)} collective-permute-done((bf16[768,256]{1,0:T(8,128)(2,1)S(1)}, bf16[768,256]{1,0:T(8,128)(2,1)S(1)}, u32[]{:S(2)}, u32[]{:S(2)}) %collective-permute-start.51) | collective-permute-done | bytes 393248 | tf_op jit(solution)/shard_map/ppermute | solution.py:1100
  512.5 2.7 collective-permute-start.59
  517.8 5.9 frames_back.1
  523.8 11.5 %collective-permute-done.60 = bf16[512,1024]{1,0:T(8,128)(2,1)S(1)} collective-permute-done((bf16[512,1024]{1,0:T(8,128)(2,1)}, bf16[512,1024]{1,0:T(8,128)(2,1)S(1)}, u32[]{:S(2)}, u32[]{:S(2)}) %collective-permute-start.60) | collective-permute-done | bytes 1048608 | tf_op jit(solution)/shard_map/ppermute | solution.py:1100
  535.3 2.6 collective-permute-start.53
  537.9 4.4 fusion
  542.3 2.5 collective-permute-done.58
  547.5 2.7 collective-permute-done.53
  550.9 2.3 collective-permute-start.61
  553.1 17.0 %collective-permute-done.64 = bf16[768,256]{1,0:T(8,128)(2,1)S(1)} collective-permute-done((bf16[768,256]{1,0:T(8,128)(2,1)S(1)}, bf16[768,256]{1,0:T(8,128)(2,1)S(1)}, u32[]{:S(2)}, u32[]{:S(2)}) %collective-permute-start.64) | collective-permute-done | bytes 393248 | tf_op jit(solution)/shard_map/ppermute | solution.py:1100
  571.3 6.4 %collective-permute-done.65 = bf16[768,256]{1,0:T(8,128)(2,1)S(1)} collective-permute-done((bf16[768,256]{1,0:T(8,128)(2,1)S(1)}, bf16[768,256]{1,0:T(8,128)(2,1)S(1)}, u32[]{:S(2)}, u32[]{:S(2)}) %collective-permute-start.65) | collective-permute-done | bytes 393248 | tf_op jit(solution)/shard_map/ppermute | solution.py:1100
  580.0 2.1 collective-permute-start.71
  584.1 5.7 collective-permute-done.69
  593.2 2.9 fusion.1
  598.7 10.9 %collective-permute-done.73 = f32[8,1024]{1,0:T(8,128)S(1)} collective-permute-done((f32[8,1024]{1,0:T(8,128)S(1)}, f32[8,1024]{1,0:T(8,128)S(1)}, u32[]{:S(2)}, u32[]{:S(2)}) %collective-permute-start.73) | collective-permute-done | bytes 32800 | tf_op jit(solution)/shard_map/ppermute | solution.py:1100
  614.7 4.7 add_convert_fusion
  619.3 3.9 fusion.2
  623.9 2.2 fusion.3
  (437 shorter events, 131.2 us)
Async XLA Ops:
  3.2 21.0 %collective-permute-start.1 = (bf16[3,1024,128]{2,1,0:T(8,128)(2,1)}, bf16[3,1024,128]{2,1,0:T(8,128)(2,1)}, u32[]{:S(2)}, u32[]{:S(2)}) collective-permute-start(bf16[3,1024,128]{2,1,0:T(8,128)(2,1)} %constant_dynamic-slice_fusion.15), channel_id=1, source_target_pairs={{0,2},{2,0},{1,3},{3,1},{4,6},{6,4},{5,7},{7,5},{8,10},{10,8},{9,1... | collective-permute-start | bytes 2359304 | tf_op jit(solution)/shard_map/ppermute | solution.py:1097
  25.2 39.0 %collective-permute-start.5 = (bf16[256,1024]{1,0:T(8,128)(2,1)}, bf16[256,1024]{1,0:T(8,128)(2,1)}, u32[]{:S(2)}, u32[]{:S(2)}) collective-permute-start(bf16[256,1024]{1,0:T(8,128)(2,1)} %refs_2_), channel_id=1, source_target_pairs={{0,1},{1,0},{2,3},{3,2},{4,5},{5,4},{6,7},{7,6},{8,9},{9,8},{10,11... | collective-permute-start | bytes 1572872 | tf_op jit(solution)/shard_map/ppermute | solution.py:1094
  25.3 9.3 %collective-permute-start.2 = (bf16[128,1024]{1,0:T(8,128)(2,1)S(1)}, bf16[128,1024]{1,0:T(8,128)(2,1)}, u32[]{:S(2)}, u32[]{:S(2)}) collective-permute-start(bf16[128,1024]{1,0:T(8,128)(2,1)S(1)} %constant_dynamic-slice_fusion.14), channel_id=1, source_target_pairs={{0,2},{2,0},{1,3},{3,1},{4,6},{6,4},{5,7},{7,5},{8,10},{10,8},{9,1... | collective-permute-start | bytes 786440 | tf_op jit(solution)/shard_map/ppermute | solution.py:1097
  27.1 37.1 %collective-permute-start.6 = (bf16[1024,256]{1,0:T(8,128)(2,1)}, bf16[1024,256]{1,0:T(8,128)(2,1)}, u32[]{:S(2)}, u32[]{:S(2)}) collective-permute-start(bf16[1024,256]{1,0:T(8,128)(2,1)} %refs_0_.2), channel_id=1, source_target_pairs={{0,1},{1,0},{2,3},{3,2},{4,5},{5,4},{6,7},{7,6},{8,9},{9,8},{10,11... | collective-permute-start | bytes 1572872 | tf_op jit(solution)/shard_map/ppermute | solution.py:1094
  27.3 37.0 %collective-permute-start.7 = (bf16[256,1024]{1,0:T(8,128)(2,1)}, bf16[256,1024]{1,0:T(8,128)(2,1)}, u32[]{:S(2)}, u32[]{:S(2)}) collective-permute-start(bf16[256,1024]{1,0:T(8,128)(2,1)} %refs_6_.1), channel_id=1, source_target_pairs={{0,1},{1,0},{2,3},{3,2},{4,5},{5,4},{6,7},{7,6},{8,9},{9,8},{10,11... | collective-permute-start | bytes 1572872 | tf_op jit(solution)/shard_map/ppermute | solution.py:1094
  28.6 11.5 %collective-permute-start.3 = (bf16[1024,128]{1,0:T(8,128)(2,1)S(1)}, bf16[1024,128]{1,0:T(8,128)(2,1)S(1)}, u32[]{:S(2)}, u32[]{:S(2)}) collective-permute-start(bf16[1024,128]{1,0:T(8,128)(2,1)S(1)} %constant_dynamic-slice_fusion.13), channel_id=1, source_target_pairs={{0,2},{2,0},{1,3},{3,1},{4,6},{6,4},{5,7},{7,5},{8,10},{10,8},{9,1... | collective-permute-start | bytes 786440 | tf_op jit(solution)/shard_map/ppermute | solution.py:1097
  34.6 29.6 %collective-permute-start.4 = (bf16[128,1024]{1,0:T(8,128)(2,1)}, bf16[128,1024]{1,0:T(8,128)(2,1)}, u32[]{:S(2)}, u32[]{:S(2)}) collective-permute-start(bf16[128,1024]{1,0:T(8,128)(2,1)} %constant_dynamic-slice_fusion.12), channel_id=1, source_target_pairs={{0,2},{2,0},{1,3},{3,1},{4,6},{6,4},{5,7},{7,5},{8,10},{10,8},{9,1... | collective-permute-start | bytes 786440 | tf_op jit(solution)/shard_map/ppermute | solution.py:1097
  40.8 41.9 %collective-permute-start.8 = (bf16[3,1024,128]{2,1,0:T(8,128)(2,1)}, bf16[3,1024,128]{2,1,0:T(8,128)(2,1)}, u32[]{:S(2)}, u32[]{:S(2)}) collective-permute-start(bf16[3,1024,128]{2,1,0:T(8,128)(2,1)} %collective-permute-done.1.weight_ref.refs_10_), channel_id=1, source_target_pairs={{0,8},{4,12},{8,0},{12,4},{16,24},{20,28},{24,16},{28,20},{1,9},{5... | collective-permute-start | bytes 2359304 | tf_op jit(solution)/shard_map/ppermute | solution.py:1100
  66.1 16.9 %collective-permute-start.10 = (bf16[832,256]{1,0:T(8,128)(2,1)}, bf16[832,256]{1,0:T(8,128)(2,1)}, u32[]{:S(2)}, u32[]{:S(2)}) collective-permute-start(bf16[832,256]{1,0:T(8,128)(2,1)} %constant_dynamic-slice_fusion.11), channel_id=1, source_target_pairs={{0,1},{1,0},{2,3},{3,2},{4,5},{5,4},{6,7},{7,6},{8,9},{9,8},{10,11... | collective-permute-start | bytes 1277960 | tf_op jit(solution)/shard_map/ppermute | solution.py:1094
  66.7 14.2 %collective-permute-start.9 = (bf16[2,64,256]{2,1,0:T(8,128)(2,1)}, bf16[2,64,256]{2,1,0:T(8,128)(2,1)S(1)}, u32[]{:S(2)}, u32[]{:S(2)}) collective-permute-start(bf16[2,64,256]{2,1,0:T(8,128)(2,1)} %get-tuple-element.535), channel_id=1, source_target_pairs={{0,2},{2,0},{1,3},{3,1},{4,6},{6,4},{5,7},{7,5},{8,10},{10,8},{9,1... | collective-permute-start | bytes 196616 | tf_op jit(solution)/shard_map/ppermute | solution.py:1097
  70.5 30.2 %collective-permute-start.14 = (bf16[1024,512]{1,0:T(8,128)(2,1)}, bf16[1024,512]{1,0:T(8,128)(2,1)}, u32[]{:S(2)}, u32[]{:S(2)}) collective-permute-start(bf16[1024,512]{1,0:T(8,128)(2,1)} %constant_dynamic-slice_fusion.10), channel_id=1, source_target_pairs={{0,2},{2,0},{1,3},{3,1},{4,6},{6,4},{5,7},{7,5},{8,10},{10,8},{9,1... | collective-permute-start | bytes 3145736 | tf_op jit(solution)/shard_map/ppermute | solution.py:1097
  72.3 11.8 %collective-permute-start.11 = (bf16[128,1024]{1,0:T(8,128)(2,1)}, bf16[128,1024]{1,0:T(8,128)(2,1)S(1)}, u32[]{:S(2)}, u32[]{:S(2)}) collective-permute-start(bf16[128,1024]{1,0:T(8,128)(2,1)} %collective-permute-done.2.refs_7_.refs_0_), channel_id=1, source_target_pairs={{0,8},{4,12},{8,0},{12,4},{16,24},{20,28},{24,16},{28,20},{1,9},{5... | collective-permute-start | bytes 786440 | tf_op jit(solution)/shard_map/ppermute | solution.py:1100
  81.0 19.7 %collective-permute-start.12 = (bf16[1024,128]{1,0:T(8,128)(2,1)}, bf16[1024,128]{1,0:T(8,128)(2,1)S(1)}, u32[]{:S(2)}, u32[]{:S(2)}) collective-permute-start(bf16[1024,128]{1,0:T(8,128)(2,1)} %copy-done.88), channel_id=1, source_target_pairs={{0,4},{4,0},{8,12},{12,8},{16,20},{20,16},{24,28},{28,24},{1,5},{5... | collective-permute-start | bytes 786440 | tf_op jit(solution)/shard_map/ppermute | solution.py:1100
  82.8 17.9 %collective-permute-start.13 = (bf16[128,1024]{1,0:T(8,128)(2,1)}, bf16[128,1024]{1,0:T(8,128)(2,1)S(1)}, u32[]{:S(2)}, u32[]{:S(2)}) collective-permute-start(bf16[128,1024]{1,0:T(8,128)(2,1)} %collective-permute-done.4.refs_19_.refs_7_), channel_id=1, source_target_pairs={{0,4},{4,0},{8,12},{12,8},{16,20},{20,16},{24,28},{28,24},{1,5},{5... | collective-permute-start | bytes 786440 | tf_op jit(solution)/shard_map/ppermute | solution.py:1100
  83.9 16.8 %collective-permute-start.16 = (bf16[832,128]{1,0:T(8,128)(2,1)S(1)}, bf16[832,128]{1,0:T(8,128)(2,1)S(1)}, u32[]{:S(2)}, u32[]{:S(2)}) collective-permute-start(bf16[832,128]{1,0:T(8,128)(2,1)S(1)} %constant_dynamic-slice_fusion.7), channel_id=1, source_target_pairs={{0,1},{1,0},{2,3},{3,2},{4,5},{5,4},{6,7},{7,6},{8,9},{9,8},{10,11... | collective-permute-start | bytes 638984 | tf_op jit(solution)/shard_map/ppermute | solution.py:1094
  84.1 16.6 %collective-permute-start.15 = (bf16[2,2,64,256]{3,2,1,0:T(8,128)(2,1)S(1)}, bf16[2,2,64,256]{3,2,1,0:T(8,128)(2,1)S(1)}, u32[]{:S(2)}, u32[]{:S(2)}) collective-permute-start(bf16[2,2,64,256]{3,2,1,0:T(8,128)(2,1)S(1)} %pad_maximum_fusion.6), channel_id=1, source_target_pairs={{0,1},{1,0},{2,3},{3,2},{4,5},{5,4},{6,7},{7,6},{8,9},{9,8},{10,11... | collective-permute-start | bytes 393224 | tf_op jit(solution)/shard_map/ppermute | solution.py:1094
  100.7 37.3 %collective-permute-start.24 = (bf16[512,1024]{1,0:T(8,128)(2,1)}, bf16[512,1024]{1,0:T(8,128)(2,1)S(1)}, u32[]{:S(2)}, u32[]{:S(2)}) collective-permute-start(bf16[512,1024]{1,0:T(8,128)(2,1)} %constant_dynamic-slice_fusion.9), channel_id=1, source_target_pairs={{0,2},{2,0},{1,3},{3,1},{4,6},{6,4},{5,7},{7,5},{8,10},{10,8},{9,1... | collective-permute-start | bytes 3145736 | tf_op jit(solution)/shard_map/ppermute | solution.py:1097
  138.1 14.8 %collective-permute-start.25 = (bf16[832,1024]{1,0:T(8,128)(2,1)}, bf16[832,1024]{1,0:T(8,128)(2,1)S(1)}, u32[]{:S(2)}, u32[]{:S(2)}) collective-permute-start(bf16[832,1024]{1,0:T(8,128)(2,1)} %get-tuple-element.305.h_ref.mine_ref), channel_id=1, source_target_pairs={{0,1},{1,0},{2,3},{3,2},{4,5},{5,4},{6,7},{7,6},{8,9},{9,8},{10,11... | collective-permute-start | bytes 5111816 | tf_op jit(solution)/shard_map/ppermute | solution.py:1094
  138.4 14.5 %collective-permute-start.26 = (bf16[832,1024]{1,0:T(8,128)(2,1)S(1)}, bf16[832,1024]{1,0:T(8,128)(2,1)S(1)}, u32[]{:S(2)}, u32[]{:S(2)}) collective-permute-start(bf16[832,1024]{1,0:T(8,128)(2,1)S(1)} %broadcast_select_fusion.d_ref.mine_ref), channel_id=1, source_target_pairs={{0,1},{1,0},{2,3},{3,2},{4,5},{5,4},{6,7},{7,6},{8,9},{9,8},{10,11... | collective-permute-start | bytes 5111816 | tf_op jit(solution)/shard_map/ppermute | solution.py:1094
  138.6 28.2 %collective-permute-start.27 = (bf16[1024,512]{1,0:T(8,128)(2,1)}, bf16[1024,512]{1,0:T(8,128)(2,1)}, u32[]{:S(2)}, u32[]{:S(2)}) collective-permute-start(bf16[1024,512]{1,0:T(8,128)(2,1)} %collective-permute-done.14.refs_0_), channel_id=1, source_target_pairs={{0,4},{4,0},{8,12},{12,8},{16,20},{20,16},{24,28},{28,24},{1,5},{5... | collective-permute-start | bytes 3145736 | tf_op jit(solution)/shard_map/ppermute | solution.py:1100
  140.1 46.6 %collective-permute-start.28 = (bf16[512,1024]{1,0:T(8,128)(2,1)S(1)}, bf16[512,1024]{1,0:T(8,128)(2,1)}, u32[]{:S(2)}, u32[]{:S(2)}) collective-permute-start(bf16[512,1024]{1,0:T(8,128)(2,1)S(1)} %collective-permute-done.24.refs_2_), channel_id=1, source_target_pairs={{0,4},{4,0},{8,12},{12,8},{16,20},{20,16},{24,28},{28,24},{1,5},{5... | collective-permute-start | bytes 3145736 | tf_op jit(solution)/shard_map/ppermute | solution.py:1100
  200.1 29.6 %collective-permute-start.30 = (bf16[832,1024]{1,0:T(8,128)(2,1)}, bf16[832,1024]{1,0:T(8,128)(2,1)}, u32[]{:S(2)}, u32[]{:S(2)}) collective-permute-start(bf16[832,1024]{1,0:T(8,128)(2,1)} %get-tuple-element.319), channel_id=1, source_target_pairs={{0,1},{1,0},{2,3},{3,2},{4,5},{5,4},{6,7},{7,6},{8,9},{9,8},{10,11... | collective-permute-start | bytes 5111816 | tf_op jit(solution)/shard_map/ppermute | solution.py:1094
  257.2 8.5 %collective-permute-start.31 = (bf16[832,1024]{1,0:T(8,128)(2,1)}, bf16[832,1024]{1,0:T(8,128)(2,1)S(1)}, u32[]{:S(2)}, u32[]{:S(2)}) collective-permute-start(bf16[832,1024]{1,0:T(8,128)(2,1)} %get-tuple-element.342.mine_ref.refs_2_.refs_1_), channel_id=1, source_target_pairs={{0,1},{1,0},{2,3},{3,2},{4,5},{5,4},{6,7},{7,6},{8,9},{9,8},{10,11... | collective-permute-start | bytes 5111816 | tf_op jit(solution)/shard_map/ppermute | solution.py:1094
  257.7 48.8 %collective-permute-start.36 = (bf16[1024,1024]{1,0:T(8,128)(2,1)}, bf16[1024,1024]{1,0:T(8,128)(2,1)}, u32[]{:S(2)}, u32[]{:S(2)}) collective-permute-start(bf16[1024,1024]{1,0:T(8,128)(2,1)} %up_grad.2), channel_id=1, source_target_pairs={{0,2},{2,0},{1,3},{3,1},{4,6},{6,4},{5,7},{7,5},{8,10},{10,8},{9,1... | collective-permute-start | bytes 6291464 | tf_op jit(solution)/shard_map/ppermute | solution.py:1097
  266.8 24.8 %collective-permute-start.32 = (bf16[832,1024]{1,0:T(8,128)(2,1)}, bf16[832,1024]{1,0:T(8,128)(2,1)}, u32[]{:S(2)}, u32[]{:S(2)}) collective-permute-start(bf16[832,1024]{1,0:T(8,128)(2,1)} %get-tuple-element.414.refs_6_.refs_5_), channel_id=1, source_target_pairs={{0,1},{1,0},{2,3},{3,2},{4,5},{5,4},{6,7},{7,6},{8,9},{9,8},{10,11... | collective-permute-start | bytes 5111816 | tf_op jit(solution)/shard_map/ppermute | solution.py:1094
  266.8 96.7 %collective-permute-start.38 = (bf16[1024,1024]{1,0:T(8,128)(2,1)}, bf16[1024,1024]{1,0:T(8,128)(2,1)}, u32[]{:S(2)}, u32[]{:S(2)}) collective-permute-start(bf16[1024,1024]{1,0:T(8,128)(2,1)} %down_grad.2), channel_id=1, source_target_pairs={{0,2},{2,0},{1,3},{3,1},{4,6},{6,4},{5,7},{7,5},{8,10},{10,8},{9,1... | collective-permute-start | bytes 6291464 | tf_op jit(solution)/shard_map/ppermute | solution.py:1097
  269.6 22.0 %collective-permute-start.33 = (bf16[832,512]{1,0:T(8,128)(2,1)}, bf16[832,512]{1,0:T(8,128)(2,1)}, u32[]{:S(2)}, u32[]{:S(2)}) collective-permute-start(bf16[832,512]{1,0:T(8,128)(2,1)} %slice.78), channel_id=1, source_target_pairs={{0,1},{1,0},{2,3},{3,2},{4,5},{5,4},{6,7},{7,6},{8,9},{9,8},{10,11... | collective-permute-start | bytes 2555912 | tf_op jit(solution)/shard_map/ppermute | solution.py:1094
  272.5 86.7 %collective-permute-start.40 = (bf16[832,1024]{1,0:T(8,128)(2,1)}, bf16[832,1024]{1,0:T(8,128)(2,1)}, u32[]{:S(2)}, u32[]{:S(2)}) collective-permute-start(bf16[832,1024]{1,0:T(8,128)(2,1)} %get-tuple-element.369.mine_ref), channel_id=1, source_target_pairs={{0,1},{1,0},{2,3},{3,2},{4,5},{5,4},{6,7},{7,6},{8,9},{9,8},{10,11... | collective-permute-start | bytes 5111816 | tf_op jit(solution)/shard_map/ppermute | solution.py:1094
  310.8 59.3 %collective-permute-start.37 = (bf16[512,1024]{1,0:T(8,128)(2,1)}, bf16[512,1024]{1,0:T(8,128)(2,1)}, u32[]{:S(2)}, u32[]{:S(2)}) collective-permute-start(bf16[512,1024]{1,0:T(8,128)(2,1)} %get-tuple-element.515), channel_id=1, source_target_pairs={{0,4},{4,0},{8,12},{12,8},{16,20},{20,16},{24,28},{28,24},{1,5},{5... | collective-permute-start | bytes 3145736 | tf_op jit(solution)/shard_map/ppermute | solution.py:1100
  313.3 38.5 %collective-permute-start.39 = (bf16[2,64,256]{2,1,0:T(8,128)(2,1)S(1)}, bf16[2,64,256]{2,1,0:T(8,128)(2,1)S(1)}, u32[]{:S(2)}, u32[]{:S(2)}) collective-permute-start(bf16[2,64,256]{2,1,0:T(8,128)(2,1)S(1)} %maximum_select_fusion.12), channel_id=1, source_target_pairs={{0,2},{2,0},{1,3},{3,1},{4,6},{6,4},{5,7},{7,5},{8,10},{10,8},{9,1... | collective-permute-start | bytes 196616 | tf_op jit(solution)/shard_map/ppermute | solution.py:1097
  314.0 298.6 %collective-permute-start.29 = (bf16[832,1024]{1,0:T(8,128)(2,1)}, bf16[832,1024]{1,0:T(8,128)(2,1)}, u32[]{:S(2)}, u32[]{:S(2)}) collective-permute-start(bf16[832,1024]{1,0:T(8,128)(2,1)} %get-tuple-element.318), channel_id=1, source_target_pairs={{0,1},{1,0},{2,3},{3,2},{4,5},{5,4},{6,7},{7,6},{8,9},{9,8},{10,11... | collective-permute-start | bytes 5111816 | tf_op jit(solution)/shard_map/ppermute | solution.py:1094
  351.9 23.8 %collective-permute-start.35 = (bf16[832,512]{1,0:T(8,128)(2,1)}, bf16[832,512]{1,0:T(8,128)(2,1)S(1)}, u32[]{:S(2)}, u32[]{:S(2)}) collective-permute-start(bf16[832,512]{1,0:T(8,128)(2,1)} %slice.81), channel_id=1, source_target_pairs={{0,1},{1,0},{2,3},{3,2},{4,5},{5,4},{6,7},{7,6},{8,9},{9,8},{10,11... | collective-permute-start | bytes 2555912 | tf_op jit(solution)/shard_map/ppermute | solution.py:1094
  359.2 67.8 %collective-permute-start.45 = (bf16[3072,256]{1,0:T(8,128)(2,1)}, bf16[3072,256]{1,0:T(8,128)(2,1)}, u32[]{:S(2)}, u32[]{:S(2)}) collective-permute-start(bf16[3072,256]{1,0:T(8,128)(2,1)} %qkv_grad.2), channel_id=1, source_target_pairs={{0,2},{2,0},{1,3},{3,1},{4,6},{6,4},{5,7},{7,5},{8,10},{10,8},{9,1... | collective-permute-start | bytes 4718600 | tf_op jit(solution)/shard_map/ppermute | solution.py:1097
  367.7 36.4 %collective-permute-start.44 = (bf16[512,1024]{1,0:T(8,128)(2,1)}, bf16[512,1024]{1,0:T(8,128)(2,1)}, u32[]{:S(2)}, u32[]{:S(2)}) collective-permute-start(bf16[512,1024]{1,0:T(8,128)(2,1)} %get-tuple-element.512), channel_id=1, source_target_pairs={{0,4},{4,0},{8,12},{12,8},{16,20},{20,16},{24,28},{28,24},{1,5},{5... | collective-permute-start | bytes 3145736 | tf_op jit(solution)/shard_map/ppermute | solution.py:1100
  371.8 31.4 %collective-permute-start.42 = (bf16[256,1024]{1,0:T(8,128)(2,1)S(1)}, bf16[256,1024]{1,0:T(8,128)(2,1)S(1)}, u32[]{:S(2)}, u32[]{:S(2)}) collective-permute-start(bf16[256,1024]{1,0:T(8,128)(2,1)S(1)} %dynamic-slice_convert_fusion.1), channel_id=1, source_target_pairs={{0,8},{4,12},{8,0},{12,4},{16,24},{20,28},{24,16},{28,20},{1,9},{5... | collective-permute-start | bytes 1572872 | tf_op jit(solution)/shard_map/ppermute | solution.py:1100
  375.7 57.7 %collective-permute-start.47 = (bf16[1024,256]{1,0:T(8,128)(2,1)S(1)}, bf16[1024,256]{1,0:T(8,128)(2,1)}, u32[]{:S(2)}, u32[]{:S(2)}) collective-permute-start(bf16[1024,256]{1,0:T(8,128)(2,1)S(1)} %query_grad.2), channel_id=1, source_target_pairs={{0,2},{2,0},{1,3},{3,1},{4,6},{6,4},{5,7},{7,5},{8,10},{10,8},{9,1... | collective-permute-start | bytes 1572872 | tf_op jit(solution)/shard_map/ppermute | solution.py:1097
  403.3 69.0 %collective-permute-start.41 = (bf16[512,1024]{1,0:T(8,128)(2,1)}, bf16[512,1024]{1,0:T(8,128)(2,1)}, u32[]{:S(2)}, u32[]{:S(2)}) collective-permute-start(bf16[512,1024]{1,0:T(8,128)(2,1)} %outputs_grad.2), channel_id=1, source_target_pairs={{0,2},{2,0},{1,3},{3,1},{4,6},{6,4},{5,7},{7,5},{8,10},{10,8},{9,1... | collective-permute-start | bytes 3145736 | tf_op jit(solution)/shard_map/ppermute | solution.py:1097
  404.1 26.6 %collective-permute-start.43 = (bf16[256,1024]{1,0:T(8,128)(2,1)S(1)}, bf16[256,1024]{1,0:T(8,128)(2,1)}, u32[]{:S(2)}, u32[]{:S(2)}) collective-permute-start(bf16[256,1024]{1,0:T(8,128)(2,1)S(1)} %add_convert_fusion.9), channel_id=1, source_target_pairs={{0,16},{4,20},{8,24},{12,28},{16,0},{20,4},{24,8},{28,12},{1,17},{... | collective-permute-start | bytes 1572872 | tf_op jit(solution)/shard_map/ppermute | solution.py:1100
  426.9 15.2 %collective-permute-start.48 = (bf16[256,1024]{1,0:T(8,128)(2,1)}, bf16[256,1024]{1,0:T(8,128)(2,1)}, u32[]{:S(2)}, u32[]{:S(2)}) collective-permute-start(bf16[256,1024]{1,0:T(8,128)(2,1)} %dynamic-slice_convert_fusion), channel_id=1, source_target_pairs={{0,8},{4,12},{8,0},{12,4},{16,24},{20,28},{24,16},{28,20},{1,9},{5... | collective-permute-start | bytes 1572872 | tf_op jit(solution)/shard_map/ppermute | solution.py:1100
  430.8 44.3 %collective-permute-start.50 = (bf16[1536,256]{1,0:T(8,128)(2,1)}, bf16[1536,256]{1,0:T(8,128)(2,1)}, u32[]{:S(2)}, u32[]{:S(2)}) collective-permute-start(bf16[1536,256]{1,0:T(8,128)(2,1)} %get-tuple-element.516), channel_id=1, source_target_pairs={{0,8},{4,12},{8,0},{12,4},{16,24},{20,28},{24,16},{28,20},{1,9},{5... | collective-permute-start | bytes 2359304 | tf_op jit(solution)/shard_map/ppermute | solution.py:1100
  433.4 35.6 %collective-permute-start.46 = (bf16[256,1024]{1,0:T(8,128)(2,1)S(1)}, bf16[256,1024]{1,0:T(8,128)(2,1)}, u32[]{:S(2)}, u32[]{:S(2)}) collective-permute-start(bf16[256,1024]{1,0:T(8,128)(2,1)S(1)} %add_convert_fusion.8), channel_id=1, source_target_pairs={{0,8},{4,12},{8,0},{12,4},{16,24},{20,28},{24,16},{28,20},{1,9},{5... | collective-permute-start | bytes 1572872 | tf_op jit(solution)/shard_map/ppermute | solution.py:1100
  442.2 74.7 %collective-permute-start.56 = (bf16[832,1024]{1,0:T(8,128)(2,1)S(1)}, bf16[832,1024]{1,0:T(8,128)(2,1)}, u32[]{:S(2)}, u32[]{:S(2)}) collective-permute-start(bf16[832,1024]{1,0:T(8,128)(2,1)S(1)} %copy-done.50), channel_id=1, source_target_pairs={{0,1},{1,0},{2,3},{3,2},{4,5},{5,4},{6,7},{7,6},{8,9},{9,8},{10,11... | collective-permute-start | bytes 5111816 | tf_op jit(solution)/shard_map/ppermute | solution.py:1094
  469.0 46.4 %collective-permute-start.54 = (bf16[256,1024]{1,0:T(8,128)(2,1)}, bf16[256,1024]{1,0:T(8,128)(2,1)S(1)}, u32[]{:S(2)}, u32[]{:S(2)}) collective-permute-start(bf16[256,1024]{1,0:T(8,128)(2,1)} %add_convert_fusion.6), channel_id=1, source_target_pairs={{0,16},{4,20},{8,24},{12,28},{16,0},{20,4},{24,8},{28,12},{1,17},{... | collective-permute-start | bytes 1572872 | tf_op jit(solution)/shard_map/ppermute | solution.py:1100
  472.3 20.5 %collective-permute-start.52 = (bf16[1536,256]{1,0:T(8,128)(2,1)S(1)}, bf16[1536,256]{1,0:T(8,128)(2,1)S(1)}, u32[]{:S(2)}, u32[]{:S(2)}) collective-permute-start(bf16[1536,256]{1,0:T(8,128)(2,1)S(1)} %copy-done.98), channel_id=1, source_target_pairs={{0,4},{4,0},{8,12},{12,8},{16,20},{20,16},{24,28},{28,24},{1,5},{5... | collective-permute-start | bytes 2359304 | tf_op jit(solution)/shard_map/ppermute | solution.py:1100
  475.1 37.4 %collective-permute-start.49 = (bf16[256,1024]{1,0:T(8,128)(2,1)S(1)}, bf16[256,1024]{1,0:T(8,128)(2,1)S(1)}, u32[]{:S(2)}, u32[]{:S(2)}) collective-permute-start(bf16[256,1024]{1,0:T(8,128)(2,1)S(1)} %get-tuple-element.521), channel_id=1, source_target_pairs={{0,4},{4,0},{8,12},{12,8},{16,20},{20,16},{24,28},{28,24},{1,5},{5... | collective-permute-start | bytes 1572872 | tf_op jit(solution)/shard_map/ppermute | solution.py:1100
  492.8 18.4 %collective-permute-start.51 = (bf16[768,256]{1,0:T(8,128)(2,1)S(1)}, bf16[768,256]{1,0:T(8,128)(2,1)S(1)}, u32[]{:S(2)}, u32[]{:S(2)}) collective-permute-start(bf16[768,256]{1,0:T(8,128)(2,1)S(1)} %dynamic-slice_convert_fusion.3), channel_id=1, source_target_pairs={{0,4},{4,0},{8,12},{12,8},{16,20},{20,16},{24,28},{28,24},{1,5},{5... | collective-permute-start | bytes 1179656 | tf_op jit(solution)/shard_map/ppermute | solution.py:1100
  511.2 24.1 %collective-permute-start.60 = (bf16[512,1024]{1,0:T(8,128)(2,1)}, bf16[512,1024]{1,0:T(8,128)(2,1)S(1)}, u32[]{:S(2)}, u32[]{:S(2)}) collective-permute-start(bf16[512,1024]{1,0:T(8,128)(2,1)} %maximum_select_fusion.4), channel_id=1, source_target_pairs={{0,4},{4,0},{8,12},{12,8},{16,20},{20,16},{24,28},{28,24},{1,5},{5... | collective-permute-start | bytes 3145736 | tf_op jit(solution)/shard_map/ppermute | solution.py:1100
  512.5 29.7 %collective-permute-start.59 = (bf16[768,256]{1,0:T(8,128)(2,1)S(1)}, bf16[768,256]{1,0:T(8,128)(2,1)S(1)}, u32[]{:S(2)}, u32[]{:S(2)}) collective-permute-start(bf16[768,256]{1,0:T(8,128)(2,1)S(1)} %dynamic-slice_convert_fusion.2), channel_id=1, source_target_pairs={{0,8},{4,12},{8,0},{12,4},{16,24},{20,28},{24,16},{28,20},{1,9},{5... | collective-permute-start | bytes 1179656 | tf_op jit(solution)/shard_map/ppermute | solution.py:1100
  516.8 28.0 %collective-permute-start.58 = (bf16[256,1024]{1,0:T(8,128)(2,1)S(1)}, bf16[256,1024]{1,0:T(8,128)(2,1)S(1)}, u32[]{:S(2)}, u32[]{:S(2)}) collective-permute-start(bf16[256,1024]{1,0:T(8,128)(2,1)S(1)} %add_convert_fusion.4), channel_id=1, source_target_pairs={{0,8},{4,12},{8,0},{12,4},{16,24},{20,28},{24,16},{28,20},{1,9},{5... | collective-permute-start | bytes 1572872 | tf_op jit(solution)/shard_map/ppermute | solution.py:1100
  516.9 29.3 %collective-permute-start.55 = (bf16[768,256]{1,0:T(8,128)(2,1)S(1)}, bf16[768,256]{1,0:T(8,128)(2,1)S(1)}, u32[]{:S(2)}, u32[]{:S(2)}) collective-permute-start(bf16[768,256]{1,0:T(8,128)(2,1)S(1)} %add_convert_fusion.13), channel_id=1, source_target_pairs={{0,16},{4,20},{8,24},{12,28},{16,0},{20,4},{24,8},{28,12},{1,17},{... | collective-permute-start | bytes 1179656 | tf_op jit(solution)/shard_map/ppermute | solution.py:1100
  535.3 14.9 %collective-permute-start.53 = (bf16[128,1024]{1,0:T(8,128)(2,1)S(1)}, bf16[128,1024]{1,0:T(8,128)(2,1)S(1)}, u32[]{:S(2)}, u32[]{:S(2)}) collective-permute-start(bf16[128,1024]{1,0:T(8,128)(2,1)S(1)} %dynamic-slice_convert_fusion.5), channel_id=1, source_target_pairs={{0,8},{4,12},{8,0},{12,4},{16,24},{20,28},{24,16},{28,20},{1,9},{5... | collective-permute-start | bytes 786440 | tf_op jit(solution)/shard_map/ppermute | solution.py:1100
  544.9 25.3 %collective-permute-start.64 = (bf16[768,256]{1,0:T(8,128)(2,1)S(1)}, bf16[768,256]{1,0:T(8,128)(2,1)S(1)}, u32[]{:S(2)}, u32[]{:S(2)}) collective-permute-start(bf16[768,256]{1,0:T(8,128)(2,1)S(1)} %add_convert_fusion.12), channel_id=1, source_target_pairs={{0,16},{4,20},{8,24},{12,28},{16,0},{20,4},{24,8},{28,12},{1,17},{... | collective-permute-start | bytes 1179656 | tf_op jit(solution)/shard_map/ppermute | solution.py:1100
  545.4 45.9 %collective-permute-start.70 = (bf16[512,1024]{1,0:T(8,128)(2,1)S(1)}, bf16[512,1024]{1,0:T(8,128)(2,1)S(1)}, u32[]{:S(2)}, u32[]{:S(2)}) collective-permute-start(bf16[512,1024]{1,0:T(8,128)(2,1)S(1)} %maximum_select_fusion.5), channel_id=1, source_target_pairs={{0,4},{4,0},{8,12},{12,8},{16,20},{20,16},{24,28},{28,24},{1,5},{5... | collective-permute-start | bytes 3145736 | tf_op jit(solution)/shard_map/ppermute | solution.py:1100
  550.2 27.5 %collective-permute-start.65 = (bf16[768,256]{1,0:T(8,128)(2,1)S(1)}, bf16[768,256]{1,0:T(8,128)(2,1)S(1)}, u32[]{:S(2)}, u32[]{:S(2)}) collective-permute-start(bf16[768,256]{1,0:T(8,128)(2,1)S(1)} %add_convert_fusion.11), channel_id=1, source_target_pairs={{0,4},{4,0},{8,12},{12,8},{16,20},{20,16},{24,28},{28,24},{1,5},{5... | collective-permute-start | bytes 1179656 | tf_op jit(solution)/shard_map/ppermute | solution.py:1100
  550.9 29.1 %collective-permute-start.61 = (bf16[128,1024]{1,0:T(8,128)(2,1)S(1)}, bf16[128,1024]{1,0:T(8,128)(2,1)S(1)}, u32[]{:S(2)}, u32[]{:S(2)}) collective-permute-start(bf16[128,1024]{1,0:T(8,128)(2,1)S(1)} %add_convert_fusion.15), channel_id=1, source_target_pairs={{0,16},{4,20},{8,24},{12,28},{16,0},{20,4},{24,8},{28,12},{1,17},{... | collective-permute-start | bytes 786440 | tf_op jit(solution)/shard_map/ppermute | solution.py:1100
  570.1 8.6 %collective-permute-start.63 = (f32[8,1024]{1,0:T(8,128)S(1)}, f32[8,1024]{1,0:T(8,128)S(1)}, u32[]{:S(2)}, u32[]{:S(2)}) collective-permute-start(f32[8,1024]{1,0:T(8,128)S(1)} %add.262), channel_id=1, source_target_pairs={{0,4},{4,0},{8,12},{12,8},{16,20},{20,16},{24,28},{28,24},{1,5},{5... | collective-permute-start | bytes 98312 | tf_op jit(solution)/shard_map/ppermute | solution.py:1100
  578.8 11.0 %collective-permute-start.69 = (bf16[768,256]{1,0:T(8,128)(2,1)S(1)}, bf16[768,256]{1,0:T(8,128)(2,1)S(1)}, u32[]{:S(2)}, u32[]{:S(2)}) collective-permute-start(bf16[768,256]{1,0:T(8,128)(2,1)S(1)} %add_convert_fusion.10), channel_id=1, source_target_pairs={{0,8},{4,12},{8,0},{12,4},{16,24},{20,28},{24,16},{28,20},{1,9},{5... | collective-permute-start | bytes 1179656 | tf_op jit(solution)/shard_map/ppermute | solution.py:1100
  580.0 11.0 %collective-permute-start.71 = (f32[8,1024]{1,0:T(8,128)S(1)}, f32[8,1024]{1,0:T(8,128)S(1)}, u32[]{:S(2)}, u32[]{:S(2)}) collective-permute-start(f32[8,1024]{1,0:T(8,128)S(1)} %add.264), channel_id=1, source_target_pairs={{0,8},{4,12},{8,0},{12,4},{16,24},{20,28},{24,16},{28,20},{1,9},{5... | collective-permute-start | bytes 98312 | tf_op jit(solution)/shard_map/ppermute | solution.py:1100
  584.0 13.8 %collective-permute-start.66 = (bf16[128,1024]{1,0:T(8,128)(2,1)S(1)}, bf16[128,1024]{1,0:T(8,128)(2,1)S(1)}, u32[]{:S(2)}, u32[]{:S(2)}) collective-permute-start(bf16[128,1024]{1,0:T(8,128)(2,1)S(1)} %add_convert_fusion.14), channel_id=1, source_target_pairs={{0,8},{4,12},{8,0},{12,4},{16,24},{20,28},{24,16},{28,20},{1,9},{5... | collective-permute-start | bytes 786440 | tf_op jit(solution)/shard_map/ppermute | solution.py:1100
  591.0 28.3 %collective-permute-start.75 = (bf16[1536,256]{1,0:T(8,128)(2,1)}, bf16[1536,256]{1,0:T(8,128)(2,1)}, u32[]{:S(2)}, u32[]{:S(2)}) collective-permute-start(bf16[1536,256]{1,0:T(8,128)(2,1)} %maximum_select_fusion.7), channel_id=1, source_target_pairs={{0,8},{4,12},{8,0},{12,4},{16,24},{20,28},{24,16},{28,20},{1,9},{5... | collective-permute-start | bytes 2359304 | tf_op jit(solution)/shard_map/ppermute | solution.py:1100
  591.3 18.4 %collective-permute-start.73 = (f32[8,1024]{1,0:T(8,128)S(1)}, f32[8,1024]{1,0:T(8,128)S(1)}, u32[]{:S(2)}, u32[]{:S(2)}) collective-permute-start(f32[8,1024]{1,0:T(8,128)S(1)} %add.268), channel_id=1, source_target_pairs={{0,16},{4,20},{8,24},{12,28},{16,0},{20,4},{24,8},{28,12},{1,17},{... | collective-permute-start | bytes 98312 | tf_op jit(solution)/shard_map/ppermute | solution.py:1100
  596.1 27.9 %collective-permute-start.74 = (bf16[1536,256]{1,0:T(8,128)(2,1)}, bf16[1536,256]{1,0:T(8,128)(2,1)}, u32[]{:S(2)}, u32[]{:S(2)}) collective-permute-start(bf16[1536,256]{1,0:T(8,128)(2,1)} %maximum_select_fusion.8), channel_id=1, source_target_pairs={{0,4},{4,0},{8,12},{12,8},{16,20},{20,16},{24,28},{28,24},{1,5},{5... | collective-permute-start | bytes 2359304 | tf_op jit(solution)/shard_map/ppermute | solution.py:1100
  610.9 16.1 %collective-permute-start.76 = (bf16[256,1024]{1,0:T(8,128)(2,1)}, bf16[256,1024]{1,0:T(8,128)(2,1)S(1)}, u32[]{:S(2)}, u32[]{:S(2)}) collective-permute-start(bf16[256,1024]{1,0:T(8,128)(2,1)} %maximum_select_fusion.9), channel_id=1, source_target_pairs={{0,4},{4,0},{8,12},{12,8},{16,20},{20,16},{24,28},{28,24},{1,5},{5... | collective-permute-start | bytes 1572872 | tf_op jit(solution)/shard_map/ppermute | solution.py:1100
  613.6 9.6 %collective-permute-start.72 = (bf16[64,1024]{1,0:T(8,128)(2,1)S(1)}, bf16[64,1024]{1,0:T(8,128)(2,1)S(1)}, u32[]{:S(2)}, u32[]{:S(2)}) collective-permute-start(bf16[64,1024]{1,0:T(8,128)(2,1)S(1)} %add_convert_fusion.16), channel_id=1, source_target_pairs={{0,2},{2,0},{1,3},{3,1},{4,6},{6,4},{5,7},{7,5},{8,10},{10,8},{9,1... | collective-permute-start | bytes 393224 | tf_op jit(solution)/shard_map/ppermute | solution.py:1097
  (125 other events, 1138.3 us)

commit v9 on v8

--- a/solution.py
+++ b/solution.py
@@ -341,8 +341,9 @@
     return pl.BlockSpec((block, width), lambda i, s: (i, 0))
 
 
-def brief():
-    return pl.CostEstimate(flops=1000, bytes_accessed=1000, transcendentals=0)
+def lasting(microseconds):
+    flops = int(microseconds * 0.28 * 1.15e9)
+    return pl.CostEstimate(flops=flops, bytes_accessed=1000, transcendentals=0)
 
 
 def params(mib):
@@ -399,7 +400,7 @@
         ),
         out_shape=[shape((2 * rows, depth), ROUND)] + [shape((2 * rows, wide), ROUND)] * count,
         compiler_params=params(40),
-        cost_estimate=brief(),
+        cost_estimate=lasting(5),
         name="first_project",
     )(place, mine, other, gains, biases, weights)
 
@@ -429,7 +430,7 @@
         ),
         out_shape=[shape((2 * rows, wide), ROUND)] * count,
         compiler_params=params(40),
-        cost_estimate=brief(),
+        cost_estimate=lasting(4),
         name="project",
     )(place, h, weights)
 
@@ -465,7 +466,7 @@
         ),
         out_shape=[shape((2 * rows, a.shape[0]), ROUND) for a in weights],
         compiler_params=params(32),
-        cost_estimate=brief(),
+        cost_estimate=lasting(3.5),
         name="pull",
     )(place, mine, other, *weights)
 
@@ -531,7 +532,7 @@
         ),
         out_shape=[shape((span, wide), ROUND), shape((pairs, 8, span), FULL)],
         compiler_params=params(56),
-        cost_estimate=brief(),
+        cost_estimate=lasting(7.3 * pairs),
         name="self_forward",
     )(limit, q, k, v)
 
@@ -613,7 +614,7 @@
         ),
         out_shape=[shape((span, wide), ROUND)] * 3,
         compiler_params=params(48),
-        cost_estimate=brief(),
+        cost_estimate=lasting(9.8 * pairs),
         name="self_back",
     )(limit, q, k, v, o, do, lse)
 
@@ -635,7 +636,10 @@
     return weights_exp / by_head(weights_exp, jnp.sum, 0.0)
 
 
-PIECES = ((0, 256), (256, 128), (384, 128), (512, 256), (768, 128), (896, 128))
+def in_groups(refs, axis):
+    for at in (0, 3):
+        yield refs[at][...]
+        yield jnp.concatenate([refs[at + 1][...], refs[at + 2][...]], axis=axis)
 
 
 def middle_forward_kernel(place_ref, frame_ref, *refs):
@@ -643,21 +647,20 @@
     ck_ref, cv_ref, gain_ref, bias_ref = refs[24:28]
     x1_ref, x2_ref, h2_ref, cq_ref, ca_ref, h3_ref = refs[28:]
     x1 = frame_ref[...].astype(FULL)
-    for o_ref, weight_ref in zip(mixed, wo):
-        x1 = x1 + nn(o_ref[...], weight_ref[...])
+    for o, weight in zip(in_groups(mixed, 1), in_groups(wo, 0)):
+        x1 = x1 + nn(o, weight)
     x1_ref[...] = x1
     scaled, _ = norm_parts(x1)
     h2 = lower(scaled * gain_ref[1:2, :] + bias_ref[1:2, :])
     h2_ref[...] = h2
-    for (start, size), weight_ref in zip(PIECES, wq):
-        cq_ref[:, start : start + size] = lower(nn(h2, weight_ref[...]))
-    for g in range(4):
+    for g, weight in enumerate(in_groups(wq, 1)):
         lanes = slice(g * 256, (g + 1) * 256)
+        cq_ref[:, lanes] = lower(nn(h2, weight))
         probability = cross_probability(cq_ref[:, lanes], ck_ref[g])
         ca_ref[:, lanes] = lower(nn(lower(probability), cv_ref[g]))
     crossed = 0.0
-    for (start, size), weight_ref in zip(PIECES, wc):
-        crossed = crossed + nn(ca_ref[:, start : start + size], weight_ref[...])
+    for g, weight in enumerate(in_groups(wc, 0)):
+        crossed = crossed + nn(ca_ref[:, g * 256 : (g + 1) * 256], weight)
     x2 = x1_ref[...] + crossed
     x2_ref[...] = x2
     scaled, _ = norm_parts(x2)
@@ -686,7 +689,7 @@
         ),
         out_shape=[shape((rows, width), FULL)] * 2 + [shape((rows, width), ROUND)] * 4,
         compiler_params=params(56),
-        cost_estimate=brief(),
+        cost_estimate=lasting(22),
         name="middle_forward",
     )(place, frames, *attended, *received, *whole)
 
@@ -703,7 +706,7 @@
         keys_kernel,
         out_shape=shape((items, 2, states, weights.shape[2]), ROUND),
         compiler_params=params(24),
-        cost_estimate=brief(),
+        cost_estimate=lasting(2),
         name="keys_of",
     )(text_states, weights)
 
@@ -763,7 +766,7 @@
         out_shape=[shape((2 * rows, hidden), ROUND)] * 2 + [shape((rows, width), kind)] * 2,
         input_output_aliases={at: 0, at + 1: 1} if shared else {},
         compiler_params=params(58),
-        cost_estimate=brief(),
+        cost_estimate=lasting(13),
         name="feed",
     )(place, h, d, *ups, *downs, *before, *shared)
 
@@ -786,7 +789,7 @@
         out_specs=pl.BlockSpec((width, tile), lambda i: (0, i)),
         out_shape=shape((width, hidden), kind),
         compiler_params=params(48),
-        cost_estimate=brief(),
+        cost_estimate=lasting(7),
         name="up_grad",
     )(mine, other, du)
 
@@ -809,7 +812,7 @@
         out_specs=pl.BlockSpec((tile, width), lambda i: (i, 0)),
         out_shape=shape((hidden, width), kind),
         compiler_params=params(48),
-        cost_estimate=brief(),
+        cost_estimate=lasting(7),
         name="down_grad",
     )(g, mine, other)
 
@@ -849,7 +852,7 @@
         ),
         out_shape=shape((3 * width, 256), kind),
         compiler_params=params(48),
-        cost_estimate=brief(),
+        cost_estimate=lasting(7),
         name="qkv_grad",
     )(place, h, *grads)
 
@@ -878,7 +881,7 @@
         ),
         out_shape=shape((width, 256), kind),
         compiler_params=params(48),
-        cost_estimate=brief(),
+        cost_estimate=lasting(4),
         name="query_grad",
     )(place, mine, other, d_mine, d_other)
 
@@ -920,7 +923,7 @@
         ),
         out_shape=shape((512, width), kind),
         compiler_params=params(48),
-        cost_estimate=brief(),
+        cost_estimate=lasting(6),
         name="outputs_grad",
     )(place, *o, dself, dself_other, ca, ca_other, dcross, dcross_other)
 
@@ -946,14 +949,9 @@
     dx1_ref[...] = dx2
     dcross = lower(dx2)
     dcross_ref[...] = dcross
-    pulled = [lower(nt(dcross, weight_ref[...])) for weight_ref in wc]
-    for g in range(4):
+    for g, weight in enumerate(in_groups(wc, 0)):
         lanes = slice(g * 256, (g + 1) * 256)
-        at = 3 * (g // 2)
-        if g % 2 == 0:
-            dcatt = pulled[at]
-        else:
-            dcatt = jnp.concatenate(pulled[at + 1 : at + 3], axis=1)
+        dcatt = lower(nt(dcross, weight))
         keys = ck_ref[g]
         cq = cq_ref[:, lanes]
         probability = cross_probability(cq, keys)
@@ -964,8 +962,8 @@
         dck_all[g] += tn(dcs, cq * HEAD ** (-0.5))
         dcv_all[g] += tn(lower(probability), dcatt)
     y2 = 0.0
-    for (start, size), weight_ref in zip(PIECES, wq):
-        y2 = y2 + nt(dcq_ref[:, start : start + size], weight_ref[...])
+    for g, weight in enumerate(in_groups(wq, 1)):
+        y2 = y2 + nt(dcq_ref[:, g * 256 : (g + 1) * 256], weight)
     scaled, inverse = norm_parts(x1_ref[...])
     sums_ref[2:3, :] += jnp.sum(y2 * scaled, axis=0, keepdims=True)
     sums_ref[3:4, :] += jnp.sum(y2, axis=0, keepdims=True)
@@ -1004,7 +1002,7 @@
         + [shape((4, 64, 256), FULL)] * 2
         + [shape((8, width), FULL)],
         compiler_params=params(56),
-        cost_estimate=brief(),
+        cost_estimate=lasting(24),
         name="middle_back",
     )(place, ym, yr, x1, x2, d, cq, *whole)
 
@@ -1038,7 +1036,7 @@
         ),
         out_shape=shape((rows, width), kind),
         compiler_params=params(40),
-        cost_estimate=brief(),
+        cost_estimate=lasting(5),
         name="first_back",
     )(place, *grads, *weights)
 
@@ -1069,7 +1067,7 @@
         ),
         out_shape=[shape((rows, width), ROUND), shape((8, width), FULL)],
         compiler_params=params(24),
-        cost_estimate=brief(),
+        cost_estimate=lasting(6),
         name="frames_back",
     )(place, ym, yr, dx1, frames, gains)
 
@@ -1302,8 +1300,8 @@
         def total(self):
             return store[self.kept] + store[self.fly]
 
-    up, down, outs, cross_in = Sum("up"), Sum("down"), Sum("outs"), Sum("cross_in")
-    qkv = Sum("qkv", (down_z, across))
+    up, down, qkv = Sum("up"), Sum("down"), Sum("qkv")
+    outs, cross_in = Sum("outs", (down_z, across)), Sum("cross_in", (down_z, across))
     store.update(h3_other=h3_other, du1=du1, g1=g1, du0=du0, g0=g0, y_m=y_m, y_fly=y_received)
     store.update(of=of, o_s=o_s, o0=o0, x2=x2, h2_other=h2_other, ca_other=ca_other)
 
@@ -1316,10 +1314,12 @@
     step(["up1"], lambda: up_grad(h3, *get("h3_other", "du1"), ROUND), "du1", "du0")
     up.over_y("up1")
     step(["down1"], lambda: down_grad(store["g1"], dout, dout_other, ROUND), "g1")
-    down.over_y("down1")
     step(["dself", "dx1", "dcross", "dcq", "dck", "dcv", "sums"], middle, "y_fly", "y_m", "x2")
     store["dself_other"] = over_core(store["dself"])
     step(["up0"], lambda: up_grad(h3, *get("h3_other", "du0"), ROUND), "du0")
+    order(up.fly, "down1", "dself_other")
+    down.over_y("down1")
+    up.first("up0")
     step(
         ["dof", "dos", "do0"],
         lambda: pull(place, *get("dself", "dself_other"), (out_first, out_second, w_out)),
@@ -1341,17 +1341,20 @@
     order("dcross_other", "dcq_other", "pair_fly", "pair_kept")
     pair_sum = lower(store["pair_kept"] + store["pair_fly"])
     store["pair"] = pair_sum[0]
-    store["pair_y"] = over_y(cross_order(pair_sum[1]))
+    store["pair_other"] = cross_order(pair_sum[1])
     step(
         ["dqs", "dks", "dvs"],
         lambda: self_back(limit, qs, ks, vs, store["o_s"], store["dos"], lse_s),
         "dos",
     )
-    up.first("up0")
+    up.second()
     step(["down0"], lambda: down_grad(store["g0"], dout, dout_other, ROUND), "g0")
     yp = ("dqf", "dkf", "dvf", "dqs", "dks", "dvs")
-    step(["qkv1"], lambda: qkv_grad(place, h1, get(*yp), ROUND), "dqs", "pair_y")
+    step(["qkv1"], lambda: qkv_grad(place, h1, get(*yp), ROUND), "dqs")
+    order(down.fly, "qkv1")
     qkv.over_y("qkv1")
+    down.first("down0")
+    up.far()
 
     def query(g):
         return query_grad(place, g, h2, *get("h2_other", "dcq", "dcq_other"), ROUND)
@@ -1363,17 +1366,17 @@
         )
 
     step(["query1"], lambda: query(1), "dcq_other", "h2_other")
-    store["query_fly"] = over_y(store["query1"])
-    down.first("down0")
-    up.second()
     step(["outs1"], lambda: outof(1, "of", "o_s"), "dcross_other", "ca_other")
     step(
         ["dq0", "dk0", "dv0"],
         lambda: self_back(limit, q0, k0, v0, store["o0"], store["do0"], lse0),
         "do0",
     )
+    order(qkv.fly, "outs1", "query1")
     outs.over_y("outs1")
-    up.far()
+    store["query_fly"] = over_y(store["query1"])
+    store["pair_y"] = over_y(store["pair_other"])
+    up.back()
     down.second()
     nine = ("dq0", "dk0", "dv0", *yp)
     weights = (w_qkv, qkv_first, qkv_second)
@@ -1381,8 +1384,12 @@
     store["yo_fly"] = over_core(store["yo"])
     step(["qkv0"], lambda: qkv_grad(place, h1, get("dq0", "dk0", "dv0"), ROUND), "dq0")
     qkv.first("qkv0")
-    up.back()
-    step(["query0"], lambda: query(0), "dcq", "query_fly")
+    up.along()
+    step(["query0"], lambda: query(0), "dcq")
+    down.far()
+    step(["outs0"], lambda: outof(0, "o0"), "dcross")
+    outs.first("outs0")
+    order("query0", "query_fly", "pair", "pair_y")
     other_text = lax.dynamic_index_in_dim(text_states, 1 - side, keepdims=False)
     texts = jnp.concatenate([text, other_text], axis=0)
     pairs = jnp.concatenate(get("pair", "pair_y"), axis=1)
@@ -1395,16 +1402,8 @@
         axis=0,
     )
     cross_in.first_alone("into0")
-    down.far()
-    step(["outs0"], lambda: outof(0, "o0"), "dcross")
-    up.along()
-    outs.first("outs0")
     qkv.second()
     step(["ym"], lambda: first_back(place, get(*nine), weights, FULL), "dq0")
-    cross_in.second()
-    qkv.far()
-    outs.second()
-    down.back()
     step(
         ["grad_frames", "first_sums"],
         lambda: frames_back(place, *get("ym", "yo_fly", "dx1"), frames, norm_gain),
@@ -1412,38 +1411,42 @@
         "yo_fly",
     )
     norms = Row("norms", store["sums"] + store["first_sums"], over_core)
+    down.back()
+    outs.second()
     up.end("grad_up")
-    cross_in.far()
+    qkv.far()
+    cross_in.second()
+    norms.then(over_y)
     down.along()
-    norms.then(over_y)
-    qkv.back()
     outs.far()
     norms.then(over_x)
-    cross_in.back()
+    qkv.back()
+    cross_in.far()
     text_part = 0.0
     for c in range(2):
         text_part = text_part + nt(pairs[c], w_cross_kv[c])
     text_mine, text_theirs = text_part[:64], text_part[64:]
     text_rows = Row("texts", text_mine, lambda v: over_y(text_theirs))
     qkv.along()
+    outs.back()
     norms.then(over_z)
     store["out_fly"] = over_core(out_o)
-    outs.back()
     text_rows.then(over_core)
-    cross_in.along()
+    cross_in.back()
+    outs.along()
     norms.then(lambda v: along_wide(v, Z_FAR))
     down.end("grad_down")
     order("texts_fly", "texts_kept")
     text_grad = lower(text_rows.total())
     text_away = over_y(text_grad)
-    outs.along()
+    cross_in.along()
     order("out_fly", "x2")
     out_rows = lower(store["x2"] + out_m + store["out_fly"].astype(FULL))
     qkv.end("grad_qkv")
+    outs.end("grad_outs")
     grad_text = ordered(text_grad[None], text_away[None], side)
+    sums = norms.total()
     cross_in.end("grad_in")
-    sums = norms.total()
-    outs.end("grad_outs")
     grad_in, grad_outs = get("grad_in", "grad_outs")
     return (
         out_rows,

time: 642 us -> 581 us (0.905)
  waiting for transfers between devices: 174 us -> 141 us
  Pallas kernels: 274 us -> 262 us
  starting transfers between devices: 64.4 us -> 56 us
    ppermute x16, waiting for transfers between devices: 49.2 us -> 22.4 us  [over_y(): return lax.ppermute(v, 'narrow', Y_PAIRS)]
    unnamed x224 -> x271, local copies, waits for them, and re-layouts: 28.8 us -> 23.8 us
    convert_element_type x16 -> x17, other arithmetic: 20.6 us -> 19.3 us  [lower(): return values_in.astype(jnp.bfloat16)]
  transfers between devices with their start and end apart: 77 -> 77, of which waited for: 21 -> 23; matrix products, arithmetic and copies ran while one was open for 13% -> 13% of each run, Pallas kernels for 37% -> 44%
where the time goes in v9:
time: 581 us; the launch traced here: 571 us
  Pallas kernels  262 us (45%)
  waiting for transfers between devices  141 us (24%)
  other arithmetic  58.2 us (10%)
  starting transfers between devices  56 us (10%)
  local copies, waits for them, and re-layouts  49.4 us (9%)
    ppermute x34, waiting for transfers between devices, along_wide(): return lax.ppermute(v, 'wide', pairs)  118 us
    pallas_call x4, Pallas kernels, feed(): pl.pallas_call(functools.partial(feed_kernel, parts=parts, carried=len(be...  51.4 us
    pallas_call x3, Pallas kernels, self_back(): pl.pallas_call(functools.partial(self_back_kernel, span=span, floor=floor...  39.3 us
    ppermute x34, starting transfers between devices, along_wide(): return lax.ppermute(v, 'wide', pairs)  34.2 us
    pallas_call x3, Pallas kernels, self_forward(): pl.pallas_call(functools.partial(self_forward_kernel, span=span, floor=fl...  31 us
    pallas_call x1, Pallas kernels, middle_forward(): pl.pallas_call(middle_forward_kernel, grid_spec=pltpu.PrefetchScalarGridS...  29.2 us
    unnamed x271, local copies, waits for them, and re-layouts  23.8 us
    pallas_call x1, Pallas kernels, middle_back(): pl.pallas_call(middle_back_kernel, grid_spec=pltpu.PrefetchScalarGridSpec...  23.2 us
  transfers between devices with their start and end apart: 77, of which 23 were waited for; matrix products, arithmetic and copies ran while one was open for 13% of the time, Pallas kernels for 44%

profile of v9, /device:TPU:0, one launch (start us, length us, event | category | flops | bytes accessed | tf_op | source)
XLA Modules:
  0.0 570.9 jit_solution(4160035007728856051)
XLA Ops:
  1.2 2.2 constant_dynamic-slice_fusion.15
  3.4 2.6 collective-permute-start.1
  10.9 6.0 %first_project.1 = (bf16[1664,1024]{1,0:T(8,128)(2,1)S(1)}, bf16[1664,256]{1,0:T(8,128)(2,1)S(1)}, bf16[1664,256]{1,0:T(8,128)(2,1)S(1)}, bf16[1664,256]{1,0:T(8,128)(2,1)S(1)}) custom-call(s32[3]{0:T(128)S(1)} %add_add_fusion.place_ref, bf16[832,1024]{1,0:T(8,128)(2,1)S(1)} %copy-done.31, bf16[832,1024]{1,0:T(8,128)(2,1)} %collective-permute-done.other_ref, ...), custom_call_target="tpu_custom_call" | custom-call | flops 1610000000 | bytes 1000 | tf_op jit(solution)/shard_map/first_project/pallas_call | solution.py:393
  20.5 3.8 collective-permute-done.1.weight_ref.refs_10_
  27.9 14.1 %self_forward.3 = (bf16[1664,256]{1,0:T(8,128)(2,1)}, f32[2,8,1664]{2,1,0:T(8,128)}) custom-call(s32[1]{0:T(128)} %dynamic_slice.129.limit_ref, bf16[1664,256]{1,0:T(8,128)(2,1)} %copy-done.89, bf16[1664,256]{1,0:T(8,128)(2,1)} %copy-done.91, bf16[1664,256]{1,0:T(8,128)(2,1)} %copy-done.93), custom_call_target="tpu_custom_call" | custom-call | flops 4701199872 | bytes 1000 | tf_op jit(solution)/shard_map/self_forward/pallas_call | solution.py:525
  48.1 2.9 project.2
  57.6 8.5 %self_forward.4 = (bf16[1664,128]{1,0:T(8,128)(2,1)}, f32[1,8,1664]{2,1,0:T(8,128)}) custom-call(s32[1]{0:T(128)} %dynamic_slice.129.limit_ref, bf16[1664,128]{1,0:T(8,128)(2,1)} %copy-done.77, bf16[1664,128]{1,0:T(8,128)(2,1)} %copy-done.79, bf16[1664,128]{1,0:T(8,128)(2,1)} %copy-done.81), custom_call_target="tpu_custom_call" | custom-call | flops 2350599936 | bytes 1000 | tf_op jit(solution)/shard_map/self_forward/pallas_call | solution.py:525
  71.9 2.7 project.3
  77.4 3.6 collective-permute-done.13.refs_20_.refs_8_
  81.8 8.4 %self_forward.5 = (bf16[1664,128]{1,0:T(8,128)(2,1)}, f32[1,8,1664]{2,1,0:T(8,128)}) custom-call(s32[1]{0:T(128)} %dynamic_slice.129.limit_ref, bf16[1664,128]{1,0:T(8,128)(2,1)} %copy-done.83, bf16[1664,128]{1,0:T(8,128)(2,1)} %copy-done.85, bf16[1664,128]{1,0:T(8,128)(2,1)} %copy-done.87), custom_call_target="tpu_custom_call" | custom-call | flops 2350599936 | bytes 1000 | tf_op jit(solution)/shard_map/self_forward/pallas_call | solution.py:525
  96.4 29.2 %middle_forward.1 = (f32[832,1024]{1,0:T(8,128)}, f32[832,1024]{1,0:T(8,128)}, bf16[832,1024]{1,0:T(8,128)(2,1)}, bf16[832,1024]{1,0:T(8,128)(2,1)}, bf16[832,10...) custom-call(s32[3]{0:T(128)} %copy-done.68, bf16[832,1024]{1,0:T(8,128)(2,1)} %frame_ref.3, ...), custom_call_target="tpu_custom_call" | custom-call | flops 7084000256 | bytes 1000 | tf_op jit(solution)/shard_map/middle_forward/pallas_call | solution.py:676
  128.2 12.1 %feed.4 = (bf16[1664,1024]{1,0:T(8,128)(2,1)}, bf16[1664,1024]{1,0:T(8,128)(2,1)}, f32[832,1024]{1,0:T(8,128)}, f32[832,1024]{1,0:T(8,128)}) custom-call(s32[3]{0:T(128)} %copy-done.68, bf16[832,1024]{1,0:T(8,128)(2,1)} %get-tuple-element.319.h_ref.mine_ref, bf16[832,1024]{1,0:T(8,128)(2,1)} %copy-done, bf16[1024,1024]{1,0:T(8,128)(2,1)} %refs_0_.1, ...), custom_call_target="tpu_custom_call" | custom-call | flops 4185999872 | bytes 1000 | tf_op jit(solution)/shard_map/feed/pallas_call | solution.py:755
  142.1 12.1 %feed.5 = (bf16[1664,1024]{1,0:T(8,128)(2,1)}, bf16[1664,1024]{1,0:T(8,128)(2,1)}, f32[832,1024]{1,0:T(8,128)}, f32[832,1024]{1,0:T(8,128)}) custom-call(s32[3]{0:T(128)} %copy-done.68, bf16[832,1024]{1,0:T(8,128)(2,1)} %copy-done.13, bf16[832,1024]{1,0:T(8,128)(2,1)} %copy-done.10, ...), custom_call_target="tpu_custom_call", output_to_operand_aliasing={{0}: (5, {}), {1}: (6, {})} | custom-call | flops 4185999872 | bytes 1000 | tf_op jit(solution)/shard_map/feed/pallas_call | solution.py:755
  154.2 20.0 %collective-permute-done.28.refs_3_ = bf16[512,1024]{1,0:T(8,128)(2,1)} collective-permute-done((bf16[512,1024]{1,0:T(8,128)(2,1)S(1)}, bf16[512,1024]{1,0:T(8,128)(2,1)}, u32[]{:S(2)}, u32[]{:S(2)}) %collective-permute-start.28) | collective-permute-done | bytes 1048608 | tf_op jit(solution)/shard_map/ppermute | solution.py:1098
  174.2 13.4 %feed.6 = (bf16[1664,1024]{1,0:T(8,128)(2,1)}, bf16[1664,1024]{1,0:T(8,128)(2,1)}, bf16[832,1024]{1,0:T(8,128)(2,1)}, bf16[832,1024]{1,0:T(8,128)(2,1)}) custom-call(s32[3]{0:T(128)} %copy-done.68, bf16[832,1024]{1,0:T(8,128)(2,1)} %copy-done.13, bf16[832,1024]{1,0:T(8,128)(2,1)} %copy-done.10, bf16[1024,512]{1,0:T(8,128)(2,1)} %collective-permute-done.14.refs_0_, ...), custom_call_target="tpu_custom_call" | custom-call | flops 4185999872 | bytes 1000 | tf_op jit(solution)/shard_map/feed/pallas_call | solution.py:755
  187.6 13.7 %feed.7 = (bf16[1664,1024]{1,0:T(8,128)(2,1)}, bf16[1664,1024]{1,0:T(8,128)(2,1)}, f32[832,1024]{1,0:T(8,128)}, f32[832,1024]{1,0:T(8,128)}) custom-call(s32[3]{0:T(128)} %copy-done.68, bf16[832,1024]{1,0:T(8,128)(2,1)} %get-tuple-element.319.h_ref.mine_ref, bf16[832,1024]{1,0:T(8,128)(2,1)} %copy-done, ...), custom_call_target="tpu_custom_call", output_to_operand_aliasing={{0}: (9, {}), {1}: (10, {})} | custom-call | flops 4185999872 | bytes 1000 | tf_op jit(solution)/shard_map/feed/pallas_call | solution.py:755
  201.4 7.3 %up_grad.2 = bf16[1024,1024]{1,0:T(8,128)(2,1)} custom-call(bf16[832,1024]{1,0:T(8,128)(2,1)S(1)} %copy-done.3, bf16[832,1024]{1,0:T(8,128)(2,1)S(1)} %copy-done.14, bf16[1664,1024]{1,0:T(8,128)(2,1)} %get-tuple-element.343.du_ref), custom_call_target="tpu_custom_call" | custom-call | flops 2254000128 | bytes 1000 | tf_op jit(solution)/shard_map/up_grad/pallas_call | solution.py:785
  209.2 6.2 %down_grad.2 = bf16[1024,1024]{1,0:T(8,128)(2,1)S(1)} custom-call(bf16[1664,1024]{1,0:T(8,128)(2,1)} %get-tuple-element.344.g_ref, bf16[832,1024]{1,0:T(8,128)(2,1)S(1)} %copy-done.1, bf16[832,1024]{1,0:T(8,128)(2,1)S(1)} %copy-done.11), custom_call_target="tpu_custom_call" | custom-call | flops 2254000128 | bytes 1000 | tf_op jit(solution)/shard_map/down_grad/pallas_call | solution.py:808
  218.0 23.2 %middle_back.1 = (f32[832,1024]{1,0:T(8,128)}, bf16[832,1024]{1,0:T(8,128)(2,1)}, bf16[832,1024]{1,0:T(8,128)(2,1)}, bf16[832,1024]{1,0:T(8,128)(2,1)}, f32[4,64...) custom-call(s32[3]{0:T(128)} %copy-done.68, f32[832,1024]{1,0:T(8,128)} %get-tuple-element.347.ym_ref, ...), custom_call_target="tpu_custom_call" | custom-call | flops 7728000000 | bytes 1000 | tf_op jit(solution)/shard_map/middle_back/pallas_call | solution.py:991
  243.0 6.3 %up_grad.3 = bf16[1024,1024]{1,0:T(8,128)(2,1)S(1)} custom-call(bf16[832,1024]{1,0:T(8,128)(2,1)S(1)} %copy-done.3, bf16[832,1024]{1,0:T(8,128)(2,1)S(1)} %copy-done.15, bf16[1664,1024]{1,0:T(8,128)(2,1)} %get-tuple-element.353.du_ref), custom_call_target="tpu_custom_call" | custom-call | flops 2254000128 | bytes 1000 | tf_op jit(solution)/shard_map/up_grad/pallas_call | solution.py:785
  249.3 7.7 %collective-permute-done.31 = bf16[1024,1024]{1,0:T(8,128)(2,1)} collective-permute-done((bf16[1024,1024]{1,0:T(8,128)(2,1)}, bf16[1024,1024]{1,0:T(8,128)(2,1)}, u32[]{:S(2)}, u32[]{:S(2)}) %collective-permute-start.31) | collective-permute-done | bytes 2097184 | tf_op jit(solution)/shard_map/ppermute | solution.py:1095
  257.1 4.7 add_convert_fusion.2
  266.5 2.1 slice.81
  271.1 3.7 pull.1
  275.9 9.5 %self_back.3 = (bf16[1664,128]{1,0:T(8,128)(2,1)S(1)}, bf16[1664,128]{1,0:T(8,128)(2,1)S(1)}, bf16[1664,128]{1,0:T(8,128)(2,1)S(1)}) custom-call(s32[1]{0:T(128)} %dynamic_slice.129.limit_ref, bf16[1664,128]{1,0:T(8,128)(2,1)S(1)} %copy-done.78, bf16[1664,128]{1,0:T(8,128)(2,1)S(1)} %copy-done.80, bf16[1664,128]{1,0:T(8,128)(2,1)S(1)} %copy-done.82, ...), custom_call_target="tpu_custom_call" | custom-call | flops 3155599872 | bytes 1000 | tf_op jit(solution)/shard_map/self_back/pallas_call | solution.py:606
  286.7 9.9 %self_back.4 = (bf16[1664,128]{1,0:T(8,128)(2,1)S(1)}, bf16[1664,128]{1,0:T(8,128)(2,1)S(1)}, bf16[1664,128]{1,0:T(8,128)(2,1)S(1)}) custom-call(s32[1]{0:T(128)} %dynamic_slice.129.limit_ref, bf16[1664,128]{1,0:T(8,128)(2,1)S(1)} %copy-done.84, bf16[1664,128]{1,0:T(8,128)(2,1)S(1)} %copy-done.86, bf16[1664,128]{1,0:T(8,128)(2,1)S(1)} %copy-done.88, ...), custom_call_target="tpu_custom_call" | custom-call | flops 3155599872 | bytes 1000 | tf_op jit(solution)/shard_map/self_back/pallas_call | solution.py:606
  297.4 2.0 convert_add_fusion.2
  302.0 6.3 %down_grad.3 = bf16[1024,1024]{1,0:T(8,128)(2,1)S(1)} custom-call(bf16[1664,1024]{1,0:T(8,128)(2,1)} %get-tuple-element.387.g_ref, bf16[832,1024]{1,0:T(8,128)(2,1)S(1)} %copy-done.2, bf16[832,1024]{1,0:T(8,128)(2,1)S(1)} %copy-done.12), custom_call_target="tpu_custom_call" | custom-call | flops 2254000128 | bytes 1000 | tf_op jit(solution)/shard_map/down_grad/pallas_call | solution.py:808
  310.9 6.1 %qkv_grad.2 = bf16[3072,256]{1,0:T(8,128)(2,1)S(1)} custom-call(s32[3]{0:T(128)S(1)} %copy-done.69, bf16[1664,1024]{1,0:T(8,128)(2,1)} %copy-done.74, bf16[1664,128]{1,0:T(8,128)(2,1)S(1)} %get-tuple-element.376.refs_0_.refs_3_, bf16[1664,128]{1,0:T(8,128)(2,1)S(1)} %get-tuple-element.377.refs_1_.refs_4_, ...), custom_call_target="tpu_custom_call" | custom-call | flops 2254000128 | bytes 1000 | tf_op jit(solution)/shard_map/qkv_grad/pallas_call | solution.py:845
  320.0 4.2 convert_add_fusion.1
  326.6 3.0 query_grad.2
  329.6 2.6 collective-permute-start.40
  332.3 6.0 %outputs_grad.2 = bf16[512,1024]{1,0:T(8,128)(2,1)} custom-call(s32[3]{0:T(128)S(1)} %copy-done.69, bf16[1664,128]{1,0:T(8,128)(2,1)S(1)} %copy-done.58, bf16[1664,128]{1,0:T(8,128)(2,1)S(1)} %copy-done.60, bf16[832,1024]{1,0:T(8,128)(2,1)S(1)} %copy-done.4, bf16[832,1024]{1,0:T(8,128)(2,1)S(1)} %copy-done.6, ...), custom_call_target="tpu_custom_call" | custom-call | flops 1932000000 | bytes 1000 | tf_op jit(solution)/shard_map/outputs_grad/pallas_call | solution.py:916
  338.4 20.0 %self_back.5 = (bf16[1664,256]{1,0:T(8,128)(2,1)S(1)}, bf16[1664,256]{1,0:T(8,128)(2,1)S(1)}, bf16[1664,256]{1,0:T(8,128)(2,1)S(1)}) custom-call(s32[1]{0:T(128)} %dynamic_slice.129.limit_ref, bf16[1664,256]{1,0:T(8,128)(2,1)S(1)} %copy-done.90, bf16[1664,256]{1,0:T(8,128)(2,1)S(1)} %copy-done.92, bf16[1664,256]{1,0:T(8,128)(2,1)S(1)} %copy-done.94, ...), custom_call_target="tpu_custom_call" | custom-call | flops 6311199744 | bytes 1000 | tf_op jit(solution)/shard_map/self_back/pallas_call | solution.py:606
  360.1 2.3 convert_add_fusion
  366.4 6.0 %first_back.2 = bf16[832,1024]{1,0:T(8,128)(2,1)} custom-call(s32[3]{0:T(128)S(1)} %add_add_fusion.1.place_ref, bf16[1664,256]{1,0:T(8,128)(2,1)S(1)} %get-tuple-element.457.refs_0_, bf16[1664,256]{1,0:T(8,128)(2,1)S(1)} %get-tuple-element.427.refs_1_, bf16[1664,256]{1,0:T(8,128)(2,1)S(1)} %get-tuple-element.428.refs_2_, bf16[1664,128]{1,0:T(8,128)(2,1)S(1)} %copy-done.34, ...), custom_call_target="tpu_custom_call" | custom-call | flops 1610000000 | bytes 1000 | tf_op jit(solution)/shard_map/first_back/pallas_call | solution.py:1025
  373.0 5.9 %qkv_grad.3 = bf16[3072,256]{1,0:T(8,128)(2,1)S(1)} custom-call(s32[3]{0:T(128)S(1)} %copy-done.69, bf16[1664,1024]{1,0:T(8,128)(2,1)} %copy-done.74, bf16[1664,256]{1,0:T(8,128)(2,1)S(1)} %get-tuple-element.457.refs_0_, bf16[1664,256]{1,0:T(8,128)(2,1)S(1)} %get-tuple-element.427.refs_1_, bf16[1664,256]{1,0:T(8,128)(2,1)S(1)} %get-tuple-element.428.refs_2_), custom_call_target="tpu_custom_call" | custom-call | flops 2254000128 | bytes 1000 | tf_op jit(solution)/shard_map/qkv_grad/pallas_call | solution.py:845
  379.0 2.6 add_convert_fusion.3
  381.6 2.6 maximum_select_fusion.4
  384.2 3.0 query_grad.3
  388.8 2.0 add_convert_fusion.7
  390.8 5.0 outputs_grad.3
  395.8 3.1 collective-permute-done.48
  400.4 2.4 add_convert_fusion.5
  403.3 3.7 collective-permute-done.46
  410.7 9.0 %collective-permute-done.50 = bf16[1536,256]{1,0:T(8,128)(2,1)S(1)} collective-permute-done((bf16[1536,256]{1,0:T(8,128)(2,1)}, bf16[1536,256]{1,0:T(8,128)(2,1)S(1)}, u32[]{:S(2)}, u32[]{:S(2)}) %collective-permute-start.50) | collective-permute-done | bytes 786464 | tf_op jit(solution)/shard_map/ppermute | solution.py:1098
  423.3 4.9 first_back.3.ym_ref
  429.9 5.9 %frames_back.1 = (bf16[832,1024]{1,0:T(8,128)(2,1)}, f32[8,1024]{1,0:T(8,128)S(1)}) custom-call(s32[3]{0:T(128)S(1)} %copy-done.69, f32[832,1024]{1,0:T(8,128)S(1)} %first_back.3.ym_ref, bf16[832,1024]{1,0:T(8,128)(2,1)} %collective-permute-done.55.yr_ref, f32[832,1024]{1,0:T(8,128)S(1)} %copy-done.20, bf16[832,1024]{1,0:T(8,128)(2,1)S(1)} %copy-done.32, ...), custom_call_target="tpu_custom_call" | custom-call | flops 1932000000 | bytes 1000 | tf_op jit(solution)/shard_map/frames_back/pallas_call | solution.py:1060
  437.7 3.9 collective-permute-done.53
  443.0 4.4 fusion
  447.3 19.5 %collective-permute-done.51 = bf16[768,256]{1,0:T(8,128)(2,1)S(1)} collective-permute-done((bf16[768,256]{1,0:T(8,128)(2,1)S(1)}, bf16[768,256]{1,0:T(8,128)(2,1)S(1)}, u32[]{:S(2)}, u32[]{:S(2)}) %collective-permute-start.51) | collective-permute-done | bytes 393248 | tf_op jit(solution)/shard_map/ppermute | solution.py:1098
  469.6 4.2 collective-permute-done.60
  474.3 2.0 collective-permute-done.61
  477.7 9.2 %collective-permute-done.58 = bf16[768,256]{1,0:T(8,128)(2,1)S(1)} collective-permute-done((bf16[768,256]{1,0:T(8,128)(2,1)S(1)}, bf16[768,256]{1,0:T(8,128)(2,1)S(1)}, u32[]{:S(2)}, u32[]{:S(2)}) %collective-permute-start.58) | collective-permute-done | bytes 393248 | tf_op jit(solution)/shard_map/ppermute | solution.py:1098
  487.7 2.8 collective-permute-start.66
  492.0 11.7 %collective-permute-done.63 = bf16[768,256]{1,0:T(8,128)(2,1)S(1)} collective-permute-done((bf16[768,256]{1,0:T(8,128)(2,1)S(1)}, bf16[768,256]{1,0:T(8,128)(2,1)S(1)}, u32[]{:S(2)}, u32[]{:S(2)}) %collective-permute-start.63) | collective-permute-done | bytes 393248 | tf_op jit(solution)/shard_map/ppermute | solution.py:1098
  505.7 9.7 %collective-permute-done.65 = f32[8,1024]{1,0:T(8,128)S(1)} collective-permute-done((f32[8,1024]{1,0:T(8,128)S(1)}, f32[8,1024]{1,0:T(8,128)S(1)}, u32[]{:S(2)}, u32[]{:S(2)}) %collective-permute-start.65) | collective-permute-done | bytes 32800 | tf_op jit(solution)/shard_map/ppermute | solution.py:1098
  517.6 4.7 collective-permute-done.62
  524.1 4.0 collective-permute-done.71
  529.9 4.5 fusion.1
  539.1 3.8 add_convert_fusion
  544.1 6.4 %collective-permute-done.75 = bf16[1536,256]{1,0:T(8,128)(2,1)} collective-permute-done((bf16[1536,256]{1,0:T(8,128)(2,1)S(1)}, bf16[1536,256]{1,0:T(8,128)(2,1)}, u32[]{:S(2)}, u32[]{:S(2)}) %collective-permute-start.75) | collective-permute-done | bytes 786464 | tf_op jit(solution)/shard_map/ppermute | solution.py:1098
  550.5 3.4 fusion.2
  555.1 9.6 %collective-permute-done.76 = bf16[1536,256]{1,0:T(8,128)(2,1)} collective-permute-done((bf16[1536,256]{1,0:T(8,128)(2,1)S(1)}, bf16[1536,256]{1,0:T(8,128)(2,1)}, u32[]{:S(2)}, u32[]{:S(2)}) %collective-permute-start.76) | collective-permute-done | bytes 786464 | tf_op jit(solution)/shard_map/ppermute | solution.py:1098
  (485 shorter events, 119.6 us)
Async XLA Ops:
  3.4 20.9 %collective-permute-start.1 = (bf16[3,1024,128]{2,1,0:T(8,128)(2,1)}, bf16[3,1024,128]{2,1,0:T(8,128)(2,1)S(1)}, u32[]{:S(2)}, u32[]{:S(2)}) collective-permute-start(bf16[3,1024,128]{2,1,0:T(8,128)(2,1)} %constant_dynamic-slice_fusion.15), channel_id=1, source_target_pairs={{0,2},{2,0},{1,3},{3,1},{4,6},{6,4},{5,7},{7,5},{8,10},{10,8},{9,1... | collective-permute-start | bytes 2359304 | tf_op jit(solution)/shard_map/ppermute | solution.py:1095
  24.3 29.3 %collective-permute-start.5 = (bf16[256,1024]{1,0:T(8,128)(2,1)S(1)}, bf16[256,1024]{1,0:T(8,128)(2,1)}, u32[]{:S(2)}, u32[]{:S(2)}) collective-permute-start(bf16[256,1024]{1,0:T(8,128)(2,1)S(1)} %copy-done.52), channel_id=1, source_target_pairs={{0,1},{1,0},{2,3},{3,2},{4,5},{5,4},{6,7},{7,6},{8,9},{9,8},{10,11... | collective-permute-start | bytes 1572872 | tf_op jit(solution)/shard_map/ppermute | solution.py:1092
  24.4 18.7 %collective-permute-start.2 = (bf16[128,1024]{1,0:T(8,128)(2,1)S(1)}, bf16[128,1024]{1,0:T(8,128)(2,1)S(1)}, u32[]{:S(2)}, u32[]{:S(2)}) collective-permute-start(bf16[128,1024]{1,0:T(8,128)(2,1)S(1)} %constant_dynamic-slice_fusion.14), channel_id=1, source_target_pairs={{0,2},{2,0},{1,3},{3,1},{4,6},{6,4},{5,7},{7,5},{8,10},{10,8},{9,1... | collective-permute-start | bytes 786440 | tf_op jit(solution)/shard_map/ppermute | solution.py:1095
  26.2 27.4 %collective-permute-start.6 = (bf16[1024,256]{1,0:T(8,128)(2,1)}, bf16[1024,256]{1,0:T(8,128)(2,1)}, u32[]{:S(2)}, u32[]{:S(2)}) collective-permute-start(bf16[1024,256]{1,0:T(8,128)(2,1)} %refs_0_.2), channel_id=1, source_target_pairs={{0,1},{1,0},{2,3},{3,2},{4,5},{5,4},{6,7},{7,6},{8,9},{9,8},{10,11... | collective-permute-start | bytes 1572872 | tf_op jit(solution)/shard_map/ppermute | solution.py:1092
  27.4 17.4 %collective-permute-start.3 = (bf16[1024,128]{1,0:T(8,128)(2,1)S(1)}, bf16[1024,128]{1,0:T(8,128)(2,1)}, u32[]{:S(2)}, u32[]{:S(2)}) collective-permute-start(bf16[1024,128]{1,0:T(8,128)(2,1)S(1)} %constant_dynamic-slice_fusion.13), channel_id=1, source_target_pairs={{0,2},{2,0},{1,3},{3,1},{4,6},{6,4},{5,7},{7,5},{8,10},{10,8},{9,1... | collective-permute-start | bytes 786440 | tf_op jit(solution)/shard_map/ppermute | solution.py:1095
  27.7 25.9 %collective-permute-start.7 = (bf16[256,1024]{1,0:T(8,128)(2,1)}, bf16[256,1024]{1,0:T(8,128)(2,1)}, u32[]{:S(2)}, u32[]{:S(2)}) collective-permute-start(bf16[256,1024]{1,0:T(8,128)(2,1)} %refs_6_.1), channel_id=1, source_target_pairs={{0,1},{1,0},{2,3},{3,2},{4,5},{5,4},{6,7},{7,6},{8,9},{9,8},{10,11... | collective-permute-start | bytes 1572872 | tf_op jit(solution)/shard_map/ppermute | solution.py:1092
  44.8 23.7 %collective-permute-start.8 = (bf16[3,1024,128]{2,1,0:T(8,128)(2,1)S(1)}, bf16[3,1024,128]{2,1,0:T(8,128)(2,1)S(1)}, u32[]{:S(2)}, u32[]{:S(2)}) collective-permute-start(bf16[3,1024,128]{2,1,0:T(8,128)(2,1)S(1)} %collective-permute-done.1.weight_ref.refs_10_), channel_id=1, source_target_pairs={{0,8},{4,12},{8,0},{12,4},{16,24},{20,28},{24,16},{28,20},{1,9},{5... | collective-permute-start | bytes 2359304 | tf_op jit(solution)/shard_map/ppermute | solution.py:1098
  51.8 15.2 %collective-permute-start.9 = (bf16[2,64,256]{2,1,0:T(8,128)(2,1)S(1)}, bf16[2,64,256]{2,1,0:T(8,128)(2,1)S(1)}, u32[]{:S(2)}, u32[]{:S(2)}) collective-permute-start(bf16[2,64,256]{2,1,0:T(8,128)(2,1)S(1)} %get-tuple-element.563), channel_id=1, source_target_pairs={{0,2},{2,0},{1,3},{3,1},{4,6},{6,4},{5,7},{7,5},{8,10},{10,8},{9,1... | collective-permute-start | bytes 196616 | tf_op jit(solution)/shard_map/ppermute | solution.py:1095
  54.4 14.7 %collective-permute-start.10 = (bf16[832,256]{1,0:T(8,128)(2,1)}, bf16[832,256]{1,0:T(8,128)(2,1)S(1)}, u32[]{:S(2)}, u32[]{:S(2)}) collective-permute-start(bf16[832,256]{1,0:T(8,128)(2,1)} %constant_dynamic-slice_fusion.11), channel_id=1, source_target_pairs={{0,1},{1,0},{2,3},{3,2},{4,5},{5,4},{6,7},{7,6},{8,9},{9,8},{10,11... | collective-permute-start | bytes 1277960 | tf_op jit(solution)/shard_map/ppermute | solution.py:1092
  54.4 22.4 %collective-permute-start.11 = (bf16[128,1024]{1,0:T(8,128)(2,1)S(1)}, bf16[128,1024]{1,0:T(8,128)(2,1)S(1)}, u32[]{:S(2)}, u32[]{:S(2)}) collective-permute-start(bf16[128,1024]{1,0:T(8,128)(2,1)S(1)} %collective-permute-done.2.refs_7_.refs_0_), channel_id=1, source_target_pairs={{0,8},{4,12},{8,0},{12,4},{16,24},{20,28},{24,16},{28,20},{1,9},{5... | collective-permute-start | bytes 786440 | tf_op jit(solution)/shard_map/ppermute | solution.py:1098
  57.1 33.2 %collective-permute-start.14 = (bf16[1024,512]{1,0:T(8,128)(2,1)}, bf16[1024,512]{1,0:T(8,128)(2,1)}, u32[]{:S(2)}, u32[]{:S(2)}) collective-permute-start(bf16[1024,512]{1,0:T(8,128)(2,1)} %constant_dynamic-slice_fusion.10), channel_id=1, source_target_pairs={{0,2},{2,0},{1,3},{3,1},{4,6},{6,4},{5,7},{7,5},{8,10},{10,8},{9,1... | collective-permute-start | bytes 3145736 | tf_op jit(solution)/shard_map/ppermute | solution.py:1095
  68.6 12.5 %collective-permute-start.13 = (bf16[128,1024]{1,0:T(8,128)(2,1)}, bf16[128,1024]{1,0:T(8,128)(2,1)S(1)}, u32[]{:S(2)}, u32[]{:S(2)}) collective-permute-start(bf16[128,1024]{1,0:T(8,128)(2,1)} %collective-permute-done.4.refs_19_.refs_7_), channel_id=1, source_target_pairs={{0,4},{4,0},{8,12},{12,8},{16,20},{20,16},{24,28},{28,24},{1,5},{5... | collective-permute-start | bytes 786440 | tf_op jit(solution)/shard_map/ppermute | solution.py:1098
  69.2 11.9 %collective-permute-start.15 = (bf16[2,2,64,256]{3,2,1,0:T(8,128)(2,1)S(1)}, bf16[2,2,64,256]{3,2,1,0:T(8,128)(2,1)S(1)}, u32[]{:S(2)}, u32[]{:S(2)}) collective-permute-start(bf16[2,2,64,256]{3,2,1,0:T(8,128)(2,1)S(1)} %pad_maximum_fusion.6), channel_id=1, source_target_pairs={{0,1},{1,0},{2,3},{3,2},{4,5},{5,4},{6,7},{7,6},{8,9},{9,8},{10,11... | collective-permute-start | bytes 393224 | tf_op jit(solution)/shard_map/ppermute | solution.py:1092
  76.8 15.5 %collective-permute-start.18 = (bf16[128,1024]{1,0:T(8,128)(2,1)S(1)}, bf16[128,1024]{1,0:T(8,128)(2,1)S(1)}, u32[]{:S(2)}, u32[]{:S(2)}) collective-permute-start(bf16[128,1024]{1,0:T(8,128)(2,1)S(1)} %collective-permute-done.2.refs_7_.refs_0_), channel_id=1, source_target_pairs={{0,1},{1,0},{2,3},{3,2},{4,5},{5,4},{6,7},{7,6},{8,9},{9,8},{10,11... | collective-permute-start | bytes 786440 | tf_op jit(solution)/shard_map/ppermute | solution.py:1092
  76.9 15.5 %collective-permute-start.20 = (bf16[1024,128]{1,0:T(8,128)(2,1)}, bf16[1024,128]{1,0:T(8,128)(2,1)S(1)}, u32[]{:S(2)}, u32[]{:S(2)}) collective-permute-start(bf16[1024,128]{1,0:T(8,128)(2,1)} %collective-permute-done.3.refs_13_.refs_1_), channel_id=1, source_target_pairs={{0,1},{1,0},{2,3},{3,2},{4,5},{5,4},{6,7},{7,6},{8,9},{9,8},{10,11... | collective-permute-start | bytes 786440 | tf_op jit(solution)/shard_map/ppermute | solution.py:1092
  81.1 12.9 %collective-permute-start.22 = (bf16[128,1024]{1,0:T(8,128)(2,1)}, bf16[128,1024]{1,0:T(8,128)(2,1)S(1)}, u32[]{:S(2)}, u32[]{:S(2)}) collective-permute-start(bf16[128,1024]{1,0:T(8,128)(2,1)} %collective-permute-done.4.refs_19_.refs_7_), channel_id=1, source_target_pairs={{0,1},{1,0},{2,3},{3,2},{4,5},{5,4},{6,7},{7,6},{8,9},{9,8},{10,11... | collective-permute-start | bytes 786440 | tf_op jit(solution)/shard_map/ppermute | solution.py:1092
  90.8 34.8 %collective-permute-start.24 = (bf16[512,1024]{1,0:T(8,128)(2,1)S(1)}, bf16[512,1024]{1,0:T(8,128)(2,1)S(1)}, u32[]{:S(2)}, u32[]{:S(2)}) collective-permute-start(bf16[512,1024]{1,0:T(8,128)(2,1)S(1)} %copy-done.109), channel_id=1, source_target_pairs={{0,2},{2,0},{1,3},{3,1},{4,6},{6,4},{5,7},{7,5},{8,10},{10,8},{9,1... | collective-permute-start | bytes 3145736 | tf_op jit(solution)/shard_map/ppermute | solution.py:1095
  125.6 14.7 %collective-permute-start.25 = (bf16[832,1024]{1,0:T(8,128)(2,1)}, bf16[832,1024]{1,0:T(8,128)(2,1)S(1)}, u32[]{:S(2)}, u32[]{:S(2)}) collective-permute-start(bf16[832,1024]{1,0:T(8,128)(2,1)} %get-tuple-element.319.h_ref.mine_ref), channel_id=1, source_target_pairs={{0,1},{1,0},{2,3},{3,2},{4,5},{5,4},{6,7},{7,6},{8,9},{9,8},{10,11... | collective-permute-start | bytes 5111816 | tf_op jit(solution)/shard_map/ppermute | solution.py:1092
  125.8 14.5 %collective-permute-start.26 = (bf16[832,1024]{1,0:T(8,128)(2,1)S(1)}, bf16[832,1024]{1,0:T(8,128)(2,1)S(1)}, u32[]{:S(2)}, u32[]{:S(2)}) collective-permute-start(bf16[832,1024]{1,0:T(8,128)(2,1)S(1)} %broadcast_select_fusion.d_ref.mine_ref), channel_id=1, source_target_pairs={{0,1},{1,0},{2,3},{3,2},{4,5},{5,4},{6,7},{7,6},{8,9},{9,8},{10,11... | collective-permute-start | bytes 5111816 | tf_op jit(solution)/shard_map/ppermute | solution.py:1092
  126.2 28.0 %collective-permute-start.27 = (bf16[1024,512]{1,0:T(8,128)(2,1)}, bf16[1024,512]{1,0:T(8,128)(2,1)}, u32[]{:S(2)}, u32[]{:S(2)}) collective-permute-start(bf16[1024,512]{1,0:T(8,128)(2,1)} %collective-permute-done.14.refs_0_), channel_id=1, source_target_pairs={{0,4},{4,0},{8,12},{12,8},{16,20},{20,16},{24,28},{28,24},{1,5},{5... | collective-permute-start | bytes 3145736 | tf_op jit(solution)/shard_map/ppermute | solution.py:1098
  127.7 46.5 %collective-permute-start.28 = (bf16[512,1024]{1,0:T(8,128)(2,1)S(1)}, bf16[512,1024]{1,0:T(8,128)(2,1)}, u32[]{:S(2)}, u32[]{:S(2)}) collective-permute-start(bf16[512,1024]{1,0:T(8,128)(2,1)S(1)} %collective-permute-done.24.refs_2_), channel_id=1, source_target_pairs={{0,4},{4,0},{8,12},{12,8},{16,20},{20,16},{24,28},{28,24},{1,5},{5... | collective-permute-start | bytes 3145736 | tf_op jit(solution)/shard_map/ppermute | solution.py:1098
  187.6 29.1 %collective-permute-start.30 = (bf16[832,1024]{1,0:T(8,128)(2,1)}, bf16[832,1024]{1,0:T(8,128)(2,1)S(1)}, u32[]{:S(2)}, u32[]{:S(2)}) collective-permute-start(bf16[832,1024]{1,0:T(8,128)(2,1)} %get-tuple-element.333), channel_id=1, source_target_pairs={{0,1},{1,0},{2,3},{3,2},{4,5},{5,4},{6,7},{7,6},{8,9},{9,8},{10,11... | collective-permute-start | bytes 5111816 | tf_op jit(solution)/shard_map/ppermute | solution.py:1092
  208.7 48.3 %collective-permute-start.31 = (bf16[1024,1024]{1,0:T(8,128)(2,1)}, bf16[1024,1024]{1,0:T(8,128)(2,1)}, u32[]{:S(2)}, u32[]{:S(2)}) collective-permute-start(bf16[1024,1024]{1,0:T(8,128)(2,1)} %up_grad.2), channel_id=1, source_target_pairs={{0,2},{2,0},{1,3},{3,1},{4,6},{6,4},{5,7},{7,5},{8,10},{10,8},{9,1... | collective-permute-start | bytes 6291464 | tf_op jit(solution)/shard_map/ppermute | solution.py:1095
  241.3 15.8 %collective-permute-start.32 = (bf16[832,1024]{1,0:T(8,128)(2,1)}, bf16[832,1024]{1,0:T(8,128)(2,1)S(1)}, u32[]{:S(2)}, u32[]{:S(2)}) collective-permute-start(bf16[832,1024]{1,0:T(8,128)(2,1)} %get-tuple-element.365.mine_ref.refs_2_.refs_1_), channel_id=1, source_target_pairs={{0,1},{1,0},{2,3},{3,2},{4,5},{5,4},{6,7},{7,6},{8,9},{9,8},{10,11... | collective-permute-start | bytes 5111816 | tf_op jit(solution)/shard_map/ppermute | solution.py:1092
  261.8 24.6 %collective-permute-start.34 = (bf16[832,1024]{1,0:T(8,128)(2,1)}, bf16[832,1024]{1,0:T(8,128)(2,1)}, u32[]{:S(2)}, u32[]{:S(2)}) collective-permute-start(bf16[832,1024]{1,0:T(8,128)(2,1)} %get-tuple-element.442.refs_6_.refs_5_), channel_id=1, source_target_pairs={{0,1},{1,0},{2,3},{3,2},{4,5},{5,4},{6,7},{7,6},{8,9},{9,8},{10,11... | collective-permute-start | bytes 5111816 | tf_op jit(solution)/shard_map/ppermute | solution.py:1092
  262.8 23.4 %collective-permute-start.35 = (bf16[832,512]{1,0:T(8,128)(2,1)}, bf16[832,512]{1,0:T(8,128)(2,1)}, u32[]{:S(2)}, u32[]{:S(2)}) collective-permute-start(bf16[832,512]{1,0:T(8,128)(2,1)} %slice.78), channel_id=1, source_target_pairs={{0,1},{1,0},{2,3},{3,2},{4,5},{5,4},{6,7},{7,6},{8,9},{9,8},{10,11... | collective-permute-start | bytes 2555912 | tf_op jit(solution)/shard_map/ppermute | solution.py:1092
  263.3 34.1 %collective-permute-start.37 = (bf16[512,1024]{1,0:T(8,128)(2,1)}, bf16[512,1024]{1,0:T(8,128)(2,1)}, u32[]{:S(2)}, u32[]{:S(2)}) collective-permute-start(bf16[512,1024]{1,0:T(8,128)(2,1)} %get-tuple-element.542), channel_id=1, source_target_pairs={{0,4},{4,0},{8,12},{12,8},{16,20},{20,16},{24,28},{28,24},{1,5},{5... | collective-permute-start | bytes 3145736 | tf_op jit(solution)/shard_map/ppermute | solution.py:1098
  270.5 14.9 %collective-permute-start.36 = (f32[2,2,64,256]{3,2,0,1:T(8,128)S(1)}, f32[2,2,64,256]{3,2,0,1:T(8,128)S(1)}, u32[]{:S(2)}, u32[]{:S(2)}) collective-permute-start(f32[2,2,64,256]{3,2,0,1:T(8,128)S(1)} %get-tuple-element.555), channel_id=1, source_target_pairs={{0,1},{1,0},{2,3},{3,2},{4,5},{5,4},{6,7},{7,6},{8,9},{9,8},{10,11... | collective-permute-start | bytes 786440 | tf_op jit(solution)/shard_map/ppermute | solution.py:1092
  270.5 48.4 %collective-permute-start.33 = (bf16[1024,1024]{1,0:T(8,128)(2,1)}, bf16[1024,1024]{1,0:T(8,128)(2,1)}, u32[]{:S(2)}, u32[]{:S(2)}) collective-permute-start(bf16[1024,1024]{1,0:T(8,128)(2,1)} %copy-done.27), channel_id=1, source_target_pairs={{0,2},{2,0},{1,3},{3,1},{4,6},{6,4},{5,7},{7,5},{8,10},{10,8},{9,1... | collective-permute-start | bytes 6291464 | tf_op jit(solution)/shard_map/ppermute | solution.py:1095
  285.4 252.5 %collective-permute-start.29 = (bf16[832,1024]{1,0:T(8,128)(2,1)}, bf16[832,1024]{1,0:T(8,128)(2,1)}, u32[]{:S(2)}, u32[]{:S(2)}) collective-permute-start(bf16[832,1024]{1,0:T(8,128)(2,1)} %get-tuple-element.332), channel_id=1, source_target_pairs={{0,1},{1,0},{2,3},{3,2},{4,5},{5,4},{6,7},{7,6},{8,9},{9,8},{10,11... | collective-permute-start | bytes 5111816 | tf_op jit(solution)/shard_map/ppermute | solution.py:1092
  286.2 39.8 %collective-permute-start.41 = (bf16[832,1024]{1,0:T(8,128)(2,1)S(1)}, bf16[832,1024]{1,0:T(8,128)(2,1)S(1)}, u32[]{:S(2)}, u32[]{:S(2)}) collective-permute-start(bf16[832,1024]{1,0:T(8,128)(2,1)S(1)} %copy-done.9), channel_id=1, source_target_pairs={{0,1},{1,0},{2,3},{3,2},{4,5},{5,4},{6,7},{7,6},{8,9},{9,8},{10,11... | collective-permute-start | bytes 5111816 | tf_op jit(solution)/shard_map/ppermute | solution.py:1092
  286.3 43.3 %collective-permute-start.43 = (bf16[832,512]{1,0:T(8,128)(2,1)}, bf16[832,512]{1,0:T(8,128)(2,1)S(1)}, u32[]{:S(2)}, u32[]{:S(2)}) collective-permute-start(bf16[832,512]{1,0:T(8,128)(2,1)} %slice.81), channel_id=1, source_target_pairs={{0,1},{1,0},{2,3},{3,2},{4,5},{5,4},{6,7},{7,6},{8,9},{9,8},{10,11... | collective-permute-start | bytes 2555912 | tf_op jit(solution)/shard_map/ppermute | solution.py:1092
  309.6 14.6 %collective-permute-start.39 = (bf16[256,1024]{1,0:T(8,128)(2,1)S(1)}, bf16[256,1024]{1,0:T(8,128)(2,1)S(1)}, u32[]{:S(2)}, u32[]{:S(2)}) collective-permute-start(bf16[256,1024]{1,0:T(8,128)(2,1)S(1)} %dynamic-slice_convert_fusion.1), channel_id=1, source_target_pairs={{0,8},{4,12},{8,0},{12,4},{16,24},{20,28},{24,16},{28,20},{1,9},{5... | collective-permute-start | bytes 1572872 | tf_op jit(solution)/shard_map/ppermute | solution.py:1098
  318.9 39.5 %collective-permute-start.42 = (bf16[3072,256]{1,0:T(8,128)(2,1)S(1)}, bf16[3072,256]{1,0:T(8,128)(2,1)}, u32[]{:S(2)}, u32[]{:S(2)}) collective-permute-start(bf16[3072,256]{1,0:T(8,128)(2,1)S(1)} %qkv_grad.2), channel_id=1, source_target_pairs={{0,2},{2,0},{1,3},{3,1},{4,6},{6,4},{5,7},{7,5},{8,10},{10,8},{9,1... | collective-permute-start | bytes 4718600 | tf_op jit(solution)/shard_map/ppermute | solution.py:1095
  324.2 78.6 %collective-permute-start.47 = (bf16[2,64,256]{2,1,0:T(8,128)(2,1)}, bf16[2,64,256]{2,1,0:T(8,128)(2,1)}, u32[]{:S(2)}, u32[]{:S(2)}) collective-permute-start(bf16[2,64,256]{2,1,0:T(8,128)(2,1)} %maximum_select_fusion.12), channel_id=1, source_target_pairs={{0,2},{2,0},{1,3},{3,1},{4,6},{6,4},{5,7},{7,5},{8,10},{10,8},{9,1... | collective-permute-start | bytes 196616 | tf_op jit(solution)/shard_map/ppermute | solution.py:1095
  326.0 34.1 %collective-permute-start.38 = (bf16[512,1024]{1,0:T(8,128)(2,1)}, bf16[512,1024]{1,0:T(8,128)(2,1)}, u32[]{:S(2)}, u32[]{:S(2)}) collective-permute-start(bf16[512,1024]{1,0:T(8,128)(2,1)} %get-tuple-element.541), channel_id=1, source_target_pairs={{0,4},{4,0},{8,12},{12,8},{16,20},{20,16},{24,28},{28,24},{1,5},{5... | collective-permute-start | bytes 3145736 | tf_op jit(solution)/shard_map/ppermute | solution.py:1098
  329.6 28.7 %collective-permute-start.40 = (bf16[256,1024]{1,0:T(8,128)(2,1)S(1)}, bf16[256,1024]{1,0:T(8,128)(2,1)}, u32[]{:S(2)}, u32[]{:S(2)}) collective-permute-start(bf16[256,1024]{1,0:T(8,128)(2,1)S(1)} %add_convert_fusion.9), channel_id=1, source_target_pairs={{0,16},{4,20},{8,24},{12,28},{16,0},{20,4},{24,8},{28,12},{1,17},{... | collective-permute-start | bytes 1572872 | tf_op jit(solution)/shard_map/ppermute | solution.py:1098
  364.4 17.2 %collective-permute-start.45 = (bf16[256,1024]{1,0:T(8,128)(2,1)S(1)}, bf16[256,1024]{1,0:T(8,128)(2,1)}, u32[]{:S(2)}, u32[]{:S(2)}) collective-permute-start(bf16[256,1024]{1,0:T(8,128)(2,1)S(1)} %add_convert_fusion.8), channel_id=1, source_target_pairs={{0,8},{4,12},{8,0},{12,4},{16,24},{20,28},{24,16},{28,20},{1,9},{5... | collective-permute-start | bytes 1572872 | tf_op jit(solution)/shard_map/ppermute | solution.py:1098
  364.8 23.3 %collective-permute-start.44 = (bf16[256,1024]{1,0:T(8,128)(2,1)}, bf16[256,1024]{1,0:T(8,128)(2,1)}, u32[]{:S(2)}, u32[]{:S(2)}) collective-permute-start(bf16[256,1024]{1,0:T(8,128)(2,1)} %dynamic-slice_convert_fusion), channel_id=1, source_target_pairs={{0,8},{4,12},{8,0},{12,4},{16,24},{20,28},{24,16},{28,20},{1,9},{5... | collective-permute-start | bytes 1572872 | tf_op jit(solution)/shard_map/ppermute | solution.py:1098
  372.5 26.5 %collective-permute-start.48 = (bf16[512,1024]{1,0:T(8,128)(2,1)}, bf16[512,1024]{1,0:T(8,128)(2,1)}, u32[]{:S(2)}, u32[]{:S(2)}) collective-permute-start(bf16[512,1024]{1,0:T(8,128)(2,1)} %outputs_grad.2), channel_id=1, source_target_pairs={{0,2},{2,0},{1,3},{3,1},{4,6},{6,4},{5,7},{7,5},{8,10},{10,8},{9,1... | collective-permute-start | bytes 3145736 | tf_op jit(solution)/shard_map/ppermute | solution.py:1095
  381.6 46.7 %collective-permute-start.55 = (bf16[832,1024]{1,0:T(8,128)(2,1)}, bf16[832,1024]{1,0:T(8,128)(2,1)}, u32[]{:S(2)}, u32[]{:S(2)}) collective-permute-start(bf16[832,1024]{1,0:T(8,128)(2,1)} %first_back.2), channel_id=1, source_target_pairs={{0,1},{1,0},{2,3},{3,2},{4,5},{5,4},{6,7},{7,6},{8,9},{9,8},{10,11... | collective-permute-start | bytes 5111816 | tf_op jit(solution)/shard_map/ppermute | solution.py:1092
  388.1 19.0 %collective-permute-start.46 = (bf16[1024,256]{1,0:T(8,128)(2,1)S(1)}, bf16[1024,256]{1,0:T(8,128)(2,1)S(1)}, u32[]{:S(2)}, u32[]{:S(2)}) collective-permute-start(bf16[1024,256]{1,0:T(8,128)(2,1)S(1)} %copy-done.62), channel_id=1, source_target_pairs={{0,2},{2,0},{1,3},{3,1},{4,6},{6,4},{5,7},{7,5},{8,10},{10,8},{9,1... | collective-permute-start | bytes 1572872 | tf_op jit(solution)/shard_map/ppermute | solution.py:1095
  398.9 20.7 %collective-permute-start.50 = (bf16[1536,256]{1,0:T(8,128)(2,1)}, bf16[1536,256]{1,0:T(8,128)(2,1)S(1)}, u32[]{:S(2)}, u32[]{:S(2)}) collective-permute-start(bf16[1536,256]{1,0:T(8,128)(2,1)} %get-tuple-element.544), channel_id=1, source_target_pairs={{0,4},{4,0},{8,12},{12,8},{16,20},{20,16},{24,28},{28,24},{1,5},{5... | collective-permute-start | bytes 2359304 | tf_op jit(solution)/shard_map/ppermute | solution.py:1098
  402.8 40.1 %collective-permute-start.52 = (bf16[512,1024]{1,0:T(8,128)(2,1)}, bf16[512,1024]{1,0:T(8,128)(2,1)S(1)}, u32[]{:S(2)}, u32[]{:S(2)}) collective-permute-start(bf16[512,1024]{1,0:T(8,128)(2,1)} %maximum_select_fusion.4), channel_id=1, source_target_pairs={{0,4},{4,0},{8,12},{12,8},{16,20},{20,16},{24,28},{28,24},{1,5},{5... | collective-permute-start | bytes 3145736 | tf_op jit(solution)/shard_map/ppermute | solution.py:1098
  407.0 28.8 %collective-permute-start.54 = (bf16[256,1024]{1,0:T(8,128)(2,1)}, bf16[256,1024]{1,0:T(8,128)(2,1)}, u32[]{:S(2)}, u32[]{:S(2)}) collective-permute-start(bf16[256,1024]{1,0:T(8,128)(2,1)} %add_convert_fusion.7), channel_id=1, source_target_pairs={{0,16},{4,20},{8,24},{12,28},{16,0},{20,4},{24,8},{28,12},{1,17},{... | collective-permute-start | bytes 1572872 | tf_op jit(solution)/shard_map/ppermute | solution.py:1098
  419.6 22.0 %collective-permute-start.53 = (bf16[256,1024]{1,0:T(8,128)(2,1)}, bf16[256,1024]{1,0:T(8,128)(2,1)}, u32[]{:S(2)}, u32[]{:S(2)}) collective-permute-start(bf16[256,1024]{1,0:T(8,128)(2,1)} %get-tuple-element.548), channel_id=1, source_target_pairs={{0,8},{4,12},{8,0},{12,4},{16,24},{20,28},{24,16},{28,20},{1,9},{5... | collective-permute-start | bytes 1572872 | tf_op jit(solution)/shard_map/ppermute | solution.py:1098
  428.2 38.9 %collective-permute-start.49 = (bf16[1536,256]{1,0:T(8,128)(2,1)}, bf16[1536,256]{1,0:T(8,128)(2,1)S(1)}, u32[]{:S(2)}, u32[]{:S(2)}) collective-permute-start(bf16[1536,256]{1,0:T(8,128)(2,1)} %get-tuple-element.551), channel_id=1, source_target_pairs={{0,8},{4,12},{8,0},{12,4},{16,24},{20,28},{24,16},{28,20},{1,9},{5... | collective-permute-start | bytes 2359304 | tf_op jit(solution)/shard_map/ppermute | solution.py:1098
  435.8 31.0 %collective-permute-start.51 = (bf16[768,256]{1,0:T(8,128)(2,1)S(1)}, bf16[768,256]{1,0:T(8,128)(2,1)S(1)}, u32[]{:S(2)}, u32[]{:S(2)}) collective-permute-start(bf16[768,256]{1,0:T(8,128)(2,1)S(1)} %dynamic-slice_convert_fusion.3), channel_id=1, source_target_pairs={{0,8},{4,12},{8,0},{12,4},{16,24},{20,28},{24,16},{28,20},{1,9},{5... | collective-permute-start | bytes 1179656 | tf_op jit(solution)/shard_map/ppermute | solution.py:1098
  441.7 32.1 %collective-permute-start.60 = (bf16[256,1024]{1,0:T(8,128)(2,1)S(1)}, bf16[256,1024]{1,0:T(8,128)(2,1)S(1)}, u32[]{:S(2)}, u32[]{:S(2)}) collective-permute-start(bf16[256,1024]{1,0:T(8,128)(2,1)S(1)} %add_convert_fusion.4), channel_id=1, source_target_pairs={{0,8},{4,12},{8,0},{12,4},{16,24},{20,28},{24,16},{28,20},{1,9},{5... | collective-permute-start | bytes 1572872 | tf_op jit(solution)/shard_map/ppermute | solution.py:1098
  467.0 19.9 %collective-permute-start.58 = (bf16[768,256]{1,0:T(8,128)(2,1)S(1)}, bf16[768,256]{1,0:T(8,128)(2,1)S(1)}, u32[]{:S(2)}, u32[]{:S(2)}) collective-permute-start(bf16[768,256]{1,0:T(8,128)(2,1)S(1)} %add_convert_fusion.13), channel_id=1, source_target_pairs={{0,16},{4,20},{8,24},{12,28},{16,0},{20,4},{24,8},{28,12},{1,17},{... | collective-permute-start | bytes 1179656 | tf_op jit(solution)/shard_map/ppermute | solution.py:1098
  469.0 21.4 %collective-permute-start.56 = (bf16[768,256]{1,0:T(8,128)(2,1)S(1)}, bf16[768,256]{1,0:T(8,128)(2,1)S(1)}, u32[]{:S(2)}, u32[]{:S(2)}) collective-permute-start(bf16[768,256]{1,0:T(8,128)(2,1)S(1)} %dynamic-slice_convert_fusion.2), channel_id=1, source_target_pairs={{0,4},{4,0},{8,12},{12,8},{16,20},{20,16},{24,28},{28,24},{1,5},{5... | collective-permute-start | bytes 1179656 | tf_op jit(solution)/shard_map/ppermute | solution.py:1098
  487.0 16.8 %collective-permute-start.63 = (bf16[768,256]{1,0:T(8,128)(2,1)S(1)}, bf16[768,256]{1,0:T(8,128)(2,1)S(1)}, u32[]{:S(2)}, u32[]{:S(2)}) collective-permute-start(bf16[768,256]{1,0:T(8,128)(2,1)S(1)} %add_convert_fusion.12), channel_id=1, source_target_pairs={{0,8},{4,12},{8,0},{12,4},{16,24},{20,28},{24,16},{28,20},{1,9},{5... | collective-permute-start | bytes 1179656 | tf_op jit(solution)/shard_map/ppermute | solution.py:1098
  487.1 30.4 %collective-permute-start.64 = (f32[64,1024]{1,0:T(8,128)S(1)}, f32[64,1024]{1,0:T(8,128)S(1)}, u32[]{:S(2)}, u32[]{:S(2)}) collective-permute-start(f32[64,1024]{1,0:T(8,128)S(1)} %get-tuple-element.553), channel_id=1, source_target_pairs={{0,2},{2,0},{1,3},{3,1},{4,6},{6,4},{5,7},{7,5},{8,10},{10,8},{9,1... | collective-permute-start | bytes 786440 | tf_op jit(solution)/shard_map/ppermute | solution.py:1095
  487.7 16.4 %collective-permute-start.66 = (bf16[128,1024]{1,0:T(8,128)(2,1)S(1)}, bf16[128,1024]{1,0:T(8,128)(2,1)S(1)}, u32[]{:S(2)}, u32[]{:S(2)}) collective-permute-start(bf16[128,1024]{1,0:T(8,128)(2,1)S(1)} %add_convert_fusion.15), channel_id=1, source_target_pairs={{0,16},{4,20},{8,24},{12,28},{16,0},{20,4},{24,8},{28,12},{1,17},{... | collective-permute-start | bytes 786440 | tf_op jit(solution)/shard_map/ppermute | solution.py:1098
  490.4 39.0 %collective-permute-start.70 = (bf16[512,1024]{1,0:T(8,128)(2,1)S(1)}, bf16[512,1024]{1,0:T(8,128)(2,1)}, u32[]{:S(2)}, u32[]{:S(2)}) collective-permute-start(bf16[512,1024]{1,0:T(8,128)(2,1)S(1)} %maximum_select_fusion.5), channel_id=1, source_target_pairs={{0,4},{4,0},{8,12},{12,8},{16,20},{20,16},{24,28},{28,24},{1,5},{5... | collective-permute-start | bytes 3145736 | tf_op jit(solution)/shard_map/ppermute | solution.py:1098
  503.8 18.6 %collective-permute-start.62 = (bf16[768,256]{1,0:T(8,128)(2,1)S(1)}, bf16[768,256]{1,0:T(8,128)(2,1)S(1)}, u32[]{:S(2)}, u32[]{:S(2)}) collective-permute-start(bf16[768,256]{1,0:T(8,128)(2,1)S(1)} %add_convert_fusion.11), channel_id=1, source_target_pairs={{0,16},{4,20},{8,24},{12,28},{16,0},{20,4},{24,8},{28,12},{1,17},{... | collective-permute-start | bytes 1179656 | tf_op jit(solution)/shard_map/ppermute | solution.py:1098
  504.1 11.3 %collective-permute-start.65 = (f32[8,1024]{1,0:T(8,128)S(1)}, f32[8,1024]{1,0:T(8,128)S(1)}, u32[]{:S(2)}, u32[]{:S(2)}) collective-permute-start(f32[8,1024]{1,0:T(8,128)S(1)} %add.254), channel_id=1, source_target_pairs={{0,4},{4,0},{8,12},{12,8},{16,20},{20,16},{24,28},{28,24},{1,5},{5... | collective-permute-start | bytes 98312 | tf_op jit(solution)/shard_map/ppermute | solution.py:1098
  522.4 13.9 %collective-permute-start.67 = (bf16[768,256]{1,0:T(8,128)(2,1)S(1)}, bf16[768,256]{1,0:T(8,128)(2,1)}, u32[]{:S(2)}, u32[]{:S(2)}) collective-permute-start(bf16[768,256]{1,0:T(8,128)(2,1)S(1)} %add_convert_fusion.10), channel_id=1, source_target_pairs={{0,4},{4,0},{8,12},{12,8},{16,20},{20,16},{24,28},{28,24},{1,5},{5... | collective-permute-start | bytes 1179656 | tf_op jit(solution)/shard_map/ppermute | solution.py:1098
  524.0 10.5 %collective-permute-start.69 = (f32[64,1024]{1,0:T(8,128)S(1)}, f32[64,1024]{1,0:T(8,128)S(1)}, u32[]{:S(2)}, u32[]{:S(2)}) collective-permute-start(f32[64,1024]{1,0:T(8,128)S(1)} %add.260), channel_id=1, source_target_pairs={{0,1},{1,0},{2,3},{3,2},{4,5},{5,4},{6,7},{7,6},{8,9},{9,8},{10,11... | collective-permute-start | bytes 786440 | tf_op jit(solution)/shard_map/ppermute | solution.py:1092
  528.1 22.4 %collective-permute-start.75 = (bf16[1536,256]{1,0:T(8,128)(2,1)S(1)}, bf16[1536,256]{1,0:T(8,128)(2,1)}, u32[]{:S(2)}, u32[]{:S(2)}) collective-permute-start(bf16[1536,256]{1,0:T(8,128)(2,1)S(1)} %maximum_select_fusion.7), channel_id=1, source_target_pairs={{0,4},{4,0},{8,12},{12,8},{16,20},{20,16},{24,28},{28,24},{1,5},{5... | collective-permute-start | bytes 2359304 | tf_op jit(solution)/shard_map/ppermute | solution.py:1098
  529.4 13.4 %collective-permute-start.73 = (f32[8,1024]{1,0:T(8,128)S(1)}, f32[8,1024]{1,0:T(8,128)S(1)}, u32[]{:S(2)}, u32[]{:S(2)}) collective-permute-start(f32[8,1024]{1,0:T(8,128)S(1)} %add.262), channel_id=1, source_target_pairs={{0,16},{4,20},{8,24},{12,28},{16,0},{20,4},{24,8},{28,12},{1,17},{... | collective-permute-start | bytes 98312 | tf_op jit(solution)/shard_map/ppermute | solution.py:1098
  534.5 19.5 %collective-permute-start.74 = (bf16[256,1024]{1,0:T(8,128)(2,1)S(1)}, bf16[256,1024]{1,0:T(8,128)(2,1)S(1)}, u32[]{:S(2)}, u32[]{:S(2)}) collective-permute-start(bf16[256,1024]{1,0:T(8,128)(2,1)S(1)} %maximum_select_fusion.9), channel_id=1, source_target_pairs={{0,8},{4,12},{8,0},{12,4},{16,24},{20,28},{24,16},{28,20},{1,9},{5... | collective-permute-start | bytes 1572872 | tf_op jit(solution)/shard_map/ppermute | solution.py:1098
  537.7 27.1 %collective-permute-start.76 = (bf16[1536,256]{1,0:T(8,128)(2,1)S(1)}, bf16[1536,256]{1,0:T(8,128)(2,1)}, u32[]{:S(2)}, u32[]{:S(2)}) collective-permute-start(bf16[1536,256]{1,0:T(8,128)(2,1)S(1)} %maximum_select_fusion.8), channel_id=1, source_target_pairs={{0,8},{4,12},{8,0},{12,4},{16,24},{20,28},{24,16},{28,20},{1,9},{5... | collective-permute-start | bytes 2359304 | tf_op jit(solution)/shard_map/ppermute | solution.py:1098
  537.9 16.0 %collective-permute-start.72 = (bf16[64,1024]{1,0:T(8,128)(2,1)S(1)}, bf16[64,1024]{1,0:T(8,128)(2,1)S(1)}, u32[]{:S(2)}, u32[]{:S(2)}) collective-permute-start(bf16[64,1024]{1,0:T(8,128)(2,1)S(1)} %add_convert_fusion.16), channel_id=1, source_target_pairs={{0,2},{2,0},{1,3},{3,1},{4,6},{6,4},{5,7},{7,5},{8,10},{10,8},{9,1... | collective-permute-start | bytes 393224 | tf_op jit(solution)/shard_map/ppermute | solution.py:1095
  (148 other events, 1157.0 us)

commit v10 on v9

--- a/solution.py
+++ b/solution.py
@@ -614,7 +614,7 @@
         ),
         out_shape=[shape((span, wide), ROUND)] * 3,
         compiler_params=params(48),
-        cost_estimate=lasting(9.8 * pairs),
+        cost_estimate=lasting(7.00 * pairs),
         name="self_back",
     )(limit, q, k, v, o, do, lse)
 
@@ -655,8 +655,9 @@
     h2_ref[...] = h2
     for g, weight in enumerate(in_groups(wq, 1)):
         lanes = slice(g * 256, (g + 1) * 256)
-        cq_ref[:, lanes] = lower(nn(h2, weight))
-        probability = cross_probability(cq_ref[:, lanes], ck_ref[g])
+        cq = lower(nn(h2, weight))
+        cq_ref[:, lanes] = cq
+        probability = cross_probability(cq, ck_ref[g])
         ca_ref[:, lanes] = lower(nn(lower(probability), cv_ref[g]))
     crossed = 0.0
     for g, weight in enumerate(in_groups(wc, 0)):
@@ -789,7 +790,7 @@
         out_specs=pl.BlockSpec((width, tile), lambda i: (0, i)),
         out_shape=shape((width, hidden), kind),
         compiler_params=params(48),
-        cost_estimate=lasting(7),
+        cost_estimate=lasting(5.00),
         name="up_grad",
     )(mine, other, du)
 
@@ -812,7 +813,7 @@
         out_specs=pl.BlockSpec((tile, width), lambda i: (i, 0)),
         out_shape=shape((hidden, width), kind),
         compiler_params=params(48),
-        cost_estimate=lasting(7),
+        cost_estimate=lasting(5.00),
         name="down_grad",
     )(g, mine, other)
 
@@ -852,7 +853,7 @@
         ),
         out_shape=shape((3 * width, 256), kind),
         compiler_params=params(48),
-        cost_estimate=lasting(7),
+        cost_estimate=lasting(5.00),
         name="qkv_grad",
     )(place, h, *grads)
 
@@ -881,7 +882,7 @@
         ),
         out_shape=shape((width, 256), kind),
         compiler_params=params(48),
-        cost_estimate=lasting(4),
+        cost_estimate=lasting(2.86),
         name="query_grad",
     )(place, mine, other, d_mine, d_other)
 
@@ -923,7 +924,7 @@
         ),
         out_shape=shape((512, width), kind),
         compiler_params=params(48),
-        cost_estimate=lasting(6),
+        cost_estimate=lasting(4.29),
         name="outputs_grad",
     )(place, *o, dself, dself_other, ca, ca_other, dcross, dcross_other)
 
@@ -1036,7 +1037,7 @@
         ),
         out_shape=shape((rows, width), kind),
         compiler_params=params(40),
-        cost_estimate=lasting(5),
+        cost_estimate=lasting(3.57),
         name="first_back",
     )(place, *grads, *weights)
 
@@ -1067,7 +1068,7 @@
         ),
         out_shape=[shape((rows, width), ROUND), shape((8, width), FULL)],
         compiler_params=params(24),
-        cost_estimate=lasting(6),
+        cost_estimate=lasting(4.29),
         name="frames_back",
     )(place, ym, yr, dx1, frames, gains)
 
@@ -1185,7 +1186,7 @@
         place, frames, (o0, of, o_s), (o0_other, of_other, os_other), wo, wq, wc, ck, cv,
         norm_gain, norm_bias,
     )
-    h3, ca, h2, down_first, dout = join((h3, ca, h2, down_first, dout))
+    h3, ca, h2, up_second, down_first, dout = join((h3, ca, h2, up_second, down_first, dout))
 
     h3_other = over_core(h3)
     dout_other = over_core(dout)
@@ -1194,7 +1195,7 @@
     g0, du0, out_o, y_o = feed(
         place, h3_other, dout_other, (w_up,), (w_down,), FULL, 1, shared=(g0, du0)
     )
-    y_o, up_second, down_second, ca, h2 = join((y_o, up_second, down_second, ca, h2))
+    y_o, down_second, ca, h2 = join((y_o, down_second, ca, h2))
 
     ups = (up_first, up_second)
     downs = (down_first, down_second)
@@ -1300,8 +1301,8 @@
         def total(self):
             return store[self.kept] + store[self.fly]
 
-    up, down, qkv = Sum("up"), Sum("down"), Sum("qkv")
-    outs, cross_in = Sum("outs", (down_z, across)), Sum("cross_in", (down_z, across))
+    up, down, outs, cross_in = Sum("up"), Sum("down"), Sum("outs"), Sum("cross_in")
+    qkv = Sum("qkv", (down_z, across))
     store.update(h3_other=h3_other, du1=du1, g1=g1, du0=du0, g0=g0, y_m=y_m, y_fly=y_received)
     store.update(of=of, o_s=o_s, o0=o0, x2=x2, h2_other=h2_other, ca_other=ca_other)
 
@@ -1319,7 +1320,7 @@
     step(["up0"], lambda: up_grad(h3, *get("h3_other", "du0"), ROUND), "du0")
     order(up.fly, "down1", "dself_other")
     down.over_y("down1")
-    up.first("up0")
+    store["up_total"] = lax.psum(plus(*get("up0", up.fly)), "wide")
     step(
         ["dof", "dos", "do0"],
         lambda: pull(place, *get("dself", "dself_other"), (out_first, out_second, w_out)),
@@ -1338,7 +1339,16 @@
         lambda: self_back(limit, qf, kf, vf, store["of"], store["dof"], lse_f),
         "dof",
     )
-    order("dcross_other", "dcq_other", "pair_fly", "pair_kept")
+    def query(g):
+        return query_grad(place, g, h2, *get("h2_other", "dcq", "dcq_other"), ROUND)
+
+    def outof(g, *o):
+        return outputs_grad(
+            place, g, get(*o), *get("dself", "dself_other"), ca,
+            *get("ca_other", "dcross", "dcross_other"), ROUND,
+        )
+
+    step(["query1"], lambda: query(1), "dcq_other", "h2_other", "pair_fly", "pair_kept")
     pair_sum = lower(store["pair_kept"] + store["pair_fly"])
     store["pair"] = pair_sum[0]
     store["pair_other"] = cross_order(pair_sum[1])
@@ -1347,48 +1357,23 @@
         lambda: self_back(limit, qs, ks, vs, store["o_s"], store["dos"], lse_s),
         "dos",
     )
-    up.second()
     step(["down0"], lambda: down_grad(store["g0"], dout, dout_other, ROUND), "g0")
     yp = ("dqf", "dkf", "dvf", "dqs", "dks", "dvs")
     step(["qkv1"], lambda: qkv_grad(place, h1, get(*yp), ROUND), "dqs")
-    order(down.fly, "qkv1")
+    order(down.fly, "qkv1", "query1", "pair_other")
+    store["query_fly"] = over_y(store["query1"])
+    store["pair_y"] = over_y(store["pair_other"])
     qkv.over_y("qkv1")
     down.first("down0")
-    up.far()
-
-    def query(g):
-        return query_grad(place, g, h2, *get("h2_other", "dcq", "dcq_other"), ROUND)
-
-    def outof(g, *o):
-        return outputs_grad(
-            place, g, get(*o), *get("dself", "dself_other"), ca,
-            *get("ca_other", "dcross", "dcross_other"), ROUND,
-        )
-
-    step(["query1"], lambda: query(1), "dcq_other", "h2_other")
-    step(["outs1"], lambda: outof(1, "of", "o_s"), "dcross_other", "ca_other")
     step(
         ["dq0", "dk0", "dv0"],
         lambda: self_back(limit, q0, k0, v0, store["o0"], store["do0"], lse0),
         "do0",
     )
-    order(qkv.fly, "outs1", "query1")
+    down.second()
+    step(["outs1"], lambda: outof(1, "of", "o_s"), "dcross_other", "ca_other")
     outs.over_y("outs1")
-    store["query_fly"] = over_y(store["query1"])
-    store["pair_y"] = over_y(store["pair_other"])
-    up.back()
-    down.second()
-    nine = ("dq0", "dk0", "dv0", *yp)
-    weights = (w_qkv, qkv_first, qkv_second)
-    step(["yo"], lambda: first_back(away, get(*nine), weights, ROUND), "dq0")
-    store["yo_fly"] = over_core(store["yo"])
-    step(["qkv0"], lambda: qkv_grad(place, h1, get("dq0", "dk0", "dv0"), ROUND), "dq0")
-    qkv.first("qkv0")
-    up.along()
     step(["query0"], lambda: query(0), "dcq")
-    down.far()
-    step(["outs0"], lambda: outof(0, "o0"), "dcross")
-    outs.first("outs0")
     order("query0", "query_fly", "pair", "pair_y")
     other_text = lax.dynamic_index_in_dim(text_states, 1 - side, keepdims=False)
     texts = jnp.concatenate([text, other_text], axis=0)
@@ -1402,8 +1387,19 @@
         axis=0,
     )
     cross_in.first_alone("into0")
+    nine = ("dq0", "dk0", "dv0", *yp)
+    weights = (w_qkv, qkv_first, qkv_second)
+    step(["yo"], lambda: first_back(away, get(*nine), weights, ROUND), "dq0")
+    store["yo_fly"] = over_core(store["yo"])
+    step(["qkv0"], lambda: qkv_grad(place, h1, get("dq0", "dk0", "dv0"), ROUND), "dq0")
+    qkv.first("qkv0")
+    down.far()
+    cross_in.second()
+    step(["outs0"], lambda: outof(0, "o0"), "dcross")
+    outs.first("outs0")
     qkv.second()
     step(["ym"], lambda: first_back(place, get(*nine), weights, FULL), "dq0")
+    cross_in.far()
     step(
         ["grad_frames", "first_sums"],
         lambda: frames_back(place, *get("ym", "yo_fly", "dx1"), frames, norm_gain),
@@ -1413,40 +1409,39 @@
     norms = Row("norms", store["sums"] + store["first_sums"], over_core)
     down.back()
     outs.second()
-    up.end("grad_up")
     qkv.far()
-    cross_in.second()
     norms.then(over_y)
+    cross_in.back()
     down.along()
+    norms.then(over_x)
     outs.far()
-    norms.then(over_x)
-    qkv.back()
-    cross_in.far()
     text_part = 0.0
     for c in range(2):
         text_part = text_part + nt(pairs[c], w_cross_kv[c])
     text_mine, text_theirs = text_part[:64], text_part[64:]
     text_rows = Row("texts", text_mine, lambda v: over_y(text_theirs))
-    qkv.along()
+    store["out_fly"] = over_core(out_o)
+    qkv.back()
+    norms.then(over_z)
+    cross_in.along()
+    text_rows.then(over_core)
     outs.back()
-    norms.then(over_z)
-    store["out_fly"] = over_core(out_o)
-    text_rows.then(over_core)
-    cross_in.back()
-    outs.along()
     norms.then(lambda v: along_wide(v, Z_FAR))
     down.end("grad_down")
-    order("texts_fly", "texts_kept")
+    order("up_total")
+    store["grad_up"] = store["up_total"].astype(FULL)
+    last[:] = ["grad_up"]
+    order("texts_fly", "texts_kept", "out_fly", "x2")
     text_grad = lower(text_rows.total())
     text_away = over_y(text_grad)
-    cross_in.along()
-    order("out_fly", "x2")
+    qkv.along()
+    outs.along()
     out_rows = lower(store["x2"] + out_m + store["out_fly"].astype(FULL))
-    qkv.end("grad_qkv")
-    outs.end("grad_outs")
     grad_text = ordered(text_grad[None], text_away[None], side)
     sums = norms.total()
     cross_in.end("grad_in")
+    qkv.end("grad_qkv")
+    outs.end("grad_outs")
     grad_in, grad_outs = get("grad_in", "grad_outs")
     return (
         out_rows,

time: 581 us -> 574 us (0.988)
  between operations: 2.94 us -> 15.9 us
  waiting for transfers between devices: 141 us -> 131 us
  other arithmetic: 58.2 us -> 50.2 us
    ppermute x34 -> x29, waiting for transfers between devices: 118 us -> 105 us  [along_wide(): return lax.ppermute(v, 'wide', pairs)]
    pallas_call x1, Pallas kernels: 29.2 us -> 20.7 us  [middle_forward(): pl.pallas_call(middle_forward_kernel, grid_spec=pltpu.PrefetchScalarGridS...]
    ppermute x34 -> x29, starting transfers between devices: 34.2 us -> 29.2 us  [along_wide(): return lax.ppermute(v, 'wide', pairs)]
    convert_element_type x5 -> x4, other arithmetic: 14.5 us -> 10.7 us  [end(): ordered(*get(self.kept, self.fly), self.axes[0][0]).astype(FULL)]
    unnamed x271 -> x241, local copies, waits for them, and re-layouts: 23.8 us -> 27.4 us
    convert_element_type x17 -> x15, other arithmetic: 19.3 us -> 16.1 us  [lower(): return values_in.astype(jnp.bfloat16)]
  transfers between devices with their start and end apart: 77 -> 73, of which waited for: 23 -> 17; matrix products, arithmetic and copies ran while one was open for 13% -> 12% of each run, Pallas kernels for 44% -> 44%
where the time goes in v10:
time: 574 us; the launch traced here: 564 us
  Pallas kernels  260 us (45%)
  waiting for transfers between devices  131 us (23%)
  starting transfers between devices  54.2 us (9%)
  other arithmetic  50.2 us (9%)
  local copies, waits for them, and re-layouts  49.7 us (9%)
  between operations  15.9 us (3%)
    ppermute x29, waiting for transfers between devices, along_wide(): return lax.ppermute(v, 'wide', pairs)  105 us
    pallas_call x4, Pallas kernels, feed(): pl.pallas_call(functools.partial(feed_kernel, parts=parts, carried=len(be...  51.7 us
    pallas_call x3, Pallas kernels, self_back(): pl.pallas_call(functools.partial(self_back_kernel, span=span, floor=floor...  39.5 us
    pallas_call x3, Pallas kernels, self_forward(): pl.pallas_call(functools.partial(self_forward_kernel, span=span, floor=fl...  30.8 us
    ppermute x29, starting transfers between devices, along_wide(): return lax.ppermute(v, 'wide', pairs)  29.2 us
    unnamed x241, local copies, waits for them, and re-layouts  27.4 us
    ppermute x16, waiting for transfers between devices, over_y(): return lax.ppermute(v, 'narrow', Y_PAIRS)  26.1 us
    pallas_call x1, Pallas kernels, middle_back(): pl.pallas_call(middle_back_kernel, grid_spec=pltpu.PrefetchScalarGridSpec...  23.1 us
  transfers between devices with their start and end apart: 73, of which 17 were waited for; matrix products, arithmetic and copies ran while one was open for 12% of the time, Pallas kernels for 44%

profile of v10, /device:TPU:0, one launch (start us, length us, event | category | flops | bytes accessed | tf_op | source)
XLA Modules:
  0.0 563.7 jit_solution(1247457434982693129)
XLA Ops:
  7.7 2.1 constant_dynamic-slice_fusion.14
  9.8 2.6 collective-permute-start.1
  21.4 4.5 first_project.1
  28.7 2.2 collective-permute-done.1.weight_ref.refs_10_
  37.1 4.0 collective-permute-done.2.refs_7_.refs_0_
  41.1 1.8 collective-permute-start.4
  42.8 3.8 collective-permute-done.3.refs_13_.refs_1_
  46.7 1.8 collective-permute-start.8
  48.5 14.1 %self_forward.3 = (bf16[1664,256]{1,0:T(8,128)(2,1)}, f32[2,8,1664]{2,1,0:T(8,128)}) custom-call(s32[1]{0:T(128)} %dynamic_slice.111.limit_ref, bf16[1664,256]{1,0:T(8,128)(2,1)} %copy-done.72, bf16[1664,256]{1,0:T(8,128)(2,1)} %copy-done.74, bf16[1664,256]{1,0:T(8,128)(2,1)} %copy-done.76), custom_call_target="tpu_custom_call" | custom-call | flops 4701199872 | bytes 1000 | tf_op jit(solution)/shard_map/self_forward/pallas_call | solution.py:525
  62.6 4.3 project.2
  70.6 8.3 %self_forward.4 = (bf16[1664,128]{1,0:T(8,128)(2,1)}, f32[1,8,1664]{2,1,0:T(8,128)}) custom-call(s32[1]{0:T(128)} %dynamic_slice.111.limit_ref, bf16[1664,128]{1,0:T(8,128)(2,1)} %copy-done.60, bf16[1664,128]{1,0:T(8,128)(2,1)} %copy-done.62, bf16[1664,128]{1,0:T(8,128)(2,1)} %copy-done.64), custom_call_target="tpu_custom_call" | custom-call | flops 2350599936 | bytes 1000 | tf_op jit(solution)/shard_map/self_forward/pallas_call | solution.py:525
  79.0 1.8 collective-permute-start.12
  82.1 2.7 project.3
  88.4 8.4 %self_forward.5 = (bf16[1664,128]{1,0:T(8,128)(2,1)}, f32[1,8,1664]{2,1,0:T(8,128)}) custom-call(s32[1]{0:T(128)} %dynamic_slice.111.limit_ref, bf16[1664,128]{1,0:T(8,128)(2,1)} %copy-done.66, bf16[1664,128]{1,0:T(8,128)(2,1)} %copy-done.68, bf16[1664,128]{1,0:T(8,128)(2,1)} %copy-done.70), custom_call_target="tpu_custom_call" | custom-call | flops 2350599936 | bytes 1000 | tf_op jit(solution)/shard_map/self_forward/pallas_call | solution.py:525
  99.0 1.8 collective-permute-start.24
  105.7 20.7 %middle_forward.1 = (f32[832,1024]{1,0:T(8,128)}, f32[832,1024]{1,0:T(8,128)}, bf16[832,1024]{1,0:T(8,128)(2,1)}, bf16[832,1024]{1,0:T(8,128)(2,1)}, bf16[832,10...) custom-call(s32[3]{0:T(128)} %copy-done.52, bf16[832,1024]{1,0:T(8,128)(2,1)} %frame_ref.3, ...), custom_call_target="tpu_custom_call" | custom-call | flops 7084000256 | bytes 1000 | tf_op jit(solution)/shard_map/middle_forward/pallas_call | solution.py:677
  128.4 12.2 %feed.4 = (bf16[1664,1024]{1,0:T(8,128)(2,1)}, bf16[1664,1024]{1,0:T(8,128)(2,1)}, f32[832,1024]{1,0:T(8,128)}, f32[832,1024]{1,0:T(8,128)}) custom-call(s32[3]{0:T(128)} %copy-done.52, bf16[832,1024]{1,0:T(8,128)(2,1)} %get-tuple-element.295.h_ref.mine_ref, bf16[832,1024]{1,0:T(8,128)(2,1)} %copy-done, bf16[1024,1024]{1,0:T(8,128)(2,1)} %refs_0_.1, ...), custom_call_target="tpu_custom_call" | custom-call | flops 4185999872 | bytes 1000 | tf_op jit(solution)/shard_map/feed/pallas_call | solution.py:756
  142.4 12.2 %feed.5 = (bf16[1664,1024]{1,0:T(8,128)(2,1)}, bf16[1664,1024]{1,0:T(8,128)(2,1)}, f32[832,1024]{1,0:T(8,128)}, f32[832,1024]{1,0:T(8,128)}) custom-call(s32[3]{0:T(128)} %copy-done.52, bf16[832,1024]{1,0:T(8,128)(2,1)} %copy-done.13, bf16[832,1024]{1,0:T(8,128)(2,1)} %copy-done.10, ...), custom_call_target="tpu_custom_call", output_to_operand_aliasing={{0}: (5, {}), {1}: (6, {})} | custom-call | flops 4185999872 | bytes 1000 | tf_op jit(solution)/shard_map/feed/pallas_call | solution.py:756
  154.5 13.6 %feed.6 = (bf16[1664,1024]{1,0:T(8,128)(2,1)}, bf16[1664,1024]{1,0:T(8,128)(2,1)}, bf16[832,1024]{1,0:T(8,128)(2,1)}, bf16[832,1024]{1,0:T(8,128)(2,1)}) custom-call(s32[3]{0:T(128)} %copy-done.52, bf16[832,1024]{1,0:T(8,128)(2,1)} %copy-done.13, bf16[832,1024]{1,0:T(8,128)(2,1)} %copy-done.10, bf16[1024,512]{1,0:T(8,128)(2,1)} %collective-permute-done.14.refs_0_, ...), custom_call_target="tpu_custom_call" | custom-call | flops 4185999872 | bytes 1000 | tf_op jit(solution)/shard_map/feed/pallas_call | solution.py:756
  168.2 13.8 %feed.7 = (bf16[1664,1024]{1,0:T(8,128)(2,1)}, bf16[1664,1024]{1,0:T(8,128)(2,1)}, f32[832,1024]{1,0:T(8,128)}, f32[832,1024]{1,0:T(8,128)}) custom-call(s32[3]{0:T(128)} %copy-done.52, bf16[832,1024]{1,0:T(8,128)(2,1)} %get-tuple-element.295.h_ref.mine_ref, bf16[832,1024]{1,0:T(8,128)(2,1)} %copy-done, ...), custom_call_target="tpu_custom_call", output_to_operand_aliasing={{0}: (9, {}), {1}: (10, {})} | custom-call | flops 4185999872 | bytes 1000 | tf_op jit(solution)/shard_map/feed/pallas_call | solution.py:756
  181.9 7.3 %up_grad.2 = bf16[1024,1024]{1,0:T(8,128)(2,1)} custom-call(bf16[832,1024]{1,0:T(8,128)(2,1)S(1)} %copy-done.3, bf16[832,1024]{1,0:T(8,128)(2,1)S(1)} %copy-done.14, bf16[1664,1024]{1,0:T(8,128)(2,1)} %get-tuple-element.319.du_ref), custom_call_target="tpu_custom_call" | custom-call | flops 1610000000 | bytes 1000 | tf_op jit(solution)/shard_map/up_grad/pallas_call | solution.py:786
  190.3 7.2 %down_grad.2 = bf16[1024,1024]{1,0:T(8,128)(2,1)} custom-call(bf16[1664,1024]{1,0:T(8,128)(2,1)} %get-tuple-element.320.g_ref, bf16[832,1024]{1,0:T(8,128)(2,1)S(1)} %copy-done.1, bf16[832,1024]{1,0:T(8,128)(2,1)S(1)} %copy-done.11), custom_call_target="tpu_custom_call" | custom-call | flops 1610000000 | bytes 1000 | tf_op jit(solution)/shard_map/down_grad/pallas_call | solution.py:809
  198.8 23.1 %middle_back.1 = (f32[832,1024]{1,0:T(8,128)}, bf16[832,1024]{1,0:T(8,128)(2,1)}, bf16[832,1024]{1,0:T(8,128)(2,1)}, bf16[832,1024]{1,0:T(8,128)(2,1)}, f32[4,64...) custom-call(s32[3]{0:T(128)} %copy-done.52, f32[832,1024]{1,0:T(8,128)} %get-tuple-element.321.ym_ref, ...), custom_call_target="tpu_custom_call" | custom-call | flops 7728000000 | bytes 1000 | tf_op jit(solution)/shard_map/middle_back/pallas_call | solution.py:992
  222.5 6.3 %up_grad.3 = bf16[1024,1024]{1,0:T(8,128)(2,1)S(1)} custom-call(bf16[832,1024]{1,0:T(8,128)(2,1)S(1)} %copy-done.3, bf16[832,1024]{1,0:T(8,128)(2,1)S(1)} %copy-done.15, bf16[1664,1024]{1,0:T(8,128)(2,1)} %get-tuple-element.329.du_ref), custom_call_target="tpu_custom_call" | custom-call | flops 1610000000 | bytes 1000 | tf_op jit(solution)/shard_map/up_grad/pallas_call | solution.py:786
  230.2 7.5 %collective-permute-done.30 = bf16[1024,1024]{1,0:T(8,128)(2,1)} collective-permute-done((bf16[1024,1024]{1,0:T(8,128)(2,1)}, bf16[1024,1024]{1,0:T(8,128)(2,1)}, u32[]{:S(2)}, u32[]{:S(2)}) %collective-permute-start.30) | collective-permute-done | bytes 2097184 | tf_op jit(solution)/shard_map/ppermute | solution.py:1096
  243.1 4.9 pull.1
  249.2 9.3 %self_back.3 = (bf16[1664,128]{1,0:T(8,128)(2,1)S(1)}, bf16[1664,128]{1,0:T(8,128)(2,1)S(1)}, bf16[1664,128]{1,0:T(8,128)(2,1)S(1)}) custom-call(s32[1]{0:T(128)} %dynamic_slice.111.limit_ref, bf16[1664,128]{1,0:T(8,128)(2,1)S(1)} %copy-done.61, bf16[1664,128]{1,0:T(8,128)(2,1)S(1)} %copy-done.63, bf16[1664,128]{1,0:T(8,128)(2,1)S(1)} %copy-done.65, ...), custom_call_target="tpu_custom_call" | custom-call | flops 2254000128 | bytes 1000 | tf_op jit(solution)/shard_map/self_back/pallas_call | solution.py:606
  258.7 4.4 query_grad.2
  263.9 9.7 %self_back.4 = (bf16[1664,128]{1,0:T(8,128)(2,1)S(1)}, bf16[1664,128]{1,0:T(8,128)(2,1)S(1)}, bf16[1664,128]{1,0:T(8,128)(2,1)S(1)}) custom-call(s32[1]{0:T(128)} %dynamic_slice.111.limit_ref, bf16[1664,128]{1,0:T(8,128)(2,1)S(1)} %copy-done.67, bf16[1664,128]{1,0:T(8,128)(2,1)S(1)} %copy-done.69, bf16[1664,128]{1,0:T(8,128)(2,1)S(1)} %copy-done.71, ...), custom_call_target="tpu_custom_call" | custom-call | flops 2254000128 | bytes 1000 | tf_op jit(solution)/shard_map/self_back/pallas_call | solution.py:606
  273.7 6.6 %down_grad.3 = bf16[1024,1024]{1,0:T(8,128)(2,1)S(1)} custom-call(bf16[1664,1024]{1,0:T(8,128)(2,1)} %get-tuple-element.358.g_ref, bf16[832,1024]{1,0:T(8,128)(2,1)S(1)} %copy-done.2, bf16[832,1024]{1,0:T(8,128)(2,1)S(1)} %copy-done.12), custom_call_target="tpu_custom_call" | custom-call | flops 1610000000 | bytes 1000 | tf_op jit(solution)/shard_map/down_grad/pallas_call | solution.py:809
  280.4 6.1 %qkv_grad.2 = bf16[3072,256]{1,0:T(8,128)(2,1)S(1)} custom-call(s32[3]{0:T(128)S(1)} %copy-done.53, bf16[1664,1024]{1,0:T(8,128)(2,1)} %copy-done.5, bf16[1664,128]{1,0:T(8,128)(2,1)S(1)} %get-tuple-element.348.refs_0_.refs_3_, bf16[1664,128]{1,0:T(8,128)(2,1)S(1)} %get-tuple-element.349.refs_1_.refs_4_, ...), custom_call_target="tpu_custom_call" | custom-call | flops 1610000000 | bytes 1000 | tf_op jit(solution)/shard_map/qkv_grad/pallas_call | solution.py:846
  287.9 4.1 convert_add_fusion.1
  293.5 1.8 dynamic-slice_bitcast_fusion.1
  295.3 2.1 slice.81
  298.0 3.9 add_convert_fusion
  307.8 20.5 %self_back.5 = (bf16[1664,256]{1,0:T(8,128)(2,1)S(1)}, bf16[1664,256]{1,0:T(8,128)(2,1)S(1)}, bf16[1664,256]{1,0:T(8,128)(2,1)S(1)}) custom-call(s32[1]{0:T(128)} %dynamic_slice.111.limit_ref, bf16[1664,256]{1,0:T(8,128)(2,1)S(1)} %copy-done.73, bf16[1664,256]{1,0:T(8,128)(2,1)S(1)} %copy-done.75, bf16[1664,256]{1,0:T(8,128)(2,1)S(1)} %copy-done.77, ...), custom_call_target="tpu_custom_call" | custom-call | flops 4508000256 | bytes 1000 | tf_op jit(solution)/shard_map/self_back/pallas_call | solution.py:606
  333.2 5.2 outputs_grad.2
  338.4 4.0 query_grad.3
  342.4 8.6 %collective-permute-done.40 = bf16[2,64,256]{2,1,0:T(8,128)(2,1)S(1)} collective-permute-done((bf16[2,64,256]{2,1,0:T(8,128)(2,1)S(1)}, bf16[2,64,256]{2,1,0:T(8,128)(2,1)S(1)}, u32[]{:S(2)}, u32[]{:S(2)}) %collective-permute-start.40) | collective-permute-done | bytes 65568 | tf_op jit(solution)/shard_map/ppermute | solution.py:1096
  359.2 7.1 %first_back.2 = bf16[832,1024]{1,0:T(8,128)(2,1)} custom-call(s32[3]{0:T(128)S(1)} %add_add_fusion.1.place_ref, bf16[1664,256]{1,0:T(8,128)(2,1)S(1)} %get-tuple-element.406.refs_0_, bf16[1664,256]{1,0:T(8,128)(2,1)S(1)} %get-tuple-element.390.refs_1_, bf16[1664,256]{1,0:T(8,128)(2,1)S(1)} %get-tuple-element.391.refs_2_, bf16[1664,128]{1,0:T(8,128)(2,1)S(1)} %copy-done.17, ...), custom_call_target="tpu_custom_call" | custom-call | flops 1149539968 | bytes 1000 | tf_op jit(solution)/shard_map/first_back/pallas_call | solution.py:1026
  366.3 6.0 %qkv_grad.3 = bf16[3072,256]{1,0:T(8,128)(2,1)S(1)} custom-call(s32[3]{0:T(128)S(1)} %copy-done.53, bf16[1664,1024]{1,0:T(8,128)(2,1)} %copy-done.5, bf16[1664,256]{1,0:T(8,128)(2,1)S(1)} %get-tuple-element.406.refs_0_, bf16[1664,256]{1,0:T(8,128)(2,1)S(1)} %get-tuple-element.390.refs_1_, bf16[1664,256]{1,0:T(8,128)(2,1)S(1)} %get-tuple-element.391.refs_2_), custom_call_target="tpu_custom_call" | custom-call | flops 1610000000 | bytes 1000 | tf_op jit(solution)/shard_map/qkv_grad/pallas_call | solution.py:846
  372.4 2.7 add_convert_fusion.3
  375.5 2.0 add_convert_fusion.6
  377.5 1.8 collective-permute-done.42
  379.3 2.6 collective-permute-start.53
  384.7 5.4 outputs_grad.3
  392.3 37.1 %collective-permute-done.46 = bf16[1536,256]{1,0:T(8,128)(2,1)} collective-permute-done((bf16[1536,256]{1,0:T(8,128)(2,1)}, bf16[1536,256]{1,0:T(8,128)(2,1)}, u32[]{:S(2)}, u32[]{:S(2)}) %collective-permute-start.46) | collective-permute-done | bytes 786464 | tf_op jit(solution)/shard_map/ppermute | solution.py:1099
  432.4 6.3 %first_back.3.ym_ref = f32[832,1024]{1,0:T(8,128)S(1)} custom-call(s32[3]{0:T(128)S(1)} %copy-done.53, bf16[1664,256]{1,0:T(8,128)(2,1)S(1)} %get-tuple-element.406.refs_0_, bf16[1664,256]{1,0:T(8,128)(2,1)S(1)} %get-tuple-element.390.refs_1_, bf16[1664,256]{1,0:T(8,128)(2,1)S(1)} %get-tuple-element.391.refs_2_, bf16[1664,128]{1,0:T(8,128)(2,1)S(1)} %copy-done.17, ...), custom_call_target="tpu_custom_call" | custom-call | flops 1149539968 | bytes 1000 | tf_op jit(solution)/shard_map/first_back/pallas_call | solution.py:1026
  439.5 2.2 collective-permute-start.48
  441.7 5.9 %frames_back.1 = (bf16[832,1024]{1,0:T(8,128)(2,1)}, f32[8,1024]{1,0:T(8,128)S(1)}) custom-call(s32[3]{0:T(128)S(1)} %copy-done.53, f32[832,1024]{1,0:T(8,128)S(1)} %first_back.3.ym_ref, bf16[832,1024]{1,0:T(8,128)(2,1)} %collective-permute-done.49.yr_ref, f32[832,1024]{1,0:T(8,128)S(1)} %copy-done.29, bf16[832,1024]{1,0:T(8,128)(2,1)S(1)} %copy-done.37, ...), custom_call_target="tpu_custom_call" | custom-call | flops 1381379968 | bytes 1000 | tf_op jit(solution)/shard_map/frames_back/pallas_call | solution.py:1061
  451.6 2.4 collective-permute-start.59
  454.0 4.9 collective-permute-done.48
  460.0 18.4 %collective-permute-done.55 = bf16[256,1024]{1,0:T(8,128)(2,1)S(1)} collective-permute-done((bf16[256,1024]{1,0:T(8,128)(2,1)S(1)}, bf16[256,1024]{1,0:T(8,128)(2,1)S(1)}, u32[]{:S(2)}, u32[]{:S(2)}) %collective-permute-start.55) | collective-permute-done | bytes 524320 | tf_op jit(solution)/shard_map/ppermute | solution.py:1099
  480.4 3.7 collective-permute-done.58
  486.4 18.3 %collective-permute-done.57 = f32[8,1024]{1,0:T(8,128)S(1)} collective-permute-done((f32[8,1024]{1,0:T(8,128)S(1)}, f32[8,1024]{1,0:T(8,128)S(1)}, u32[]{:S(2)}, u32[]{:S(2)}) %collective-permute-start.57) | collective-permute-done | bytes 32800 | tf_op jit(solution)/shard_map/ppermute | solution.py:1099
  506.0 11.5 %collective-permute-done.61 = bf16[128,1024]{1,0:T(8,128)(2,1)S(1)} collective-permute-done((bf16[128,1024]{1,0:T(8,128)(2,1)S(1)}, bf16[128,1024]{1,0:T(8,128)(2,1)S(1)}, u32[]{:S(2)}, u32[]{:S(2)}) %collective-permute-start.61) | collective-permute-done | bytes 262176 | tf_op jit(solution)/shard_map/ppermute | solution.py:1099
  517.7 2.9 fusion
  520.6 4.2 convert_element_type.237
  529.0 2.0 collective-permute-start.69
  531.0 6.9 %collective-permute-done.70 = bf16[1536,256]{1,0:T(8,128)(2,1)S(1)} collective-permute-done((bf16[1536,256]{1,0:T(8,128)(2,1)S(1)}, bf16[1536,256]{1,0:T(8,128)(2,1)S(1)}, u32[]{:S(2)}, u32[]{:S(2)}) %collective-permute-start.70) | collective-permute-done | bytes 786464 | tf_op jit(solution)/shard_map/ppermute | solution.py:1099
  539.0 3.8 add_convert_fusion.1
  542.8 2.0 fusion.1
  549.3 3.9 fusion.2
  553.2 1.9 fusion.3
  (442 shorter events, 102.8 us)
Async XLA Ops:
  7.2 513.4 %all-reduce.2.cloned.1.call-start = ((), (), s32[]{:S(2)}) async-start(), calls=%async_computation | async-start | bytes 4194304 | tf_op jit(solution)/shard_map/psum | solution.py:1323
  9.8 21.0 %collective-permute-start.1 = (bf16[3,1024,128]{2,1,0:T(8,128)(2,1)}, bf16[3,1024,128]{2,1,0:T(8,128)(2,1)}, u32[]{:S(2)}, u32[]{:S(2)}) collective-permute-start(bf16[3,1024,128]{2,1,0:T(8,128)(2,1)} %constant_dynamic-slice_fusion.14), channel_id=1, source_target_pairs={{0,2},{2,0},{1,3},{3,1},{4,6},{6,4},{5,7},{7,5},{8,10},{10,8},{9,1... | collective-permute-start | bytes 2359304 | tf_op jit(solution)/shard_map/ppermute | solution.py:1096
  31.6 9.5 %collective-permute-start.2 = (bf16[128,1024]{1,0:T(8,128)(2,1)}, bf16[128,1024]{1,0:T(8,128)(2,1)}, u32[]{:S(2)}, u32[]{:S(2)}) collective-permute-start(bf16[128,1024]{1,0:T(8,128)(2,1)} %constant_dynamic-slice_fusion.13), channel_id=1, source_target_pairs={{0,2},{2,0},{1,3},{3,1},{4,6},{6,4},{5,7},{7,5},{8,10},{10,8},{9,1... | collective-permute-start | bytes 786440 | tf_op jit(solution)/shard_map/ppermute | solution.py:1096
  34.0 12.7 %collective-permute-start.3 = (bf16[1024,128]{1,0:T(8,128)(2,1)}, bf16[1024,128]{1,0:T(8,128)(2,1)}, u32[]{:S(2)}, u32[]{:S(2)}) collective-permute-start(bf16[1024,128]{1,0:T(8,128)(2,1)} %constant_dynamic-slice_fusion.12), channel_id=1, source_target_pairs={{0,2},{2,0},{1,3},{3,1},{4,6},{6,4},{5,7},{7,5},{8,10},{10,8},{9,1... | collective-permute-start | bytes 786440 | tf_op jit(solution)/shard_map/ppermute | solution.py:1096
  35.5 33.0 %collective-permute-start.5 = (bf16[256,1024]{1,0:T(8,128)(2,1)}, bf16[256,1024]{1,0:T(8,128)(2,1)}, u32[]{:S(2)}, u32[]{:S(2)}) collective-permute-start(bf16[256,1024]{1,0:T(8,128)(2,1)} %refs_2_), channel_id=1, source_target_pairs={{0,1},{1,0},{2,3},{3,2},{4,5},{5,4},{6,7},{7,6},{8,9},{9,8},{10,11... | collective-permute-start | bytes 1572872 | tf_op jit(solution)/shard_map/ppermute | solution.py:1093
  35.6 33.0 %collective-permute-start.6 = (bf16[1024,256]{1,0:T(8,128)(2,1)}, bf16[1024,256]{1,0:T(8,128)(2,1)S(1)}, u32[]{:S(2)}, u32[]{:S(2)}) collective-permute-start(bf16[1024,256]{1,0:T(8,128)(2,1)} %refs_0_.2), channel_id=1, source_target_pairs={{0,1},{1,0},{2,3},{3,2},{4,5},{5,4},{6,7},{7,6},{8,9},{9,8},{10,11... | collective-permute-start | bytes 1572872 | tf_op jit(solution)/shard_map/ppermute | solution.py:1093
  36.0 32.5 %collective-permute-start.7 = (bf16[256,1024]{1,0:T(8,128)(2,1)}, bf16[256,1024]{1,0:T(8,128)(2,1)}, u32[]{:S(2)}, u32[]{:S(2)}) collective-permute-start(bf16[256,1024]{1,0:T(8,128)(2,1)} %refs_6_.1), channel_id=1, source_target_pairs={{0,1},{1,0},{2,3},{3,2},{4,5},{5,4},{6,7},{7,6},{8,9},{9,8},{10,11... | collective-permute-start | bytes 1572872 | tf_op jit(solution)/shard_map/ppermute | solution.py:1093
  41.1 25.8 %collective-permute-start.4 = (bf16[128,1024]{1,0:T(8,128)(2,1)S(1)}, bf16[128,1024]{1,0:T(8,128)(2,1)}, u32[]{:S(2)}, u32[]{:S(2)}) collective-permute-start(bf16[128,1024]{1,0:T(8,128)(2,1)S(1)} %constant_dynamic-slice_fusion.11), channel_id=1, source_target_pairs={{0,2},{2,0},{1,3},{3,1},{4,6},{6,4},{5,7},{7,5},{8,10},{10,8},{9,1... | collective-permute-start | bytes 786440 | tf_op jit(solution)/shard_map/ppermute | solution.py:1096
  46.7 32.3 %collective-permute-start.8 = (bf16[3,1024,128]{2,1,0:T(8,128)(2,1)}, bf16[3,1024,128]{2,1,0:T(8,128)(2,1)S(1)}, u32[]{:S(2)}, u32[]{:S(2)}) collective-permute-start(bf16[3,1024,128]{2,1,0:T(8,128)(2,1)} %collective-permute-done.1.weight_ref.refs_10_), channel_id=1, source_target_pairs={{0,8},{4,12},{8,0},{12,4},{16,24},{20,28},{24,16},{28,20},{1,9},{5... | collective-permute-start | bytes 2359304 | tf_op jit(solution)/shard_map/ppermute | solution.py:1099
  66.9 12.0 %collective-permute-start.9 = (bf16[2,64,256]{2,1,0:T(8,128)(2,1)S(1)}, bf16[2,64,256]{2,1,0:T(8,128)(2,1)S(1)}, u32[]{:S(2)}, u32[]{:S(2)}) collective-permute-start(bf16[2,64,256]{2,1,0:T(8,128)(2,1)S(1)} %get-tuple-element.511), channel_id=1, source_target_pairs={{0,2},{2,0},{1,3},{3,1},{4,6},{6,4},{5,7},{7,5},{8,10},{10,8},{9,1... | collective-permute-start | bytes 196616 | tf_op jit(solution)/shard_map/ppermute | solution.py:1096
  68.6 12.2 %collective-permute-start.10 = (bf16[832,256]{1,0:T(8,128)(2,1)S(1)}, bf16[832,256]{1,0:T(8,128)(2,1)}, u32[]{:S(2)}, u32[]{:S(2)}) collective-permute-start(bf16[832,256]{1,0:T(8,128)(2,1)S(1)} %constant_dynamic-slice_fusion.10), channel_id=1, source_target_pairs={{0,1},{1,0},{2,3},{3,2},{4,5},{5,4},{6,7},{7,6},{8,9},{9,8},{10,11... | collective-permute-start | bytes 1277960 | tf_op jit(solution)/shard_map/ppermute | solution.py:1093
  68.8 28.7 %collective-permute-start.14 = (bf16[1024,512]{1,0:T(8,128)(2,1)S(1)}, bf16[1024,512]{1,0:T(8,128)(2,1)}, u32[]{:S(2)}, u32[]{:S(2)}) collective-permute-start(bf16[1024,512]{1,0:T(8,128)(2,1)S(1)} %constant_dynamic-slice_fusion.9), channel_id=1, source_target_pairs={{0,2},{2,0},{1,3},{3,1},{4,6},{6,4},{5,7},{7,5},{8,10},{10,8},{9,1... | collective-permute-start | bytes 3145736 | tf_op jit(solution)/shard_map/ppermute | solution.py:1096
  69.4 17.7 %collective-permute-start.11 = (bf16[128,1024]{1,0:T(8,128)(2,1)}, bf16[128,1024]{1,0:T(8,128)(2,1)S(1)}, u32[]{:S(2)}, u32[]{:S(2)}) collective-permute-start(bf16[128,1024]{1,0:T(8,128)(2,1)} %collective-permute-done.2.refs_7_.refs_0_), channel_id=1, source_target_pairs={{0,8},{4,12},{8,0},{12,4},{16,24},{20,28},{24,16},{28,20},{1,9},{5... | collective-permute-start | bytes 786440 | tf_op jit(solution)/shard_map/ppermute | solution.py:1099
  78.9 21.9 %collective-permute-start.18 = (bf16[128,1024]{1,0:T(8,128)(2,1)}, bf16[128,1024]{1,0:T(8,128)(2,1)}, u32[]{:S(2)}, u32[]{:S(2)}) collective-permute-start(bf16[128,1024]{1,0:T(8,128)(2,1)} %collective-permute-done.2.refs_7_.refs_0_), channel_id=1, source_target_pairs={{0,1},{1,0},{2,3},{3,2},{4,5},{5,4},{6,7},{7,6},{8,9},{9,8},{10,11... | collective-permute-start | bytes 786440 | tf_op jit(solution)/shard_map/ppermute | solution.py:1093
  79.0 9.4 %collective-permute-start.12 = (bf16[1024,128]{1,0:T(8,128)(2,1)}, bf16[1024,128]{1,0:T(8,128)(2,1)S(1)}, u32[]{:S(2)}, u32[]{:S(2)}) collective-permute-start(bf16[1024,128]{1,0:T(8,128)(2,1)} %collective-permute-done.3.refs_13_.refs_1_), channel_id=1, source_target_pairs={{0,4},{4,0},{8,12},{12,8},{16,20},{20,16},{24,28},{28,24},{1,5},{5... | collective-permute-start | bytes 786440 | tf_op jit(solution)/shard_map/ppermute | solution.py:1099
  80.8 16.0 %collective-permute-start.13 = (bf16[128,1024]{1,0:T(8,128)(2,1)}, bf16[128,1024]{1,0:T(8,128)(2,1)S(1)}, u32[]{:S(2)}, u32[]{:S(2)}) collective-permute-start(bf16[128,1024]{1,0:T(8,128)(2,1)} %collective-permute-done.4.refs_19_.refs_7_), channel_id=1, source_target_pairs={{0,4},{4,0},{8,12},{12,8},{16,20},{20,16},{24,28},{28,24},{1,5},{5... | collective-permute-start | bytes 786440 | tf_op jit(solution)/shard_map/ppermute | solution.py:1099
  87.1 10.3 %collective-permute-start.15 = (bf16[2,2,64,256]{3,2,1,0:T(8,128)(2,1)S(1)}, bf16[2,2,64,256]{3,2,1,0:T(8,128)(2,1)S(1)}, u32[]{:S(2)}, u32[]{:S(2)}) collective-permute-start(bf16[2,2,64,256]{3,2,1,0:T(8,128)(2,1)S(1)} %pad_maximum_fusion.6), channel_id=1, source_target_pairs={{0,1},{1,0},{2,3},{3,2},{4,5},{5,4},{6,7},{7,6},{8,9},{9,8},{10,11... | collective-permute-start | bytes 393224 | tf_op jit(solution)/shard_map/ppermute | solution.py:1093
  88.4 9.1 %collective-permute-start.16 = (bf16[832,128]{1,0:T(8,128)(2,1)S(1)}, bf16[832,128]{1,0:T(8,128)(2,1)S(1)}, u32[]{:S(2)}, u32[]{:S(2)}) collective-permute-start(bf16[832,128]{1,0:T(8,128)(2,1)S(1)} %constant_dynamic-slice_fusion.6), channel_id=1, source_target_pairs={{0,1},{1,0},{2,3},{3,2},{4,5},{5,4},{6,7},{7,6},{8,9},{9,8},{10,11... | collective-permute-start | bytes 638984 | tf_op jit(solution)/shard_map/ppermute | solution.py:1093
  99.0 27.3 %collective-permute-start.24 = (bf16[1024,512]{1,0:T(8,128)(2,1)}, bf16[1024,512]{1,0:T(8,128)(2,1)S(1)}, u32[]{:S(2)}, u32[]{:S(2)}) collective-permute-start(bf16[1024,512]{1,0:T(8,128)(2,1)} %collective-permute-done.14.refs_0_), channel_id=1, source_target_pairs={{0,4},{4,0},{8,12},{12,8},{16,20},{20,16},{24,28},{28,24},{1,5},{5... | collective-permute-start | bytes 3145736 | tf_op jit(solution)/shard_map/ppermute | solution.py:1099
  100.8 25.6 %collective-permute-start.25 = (bf16[512,1024]{1,0:T(8,128)(2,1)}, bf16[512,1024]{1,0:T(8,128)(2,1)S(1)}, u32[]{:S(2)}, u32[]{:S(2)}) collective-permute-start(bf16[512,1024]{1,0:T(8,128)(2,1)} %constant_dynamic-slice_fusion.8), channel_id=1, source_target_pairs={{0,2},{2,0},{1,3},{3,1},{4,6},{6,4},{5,7},{7,5},{8,10},{10,8},{9,1... | collective-permute-start | bytes 3145736 | tf_op jit(solution)/shard_map/ppermute | solution.py:1096
  127.4 13.2 %collective-permute-start.26 = (bf16[832,1024]{1,0:T(8,128)(2,1)}, bf16[832,1024]{1,0:T(8,128)(2,1)S(1)}, u32[]{:S(2)}, u32[]{:S(2)}) collective-permute-start(bf16[832,1024]{1,0:T(8,128)(2,1)} %get-tuple-element.295.h_ref.mine_ref), channel_id=1, source_target_pairs={{0,1},{1,0},{2,3},{3,2},{4,5},{5,4},{6,7},{7,6},{8,9},{9,8},{10,11... | collective-permute-start | bytes 5111816 | tf_op jit(solution)/shard_map/ppermute | solution.py:1093
  127.6 13.0 %collective-permute-start.27 = (bf16[832,1024]{1,0:T(8,128)(2,1)S(1)}, bf16[832,1024]{1,0:T(8,128)(2,1)S(1)}, u32[]{:S(2)}, u32[]{:S(2)}) collective-permute-start(bf16[832,1024]{1,0:T(8,128)(2,1)S(1)} %broadcast_select_fusion.d_ref.mine_ref), channel_id=1, source_target_pairs={{0,1},{1,0},{2,3},{3,2},{4,5},{5,4},{6,7},{7,6},{8,9},{9,8},{10,11... | collective-permute-start | bytes 5111816 | tf_op jit(solution)/shard_map/ppermute | solution.py:1093
  127.9 26.6 %collective-permute-start.28 = (bf16[512,1024]{1,0:T(8,128)(2,1)}, bf16[512,1024]{1,0:T(8,128)(2,1)}, u32[]{:S(2)}, u32[]{:S(2)}) collective-permute-start(bf16[512,1024]{1,0:T(8,128)(2,1)} %copy-done.95), channel_id=1, source_target_pairs={{0,4},{4,0},{8,12},{12,8},{16,20},{20,16},{24,28},{28,24},{1,5},{5... | collective-permute-start | bytes 3145736 | tf_op jit(solution)/shard_map/ppermute | solution.py:1099
  168.1 29.4 %collective-permute-start.29 = (bf16[832,1024]{1,0:T(8,128)(2,1)}, bf16[832,1024]{1,0:T(8,128)(2,1)S(1)}, u32[]{:S(2)}, u32[]{:S(2)}) collective-permute-start(bf16[832,1024]{1,0:T(8,128)(2,1)} %get-tuple-element.315), channel_id=1, source_target_pairs={{0,1},{1,0},{2,3},{3,2},{4,5},{5,4},{6,7},{7,6},{8,9},{9,8},{10,11... | collective-permute-start | bytes 5111816 | tf_op jit(solution)/shard_map/ppermute | solution.py:1093
  189.3 48.3 %collective-permute-start.30 = (bf16[1024,1024]{1,0:T(8,128)(2,1)}, bf16[1024,1024]{1,0:T(8,128)(2,1)}, u32[]{:S(2)}, u32[]{:S(2)}) collective-permute-start(bf16[1024,1024]{1,0:T(8,128)(2,1)} %up_grad.2), channel_id=1, source_target_pairs={{0,2},{2,0},{1,3},{3,1},{4,6},{6,4},{5,7},{7,5},{8,10},{10,8},{9,1... | collective-permute-start | bytes 6291464 | tf_op jit(solution)/shard_map/ppermute | solution.py:1096
  221.9 15.7 %collective-permute-start.31 = (bf16[832,1024]{1,0:T(8,128)(2,1)}, bf16[832,1024]{1,0:T(8,128)(2,1)S(1)}, u32[]{:S(2)}, u32[]{:S(2)}) collective-permute-start(bf16[832,1024]{1,0:T(8,128)(2,1)} %get-tuple-element.339.mine_ref.refs_2_.refs_1_), channel_id=1, source_target_pairs={{0,1},{1,0},{2,3},{3,2},{4,5},{5,4},{6,7},{7,6},{8,9},{9,8},{10,11... | collective-permute-start | bytes 5111816 | tf_op jit(solution)/shard_map/ppermute | solution.py:1093
  222.2 36.4 %collective-permute-start.33 = (bf16[832,1024]{1,0:T(8,128)(2,1)}, bf16[832,1024]{1,0:T(8,128)(2,1)}, u32[]{:S(2)}, u32[]{:S(2)}) collective-permute-start(bf16[832,1024]{1,0:T(8,128)(2,1)} %get-tuple-element.303.mine_ref), channel_id=1, source_target_pairs={{0,1},{1,0},{2,3},{3,2},{4,5},{5,4},{6,7},{7,6},{8,9},{9,8},{10,11... | collective-permute-start | bytes 5111816 | tf_op jit(solution)/shard_map/ppermute | solution.py:1093
  238.6 20.0 %collective-permute-start.32 = (bf16[832,512]{1,0:T(8,128)(2,1)}, bf16[832,512]{1,0:T(8,128)(2,1)}, u32[]{:S(2)}, u32[]{:S(2)}) collective-permute-start(bf16[832,512]{1,0:T(8,128)(2,1)} %slice.78), channel_id=1, source_target_pairs={{0,1},{1,0},{2,3},{3,2},{4,5},{5,4},{6,7},{7,6},{8,9},{9,8},{10,11... | collective-permute-start | bytes 2555912 | tf_op jit(solution)/shard_map/ppermute | solution.py:1093
  238.6 49.3 %collective-permute-start.37 = (bf16[1024,1024]{1,0:T(8,128)(2,1)}, bf16[1024,1024]{1,0:T(8,128)(2,1)}, u32[]{:S(2)}, u32[]{:S(2)}) collective-permute-start(bf16[1024,1024]{1,0:T(8,128)(2,1)} %down_grad.2), channel_id=1, source_target_pairs={{0,2},{2,0},{1,3},{3,1},{4,6},{6,4},{5,7},{7,5},{8,10},{10,8},{9,1... | collective-permute-start | bytes 6291464 | tf_op jit(solution)/shard_map/ppermute | solution.py:1096
  240.8 17.8 %collective-permute-start.34 = (f32[2,2,64,256]{3,2,0,1:T(8,128)S(1)}, f32[2,2,64,256]{3,2,0,1:T(8,128)S(1)}, u32[]{:S(2)}, u32[]{:S(2)}) collective-permute-start(f32[2,2,64,256]{3,2,0,1:T(8,128)S(1)} %get-tuple-element.503), channel_id=1, source_target_pairs={{0,1},{1,0},{2,3},{3,2},{4,5},{5,4},{6,7},{7,6},{8,9},{9,8},{10,11... | collective-permute-start | bytes 786440 | tf_op jit(solution)/shard_map/ppermute | solution.py:1093
  248.9 84.3 %collective-permute-start.35 = (bf16[832,1024]{1,0:T(8,128)(2,1)}, bf16[832,1024]{1,0:T(8,128)(2,1)}, u32[]{:S(2)}, u32[]{:S(2)}) collective-permute-start(bf16[832,1024]{1,0:T(8,128)(2,1)} %get-tuple-element.401.refs_6_.refs_5_), channel_id=1, source_target_pairs={{0,1},{1,0},{2,3},{3,2},{4,5},{5,4},{6,7},{7,6},{8,9},{9,8},{10,11... | collective-permute-start | bytes 5111816 | tf_op jit(solution)/shard_map/ppermute | solution.py:1093
  292.0 36.3 %collective-permute-start.38 = (bf16[512,1024]{1,0:T(8,128)(2,1)}, bf16[512,1024]{1,0:T(8,128)(2,1)}, u32[]{:S(2)}, u32[]{:S(2)}) collective-permute-start(bf16[512,1024]{1,0:T(8,128)(2,1)} %get-tuple-element.491), channel_id=1, source_target_pairs={{0,4},{4,0},{8,12},{12,8},{16,20},{20,16},{24,28},{28,24},{1,5},{5... | collective-permute-start | bytes 3145736 | tf_op jit(solution)/shard_map/ppermute | solution.py:1099
  297.5 34.5 %collective-permute-start.36 = (bf16[832,512]{1,0:T(8,128)(2,1)}, bf16[832,512]{1,0:T(8,128)(2,1)}, u32[]{:S(2)}, u32[]{:S(2)}) collective-permute-start(bf16[832,512]{1,0:T(8,128)(2,1)} %slice.81), channel_id=1, source_target_pairs={{0,1},{1,0},{2,3},{3,2},{4,5},{5,4},{6,7},{7,6},{8,9},{9,8},{10,11... | collective-permute-start | bytes 2555912 | tf_op jit(solution)/shard_map/ppermute | solution.py:1093
  297.5 227.3 %collective-permute-start.62 = (bf16[832,1024]{1,0:T(8,128)(2,1)}, bf16[832,1024]{1,0:T(8,128)(2,1)}, u32[]{:S(2)}, u32[]{:S(2)}) collective-permute-start(bf16[832,1024]{1,0:T(8,128)(2,1)} %get-tuple-element.452), channel_id=1, source_target_pairs={{0,1},{1,0},{2,3},{3,2},{4,5},{5,4},{6,7},{7,6},{8,9},{9,8},{10,11... | collective-permute-start | bytes 5111816 | tf_op jit(solution)/shard_map/ppermute | solution.py:1093
  301.9 70.4 %collective-permute-start.44 = (bf16[3072,256]{1,0:T(8,128)(2,1)}, bf16[3072,256]{1,0:T(8,128)(2,1)}, u32[]{:S(2)}, u32[]{:S(2)}) collective-permute-start(bf16[3072,256]{1,0:T(8,128)(2,1)} %copy-done.38), channel_id=1, source_target_pairs={{0,2},{2,0},{1,3},{3,1},{4,6},{6,4},{5,7},{7,5},{8,10},{10,8},{9,1... | collective-permute-start | bytes 4718600 | tf_op jit(solution)/shard_map/ppermute | solution.py:1096
  328.3 22.8 %collective-permute-start.39 = (bf16[1024,256]{1,0:T(8,128)(2,1)S(1)}, bf16[1024,256]{1,0:T(8,128)(2,1)S(1)}, u32[]{:S(2)}, u32[]{:S(2)}) collective-permute-start(bf16[1024,256]{1,0:T(8,128)(2,1)S(1)} %copy-done.48), channel_id=1, source_target_pairs={{0,2},{2,0},{1,3},{3,1},{4,6},{6,4},{5,7},{7,5},{8,10},{10,8},{9,1... | collective-permute-start | bytes 1572872 | tf_op jit(solution)/shard_map/ppermute | solution.py:1096
  332.0 19.1 %collective-permute-start.40 = (bf16[2,64,256]{2,1,0:T(8,128)(2,1)S(1)}, bf16[2,64,256]{2,1,0:T(8,128)(2,1)S(1)}, u32[]{:S(2)}, u32[]{:S(2)}) collective-permute-start(bf16[2,64,256]{2,1,0:T(8,128)(2,1)S(1)} %copy-done.104), channel_id=1, source_target_pairs={{0,2},{2,0},{1,3},{3,1},{4,6},{6,4},{5,7},{7,5},{8,10},{10,8},{9,1... | collective-permute-start | bytes 196616 | tf_op jit(solution)/shard_map/ppermute | solution.py:1096
  351.8 38.3 %collective-permute-start.47 = (bf16[512,1024]{1,0:T(8,128)(2,1)S(1)}, bf16[512,1024]{1,0:T(8,128)(2,1)}, u32[]{:S(2)}, u32[]{:S(2)}) collective-permute-start(bf16[512,1024]{1,0:T(8,128)(2,1)S(1)} %outputs_grad.2), channel_id=1, source_target_pairs={{0,2},{2,0},{1,3},{3,1},{4,6},{6,4},{5,7},{7,5},{8,10},{10,8},{9,1... | collective-permute-start | bytes 3145736 | tf_op jit(solution)/shard_map/ppermute | solution.py:1096
  355.6 19.5 %collective-permute-start.43 = (bf16[256,1024]{1,0:T(8,128)(2,1)}, bf16[256,1024]{1,0:T(8,128)(2,1)}, u32[]{:S(2)}, u32[]{:S(2)}) collective-permute-start(bf16[256,1024]{1,0:T(8,128)(2,1)} %dynamic-slice_convert_fusion), channel_id=1, source_target_pairs={{0,8},{4,12},{8,0},{12,4},{16,24},{20,28},{24,16},{28,20},{1,9},{5... | collective-permute-start | bytes 1572872 | tf_op jit(solution)/shard_map/ppermute | solution.py:1099
  357.2 22.1 %collective-permute-start.42 = (bf16[1536,256]{1,0:T(8,128)(2,1)}, bf16[1536,256]{1,0:T(8,128)(2,1)}, u32[]{:S(2)}, u32[]{:S(2)}) collective-permute-start(bf16[1536,256]{1,0:T(8,128)(2,1)} %get-tuple-element.499), channel_id=1, source_target_pairs={{0,4},{4,0},{8,12},{12,8},{16,20},{20,16},{24,28},{28,24},{1,5},{5... | collective-permute-start | bytes 2359304 | tf_op jit(solution)/shard_map/ppermute | solution.py:1099
  372.3 67.2 %collective-permute-start.49 = (bf16[832,1024]{1,0:T(8,128)(2,1)}, bf16[832,1024]{1,0:T(8,128)(2,1)}, u32[]{:S(2)}, u32[]{:S(2)}) collective-permute-start(bf16[832,1024]{1,0:T(8,128)(2,1)} %first_back.2), channel_id=1, source_target_pairs={{0,1},{1,0},{2,3},{3,2},{4,5},{5,4},{6,7},{7,6},{8,9},{9,8},{10,11... | collective-permute-start | bytes 5111816 | tf_op jit(solution)/shard_map/ppermute | solution.py:1093
  375.0 54.3 %collective-permute-start.46 = (bf16[1536,256]{1,0:T(8,128)(2,1)}, bf16[1536,256]{1,0:T(8,128)(2,1)}, u32[]{:S(2)}, u32[]{:S(2)}) collective-permute-start(bf16[1536,256]{1,0:T(8,128)(2,1)} %get-tuple-element.492), channel_id=1, source_target_pairs={{0,8},{4,12},{8,0},{12,4},{16,24},{20,28},{24,16},{28,20},{1,9},{5... | collective-permute-start | bytes 2359304 | tf_op jit(solution)/shard_map/ppermute | solution.py:1099
  379.3 68.3 %collective-permute-start.53 = (bf16[256,1024]{1,0:T(8,128)(2,1)}, bf16[256,1024]{1,0:T(8,128)(2,1)}, u32[]{:S(2)}, u32[]{:S(2)}) collective-permute-start(bf16[256,1024]{1,0:T(8,128)(2,1)} %add_convert_fusion.6), channel_id=1, source_target_pairs={{0,16},{4,20},{8,24},{12,28},{16,0},{20,4},{24,8},{28,12},{1,17},{... | collective-permute-start | bytes 1572872 | tf_op jit(solution)/shard_map/ppermute | solution.py:1099
  390.1 48.6 %collective-permute-start.45 = (bf16[768,256]{1,0:T(8,128)(2,1)S(1)}, bf16[768,256]{1,0:T(8,128)(2,1)S(1)}, u32[]{:S(2)}, u32[]{:S(2)}) collective-permute-start(bf16[768,256]{1,0:T(8,128)(2,1)S(1)} %dynamic-slice_convert_fusion.2), channel_id=1, source_target_pairs={{0,8},{4,12},{8,0},{12,4},{16,24},{20,28},{24,16},{28,20},{1,9},{5... | collective-permute-start | bytes 1179656 | tf_op jit(solution)/shard_map/ppermute | solution.py:1099
  429.4 20.6 %collective-permute-start.52 = (bf16[256,1024]{1,0:T(8,128)(2,1)S(1)}, bf16[256,1024]{1,0:T(8,128)(2,1)S(1)}, u32[]{:S(2)}, u32[]{:S(2)}) collective-permute-start(bf16[256,1024]{1,0:T(8,128)(2,1)S(1)} %get-tuple-element.496), channel_id=1, source_target_pairs={{0,4},{4,0},{8,12},{12,8},{16,20},{20,16},{24,28},{28,24},{1,5},{5... | collective-permute-start | bytes 1572872 | tf_op jit(solution)/shard_map/ppermute | solution.py:1099
  438.8 12.2 %collective-permute-start.51 = (bf16[768,256]{1,0:T(8,128)(2,1)S(1)}, bf16[768,256]{1,0:T(8,128)(2,1)S(1)}, u32[]{:S(2)}, u32[]{:S(2)}) collective-permute-start(bf16[768,256]{1,0:T(8,128)(2,1)S(1)} %dynamic-slice_convert_fusion.1), channel_id=1, source_target_pairs={{0,4},{4,0},{8,12},{12,8},{16,20},{20,16},{24,28},{28,24},{1,5},{5... | collective-permute-start | bytes 1179656 | tf_op jit(solution)/shard_map/ppermute | solution.py:1099
  439.5 19.4 %collective-permute-start.48 = (bf16[768,256]{1,0:T(8,128)(2,1)S(1)}, bf16[768,256]{1,0:T(8,128)(2,1)S(1)}, u32[]{:S(2)}, u32[]{:S(2)}) collective-permute-start(bf16[768,256]{1,0:T(8,128)(2,1)S(1)} %add_convert_fusion.11), channel_id=1, source_target_pairs={{0,16},{4,20},{8,24},{12,28},{16,0},{20,4},{24,8},{28,12},{1,17},{... | collective-permute-start | bytes 1179656 | tf_op jit(solution)/shard_map/ppermute | solution.py:1099
  449.0 29.5 %collective-permute-start.55 = (bf16[256,1024]{1,0:T(8,128)(2,1)S(1)}, bf16[256,1024]{1,0:T(8,128)(2,1)S(1)}, u32[]{:S(2)}, u32[]{:S(2)}) collective-permute-start(bf16[256,1024]{1,0:T(8,128)(2,1)S(1)} %add_convert_fusion.4), channel_id=1, source_target_pairs={{0,8},{4,12},{8,0},{12,4},{16,24},{20,28},{24,16},{28,20},{1,9},{5... | collective-permute-start | bytes 1572872 | tf_op jit(solution)/shard_map/ppermute | solution.py:1099
  451.0 33.1 %collective-permute-start.58 = (bf16[128,1024]{1,0:T(8,128)(2,1)S(1)}, bf16[128,1024]{1,0:T(8,128)(2,1)S(1)}, u32[]{:S(2)}, u32[]{:S(2)}) collective-permute-start(bf16[128,1024]{1,0:T(8,128)(2,1)S(1)} %dynamic-slice_convert_fusion.4), channel_id=1, source_target_pairs={{0,8},{4,12},{8,0},{12,4},{16,24},{20,28},{24,16},{28,20},{1,9},{5... | collective-permute-start | bytes 786440 | tf_op jit(solution)/shard_map/ppermute | solution.py:1099
  451.6 33.8 %collective-permute-start.59 = (bf16[768,256]{1,0:T(8,128)(2,1)S(1)}, bf16[768,256]{1,0:T(8,128)(2,1)S(1)}, u32[]{:S(2)}, u32[]{:S(2)}) collective-permute-start(bf16[768,256]{1,0:T(8,128)(2,1)S(1)} %add_convert_fusion.10), channel_id=1, source_target_pairs={{0,16},{4,20},{8,24},{12,28},{16,0},{20,4},{24,8},{28,12},{1,17},{... | collective-permute-start | bytes 1179656 | tf_op jit(solution)/shard_map/ppermute | solution.py:1099
  458.9 21.4 %collective-permute-start.56 = (f32[8,1024]{1,0:T(8,128)S(1)}, f32[8,1024]{1,0:T(8,128)S(1)}, u32[]{:S(2)}, u32[]{:S(2)}) collective-permute-start(f32[8,1024]{1,0:T(8,128)S(1)} %add.238), channel_id=1, source_target_pairs={{0,2},{2,0},{1,3},{3,1},{4,6},{6,4},{5,7},{7,5},{8,10},{10,8},{9,1... | collective-permute-start | bytes 98312 | tf_op jit(solution)/shard_map/ppermute | solution.py:1096
  479.0 38.6 %collective-permute-start.63 = (bf16[512,1024]{1,0:T(8,128)(2,1)S(1)}, bf16[512,1024]{1,0:T(8,128)(2,1)S(1)}, u32[]{:S(2)}, u32[]{:S(2)}) collective-permute-start(bf16[512,1024]{1,0:T(8,128)(2,1)S(1)} %maximum_select_fusion.3), channel_id=1, source_target_pairs={{0,4},{4,0},{8,12},{12,8},{16,20},{20,16},{24,28},{28,24},{1,5},{5... | collective-permute-start | bytes 3145736 | tf_op jit(solution)/shard_map/ppermute | solution.py:1099
  480.3 24.5 %collective-permute-start.54 = (bf16[768,256]{1,0:T(8,128)(2,1)S(1)}, bf16[768,256]{1,0:T(8,128)(2,1)S(1)}, u32[]{:S(2)}, u32[]{:S(2)}) collective-permute-start(bf16[768,256]{1,0:T(8,128)(2,1)S(1)} %add_convert_fusion.9), channel_id=1, source_target_pairs={{0,8},{4,12},{8,0},{12,4},{16,24},{20,28},{24,16},{28,20},{1,9},{5... | collective-permute-start | bytes 1179656 | tf_op jit(solution)/shard_map/ppermute | solution.py:1099
  484.1 20.6 %collective-permute-start.57 = (f32[8,1024]{1,0:T(8,128)S(1)}, f32[8,1024]{1,0:T(8,128)S(1)}, u32[]{:S(2)}, u32[]{:S(2)}) collective-permute-start(f32[8,1024]{1,0:T(8,128)S(1)} %add.240), channel_id=1, source_target_pairs={{0,4},{4,0},{8,12},{12,8},{16,20},{20,16},{24,28},{28,24},{1,5},{5... | collective-permute-start | bytes 98312 | tf_op jit(solution)/shard_map/ppermute | solution.py:1099
  485.4 19.9 %collective-permute-start.41 = (f32[64,1024]{1,0:T(8,128)S(1)}, f32[64,1024]{1,0:T(8,128)S(1)}, u32[]{:S(2)}, u32[]{:S(2)}) collective-permute-start(f32[64,1024]{1,0:T(8,128)S(1)} %get-tuple-element.501), channel_id=1, source_target_pairs={{0,2},{2,0},{1,3},{3,1},{4,6},{6,4},{5,7},{7,5},{8,10},{10,8},{9,1... | collective-permute-start | bytes 786440 | tf_op jit(solution)/shard_map/ppermute | solution.py:1096
  504.7 12.8 %collective-permute-start.61 = (bf16[128,1024]{1,0:T(8,128)(2,1)S(1)}, bf16[128,1024]{1,0:T(8,128)(2,1)S(1)}, u32[]{:S(2)}, u32[]{:S(2)}) collective-permute-start(bf16[128,1024]{1,0:T(8,128)(2,1)S(1)} %add_convert_fusion.13), channel_id=1, source_target_pairs={{0,16},{4,20},{8,24},{12,28},{16,0},{20,4},{24,8},{28,12},{1,17},{... | collective-permute-start | bytes 786440 | tf_op jit(solution)/shard_map/ppermute | solution.py:1099
  504.8 12.7 %collective-permute-start.64 = (f32[8,1024]{1,0:T(8,128)S(1)}, f32[8,1024]{1,0:T(8,128)S(1)}, u32[]{:S(2)}, u32[]{:S(2)}) collective-permute-start(f32[8,1024]{1,0:T(8,128)S(1)} %add.244), channel_id=1, source_target_pairs={{0,8},{4,12},{8,0},{12,4},{16,24},{20,28},{24,16},{28,20},{1,9},{5... | collective-permute-start | bytes 98312 | tf_op jit(solution)/shard_map/ppermute | solution.py:1099
  505.3 20.3 %collective-permute-start.68 = (bf16[768,256]{1,0:T(8,128)(2,1)S(1)}, bf16[768,256]{1,0:T(8,128)(2,1)S(1)}, u32[]{:S(2)}, u32[]{:S(2)}) collective-permute-start(bf16[768,256]{1,0:T(8,128)(2,1)S(1)} %add_convert_fusion.8), channel_id=1, source_target_pairs={{0,4},{4,0},{8,12},{12,8},{16,20},{20,16},{24,28},{28,24},{1,5},{5... | collective-permute-start | bytes 1179656 | tf_op jit(solution)/shard_map/ppermute | solution.py:1099
  517.5 20.3 %collective-permute-start.70 = (bf16[1536,256]{1,0:T(8,128)(2,1)S(1)}, bf16[1536,256]{1,0:T(8,128)(2,1)S(1)}, u32[]{:S(2)}, u32[]{:S(2)}) collective-permute-start(bf16[1536,256]{1,0:T(8,128)(2,1)S(1)} %maximum_select_fusion.5), channel_id=1, source_target_pairs={{0,4},{4,0},{8,12},{12,8},{16,20},{20,16},{24,28},{28,24},{1,5},{5... | collective-permute-start | bytes 2359304 | tf_op jit(solution)/shard_map/ppermute | solution.py:1099
  517.6 10.4 %collective-permute-start.67 = (bf16[128,1024]{1,0:T(8,128)(2,1)S(1)}, bf16[128,1024]{1,0:T(8,128)(2,1)S(1)}, u32[]{:S(2)}, u32[]{:S(2)}) collective-permute-start(bf16[128,1024]{1,0:T(8,128)(2,1)S(1)} %add_convert_fusion.12), channel_id=1, source_target_pairs={{0,8},{4,12},{8,0},{12,4},{16,24},{20,28},{24,16},{28,20},{1,9},{5... | collective-permute-start | bytes 786440 | tf_op jit(solution)/shard_map/ppermute | solution.py:1099
  524.8 20.0 %collective-permute-start.66 = (f32[8,1024]{1,0:T(8,128)S(1)}, f32[8,1024]{1,0:T(8,128)S(1)}, u32[]{:S(2)}, u32[]{:S(2)}) collective-permute-start(f32[8,1024]{1,0:T(8,128)S(1)} %add.248), channel_id=1, source_target_pairs={{0,16},{4,20},{8,24},{12,28},{16,0},{20,4},{24,8},{28,12},{1,17},{... | collective-permute-start | bytes 98312 | tf_op jit(solution)/shard_map/ppermute | solution.py:1099
  526.8 20.0 %collective-permute-start.71 = (bf16[1536,256]{1,0:T(8,128)(2,1)}, bf16[1536,256]{1,0:T(8,128)(2,1)}, u32[]{:S(2)}, u32[]{:S(2)}) collective-permute-start(bf16[1536,256]{1,0:T(8,128)(2,1)} %maximum_select_fusion.6), channel_id=1, source_target_pairs={{0,8},{4,12},{8,0},{12,4},{16,24},{20,28},{24,16},{28,20},{1,9},{5... | collective-permute-start | bytes 2359304 | tf_op jit(solution)/shard_map/ppermute | solution.py:1099
  529.0 24.3 %collective-permute-start.69 = (bf16[256,1024]{1,0:T(8,128)(2,1)}, bf16[256,1024]{1,0:T(8,128)(2,1)}, u32[]{:S(2)}, u32[]{:S(2)}) collective-permute-start(bf16[256,1024]{1,0:T(8,128)(2,1)} %maximum_select_fusion.7), channel_id=1, source_target_pairs={{0,4},{4,0},{8,12},{12,8},{16,20},{20,16},{24,28},{28,24},{1,5},{5... | collective-permute-start | bytes 1572872 | tf_op jit(solution)/shard_map/ppermute | solution.py:1099
  537.9 8.2 %collective-permute-start.65 = (bf16[64,1024]{1,0:T(8,128)(2,1)S(1)}, bf16[64,1024]{1,0:T(8,128)(2,1)S(1)}, u32[]{:S(2)}, u32[]{:S(2)}) collective-permute-start(bf16[64,1024]{1,0:T(8,128)(2,1)S(1)} %add_convert_fusion.14), channel_id=1, source_target_pairs={{0,2},{2,0},{1,3},{3,1},{4,6},{6,4},{5,7},{7,5},{8,10},{10,8},{9,1... | collective-permute-start | bytes 393224 | tf_op jit(solution)/shard_map/ppermute | solution.py:1096
  (129 other events, 984.9 us)
Sparse Core Ops, SparseCore 0:
  302.0 128.5 all-reduce.1

commit v11 on v10

--- a/solution.py
+++ b/solution.py
@@ -1216,8 +1216,11 @@
     down_z = (near, Z_NEAR)
     store = {}
     last = []
+    free = []
 
     def order(*names):
+        if free:
+            return
         names = tuple(dict.fromkeys((*names, *last)))
         for name, value in zip(names, join(tuple(store[name] for name in names))):
             store[name] = value
@@ -1320,7 +1323,7 @@
     step(["up0"], lambda: up_grad(h3, *get("h3_other", "du0"), ROUND), "du0")
     order(up.fly, "down1", "dself_other")
     down.over_y("down1")
-    store["up_total"] = lax.psum(plus(*get("up0", up.fly)), "wide")
+    up.first("up0")
     step(
         ["dof", "dos", "do0"],
         lambda: pull(place, *get("dself", "dself_other"), (out_first, out_second, w_out)),
@@ -1357,6 +1360,7 @@
         lambda: self_back(limit, qs, ks, vs, store["o_s"], store["dos"], lse_s),
         "dos",
     )
+    up.second()
     step(["down0"], lambda: down_grad(store["g0"], dout, dout_other, ROUND), "g0")
     yp = ("dqf", "dkf", "dvf", "dqs", "dks", "dvs")
     step(["qkv1"], lambda: qkv_grad(place, h1, get(*yp), ROUND), "dqs")
@@ -1365,6 +1369,7 @@
     store["pair_y"] = over_y(store["pair_other"])
     qkv.over_y("qkv1")
     down.first("down0")
+    up.far()
     step(
         ["dq0", "dk0", "dv0"],
         lambda: self_back(limit, q0, k0, v0, store["o0"], store["do0"], lse0),
@@ -1387,6 +1392,13 @@
         axis=0,
     )
     cross_in.first_alone("into0")
+    up.back()
+    text_part = 0.0
+    for c in range(2):
+        text_part = text_part + nt(pairs[c], w_cross_kv[c])
+    text_mine, text_theirs = text_part[:64], text_part[64:]
+    text_rows = Row("texts", text_mine, lambda v: over_y(text_theirs))
+    last[:] = ["texts_kept"]
     nine = ("dq0", "dk0", "dv0", *yp)
     weights = (w_qkv, qkv_first, qkv_second)
     step(["yo"], lambda: first_back(away, get(*nine), weights, ROUND), "dq0")
@@ -1395,9 +1407,12 @@
     qkv.first("qkv0")
     down.far()
     cross_in.second()
+    up.along()
+    store["out_fly"] = over_core(out_o)
     step(["outs0"], lambda: outof(0, "o0"), "dcross")
     outs.first("outs0")
     qkv.second()
+    text_rows.then(over_core)
     step(["ym"], lambda: first_back(place, get(*nine), weights, FULL), "dq0")
     cross_in.far()
     step(
@@ -1407,38 +1422,24 @@
         "yo_fly",
     )
     norms = Row("norms", store["sums"] + store["first_sums"], over_core)
-    down.back()
-    outs.second()
-    qkv.far()
-    norms.then(over_y)
-    cross_in.back()
-    down.along()
-    norms.then(over_x)
-    outs.far()
-    text_part = 0.0
-    for c in range(2):
-        text_part = text_part + nt(pairs[c], w_cross_kv[c])
-    text_mine, text_theirs = text_part[:64], text_part[64:]
-    text_rows = Row("texts", text_mine, lambda v: over_y(text_theirs))
-    store["out_fly"] = over_core(out_o)
-    qkv.back()
-    norms.then(over_z)
-    cross_in.along()
-    text_rows.then(over_core)
-    outs.back()
-    norms.then(lambda v: along_wide(v, Z_FAR))
-    down.end("grad_down")
-    order("up_total")
-    store["grad_up"] = store["up_total"].astype(FULL)
-    last[:] = ["grad_up"]
-    order("texts_fly", "texts_kept", "out_fly", "x2")
+    up.end("grad_up")
     text_grad = lower(text_rows.total())
     text_away = over_y(text_grad)
-    qkv.along()
-    outs.along()
+    grad_text = ordered(text_grad[None], text_away[None], side)
+    order("x2", "out_fly")
     out_rows = lower(store["x2"] + out_m + store["out_fly"].astype(FULL))
-    grad_text = ordered(text_grad[None], text_away[None], side)
+    free[:] = [True]
+    for each in (down, outs, qkv, cross_in):
+        if each is outs:
+            each.second()
+        if each is not cross_in and each is not down:
+            each.far()
+        each.back()
+        each.along()
+    for move in (over_y, over_x, over_z, lambda v: along_wide(v, Z_FAR)):
+        norms.then(move)
     sums = norms.total()
+    down.end("grad_down")
     cross_in.end("grad_in")
     qkv.end("grad_qkv")
     outs.end("grad_outs")

time: 574 us -> 573 us (level)
  between operations: 15.9 us -> 2.52 us
  waiting for transfers between devices: 131 us -> 140 us
  starting transfers between devices: 54.2 us -> 60.3 us
    ppermute x16, waiting for transfers between devices: 26.1 us -> 35.9 us  [over_y(): return lax.ppermute(v, 'narrow', Y_PAIRS)]
    ppermute x29 -> x34, starting transfers between devices: 29.2 us -> 35.3 us  [along_wide(): return lax.ppermute(v, 'wide', pairs)]
    convert_element_type x2 -> x0, other arithmetic: 5.8 us -> none  [the longest x1 4.22 us: chip_local(): store['grad_up'] = store['up_total'].astype(FULL)]
    ppermute x29 -> x34, waiting for transfers between devices: 105 us -> 101 us  [along_wide(): return lax.ppermute(v, 'wide', pairs)]
    convert_element_type x15 -> x17, other arithmetic: 16.1 us -> 18.6 us  [lower(): return values_in.astype(jnp.bfloat16)]
    unnamed x241 -> x219, local copies, waits for them, and re-layouts: 27.4 us -> 24.9 us
  transfers between devices with their start and end apart: 73 -> 77, of which waited for: 17 -> 24; matrix products, arithmetic and copies ran while one was open for 12% -> 13% of each run, Pallas kernels for 44% -> 44%
where the time goes in v11:
time: 573 us; the launch traced here: 563 us
  Pallas kernels  260 us (45%)
  waiting for transfers between devices  140 us (24%)
  starting transfers between devices  60.3 us (11%)
  local copies, waits for them, and re-layouts  50.5 us (9%)
  other arithmetic  48.8 us (9%)
    ppermute x34, waiting for transfers between devices, along_wide(): return lax.ppermute(v, 'wide', pairs)  101 us
    pallas_call x4, Pallas kernels, feed(): pl.pallas_call(functools.partial(feed_kernel, parts=parts, carried=len(be...  51.7 us
    pallas_call x3, Pallas kernels, self_back(): pl.pallas_call(functools.partial(self_back_kernel, span=span, floor=floor...  39.5 us
    ppermute x16, waiting for transfers between devices, over_y(): return lax.ppermute(v, 'narrow', Y_PAIRS)  35.9 us
    ppermute x34, starting transfers between devices, along_wide(): return lax.ppermute(v, 'wide', pairs)  35.3 us
    pallas_call x3, Pallas kernels, self_forward(): pl.pallas_call(functools.partial(self_forward_kernel, span=span, floor=fl...  30.8 us
    unnamed x219, local copies, waits for them, and re-layouts  24.9 us
    pallas_call x1, Pallas kernels, middle_back(): pl.pallas_call(middle_back_kernel, grid_spec=pltpu.PrefetchScalarGridSpec...  23.1 us
  transfers between devices with their start and end apart: 77, of which 24 were waited for; matrix products, arithmetic and copies ran while one was open for 13% of the time, Pallas kernels for 44%

profile of v11, /device:TPU:0, one launch (start us, length us, event | category | flops | bytes accessed | tf_op | source)
XLA Modules:
  0.0 563.1 jit_solution(1149633108357073637)
XLA Ops:
  1.2 2.1 constant_dynamic-slice_fusion.14
  3.2 2.6 collective-permute-start.1
  14.8 4.5 first_project.1
  22.1 2.1 collective-permute-done.1.weight_ref.refs_10_
  30.5 4.0 collective-permute-done.2.refs_7_.refs_0_
  36.3 3.8 collective-permute-done.3.refs_13_.refs_1_
  41.9 14.0 %self_forward.3 = (bf16[1664,256]{1,0:T(8,128)(2,1)}, f32[2,8,1664]{2,1,0:T(8,128)}) custom-call(s32[1]{0:T(128)} %dynamic_slice.129.limit_ref, bf16[1664,256]{1,0:T(8,128)(2,1)} %copy-done.62, bf16[1664,256]{1,0:T(8,128)(2,1)} %copy-done.64, bf16[1664,256]{1,0:T(8,128)(2,1)} %copy-done.66), custom_call_target="tpu_custom_call" | custom-call | flops 4701199872 | bytes 1000 | tf_op jit(solution)/shard_map/self_forward/pallas_call | solution.py:525
  56.0 4.3 project.2
  64.0 8.3 %self_forward.4 = (bf16[1664,128]{1,0:T(8,128)(2,1)}, f32[1,8,1664]{2,1,0:T(8,128)}) custom-call(s32[1]{0:T(128)} %dynamic_slice.129.limit_ref, bf16[1664,128]{1,0:T(8,128)(2,1)} %copy-done.50, bf16[1664,128]{1,0:T(8,128)(2,1)} %copy-done.52, bf16[1664,128]{1,0:T(8,128)(2,1)} %copy-done.54), custom_call_target="tpu_custom_call" | custom-call | flops 2350599936 | bytes 1000 | tf_op jit(solution)/shard_map/self_forward/pallas_call | solution.py:525
  75.5 2.7 project.3
  81.8 8.4 %self_forward.5 = (bf16[1664,128]{1,0:T(8,128)(2,1)}, f32[1,8,1664]{2,1,0:T(8,128)}) custom-call(s32[1]{0:T(128)} %dynamic_slice.129.limit_ref, bf16[1664,128]{1,0:T(8,128)(2,1)} %copy-done.56, bf16[1664,128]{1,0:T(8,128)(2,1)} %copy-done.58, bf16[1664,128]{1,0:T(8,128)(2,1)} %copy-done.60), custom_call_target="tpu_custom_call" | custom-call | flops 2350599936 | bytes 1000 | tf_op jit(solution)/shard_map/self_forward/pallas_call | solution.py:525
  99.0 20.7 %middle_forward.1 = (f32[832,1024]{1,0:T(8,128)}, f32[832,1024]{1,0:T(8,128)}, bf16[832,1024]{1,0:T(8,128)(2,1)}, bf16[832,1024]{1,0:T(8,128)(2,1)}, bf16[832,10...) custom-call(s32[3]{0:T(128)} %copy-done.42, bf16[832,1024]{1,0:T(8,128)(2,1)} %frame_ref.3, ...), custom_call_target="tpu_custom_call" | custom-call | flops 7084000256 | bytes 1000 | tf_op jit(solution)/shard_map/middle_forward/pallas_call | solution.py:677
  121.8 12.2 %feed.4 = (bf16[1664,1024]{1,0:T(8,128)(2,1)}, bf16[1664,1024]{1,0:T(8,128)(2,1)}, f32[832,1024]{1,0:T(8,128)}, f32[832,1024]{1,0:T(8,128)}) custom-call(s32[3]{0:T(128)} %copy-done.42, bf16[832,1024]{1,0:T(8,128)(2,1)} %get-tuple-element.252.h_ref.mine_ref, bf16[832,1024]{1,0:T(8,128)(2,1)} %copy-done, bf16[1024,1024]{1,0:T(8,128)(2,1)} %refs_0_.1, ...), custom_call_target="tpu_custom_call" | custom-call | flops 4185999872 | bytes 1000 | tf_op jit(solution)/shard_map/feed/pallas_call | solution.py:756
  135.7 12.2 %feed.5 = (bf16[1664,1024]{1,0:T(8,128)(2,1)}, bf16[1664,1024]{1,0:T(8,128)(2,1)}, f32[832,1024]{1,0:T(8,128)}, f32[832,1024]{1,0:T(8,128)}) custom-call(s32[3]{0:T(128)} %copy-done.42, bf16[832,1024]{1,0:T(8,128)(2,1)} %copy-done.14, bf16[832,1024]{1,0:T(8,128)(2,1)} %copy-done.11, ...), custom_call_target="tpu_custom_call", output_to_operand_aliasing={{0}: (5, {}), {1}: (6, {})} | custom-call | flops 4185999872 | bytes 1000 | tf_op jit(solution)/shard_map/feed/pallas_call | solution.py:756
  147.8 13.6 %feed.6 = (bf16[1664,1024]{1,0:T(8,128)(2,1)}, bf16[1664,1024]{1,0:T(8,128)(2,1)}, bf16[832,1024]{1,0:T(8,128)(2,1)}, bf16[832,1024]{1,0:T(8,128)(2,1)}) custom-call(s32[3]{0:T(128)} %copy-done.42, bf16[832,1024]{1,0:T(8,128)(2,1)} %copy-done.14, bf16[832,1024]{1,0:T(8,128)(2,1)} %copy-done.11, bf16[1024,512]{1,0:T(8,128)(2,1)} %collective-permute-done.14.refs_0_, ...), custom_call_target="tpu_custom_call" | custom-call | flops 4185999872 | bytes 1000 | tf_op jit(solution)/shard_map/feed/pallas_call | solution.py:756
  161.5 13.7 %feed.7 = (bf16[1664,1024]{1,0:T(8,128)(2,1)}, bf16[1664,1024]{1,0:T(8,128)(2,1)}, f32[832,1024]{1,0:T(8,128)}, f32[832,1024]{1,0:T(8,128)}) custom-call(s32[3]{0:T(128)} %copy-done.42, bf16[832,1024]{1,0:T(8,128)(2,1)} %get-tuple-element.252.h_ref.mine_ref, bf16[832,1024]{1,0:T(8,128)(2,1)} %copy-done, ...), custom_call_target="tpu_custom_call", output_to_operand_aliasing={{0}: (9, {}), {1}: (10, {})} | custom-call | flops 4185999872 | bytes 1000 | tf_op jit(solution)/shard_map/feed/pallas_call | solution.py:756
  175.3 7.3 %up_grad.2 = bf16[1024,1024]{1,0:T(8,128)(2,1)} custom-call(bf16[832,1024]{1,0:T(8,128)(2,1)S(1)} %copy-done.3, bf16[832,1024]{1,0:T(8,128)(2,1)S(1)} %copy-done.15, bf16[1664,1024]{1,0:T(8,128)(2,1)} %get-tuple-element.274.du_ref), custom_call_target="tpu_custom_call" | custom-call | flops 1610000000 | bytes 1000 | tf_op jit(solution)/shard_map/up_grad/pallas_call | solution.py:786
  183.6 6.2 %down_grad.2 = bf16[1024,1024]{1,0:T(8,128)(2,1)S(1)} custom-call(bf16[1664,1024]{1,0:T(8,128)(2,1)} %get-tuple-element.275.g_ref, bf16[832,1024]{1,0:T(8,128)(2,1)S(1)} %copy-done.1, bf16[832,1024]{1,0:T(8,128)(2,1)S(1)} %copy-done.12), custom_call_target="tpu_custom_call" | custom-call | flops 1610000000 | bytes 1000 | tf_op jit(solution)/shard_map/down_grad/pallas_call | solution.py:809
  192.4 23.1 %middle_back.1 = (f32[832,1024]{1,0:T(8,128)}, bf16[832,1024]{1,0:T(8,128)(2,1)}, bf16[832,1024]{1,0:T(8,128)(2,1)}, bf16[832,1024]{1,0:T(8,128)(2,1)}, f32[4,64...) custom-call(s32[3]{0:T(128)} %copy-done.42, f32[832,1024]{1,0:T(8,128)} %get-tuple-element.279.ym_ref, ...), custom_call_target="tpu_custom_call" | custom-call | flops 7728000000 | bytes 1000 | tf_op jit(solution)/shard_map/middle_back/pallas_call | solution.py:992
  217.5 6.3 %up_grad.3 = bf16[1024,1024]{1,0:T(8,128)(2,1)S(1)} custom-call(bf16[832,1024]{1,0:T(8,128)(2,1)S(1)} %copy-done.3, bf16[832,1024]{1,0:T(8,128)(2,1)S(1)} %copy-done.16, bf16[1664,1024]{1,0:T(8,128)(2,1)} %get-tuple-element.285.du_ref), custom_call_target="tpu_custom_call" | custom-call | flops 1610000000 | bytes 1000 | tf_op jit(solution)/shard_map/up_grad/pallas_call | solution.py:786
  223.9 7.1 %collective-permute-done.31 = bf16[1024,1024]{1,0:T(8,128)(2,1)} collective-permute-done((bf16[1024,1024]{1,0:T(8,128)(2,1)}, bf16[1024,1024]{1,0:T(8,128)(2,1)}, u32[]{:S(2)}, u32[]{:S(2)}) %collective-permute-start.31) | collective-permute-done | bytes 2097184 | tf_op jit(solution)/shard_map/ppermute | solution.py:1096
  232.1 4.1 convert_add_fusion.3
  240.4 5.2 pull.1
  249.1 9.3 %self_back.3 = (bf16[1664,128]{1,0:T(8,128)(2,1)S(1)}, bf16[1664,128]{1,0:T(8,128)(2,1)S(1)}, bf16[1664,128]{1,0:T(8,128)(2,1)S(1)}) custom-call(s32[1]{0:T(128)} %dynamic_slice.129.limit_ref, bf16[1664,128]{1,0:T(8,128)(2,1)S(1)} %copy-done.51, bf16[1664,128]{1,0:T(8,128)(2,1)S(1)} %copy-done.53, bf16[1664,128]{1,0:T(8,128)(2,1)S(1)} %copy-done.55, ...), custom_call_target="tpu_custom_call" | custom-call | flops 2254000128 | bytes 1000 | tf_op jit(solution)/shard_map/self_back/pallas_call | solution.py:606
  259.3 4.9 query_grad.2
  264.2 9.7 %self_back.4 = (bf16[1664,128]{1,0:T(8,128)(2,1)S(1)}, bf16[1664,128]{1,0:T(8,128)(2,1)S(1)}, bf16[1664,128]{1,0:T(8,128)(2,1)S(1)}) custom-call(s32[1]{0:T(128)} %dynamic_slice.129.limit_ref, bf16[1664,128]{1,0:T(8,128)(2,1)S(1)} %copy-done.57, bf16[1664,128]{1,0:T(8,128)(2,1)S(1)} %copy-done.59, bf16[1664,128]{1,0:T(8,128)(2,1)S(1)} %copy-done.61, ...), custom_call_target="tpu_custom_call" | custom-call | flops 2254000128 | bytes 1000 | tf_op jit(solution)/shard_map/self_back/pallas_call | solution.py:606
  276.6 6.2 %down_grad.3 = bf16[1024,1024]{1,0:T(8,128)(2,1)S(1)} custom-call(bf16[1664,1024]{1,0:T(8,128)(2,1)} %get-tuple-element.321.g_ref, bf16[832,1024]{1,0:T(8,128)(2,1)S(1)} %copy-done.2, bf16[832,1024]{1,0:T(8,128)(2,1)S(1)} %copy-done.13), custom_call_target="tpu_custom_call" | custom-call | flops 1610000000 | bytes 1000 | tf_op jit(solution)/shard_map/down_grad/pallas_call | solution.py:809
  285.3 7.3 %qkv_grad.2 = bf16[3072,256]{1,0:T(8,128)(2,1)} custom-call(s32[3]{0:T(128)S(1)} %copy-done.43, bf16[1664,1024]{1,0:T(8,128)(2,1)} %copy-done.8, bf16[1664,128]{1,0:T(8,128)(2,1)S(1)} %get-tuple-element.317.refs_0_.refs_3_, bf16[1664,128]{1,0:T(8,128)(2,1)S(1)} %get-tuple-element.318.refs_1_.refs_4_, ...), custom_call_target="tpu_custom_call" | custom-call | flops 1610000000 | bytes 1000 | tf_op jit(solution)/shard_map/qkv_grad/pallas_call | solution.py:846
  292.6 2.8 collective-permute-done.38
  295.4 2.6 add_convert_fusion.1
  299.7 2.1 slice.84
  305.0 20.5 %self_back.5 = (bf16[1664,256]{1,0:T(8,128)(2,1)S(1)}, bf16[1664,256]{1,0:T(8,128)(2,1)S(1)}, bf16[1664,256]{1,0:T(8,128)(2,1)S(1)}) custom-call(s32[1]{0:T(128)} %dynamic_slice.129.limit_ref, bf16[1664,256]{1,0:T(8,128)(2,1)S(1)} %copy-done.63, bf16[1664,256]{1,0:T(8,128)(2,1)S(1)} %copy-done.65, bf16[1664,256]{1,0:T(8,128)(2,1)S(1)} %copy-done.67, ...), custom_call_target="tpu_custom_call" | custom-call | flops 4508000256 | bytes 1000 | tf_op jit(solution)/shard_map/self_back/pallas_call | solution.py:606
  329.4 2.6 collective-permute-start.39
  333.1 5.1 outputs_grad.2
  338.1 4.0 query_grad.3
  342.1 9.4 %collective-permute-done.44 = bf16[2,64,256]{2,1,0:T(8,128)(2,1)S(1)} collective-permute-done((bf16[2,64,256]{2,1,0:T(8,128)(2,1)S(1)}, bf16[2,64,256]{2,1,0:T(8,128)(2,1)S(1)}, u32[]{:S(2)}, u32[]{:S(2)}) %collective-permute-start.44) | collective-permute-done | bytes 65568 | tf_op jit(solution)/shard_map/ppermute | solution.py:1096
  354.8 2.1 dynamic-slice_convert_fusion
  364.1 7.1 %first_back.2 = bf16[832,1024]{1,0:T(8,128)(2,1)} custom-call(s32[3]{0:T(128)S(1)} %add_add_fusion.1.place_ref, bf16[1664,256]{1,0:T(8,128)(2,1)S(1)} %get-tuple-element.382.refs_0_, bf16[1664,256]{1,0:T(8,128)(2,1)S(1)} %get-tuple-element.360.refs_1_, bf16[1664,256]{1,0:T(8,128)(2,1)S(1)} %get-tuple-element.361.refs_2_, ...), custom_call_target="tpu_custom_call" | custom-call | flops 1149539968 | bytes 1000 | tf_op jit(solution)/shard_map/first_back/pallas_call | solution.py:1026
  371.2 5.9 %qkv_grad.3 = bf16[3072,256]{1,0:T(8,128)(2,1)S(1)} custom-call(s32[3]{0:T(128)S(1)} %copy-done.43, bf16[1664,1024]{1,0:T(8,128)(2,1)} %copy-done.8, bf16[1664,256]{1,0:T(8,128)(2,1)S(1)} %get-tuple-element.382.refs_0_, bf16[1664,256]{1,0:T(8,128)(2,1)S(1)} %get-tuple-element.360.refs_1_, bf16[1664,256]{1,0:T(8,128)(2,1)S(1)} %get-tuple-element.361.refs_2_), custom_call_target="tpu_custom_call" | custom-call | flops 1610000000 | bytes 1000 | tf_op jit(solution)/shard_map/qkv_grad/pallas_call | solution.py:846
  377.3 2.7 add_convert_fusion.3
  380.5 2.0 add_convert_fusion.6
  382.5 2.6 collective-permute-start.74
  387.4 16.8 %collective-permute-done.45 = bf16[256,1024]{1,0:T(8,128)(2,1)S(1)} collective-permute-done((bf16[256,1024]{1,0:T(8,128)(2,1)S(1)}, bf16[256,1024]{1,0:T(8,128)(2,1)S(1)}, u32[]{:S(2)}, u32[]{:S(2)}) %collective-permute-start.45) | collective-permute-done | bytes 524320 | tf_op jit(solution)/shard_map/ppermute | solution.py:1099
  406.5 5.0 outputs_grad.3
  414.2 2.1 collective-permute-start.50
  417.6 8.3 %collective-permute-done.52 = bf16[1536,256]{1,0:T(8,128)(2,1)} collective-permute-done((bf16[1536,256]{1,0:T(8,128)(2,1)}, bf16[1536,256]{1,0:T(8,128)(2,1)}, u32[]{:S(2)}, u32[]{:S(2)}) %collective-permute-start.52) | collective-permute-done | bytes 786464 | tf_op jit(solution)/shard_map/ppermute | solution.py:1099
  429.6 6.0 %first_back.3.ym_ref = f32[832,1024]{1,0:T(8,128)S(1)} custom-call(s32[3]{0:T(128)S(1)} %copy-done.43, bf16[1664,256]{1,0:T(8,128)(2,1)S(1)} %get-tuple-element.382.refs_0_, bf16[1664,256]{1,0:T(8,128)(2,1)S(1)} %get-tuple-element.360.refs_1_, bf16[1664,256]{1,0:T(8,128)(2,1)S(1)} %get-tuple-element.361.refs_2_, ...), custom_call_target="tpu_custom_call" | custom-call | flops 1149539968 | bytes 1000 | tf_op jit(solution)/shard_map/first_back/pallas_call | solution.py:1026
  435.9 4.8 collective-permute-done.66
  443.9 5.9 %frames_back.1 = (bf16[832,1024]{1,0:T(8,128)(2,1)}, f32[8,1024]{1,0:T(8,128)S(1)}) custom-call(s32[3]{0:T(128)S(1)} %copy-done.43, f32[832,1024]{1,0:T(8,128)S(1)} %first_back.3.ym_ref, bf16[832,1024]{1,0:T(8,128)(2,1)} %collective-permute-done.54.yr_ref, f32[832,1024]{1,0:T(8,128)S(1)} %copy-done.21, bf16[832,1024]{1,0:T(8,128)(2,1)S(1)} %copy-done.30, ...), custom_call_target="tpu_custom_call" | custom-call | flops 1381379968 | bytes 1000 | tf_op jit(solution)/shard_map/frames_back/pallas_call | solution.py:1061
  451.1 2.5 collective-permute-start.67
  453.6 15.4 %collective-permute-done.62 = bf16[768,256]{1,0:T(8,128)(2,1)S(1)} collective-permute-done((bf16[768,256]{1,0:T(8,128)(2,1)S(1)}, bf16[768,256]{1,0:T(8,128)(2,1)S(1)}, u32[]{:S(2)}, u32[]{:S(2)}) %collective-permute-start.62) | collective-permute-done | bytes 393248 | tf_op jit(solution)/shard_map/ppermute | solution.py:1099
  470.1 2.8 collective-permute-done.58
  475.1 19.8 %collective-permute-done.59 = f32[8,1024]{1,0:T(8,128)S(1)} collective-permute-done((f32[8,1024]{1,0:T(8,128)S(1)}, f32[8,1024]{1,0:T(8,128)S(1)}, u32[]{:S(2)}, u32[]{:S(2)}) %collective-permute-start.59) | collective-permute-done | bytes 32800 | tf_op jit(solution)/shard_map/ppermute | solution.py:1099
  496.1 3.8 collective-permute-done.56
  501.0 3.4 collective-permute-done.60
  504.5 3.0 fusion
  507.5 2.9 collective-permute-start.61
  510.4 6.7 %collective-permute-done.68 = bf16[128,1024]{1,0:T(8,128)(2,1)S(1)} collective-permute-done((bf16[128,1024]{1,0:T(8,128)(2,1)S(1)}, bf16[128,1024]{1,0:T(8,128)(2,1)S(1)}, u32[]{:S(2)}, u32[]{:S(2)}) %collective-permute-start.68) | collective-permute-done | bytes 262176 | tf_op jit(solution)/shard_map/ppermute | solution.py:1099
  517.2 9.0 %collective-permute-done.63 = bf16[768,256]{1,0:T(8,128)(2,1)S(1)} collective-permute-done((bf16[768,256]{1,0:T(8,128)(2,1)S(1)}, bf16[768,256]{1,0:T(8,128)(2,1)S(1)}, u32[]{:S(2)}, u32[]{:S(2)}) %collective-permute-start.63) | collective-permute-done | bytes 393248 | tf_op jit(solution)/shard_map/ppermute | solution.py:1099
  527.0 3.8 add_convert_fusion
  535.7 2.9 collective-permute-done.64
  540.1 2.9 fusion.1
  543.0 6.3 %collective-permute-done.70 = bf16[256,1024]{1,0:T(8,128)(2,1)S(1)} collective-permute-done((bf16[256,1024]{1,0:T(8,128)(2,1)S(1)}, bf16[256,1024]{1,0:T(8,128)(2,1)S(1)}, u32[]{:S(2)}, u32[]{:S(2)}) %collective-permute-start.70) | collective-permute-done | bytes 524320 | tf_op jit(solution)/shard_map/ppermute | solution.py:1099
  551.2 6.5 %collective-permute-done.73 = bf16[1536,256]{1,0:T(8,128)(2,1)S(1)} collective-permute-done((bf16[1536,256]{1,0:T(8,128)(2,1)S(1)}, bf16[1536,256]{1,0:T(8,128)(2,1)S(1)}, u32[]{:S(2)}, u32[]{:S(2)}) %collective-permute-start.73) | collective-permute-done | bytes 786464 | tf_op jit(solution)/shard_map/ppermute | solution.py:1099
  (433 shorter events, 122.6 us)
Async XLA Ops:
  3.2 21.0 %collective-permute-start.1 = (bf16[3,1024,128]{2,1,0:T(8,128)(2,1)}, bf16[3,1024,128]{2,1,0:T(8,128)(2,1)}, u32[]{:S(2)}, u32[]{:S(2)}) collective-permute-start(bf16[3,1024,128]{2,1,0:T(8,128)(2,1)} %constant_dynamic-slice_fusion.14), channel_id=1, source_target_pairs={{0,2},{2,0},{1,3},{3,1},{4,6},{6,4},{5,7},{7,5},{8,10},{10,8},{9,1... | collective-permute-start | bytes 2359304 | tf_op jit(solution)/shard_map/ppermute | solution.py:1096
  25.0 9.5 %collective-permute-start.2 = (bf16[128,1024]{1,0:T(8,128)(2,1)}, bf16[128,1024]{1,0:T(8,128)(2,1)}, u32[]{:S(2)}, u32[]{:S(2)}) collective-permute-start(bf16[128,1024]{1,0:T(8,128)(2,1)} %constant_dynamic-slice_fusion.13), channel_id=1, source_target_pairs={{0,2},{2,0},{1,3},{3,1},{4,6},{6,4},{5,7},{7,5},{8,10},{10,8},{9,1... | collective-permute-start | bytes 786440 | tf_op jit(solution)/shard_map/ppermute | solution.py:1096
  27.5 12.7 %collective-permute-start.3 = (bf16[1024,128]{1,0:T(8,128)(2,1)}, bf16[1024,128]{1,0:T(8,128)(2,1)}, u32[]{:S(2)}, u32[]{:S(2)}) collective-permute-start(bf16[1024,128]{1,0:T(8,128)(2,1)} %constant_dynamic-slice_fusion.12), channel_id=1, source_target_pairs={{0,2},{2,0},{1,3},{3,1},{4,6},{6,4},{5,7},{7,5},{8,10},{10,8},{9,1... | collective-permute-start | bytes 786440 | tf_op jit(solution)/shard_map/ppermute | solution.py:1096
  28.9 33.0 %collective-permute-start.5 = (bf16[256,1024]{1,0:T(8,128)(2,1)}, bf16[256,1024]{1,0:T(8,128)(2,1)}, u32[]{:S(2)}, u32[]{:S(2)}) collective-permute-start(bf16[256,1024]{1,0:T(8,128)(2,1)} %refs_2_), channel_id=1, source_target_pairs={{0,1},{1,0},{2,3},{3,2},{4,5},{5,4},{6,7},{7,6},{8,9},{9,8},{10,11... | collective-permute-start | bytes 1572872 | tf_op jit(solution)/shard_map/ppermute | solution.py:1093
  29.0 32.9 %collective-permute-start.6 = (bf16[1024,256]{1,0:T(8,128)(2,1)}, bf16[1024,256]{1,0:T(8,128)(2,1)S(1)}, u32[]{:S(2)}, u32[]{:S(2)}) collective-permute-start(bf16[1024,256]{1,0:T(8,128)(2,1)} %refs_0_.2), channel_id=1, source_target_pairs={{0,1},{1,0},{2,3},{3,2},{4,5},{5,4},{6,7},{7,6},{8,9},{9,8},{10,11... | collective-permute-start | bytes 1572872 | tf_op jit(solution)/shard_map/ppermute | solution.py:1093
  29.5 32.4 %collective-permute-start.7 = (bf16[256,1024]{1,0:T(8,128)(2,1)}, bf16[256,1024]{1,0:T(8,128)(2,1)}, u32[]{:S(2)}, u32[]{:S(2)}) collective-permute-start(bf16[256,1024]{1,0:T(8,128)(2,1)} %refs_6_.1), channel_id=1, source_target_pairs={{0,1},{1,0},{2,3},{3,2},{4,5},{5,4},{6,7},{7,6},{8,9},{9,8},{10,11... | collective-permute-start | bytes 1572872 | tf_op jit(solution)/shard_map/ppermute | solution.py:1093
  34.5 25.8 %collective-permute-start.4 = (bf16[128,1024]{1,0:T(8,128)(2,1)S(1)}, bf16[128,1024]{1,0:T(8,128)(2,1)}, u32[]{:S(2)}, u32[]{:S(2)}) collective-permute-start(bf16[128,1024]{1,0:T(8,128)(2,1)S(1)} %constant_dynamic-slice_fusion.11), channel_id=1, source_target_pairs={{0,2},{2,0},{1,3},{3,1},{4,6},{6,4},{5,7},{7,5},{8,10},{10,8},{9,1... | collective-permute-start | bytes 786440 | tf_op jit(solution)/shard_map/ppermute | solution.py:1096
  40.1 32.3 %collective-permute-start.8 = (bf16[3,1024,128]{2,1,0:T(8,128)(2,1)}, bf16[3,1024,128]{2,1,0:T(8,128)(2,1)S(1)}, u32[]{:S(2)}, u32[]{:S(2)}) collective-permute-start(bf16[3,1024,128]{2,1,0:T(8,128)(2,1)} %collective-permute-done.1.weight_ref.refs_10_), channel_id=1, source_target_pairs={{0,8},{4,12},{8,0},{12,4},{16,24},{20,28},{24,16},{28,20},{1,9},{5... | collective-permute-start | bytes 2359304 | tf_op jit(solution)/shard_map/ppermute | solution.py:1099
  60.3 12.0 %collective-permute-start.9 = (bf16[2,64,256]{2,1,0:T(8,128)(2,1)S(1)}, bf16[2,64,256]{2,1,0:T(8,128)(2,1)S(1)}, u32[]{:S(2)}, u32[]{:S(2)}) collective-permute-start(bf16[2,64,256]{2,1,0:T(8,128)(2,1)S(1)} %get-tuple-element.427), channel_id=1, source_target_pairs={{0,2},{2,0},{1,3},{3,1},{4,6},{6,4},{5,7},{7,5},{8,10},{10,8},{9,1... | collective-permute-start | bytes 196616 | tf_op jit(solution)/shard_map/ppermute | solution.py:1096
  62.0 12.2 %collective-permute-start.10 = (bf16[832,256]{1,0:T(8,128)(2,1)S(1)}, bf16[832,256]{1,0:T(8,128)(2,1)}, u32[]{:S(2)}, u32[]{:S(2)}) collective-permute-start(bf16[832,256]{1,0:T(8,128)(2,1)S(1)} %constant_dynamic-slice_fusion.10), channel_id=1, source_target_pairs={{0,1},{1,0},{2,3},{3,2},{4,5},{5,4},{6,7},{7,6},{8,9},{9,8},{10,11... | collective-permute-start | bytes 1277960 | tf_op jit(solution)/shard_map/ppermute | solution.py:1093
  62.2 28.7 %collective-permute-start.14 = (bf16[1024,512]{1,0:T(8,128)(2,1)S(1)}, bf16[1024,512]{1,0:T(8,128)(2,1)}, u32[]{:S(2)}, u32[]{:S(2)}) collective-permute-start(bf16[1024,512]{1,0:T(8,128)(2,1)S(1)} %constant_dynamic-slice_fusion.9), channel_id=1, source_target_pairs={{0,2},{2,0},{1,3},{3,1},{4,6},{6,4},{5,7},{7,5},{8,10},{10,8},{9,1... | collective-permute-start | bytes 3145736 | tf_op jit(solution)/shard_map/ppermute | solution.py:1096
  62.8 17.8 %collective-permute-start.11 = (bf16[128,1024]{1,0:T(8,128)(2,1)}, bf16[128,1024]{1,0:T(8,128)(2,1)S(1)}, u32[]{:S(2)}, u32[]{:S(2)}) collective-permute-start(bf16[128,1024]{1,0:T(8,128)(2,1)} %collective-permute-done.2.refs_7_.refs_0_), channel_id=1, source_target_pairs={{0,8},{4,12},{8,0},{12,4},{16,24},{20,28},{24,16},{28,20},{1,9},{5... | collective-permute-start | bytes 786440 | tf_op jit(solution)/shard_map/ppermute | solution.py:1099
  72.3 21.8 %collective-permute-start.18 = (bf16[128,1024]{1,0:T(8,128)(2,1)}, bf16[128,1024]{1,0:T(8,128)(2,1)}, u32[]{:S(2)}, u32[]{:S(2)}) collective-permute-start(bf16[128,1024]{1,0:T(8,128)(2,1)} %collective-permute-done.2.refs_7_.refs_0_), channel_id=1, source_target_pairs={{0,1},{1,0},{2,3},{3,2},{4,5},{5,4},{6,7},{7,6},{8,9},{9,8},{10,11... | collective-permute-start | bytes 786440 | tf_op jit(solution)/shard_map/ppermute | solution.py:1093
  72.4 9.4 %collective-permute-start.12 = (bf16[1024,128]{1,0:T(8,128)(2,1)}, bf16[1024,128]{1,0:T(8,128)(2,1)S(1)}, u32[]{:S(2)}, u32[]{:S(2)}) collective-permute-start(bf16[1024,128]{1,0:T(8,128)(2,1)} %collective-permute-done.3.refs_13_.refs_1_), channel_id=1, source_target_pairs={{0,4},{4,0},{8,12},{12,8},{16,20},{20,16},{24,28},{28,24},{1,5},{5... | collective-permute-start | bytes 786440 | tf_op jit(solution)/shard_map/ppermute | solution.py:1099
  74.2 16.0 %collective-permute-start.13 = (bf16[128,1024]{1,0:T(8,128)(2,1)}, bf16[128,1024]{1,0:T(8,128)(2,1)S(1)}, u32[]{:S(2)}, u32[]{:S(2)}) collective-permute-start(bf16[128,1024]{1,0:T(8,128)(2,1)} %collective-permute-done.4.refs_19_.refs_7_), channel_id=1, source_target_pairs={{0,4},{4,0},{8,12},{12,8},{16,20},{20,16},{24,28},{28,24},{1,5},{5... | collective-permute-start | bytes 786440 | tf_op jit(solution)/shard_map/ppermute | solution.py:1099
  80.5 10.2 %collective-permute-start.15 = (bf16[2,2,64,256]{3,2,1,0:T(8,128)(2,1)S(1)}, bf16[2,2,64,256]{3,2,1,0:T(8,128)(2,1)S(1)}, u32[]{:S(2)}, u32[]{:S(2)}) collective-permute-start(bf16[2,2,64,256]{3,2,1,0:T(8,128)(2,1)S(1)} %pad_maximum_fusion.6), channel_id=1, source_target_pairs={{0,1},{1,0},{2,3},{3,2},{4,5},{5,4},{6,7},{7,6},{8,9},{9,8},{10,11... | collective-permute-start | bytes 393224 | tf_op jit(solution)/shard_map/ppermute | solution.py:1093
  92.4 27.3 %collective-permute-start.24 = (bf16[1024,512]{1,0:T(8,128)(2,1)}, bf16[1024,512]{1,0:T(8,128)(2,1)S(1)}, u32[]{:S(2)}, u32[]{:S(2)}) collective-permute-start(bf16[1024,512]{1,0:T(8,128)(2,1)} %collective-permute-done.14.refs_0_), channel_id=1, source_target_pairs={{0,4},{4,0},{8,12},{12,8},{16,20},{20,16},{24,28},{28,24},{1,5},{5... | collective-permute-start | bytes 3145736 | tf_op jit(solution)/shard_map/ppermute | solution.py:1099
  94.2 25.6 %collective-permute-start.25 = (bf16[512,1024]{1,0:T(8,128)(2,1)}, bf16[512,1024]{1,0:T(8,128)(2,1)S(1)}, u32[]{:S(2)}, u32[]{:S(2)}) collective-permute-start(bf16[512,1024]{1,0:T(8,128)(2,1)} %constant_dynamic-slice_fusion.8), channel_id=1, source_target_pairs={{0,2},{2,0},{1,3},{3,1},{4,6},{6,4},{5,7},{7,5},{8,10},{10,8},{9,1... | collective-permute-start | bytes 3145736 | tf_op jit(solution)/shard_map/ppermute | solution.py:1096
  120.7 13.2 %collective-permute-start.26 = (bf16[832,1024]{1,0:T(8,128)(2,1)}, bf16[832,1024]{1,0:T(8,128)(2,1)S(1)}, u32[]{:S(2)}, u32[]{:S(2)}) collective-permute-start(bf16[832,1024]{1,0:T(8,128)(2,1)} %get-tuple-element.252.h_ref.mine_ref), channel_id=1, source_target_pairs={{0,1},{1,0},{2,3},{3,2},{4,5},{5,4},{6,7},{7,6},{8,9},{9,8},{10,11... | collective-permute-start | bytes 5111816 | tf_op jit(solution)/shard_map/ppermute | solution.py:1093
  120.9 13.0 %collective-permute-start.27 = (bf16[832,1024]{1,0:T(8,128)(2,1)S(1)}, bf16[832,1024]{1,0:T(8,128)(2,1)S(1)}, u32[]{:S(2)}, u32[]{:S(2)}) collective-permute-start(bf16[832,1024]{1,0:T(8,128)(2,1)S(1)} %broadcast_select_fusion.d_ref.mine_ref), channel_id=1, source_target_pairs={{0,1},{1,0},{2,3},{3,2},{4,5},{5,4},{6,7},{7,6},{8,9},{9,8},{10,11... | collective-permute-start | bytes 5111816 | tf_op jit(solution)/shard_map/ppermute | solution.py:1093
  121.2 26.6 %collective-permute-start.28 = (bf16[512,1024]{1,0:T(8,128)(2,1)}, bf16[512,1024]{1,0:T(8,128)(2,1)}, u32[]{:S(2)}, u32[]{:S(2)}) collective-permute-start(bf16[512,1024]{1,0:T(8,128)(2,1)} %copy-done.83), channel_id=1, source_target_pairs={{0,4},{4,0},{8,12},{12,8},{16,20},{20,16},{24,28},{28,24},{1,5},{5... | collective-permute-start | bytes 3145736 | tf_op jit(solution)/shard_map/ppermute | solution.py:1099
  161.4 29.7 %collective-permute-start.29 = (bf16[832,1024]{1,0:T(8,128)(2,1)}, bf16[832,1024]{1,0:T(8,128)(2,1)S(1)}, u32[]{:S(2)}, u32[]{:S(2)}) collective-permute-start(bf16[832,1024]{1,0:T(8,128)(2,1)} %get-tuple-element.264), channel_id=1, source_target_pairs={{0,1},{1,0},{2,3},{3,2},{4,5},{5,4},{6,7},{7,6},{8,9},{9,8},{10,11... | collective-permute-start | bytes 5111816 | tf_op jit(solution)/shard_map/ppermute | solution.py:1093
  182.6 48.4 %collective-permute-start.31 = (bf16[1024,1024]{1,0:T(8,128)(2,1)}, bf16[1024,1024]{1,0:T(8,128)(2,1)}, u32[]{:S(2)}, u32[]{:S(2)}) collective-permute-start(bf16[1024,1024]{1,0:T(8,128)(2,1)} %up_grad.2), channel_id=1, source_target_pairs={{0,2},{2,0},{1,3},{3,1},{4,6},{6,4},{5,7},{7,5},{8,10},{10,8},{9,1... | collective-permute-start | bytes 6291464 | tf_op jit(solution)/shard_map/ppermute | solution.py:1096
  215.5 15.4 %collective-permute-start.32 = (bf16[832,1024]{1,0:T(8,128)(2,1)}, bf16[832,1024]{1,0:T(8,128)(2,1)S(1)}, u32[]{:S(2)}, u32[]{:S(2)}) collective-permute-start(bf16[832,1024]{1,0:T(8,128)(2,1)} %get-tuple-element.297.mine_ref.refs_2_.refs_1_), channel_id=1, source_target_pairs={{0,1},{1,0},{2,3},{3,2},{4,5},{5,4},{6,7},{7,6},{8,9},{9,8},{10,11... | collective-permute-start | bytes 5111816 | tf_op jit(solution)/shard_map/ppermute | solution.py:1093
  215.8 42.7 %collective-permute-start.35 = (bf16[832,1024]{1,0:T(8,128)(2,1)}, bf16[832,1024]{1,0:T(8,128)(2,1)}, u32[]{:S(2)}, u32[]{:S(2)}) collective-permute-start(bf16[832,1024]{1,0:T(8,128)(2,1)} %get-tuple-element.300.mine_ref), channel_id=1, source_target_pairs={{0,1},{1,0},{2,3},{3,2},{4,5},{5,4},{6,7},{7,6},{8,9},{9,8},{10,11... | collective-permute-start | bytes 5111816 | tf_op jit(solution)/shard_map/ppermute | solution.py:1093
  237.2 21.4 %collective-permute-start.34 = (bf16[832,512]{1,0:T(8,128)(2,1)}, bf16[832,512]{1,0:T(8,128)(2,1)}, u32[]{:S(2)}, u32[]{:S(2)}) collective-permute-start(bf16[832,512]{1,0:T(8,128)(2,1)} %slice.78), channel_id=1, source_target_pairs={{0,1},{1,0},{2,3},{3,2},{4,5},{5,4},{6,7},{7,6},{8,9},{9,8},{10,11... | collective-permute-start | bytes 2555912 | tf_op jit(solution)/shard_map/ppermute | solution.py:1093
  238.4 20.2 %collective-permute-start.36 = (f32[2,2,64,256]{3,2,0,1:T(8,128)S(1)}, f32[2,2,64,256]{3,2,0,1:T(8,128)S(1)}, u32[]{:S(2)}, u32[]{:S(2)}) collective-permute-start(f32[2,2,64,256]{3,2,0,1:T(8,128)S(1)} %get-tuple-element.419), channel_id=1, source_target_pairs={{0,1},{1,0},{2,3},{3,2},{4,5},{5,4},{6,7},{7,6},{8,9},{9,8},{10,11... | collective-permute-start | bytes 786440 | tf_op jit(solution)/shard_map/ppermute | solution.py:1093
  246.6 27.5 %collective-permute-start.33 = (bf16[512,1024]{1,0:T(8,128)(2,1)}, bf16[512,1024]{1,0:T(8,128)(2,1)S(1)}, u32[]{:S(2)}, u32[]{:S(2)}) collective-permute-start(bf16[512,1024]{1,0:T(8,128)(2,1)} %get-tuple-element.407), channel_id=1, source_target_pairs={{0,4},{4,0},{8,12},{12,8},{16,20},{20,16},{24,28},{28,24},{1,5},{5... | collective-permute-start | bytes 3145736 | tf_op jit(solution)/shard_map/ppermute | solution.py:1099
  248.1 47.3 %collective-permute-start.38 = (bf16[1024,1024]{1,0:T(8,128)(2,1)S(1)}, bf16[1024,1024]{1,0:T(8,128)(2,1)S(1)}, u32[]{:S(2)}, u32[]{:S(2)}) collective-permute-start(bf16[1024,1024]{1,0:T(8,128)(2,1)S(1)} %copy-done.25), channel_id=1, source_target_pairs={{0,2},{2,0},{1,3},{3,1},{4,6},{6,4},{5,7},{7,5},{8,10},{10,8},{9,1... | collective-permute-start | bytes 6291464 | tf_op jit(solution)/shard_map/ppermute | solution.py:1096
  258.5 73.5 %collective-permute-start.40 = (bf16[832,1024]{1,0:T(8,128)(2,1)}, bf16[832,1024]{1,0:T(8,128)(2,1)}, u32[]{:S(2)}, u32[]{:S(2)}) collective-permute-start(bf16[832,1024]{1,0:T(8,128)(2,1)} %get-tuple-element.375.refs_6_.refs_5_), channel_id=1, source_target_pairs={{0,1},{1,0},{2,3},{3,2},{4,5},{5,4},{6,7},{7,6},{8,9},{9,8},{10,11... | collective-permute-start | bytes 5111816 | tf_op jit(solution)/shard_map/ppermute | solution.py:1093
  283.7 18.6 %collective-permute-start.37 = (bf16[256,1024]{1,0:T(8,128)(2,1)}, bf16[256,1024]{1,0:T(8,128)(2,1)}, u32[]{:S(2)}, u32[]{:S(2)}) collective-permute-start(bf16[256,1024]{1,0:T(8,128)(2,1)} %dynamic-slice_convert_fusion.1), channel_id=1, source_target_pairs={{0,8},{4,12},{8,0},{12,4},{16,24},{20,28},{24,16},{28,20},{1,9},{5... | collective-permute-start | bytes 1572872 | tf_op jit(solution)/shard_map/ppermute | solution.py:1099
  297.9 27.6 %collective-permute-start.42 = (bf16[512,1024]{1,0:T(8,128)(2,1)}, bf16[512,1024]{1,0:T(8,128)(2,1)}, u32[]{:S(2)}, u32[]{:S(2)}) collective-permute-start(bf16[512,1024]{1,0:T(8,128)(2,1)} %get-tuple-element.404), channel_id=1, source_target_pairs={{0,4},{4,0},{8,12},{12,8},{16,20},{20,16},{24,28},{28,24},{1,5},{5... | collective-permute-start | bytes 3145736 | tf_op jit(solution)/shard_map/ppermute | solution.py:1099
  301.8 27.6 %collective-permute-start.41 = (bf16[832,512]{1,0:T(8,128)(2,1)}, bf16[832,512]{1,0:T(8,128)(2,1)S(1)}, u32[]{:S(2)}, u32[]{:S(2)}) collective-permute-start(bf16[832,512]{1,0:T(8,128)(2,1)} %slice.84), channel_id=1, source_target_pairs={{0,1},{1,0},{2,3},{3,2},{4,5},{5,4},{6,7},{7,6},{8,9},{9,8},{10,11... | collective-permute-start | bytes 2555912 | tf_op jit(solution)/shard_map/ppermute | solution.py:1093
  301.8 205.6 %collective-permute-start.30 = (bf16[832,1024]{1,0:T(8,128)(2,1)}, bf16[832,1024]{1,0:T(8,128)(2,1)}, u32[]{:S(2)}, u32[]{:S(2)}) collective-permute-start(bf16[832,1024]{1,0:T(8,128)(2,1)} %get-tuple-element.277), channel_id=1, source_target_pairs={{0,1},{1,0},{2,3},{3,2},{4,5},{5,4},{6,7},{7,6},{8,9},{9,8},{10,11... | collective-permute-start | bytes 5111816 | tf_op jit(solution)/shard_map/ppermute | solution.py:1093
  302.3 74.9 %collective-permute-start.48 = (bf16[3072,256]{1,0:T(8,128)(2,1)}, bf16[3072,256]{1,0:T(8,128)(2,1)}, u32[]{:S(2)}, u32[]{:S(2)}) collective-permute-start(bf16[3072,256]{1,0:T(8,128)(2,1)} %qkv_grad.2), channel_id=1, source_target_pairs={{0,2},{2,0},{1,3},{3,1},{4,6},{6,4},{5,7},{7,5},{8,10},{10,8},{9,1... | collective-permute-start | bytes 4718600 | tf_op jit(solution)/shard_map/ppermute | solution.py:1096
  325.5 26.0 %collective-permute-start.43 = (bf16[1024,256]{1,0:T(8,128)(2,1)}, bf16[1024,256]{1,0:T(8,128)(2,1)}, u32[]{:S(2)}, u32[]{:S(2)}) collective-permute-start(bf16[1024,256]{1,0:T(8,128)(2,1)} %query_grad.2), channel_id=1, source_target_pairs={{0,2},{2,0},{1,3},{3,1},{4,6},{6,4},{5,7},{7,5},{8,10},{10,8},{9,1... | collective-permute-start | bytes 1572872 | tf_op jit(solution)/shard_map/ppermute | solution.py:1096
  329.4 32.0 %collective-permute-start.39 = (bf16[256,1024]{1,0:T(8,128)(2,1)S(1)}, bf16[256,1024]{1,0:T(8,128)(2,1)}, u32[]{:S(2)}, u32[]{:S(2)}) collective-permute-start(bf16[256,1024]{1,0:T(8,128)(2,1)S(1)} %add_convert_fusion.9), channel_id=1, source_target_pairs={{0,16},{4,20},{8,24},{12,28},{16,0},{20,4},{24,8},{28,12},{1,17},{... | collective-permute-start | bytes 1572872 | tf_op jit(solution)/shard_map/ppermute | solution.py:1099
  332.0 19.5 %collective-permute-start.44 = (bf16[2,64,256]{2,1,0:T(8,128)(2,1)S(1)}, bf16[2,64,256]{2,1,0:T(8,128)(2,1)S(1)}, u32[]{:S(2)}, u32[]{:S(2)}) collective-permute-start(bf16[2,64,256]{2,1,0:T(8,128)(2,1)S(1)} %maximum_select_fusion.12), channel_id=1, source_target_pairs={{0,2},{2,0},{1,3},{3,1},{4,6},{6,4},{5,7},{7,5},{8,10},{10,8},{9,1... | collective-permute-start | bytes 196616 | tf_op jit(solution)/shard_map/ppermute | solution.py:1096
  352.5 59.0 %collective-permute-start.53 = (bf16[512,1024]{1,0:T(8,128)(2,1)S(1)}, bf16[512,1024]{1,0:T(8,128)(2,1)}, u32[]{:S(2)}, u32[]{:S(2)}) collective-permute-start(bf16[512,1024]{1,0:T(8,128)(2,1)S(1)} %outputs_grad.2), channel_id=1, source_target_pairs={{0,2},{2,0},{1,3},{3,1},{4,6},{6,4},{5,7},{7,5},{8,10},{10,8},{9,1... | collective-permute-start | bytes 3145736 | tf_op jit(solution)/shard_map/ppermute | solution.py:1096
  356.9 23.2 %collective-permute-start.47 = (bf16[256,1024]{1,0:T(8,128)(2,1)}, bf16[256,1024]{1,0:T(8,128)(2,1)}, u32[]{:S(2)}, u32[]{:S(2)}) collective-permute-start(bf16[256,1024]{1,0:T(8,128)(2,1)} %dynamic-slice_convert_fusion), channel_id=1, source_target_pairs={{0,8},{4,12},{8,0},{12,4},{16,24},{20,28},{24,16},{28,20},{1,9},{5... | collective-permute-start | bytes 1572872 | tf_op jit(solution)/shard_map/ppermute | solution.py:1099
  361.4 21.2 %collective-permute-start.46 = (bf16[1536,256]{1,0:T(8,128)(2,1)}, bf16[1536,256]{1,0:T(8,128)(2,1)}, u32[]{:S(2)}, u32[]{:S(2)}) collective-permute-start(bf16[1536,256]{1,0:T(8,128)(2,1)} %get-tuple-element.414), channel_id=1, source_target_pairs={{0,4},{4,0},{8,12},{12,8},{16,20},{20,16},{24,28},{28,24},{1,5},{5... | collective-permute-start | bytes 2359304 | tf_op jit(solution)/shard_map/ppermute | solution.py:1099
  377.2 65.7 %collective-permute-start.54 = (bf16[832,1024]{1,0:T(8,128)(2,1)}, bf16[832,1024]{1,0:T(8,128)(2,1)}, u32[]{:S(2)}, u32[]{:S(2)}) collective-permute-start(bf16[832,1024]{1,0:T(8,128)(2,1)} %first_back.2), channel_id=1, source_target_pairs={{0,1},{1,0},{2,3},{3,2},{4,5},{5,4},{6,7},{7,6},{8,9},{9,8},{10,11... | collective-permute-start | bytes 5111816 | tf_op jit(solution)/shard_map/ppermute | solution.py:1093
  380.0 24.2 %collective-permute-start.45 = (bf16[256,1024]{1,0:T(8,128)(2,1)S(1)}, bf16[256,1024]{1,0:T(8,128)(2,1)S(1)}, u32[]{:S(2)}, u32[]{:S(2)}) collective-permute-start(bf16[256,1024]{1,0:T(8,128)(2,1)S(1)} %add_convert_fusion.7), channel_id=1, source_target_pairs={{0,8},{4,12},{8,0},{12,4},{16,24},{20,28},{24,16},{28,20},{1,9},{5... | collective-permute-start | bytes 1572872 | tf_op jit(solution)/shard_map/ppermute | solution.py:1099
  382.5 31.6 %collective-permute-start.74 = (bf16[256,1024]{1,0:T(8,128)(2,1)}, bf16[256,1024]{1,0:T(8,128)(2,1)}, u32[]{:S(2)}, u32[]{:S(2)}) collective-permute-start(bf16[256,1024]{1,0:T(8,128)(2,1)} %add_convert_fusion.6), channel_id=1, source_target_pairs={{0,16},{4,20},{8,24},{12,28},{16,0},{20,4},{24,8},{28,12},{1,17},{... | collective-permute-start | bytes 1572872 | tf_op jit(solution)/shard_map/ppermute | solution.py:1099
  404.2 21.7 %collective-permute-start.52 = (bf16[1536,256]{1,0:T(8,128)(2,1)}, bf16[1536,256]{1,0:T(8,128)(2,1)}, u32[]{:S(2)}, u32[]{:S(2)}) collective-permute-start(bf16[1536,256]{1,0:T(8,128)(2,1)} %get-tuple-element.408), channel_id=1, source_target_pairs={{0,8},{4,12},{8,0},{12,4},{16,24},{20,28},{24,16},{28,20},{1,9},{5... | collective-permute-start | bytes 2359304 | tf_op jit(solution)/shard_map/ppermute | solution.py:1099
  411.5 16.4 %collective-permute-start.51 = (f32[64,1024]{1,0:T(8,128)}, f32[64,1024]{1,0:T(8,128)S(1)}, u32[]{:S(2)}, u32[]{:S(2)}) collective-permute-start(f32[64,1024]{1,0:T(8,128)} %get-tuple-element.416), channel_id=1, source_target_pairs={{0,2},{2,0},{1,3},{3,1},{4,6},{6,4},{5,7},{7,5},{8,10},{10,8},{9,1... | collective-permute-start | bytes 786440 | tf_op jit(solution)/shard_map/ppermute | solution.py:1096
  414.2 21.5 %collective-permute-start.50 = (bf16[768,256]{1,0:T(8,128)(2,1)S(1)}, bf16[768,256]{1,0:T(8,128)(2,1)S(1)}, u32[]{:S(2)}, u32[]{:S(2)}) collective-permute-start(bf16[768,256]{1,0:T(8,128)(2,1)S(1)} %copy-done.89), channel_id=1, source_target_pairs={{0,8},{4,12},{8,0},{12,4},{16,24},{20,28},{24,16},{28,20},{1,9},{5... | collective-permute-start | bytes 1179656 | tf_op jit(solution)/shard_map/ppermute | solution.py:1099
  425.9 14.9 %collective-permute-start.66 = (bf16[256,1024]{1,0:T(8,128)(2,1)S(1)}, bf16[256,1024]{1,0:T(8,128)(2,1)S(1)}, u32[]{:S(2)}, u32[]{:S(2)}) collective-permute-start(bf16[256,1024]{1,0:T(8,128)(2,1)S(1)} %get-tuple-element.412), channel_id=1, source_target_pairs={{0,4},{4,0},{8,12},{12,8},{16,20},{20,16},{24,28},{28,24},{1,5},{5... | collective-permute-start | bytes 1572872 | tf_op jit(solution)/shard_map/ppermute | solution.py:1099
  428.0 76.4 %collective-permute-start.49 = (bf16[512,1024]{1,0:T(8,128)(2,1)S(1)}, bf16[512,1024]{1,0:T(8,128)(2,1)S(1)}, u32[]{:S(2)}, u32[]{:S(2)}) collective-permute-start(bf16[512,1024]{1,0:T(8,128)(2,1)S(1)} %copy-done.76), channel_id=1, source_target_pairs={{0,4},{4,0},{8,12},{12,8},{16,20},{20,16},{24,28},{28,24},{1,5},{5... | collective-permute-start | bytes 3145736 | tf_op jit(solution)/shard_map/ppermute | solution.py:1099
  435.7 14.2 %collective-permute-start.75 = (bf16[256,1024]{1,0:T(8,128)(2,1)S(1)}, bf16[256,1024]{1,0:T(8,128)(2,1)S(1)}, u32[]{:S(2)}, u32[]{:S(2)}) collective-permute-start(bf16[256,1024]{1,0:T(8,128)(2,1)S(1)} %add_convert_fusion.4), channel_id=1, source_target_pairs={{0,8},{4,12},{8,0},{12,4},{16,24},{20,28},{24,16},{28,20},{1,9},{5... | collective-permute-start | bytes 1572872 | tf_op jit(solution)/shard_map/ppermute | solution.py:1099
  442.3 26.7 %collective-permute-start.62 = (bf16[768,256]{1,0:T(8,128)(2,1)S(1)}, bf16[768,256]{1,0:T(8,128)(2,1)S(1)}, u32[]{:S(2)}, u32[]{:S(2)}) collective-permute-start(bf16[768,256]{1,0:T(8,128)(2,1)S(1)} %dynamic-slice_convert_fusion.2), channel_id=1, source_target_pairs={{0,4},{4,0},{8,12},{12,8},{16,20},{20,16},{24,28},{28,24},{1,5},{5... | collective-permute-start | bytes 1179656 | tf_op jit(solution)/shard_map/ppermute | solution.py:1099
  442.9 30.6 %collective-permute-start.71 = (bf16[768,256]{1,0:T(8,128)(2,1)S(1)}, bf16[768,256]{1,0:T(8,128)(2,1)S(1)}, u32[]{:S(2)}, u32[]{:S(2)}) collective-permute-start(bf16[768,256]{1,0:T(8,128)(2,1)S(1)} %add_convert_fusion.13), channel_id=1, source_target_pairs={{0,16},{4,20},{8,24},{12,28},{16,0},{20,4},{24,8},{28,12},{1,17},{... | collective-permute-start | bytes 1179656 | tf_op jit(solution)/shard_map/ppermute | solution.py:1099
  451.1 44.9 %collective-permute-start.67 = (bf16[128,1024]{1,0:T(8,128)(2,1)S(1)}, bf16[128,1024]{1,0:T(8,128)(2,1)S(1)}, u32[]{:S(2)}, u32[]{:S(2)}) collective-permute-start(bf16[128,1024]{1,0:T(8,128)(2,1)S(1)} %dynamic-slice_convert_fusion.5), channel_id=1, source_target_pairs={{0,8},{4,12},{8,0},{12,4},{16,24},{20,28},{24,16},{28,20},{1,9},{5... | collective-permute-start | bytes 786440 | tf_op jit(solution)/shard_map/ppermute | solution.py:1099
  472.9 67.2 %collective-permute-start.76 = (bf16[512,1024]{1,0:T(8,128)(2,1)S(1)}, bf16[512,1024]{1,0:T(8,128)(2,1)S(1)}, u32[]{:S(2)}, u32[]{:S(2)}) collective-permute-start(bf16[512,1024]{1,0:T(8,128)(2,1)S(1)} %maximum_select_fusion.6), channel_id=1, source_target_pairs={{0,4},{4,0},{8,12},{12,8},{16,20},{20,16},{24,28},{28,24},{1,5},{5... | collective-permute-start | bytes 3145736 | tf_op jit(solution)/shard_map/ppermute | solution.py:1099
  473.5 21.5 %collective-permute-start.59 = (f32[8,1024]{1,0:T(8,128)S(1)}, f32[8,1024]{1,0:T(8,128)S(1)}, u32[]{:S(2)}, u32[]{:S(2)}) collective-permute-start(f32[8,1024]{1,0:T(8,128)S(1)} %add.258), channel_id=1, source_target_pairs={{0,4},{4,0},{8,12},{12,8},{16,20},{20,16},{24,28},{28,24},{1,5},{5... | collective-permute-start | bytes 98312 | tf_op jit(solution)/shard_map/ppermute | solution.py:1099
  499.9 17.1 %collective-permute-start.68 = (bf16[128,1024]{1,0:T(8,128)(2,1)S(1)}, bf16[128,1024]{1,0:T(8,128)(2,1)S(1)}, u32[]{:S(2)}, u32[]{:S(2)}) collective-permute-start(bf16[128,1024]{1,0:T(8,128)(2,1)S(1)} %add_convert_fusion.15), channel_id=1, source_target_pairs={{0,16},{4,20},{8,24},{12,28},{16,0},{20,4},{24,8},{28,12},{1,17},{... | collective-permute-start | bytes 786440 | tf_op jit(solution)/shard_map/ppermute | solution.py:1099
  504.4 29.3 %collective-permute-start.72 = (bf16[768,256]{1,0:T(8,128)(2,1)S(1)}, bf16[768,256]{1,0:T(8,128)(2,1)}, u32[]{:S(2)}, u32[]{:S(2)}) collective-permute-start(bf16[768,256]{1,0:T(8,128)(2,1)S(1)} %add_convert_fusion.10), channel_id=1, source_target_pairs={{0,8},{4,12},{8,0},{12,4},{16,24},{20,28},{24,16},{28,20},{1,9},{5... | collective-permute-start | bytes 1179656 | tf_op jit(solution)/shard_map/ppermute | solution.py:1099
  504.4 21.9 %collective-permute-start.63 = (bf16[768,256]{1,0:T(8,128)(2,1)S(1)}, bf16[768,256]{1,0:T(8,128)(2,1)S(1)}, u32[]{:S(2)}, u32[]{:S(2)}) collective-permute-start(bf16[768,256]{1,0:T(8,128)(2,1)S(1)} %add_convert_fusion.12), channel_id=1, source_target_pairs={{0,16},{4,20},{8,24},{12,28},{16,0},{20,4},{24,8},{28,12},{1,17},{... | collective-permute-start | bytes 1179656 | tf_op jit(solution)/shard_map/ppermute | solution.py:1099
  507.5 23.3 %collective-permute-start.61 = (f32[8,1024]{1,0:T(8,128)S(1)}, f32[8,1024]{1,0:T(8,128)S(1)}, u32[]{:S(2)}, u32[]{:S(2)}) collective-permute-start(f32[8,1024]{1,0:T(8,128)S(1)} %add.260), channel_id=1, source_target_pairs={{0,16},{4,20},{8,24},{12,28},{16,0},{20,4},{24,8},{28,12},{1,17},{... | collective-permute-start | bytes 98312 | tf_op jit(solution)/shard_map/ppermute | solution.py:1099
  517.2 14.9 %collective-permute-start.69 = (bf16[128,1024]{1,0:T(8,128)(2,1)S(1)}, bf16[128,1024]{1,0:T(8,128)(2,1)S(1)}, u32[]{:S(2)}, u32[]{:S(2)}) collective-permute-start(bf16[128,1024]{1,0:T(8,128)(2,1)S(1)} %add_convert_fusion.14), channel_id=1, source_target_pairs={{0,8},{4,12},{8,0},{12,4},{16,24},{20,28},{24,16},{28,20},{1,9},{5... | collective-permute-start | bytes 786440 | tf_op jit(solution)/shard_map/ppermute | solution.py:1099
  526.4 12.2 %collective-permute-start.64 = (bf16[768,256]{1,0:T(8,128)(2,1)S(1)}, bf16[768,256]{1,0:T(8,128)(2,1)}, u32[]{:S(2)}, u32[]{:S(2)}) collective-permute-start(bf16[768,256]{1,0:T(8,128)(2,1)S(1)} %add_convert_fusion.11), channel_id=1, source_target_pairs={{0,4},{4,0},{8,12},{12,8},{16,20},{20,16},{24,28},{28,24},{1,5},{5... | collective-permute-start | bytes 1179656 | tf_op jit(solution)/shard_map/ppermute | solution.py:1099
  532.2 17.2 %collective-permute-start.70 = (bf16[256,1024]{1,0:T(8,128)(2,1)S(1)}, bf16[256,1024]{1,0:T(8,128)(2,1)S(1)}, u32[]{:S(2)}, u32[]{:S(2)}) collective-permute-start(bf16[256,1024]{1,0:T(8,128)(2,1)S(1)} %maximum_select_fusion.9), channel_id=1, source_target_pairs={{0,4},{4,0},{8,12},{12,8},{16,20},{20,16},{24,28},{28,24},{1,5},{5... | collective-permute-start | bytes 1572872 | tf_op jit(solution)/shard_map/ppermute | solution.py:1099
  535.1 22.7 %collective-permute-start.73 = (bf16[1536,256]{1,0:T(8,128)(2,1)S(1)}, bf16[1536,256]{1,0:T(8,128)(2,1)S(1)}, u32[]{:S(2)}, u32[]{:S(2)}) collective-permute-start(bf16[1536,256]{1,0:T(8,128)(2,1)S(1)} %maximum_select_fusion.8), channel_id=1, source_target_pairs={{0,4},{4,0},{8,12},{12,8},{16,20},{20,16},{24,28},{28,24},{1,5},{5... | collective-permute-start | bytes 2359304 | tf_op jit(solution)/shard_map/ppermute | solution.py:1099
  540.0 20.6 %collective-permute-start.65 = (bf16[1536,256]{1,0:T(8,128)(2,1)S(1)}, bf16[1536,256]{1,0:T(8,128)(2,1)S(1)}, u32[]{:S(2)}, u32[]{:S(2)}) collective-permute-start(bf16[1536,256]{1,0:T(8,128)(2,1)S(1)} %maximum_select_fusion.7), channel_id=1, source_target_pairs={{0,8},{4,12},{8,0},{12,4},{16,24},{20,28},{24,16},{28,20},{1,9},{5... | collective-permute-start | bytes 2359304 | tf_op jit(solution)/shard_map/ppermute | solution.py:1099
  (122 other events, 881.6 us)

commit v12 on v10

--- a/solution.py
+++ b/solution.py
@@ -466,7 +466,7 @@
         ),
         out_shape=[shape((2 * rows, a.shape[0]), ROUND) for a in weights],
         compiler_params=params(32),
-        cost_estimate=lasting(3.5),
+        cost_estimate=lasting(0.375),
         name="pull",
     )(place, mine, other, *weights)
 
@@ -614,7 +614,7 @@
         ),
         out_shape=[shape((span, wide), ROUND)] * 3,
         compiler_params=params(48),
-        cost_estimate=lasting(7.00 * pairs),
+        cost_estimate=lasting(1.050 * pairs),
         name="self_back",
     )(limit, q, k, v, o, do, lse)
 
@@ -790,7 +790,7 @@
         out_specs=pl.BlockSpec((width, tile), lambda i: (0, i)),
         out_shape=shape((width, hidden), kind),
         compiler_params=params(48),
-        cost_estimate=lasting(5.00),
+        cost_estimate=lasting(0.750),
         name="up_grad",
     )(mine, other, du)
 
@@ -813,7 +813,7 @@
         out_specs=pl.BlockSpec((tile, width), lambda i: (i, 0)),
         out_shape=shape((hidden, width), kind),
         compiler_params=params(48),
-        cost_estimate=lasting(5.00),
+        cost_estimate=lasting(0.750),
         name="down_grad",
     )(g, mine, other)
 
@@ -853,7 +853,7 @@
         ),
         out_shape=shape((3 * width, 256), kind),
         compiler_params=params(48),
-        cost_estimate=lasting(5.00),
+        cost_estimate=lasting(0.750),
         name="qkv_grad",
     )(place, h, *grads)
 
@@ -882,7 +882,7 @@
         ),
         out_shape=shape((width, 256), kind),
         compiler_params=params(48),
-        cost_estimate=lasting(2.86),
+        cost_estimate=lasting(0.429),
         name="query_grad",
     )(place, mine, other, d_mine, d_other)
 
@@ -924,7 +924,7 @@
         ),
         out_shape=shape((512, width), kind),
         compiler_params=params(48),
-        cost_estimate=lasting(4.29),
+        cost_estimate=lasting(0.643),
         name="outputs_grad",
     )(place, *o, dself, dself_other, ca, ca_other, dcross, dcross_other)
 
@@ -1003,7 +1003,7 @@
         + [shape((4, 64, 256), FULL)] * 2
         + [shape((8, width), FULL)],
         compiler_params=params(56),
-        cost_estimate=lasting(24),
+        cost_estimate=lasting(2.571),
         name="middle_back",
     )(place, ym, yr, x1, x2, d, cq, *whole)
 
@@ -1037,7 +1037,7 @@
         ),
         out_shape=shape((rows, width), kind),
         compiler_params=params(40),
-        cost_estimate=lasting(3.57),
+        cost_estimate=lasting(0.535),
         name="first_back",
     )(place, *grads, *weights)
 
@@ -1068,7 +1068,7 @@
         ),
         out_shape=[shape((rows, width), ROUND), shape((8, width), FULL)],
         compiler_params=params(24),
-        cost_estimate=lasting(4.29),
+        cost_estimate=lasting(0.643),
         name="frames_back",
     )(place, ym, yr, dx1, frames, gains)
 
@@ -1216,8 +1216,11 @@
     down_z = (near, Z_NEAR)
     store = {}
     last = []
+    free = []
 
     def order(*names):
+        if free:
+            return
         names = tuple(dict.fromkeys((*names, *last)))
         for name, value in zip(names, join(tuple(store[name] for name in names))):
             store[name] = value
@@ -1320,7 +1323,7 @@
     step(["up0"], lambda: up_grad(h3, *get("h3_other", "du0"), ROUND), "du0")
     order(up.fly, "down1", "dself_other")
     down.over_y("down1")
-    store["up_total"] = lax.psum(plus(*get("up0", up.fly)), "wide")
+    up.first("up0")
     step(
         ["dof", "dos", "do0"],
         lambda: pull(place, *get("dself", "dself_other"), (out_first, out_second, w_out)),
@@ -1357,6 +1360,7 @@
         lambda: self_back(limit, qs, ks, vs, store["o_s"], store["dos"], lse_s),
         "dos",
     )
+    up.second()
     step(["down0"], lambda: down_grad(store["g0"], dout, dout_other, ROUND), "g0")
     yp = ("dqf", "dkf", "dvf", "dqs", "dks", "dvs")
     step(["qkv1"], lambda: qkv_grad(place, h1, get(*yp), ROUND), "dqs")
@@ -1370,9 +1374,16 @@
         lambda: self_back(limit, q0, k0, v0, store["o0"], store["do0"], lse0),
         "do0",
     )
+    up.far()
     down.second()
     step(["outs1"], lambda: outof(1, "of", "o_s"), "dcross_other", "ca_other")
     outs.over_y("outs1")
+    nine = ("dq0", "dk0", "dv0", *yp)
+    weights = (w_qkv, qkv_first, qkv_second)
+    step(["yo"], lambda: first_back(away, get(*nine), weights, ROUND), "dq0")
+    store["yo_fly"] = over_core(store["yo"])
+    step(["qkv0"], lambda: qkv_grad(place, h1, get("dq0", "dk0", "dv0"), ROUND), "dq0")
+    qkv.first("qkv0")
     step(["query0"], lambda: query(0), "dcq")
     order("query0", "query_fly", "pair", "pair_y")
     other_text = lax.dynamic_index_in_dim(text_states, 1 - side, keepdims=False)
@@ -1387,19 +1398,8 @@
         axis=0,
     )
     cross_in.first_alone("into0")
-    nine = ("dq0", "dk0", "dv0", *yp)
-    weights = (w_qkv, qkv_first, qkv_second)
-    step(["yo"], lambda: first_back(away, get(*nine), weights, ROUND), "dq0")
-    store["yo_fly"] = over_core(store["yo"])
-    step(["qkv0"], lambda: qkv_grad(place, h1, get("dq0", "dk0", "dv0"), ROUND), "dq0")
-    qkv.first("qkv0")
-    down.far()
-    cross_in.second()
-    step(["outs0"], lambda: outof(0, "o0"), "dcross")
-    outs.first("outs0")
-    qkv.second()
+    up.back()
     step(["ym"], lambda: first_back(place, get(*nine), weights, FULL), "dq0")
-    cross_in.far()
     step(
         ["grad_frames", "first_sums"],
         lambda: frames_back(place, *get("ym", "yo_fly", "dx1"), frames, norm_gain),
@@ -1407,39 +1407,46 @@
         "yo_fly",
     )
     norms = Row("norms", store["sums"] + store["first_sums"], over_core)
-    down.back()
-    outs.second()
-    qkv.far()
+    down.far()
     norms.then(over_y)
-    cross_in.back()
-    down.along()
-    norms.then(over_x)
-    outs.far()
+    up.along()
+    cross_in.second()
+    step(["outs0"], lambda: outof(0, "o0"), "dcross")
+    outs.first("outs0")
+    norms.then(over_z)
     text_part = 0.0
     for c in range(2):
         text_part = text_part + nt(pairs[c], w_cross_kv[c])
     text_mine, text_theirs = text_part[:64], text_part[64:]
     text_rows = Row("texts", text_mine, lambda v: over_y(text_theirs))
+    last[:] = ["texts_kept"]
+    qkv.second()
+    down.back()
+    cross_in.far()
     store["out_fly"] = over_core(out_o)
-    qkv.back()
-    norms.then(over_z)
-    cross_in.along()
     text_rows.then(over_core)
-    outs.back()
     norms.then(lambda v: along_wide(v, Z_FAR))
-    down.end("grad_down")
-    order("up_total")
-    store["grad_up"] = store["up_total"].astype(FULL)
-    last[:] = ["grad_up"]
-    order("texts_fly", "texts_kept", "out_fly", "x2")
+    outs.second()
+    qkv.far()
+    order("x2", "out_fly")
+    out_rows = lower(store["x2"] + out_m + store["out_fly"].astype(FULL))
+    down.along()
+    cross_in.back()
+    order("texts_fly", "texts_kept")
     text_grad = lower(text_rows.total())
     text_away = over_y(text_grad)
+    grad_text = ordered(text_grad[None], text_away[None], side)
+    up.end("grad_up")
+    outs.far()
+    norms.then(over_x)
+    qkv.back()
+    cross_in.along()
+    outs.back()
+    down.end("grad_down")
     qkv.along()
     outs.along()
-    out_rows = lower(store["x2"] + out_m + store["out_fly"].astype(FULL))
-    grad_text = ordered(text_grad[None], text_away[None], side)
+    cross_in.end("grad_in")
     sums = norms.total()
-    cross_in.end("grad_in")
     qkv.end("grad_qkv")
     outs.end("grad_outs")
     grad_in, grad_outs = get("grad_in", "grad_outs")

time: 574 us -> 560 us (0.976)
  between operations: 15.9 us -> 2.74 us
  Pallas kernels: 260 us -> 270 us
  waiting for transfers between devices: 131 us -> 122 us
  local copies, waits for them, and re-layouts: 49.7 us -> 56.8 us
    pallas_call x2, Pallas kernels: 6.96 us -> 16.7 us  [project(): pl.pallas_call(project_kernel, grid_spec=pltpu.PrefetchScalarGridSpec(num...]
    ppermute x29 -> x34, waiting for transfers between devices: 105 us -> 97.6 us  [along_wide(): return lax.ppermute(v, 'wide', pairs)]
    convert_element_type x2 -> x0, other arithmetic: 5.8 us -> none  [the longest x1 4.22 us: chip_local(): store['grad_up'] = store['up_total'].astype(FULL)]
    convert_element_type x15 -> x16, other arithmetic: 16.1 us -> 19.6 us  [lower(): return values_in.astype(jnp.bfloat16)]
    ppermute x29 -> x34, starting transfers between devices: 29.2 us -> 31.6 us  [along_wide(): return lax.ppermute(v, 'wide', pairs)]
    unnamed x241 -> x265, local copies, waits for them, and re-layouts: 27.4 us -> 29.7 us
  transfers between devices with their start and end apart: 73 -> 77, of which waited for: 17 -> 24; matrix products, arithmetic and copies ran while one was open for 12% -> 13% of each run, Pallas kernels for 44% -> 46%
where the time goes in v12:
time: 560 us; the launch traced here: 555 us
  Pallas kernels  270 us (48%)
  waiting for transfers between devices  122 us (22%)
  local copies, waits for them, and re-layouts  56.8 us (10%)
  starting transfers between devices  56.7 us (10%)
  other arithmetic  45.7 us (8%)
    ppermute x34, waiting for transfers between devices, along_wide(): return lax.ppermute(v, 'wide', pairs)  97.6 us
    pallas_call x4, Pallas kernels, feed(): pl.pallas_call(functools.partial(feed_kernel, parts=parts, carried=len(be...  51.6 us
    pallas_call x3, Pallas kernels, self_back(): pl.pallas_call(functools.partial(self_back_kernel, span=span, floor=floor...  39.5 us
    ppermute x34, starting transfers between devices, along_wide(): return lax.ppermute(v, 'wide', pairs)  31.6 us
    pallas_call x3, Pallas kernels, self_forward(): pl.pallas_call(functools.partial(self_forward_kernel, span=span, floor=fl...  30.7 us
    unnamed x265, local copies, waits for them, and re-layouts  29.7 us
    ppermute x16, waiting for transfers between devices, over_y(): return lax.ppermute(v, 'narrow', Y_PAIRS)  23.8 us
    pallas_call x1, Pallas kernels, middle_back(): pl.pallas_call(middle_back_kernel, grid_spec=pltpu.PrefetchScalarGridSpec...  23 us
  transfers between devices with their start and end apart: 77, of which 24 were waited for; matrix products, arithmetic and copies ran while one was open for 13% of the time, Pallas kernels for 46%

profile of v12, /device:TPU:0, one launch (start us, length us, event | category | flops | bytes accessed | tf_op | source)
XLA Modules:
  0.0 554.8 jit_solution(9521944420678134454)
XLA Ops:
  1.2 2.1 constant_dynamic-slice_fusion.15
  3.2 2.6 collective-permute-start.1
  14.8 4.5 first_project.1
  22.1 2.2 collective-permute-done.1.weight_ref.refs_10_
  30.5 4.0 collective-permute-done.2.refs_7_.refs_0_
  36.3 3.8 collective-permute-done.3.refs_13_.refs_1_
  41.9 14.0 %self_forward.3 = (bf16[1664,256]{1,0:T(8,128)(2,1)}, f32[2,8,1664]{2,1,0:T(8,128)}) custom-call(s32[1]{0:T(128)} %dynamic_slice.129.limit_ref, bf16[1664,256]{1,0:T(8,128)(2,1)} %copy-done.56, bf16[1664,256]{1,0:T(8,128)(2,1)} %copy-done.58, bf16[1664,256]{1,0:T(8,128)(2,1)} %copy-done.60), custom_call_target="tpu_custom_call" | custom-call | flops 4701199872 | bytes 1000 | tf_op jit(solution)/shard_map/self_forward/pallas_call | solution.py:525
  56.0 14.0 %project.2 = (bf16[1664,128]{1,0:T(8,128)(2,1)S(1)}, bf16[1664,128]{1,0:T(8,128)(2,1)S(1)}, bf16[1664,128]{1,0:T(8,128)(2,1)S(1)}) custom-call(s32[3]{0:T(128)S(1)} %add_add_fusion.place_ref, bf16[1664,1024]{1,0:T(8,128)(2,1)S(1)} %get-tuple-element.267.h_ref, bf16[3,1024,128]{2,1,0:T(8,128)(2,1)} %collective-permute-done.1.weight_ref.refs_10_), custom_call_target="tpu_custom_call" | custom-call | flops 1288000000 | bytes 1000 | tf_op jit(solution)/shard_map/project/pallas_call | solution.py:423
  73.8 8.3 %self_forward.4 = (bf16[1664,128]{1,0:T(8,128)(2,1)}, f32[1,8,1664]{2,1,0:T(8,128)}) custom-call(s32[1]{0:T(128)} %dynamic_slice.129.limit_ref, bf16[1664,128]{1,0:T(8,128)(2,1)} %copy-done.65, bf16[1664,128]{1,0:T(8,128)(2,1)} %copy-done.67, bf16[1664,128]{1,0:T(8,128)(2,1)} %copy-done.69), custom_call_target="tpu_custom_call" | custom-call | flops 2350599936 | bytes 1000 | tf_op jit(solution)/shard_map/self_forward/pallas_call | solution.py:525
  85.2 2.7 project.3
  91.5 8.4 %self_forward.5 = (bf16[1664,128]{1,0:T(8,128)(2,1)}, f32[1,8,1664]{2,1,0:T(8,128)}) custom-call(s32[1]{0:T(128)} %dynamic_slice.129.limit_ref, bf16[1664,128]{1,0:T(8,128)(2,1)} %copy-done.71, bf16[1664,128]{1,0:T(8,128)(2,1)} %copy-done.73, bf16[1664,128]{1,0:T(8,128)(2,1)} %copy-done.75), custom_call_target="tpu_custom_call" | custom-call | flops 2350599936 | bytes 1000 | tf_op jit(solution)/shard_map/self_forward/pallas_call | solution.py:525
  108.8 20.7 %middle_forward.1 = (f32[832,1024]{1,0:T(8,128)}, f32[832,1024]{1,0:T(8,128)}, bf16[832,1024]{1,0:T(8,128)(2,1)}, bf16[832,1024]{1,0:T(8,128)(2,1)}, bf16[832,10...) custom-call(s32[3]{0:T(128)} %copy-done.81, bf16[832,1024]{1,0:T(8,128)(2,1)} %frame_ref.3, ...), custom_call_target="tpu_custom_call" | custom-call | flops 7084000256 | bytes 1000 | tf_op jit(solution)/shard_map/middle_forward/pallas_call | solution.py:677
  131.5 12.1 %feed.4 = (bf16[1664,1024]{1,0:T(8,128)(2,1)}, bf16[1664,1024]{1,0:T(8,128)(2,1)}, f32[832,1024]{1,0:T(8,128)}, f32[832,1024]{1,0:T(8,128)}) custom-call(s32[3]{0:T(128)} %copy-done.81, bf16[832,1024]{1,0:T(8,128)(2,1)} %get-tuple-element.311.h_ref.mine_ref, bf16[832,1024]{1,0:T(8,128)(2,1)} %copy-done, bf16[1024,1024]{1,0:T(8,128)(2,1)} %refs_0_.1, ...), custom_call_target="tpu_custom_call" | custom-call | flops 4185999872 | bytes 1000 | tf_op jit(solution)/shard_map/feed/pallas_call | solution.py:756
  145.4 12.1 %feed.5 = (bf16[1664,1024]{1,0:T(8,128)(2,1)}, bf16[1664,1024]{1,0:T(8,128)(2,1)}, f32[832,1024]{1,0:T(8,128)}, f32[832,1024]{1,0:T(8,128)}) custom-call(s32[3]{0:T(128)} %copy-done.81, bf16[832,1024]{1,0:T(8,128)(2,1)} %copy-done.16, bf16[832,1024]{1,0:T(8,128)(2,1)} %copy-done.13, ...), custom_call_target="tpu_custom_call", output_to_operand_aliasing={{0}: (5, {}), {1}: (6, {})} | custom-call | flops 4185999872 | bytes 1000 | tf_op jit(solution)/shard_map/feed/pallas_call | solution.py:756
  157.5 13.6 %feed.6 = (bf16[1664,1024]{1,0:T(8,128)(2,1)}, bf16[1664,1024]{1,0:T(8,128)(2,1)}, bf16[832,1024]{1,0:T(8,128)(2,1)}, bf16[832,1024]{1,0:T(8,128)(2,1)}) custom-call(s32[3]{0:T(128)} %copy-done.81, bf16[832,1024]{1,0:T(8,128)(2,1)} %copy-done.16, bf16[832,1024]{1,0:T(8,128)(2,1)} %copy-done.13, bf16[1024,512]{1,0:T(8,128)(2,1)} %collective-permute-done.14.refs_0_, ...), custom_call_target="tpu_custom_call" | custom-call | flops 4185999872 | bytes 1000 | tf_op jit(solution)/shard_map/feed/pallas_call | solution.py:756
  171.1 13.7 %feed.7 = (bf16[1664,1024]{1,0:T(8,128)(2,1)}, bf16[1664,1024]{1,0:T(8,128)(2,1)}, f32[832,1024]{1,0:T(8,128)}, f32[832,1024]{1,0:T(8,128)}) custom-call(s32[3]{0:T(128)} %copy-done.81, bf16[832,1024]{1,0:T(8,128)(2,1)} %get-tuple-element.311.h_ref.mine_ref, bf16[832,1024]{1,0:T(8,128)(2,1)} %copy-done, ...), custom_call_target="tpu_custom_call", output_to_operand_aliasing={{0}: (9, {}), {1}: (10, {})} | custom-call | flops 4185999872 | bytes 1000 | tf_op jit(solution)/shard_map/feed/pallas_call | solution.py:756
  184.9 7.3 %up_grad.2 = bf16[1024,1024]{1,0:T(8,128)(2,1)} custom-call(bf16[832,1024]{1,0:T(8,128)(2,1)S(1)} %copy-done.3, bf16[832,1024]{1,0:T(8,128)(2,1)S(1)} %copy-done.17, bf16[1664,1024]{1,0:T(8,128)(2,1)} %get-tuple-element.333.du_ref), custom_call_target="tpu_custom_call" | custom-call | flops 241500000 | bytes 1000 | tf_op jit(solution)/shard_map/up_grad/pallas_call | solution.py:786
  193.3 7.1 %down_grad.2 = bf16[1024,1024]{1,0:T(8,128)(2,1)} custom-call(bf16[1664,1024]{1,0:T(8,128)(2,1)} %get-tuple-element.334.g_ref, bf16[832,1024]{1,0:T(8,128)(2,1)S(1)} %copy-done.1, bf16[832,1024]{1,0:T(8,128)(2,1)S(1)} %copy-done.14), custom_call_target="tpu_custom_call" | custom-call | flops 241500000 | bytes 1000 | tf_op jit(solution)/shard_map/down_grad/pallas_call | solution.py:809
  201.6 23.0 %middle_back.1 = (f32[832,1024]{1,0:T(8,128)}, bf16[832,1024]{1,0:T(8,128)(2,1)}, bf16[832,1024]{1,0:T(8,128)(2,1)}, bf16[832,1024]{1,0:T(8,128)(2,1)}, f32[4,64...) custom-call(s32[3]{0:T(128)} %copy-done.81, f32[832,1024]{1,0:T(8,128)} %get-tuple-element.338.ym_ref, ...), custom_call_target="tpu_custom_call" | custom-call | flops 827862016 | bytes 1000 | tf_op jit(solution)/shard_map/middle_back/pallas_call | solution.py:992
  226.6 6.3 %up_grad.3 = bf16[1024,1024]{1,0:T(8,128)(2,1)S(1)} custom-call(bf16[832,1024]{1,0:T(8,128)(2,1)S(1)} %copy-done.3, bf16[832,1024]{1,0:T(8,128)(2,1)S(1)} %copy-done.18, bf16[1664,1024]{1,0:T(8,128)(2,1)} %get-tuple-element.344.du_ref), custom_call_target="tpu_custom_call" | custom-call | flops 241500000 | bytes 1000 | tf_op jit(solution)/shard_map/up_grad/pallas_call | solution.py:786
  233.0 7.5 %collective-permute-done.31 = bf16[1024,1024]{1,0:T(8,128)(2,1)} collective-permute-done((bf16[1024,1024]{1,0:T(8,128)(2,1)}, bf16[1024,1024]{1,0:T(8,128)(2,1)}, u32[]{:S(2)}, u32[]{:S(2)}) %collective-permute-start.31) | collective-permute-done | bytes 2097184 | tf_op jit(solution)/shard_map/ppermute | solution.py:1096
  241.7 4.1 add_convert_fusion.2
  251.9 4.9 pull.1
  257.8 9.3 %self_back.3 = (bf16[1664,128]{1,0:T(8,128)(2,1)S(1)}, bf16[1664,128]{1,0:T(8,128)(2,1)S(1)}, bf16[1664,128]{1,0:T(8,128)(2,1)S(1)}) custom-call(s32[1]{0:T(128)} %dynamic_slice.129.limit_ref, bf16[1664,128]{1,0:T(8,128)(2,1)S(1)} %copy-done.66, bf16[1664,128]{1,0:T(8,128)(2,1)S(1)} %copy-done.68, bf16[1664,128]{1,0:T(8,128)(2,1)S(1)} %copy-done.70, ...), custom_call_target="tpu_custom_call" | custom-call | flops 338100000 | bytes 1000 | tf_op jit(solution)/shard_map/self_back/pallas_call | solution.py:606
  267.4 4.5 query_grad.2
  272.7 9.7 %self_back.4 = (bf16[1664,128]{1,0:T(8,128)(2,1)S(1)}, bf16[1664,128]{1,0:T(8,128)(2,1)S(1)}, bf16[1664,128]{1,0:T(8,128)(2,1)S(1)}) custom-call(s32[1]{0:T(128)} %dynamic_slice.129.limit_ref, bf16[1664,128]{1,0:T(8,128)(2,1)S(1)} %copy-done.72, bf16[1664,128]{1,0:T(8,128)(2,1)S(1)} %copy-done.74, bf16[1664,128]{1,0:T(8,128)(2,1)S(1)} %copy-done.76, ...), custom_call_target="tpu_custom_call" | custom-call | flops 338100000 | bytes 1000 | tf_op jit(solution)/shard_map/self_back/pallas_call | solution.py:606
  289.3 6.2 %down_grad.3 = bf16[1024,1024]{1,0:T(8,128)(2,1)S(1)} custom-call(bf16[1664,1024]{1,0:T(8,128)(2,1)} %get-tuple-element.379.g_ref, bf16[832,1024]{1,0:T(8,128)(2,1)S(1)} %copy-done.2, bf16[832,1024]{1,0:T(8,128)(2,1)S(1)} %copy-done.15), custom_call_target="tpu_custom_call" | custom-call | flops 241500000 | bytes 1000 | tf_op jit(solution)/shard_map/down_grad/pallas_call | solution.py:809
  295.6 7.2 %qkv_grad.2 = bf16[3072,256]{1,0:T(8,128)(2,1)} custom-call(s32[3]{0:T(128)S(1)} %copy-done.82, bf16[1664,1024]{1,0:T(8,128)(2,1)} %copy-done.8, bf16[1664,128]{1,0:T(8,128)(2,1)S(1)} %get-tuple-element.365.refs_0_.refs_3_, bf16[1664,128]{1,0:T(8,128)(2,1)S(1)} %get-tuple-element.366.refs_1_.refs_4_, ...), custom_call_target="tpu_custom_call" | custom-call | flops 241500000 | bytes 1000 | tf_op jit(solution)/shard_map/qkv_grad/pallas_call | solution.py:846
  302.8 4.1 add_convert_fusion.1
  308.5 2.1 dynamic-slice_convert_fusion.1
  313.9 2.1 slice.84
  318.5 20.5 %self_back.5 = (bf16[1664,256]{1,0:T(8,128)(2,1)S(1)}, bf16[1664,256]{1,0:T(8,128)(2,1)S(1)}, bf16[1664,256]{1,0:T(8,128)(2,1)S(1)}) custom-call(s32[1]{0:T(128)} %dynamic_slice.129.limit_ref, bf16[1664,256]{1,0:T(8,128)(2,1)S(1)} %copy-done.57, bf16[1664,256]{1,0:T(8,128)(2,1)S(1)} %copy-done.59, bf16[1664,256]{1,0:T(8,128)(2,1)S(1)} %copy-done.61, ...), custom_call_target="tpu_custom_call" | custom-call | flops 676200000 | bytes 1000 | tf_op jit(solution)/shard_map/self_back/pallas_call | solution.py:606
  339.6 2.0 add_convert_fusion.9
  346.9 2.7 collective-permute-start.48
  350.5 5.2 outputs_grad.2
  355.8 7.0 %first_back.2 = bf16[832,1024]{1,0:T(8,128)(2,1)} custom-call(s32[3]{0:T(128)S(1)} %add_add_fusion.1.place_ref, bf16[1664,256]{1,0:T(8,128)(2,1)S(1)} %get-tuple-element.426.refs_0_, bf16[1664,256]{1,0:T(8,128)(2,1)S(1)} %get-tuple-element.407.refs_1_, bf16[1664,256]{1,0:T(8,128)(2,1)S(1)} %get-tuple-element.408.refs_2_, bf16[1664,128]{1,0:T(8,128)(2,1)S(1)} %copy-done.23, ...), custom_call_target="tpu_custom_call" | custom-call | flops 172270000 | bytes 1000 | tf_op jit(solution)/shard_map/first_back/pallas_call | solution.py:1026
  362.8 5.9 %qkv_grad.3 = bf16[3072,256]{1,0:T(8,128)(2,1)S(1)} custom-call(s32[3]{0:T(128)S(1)} %copy-done.82, bf16[1664,1024]{1,0:T(8,128)(2,1)} %copy-done.8, bf16[1664,256]{1,0:T(8,128)(2,1)S(1)} %get-tuple-element.426.refs_0_, bf16[1664,256]{1,0:T(8,128)(2,1)S(1)} %get-tuple-element.407.refs_1_, bf16[1664,256]{1,0:T(8,128)(2,1)S(1)} %get-tuple-element.408.refs_2_), custom_call_target="tpu_custom_call" | custom-call | flops 241500000 | bytes 1000 | tf_op jit(solution)/shard_map/qkv_grad/pallas_call | solution.py:846
  368.7 2.1 dynamic-slice_convert_fusion
  370.8 2.7 convert_add_fusion.6
  373.5 3.9 query_grad.3
  384.4 6.0 %first_back.3.ym_ref = f32[832,1024]{1,0:T(8,128)S(1)} custom-call(s32[3]{0:T(128)S(1)} %copy-done.82, bf16[1664,256]{1,0:T(8,128)(2,1)S(1)} %get-tuple-element.426.refs_0_, bf16[1664,256]{1,0:T(8,128)(2,1)S(1)} %get-tuple-element.407.refs_1_, bf16[1664,256]{1,0:T(8,128)(2,1)S(1)} %copy-done.12, bf16[1664,128]{1,0:T(8,128)(2,1)S(1)} %copy-done.24, ...), custom_call_target="tpu_custom_call" | custom-call | flops 172270000 | bytes 1000 | tf_op jit(solution)/shard_map/first_back/pallas_call | solution.py:1026
  391.2 18.1 %collective-permute-done.43 = bf16[1536,256]{1,0:T(8,128)(2,1)S(1)} collective-permute-done((bf16[1536,256]{1,0:T(8,128)(2,1)S(1)}, bf16[1536,256]{1,0:T(8,128)(2,1)S(1)}, u32[]{:S(2)}, u32[]{:S(2)}) %collective-permute-start.43) | collective-permute-done | bytes 786464 | tf_op jit(solution)/shard_map/ppermute | solution.py:1099
  413.2 5.9 %frames_back.1 = (bf16[832,1024]{1,0:T(8,128)(2,1)}, f32[8,1024]{1,0:T(8,128)S(1)}) custom-call(s32[3]{0:T(128)S(1)} %copy-done.82, f32[832,1024]{1,0:T(8,128)S(1)} %first_back.3.ym_ref, bf16[832,1024]{1,0:T(8,128)(2,1)} %collective-permute-done.49.yr_ref, f32[832,1024]{1,0:T(8,128)S(1)} %copy-done.42, bf16[832,1024]{1,0:T(8,128)(2,1)S(1)} %copy-done.51, ...), custom_call_target="tpu_custom_call" | custom-call | flops 207046000 | bytes 1000 | tf_op jit(solution)/shard_map/frames_back/pallas_call | solution.py:1061
  422.4 5.4 collective-permute-done.53
  429.2 5.1 outputs_grad.3
  434.4 2.9 collective-permute-done.52
  438.0 3.4 collective-permute-done.56
  442.0 5.8 %collective-permute-done.50 = bf16[256,1024]{1,0:T(8,128)(2,1)S(1)} collective-permute-done((bf16[256,1024]{1,0:T(8,128)(2,1)S(1)}, bf16[256,1024]{1,0:T(8,128)(2,1)S(1)}, u32[]{:S(2)}, u32[]{:S(2)}) %collective-permute-start.50) | collective-permute-done | bytes 524320 | tf_op jit(solution)/shard_map/ppermute | solution.py:1099
  448.5 6.7 %collective-permute-done.59 = bf16[768,256]{1,0:T(8,128)(2,1)S(1)} collective-permute-done((bf16[768,256]{1,0:T(8,128)(2,1)S(1)}, bf16[768,256]{1,0:T(8,128)(2,1)S(1)}, u32[]{:S(2)}, u32[]{:S(2)}) %collective-permute-start.59) | collective-permute-done | bytes 393248 | tf_op jit(solution)/shard_map/ppermute | solution.py:1099
  456.2 2.9 collective-permute-done.57
  459.2 3.4 collective-permute-done.55
  463.2 2.8 collective-permute-start.65
  466.0 8.9 %collective-permute-done.62 = bf16[256,1024]{1,0:T(8,128)(2,1)S(1)} collective-permute-done((bf16[256,1024]{1,0:T(8,128)(2,1)S(1)}, bf16[256,1024]{1,0:T(8,128)(2,1)S(1)}, u32[]{:S(2)}, u32[]{:S(2)}) %collective-permute-start.62) | collective-permute-done | bytes 524320 | tf_op jit(solution)/shard_map/ppermute | solution.py:1099
  476.7 14.7 %collective-permute-done.61 = bf16[768,256]{1,0:T(8,128)(2,1)S(1)} collective-permute-done((bf16[768,256]{1,0:T(8,128)(2,1)S(1)}, bf16[768,256]{1,0:T(8,128)(2,1)S(1)}, u32[]{:S(2)}, u32[]{:S(2)}) %collective-permute-start.61) | collective-permute-done | bytes 393248 | tf_op jit(solution)/shard_map/ppermute | solution.py:1099
  491.5 2.1 collective-permute-start.70
  494.7 2.9 fusion
  497.6 7.2 %collective-permute-done.66 = bf16[128,1024]{1,0:T(8,128)(2,1)S(1)} collective-permute-done((bf16[128,1024]{1,0:T(8,128)(2,1)S(1)}, bf16[128,1024]{1,0:T(8,128)(2,1)S(1)}, u32[]{:S(2)}, u32[]{:S(2)}) %collective-permute-start.66) | collective-permute-done | bytes 262176 | tf_op jit(solution)/shard_map/ppermute | solution.py:1099
  507.3 6.0 %collective-permute-done.70 = bf16[768,256]{1,0:T(8,128)(2,1)S(1)} collective-permute-done((bf16[768,256]{1,0:T(8,128)(2,1)S(1)}, bf16[768,256]{1,0:T(8,128)(2,1)S(1)}, u32[]{:S(2)}, u32[]{:S(2)}) %collective-permute-start.70) | collective-permute-done | bytes 393248 | tf_op jit(solution)/shard_map/ppermute | solution.py:1099
  514.4 5.1 collective-permute-done.69
  520.6 3.0 fusion.1
  526.4 3.7 add_convert_fusion
  537.2 4.9 collective-permute-done.75
  542.4 2.9 collective-permute-done.76
  549.9 2.9 collective-permute-done.74
  (479 shorter events, 123.3 us)
Async XLA Ops:
  3.2 21.0 %collective-permute-start.1 = (bf16[3,1024,128]{2,1,0:T(8,128)(2,1)}, bf16[3,1024,128]{2,1,0:T(8,128)(2,1)}, u32[]{:S(2)}, u32[]{:S(2)}) collective-permute-start(bf16[3,1024,128]{2,1,0:T(8,128)(2,1)} %constant_dynamic-slice_fusion.15), channel_id=1, source_target_pairs={{0,2},{2,0},{1,3},{3,1},{4,6},{6,4},{5,7},{7,5},{8,10},{10,8},{9,1... | collective-permute-start | bytes 2359304 | tf_op jit(solution)/shard_map/ppermute | solution.py:1096
  27.5 12.7 %collective-permute-start.3 = (bf16[1024,128]{1,0:T(8,128)(2,1)}, bf16[1024,128]{1,0:T(8,128)(2,1)}, u32[]{:S(2)}, u32[]{:S(2)}) collective-permute-start(bf16[1024,128]{1,0:T(8,128)(2,1)} %constant_dynamic-slice_fusion.13), channel_id=1, source_target_pairs={{0,2},{2,0},{1,3},{3,1},{4,6},{6,4},{5,7},{7,5},{8,10},{10,8},{9,1... | collective-permute-start | bytes 786440 | tf_op jit(solution)/shard_map/ppermute | solution.py:1096
  28.9 42.8 %collective-permute-start.5 = (bf16[256,1024]{1,0:T(8,128)(2,1)}, bf16[256,1024]{1,0:T(8,128)(2,1)}, u32[]{:S(2)}, u32[]{:S(2)}) collective-permute-start(bf16[256,1024]{1,0:T(8,128)(2,1)} %refs_2_), channel_id=1, source_target_pairs={{0,1},{1,0},{2,3},{3,2},{4,5},{5,4},{6,7},{7,6},{8,9},{9,8},{10,11... | collective-permute-start | bytes 1572872 | tf_op jit(solution)/shard_map/ppermute | solution.py:1093
  29.0 42.7 %collective-permute-start.6 = (bf16[1024,256]{1,0:T(8,128)(2,1)}, bf16[1024,256]{1,0:T(8,128)(2,1)S(1)}, u32[]{:S(2)}, u32[]{:S(2)}) collective-permute-start(bf16[1024,256]{1,0:T(8,128)(2,1)} %refs_0_.2), channel_id=1, source_target_pairs={{0,1},{1,0},{2,3},{3,2},{4,5},{5,4},{6,7},{7,6},{8,9},{9,8},{10,11... | collective-permute-start | bytes 1572872 | tf_op jit(solution)/shard_map/ppermute | solution.py:1093
  29.5 42.2 %collective-permute-start.7 = (bf16[256,1024]{1,0:T(8,128)(2,1)}, bf16[256,1024]{1,0:T(8,128)(2,1)}, u32[]{:S(2)}, u32[]{:S(2)}) collective-permute-start(bf16[256,1024]{1,0:T(8,128)(2,1)} %refs_6_.1), channel_id=1, source_target_pairs={{0,1},{1,0},{2,3},{3,2},{4,5},{5,4},{6,7},{7,6},{8,9},{9,8},{10,11... | collective-permute-start | bytes 1572872 | tf_op jit(solution)/shard_map/ppermute | solution.py:1093
  34.5 35.6 %collective-permute-start.4 = (bf16[128,1024]{1,0:T(8,128)(2,1)S(1)}, bf16[128,1024]{1,0:T(8,128)(2,1)}, u32[]{:S(2)}, u32[]{:S(2)}) collective-permute-start(bf16[128,1024]{1,0:T(8,128)(2,1)S(1)} %constant_dynamic-slice_fusion.12), channel_id=1, source_target_pairs={{0,2},{2,0},{1,3},{3,1},{4,6},{6,4},{5,7},{7,5},{8,10},{10,8},{9,1... | collective-permute-start | bytes 786440 | tf_op jit(solution)/shard_map/ppermute | solution.py:1096
  40.1 42.0 %collective-permute-start.8 = (bf16[3,1024,128]{2,1,0:T(8,128)(2,1)}, bf16[3,1024,128]{2,1,0:T(8,128)(2,1)S(1)}, u32[]{:S(2)}, u32[]{:S(2)}) collective-permute-start(bf16[3,1024,128]{2,1,0:T(8,128)(2,1)} %collective-permute-done.1.weight_ref.refs_10_), channel_id=1, source_target_pairs={{0,8},{4,12},{8,0},{12,4},{16,24},{20,28},{24,16},{28,20},{1,9},{5... | collective-permute-start | bytes 2359304 | tf_op jit(solution)/shard_map/ppermute | solution.py:1099
  70.1 12.0 %collective-permute-start.9 = (bf16[2,64,256]{2,1,0:T(8,128)(2,1)S(1)}, bf16[2,64,256]{2,1,0:T(8,128)(2,1)S(1)}, u32[]{:S(2)}, u32[]{:S(2)}) collective-permute-start(bf16[2,64,256]{2,1,0:T(8,128)(2,1)S(1)} %get-tuple-element.545), channel_id=1, source_target_pairs={{0,2},{2,0},{1,3},{3,1},{4,6},{6,4},{5,7},{7,5},{8,10},{10,8},{9,1... | collective-permute-start | bytes 196616 | tf_op jit(solution)/shard_map/ppermute | solution.py:1096
  71.7 12.2 %collective-permute-start.10 = (bf16[832,256]{1,0:T(8,128)(2,1)S(1)}, bf16[832,256]{1,0:T(8,128)(2,1)}, u32[]{:S(2)}, u32[]{:S(2)}) collective-permute-start(bf16[832,256]{1,0:T(8,128)(2,1)S(1)} %constant_dynamic-slice_fusion.11), channel_id=1, source_target_pairs={{0,1},{1,0},{2,3},{3,2},{4,5},{5,4},{6,7},{7,6},{8,9},{9,8},{10,11... | collective-permute-start | bytes 1277960 | tf_op jit(solution)/shard_map/ppermute | solution.py:1093
  71.9 28.7 %collective-permute-start.14 = (bf16[1024,512]{1,0:T(8,128)(2,1)S(1)}, bf16[1024,512]{1,0:T(8,128)(2,1)}, u32[]{:S(2)}, u32[]{:S(2)}) collective-permute-start(bf16[1024,512]{1,0:T(8,128)(2,1)S(1)} %constant_dynamic-slice_fusion.10), channel_id=1, source_target_pairs={{0,2},{2,0},{1,3},{3,1},{4,6},{6,4},{5,7},{7,5},{8,10},{10,8},{9,1... | collective-permute-start | bytes 3145736 | tf_op jit(solution)/shard_map/ppermute | solution.py:1096
  72.5 17.7 %collective-permute-start.11 = (bf16[128,1024]{1,0:T(8,128)(2,1)}, bf16[128,1024]{1,0:T(8,128)(2,1)S(1)}, u32[]{:S(2)}, u32[]{:S(2)}) collective-permute-start(bf16[128,1024]{1,0:T(8,128)(2,1)} %collective-permute-done.2.refs_7_.refs_0_), channel_id=1, source_target_pairs={{0,8},{4,12},{8,0},{12,4},{16,24},{20,28},{24,16},{28,20},{1,9},{5... | collective-permute-start | bytes 786440 | tf_op jit(solution)/shard_map/ppermute | solution.py:1099
  82.0 21.8 %collective-permute-start.18 = (bf16[128,1024]{1,0:T(8,128)(2,1)}, bf16[128,1024]{1,0:T(8,128)(2,1)}, u32[]{:S(2)}, u32[]{:S(2)}) collective-permute-start(bf16[128,1024]{1,0:T(8,128)(2,1)} %collective-permute-done.2.refs_7_.refs_0_), channel_id=1, source_target_pairs={{0,1},{1,0},{2,3},{3,2},{4,5},{5,4},{6,7},{7,6},{8,9},{9,8},{10,11... | collective-permute-start | bytes 786440 | tf_op jit(solution)/shard_map/ppermute | solution.py:1093
  83.9 16.0 %collective-permute-start.13 = (bf16[128,1024]{1,0:T(8,128)(2,1)}, bf16[128,1024]{1,0:T(8,128)(2,1)S(1)}, u32[]{:S(2)}, u32[]{:S(2)}) collective-permute-start(bf16[128,1024]{1,0:T(8,128)(2,1)} %collective-permute-done.4.refs_19_.refs_7_), channel_id=1, source_target_pairs={{0,4},{4,0},{8,12},{12,8},{16,20},{20,16},{24,28},{28,24},{1,5},{5... | collective-permute-start | bytes 786440 | tf_op jit(solution)/shard_map/ppermute | solution.py:1099
  102.1 27.3 %collective-permute-start.24 = (bf16[1024,512]{1,0:T(8,128)(2,1)}, bf16[1024,512]{1,0:T(8,128)(2,1)S(1)}, u32[]{:S(2)}, u32[]{:S(2)}) collective-permute-start(bf16[1024,512]{1,0:T(8,128)(2,1)} %collective-permute-done.14.refs_0_), channel_id=1, source_target_pairs={{0,4},{4,0},{8,12},{12,8},{16,20},{20,16},{24,28},{28,24},{1,5},{5... | collective-permute-start | bytes 3145736 | tf_op jit(solution)/shard_map/ppermute | solution.py:1099
  103.9 25.6 %collective-permute-start.25 = (bf16[512,1024]{1,0:T(8,128)(2,1)}, bf16[512,1024]{1,0:T(8,128)(2,1)S(1)}, u32[]{:S(2)}, u32[]{:S(2)}) collective-permute-start(bf16[512,1024]{1,0:T(8,128)(2,1)} %constant_dynamic-slice_fusion.9), channel_id=1, source_target_pairs={{0,2},{2,0},{1,3},{3,1},{4,6},{6,4},{5,7},{7,5},{8,10},{10,8},{9,1... | collective-permute-start | bytes 3145736 | tf_op jit(solution)/shard_map/ppermute | solution.py:1096
  130.5 13.2 %collective-permute-start.26 = (bf16[832,1024]{1,0:T(8,128)(2,1)}, bf16[832,1024]{1,0:T(8,128)(2,1)S(1)}, u32[]{:S(2)}, u32[]{:S(2)}) collective-permute-start(bf16[832,1024]{1,0:T(8,128)(2,1)} %get-tuple-element.311.h_ref.mine_ref), channel_id=1, source_target_pairs={{0,1},{1,0},{2,3},{3,2},{4,5},{5,4},{6,7},{7,6},{8,9},{9,8},{10,11... | collective-permute-start | bytes 5111816 | tf_op jit(solution)/shard_map/ppermute | solution.py:1093
  130.7 13.0 %collective-permute-start.27 = (bf16[832,1024]{1,0:T(8,128)(2,1)S(1)}, bf16[832,1024]{1,0:T(8,128)(2,1)S(1)}, u32[]{:S(2)}, u32[]{:S(2)}) collective-permute-start(bf16[832,1024]{1,0:T(8,128)(2,1)S(1)} %broadcast_select_fusion.d_ref.mine_ref), channel_id=1, source_target_pairs={{0,1},{1,0},{2,3},{3,2},{4,5},{5,4},{6,7},{7,6},{8,9},{9,8},{10,11... | collective-permute-start | bytes 5111816 | tf_op jit(solution)/shard_map/ppermute | solution.py:1093
  131.0 26.5 %collective-permute-start.28 = (bf16[512,1024]{1,0:T(8,128)(2,1)}, bf16[512,1024]{1,0:T(8,128)(2,1)}, u32[]{:S(2)}, u32[]{:S(2)}) collective-permute-start(bf16[512,1024]{1,0:T(8,128)(2,1)} %copy-done.105), channel_id=1, source_target_pairs={{0,4},{4,0},{8,12},{12,8},{16,20},{20,16},{24,28},{28,24},{1,5},{5... | collective-permute-start | bytes 3145736 | tf_op jit(solution)/shard_map/ppermute | solution.py:1099
  171.1 29.4 %collective-permute-start.29 = (bf16[832,1024]{1,0:T(8,128)(2,1)}, bf16[832,1024]{1,0:T(8,128)(2,1)S(1)}, u32[]{:S(2)}, u32[]{:S(2)}) collective-permute-start(bf16[832,1024]{1,0:T(8,128)(2,1)} %get-tuple-element.323), channel_id=1, source_target_pairs={{0,1},{1,0},{2,3},{3,2},{4,5},{5,4},{6,7},{7,6},{8,9},{9,8},{10,11... | collective-permute-start | bytes 5111816 | tf_op jit(solution)/shard_map/ppermute | solution.py:1093
  192.2 48.3 %collective-permute-start.31 = (bf16[1024,1024]{1,0:T(8,128)(2,1)}, bf16[1024,1024]{1,0:T(8,128)(2,1)}, u32[]{:S(2)}, u32[]{:S(2)}) collective-permute-start(bf16[1024,1024]{1,0:T(8,128)(2,1)} %up_grad.2), channel_id=1, source_target_pairs={{0,2},{2,0},{1,3},{3,1},{4,6},{6,4},{5,7},{7,5},{8,10},{10,8},{9,1... | collective-permute-start | bytes 6291464 | tf_op jit(solution)/shard_map/ppermute | solution.py:1096
  224.6 15.9 %collective-permute-start.32 = (bf16[832,1024]{1,0:T(8,128)(2,1)}, bf16[832,1024]{1,0:T(8,128)(2,1)S(1)}, u32[]{:S(2)}, u32[]{:S(2)}) collective-permute-start(bf16[832,1024]{1,0:T(8,128)(2,1)} %get-tuple-element.360.mine_ref.refs_2_.refs_1_), channel_id=1, source_target_pairs={{0,1},{1,0},{2,3},{3,2},{4,5},{5,4},{6,7},{7,6},{8,9},{9,8},{10,11... | collective-permute-start | bytes 5111816 | tf_op jit(solution)/shard_map/ppermute | solution.py:1093
  224.9 42.3 %collective-permute-start.35 = (bf16[832,1024]{1,0:T(8,128)(2,1)}, bf16[832,1024]{1,0:T(8,128)(2,1)}, u32[]{:S(2)}, u32[]{:S(2)}) collective-permute-start(bf16[832,1024]{1,0:T(8,128)(2,1)} %get-tuple-element.357.mine_ref), channel_id=1, source_target_pairs={{0,1},{1,0},{2,3},{3,2},{4,5},{5,4},{6,7},{7,6},{8,9},{9,8},{10,11... | collective-permute-start | bytes 5111816 | tf_op jit(solution)/shard_map/ppermute | solution.py:1093
  246.9 20.4 %collective-permute-start.34 = (bf16[832,512]{1,0:T(8,128)(2,1)}, bf16[832,512]{1,0:T(8,128)(2,1)S(1)}, u32[]{:S(2)}, u32[]{:S(2)}) collective-permute-start(bf16[832,512]{1,0:T(8,128)(2,1)} %slice.78), channel_id=1, source_target_pairs={{0,1},{1,0},{2,3},{3,2},{4,5},{5,4},{6,7},{7,6},{8,9},{9,8},{10,11... | collective-permute-start | bytes 2555912 | tf_op jit(solution)/shard_map/ppermute | solution.py:1093
  246.9 56.0 %collective-permute-start.33 = (bf16[1024,1024]{1,0:T(8,128)(2,1)}, bf16[1024,1024]{1,0:T(8,128)(2,1)}, u32[]{:S(2)}, u32[]{:S(2)}) collective-permute-start(bf16[1024,1024]{1,0:T(8,128)(2,1)} %down_grad.2), channel_id=1, source_target_pairs={{0,2},{2,0},{1,3},{3,1},{4,6},{6,4},{5,7},{7,5},{8,10},{10,8},{9,1... | collective-permute-start | bytes 6291464 | tf_op jit(solution)/shard_map/ppermute | solution.py:1096
  248.8 18.5 %collective-permute-start.36 = (f32[2,2,64,256]{3,2,0,1:T(8,128)}, f32[2,2,64,256]{3,2,0,1:T(8,128)}, u32[]{:S(2)}, u32[]{:S(2)}) collective-permute-start(f32[2,2,64,256]{3,2,0,1:T(8,128)} %get-tuple-element.537), channel_id=1, source_target_pairs={{0,1},{1,0},{2,3},{3,2},{4,5},{5,4},{6,7},{7,6},{8,9},{9,8},{10,11... | collective-permute-start | bytes 786440 | tf_op jit(solution)/shard_map/ppermute | solution.py:1093
  249.0 36.0 %collective-permute-start.37 = (bf16[512,1024]{1,0:T(8,128)(2,1)}, bf16[512,1024]{1,0:T(8,128)(2,1)}, u32[]{:S(2)}, u32[]{:S(2)}) collective-permute-start(bf16[512,1024]{1,0:T(8,128)(2,1)} %get-tuple-element.524), channel_id=1, source_target_pairs={{0,4},{4,0},{8,12},{12,8},{16,20},{20,16},{24,28},{28,24},{1,5},{5... | collective-permute-start | bytes 3145736 | tf_op jit(solution)/shard_map/ppermute | solution.py:1099
  267.2 82.4 %collective-permute-start.40 = (bf16[832,1024]{1,0:T(8,128)(2,1)}, bf16[832,1024]{1,0:T(8,128)(2,1)}, u32[]{:S(2)}, u32[]{:S(2)}) collective-permute-start(bf16[832,1024]{1,0:T(8,128)(2,1)} %get-tuple-element.445.refs_6_.refs_5_), channel_id=1, source_target_pairs={{0,1},{1,0},{2,3},{3,2},{4,5},{5,4},{6,7},{7,6},{8,9},{9,8},{10,11... | collective-permute-start | bytes 5111816 | tf_op jit(solution)/shard_map/ppermute | solution.py:1093
  307.0 34.6 %collective-permute-start.42 = (bf16[512,1024]{1,0:T(8,128)(2,1)}, bf16[512,1024]{1,0:T(8,128)(2,1)}, u32[]{:S(2)}, u32[]{:S(2)}) collective-permute-start(bf16[512,1024]{1,0:T(8,128)(2,1)} %get-tuple-element.522), channel_id=1, source_target_pairs={{0,4},{4,0},{8,12},{12,8},{16,20},{20,16},{24,28},{28,24},{1,5},{5... | collective-permute-start | bytes 3145736 | tf_op jit(solution)/shard_map/ppermute | solution.py:1099
  307.6 63.2 %collective-permute-start.38 = (bf16[3072,256]{1,0:T(8,128)(2,1)}, bf16[3072,256]{1,0:T(8,128)(2,1)}, u32[]{:S(2)}, u32[]{:S(2)}) collective-permute-start(bf16[3072,256]{1,0:T(8,128)(2,1)} %qkv_grad.2), channel_id=1, source_target_pairs={{0,2},{2,0},{1,3},{3,1},{4,6},{6,4},{5,7},{7,5},{8,10},{10,8},{9,1... | collective-permute-start | bytes 4718600 | tf_op jit(solution)/shard_map/ppermute | solution.py:1096
  310.7 28.3 %collective-permute-start.39 = (bf16[256,1024]{1,0:T(8,128)(2,1)}, bf16[256,1024]{1,0:T(8,128)(2,1)}, u32[]{:S(2)}, u32[]{:S(2)}) collective-permute-start(bf16[256,1024]{1,0:T(8,128)(2,1)} %dynamic-slice_convert_fusion.1), channel_id=1, source_target_pairs={{0,8},{4,12},{8,0},{12,4},{16,24},{20,28},{24,16},{28,20},{1,9},{5... | collective-permute-start | bytes 1572872 | tf_op jit(solution)/shard_map/ppermute | solution.py:1099
  316.0 30.9 %collective-permute-start.41 = (bf16[832,512]{1,0:T(8,128)(2,1)}, bf16[832,512]{1,0:T(8,128)(2,1)}, u32[]{:S(2)}, u32[]{:S(2)}) collective-permute-start(bf16[832,512]{1,0:T(8,128)(2,1)} %slice.84), channel_id=1, source_target_pairs={{0,1},{1,0},{2,3},{3,2},{4,5},{5,4},{6,7},{7,6},{8,9},{9,8},{10,11... | collective-permute-start | bytes 2555912 | tf_op jit(solution)/shard_map/ppermute | solution.py:1093
  339.0 124.2 %collective-permute-start.30 = (bf16[832,1024]{1,0:T(8,128)(2,1)}, bf16[832,1024]{1,0:T(8,128)(2,1)}, u32[]{:S(2)}, u32[]{:S(2)}) collective-permute-start(bf16[832,1024]{1,0:T(8,128)(2,1)} %get-tuple-element.336), channel_id=1, source_target_pairs={{0,1},{1,0},{2,3},{3,2},{4,5},{5,4},{6,7},{7,6},{8,9},{9,8},{10,11... | collective-permute-start | bytes 5111816 | tf_op jit(solution)/shard_map/ppermute | solution.py:1093
  341.6 36.3 %collective-permute-start.44 = (bf16[1024,256]{1,0:T(8,128)(2,1)S(1)}, bf16[1024,256]{1,0:T(8,128)(2,1)}, u32[]{:S(2)}, u32[]{:S(2)}) collective-permute-start(bf16[1024,256]{1,0:T(8,128)(2,1)S(1)} %copy-done.64), channel_id=1, source_target_pairs={{0,2},{2,0},{1,3},{3,1},{4,6},{6,4},{5,7},{7,5},{8,10},{10,8},{9,1... | collective-permute-start | bytes 1572872 | tf_op jit(solution)/shard_map/ppermute | solution.py:1096
  346.9 33.2 %collective-permute-start.48 = (bf16[256,1024]{1,0:T(8,128)(2,1)}, bf16[256,1024]{1,0:T(8,128)(2,1)}, u32[]{:S(2)}, u32[]{:S(2)}) collective-permute-start(bf16[256,1024]{1,0:T(8,128)(2,1)} %add_convert_fusion.9), channel_id=1, source_target_pairs={{0,16},{4,20},{8,24},{12,28},{16,0},{20,4},{24,8},{28,12},{1,17},{... | collective-permute-start | bytes 1572872 | tf_op jit(solution)/shard_map/ppermute | solution.py:1099
  349.6 27.8 %collective-permute-start.45 = (bf16[2,64,256]{2,1,0:T(8,128)(2,1)S(1)}, bf16[2,64,256]{2,1,0:T(8,128)(2,1)S(1)}, u32[]{:S(2)}, u32[]{:S(2)}) collective-permute-start(bf16[2,64,256]{2,1,0:T(8,128)(2,1)S(1)} %copy-done.125), channel_id=1, source_target_pairs={{0,2},{2,0},{1,3},{3,1},{4,6},{6,4},{5,7},{7,5},{8,10},{10,8},{9,1... | collective-permute-start | bytes 196616 | tf_op jit(solution)/shard_map/ppermute | solution.py:1096
  370.8 40.3 %collective-permute-start.49 = (bf16[832,1024]{1,0:T(8,128)(2,1)}, bf16[832,1024]{1,0:T(8,128)(2,1)}, u32[]{:S(2)}, u32[]{:S(2)}) collective-permute-start(bf16[832,1024]{1,0:T(8,128)(2,1)} %first_back.2), channel_id=1, source_target_pairs={{0,1},{1,0},{2,3},{3,2},{4,5},{5,4},{6,7},{7,6},{8,9},{9,8},{10,11... | collective-permute-start | bytes 5111816 | tf_op jit(solution)/shard_map/ppermute | solution.py:1093
  377.4 41.8 %collective-permute-start.47 = (bf16[256,1024]{1,0:T(8,128)(2,1)}, bf16[256,1024]{1,0:T(8,128)(2,1)}, u32[]{:S(2)}, u32[]{:S(2)}) collective-permute-start(bf16[256,1024]{1,0:T(8,128)(2,1)} %dynamic-slice_convert_fusion), channel_id=1, source_target_pairs={{0,8},{4,12},{8,0},{12,4},{16,24},{20,28},{24,16},{28,20},{1,9},{5... | collective-permute-start | bytes 1572872 | tf_op jit(solution)/shard_map/ppermute | solution.py:1099
  380.9 28.3 %collective-permute-start.43 = (bf16[1536,256]{1,0:T(8,128)(2,1)S(1)}, bf16[1536,256]{1,0:T(8,128)(2,1)S(1)}, u32[]{:S(2)}, u32[]{:S(2)}) collective-permute-start(bf16[1536,256]{1,0:T(8,128)(2,1)S(1)} %copy-done.107), channel_id=1, source_target_pairs={{0,8},{4,12},{8,0},{12,4},{16,24},{20,28},{24,16},{28,20},{1,9},{5... | collective-permute-start | bytes 2359304 | tf_op jit(solution)/shard_map/ppermute | solution.py:1099
  383.9 37.7 %collective-permute-start.54 = (bf16[256,1024]{1,0:T(8,128)(2,1)S(1)}, bf16[256,1024]{1,0:T(8,128)(2,1)S(1)}, u32[]{:S(2)}, u32[]{:S(2)}) collective-permute-start(bf16[256,1024]{1,0:T(8,128)(2,1)S(1)} %add_convert_fusion.7), channel_id=1, source_target_pairs={{0,8},{4,12},{8,0},{12,4},{16,24},{20,28},{24,16},{28,20},{1,9},{5... | collective-permute-start | bytes 1572872 | tf_op jit(solution)/shard_map/ppermute | solution.py:1099
  409.2 18.6 %collective-permute-start.53 = (bf16[1536,256]{1,0:T(8,128)(2,1)S(1)}, bf16[1536,256]{1,0:T(8,128)(2,1)S(1)}, u32[]{:S(2)}, u32[]{:S(2)}) collective-permute-start(bf16[1536,256]{1,0:T(8,128)(2,1)S(1)} %get-tuple-element.532), channel_id=1, source_target_pairs={{0,4},{4,0},{8,12},{12,8},{16,20},{20,16},{24,28},{28,24},{1,5},{5... | collective-permute-start | bytes 2359304 | tf_op jit(solution)/shard_map/ppermute | solution.py:1099
  411.1 26.2 %collective-permute-start.52 = (bf16[512,1024]{1,0:T(8,128)(2,1)S(1)}, bf16[512,1024]{1,0:T(8,128)(2,1)S(1)}, u32[]{:S(2)}, u32[]{:S(2)}) collective-permute-start(bf16[512,1024]{1,0:T(8,128)(2,1)S(1)} %outputs_grad.2), channel_id=1, source_target_pairs={{0,2},{2,0},{1,3},{3,1},{4,6},{6,4},{5,7},{7,5},{8,10},{10,8},{9,1... | collective-permute-start | bytes 3145736 | tf_op jit(solution)/shard_map/ppermute | solution.py:1096
  420.4 34.9 %collective-permute-start.58 = (f32[64,1024]{1,0:T(8,128)S(1)}, f32[64,1024]{1,0:T(8,128)S(1)}, u32[]{:S(2)}, u32[]{:S(2)}) collective-permute-start(f32[64,1024]{1,0:T(8,128)S(1)} %get-tuple-element.534), channel_id=1, source_target_pairs={{0,2},{2,0},{1,3},{3,1},{4,6},{6,4},{5,7},{7,5},{8,10},{10,8},{9,1... | collective-permute-start | bytes 786440 | tf_op jit(solution)/shard_map/ppermute | solution.py:1096
  421.5 26.2 %collective-permute-start.50 = (bf16[256,1024]{1,0:T(8,128)(2,1)S(1)}, bf16[256,1024]{1,0:T(8,128)(2,1)S(1)}, u32[]{:S(2)}, u32[]{:S(2)}) collective-permute-start(bf16[256,1024]{1,0:T(8,128)(2,1)S(1)} %add_convert_fusion.6), channel_id=1, source_target_pairs={{0,16},{4,20},{8,24},{12,28},{16,0},{20,4},{24,8},{28,12},{1,17},{... | collective-permute-start | bytes 1572872 | tf_op jit(solution)/shard_map/ppermute | solution.py:1099
  427.8 13.6 %collective-permute-start.56 = (f32[8,1024]{1,0:T(8,128)S(1)}, f32[8,1024]{1,0:T(8,128)S(1)}, u32[]{:S(2)}, u32[]{:S(2)}) collective-permute-start(f32[8,1024]{1,0:T(8,128)S(1)} %add.248), channel_id=1, source_target_pairs={{0,2},{2,0},{1,3},{3,1},{4,6},{6,4},{5,7},{7,5},{8,10},{10,8},{9,1... | collective-permute-start | bytes 98312 | tf_op jit(solution)/shard_map/ppermute | solution.py:1096
  437.2 18.0 %collective-permute-start.59 = (bf16[768,256]{1,0:T(8,128)(2,1)S(1)}, bf16[768,256]{1,0:T(8,128)(2,1)S(1)}, u32[]{:S(2)}, u32[]{:S(2)}) collective-permute-start(bf16[768,256]{1,0:T(8,128)(2,1)S(1)} %dynamic-slice_convert_fusion.2), channel_id=1, source_target_pairs={{0,8},{4,12},{8,0},{12,4},{16,24},{20,28},{24,16},{28,20},{1,9},{5... | collective-permute-start | bytes 1179656 | tf_op jit(solution)/shard_map/ppermute | solution.py:1099
  441.4 21.6 %collective-permute-start.46 = (bf16[768,256]{1,0:T(8,128)(2,1)S(1)}, bf16[768,256]{1,0:T(8,128)(2,1)S(1)}, u32[]{:S(2)}, u32[]{:S(2)}) collective-permute-start(bf16[768,256]{1,0:T(8,128)(2,1)S(1)} %dynamic-slice_convert_fusion.4), channel_id=1, source_target_pairs={{0,4},{4,0},{8,12},{12,8},{16,20},{20,16},{24,28},{28,24},{1,5},{5... | collective-permute-start | bytes 1179656 | tf_op jit(solution)/shard_map/ppermute | solution.py:1099
  447.8 14.8 %collective-permute-start.55 = (bf16[256,1024]{1,0:T(8,128)(2,1)S(1)}, bf16[256,1024]{1,0:T(8,128)(2,1)S(1)}, u32[]{:S(2)}, u32[]{:S(2)}) collective-permute-start(bf16[256,1024]{1,0:T(8,128)(2,1)S(1)} %get-tuple-element.531), channel_id=1, source_target_pairs={{0,4},{4,0},{8,12},{12,8},{16,20},{20,16},{24,28},{28,24},{1,5},{5... | collective-permute-start | bytes 1572872 | tf_op jit(solution)/shard_map/ppermute | solution.py:1099
  455.3 38.3 %collective-permute-start.67 = (bf16[512,1024]{1,0:T(8,128)(2,1)S(1)}, bf16[512,1024]{1,0:T(8,128)(2,1)S(1)}, u32[]{:S(2)}, u32[]{:S(2)}) collective-permute-start(bf16[512,1024]{1,0:T(8,128)(2,1)S(1)} %maximum_select_fusion.4), channel_id=1, source_target_pairs={{0,4},{4,0},{8,12},{12,8},{16,20},{20,16},{24,28},{28,24},{1,5},{5... | collective-permute-start | bytes 3145736 | tf_op jit(solution)/shard_map/ppermute | solution.py:1099
  459.1 15.7 %collective-permute-start.62 = (bf16[256,1024]{1,0:T(8,128)(2,1)S(1)}, bf16[256,1024]{1,0:T(8,128)(2,1)S(1)}, u32[]{:S(2)}, u32[]{:S(2)}) collective-permute-start(bf16[256,1024]{1,0:T(8,128)(2,1)S(1)} %add_convert_fusion.4), channel_id=1, source_target_pairs={{0,8},{4,12},{8,0},{12,4},{16,24},{20,28},{24,16},{28,20},{1,9},{5... | collective-permute-start | bytes 1572872 | tf_op jit(solution)/shard_map/ppermute | solution.py:1099
  462.6 28.8 %collective-permute-start.61 = (bf16[768,256]{1,0:T(8,128)(2,1)S(1)}, bf16[768,256]{1,0:T(8,128)(2,1)S(1)}, u32[]{:S(2)}, u32[]{:S(2)}) collective-permute-start(bf16[768,256]{1,0:T(8,128)(2,1)S(1)} %add_convert_fusion.13), channel_id=1, source_target_pairs={{0,16},{4,20},{8,24},{12,28},{16,0},{20,4},{24,8},{28,12},{1,17},{... | collective-permute-start | bytes 1179656 | tf_op jit(solution)/shard_map/ppermute | solution.py:1099
  463.0 28.5 %collective-permute-start.60 = (f32[64,1024]{1,0:T(8,128)S(1)}, f32[64,1024]{1,0:T(8,128)S(1)}, u32[]{:S(2)}, u32[]{:S(2)}) collective-permute-start(f32[64,1024]{1,0:T(8,128)S(1)} %add.259), channel_id=1, source_target_pairs={{0,1},{1,0},{2,3},{3,2},{4,5},{5,4},{6,7},{7,6},{8,9},{9,8},{10,11... | collective-permute-start | bytes 786440 | tf_op jit(solution)/shard_map/ppermute | solution.py:1093
  463.2 42.9 %collective-permute-start.65 = (f32[8,1024]{1,0:T(8,128)S(1)}, f32[8,1024]{1,0:T(8,128)S(1)}, u32[]{:S(2)}, u32[]{:S(2)}) collective-permute-start(f32[8,1024]{1,0:T(8,128)S(1)} %add.260), channel_id=1, source_target_pairs={{0,16},{4,20},{8,24},{12,28},{16,0},{20,4},{24,8},{28,12},{1,17},{... | collective-permute-start | bytes 98312 | tf_op jit(solution)/shard_map/ppermute | solution.py:1099
  474.9 31.3 %collective-permute-start.64 = (bf16[768,256]{1,0:T(8,128)(2,1)S(1)}, bf16[768,256]{1,0:T(8,128)(2,1)S(1)}, u32[]{:S(2)}, u32[]{:S(2)}) collective-permute-start(bf16[768,256]{1,0:T(8,128)(2,1)S(1)} %add_convert_fusion.12), channel_id=1, source_target_pairs={{0,16},{4,20},{8,24},{12,28},{16,0},{20,4},{24,8},{28,12},{1,17},{... | collective-permute-start | bytes 1179656 | tf_op jit(solution)/shard_map/ppermute | solution.py:1099
  491.4 13.4 %collective-permute-start.66 = (bf16[128,1024]{1,0:T(8,128)(2,1)S(1)}, bf16[128,1024]{1,0:T(8,128)(2,1)S(1)}, u32[]{:S(2)}, u32[]{:S(2)}) collective-permute-start(bf16[128,1024]{1,0:T(8,128)(2,1)S(1)} %dynamic-slice_convert_fusion.5), channel_id=1, source_target_pairs={{0,8},{4,12},{8,0},{12,4},{16,24},{20,28},{24,16},{28,20},{1,9},{5... | collective-permute-start | bytes 786440 | tf_op jit(solution)/shard_map/ppermute | solution.py:1099
  491.5 21.7 %collective-permute-start.70 = (bf16[768,256]{1,0:T(8,128)(2,1)S(1)}, bf16[768,256]{1,0:T(8,128)(2,1)S(1)}, u32[]{:S(2)}, u32[]{:S(2)}) collective-permute-start(bf16[768,256]{1,0:T(8,128)(2,1)S(1)} %add_convert_fusion.11), channel_id=1, source_target_pairs={{0,8},{4,12},{8,0},{12,4},{16,24},{20,28},{24,16},{28,20},{1,9},{5... | collective-permute-start | bytes 1179656 | tf_op jit(solution)/shard_map/ppermute | solution.py:1099
  493.6 26.8 %collective-permute-start.72 = (bf16[512,1024]{1,0:T(8,128)(2,1)S(1)}, bf16[512,1024]{1,0:T(8,128)(2,1)S(1)}, u32[]{:S(2)}, u32[]{:S(2)}) collective-permute-start(bf16[512,1024]{1,0:T(8,128)(2,1)S(1)} %maximum_select_fusion.5), channel_id=1, source_target_pairs={{0,4},{4,0},{8,12},{12,8},{16,20},{20,16},{24,28},{28,24},{1,5},{5... | collective-permute-start | bytes 3145736 | tf_op jit(solution)/shard_map/ppermute | solution.py:1099
  504.8 28.6 %collective-permute-start.63 = (bf16[64,1024]{1,0:T(8,128)(2,1)S(1)}, bf16[64,1024]{1,0:T(8,128)(2,1)}, u32[]{:S(2)}, u32[]{:S(2)}) collective-permute-start(bf16[64,1024]{1,0:T(8,128)(2,1)S(1)} %add_convert_fusion.16), channel_id=1, source_target_pairs={{0,2},{2,0},{1,3},{3,1},{4,6},{6,4},{5,7},{7,5},{8,10},{10,8},{9,1... | collective-permute-start | bytes 393224 | tf_op jit(solution)/shard_map/ppermute | solution.py:1096
  506.1 13.4 %collective-permute-start.69 = (bf16[128,1024]{1,0:T(8,128)(2,1)S(1)}, bf16[128,1024]{1,0:T(8,128)(2,1)S(1)}, u32[]{:S(2)}, u32[]{:S(2)}) collective-permute-start(bf16[128,1024]{1,0:T(8,128)(2,1)S(1)} %add_convert_fusion.15), channel_id=1, source_target_pairs={{0,16},{4,20},{8,24},{12,28},{16,0},{20,4},{24,8},{28,12},{1,17},{... | collective-permute-start | bytes 786440 | tf_op jit(solution)/shard_map/ppermute | solution.py:1099
  506.2 23.8 %collective-permute-start.68 = (f32[8,1024]{1,0:T(8,128)S(1)}, f32[8,1024]{1,0:T(8,128)S(1)}, u32[]{:S(2)}, u32[]{:S(2)}) collective-permute-start(f32[8,1024]{1,0:T(8,128)S(1)} %add.269), channel_id=1, source_target_pairs={{0,4},{4,0},{8,12},{12,8},{16,20},{20,16},{24,28},{28,24},{1,5},{5... | collective-permute-start | bytes 98312 | tf_op jit(solution)/shard_map/ppermute | solution.py:1099
  513.2 12.0 %collective-permute-start.73 = (bf16[768,256]{1,0:T(8,128)(2,1)S(1)}, bf16[768,256]{1,0:T(8,128)(2,1)S(1)}, u32[]{:S(2)}, u32[]{:S(2)}) collective-permute-start(bf16[768,256]{1,0:T(8,128)(2,1)S(1)} %add_convert_fusion.10), channel_id=1, source_target_pairs={{0,4},{4,0},{8,12},{12,8},{16,20},{20,16},{24,28},{28,24},{1,5},{5... | collective-permute-start | bytes 1179656 | tf_op jit(solution)/shard_map/ppermute | solution.py:1099
  519.5 22.6 %collective-permute-start.75 = (bf16[1536,256]{1,0:T(8,128)(2,1)S(1)}, bf16[1536,256]{1,0:T(8,128)(2,1)S(1)}, u32[]{:S(2)}, u32[]{:S(2)}) collective-permute-start(bf16[1536,256]{1,0:T(8,128)(2,1)S(1)} %maximum_select_fusion.7), channel_id=1, source_target_pairs={{0,4},{4,0},{8,12},{12,8},{16,20},{20,16},{24,28},{28,24},{1,5},{5... | collective-permute-start | bytes 2359304 | tf_op jit(solution)/shard_map/ppermute | solution.py:1099
  520.5 14.6 %collective-permute-start.71 = (bf16[128,1024]{1,0:T(8,128)(2,1)S(1)}, bf16[128,1024]{1,0:T(8,128)(2,1)}, u32[]{:S(2)}, u32[]{:S(2)}) collective-permute-start(bf16[128,1024]{1,0:T(8,128)(2,1)S(1)} %add_convert_fusion.14), channel_id=1, source_target_pairs={{0,8},{4,12},{8,0},{12,4},{16,24},{20,28},{24,16},{28,20},{1,9},{5... | collective-permute-start | bytes 786440 | tf_op jit(solution)/shard_map/ppermute | solution.py:1099
  525.5 19.8 %collective-permute-start.76 = (bf16[1536,256]{1,0:T(8,128)(2,1)S(1)}, bf16[1536,256]{1,0:T(8,128)(2,1)S(1)}, u32[]{:S(2)}, u32[]{:S(2)}) collective-permute-start(bf16[1536,256]{1,0:T(8,128)(2,1)S(1)} %maximum_select_fusion.8), channel_id=1, source_target_pairs={{0,8},{4,12},{8,0},{12,4},{16,24},{20,28},{24,16},{28,20},{1,9},{5... | collective-permute-start | bytes 2359304 | tf_op jit(solution)/shard_map/ppermute | solution.py:1099
  536.3 16.4 %collective-permute-start.74 = (bf16[256,1024]{1,0:T(8,128)(2,1)S(1)}, bf16[256,1024]{1,0:T(8,128)(2,1)S(1)}, u32[]{:S(2)}, u32[]{:S(2)}) collective-permute-start(bf16[256,1024]{1,0:T(8,128)(2,1)S(1)} %maximum_select_fusion.9), channel_id=1, source_target_pairs={{0,4},{4,0},{8,12},{12,8},{16,20},{20,16},{24,28},{28,24},{1,5},{5... | collective-permute-start | bytes 1572872 | tf_op jit(solution)/shard_map/ppermute | solution.py:1099
  (145 other events, 1161.8 us)

commit v13 on v12

--- a/solution.py
+++ b/solution.py
@@ -813,7 +813,7 @@
         out_specs=pl.BlockSpec((tile, width), lambda i: (i, 0)),
         out_shape=shape((hidden, width), kind),
         compiler_params=params(48),
-        cost_estimate=lasting(0.750),
+        cost_estimate=lasting(3.50),
         name="down_grad",
     )(g, mine, other)
 
@@ -853,7 +853,7 @@
         ),
         out_shape=shape((3 * width, 256), kind),
         compiler_params=params(48),
-        cost_estimate=lasting(0.750),
+        cost_estimate=lasting(3.50),
         name="qkv_grad",
     )(place, h, *grads)
 
@@ -1304,8 +1304,8 @@
         def total(self):
             return store[self.kept] + store[self.fly]
 
-    up, down, outs, cross_in = Sum("up"), Sum("down"), Sum("outs"), Sum("cross_in")
-    qkv = Sum("qkv", (down_z, across))
+    up, down, outs, qkv = Sum("up"), Sum("down"), Sum("outs"), Sum("qkv")
+    cross_in = Sum("cross_in", (down_z, across))
     store.update(h3_other=h3_other, du1=du1, g1=g1, du0=du0, g0=g0, y_m=y_m, y_fly=y_received)
     store.update(of=of, o_s=o_s, o0=o0, x2=x2, h2_other=h2_other, ca_other=ca_other)
 
@@ -1355,12 +1355,13 @@
     pair_sum = lower(store["pair_kept"] + store["pair_fly"])
     store["pair"] = pair_sum[0]
     store["pair_other"] = cross_order(pair_sum[1])
+    up.second()
     step(
         ["dqs", "dks", "dvs"],
         lambda: self_back(limit, qs, ks, vs, store["o_s"], store["dos"], lse_s),
         "dos",
     )
-    up.second()
+    up.far()
     step(["down0"], lambda: down_grad(store["g0"], dout, dout_other, ROUND), "g0")
     yp = ("dqf", "dkf", "dvf", "dqs", "dks", "dvs")
     step(["qkv1"], lambda: qkv_grad(place, h1, get(*yp), ROUND), "dqs")
@@ -1374,8 +1375,8 @@
         lambda: self_back(limit, q0, k0, v0, store["o0"], store["do0"], lse0),
         "do0",
     )
-    up.far()
     down.second()
+    up.back()
     step(["outs1"], lambda: outof(1, "of", "o_s"), "dcross_other", "ca_other")
     outs.over_y("outs1")
     nine = ("dq0", "dk0", "dv0", *yp)
@@ -1384,6 +1385,8 @@
     store["yo_fly"] = over_core(store["yo"])
     step(["qkv0"], lambda: qkv_grad(place, h1, get("dq0", "dk0", "dv0"), ROUND), "dq0")
     qkv.first("qkv0")
+    up.along()
+    down.far()
     step(["query0"], lambda: query(0), "dcq")
     order("query0", "query_fly", "pair", "pair_y")
     other_text = lax.dynamic_index_in_dim(text_states, 1 - side, keepdims=False)
@@ -1398,19 +1401,18 @@
         axis=0,
     )
     cross_in.first_alone("into0")
-    up.back()
     step(["ym"], lambda: first_back(place, get(*nine), weights, FULL), "dq0")
     step(
         ["grad_frames", "first_sums"],
         lambda: frames_back(place, *get("ym", "yo_fly", "dx1"), frames, norm_gain),
         "ym",
         "yo_fly",
+        "outs_fly",
     )
     norms = Row("norms", store["sums"] + store["first_sums"], over_core)
-    down.far()
     norms.then(over_y)
-    up.along()
     cross_in.second()
+    qkv.second()
     step(["outs0"], lambda: outof(0, "o0"), "dcross")
     outs.first("outs0")
     norms.then(over_z)
@@ -1420,8 +1422,8 @@
     text_mine, text_theirs = text_part[:64], text_part[64:]
     text_rows = Row("texts", text_mine, lambda v: over_y(text_theirs))
     last[:] = ["texts_kept"]
-    qkv.second()
     down.back()
+    up.end("grad_up")
     cross_in.far()
     store["out_fly"] = over_core(out_o)
     text_rows.then(over_core)
@@ -1436,7 +1438,6 @@
     text_grad = lower(text_rows.total())
     text_away = over_y(text_grad)
     grad_text = ordered(text_grad[None], text_away[None], side)
-    up.end("grad_up")
     outs.far()
     norms.then(over_x)
     qkv.back()

time: 560 us -> 542 us (0.968)
  waiting for transfers between devices: 122 us -> 101 us
  starting transfers between devices: 56.7 us -> 68.5 us
  local copies, waits for them, and re-layouts: 56.8 us -> 46.3 us
    ppermute x34, waiting for transfers between devices: 97.6 us -> 79.8 us  [along_wide(): return lax.ppermute(v, 'wide', pairs)]
    ppermute x34, starting transfers between devices: 31.6 us -> 43.8 us  [along_wide(): return lax.ppermute(v, 'wide', pairs)]
    convert_element_type x16 -> x15, other arithmetic: 19.6 us -> 12.3 us  [lower(): return values_in.astype(jnp.bfloat16)]
    unnamed x265 -> x269, local copies, waits for them, and re-layouts: 29.7 us -> 24.5 us
  transfers between devices with their start and end apart: 77 -> 77, of which waited for: 24 -> 23; matrix products, arithmetic and copies ran while one was open for 13% -> 12% of each run, Pallas kernels for 46% -> 48%
where the time goes in v13:
time: 542 us; the launch traced here: 538 us
  Pallas kernels  270 us (50%)
  waiting for transfers between devices  101 us (19%)
  starting transfers between devices  68.5 us (13%)
  other arithmetic  46.9 us (9%)
  local copies, waits for them, and re-layouts  46.3 us (9%)
    ppermute x34, waiting for transfers between devices, along_wide(): return lax.ppermute(v, 'wide', pairs)  79.8 us
    pallas_call x4, Pallas kernels, feed(): pl.pallas_call(functools.partial(feed_kernel, parts=parts, carried=len(be...  51.6 us
    ppermute x34, starting transfers between devices, along_wide(): return lax.ppermute(v, 'wide', pairs)  43.8 us
    pallas_call x3, Pallas kernels, self_back(): pl.pallas_call(functools.partial(self_back_kernel, span=span, floor=floor...  39.5 us
    pallas_call x3, Pallas kernels, self_forward(): pl.pallas_call(functools.partial(self_forward_kernel, span=span, floor=fl...  30.8 us
    unnamed x269, local copies, waits for them, and re-layouts  24.5 us
    pallas_call x1, Pallas kernels, middle_back(): pl.pallas_call(middle_back_kernel, grid_spec=pltpu.PrefetchScalarGridSpec...  23 us
    ppermute x16, waiting for transfers between devices, over_y(): return lax.ppermute(v, 'narrow', Y_PAIRS)  21 us
  transfers between devices with their start and end apart: 77, of which 23 were waited for; matrix products, arithmetic and copies ran while one was open for 12% of the time, Pallas kernels for 48%

profile of v13, /device:TPU:0, one launch (start us, length us, event | category | flops | bytes accessed | tf_op | source)
XLA Modules:
  0.0 537.6 jit_solution(1267166470445128242)
XLA Ops:
  1.2 2.1 constant_dynamic-slice_fusion.15
  3.2 2.6 collective-permute-start.1
  14.8 4.5 first_project.1
  22.1 2.2 collective-permute-done.1.weight_ref.refs_10_
  30.5 4.0 collective-permute-done.2.refs_7_.refs_0_
  34.5 1.8 collective-permute-start.4
  36.3 3.8 collective-permute-done.3.refs_13_.refs_1_
  40.1 1.8 collective-permute-start.8
  41.9 14.1 %self_forward.3 = (bf16[1664,256]{1,0:T(8,128)(2,1)}, f32[2,8,1664]{2,1,0:T(8,128)}) custom-call(s32[1]{0:T(128)} %dynamic_slice.129.limit_ref, bf16[1664,256]{1,0:T(8,128)(2,1)} %copy-done.56, bf16[1664,256]{1,0:T(8,128)(2,1)} %copy-done.58, bf16[1664,256]{1,0:T(8,128)(2,1)} %copy-done.60), custom_call_target="tpu_custom_call" | custom-call | flops 4701199872 | bytes 1000 | tf_op jit(solution)/shard_map/self_forward/pallas_call | solution.py:525
  56.0 14.0 %project.2 = (bf16[1664,128]{1,0:T(8,128)(2,1)S(1)}, bf16[1664,128]{1,0:T(8,128)(2,1)S(1)}, bf16[1664,128]{1,0:T(8,128)(2,1)S(1)}) custom-call(s32[3]{0:T(128)S(1)} %add_add_fusion.place_ref, bf16[1664,1024]{1,0:T(8,128)(2,1)S(1)} %get-tuple-element.268.h_ref, bf16[3,1024,128]{2,1,0:T(8,128)(2,1)} %collective-permute-done.1.weight_ref.refs_10_), custom_call_target="tpu_custom_call" | custom-call | flops 1288000000 | bytes 1000 | tf_op jit(solution)/shard_map/project/pallas_call | solution.py:423
  73.8 8.3 %self_forward.4 = (bf16[1664,128]{1,0:T(8,128)(2,1)}, f32[1,8,1664]{2,1,0:T(8,128)}) custom-call(s32[1]{0:T(128)} %dynamic_slice.129.limit_ref, bf16[1664,128]{1,0:T(8,128)(2,1)} %copy-done.65, bf16[1664,128]{1,0:T(8,128)(2,1)} %copy-done.67, bf16[1664,128]{1,0:T(8,128)(2,1)} %copy-done.69), custom_call_target="tpu_custom_call" | custom-call | flops 2350599936 | bytes 1000 | tf_op jit(solution)/shard_map/self_forward/pallas_call | solution.py:525
  82.1 1.8 collective-permute-start.12
  85.2 2.7 project.3
  91.5 8.4 %self_forward.5 = (bf16[1664,128]{1,0:T(8,128)(2,1)}, f32[1,8,1664]{2,1,0:T(8,128)}) custom-call(s32[1]{0:T(128)} %dynamic_slice.129.limit_ref, bf16[1664,128]{1,0:T(8,128)(2,1)} %copy-done.71, bf16[1664,128]{1,0:T(8,128)(2,1)} %copy-done.73, bf16[1664,128]{1,0:T(8,128)(2,1)} %copy-done.75), custom_call_target="tpu_custom_call" | custom-call | flops 2350599936 | bytes 1000 | tf_op jit(solution)/shard_map/self_forward/pallas_call | solution.py:525
  102.1 1.8 collective-permute-start.24
  108.8 20.7 %middle_forward.1 = (f32[832,1024]{1,0:T(8,128)}, f32[832,1024]{1,0:T(8,128)}, bf16[832,1024]{1,0:T(8,128)(2,1)}, bf16[832,1024]{1,0:T(8,128)(2,1)}, bf16[832,10...) custom-call(s32[3]{0:T(128)} %copy-done.82, bf16[832,1024]{1,0:T(8,128)(2,1)} %frame_ref.3, ...), custom_call_target="tpu_custom_call" | custom-call | flops 7084000256 | bytes 1000 | tf_op jit(solution)/shard_map/middle_forward/pallas_call | solution.py:677
  131.5 12.1 %feed.4 = (bf16[1664,1024]{1,0:T(8,128)(2,1)}, bf16[1664,1024]{1,0:T(8,128)(2,1)}, f32[832,1024]{1,0:T(8,128)}, f32[832,1024]{1,0:T(8,128)}) custom-call(s32[3]{0:T(128)} %copy-done.82, bf16[832,1024]{1,0:T(8,128)(2,1)} %get-tuple-element.312.h_ref.mine_ref, bf16[832,1024]{1,0:T(8,128)(2,1)} %copy-done, bf16[1024,1024]{1,0:T(8,128)(2,1)} %refs_0_.1, ...), custom_call_target="tpu_custom_call" | custom-call | flops 4185999872 | bytes 1000 | tf_op jit(solution)/shard_map/feed/pallas_call | solution.py:756
  145.4 12.1 %feed.5 = (bf16[1664,1024]{1,0:T(8,128)(2,1)}, bf16[1664,1024]{1,0:T(8,128)(2,1)}, f32[832,1024]{1,0:T(8,128)}, f32[832,1024]{1,0:T(8,128)}) custom-call(s32[3]{0:T(128)} %copy-done.82, bf16[832,1024]{1,0:T(8,128)(2,1)} %copy-done.16, bf16[832,1024]{1,0:T(8,128)(2,1)} %copy-done.13, ...), custom_call_target="tpu_custom_call", output_to_operand_aliasing={{0}: (5, {}), {1}: (6, {})} | custom-call | flops 4185999872 | bytes 1000 | tf_op jit(solution)/shard_map/feed/pallas_call | solution.py:756
  157.5 13.6 %feed.6 = (bf16[1664,1024]{1,0:T(8,128)(2,1)}, bf16[1664,1024]{1,0:T(8,128)(2,1)}, bf16[832,1024]{1,0:T(8,128)(2,1)}, bf16[832,1024]{1,0:T(8,128)(2,1)}) custom-call(s32[3]{0:T(128)} %copy-done.82, bf16[832,1024]{1,0:T(8,128)(2,1)} %copy-done.16, bf16[832,1024]{1,0:T(8,128)(2,1)} %copy-done.13, bf16[1024,512]{1,0:T(8,128)(2,1)} %collective-permute-done.14.refs_0_, ...), custom_call_target="tpu_custom_call" | custom-call | flops 4185999872 | bytes 1000 | tf_op jit(solution)/shard_map/feed/pallas_call | solution.py:756
  171.1 13.7 %feed.7 = (bf16[1664,1024]{1,0:T(8,128)(2,1)}, bf16[1664,1024]{1,0:T(8,128)(2,1)}, f32[832,1024]{1,0:T(8,128)}, f32[832,1024]{1,0:T(8,128)}) custom-call(s32[3]{0:T(128)} %copy-done.82, bf16[832,1024]{1,0:T(8,128)(2,1)} %get-tuple-element.312.h_ref.mine_ref, bf16[832,1024]{1,0:T(8,128)(2,1)} %copy-done, ...), custom_call_target="tpu_custom_call", output_to_operand_aliasing={{0}: (9, {}), {1}: (10, {})} | custom-call | flops 4185999872 | bytes 1000 | tf_op jit(solution)/shard_map/feed/pallas_call | solution.py:756
  184.9 7.3 %up_grad.2 = bf16[1024,1024]{1,0:T(8,128)(2,1)} custom-call(bf16[832,1024]{1,0:T(8,128)(2,1)S(1)} %copy-done.3, bf16[832,1024]{1,0:T(8,128)(2,1)S(1)} %copy-done.17, bf16[1664,1024]{1,0:T(8,128)(2,1)} %get-tuple-element.334.du_ref), custom_call_target="tpu_custom_call" | custom-call | flops 241500000 | bytes 1000 | tf_op jit(solution)/shard_map/up_grad/pallas_call | solution.py:786
  193.3 7.1 %down_grad.2 = bf16[1024,1024]{1,0:T(8,128)(2,1)} custom-call(bf16[1664,1024]{1,0:T(8,128)(2,1)} %get-tuple-element.335.g_ref, bf16[832,1024]{1,0:T(8,128)(2,1)S(1)} %copy-done.1, bf16[832,1024]{1,0:T(8,128)(2,1)S(1)} %copy-done.14), custom_call_target="tpu_custom_call" | custom-call | flops 1127000064 | bytes 1000 | tf_op jit(solution)/shard_map/down_grad/pallas_call | solution.py:809
  201.7 23.0 %middle_back.1 = (f32[832,1024]{1,0:T(8,128)}, bf16[832,1024]{1,0:T(8,128)(2,1)}, bf16[832,1024]{1,0:T(8,128)(2,1)}, bf16[832,1024]{1,0:T(8,128)(2,1)}, f32[4,64...) custom-call(s32[3]{0:T(128)} %copy-done.82, f32[832,1024]{1,0:T(8,128)} %get-tuple-element.339.ym_ref, ...), custom_call_target="tpu_custom_call" | custom-call | flops 827862016 | bytes 1000 | tf_op jit(solution)/shard_map/middle_back/pallas_call | solution.py:992
  226.7 6.3 %up_grad.3 = bf16[1024,1024]{1,0:T(8,128)(2,1)S(1)} custom-call(bf16[832,1024]{1,0:T(8,128)(2,1)S(1)} %copy-done.3, bf16[832,1024]{1,0:T(8,128)(2,1)S(1)} %copy-done.18, bf16[1664,1024]{1,0:T(8,128)(2,1)} %get-tuple-element.345.du_ref), custom_call_target="tpu_custom_call" | custom-call | flops 241500000 | bytes 1000 | tf_op jit(solution)/shard_map/up_grad/pallas_call | solution.py:786
  233.1 7.5 %collective-permute-done.31 = bf16[1024,1024]{1,0:T(8,128)(2,1)} collective-permute-done((bf16[1024,1024]{1,0:T(8,128)(2,1)}, bf16[1024,1024]{1,0:T(8,128)(2,1)}, u32[]{:S(2)}, u32[]{:S(2)}) %collective-permute-start.31) | collective-permute-done | bytes 2097184 | tf_op jit(solution)/shard_map/ppermute | solution.py:1096
  241.8 4.1 add_convert_fusion.2
  251.0 4.7 pull.1
  257.7 9.3 %self_back.3 = (bf16[1664,128]{1,0:T(8,128)(2,1)S(1)}, bf16[1664,128]{1,0:T(8,128)(2,1)S(1)}, bf16[1664,128]{1,0:T(8,128)(2,1)S(1)}) custom-call(s32[1]{0:T(128)} %dynamic_slice.129.limit_ref, bf16[1664,128]{1,0:T(8,128)(2,1)S(1)} %copy-done.66, bf16[1664,128]{1,0:T(8,128)(2,1)S(1)} %copy-done.68, bf16[1664,128]{1,0:T(8,128)(2,1)S(1)} %copy-done.70, ...), custom_call_target="tpu_custom_call" | custom-call | flops 338100000 | bytes 1000 | tf_op jit(solution)/shard_map/self_back/pallas_call | solution.py:606
  267.1 4.8 query_grad.2
  277.9 9.9 %self_back.4 = (bf16[1664,128]{1,0:T(8,128)(2,1)S(1)}, bf16[1664,128]{1,0:T(8,128)(2,1)S(1)}, bf16[1664,128]{1,0:T(8,128)(2,1)S(1)}) custom-call(s32[1]{0:T(128)} %dynamic_slice.129.limit_ref, bf16[1664,128]{1,0:T(8,128)(2,1)S(1)} %copy-done.72, bf16[1664,128]{1,0:T(8,128)(2,1)S(1)} %copy-done.74, bf16[1664,128]{1,0:T(8,128)(2,1)S(1)} %copy-done.76, ...), custom_call_target="tpu_custom_call" | custom-call | flops 338100000 | bytes 1000 | tf_op jit(solution)/shard_map/self_back/pallas_call | solution.py:606
  290.3 6.4 %down_grad.3 = bf16[1024,1024]{1,0:T(8,128)(2,1)S(1)} custom-call(bf16[1664,1024]{1,0:T(8,128)(2,1)} %get-tuple-element.383.g_ref, bf16[832,1024]{1,0:T(8,128)(2,1)S(1)} %copy-done.2, bf16[832,1024]{1,0:T(8,128)(2,1)S(1)} %copy-done.15), custom_call_target="tpu_custom_call" | custom-call | flops 1127000064 | bytes 1000 | tf_op jit(solution)/shard_map/down_grad/pallas_call | solution.py:809
  296.7 7.2 %qkv_grad.2 = bf16[3072,256]{1,0:T(8,128)(2,1)} custom-call(s32[3]{0:T(128)S(1)} %copy-done.83, bf16[1664,1024]{1,0:T(8,128)(2,1)} %copy-done.8, bf16[1664,128]{1,0:T(8,128)(2,1)S(1)} %get-tuple-element.366.refs_0_.refs_3_, bf16[1664,128]{1,0:T(8,128)(2,1)S(1)} %get-tuple-element.367.refs_1_.refs_4_, ...), custom_call_target="tpu_custom_call" | custom-call | flops 1127000064 | bytes 1000 | tf_op jit(solution)/shard_map/qkv_grad/pallas_call | solution.py:846
  304.6 2.6 convert_add_fusion.1
  310.9 2.6 collective-permute-start.43
  315.8 20.3 %self_back.5 = (bf16[1664,256]{1,0:T(8,128)(2,1)S(1)}, bf16[1664,256]{1,0:T(8,128)(2,1)S(1)}, bf16[1664,256]{1,0:T(8,128)(2,1)S(1)}) custom-call(s32[1]{0:T(128)} %dynamic_slice.129.limit_ref, bf16[1664,256]{1,0:T(8,128)(2,1)S(1)} %copy-done.57, bf16[1664,256]{1,0:T(8,128)(2,1)S(1)} %copy-done.59, bf16[1664,256]{1,0:T(8,128)(2,1)S(1)} %copy-done.61, ...), custom_call_target="tpu_custom_call" | custom-call | flops 676200000 | bytes 1000 | tf_op jit(solution)/shard_map/self_back/pallas_call | solution.py:606
  343.1 5.2 outputs_grad.2
  348.3 7.0 %first_back.2 = bf16[832,1024]{1,0:T(8,128)(2,1)} custom-call(s32[3]{0:T(128)S(1)} %add_add_fusion.1.place_ref, bf16[1664,256]{1,0:T(8,128)(2,1)S(1)} %get-tuple-element.432.refs_0_, bf16[1664,256]{1,0:T(8,128)(2,1)S(1)} %get-tuple-element.411.refs_1_, bf16[1664,256]{1,0:T(8,128)(2,1)S(1)} %get-tuple-element.412.refs_2_, bf16[1664,128]{1,0:T(8,128)(2,1)S(1)} %copy-done.23, ...), custom_call_target="tpu_custom_call" | custom-call | flops 172270000 | bytes 1000 | tf_op jit(solution)/shard_map/first_back/pallas_call | solution.py:1026
  357.4 5.9 %qkv_grad.3 = bf16[3072,256]{1,0:T(8,128)(2,1)S(1)} custom-call(s32[3]{0:T(128)S(1)} %copy-done.83, bf16[1664,1024]{1,0:T(8,128)(2,1)} %copy-done.8, bf16[1664,256]{1,0:T(8,128)(2,1)S(1)} %get-tuple-element.432.refs_0_, bf16[1664,256]{1,0:T(8,128)(2,1)S(1)} %get-tuple-element.411.refs_1_, bf16[1664,256]{1,0:T(8,128)(2,1)S(1)} %get-tuple-element.412.refs_2_), custom_call_target="tpu_custom_call" | custom-call | flops 1127000064 | bytes 1000 | tf_op jit(solution)/shard_map/qkv_grad/pallas_call | solution.py:846
  363.4 3.1 convert_add_fusion.6
  370.2 3.9 query_grad.3
  379.3 6.3 %first_back.3.ym_ref = f32[832,1024]{1,0:T(8,128)S(1)} custom-call(s32[3]{0:T(128)S(1)} %copy-done.83, bf16[1664,256]{1,0:T(8,128)(2,1)S(1)} %get-tuple-element.432.refs_0_, bf16[1664,256]{1,0:T(8,128)(2,1)S(1)} %get-tuple-element.411.refs_1_, bf16[1664,256]{1,0:T(8,128)(2,1)S(1)} %copy-done.12, bf16[1664,128]{1,0:T(8,128)(2,1)S(1)} %copy-done.24, ...), custom_call_target="tpu_custom_call" | custom-call | flops 172270000 | bytes 1000 | tf_op jit(solution)/shard_map/first_back/pallas_call | solution.py:1026
  386.7 8.9 %collective-permute-done.58 = bf16[256,1024]{1,0:T(8,128)(2,1)} collective-permute-done((bf16[256,1024]{1,0:T(8,128)(2,1)S(1)}, bf16[256,1024]{1,0:T(8,128)(2,1)}, u32[]{:S(2)}, u32[]{:S(2)}) %collective-permute-start.58) | collective-permute-done | bytes 524320 | tf_op jit(solution)/shard_map/ppermute | solution.py:1099
  397.2 5.9 %frames_back.1 = (bf16[832,1024]{1,0:T(8,128)(2,1)}, f32[8,1024]{1,0:T(8,128)S(1)}) custom-call(s32[3]{0:T(128)S(1)} %copy-done.83, f32[832,1024]{1,0:T(8,128)S(1)} %first_back.3.ym_ref, bf16[832,1024]{1,0:T(8,128)(2,1)} %collective-permute-done.50.yr_ref, f32[832,1024]{1,0:T(8,128)S(1)} %copy-done.42, bf16[832,1024]{1,0:T(8,128)(2,1)S(1)} %copy-done.51, ...), custom_call_target="tpu_custom_call" | custom-call | flops 207046000 | bytes 1000 | tf_op jit(solution)/shard_map/frames_back/pallas_call | solution.py:1061
  408.9 7.1 %collective-permute-done.44 = bf16[1536,256]{1,0:T(8,128)(2,1)S(1)} collective-permute-done((bf16[1536,256]{1,0:T(8,128)(2,1)S(1)}, bf16[1536,256]{1,0:T(8,128)(2,1)S(1)}, u32[]{:S(2)}, u32[]{:S(2)}) %collective-permute-start.44) | collective-permute-done | bytes 786464 | tf_op jit(solution)/shard_map/ppermute | solution.py:1099
  416.3 5.1 outputs_grad.3
  424.6 4.4 fusion
  430.0 2.8 collective-permute-done.55
  432.8 2.3 collective-permute-start.63
  435.3 2.1 collective-permute-start.53
  437.4 15.4 %collective-permute-done.56 = f32[8,1024]{1,0:T(8,128)S(1)} collective-permute-done((f32[8,1024]{1,0:T(8,128)S(1)}, f32[8,1024]{1,0:T(8,128)S(1)}, u32[]{:S(2)}, u32[]{:S(2)}) %collective-permute-start.56) | collective-permute-done | bytes 32800 | tf_op jit(solution)/shard_map/ppermute | solution.py:1099
  454.6 5.0 collective-permute-done.53
  459.6 3.0 collective-permute-start.65
  463.2 14.7 %collective-permute-done.62 = bf16[768,256]{1,0:T(8,128)(2,1)S(1)} collective-permute-done((bf16[768,256]{1,0:T(8,128)(2,1)S(1)}, bf16[768,256]{1,0:T(8,128)(2,1)S(1)}, u32[]{:S(2)}, u32[]{:S(2)}) %collective-permute-start.62) | collective-permute-done | bytes 393248 | tf_op jit(solution)/shard_map/ppermute | solution.py:1099
  477.9 3.3 collective-permute-start.72
  481.6 2.1 collective-permute-start.68
  483.7 6.9 %collective-permute-done.65 = bf16[768,256]{1,0:T(8,128)(2,1)S(1)} collective-permute-done((bf16[768,256]{1,0:T(8,128)(2,1)S(1)}, bf16[768,256]{1,0:T(8,128)(2,1)S(1)}, u32[]{:S(2)}, u32[]{:S(2)}) %collective-permute-start.65) | collective-permute-done | bytes 393248 | tf_op jit(solution)/shard_map/ppermute | solution.py:1099
  491.9 6.4 %collective-permute-done.70 = bf16[768,256]{1,0:T(8,128)(2,1)S(1)} collective-permute-done((bf16[768,256]{1,0:T(8,128)(2,1)S(1)}, bf16[768,256]{1,0:T(8,128)(2,1)S(1)}, u32[]{:S(2)}, u32[]{:S(2)}) %collective-permute-start.70) | collective-permute-done | bytes 393248 | tf_op jit(solution)/shard_map/ppermute | solution.py:1099
  498.2 4.2 collective-permute-start.73
  503.0 2.1 collective-permute-start.71
  505.0 3.0 fusion.1
  508.0 4.1 collective-permute-done.73
  513.1 3.8 add_convert_fusion
  525.7 4.2 collective-permute-done.76
  532.4 2.0 fusion.3
  (483 shorter events, 115.5 us)
Async XLA Ops:
  3.2 21.0 %collective-permute-start.1 = (bf16[3,1024,128]{2,1,0:T(8,128)(2,1)}, bf16[3,1024,128]{2,1,0:T(8,128)(2,1)}, u32[]{:S(2)}, u32[]{:S(2)}) collective-permute-start(bf16[3,1024,128]{2,1,0:T(8,128)(2,1)} %constant_dynamic-slice_fusion.15), channel_id=1, source_target_pairs={{0,2},{2,0},{1,3},{3,1},{4,6},{6,4},{5,7},{7,5},{8,10},{10,8},{9,1... | collective-permute-start | bytes 2359304 | tf_op jit(solution)/shard_map/ppermute | solution.py:1096
  27.5 12.7 %collective-permute-start.3 = (bf16[1024,128]{1,0:T(8,128)(2,1)}, bf16[1024,128]{1,0:T(8,128)(2,1)}, u32[]{:S(2)}, u32[]{:S(2)}) collective-permute-start(bf16[1024,128]{1,0:T(8,128)(2,1)} %constant_dynamic-slice_fusion.13), channel_id=1, source_target_pairs={{0,2},{2,0},{1,3},{3,1},{4,6},{6,4},{5,7},{7,5},{8,10},{10,8},{9,1... | collective-permute-start | bytes 786440 | tf_op jit(solution)/shard_map/ppermute | solution.py:1096
  28.9 42.8 %collective-permute-start.5 = (bf16[256,1024]{1,0:T(8,128)(2,1)}, bf16[256,1024]{1,0:T(8,128)(2,1)}, u32[]{:S(2)}, u32[]{:S(2)}) collective-permute-start(bf16[256,1024]{1,0:T(8,128)(2,1)} %refs_2_), channel_id=1, source_target_pairs={{0,1},{1,0},{2,3},{3,2},{4,5},{5,4},{6,7},{7,6},{8,9},{9,8},{10,11... | collective-permute-start | bytes 1572872 | tf_op jit(solution)/shard_map/ppermute | solution.py:1093
  29.0 42.7 %collective-permute-start.6 = (bf16[1024,256]{1,0:T(8,128)(2,1)}, bf16[1024,256]{1,0:T(8,128)(2,1)S(1)}, u32[]{:S(2)}, u32[]{:S(2)}) collective-permute-start(bf16[1024,256]{1,0:T(8,128)(2,1)} %refs_0_.2), channel_id=1, source_target_pairs={{0,1},{1,0},{2,3},{3,2},{4,5},{5,4},{6,7},{7,6},{8,9},{9,8},{10,11... | collective-permute-start | bytes 1572872 | tf_op jit(solution)/shard_map/ppermute | solution.py:1093
  29.5 42.2 %collective-permute-start.7 = (bf16[256,1024]{1,0:T(8,128)(2,1)}, bf16[256,1024]{1,0:T(8,128)(2,1)}, u32[]{:S(2)}, u32[]{:S(2)}) collective-permute-start(bf16[256,1024]{1,0:T(8,128)(2,1)} %refs_6_.1), channel_id=1, source_target_pairs={{0,1},{1,0},{2,3},{3,2},{4,5},{5,4},{6,7},{7,6},{8,9},{9,8},{10,11... | collective-permute-start | bytes 1572872 | tf_op jit(solution)/shard_map/ppermute | solution.py:1093
  34.5 35.6 %collective-permute-start.4 = (bf16[128,1024]{1,0:T(8,128)(2,1)S(1)}, bf16[128,1024]{1,0:T(8,128)(2,1)}, u32[]{:S(2)}, u32[]{:S(2)}) collective-permute-start(bf16[128,1024]{1,0:T(8,128)(2,1)S(1)} %constant_dynamic-slice_fusion.12), channel_id=1, source_target_pairs={{0,2},{2,0},{1,3},{3,1},{4,6},{6,4},{5,7},{7,5},{8,10},{10,8},{9,1... | collective-permute-start | bytes 786440 | tf_op jit(solution)/shard_map/ppermute | solution.py:1096
  40.1 42.0 %collective-permute-start.8 = (bf16[3,1024,128]{2,1,0:T(8,128)(2,1)}, bf16[3,1024,128]{2,1,0:T(8,128)(2,1)S(1)}, u32[]{:S(2)}, u32[]{:S(2)}) collective-permute-start(bf16[3,1024,128]{2,1,0:T(8,128)(2,1)} %collective-permute-done.1.weight_ref.refs_10_), channel_id=1, source_target_pairs={{0,8},{4,12},{8,0},{12,4},{16,24},{20,28},{24,16},{28,20},{1,9},{5... | collective-permute-start | bytes 2359304 | tf_op jit(solution)/shard_map/ppermute | solution.py:1099
  70.1 12.0 %collective-permute-start.9 = (bf16[2,64,256]{2,1,0:T(8,128)(2,1)S(1)}, bf16[2,64,256]{2,1,0:T(8,128)(2,1)S(1)}, u32[]{:S(2)}, u32[]{:S(2)}) collective-permute-start(bf16[2,64,256]{2,1,0:T(8,128)(2,1)S(1)} %get-tuple-element.547), channel_id=1, source_target_pairs={{0,2},{2,0},{1,3},{3,1},{4,6},{6,4},{5,7},{7,5},{8,10},{10,8},{9,1... | collective-permute-start | bytes 196616 | tf_op jit(solution)/shard_map/ppermute | solution.py:1096
  71.7 12.2 %collective-permute-start.10 = (bf16[832,256]{1,0:T(8,128)(2,1)S(1)}, bf16[832,256]{1,0:T(8,128)(2,1)}, u32[]{:S(2)}, u32[]{:S(2)}) collective-permute-start(bf16[832,256]{1,0:T(8,128)(2,1)S(1)} %constant_dynamic-slice_fusion.11), channel_id=1, source_target_pairs={{0,1},{1,0},{2,3},{3,2},{4,5},{5,4},{6,7},{7,6},{8,9},{9,8},{10,11... | collective-permute-start | bytes 1277960 | tf_op jit(solution)/shard_map/ppermute | solution.py:1093
  72.0 28.6 %collective-permute-start.14 = (bf16[1024,512]{1,0:T(8,128)(2,1)S(1)}, bf16[1024,512]{1,0:T(8,128)(2,1)}, u32[]{:S(2)}, u32[]{:S(2)}) collective-permute-start(bf16[1024,512]{1,0:T(8,128)(2,1)S(1)} %constant_dynamic-slice_fusion.10), channel_id=1, source_target_pairs={{0,2},{2,0},{1,3},{3,1},{4,6},{6,4},{5,7},{7,5},{8,10},{10,8},{9,1... | collective-permute-start | bytes 3145736 | tf_op jit(solution)/shard_map/ppermute | solution.py:1096
  72.5 17.7 %collective-permute-start.11 = (bf16[128,1024]{1,0:T(8,128)(2,1)}, bf16[128,1024]{1,0:T(8,128)(2,1)S(1)}, u32[]{:S(2)}, u32[]{:S(2)}) collective-permute-start(bf16[128,1024]{1,0:T(8,128)(2,1)} %collective-permute-done.2.refs_7_.refs_0_), channel_id=1, source_target_pairs={{0,8},{4,12},{8,0},{12,4},{16,24},{20,28},{24,16},{28,20},{1,9},{5... | collective-permute-start | bytes 786440 | tf_op jit(solution)/shard_map/ppermute | solution.py:1099
  82.1 21.9 %collective-permute-start.18 = (bf16[128,1024]{1,0:T(8,128)(2,1)}, bf16[128,1024]{1,0:T(8,128)(2,1)}, u32[]{:S(2)}, u32[]{:S(2)}) collective-permute-start(bf16[128,1024]{1,0:T(8,128)(2,1)} %collective-permute-done.2.refs_7_.refs_0_), channel_id=1, source_target_pairs={{0,1},{1,0},{2,3},{3,2},{4,5},{5,4},{6,7},{7,6},{8,9},{9,8},{10,11... | collective-permute-start | bytes 786440 | tf_op jit(solution)/shard_map/ppermute | solution.py:1093
  83.9 16.0 %collective-permute-start.13 = (bf16[128,1024]{1,0:T(8,128)(2,1)}, bf16[128,1024]{1,0:T(8,128)(2,1)S(1)}, u32[]{:S(2)}, u32[]{:S(2)}) collective-permute-start(bf16[128,1024]{1,0:T(8,128)(2,1)} %collective-permute-done.4.refs_19_.refs_7_), channel_id=1, source_target_pairs={{0,4},{4,0},{8,12},{12,8},{16,20},{20,16},{24,28},{28,24},{1,5},{5... | collective-permute-start | bytes 786440 | tf_op jit(solution)/shard_map/ppermute | solution.py:1099
  102.1 27.3 %collective-permute-start.24 = (bf16[1024,512]{1,0:T(8,128)(2,1)}, bf16[1024,512]{1,0:T(8,128)(2,1)S(1)}, u32[]{:S(2)}, u32[]{:S(2)}) collective-permute-start(bf16[1024,512]{1,0:T(8,128)(2,1)} %collective-permute-done.14.refs_0_), channel_id=1, source_target_pairs={{0,4},{4,0},{8,12},{12,8},{16,20},{20,16},{24,28},{28,24},{1,5},{5... | collective-permute-start | bytes 3145736 | tf_op jit(solution)/shard_map/ppermute | solution.py:1099
  103.9 25.5 %collective-permute-start.25 = (bf16[512,1024]{1,0:T(8,128)(2,1)}, bf16[512,1024]{1,0:T(8,128)(2,1)S(1)}, u32[]{:S(2)}, u32[]{:S(2)}) collective-permute-start(bf16[512,1024]{1,0:T(8,128)(2,1)} %constant_dynamic-slice_fusion.9), channel_id=1, source_target_pairs={{0,2},{2,0},{1,3},{3,1},{4,6},{6,4},{5,7},{7,5},{8,10},{10,8},{9,1... | collective-permute-start | bytes 3145736 | tf_op jit(solution)/shard_map/ppermute | solution.py:1096
  130.5 13.2 %collective-permute-start.26 = (bf16[832,1024]{1,0:T(8,128)(2,1)}, bf16[832,1024]{1,0:T(8,128)(2,1)S(1)}, u32[]{:S(2)}, u32[]{:S(2)}) collective-permute-start(bf16[832,1024]{1,0:T(8,128)(2,1)} %get-tuple-element.312.h_ref.mine_ref), channel_id=1, source_target_pairs={{0,1},{1,0},{2,3},{3,2},{4,5},{5,4},{6,7},{7,6},{8,9},{9,8},{10,11... | collective-permute-start | bytes 5111816 | tf_op jit(solution)/shard_map/ppermute | solution.py:1093
  130.7 13.0 %collective-permute-start.27 = (bf16[832,1024]{1,0:T(8,128)(2,1)S(1)}, bf16[832,1024]{1,0:T(8,128)(2,1)S(1)}, u32[]{:S(2)}, u32[]{:S(2)}) collective-permute-start(bf16[832,1024]{1,0:T(8,128)(2,1)S(1)} %broadcast_select_fusion.d_ref.mine_ref), channel_id=1, source_target_pairs={{0,1},{1,0},{2,3},{3,2},{4,5},{5,4},{6,7},{7,6},{8,9},{9,8},{10,11... | collective-permute-start | bytes 5111816 | tf_op jit(solution)/shard_map/ppermute | solution.py:1093
  131.0 26.5 %collective-permute-start.28 = (bf16[512,1024]{1,0:T(8,128)(2,1)}, bf16[512,1024]{1,0:T(8,128)(2,1)}, u32[]{:S(2)}, u32[]{:S(2)}) collective-permute-start(bf16[512,1024]{1,0:T(8,128)(2,1)} %copy-done.107), channel_id=1, source_target_pairs={{0,4},{4,0},{8,12},{12,8},{16,20},{20,16},{24,28},{28,24},{1,5},{5... | collective-permute-start | bytes 3145736 | tf_op jit(solution)/shard_map/ppermute | solution.py:1099
  171.1 29.4 %collective-permute-start.29 = (bf16[832,1024]{1,0:T(8,128)(2,1)}, bf16[832,1024]{1,0:T(8,128)(2,1)S(1)}, u32[]{:S(2)}, u32[]{:S(2)}) collective-permute-start(bf16[832,1024]{1,0:T(8,128)(2,1)} %get-tuple-element.324), channel_id=1, source_target_pairs={{0,1},{1,0},{2,3},{3,2},{4,5},{5,4},{6,7},{7,6},{8,9},{9,8},{10,11... | collective-permute-start | bytes 5111816 | tf_op jit(solution)/shard_map/ppermute | solution.py:1093
  192.2 48.4 %collective-permute-start.31 = (bf16[1024,1024]{1,0:T(8,128)(2,1)}, bf16[1024,1024]{1,0:T(8,128)(2,1)}, u32[]{:S(2)}, u32[]{:S(2)}) collective-permute-start(bf16[1024,1024]{1,0:T(8,128)(2,1)} %up_grad.2), channel_id=1, source_target_pairs={{0,2},{2,0},{1,3},{3,1},{4,6},{6,4},{5,7},{7,5},{8,10},{10,8},{9,1... | collective-permute-start | bytes 6291464 | tf_op jit(solution)/shard_map/ppermute | solution.py:1096
  224.7 15.9 %collective-permute-start.32 = (bf16[832,1024]{1,0:T(8,128)(2,1)}, bf16[832,1024]{1,0:T(8,128)(2,1)S(1)}, u32[]{:S(2)}, u32[]{:S(2)}) collective-permute-start(bf16[832,1024]{1,0:T(8,128)(2,1)} %get-tuple-element.361.mine_ref.refs_2_.refs_1_), channel_id=1, source_target_pairs={{0,1},{1,0},{2,3},{3,2},{4,5},{5,4},{6,7},{7,6},{8,9},{9,8},{10,11... | collective-permute-start | bytes 5111816 | tf_op jit(solution)/shard_map/ppermute | solution.py:1093
  225.0 42.1 %collective-permute-start.35 = (bf16[832,1024]{1,0:T(8,128)(2,1)}, bf16[832,1024]{1,0:T(8,128)(2,1)}, u32[]{:S(2)}, u32[]{:S(2)}) collective-permute-start(bf16[832,1024]{1,0:T(8,128)(2,1)} %get-tuple-element.358.mine_ref), channel_id=1, source_target_pairs={{0,1},{1,0},{2,3},{3,2},{4,5},{5,4},{6,7},{7,6},{8,9},{9,8},{10,11... | collective-permute-start | bytes 5111816 | tf_op jit(solution)/shard_map/ppermute | solution.py:1093
  246.9 20.2 %collective-permute-start.34 = (bf16[832,512]{1,0:T(8,128)(2,1)}, bf16[832,512]{1,0:T(8,128)(2,1)S(1)}, u32[]{:S(2)}, u32[]{:S(2)}) collective-permute-start(bf16[832,512]{1,0:T(8,128)(2,1)} %slice.78), channel_id=1, source_target_pairs={{0,1},{1,0},{2,3},{3,2},{4,5},{5,4},{6,7},{7,6},{8,9},{9,8},{10,11... | collective-permute-start | bytes 2555912 | tf_op jit(solution)/shard_map/ppermute | solution.py:1093
  246.9 26.8 %collective-permute-start.37 = (bf16[512,1024]{1,0:T(8,128)(2,1)}, bf16[512,1024]{1,0:T(8,128)(2,1)}, u32[]{:S(2)}, u32[]{:S(2)}) collective-permute-start(bf16[512,1024]{1,0:T(8,128)(2,1)} %get-tuple-element.526), channel_id=1, source_target_pairs={{0,4},{4,0},{8,12},{12,8},{16,20},{20,16},{24,28},{28,24},{1,5},{5... | collective-permute-start | bytes 3145736 | tf_op jit(solution)/shard_map/ppermute | solution.py:1099
  249.3 17.8 %collective-permute-start.36 = (f32[2,2,64,256]{3,2,0,1:T(8,128)}, f32[2,2,64,256]{3,2,0,1:T(8,128)}, u32[]{:S(2)}, u32[]{:S(2)}) collective-permute-start(f32[2,2,64,256]{3,2,0,1:T(8,128)} %get-tuple-element.539), channel_id=1, source_target_pairs={{0,1},{1,0},{2,3},{3,2},{4,5},{5,4},{6,7},{7,6},{8,9},{9,8},{10,11... | collective-permute-start | bytes 786440 | tf_op jit(solution)/shard_map/ppermute | solution.py:1093
  256.6 48.0 %collective-permute-start.33 = (bf16[1024,1024]{1,0:T(8,128)(2,1)}, bf16[1024,1024]{1,0:T(8,128)(2,1)S(1)}, u32[]{:S(2)}, u32[]{:S(2)}) collective-permute-start(bf16[1024,1024]{1,0:T(8,128)(2,1)} %down_grad.2), channel_id=1, source_target_pairs={{0,2},{2,0},{1,3},{3,1},{4,6},{6,4},{5,7},{7,5},{8,10},{10,8},{9,1... | collective-permute-start | bytes 6291464 | tf_op jit(solution)/shard_map/ppermute | solution.py:1096
  275.4 13.9 %collective-permute-start.38 = (bf16[256,1024]{1,0:T(8,128)(2,1)S(1)}, bf16[256,1024]{1,0:T(8,128)(2,1)S(1)}, u32[]{:S(2)}, u32[]{:S(2)}) collective-permute-start(bf16[256,1024]{1,0:T(8,128)(2,1)S(1)} %dynamic-slice_convert_fusion.1), channel_id=1, source_target_pairs={{0,8},{4,12},{8,0},{12,4},{16,24},{20,28},{24,16},{28,20},{1,9},{5... | collective-permute-start | bytes 1572872 | tf_op jit(solution)/shard_map/ppermute | solution.py:1099
  307.2 28.9 %collective-permute-start.40 = (bf16[512,1024]{1,0:T(8,128)(2,1)}, bf16[512,1024]{1,0:T(8,128)(2,1)}, u32[]{:S(2)}, u32[]{:S(2)}) collective-permute-start(bf16[512,1024]{1,0:T(8,128)(2,1)} %get-tuple-element.525), channel_id=1, source_target_pairs={{0,4},{4,0},{8,12},{12,8},{16,20},{20,16},{24,28},{28,24},{1,5},{5... | collective-permute-start | bytes 3145736 | tf_op jit(solution)/shard_map/ppermute | solution.py:1099
  307.7 35.3 %collective-permute-start.41 = (bf16[832,1024]{1,0:T(8,128)(2,1)}, bf16[832,1024]{1,0:T(8,128)(2,1)}, u32[]{:S(2)}, u32[]{:S(2)}) collective-permute-start(bf16[832,1024]{1,0:T(8,128)(2,1)} %get-tuple-element.446.refs_6_.refs_5_), channel_id=1, source_target_pairs={{0,1},{1,0},{2,3},{3,2},{4,5},{5,4},{6,7},{7,6},{8,9},{9,8},{10,11... | collective-permute-start | bytes 5111816 | tf_op jit(solution)/shard_map/ppermute | solution.py:1093
  307.8 55.6 %collective-permute-start.39 = (bf16[3072,256]{1,0:T(8,128)(2,1)}, bf16[3072,256]{1,0:T(8,128)(2,1)}, u32[]{:S(2)}, u32[]{:S(2)}) collective-permute-start(bf16[3072,256]{1,0:T(8,128)(2,1)} %qkv_grad.2), channel_id=1, source_target_pairs={{0,2},{2,0},{1,3},{3,1},{4,6},{6,4},{5,7},{7,5},{8,10},{10,8},{9,1... | collective-permute-start | bytes 4718600 | tf_op jit(solution)/shard_map/ppermute | solution.py:1096
  310.5 30.9 %collective-permute-start.42 = (bf16[832,512]{1,0:T(8,128)(2,1)}, bf16[832,512]{1,0:T(8,128)(2,1)}, u32[]{:S(2)}, u32[]{:S(2)}) collective-permute-start(bf16[832,512]{1,0:T(8,128)(2,1)} %slice.84), channel_id=1, source_target_pairs={{0,1},{1,0},{2,3},{3,2},{4,5},{5,4},{6,7},{7,6},{8,9},{9,8},{10,11... | collective-permute-start | bytes 2555912 | tf_op jit(solution)/shard_map/ppermute | solution.py:1093
  310.9 29.2 %collective-permute-start.43 = (bf16[256,1024]{1,0:T(8,128)(2,1)}, bf16[256,1024]{1,0:T(8,128)(2,1)S(1)}, u32[]{:S(2)}, u32[]{:S(2)}) collective-permute-start(bf16[256,1024]{1,0:T(8,128)(2,1)} %add_convert_fusion.9), channel_id=1, source_target_pairs={{0,16},{4,20},{8,24},{12,28},{16,0},{20,4},{24,8},{28,12},{1,17},{... | collective-permute-start | bytes 1572872 | tf_op jit(solution)/shard_map/ppermute | solution.py:1099
  336.2 39.5 %collective-permute-start.47 = (bf16[1024,256]{1,0:T(8,128)(2,1)S(1)}, bf16[1024,256]{1,0:T(8,128)(2,1)S(1)}, u32[]{:S(2)}, u32[]{:S(2)}) collective-permute-start(bf16[1024,256]{1,0:T(8,128)(2,1)S(1)} %copy-done.64), channel_id=1, source_target_pairs={{0,2},{2,0},{1,3},{3,1},{4,6},{6,4},{5,7},{7,5},{8,10},{10,8},{9,1... | collective-permute-start | bytes 1572872 | tf_op jit(solution)/shard_map/ppermute | solution.py:1096
  340.1 34.1 %collective-permute-start.48 = (bf16[2,64,256]{2,1,0:T(8,128)(2,1)S(1)}, bf16[2,64,256]{2,1,0:T(8,128)(2,1)S(1)}, u32[]{:S(2)}, u32[]{:S(2)}) collective-permute-start(bf16[2,64,256]{2,1,0:T(8,128)(2,1)S(1)} %copy-done.127), channel_id=1, source_target_pairs={{0,2},{2,0},{1,3},{3,1},{4,6},{6,4},{5,7},{7,5},{8,10},{10,8},{9,1... | collective-permute-start | bytes 196616 | tf_op jit(solution)/shard_map/ppermute | solution.py:1096
  341.4 25.1 %collective-permute-start.45 = (bf16[256,1024]{1,0:T(8,128)(2,1)S(1)}, bf16[256,1024]{1,0:T(8,128)(2,1)S(1)}, u32[]{:S(2)}, u32[]{:S(2)}) collective-permute-start(bf16[256,1024]{1,0:T(8,128)(2,1)S(1)} %add_convert_fusion.8), channel_id=1, source_target_pairs={{0,8},{4,12},{8,0},{12,4},{16,24},{20,28},{24,16},{28,20},{1,9},{5... | collective-permute-start | bytes 1572872 | tf_op jit(solution)/shard_map/ppermute | solution.py:1099
  356.6 13.1 %collective-permute-start.46 = (bf16[256,1024]{1,0:T(8,128)(2,1)S(1)}, bf16[256,1024]{1,0:T(8,128)(2,1)S(1)}, u32[]{:S(2)}, u32[]{:S(2)}) collective-permute-start(bf16[256,1024]{1,0:T(8,128)(2,1)S(1)} %dynamic-slice_convert_fusion), channel_id=1, source_target_pairs={{0,8},{4,12},{8,0},{12,4},{16,24},{20,28},{24,16},{28,20},{1,9},{5... | collective-permute-start | bytes 1572872 | tf_op jit(solution)/shard_map/ppermute | solution.py:1099
  363.4 33.8 %collective-permute-start.50 = (bf16[832,1024]{1,0:T(8,128)(2,1)}, bf16[832,1024]{1,0:T(8,128)(2,1)}, u32[]{:S(2)}, u32[]{:S(2)}) collective-permute-start(bf16[832,1024]{1,0:T(8,128)(2,1)} %first_back.2), channel_id=1, source_target_pairs={{0,1},{1,0},{2,3},{3,2},{4,5},{5,4},{6,7},{7,6},{8,9},{9,8},{10,11... | collective-permute-start | bytes 5111816 | tf_op jit(solution)/shard_map/ppermute | solution.py:1093
  366.5 29.1 %collective-permute-start.51 = (bf16[512,1024]{1,0:T(8,128)(2,1)S(1)}, bf16[512,1024]{1,0:T(8,128)(2,1)}, u32[]{:S(2)}, u32[]{:S(2)}) collective-permute-start(bf16[512,1024]{1,0:T(8,128)(2,1)S(1)} %outputs_grad.2), channel_id=1, source_target_pairs={{0,2},{2,0},{1,3},{3,1},{4,6},{6,4},{5,7},{7,5},{8,10},{10,8},{9,1... | collective-permute-start | bytes 3145736 | tf_op jit(solution)/shard_map/ppermute | solution.py:1096
  369.9 25.7 %collective-permute-start.58 = (bf16[256,1024]{1,0:T(8,128)(2,1)S(1)}, bf16[256,1024]{1,0:T(8,128)(2,1)}, u32[]{:S(2)}, u32[]{:S(2)}) collective-permute-start(bf16[256,1024]{1,0:T(8,128)(2,1)S(1)} %add_convert_fusion.7), channel_id=1, source_target_pairs={{0,16},{4,20},{8,24},{12,28},{16,0},{20,4},{24,8},{28,12},{1,17},{... | collective-permute-start | bytes 1572872 | tf_op jit(solution)/shard_map/ppermute | solution.py:1099
  374.1 30.4 %collective-permute-start.60 = (bf16[512,1024]{1,0:T(8,128)(2,1)}, bf16[512,1024]{1,0:T(8,128)(2,1)S(1)}, u32[]{:S(2)}, u32[]{:S(2)}) collective-permute-start(bf16[512,1024]{1,0:T(8,128)(2,1)} %maximum_select_fusion.4), channel_id=1, source_target_pairs={{0,4},{4,0},{8,12},{12,8},{16,20},{20,16},{24,28},{28,24},{1,5},{5... | collective-permute-start | bytes 3145736 | tf_op jit(solution)/shard_map/ppermute | solution.py:1099
  377.8 29.1 %collective-permute-start.49 = (bf16[1536,256]{1,0:T(8,128)(2,1)}, bf16[1536,256]{1,0:T(8,128)(2,1)}, u32[]{:S(2)}, u32[]{:S(2)}) collective-permute-start(bf16[1536,256]{1,0:T(8,128)(2,1)} %get-tuple-element.535), channel_id=1, source_target_pairs={{0,8},{4,12},{8,0},{12,4},{16,24},{20,28},{24,16},{28,20},{1,9},{5... | collective-permute-start | bytes 2359304 | tf_op jit(solution)/shard_map/ppermute | solution.py:1099
  395.6 64.0 %collective-permute-start.30 = (bf16[832,1024]{1,0:T(8,128)(2,1)}, bf16[832,1024]{1,0:T(8,128)(2,1)}, u32[]{:S(2)}, u32[]{:S(2)}) collective-permute-start(bf16[832,1024]{1,0:T(8,128)(2,1)} %get-tuple-element.337), channel_id=1, source_target_pairs={{0,1},{1,0},{2,3},{3,2},{4,5},{5,4},{6,7},{7,6},{8,9},{9,8},{10,11... | collective-permute-start | bytes 5111816 | tf_op jit(solution)/shard_map/ppermute | solution.py:1093
  395.6 20.4 %collective-permute-start.44 = (bf16[1536,256]{1,0:T(8,128)(2,1)S(1)}, bf16[1536,256]{1,0:T(8,128)(2,1)S(1)}, u32[]{:S(2)}, u32[]{:S(2)}) collective-permute-start(bf16[1536,256]{1,0:T(8,128)(2,1)S(1)} %copy-done.109), channel_id=1, source_target_pairs={{0,4},{4,0},{8,12},{12,8},{16,20},{20,16},{24,28},{28,24},{1,5},{5... | collective-permute-start | bytes 2359304 | tf_op jit(solution)/shard_map/ppermute | solution.py:1099
  404.5 30.7 %collective-permute-start.57 = (f32[64,1024]{1,0:T(8,128)}, f32[64,1024]{1,0:T(8,128)S(1)}, u32[]{:S(2)}, u32[]{:S(2)}) collective-permute-start(f32[64,1024]{1,0:T(8,128)} %get-tuple-element.537), channel_id=1, source_target_pairs={{0,2},{2,0},{1,3},{3,1},{4,6},{6,4},{5,7},{7,5},{8,10},{10,8},{9,1... | collective-permute-start | bytes 786440 | tf_op jit(solution)/shard_map/ppermute | solution.py:1096
  408.2 26.9 %collective-permute-start.59 = (bf16[768,256]{1,0:T(8,128)(2,1)S(1)}, bf16[768,256]{1,0:T(8,128)(2,1)S(1)}, u32[]{:S(2)}, u32[]{:S(2)}) collective-permute-start(bf16[768,256]{1,0:T(8,128)(2,1)S(1)} %dynamic-slice_convert_fusion.2), channel_id=1, source_target_pairs={{0,4},{4,0},{8,12},{12,8},{16,20},{20,16},{24,28},{28,24},{1,5},{5... | collective-permute-start | bytes 1179656 | tf_op jit(solution)/shard_map/ppermute | solution.py:1099
  423.0 31.3 %collective-permute-start.54 = (bf16[256,1024]{1,0:T(8,128)(2,1)S(1)}, bf16[256,1024]{1,0:T(8,128)(2,1)S(1)}, u32[]{:S(2)}, u32[]{:S(2)}) collective-permute-start(bf16[256,1024]{1,0:T(8,128)(2,1)S(1)} %get-tuple-element.533), channel_id=1, source_target_pairs={{0,4},{4,0},{8,12},{12,8},{16,20},{20,16},{24,28},{28,24},{1,5},{5... | collective-permute-start | bytes 1572872 | tf_op jit(solution)/shard_map/ppermute | solution.py:1099
  432.8 29.8 %collective-permute-start.63 = (bf16[256,1024]{1,0:T(8,128)(2,1)S(1)}, bf16[256,1024]{1,0:T(8,128)(2,1)S(1)}, u32[]{:S(2)}, u32[]{:S(2)}) collective-permute-start(bf16[256,1024]{1,0:T(8,128)(2,1)S(1)} %add_convert_fusion.4), channel_id=1, source_target_pairs={{0,8},{4,12},{8,0},{12,4},{16,24},{20,28},{24,16},{28,20},{1,9},{5... | collective-permute-start | bytes 1572872 | tf_op jit(solution)/shard_map/ppermute | solution.py:1099
  435.1 17.7 %collective-permute-start.56 = (f32[8,1024]{1,0:T(8,128)S(1)}, f32[8,1024]{1,0:T(8,128)S(1)}, u32[]{:S(2)}, u32[]{:S(2)}) collective-permute-start(f32[8,1024]{1,0:T(8,128)S(1)} %add.254), channel_id=1, source_target_pairs={{0,8},{4,12},{8,0},{12,4},{16,24},{20,28},{24,16},{28,20},{1,9},{5... | collective-permute-start | bytes 98312 | tf_op jit(solution)/shard_map/ppermute | solution.py:1099
  435.3 24.3 %collective-permute-start.53 = (bf16[768,256]{1,0:T(8,128)(2,1)S(1)}, bf16[768,256]{1,0:T(8,128)(2,1)S(1)}, u32[]{:S(2)}, u32[]{:S(2)}) collective-permute-start(bf16[768,256]{1,0:T(8,128)(2,1)S(1)} %dynamic-slice_convert_fusion.3), channel_id=1, source_target_pairs={{0,8},{4,12},{8,0},{12,4},{16,24},{20,28},{24,16},{28,20},{1,9},{5... | collective-permute-start | bytes 1179656 | tf_op jit(solution)/shard_map/ppermute | solution.py:1099
  452.9 25.1 %collective-permute-start.62 = (bf16[768,256]{1,0:T(8,128)(2,1)S(1)}, bf16[768,256]{1,0:T(8,128)(2,1)S(1)}, u32[]{:S(2)}, u32[]{:S(2)}) collective-permute-start(bf16[768,256]{1,0:T(8,128)(2,1)S(1)} %add_convert_fusion.13), channel_id=1, source_target_pairs={{0,16},{4,20},{8,24},{12,28},{16,0},{20,4},{24,8},{28,12},{1,17},{... | collective-permute-start | bytes 1179656 | tf_op jit(solution)/shard_map/ppermute | solution.py:1099
  454.3 27.1 %collective-permute-start.61 = (f32[64,1024]{1,0:T(8,128)S(1)}, f32[64,1024]{1,0:T(8,128)S(1)}, u32[]{:S(2)}, u32[]{:S(2)}) collective-permute-start(f32[64,1024]{1,0:T(8,128)S(1)} %add.259), channel_id=1, source_target_pairs={{0,1},{1,0},{2,3},{3,2},{4,5},{5,4},{6,7},{7,6},{8,9},{9,8},{10,11... | collective-permute-start | bytes 786440 | tf_op jit(solution)/shard_map/ppermute | solution.py:1093
  459.5 22.1 %collective-permute-start.66 = (f32[8,1024]{1,0:T(8,128)S(1)}, f32[8,1024]{1,0:T(8,128)S(1)}, u32[]{:S(2)}, u32[]{:S(2)}) collective-permute-start(f32[8,1024]{1,0:T(8,128)S(1)} %add.260), channel_id=1, source_target_pairs={{0,16},{4,20},{8,24},{12,28},{16,0},{20,4},{24,8},{28,12},{1,17},{... | collective-permute-start | bytes 98312 | tf_op jit(solution)/shard_map/ppermute | solution.py:1099
  459.6 31.0 %collective-permute-start.65 = (bf16[768,256]{1,0:T(8,128)(2,1)S(1)}, bf16[768,256]{1,0:T(8,128)(2,1)S(1)}, u32[]{:S(2)}, u32[]{:S(2)}) collective-permute-start(bf16[768,256]{1,0:T(8,128)(2,1)S(1)} %add_convert_fusion.12), channel_id=1, source_target_pairs={{0,16},{4,20},{8,24},{12,28},{16,0},{20,4},{24,8},{28,12},{1,17},{... | collective-permute-start | bytes 1179656 | tf_op jit(solution)/shard_map/ppermute | solution.py:1099
  462.7 18.8 %collective-permute-start.67 = (bf16[128,1024]{1,0:T(8,128)(2,1)S(1)}, bf16[128,1024]{1,0:T(8,128)(2,1)S(1)}, u32[]{:S(2)}, u32[]{:S(2)}) collective-permute-start(bf16[128,1024]{1,0:T(8,128)(2,1)S(1)} %dynamic-slice_convert_fusion.5), channel_id=1, source_target_pairs={{0,8},{4,12},{8,0},{12,4},{16,24},{20,28},{24,16},{28,20},{1,9},{5... | collective-permute-start | bytes 786440 | tf_op jit(solution)/shard_map/ppermute | solution.py:1099
  477.9 25.0 %collective-permute-start.72 = (bf16[512,1024]{1,0:T(8,128)(2,1)S(1)}, bf16[512,1024]{1,0:T(8,128)(2,1)S(1)}, u32[]{:S(2)}, u32[]{:S(2)}) collective-permute-start(bf16[512,1024]{1,0:T(8,128)(2,1)S(1)} %maximum_select_fusion.5), channel_id=1, source_target_pairs={{0,4},{4,0},{8,12},{12,8},{16,20},{20,16},{24,28},{28,24},{1,5},{5... | collective-permute-start | bytes 3145736 | tf_op jit(solution)/shard_map/ppermute | solution.py:1099
  481.4 16.9 %collective-permute-start.70 = (bf16[768,256]{1,0:T(8,128)(2,1)S(1)}, bf16[768,256]{1,0:T(8,128)(2,1)S(1)}, u32[]{:S(2)}, u32[]{:S(2)}) collective-permute-start(bf16[768,256]{1,0:T(8,128)(2,1)S(1)} %add_convert_fusion.11), channel_id=1, source_target_pairs={{0,4},{4,0},{8,12},{12,8},{16,20},{20,16},{24,28},{28,24},{1,5},{5... | collective-permute-start | bytes 1179656 | tf_op jit(solution)/shard_map/ppermute | solution.py:1099
  481.5 21.2 %collective-permute-start.69 = (bf16[128,1024]{1,0:T(8,128)(2,1)S(1)}, bf16[128,1024]{1,0:T(8,128)(2,1)S(1)}, u32[]{:S(2)}, u32[]{:S(2)}) collective-permute-start(bf16[128,1024]{1,0:T(8,128)(2,1)S(1)} %add_convert_fusion.15), channel_id=1, source_target_pairs={{0,16},{4,20},{8,24},{12,28},{16,0},{20,4},{24,8},{28,12},{1,17},{... | collective-permute-start | bytes 786440 | tf_op jit(solution)/shard_map/ppermute | solution.py:1099
  481.6 35.2 %collective-permute-start.68 = (f32[8,1024]{1,0:T(8,128)S(1)}, f32[8,1024]{1,0:T(8,128)S(1)}, u32[]{:S(2)}, u32[]{:S(2)}) collective-permute-start(f32[8,1024]{1,0:T(8,128)S(1)} %add.269), channel_id=1, source_target_pairs={{0,4},{4,0},{8,12},{12,8},{16,20},{20,16},{24,28},{28,24},{1,5},{5... | collective-permute-start | bytes 98312 | tf_op jit(solution)/shard_map/ppermute | solution.py:1099
  490.7 29.6 %collective-permute-start.64 = (bf16[64,1024]{1,0:T(8,128)(2,1)S(1)}, bf16[64,1024]{1,0:T(8,128)(2,1)}, u32[]{:S(2)}, u32[]{:S(2)}) collective-permute-start(bf16[64,1024]{1,0:T(8,128)(2,1)S(1)} %add_convert_fusion.16), channel_id=1, source_target_pairs={{0,2},{2,0},{1,3},{3,1},{4,6},{6,4},{5,7},{7,5},{8,10},{10,8},{9,1... | collective-permute-start | bytes 393224 | tf_op jit(solution)/shard_map/ppermute | solution.py:1096
  498.2 13.9 %collective-permute-start.73 = (bf16[768,256]{1,0:T(8,128)(2,1)S(1)}, bf16[768,256]{1,0:T(8,128)(2,1)S(1)}, u32[]{:S(2)}, u32[]{:S(2)}) collective-permute-start(bf16[768,256]{1,0:T(8,128)(2,1)S(1)} %add_convert_fusion.10), channel_id=1, source_target_pairs={{0,8},{4,12},{8,0},{12,4},{16,24},{20,28},{24,16},{28,20},{1,9},{5... | collective-permute-start | bytes 1179656 | tf_op jit(solution)/shard_map/ppermute | solution.py:1099
  502.8 22.6 %collective-permute-start.75 = (bf16[1536,256]{1,0:T(8,128)(2,1)S(1)}, bf16[1536,256]{1,0:T(8,128)(2,1)S(1)}, u32[]{:S(2)}, u32[]{:S(2)}) collective-permute-start(bf16[1536,256]{1,0:T(8,128)(2,1)S(1)} %maximum_select_fusion.7), channel_id=1, source_target_pairs={{0,8},{4,12},{8,0},{12,4},{16,24},{20,28},{24,16},{28,20},{1,9},{5... | collective-permute-start | bytes 2359304 | tf_op jit(solution)/shard_map/ppermute | solution.py:1099
  503.0 20.5 %collective-permute-start.71 = (bf16[128,1024]{1,0:T(8,128)(2,1)S(1)}, bf16[128,1024]{1,0:T(8,128)(2,1)}, u32[]{:S(2)}, u32[]{:S(2)}) collective-permute-start(bf16[128,1024]{1,0:T(8,128)(2,1)S(1)} %add_convert_fusion.14), channel_id=1, source_target_pairs={{0,8},{4,12},{8,0},{12,4},{16,24},{20,28},{24,16},{28,20},{1,9},{5... | collective-permute-start | bytes 786440 | tf_op jit(solution)/shard_map/ppermute | solution.py:1099
  512.5 17.4 %collective-permute-start.76 = (bf16[1536,256]{1,0:T(8,128)(2,1)S(1)}, bf16[1536,256]{1,0:T(8,128)(2,1)S(1)}, u32[]{:S(2)}, u32[]{:S(2)}) collective-permute-start(bf16[1536,256]{1,0:T(8,128)(2,1)S(1)} %maximum_select_fusion.8), channel_id=1, source_target_pairs={{0,4},{4,0},{8,12},{12,8},{16,20},{20,16},{24,28},{28,24},{1,5},{5... | collective-permute-start | bytes 2359304 | tf_op jit(solution)/shard_map/ppermute | solution.py:1099
  524.7 10.8 %collective-permute-start.74 = (bf16[256,1024]{1,0:T(8,128)(2,1)S(1)}, bf16[256,1024]{1,0:T(8,128)(2,1)S(1)}, u32[]{:S(2)}, u32[]{:S(2)}) collective-permute-start(bf16[256,1024]{1,0:T(8,128)(2,1)S(1)} %maximum_select_fusion.9), channel_id=1, source_target_pairs={{0,4},{4,0},{8,12},{12,8},{16,20},{20,16},{24,28},{28,24},{1,5},{5... | collective-permute-start | bytes 1572872 | tf_op jit(solution)/shard_map/ppermute | solution.py:1099
  (147 other events, 1149.2 us)

commit v14 on v13

--- a/solution.py
+++ b/solution.py
@@ -1129,16 +1129,18 @@
     )
 
     qkv_second = over_z(qkv_first)
-    out_first = over_y(half_of(w_out, near))
+    both_first = over_y(
+        jnp.concatenate([half_of(w_out, near), half_of(w_cross_out, column)], axis=0)
+    )
     query_first = over_y(half_of(w_cross_q, column, 1))
-    cross_out_first = over_y(half_of(w_cross_out, column))
     o0, lse0 = self_forward(limit, q0, k0, v0)
     qf, kf, vf = project(place, h1, qkv_first)
     out_other, query_other, cross_out_other = map(over_core, (w_out, w_cross_q, w_cross_out))
-    qf, o0, out_first, query_first, cross_out_first, w_up, w_down, *core_got = join(
-        (qf, o0, out_first, query_first, cross_out_first, w_up, w_down)
+    qf, o0, both_first, query_first, w_up, w_down, *core_got = join(
+        (qf, o0, both_first, query_first, w_up, w_down)
         + (out_other, query_other, cross_out_other)
     )
+    out_first, cross_out_first = both_first[:128], both_first[128:]
 
     out_other, query_other, cross_out_other = core_got
     out_second = over_z(out_first)
@@ -1427,9 +1429,9 @@
     cross_in.far()
     store["out_fly"] = over_core(out_o)
     text_rows.then(over_core)
-    norms.then(lambda v: along_wide(v, Z_FAR))
     outs.second()
     qkv.far()
+    norms.then(lambda v: along_wide(v, Z_FAR))
     order("x2", "out_fly")
     out_rows = lower(store["x2"] + out_m + store["out_fly"].astype(FULL))
     down.along()

time: 542 us -> 551 us (1.017)
  waiting for transfers between devices: 101 us -> 122 us
  other arithmetic: 46.9 us -> 40.6 us
  starting transfers between devices: 68.5 us -> 62.3 us
    ppermute x34, waiting for transfers between devices: 79.8 us -> 103 us  [along_wide(): return lax.ppermute(v, 'wide', pairs)]
    ppermute x16 -> x15, starting transfers between devices: 19.6 us -> 14.4 us  [over_y(): return lax.ppermute(v, 'narrow', Y_PAIRS)]
    dynamic_slice x14 -> x13, local copies, waits for them, and re-layouts: 8.99 us -> 12.2 us  [half_of(): return lax.dynamic_slice_in_dim(v, which * half, half, axis=axis)]
    convert_element_type x15 -> x17, other arithmetic: 12.3 us -> 14.7 us  [lower(): return values_in.astype(jnp.bfloat16)]
    ppermute x16 -> x15, waiting for transfers between devices: 21 us -> 18.7 us  [over_y(): return lax.ppermute(v, 'narrow', Y_PAIRS)]
    unnamed x269 -> x259, local copies, waits for them, and re-layouts: 24.5 us -> 25.9 us
  transfers between devices with their start and end apart: 77 -> 76, of which waited for: 23 -> 20; matrix products, arithmetic and copies ran while one was open for 12% -> 11% of each run, Pallas kernels for 48% -> 47%
where the time goes in v14:
time: 551 us; the launch traced here: 547 us
  Pallas kernels  269 us (49%)
  waiting for transfers between devices  122 us (22%)
  starting transfers between devices  62.3 us (11%)
  local copies, waits for them, and re-layouts  49.2 us (9%)
  other arithmetic  40.6 us (7%)
    ppermute x34, waiting for transfers between devices, along_wide(): return lax.ppermute(v, 'wide', pairs)  103 us
    pallas_call x4, Pallas kernels, feed(): pl.pallas_call(functools.partial(feed_kernel, parts=parts, carried=len(be...  51.6 us
    ppermute x34, starting transfers between devices, along_wide(): return lax.ppermute(v, 'wide', pairs)  42.9 us
    pallas_call x3, Pallas kernels, self_back(): pl.pallas_call(functools.partial(self_back_kernel, span=span, floor=floor...  39.7 us
    pallas_call x3, Pallas kernels, self_forward(): pl.pallas_call(functools.partial(self_forward_kernel, span=span, floor=fl...  30.8 us
    unnamed x259, local copies, waits for them, and re-layouts  25.9 us
    pallas_call x1, Pallas kernels, middle_back(): pl.pallas_call(middle_back_kernel, grid_spec=pltpu.PrefetchScalarGridSpec...  23 us
    pallas_call x1, Pallas kernels, middle_forward(): pl.pallas_call(middle_forward_kernel, grid_spec=pltpu.PrefetchScalarGridS...  20.7 us
  transfers between devices with their start and end apart: 76, of which 20 were waited for; matrix products, arithmetic and copies ran while one was open for 11% of the time, Pallas kernels for 47%

profile of v14, /device:TPU:0, one launch (start us, length us, event | category | flops | bytes accessed | tf_op | source)
XLA Modules:
  0.0 546.6 jit_solution(5642660036704617941)
XLA Ops:
  1.2 2.2 constant_dynamic-slice_fusion.15
  3.4 2.6 collective-permute-start.1
  10.9 6.2 %first_project.1 = (bf16[1664,1024]{1,0:T(8,128)(2,1)S(1)}, bf16[1664,256]{1,0:T(8,128)(2,1)S(1)}, bf16[1664,256]{1,0:T(8,128)(2,1)S(1)}, bf16[1664,256]{1,0:T(8,128)(2,1)S(1)}) custom-call(s32[3]{0:T(128)S(1)} %add_add_fusion.place_ref, bf16[832,1024]{1,0:T(8,128)(2,1)S(1)} %copy-done.53, bf16[832,1024]{1,0:T(8,128)(2,1)} %collective-permute-done.other_ref, ...), custom_call_target="tpu_custom_call" | custom-call | flops 1610000000 | bytes 1000 | tf_op jit(solution)/shard_map/first_project/pallas_call | solution.py:393
  19.9 4.4 collective-permute-done.1.weight_ref.refs_10_
  24.3 1.8 constant_dynamic-slice_fusion.12
  27.8 1.8 collective-permute-start.2
  29.9 14.1 %self_forward.3 = (bf16[1664,256]{1,0:T(8,128)(2,1)}, f32[2,8,1664]{2,1,0:T(8,128)}) custom-call(s32[1]{0:T(128)} %dynamic_slice.129.limit_ref, bf16[1664,256]{1,0:T(8,128)(2,1)} %copy-done.61, bf16[1664,256]{1,0:T(8,128)(2,1)} %copy-done.63, bf16[1664,256]{1,0:T(8,128)(2,1)} %copy-done.65), custom_call_target="tpu_custom_call" | custom-call | flops 4701199872 | bytes 1000 | tf_op jit(solution)/shard_map/self_forward/pallas_call | solution.py:525
  43.9 12.7 %project.2 = (bf16[1664,128]{1,0:T(8,128)(2,1)S(1)}, bf16[1664,128]{1,0:T(8,128)(2,1)S(1)}, bf16[1664,128]{1,0:T(8,128)(2,1)S(1)}) custom-call(s32[3]{0:T(128)S(1)} %add_add_fusion.place_ref, bf16[1664,1024]{1,0:T(8,128)(2,1)S(1)} %get-tuple-element.267.h_ref, bf16[3,1024,128]{2,1,0:T(8,128)(2,1)S(1)} %collective-permute-done.1.weight_ref.refs_10_), custom_call_target="tpu_custom_call" | custom-call | flops 1288000000 | bytes 1000 | tf_op jit(solution)/shard_map/project/pallas_call | solution.py:423
  58.2 1.8 collective-permute-start.8
  67.0 8.3 %self_forward.4 = (bf16[1664,128]{1,0:T(8,128)(2,1)}, f32[1,8,1664]{2,1,0:T(8,128)}) custom-call(s32[1]{0:T(128)} %dynamic_slice.129.limit_ref, bf16[1664,128]{1,0:T(8,128)(2,1)} %copy-done.68, bf16[1664,128]{1,0:T(8,128)(2,1)} %copy-done.70, bf16[1664,128]{1,0:T(8,128)(2,1)} %copy-done.72), custom_call_target="tpu_custom_call" | custom-call | flops 2350599936 | bytes 1000 | tf_op jit(solution)/shard_map/self_forward/pallas_call | solution.py:525
  75.4 5.2 collective-permute-done.7.weight_ref.refs_11_
  84.3 2.7 project.3
  89.9 8.4 %self_forward.5 = (bf16[1664,128]{1,0:T(8,128)(2,1)}, f32[1,8,1664]{2,1,0:T(8,128)}) custom-call(s32[1]{0:T(128)} %dynamic_slice.129.limit_ref, bf16[1664,128]{1,0:T(8,128)(2,1)} %copy-done.74, bf16[1664,128]{1,0:T(8,128)(2,1)} %copy-done.76, bf16[1664,128]{1,0:T(8,128)(2,1)} %copy-done.78), custom_call_target="tpu_custom_call" | custom-call | flops 2350599936 | bytes 1000 | tf_op jit(solution)/shard_map/self_forward/pallas_call | solution.py:525
  105.6 20.7 %middle_forward.1 = (f32[832,1024]{1,0:T(8,128)}, f32[832,1024]{1,0:T(8,128)}, bf16[832,1024]{1,0:T(8,128)(2,1)}, bf16[832,1024]{1,0:T(8,128)(2,1)}, bf16[832,10...) custom-call(s32[3]{0:T(128)} %copy-done.85, bf16[832,1024]{1,0:T(8,128)(2,1)} %frame_ref.3, ...), custom_call_target="tpu_custom_call" | custom-call | flops 7084000256 | bytes 1000 | tf_op jit(solution)/shard_map/middle_forward/pallas_call | solution.py:677
  128.4 12.1 %feed.4 = (bf16[1664,1024]{1,0:T(8,128)(2,1)}, bf16[1664,1024]{1,0:T(8,128)(2,1)}, f32[832,1024]{1,0:T(8,128)}, f32[832,1024]{1,0:T(8,128)}) custom-call(s32[3]{0:T(128)} %copy-done.85, bf16[832,1024]{1,0:T(8,128)(2,1)} %get-tuple-element.310.h_ref.mine_ref, bf16[832,1024]{1,0:T(8,128)(2,1)} %copy-done, bf16[1024,1024]{1,0:T(8,128)(2,1)} %refs_0_.1, ...), custom_call_target="tpu_custom_call" | custom-call | flops 4185999872 | bytes 1000 | tf_op jit(solution)/shard_map/feed/pallas_call | solution.py:756
  142.2 12.1 %feed.5 = (bf16[1664,1024]{1,0:T(8,128)(2,1)}, bf16[1664,1024]{1,0:T(8,128)(2,1)}, f32[832,1024]{1,0:T(8,128)}, f32[832,1024]{1,0:T(8,128)}) custom-call(s32[3]{0:T(128)} %copy-done.85, bf16[832,1024]{1,0:T(8,128)(2,1)} %copy-done.16, bf16[832,1024]{1,0:T(8,128)(2,1)} %copy-done.13, ...), custom_call_target="tpu_custom_call", output_to_operand_aliasing={{0}: (5, {}), {1}: (6, {})} | custom-call | flops 4185999872 | bytes 1000 | tf_op jit(solution)/shard_map/feed/pallas_call | solution.py:756
  155.3 13.6 %feed.6 = (bf16[1664,1024]{1,0:T(8,128)(2,1)}, bf16[1664,1024]{1,0:T(8,128)(2,1)}, bf16[832,1024]{1,0:T(8,128)(2,1)}, bf16[832,1024]{1,0:T(8,128)(2,1)}) custom-call(s32[3]{0:T(128)} %copy-done.85, bf16[832,1024]{1,0:T(8,128)(2,1)} %copy-done.16, bf16[832,1024]{1,0:T(8,128)(2,1)} %copy-done.13, bf16[1024,512]{1,0:T(8,128)(2,1)} %copy-done.106, ...), custom_call_target="tpu_custom_call" | custom-call | flops 4185999872 | bytes 1000 | tf_op jit(solution)/shard_map/feed/pallas_call | solution.py:756
  168.9 13.7 %feed.7 = (bf16[1664,1024]{1,0:T(8,128)(2,1)}, bf16[1664,1024]{1,0:T(8,128)(2,1)}, f32[832,1024]{1,0:T(8,128)}, f32[832,1024]{1,0:T(8,128)}) custom-call(s32[3]{0:T(128)} %copy-done.85, bf16[832,1024]{1,0:T(8,128)(2,1)} %get-tuple-element.310.h_ref.mine_ref, bf16[832,1024]{1,0:T(8,128)(2,1)} %copy-done, ...), custom_call_target="tpu_custom_call", output_to_operand_aliasing={{0}: (9, {}), {1}: (10, {})} | custom-call | flops 4185999872 | bytes 1000 | tf_op jit(solution)/shard_map/feed/pallas_call | solution.py:756
  182.7 7.4 %up_grad.2 = bf16[1024,1024]{1,0:T(8,128)(2,1)} custom-call(bf16[832,1024]{1,0:T(8,128)(2,1)S(1)} %copy-done.3, bf16[832,1024]{1,0:T(8,128)(2,1)S(1)} %copy-done.17, bf16[1664,1024]{1,0:T(8,128)(2,1)} %get-tuple-element.332.du_ref), custom_call_target="tpu_custom_call" | custom-call | flops 241500000 | bytes 1000 | tf_op jit(solution)/shard_map/up_grad/pallas_call | solution.py:786
  190.6 7.2 %down_grad.2 = bf16[1024,1024]{1,0:T(8,128)(2,1)} custom-call(bf16[1664,1024]{1,0:T(8,128)(2,1)} %get-tuple-element.333.g_ref, bf16[832,1024]{1,0:T(8,128)(2,1)S(1)} %copy-done.1, bf16[832,1024]{1,0:T(8,128)(2,1)S(1)} %copy-done.14), custom_call_target="tpu_custom_call" | custom-call | flops 1127000064 | bytes 1000 | tf_op jit(solution)/shard_map/down_grad/pallas_call | solution.py:809
  199.1 23.0 %middle_back.1 = (f32[832,1024]{1,0:T(8,128)}, bf16[832,1024]{1,0:T(8,128)(2,1)}, bf16[832,1024]{1,0:T(8,128)(2,1)}, bf16[832,1024]{1,0:T(8,128)(2,1)}, f32[4,64...) custom-call(s32[3]{0:T(128)} %copy-done.85, f32[832,1024]{1,0:T(8,128)} %get-tuple-element.336.ym_ref, ...), custom_call_target="tpu_custom_call" | custom-call | flops 827862016 | bytes 1000 | tf_op jit(solution)/shard_map/middle_back/pallas_call | solution.py:992
  224.1 6.4 %up_grad.3 = bf16[1024,1024]{1,0:T(8,128)(2,1)S(1)} custom-call(bf16[832,1024]{1,0:T(8,128)(2,1)S(1)} %copy-done.3, bf16[832,1024]{1,0:T(8,128)(2,1)S(1)} %copy-done.18, bf16[1664,1024]{1,0:T(8,128)(2,1)} %get-tuple-element.344.du_ref), custom_call_target="tpu_custom_call" | custom-call | flops 241500000 | bytes 1000 | tf_op jit(solution)/shard_map/up_grad/pallas_call | solution.py:786
  230.5 7.9 %collective-permute-done.30 = bf16[1024,1024]{1,0:T(8,128)(2,1)} collective-permute-done((bf16[1024,1024]{1,0:T(8,128)(2,1)}, bf16[1024,1024]{1,0:T(8,128)(2,1)}, u32[]{:S(2)}, u32[]{:S(2)}) %collective-permute-start.30) | collective-permute-done | bytes 2097184 | tf_op jit(solution)/shard_map/ppermute | solution.py:1096
  239.6 4.1 add_convert_fusion.2
  249.8 4.0 pull.1
  255.2 9.4 %self_back.3 = (bf16[1664,128]{1,0:T(8,128)(2,1)S(1)}, bf16[1664,128]{1,0:T(8,128)(2,1)S(1)}, bf16[1664,128]{1,0:T(8,128)(2,1)S(1)}) custom-call(s32[1]{0:T(128)} %dynamic_slice.129.limit_ref, bf16[1664,128]{1,0:T(8,128)(2,1)S(1)} %copy-done.69, bf16[1664,128]{1,0:T(8,128)(2,1)S(1)} %copy-done.71, bf16[1664,128]{1,0:T(8,128)(2,1)S(1)} %copy-done.73, ...), custom_call_target="tpu_custom_call" | custom-call | flops 338100000 | bytes 1000 | tf_op jit(solution)/shard_map/self_back/pallas_call | solution.py:606
  264.7 5.6 %query_grad.2 = bf16[1024,256]{1,0:T(8,128)(2,1)} custom-call(s32[3]{0:T(128)S(1)} %copy-done.86, bf16[832,1024]{1,0:T(8,128)(2,1)} %get-tuple-element.357.mine_ref, bf16[832,1024]{1,0:T(8,128)(2,1)} %collective-permute-done.34.other_ref, bf16[832,1024]{1,0:T(8,128)(2,1)} %get-tuple-element.421.dm_ref, bf16[832,512]{1,0:T(8,128)(2,1)S(1)} %collective-permute-done.33.do_ref), custom_call_target="tpu_custom_call" | custom-call | flops 138138000 | bytes 1000 | tf_op jit(solution)/shard_map/query_grad/pallas_call | solution.py:875
  274.9 9.8 %self_back.4 = (bf16[1664,128]{1,0:T(8,128)(2,1)S(1)}, bf16[1664,128]{1,0:T(8,128)(2,1)S(1)}, bf16[1664,128]{1,0:T(8,128)(2,1)S(1)}) custom-call(s32[1]{0:T(128)} %dynamic_slice.129.limit_ref, bf16[1664,128]{1,0:T(8,128)(2,1)S(1)} %copy-done.75, bf16[1664,128]{1,0:T(8,128)(2,1)S(1)} %copy-done.77, bf16[1664,128]{1,0:T(8,128)(2,1)S(1)} %copy-done.79, ...), custom_call_target="tpu_custom_call" | custom-call | flops 338100000 | bytes 1000 | tf_op jit(solution)/shard_map/self_back/pallas_call | solution.py:606
  284.8 2.2 collective-permute-done.37
  287.1 6.2 %down_grad.3 = bf16[1024,1024]{1,0:T(8,128)(2,1)S(1)} custom-call(bf16[1664,1024]{1,0:T(8,128)(2,1)} %get-tuple-element.382.g_ref, bf16[832,1024]{1,0:T(8,128)(2,1)S(1)} %copy-done.2, bf16[832,1024]{1,0:T(8,128)(2,1)S(1)} %copy-done.15), custom_call_target="tpu_custom_call" | custom-call | flops 1127000064 | bytes 1000 | tf_op jit(solution)/shard_map/down_grad/pallas_call | solution.py:809
  293.4 7.3 %qkv_grad.2 = bf16[3072,256]{1,0:T(8,128)(2,1)} custom-call(s32[3]{0:T(128)S(1)} %copy-done.86, bf16[1664,1024]{1,0:T(8,128)(2,1)} %copy-done.8, bf16[1664,128]{1,0:T(8,128)(2,1)S(1)} %get-tuple-element.365.refs_0_.refs_3_, bf16[1664,128]{1,0:T(8,128)(2,1)S(1)} %get-tuple-element.366.refs_1_.refs_4_, ...), custom_call_target="tpu_custom_call" | custom-call | flops 1127000064 | bytes 1000 | tf_op jit(solution)/shard_map/qkv_grad/pallas_call | solution.py:846
  300.7 2.0 collective-permute-done.32
  302.7 2.6 convert_add_fusion.1
  307.7 2.7 collective-permute-start.41
  315.0 20.5 %self_back.5 = (bf16[1664,256]{1,0:T(8,128)(2,1)S(1)}, bf16[1664,256]{1,0:T(8,128)(2,1)S(1)}, bf16[1664,256]{1,0:T(8,128)(2,1)S(1)}) custom-call(s32[1]{0:T(128)} %dynamic_slice.129.limit_ref, bf16[1664,256]{1,0:T(8,128)(2,1)S(1)} %copy-done.62, bf16[1664,256]{1,0:T(8,128)(2,1)S(1)} %copy-done.64, bf16[1664,256]{1,0:T(8,128)(2,1)S(1)} %copy-done.66, ...), custom_call_target="tpu_custom_call" | custom-call | flops 676200000 | bytes 1000 | tf_op jit(solution)/shard_map/self_back/pallas_call | solution.py:606
  342.4 5.2 outputs_grad.2
  347.6 5.8 %first_back.2 = bf16[832,1024]{1,0:T(8,128)(2,1)} custom-call(s32[3]{0:T(128)S(1)} %add_add_fusion.1.place_ref, bf16[1664,256]{1,0:T(8,128)(2,1)S(1)} %get-tuple-element.428.refs_0_, bf16[1664,256]{1,0:T(8,128)(2,1)S(1)} %get-tuple-element.410.refs_1_, bf16[1664,256]{1,0:T(8,128)(2,1)S(1)} %get-tuple-element.411.refs_2_, bf16[1664,128]{1,0:T(8,128)(2,1)S(1)} %copy-done.23, ...), custom_call_target="tpu_custom_call" | custom-call | flops 172270000 | bytes 1000 | tf_op jit(solution)/shard_map/first_back/pallas_call | solution.py:1026
  356.0 6.0 %qkv_grad.3 = bf16[3072,256]{1,0:T(8,128)(2,1)S(1)} custom-call(s32[3]{0:T(128)S(1)} %copy-done.86, bf16[1664,1024]{1,0:T(8,128)(2,1)} %copy-done.8, bf16[1664,256]{1,0:T(8,128)(2,1)S(1)} %get-tuple-element.428.refs_0_, bf16[1664,256]{1,0:T(8,128)(2,1)S(1)} %get-tuple-element.410.refs_1_, bf16[1664,256]{1,0:T(8,128)(2,1)S(1)} %get-tuple-element.411.refs_2_), custom_call_target="tpu_custom_call" | custom-call | flops 1127000064 | bytes 1000 | tf_op jit(solution)/shard_map/qkv_grad/pallas_call | solution.py:846
  362.0 3.2 add_convert_fusion.3
  368.8 3.9 query_grad.3
  377.9 4.9 first_back.3.ym_ref
  383.2 11.6 %collective-permute-done.57 = bf16[256,1024]{1,0:T(8,128)(2,1)} collective-permute-done((bf16[256,1024]{1,0:T(8,128)(2,1)S(1)}, bf16[256,1024]{1,0:T(8,128)(2,1)}, u32[]{:S(2)}, u32[]{:S(2)}) %collective-permute-start.57) | collective-permute-done | bytes 524320 | tf_op jit(solution)/shard_map/ppermute | solution.py:1099
  396.4 6.0 %frames_back.1 = (bf16[832,1024]{1,0:T(8,128)(2,1)}, f32[8,1024]{1,0:T(8,128)S(1)}) custom-call(s32[3]{0:T(128)S(1)} %copy-done.86, f32[832,1024]{1,0:T(8,128)S(1)} %first_back.3.ym_ref, bf16[832,1024]{1,0:T(8,128)(2,1)} %collective-permute-done.47.yr_ref, f32[832,1024]{1,0:T(8,128)S(1)} %copy-done.42, bf16[832,1024]{1,0:T(8,128)(2,1)S(1)} %copy-done.54, ...), custom_call_target="tpu_custom_call" | custom-call | flops 207046000 | bytes 1000 | tf_op jit(solution)/shard_map/frames_back/pallas_call | solution.py:1061
  406.4 8.9 %collective-permute-done.52 = bf16[1536,256]{1,0:T(8,128)(2,1)S(1)} collective-permute-done((bf16[1536,256]{1,0:T(8,128)(2,1)S(1)}, bf16[1536,256]{1,0:T(8,128)(2,1)S(1)}, u32[]{:S(2)}, u32[]{:S(2)}) %collective-permute-start.52) | collective-permute-done | bytes 786464 | tf_op jit(solution)/shard_map/ppermute | solution.py:1099
  415.6 5.1 outputs_grad.3
  423.8 5.2 fusion
  429.6 3.3 collective-permute-done.50
  433.0 1.9 collective-permute-start.62
  435.2 2.0 collective-permute-start.53
  437.2 2.7 collective-permute-start.61
  440.0 22.0 %collective-permute-done.54 = bf16[768,256]{1,0:T(8,128)(2,1)S(1)} collective-permute-done((bf16[768,256]{1,0:T(8,128)(2,1)S(1)}, bf16[768,256]{1,0:T(8,128)(2,1)S(1)}, u32[]{:S(2)}, u32[]{:S(2)}) %collective-permute-start.54) | collective-permute-done | bytes 393248 | tf_op jit(solution)/shard_map/ppermute | solution.py:1099
  462.4 3.0 collective-permute-start.65
  468.3 9.6 %collective-permute-done.66 = bf16[128,1024]{1,0:T(8,128)(2,1)S(1)} collective-permute-done((bf16[128,1024]{1,0:T(8,128)(2,1)S(1)}, bf16[128,1024]{1,0:T(8,128)(2,1)S(1)}, u32[]{:S(2)}, u32[]{:S(2)}) %collective-permute-start.66) | collective-permute-done | bytes 262176 | tf_op jit(solution)/shard_map/ppermute | solution.py:1099
  478.0 2.9 collective-permute-start.68
  480.9 8.4 %collective-permute-done.65 = f32[8,1024]{1,0:T(8,128)S(1)} collective-permute-done((f32[8,1024]{1,0:T(8,128)S(1)}, f32[8,1024]{1,0:T(8,128)S(1)}, u32[]{:S(2)}, u32[]{:S(2)}) %collective-permute-start.65) | collective-permute-done | bytes 32800 | tf_op jit(solution)/shard_map/ppermute | solution.py:1099
  490.4 9.3 %collective-permute-done.69 = bf16[768,256]{1,0:T(8,128)(2,1)S(1)} collective-permute-done((bf16[768,256]{1,0:T(8,128)(2,1)S(1)}, bf16[768,256]{1,0:T(8,128)(2,1)S(1)}, u32[]{:S(2)}, u32[]{:S(2)}) %collective-permute-start.69) | collective-permute-done | bytes 393248 | tf_op jit(solution)/shard_map/ppermute | solution.py:1099
  499.7 1.7 collective-permute-start.72
  502.2 1.8 collective-permute-start.70
  504.0 3.0 fusion.1
  507.0 4.8 collective-permute-done.72
  512.7 2.3 add_convert_fusion
  517.0 14.8 %collective-permute-done.70 = bf16[128,1024]{1,0:T(8,128)(2,1)} collective-permute-done((bf16[128,1024]{1,0:T(8,128)(2,1)S(1)}, bf16[128,1024]{1,0:T(8,128)(2,1)}, u32[]{:S(2)}, u32[]{:S(2)}) %collective-permute-start.70) | collective-permute-done | bytes 262176 | tf_op jit(solution)/shard_map/ppermute | solution.py:1099
  536.5 3.4 fusion.3
  539.8 4.7 collective-permute-done.73
  (472 shorter events, 103.9 us)
Async XLA Ops:
  3.4 20.9 %collective-permute-start.1 = (bf16[3,1024,128]{2,1,0:T(8,128)(2,1)}, bf16[3,1024,128]{2,1,0:T(8,128)(2,1)S(1)}, u32[]{:S(2)}, u32[]{:S(2)}) collective-permute-start(bf16[3,1024,128]{2,1,0:T(8,128)(2,1)} %constant_dynamic-slice_fusion.15), channel_id=1, source_target_pairs={{0,2},{2,0},{1,3},{3,1},{4,6},{6,4},{5,7},{7,5},{8,10},{10,8},{9,1... | collective-permute-start | bytes 2359304 | tf_op jit(solution)/shard_map/ppermute | solution.py:1096
  24.3 37.4 %collective-permute-start.5 = (bf16[1024,256]{1,0:T(8,128)(2,1)}, bf16[1024,256]{1,0:T(8,128)(2,1)S(1)}, u32[]{:S(2)}, u32[]{:S(2)}) collective-permute-start(bf16[1024,256]{1,0:T(8,128)(2,1)} %refs_0_.2), channel_id=1, source_target_pairs={{0,1},{1,0},{2,3},{3,2},{4,5},{5,4},{6,7},{7,6},{8,9},{9,8},{10,11... | collective-permute-start | bytes 1572872 | tf_op jit(solution)/shard_map/ppermute | solution.py:1093
  26.1 35.5 %collective-permute-start.4 = (bf16[256,1024]{1,0:T(8,128)(2,1)S(1)}, bf16[256,1024]{1,0:T(8,128)(2,1)}, u32[]{:S(2)}, u32[]{:S(2)}) collective-permute-start(bf16[256,1024]{1,0:T(8,128)(2,1)S(1)} %copy-done.55), channel_id=1, source_target_pairs={{0,1},{1,0},{2,3},{3,2},{4,5},{5,4},{6,7},{7,6},{8,9},{9,8},{10,11... | collective-permute-start | bytes 1572872 | tf_op jit(solution)/shard_map/ppermute | solution.py:1093
  27.5 34.2 %collective-permute-start.6 = (bf16[256,1024]{1,0:T(8,128)(2,1)}, bf16[256,1024]{1,0:T(8,128)(2,1)S(1)}, u32[]{:S(2)}, u32[]{:S(2)}) collective-permute-start(bf16[256,1024]{1,0:T(8,128)(2,1)} %refs_6_.1), channel_id=1, source_target_pairs={{0,1},{1,0},{2,3},{3,2},{4,5},{5,4},{6,7},{7,6},{8,9},{9,8},{10,11... | collective-permute-start | bytes 1572872 | tf_op jit(solution)/shard_map/ppermute | solution.py:1093
  27.8 32.3 %collective-permute-start.2 = (bf16[256,1024]{1,0:T(8,128)(2,1)S(1)}, bf16[256,1024]{1,0:T(8,128)(2,1)}, u32[]{:S(2)}, u32[]{:S(2)}) collective-permute-start(bf16[256,1024]{1,0:T(8,128)(2,1)S(1)} %pad_maximum_fusion.1), channel_id=1, source_target_pairs={{0,2},{2,0},{1,3},{3,1},{4,6},{6,4},{5,7},{7,5},{8,10},{10,8},{9,1... | collective-permute-start | bytes 1572872 | tf_op jit(solution)/shard_map/ppermute | solution.py:1096
  29.6 28.6 %collective-permute-start.3 = (bf16[1024,128]{1,0:T(8,128)(2,1)}, bf16[1024,128]{1,0:T(8,128)(2,1)S(1)}, u32[]{:S(2)}, u32[]{:S(2)}) collective-permute-start(bf16[1024,128]{1,0:T(8,128)(2,1)} %constant_dynamic-slice_fusion.12), channel_id=1, source_target_pairs={{0,2},{2,0},{1,3},{3,1},{4,6},{6,4},{5,7},{7,5},{8,10},{10,8},{9,1... | collective-permute-start | bytes 786440 | tf_op jit(solution)/shard_map/ppermute | solution.py:1096
  58.2 17.1 %collective-permute-start.8 = (bf16[2,64,256]{2,1,0:T(8,128)(2,1)S(1)}, bf16[2,64,256]{2,1,0:T(8,128)(2,1)S(1)}, u32[]{:S(2)}, u32[]{:S(2)}) collective-permute-start(bf16[2,64,256]{2,1,0:T(8,128)(2,1)S(1)} %get-tuple-element.547), channel_id=1, source_target_pairs={{0,2},{2,0},{1,3},{3,1},{4,6},{6,4},{5,7},{7,5},{8,10},{10,8},{9,1... | collective-permute-start | bytes 196616 | tf_op jit(solution)/shard_map/ppermute | solution.py:1096
  60.0 20.5 %collective-permute-start.7 = (bf16[3,1024,128]{2,1,0:T(8,128)(2,1)S(1)}, bf16[3,1024,128]{2,1,0:T(8,128)(2,1)S(1)}, u32[]{:S(2)}, u32[]{:S(2)}) collective-permute-start(bf16[3,1024,128]{2,1,0:T(8,128)(2,1)S(1)} %collective-permute-done.1.weight_ref.refs_10_), channel_id=1, source_target_pairs={{0,8},{4,12},{8,0},{12,4},{16,24},{20,28},{24,16},{28,20},{1,9},{5... | collective-permute-start | bytes 2359304 | tf_op jit(solution)/shard_map/ppermute | solution.py:1099
  62.6 19.5 %collective-permute-start.9 = (bf16[832,256]{1,0:T(8,128)(2,1)}, bf16[832,256]{1,0:T(8,128)(2,1)}, u32[]{:S(2)}, u32[]{:S(2)}) collective-permute-start(bf16[832,256]{1,0:T(8,128)(2,1)} %constant_dynamic-slice_fusion.11), channel_id=1, source_target_pairs={{0,1},{1,0},{2,3},{3,2},{4,5},{5,4},{6,7},{7,6},{8,9},{9,8},{10,11... | collective-permute-start | bytes 1277960 | tf_op jit(solution)/shard_map/ppermute | solution.py:1093
  63.8 35.2 %collective-permute-start.13 = (bf16[1024,512]{1,0:T(8,128)(2,1)}, bf16[1024,512]{1,0:T(8,128)(2,1)S(1)}, u32[]{:S(2)}, u32[]{:S(2)}) collective-permute-start(bf16[1024,512]{1,0:T(8,128)(2,1)} %constant_dynamic-slice_fusion.10), channel_id=1, source_target_pairs={{0,2},{2,0},{1,3},{3,1},{4,6},{6,4},{5,7},{7,5},{8,10},{10,8},{9,1... | collective-permute-start | bytes 3145736 | tf_op jit(solution)/shard_map/ppermute | solution.py:1096
  65.4 23.9 %collective-permute-start.10 = (bf16[128,1024]{1,0:T(8,128)(2,1)S(1)}, bf16[128,1024]{1,0:T(8,128)(2,1)S(1)}, u32[]{:S(2)}, u32[]{:S(2)}) collective-permute-start(bf16[128,1024]{1,0:T(8,128)(2,1)S(1)} %get-tuple-element.539.refs_7_.refs_0_), channel_id=1, source_target_pairs={{0,8},{4,12},{8,0},{12,4},{16,24},{20,28},{24,16},{28,20},{1,9},{5... | collective-permute-start | bytes 786440 | tf_op jit(solution)/shard_map/ppermute | solution.py:1099
  75.3 26.5 %collective-permute-start.17 = (bf16[128,1024]{1,0:T(8,128)(2,1)S(1)}, bf16[128,1024]{1,0:T(8,128)(2,1)}, u32[]{:S(2)}, u32[]{:S(2)}) collective-permute-start(bf16[128,1024]{1,0:T(8,128)(2,1)S(1)} %get-tuple-element.539.refs_7_.refs_0_), channel_id=1, source_target_pairs={{0,1},{1,0},{2,3},{3,2},{4,5},{5,4},{6,7},{7,6},{8,9},{9,8},{10,11... | collective-permute-start | bytes 786440 | tf_op jit(solution)/shard_map/ppermute | solution.py:1093
  82.1 16.2 %collective-permute-start.11 = (bf16[1024,128]{1,0:T(8,128)(2,1)S(1)}, bf16[1024,128]{1,0:T(8,128)(2,1)S(1)}, u32[]{:S(2)}, u32[]{:S(2)}) collective-permute-start(bf16[1024,128]{1,0:T(8,128)(2,1)S(1)} %copy-done.115), channel_id=1, source_target_pairs={{0,4},{4,0},{8,12},{12,8},{16,20},{20,16},{24,28},{28,24},{1,5},{5... | collective-permute-start | bytes 786440 | tf_op jit(solution)/shard_map/ppermute | solution.py:1099
  89.4 9.5 %collective-permute-start.15 = (bf16[832,128]{1,0:T(8,128)(2,1)}, bf16[832,128]{1,0:T(8,128)(2,1)S(1)}, u32[]{:S(2)}, u32[]{:S(2)}) collective-permute-start(bf16[832,128]{1,0:T(8,128)(2,1)} %constant_dynamic-slice_fusion.7), channel_id=1, source_target_pairs={{0,1},{1,0},{2,3},{3,2},{4,5},{5,4},{6,7},{7,6},{8,9},{9,8},{10,11... | collective-permute-start | bytes 638984 | tf_op jit(solution)/shard_map/ppermute | solution.py:1093
  100.3 26.0 %collective-permute-start.23 = (bf16[1024,512]{1,0:T(8,128)(2,1)S(1)}, bf16[1024,512]{1,0:T(8,128)(2,1)}, u32[]{:S(2)}, u32[]{:S(2)}) collective-permute-start(bf16[1024,512]{1,0:T(8,128)(2,1)S(1)} %collective-permute-done.13.refs_0_), channel_id=1, source_target_pairs={{0,4},{4,0},{8,12},{12,8},{16,20},{20,16},{24,28},{28,24},{1,5},{5... | collective-permute-start | bytes 3145736 | tf_op jit(solution)/shard_map/ppermute | solution.py:1099
  101.8 25.5 %collective-permute-start.24 = (bf16[512,1024]{1,0:T(8,128)(2,1)}, bf16[512,1024]{1,0:T(8,128)(2,1)}, u32[]{:S(2)}, u32[]{:S(2)}) collective-permute-start(bf16[512,1024]{1,0:T(8,128)(2,1)} %constant_dynamic-slice_fusion.9), channel_id=1, source_target_pairs={{0,2},{2,0},{1,3},{3,1},{4,6},{6,4},{5,7},{7,5},{8,10},{10,8},{9,1... | collective-permute-start | bytes 3145736 | tf_op jit(solution)/shard_map/ppermute | solution.py:1096
  127.4 13.2 %collective-permute-start.25 = (bf16[832,1024]{1,0:T(8,128)(2,1)}, bf16[832,1024]{1,0:T(8,128)(2,1)S(1)}, u32[]{:S(2)}, u32[]{:S(2)}) collective-permute-start(bf16[832,1024]{1,0:T(8,128)(2,1)} %get-tuple-element.310.h_ref.mine_ref), channel_id=1, source_target_pairs={{0,1},{1,0},{2,3},{3,2},{4,5},{5,4},{6,7},{7,6},{8,9},{9,8},{10,11... | collective-permute-start | bytes 5111816 | tf_op jit(solution)/shard_map/ppermute | solution.py:1093
  127.4 13.2 %collective-permute-start.26 = (bf16[832,1024]{1,0:T(8,128)(2,1)S(1)}, bf16[832,1024]{1,0:T(8,128)(2,1)S(1)}, u32[]{:S(2)}, u32[]{:S(2)}) collective-permute-start(bf16[832,1024]{1,0:T(8,128)(2,1)S(1)} %broadcast_select_fusion.d_ref.mine_ref), channel_id=1, source_target_pairs={{0,1},{1,0},{2,3},{3,2},{4,5},{5,4},{6,7},{7,6},{8,9},{9,8},{10,11... | collective-permute-start | bytes 5111816 | tf_op jit(solution)/shard_map/ppermute | solution.py:1093
  127.9 26.5 %collective-permute-start.27 = (bf16[512,1024]{1,0:T(8,128)(2,1)}, bf16[512,1024]{1,0:T(8,128)(2,1)S(1)}, u32[]{:S(2)}, u32[]{:S(2)}) collective-permute-start(bf16[512,1024]{1,0:T(8,128)(2,1)} %collective-permute-done.24.refs_2_), channel_id=1, source_target_pairs={{0,4},{4,0},{8,12},{12,8},{16,20},{20,16},{24,28},{28,24},{1,5},{5... | collective-permute-start | bytes 3145736 | tf_op jit(solution)/shard_map/ppermute | solution.py:1099
  168.9 28.9 %collective-permute-start.28 = (bf16[832,1024]{1,0:T(8,128)(2,1)}, bf16[832,1024]{1,0:T(8,128)(2,1)S(1)}, u32[]{:S(2)}, u32[]{:S(2)}) collective-permute-start(bf16[832,1024]{1,0:T(8,128)(2,1)} %get-tuple-element.322), channel_id=1, source_target_pairs={{0,1},{1,0},{2,3},{3,2},{4,5},{5,4},{6,7},{7,6},{8,9},{9,8},{10,11... | collective-permute-start | bytes 5111816 | tf_op jit(solution)/shard_map/ppermute | solution.py:1093
  190.0 48.3 %collective-permute-start.30 = (bf16[1024,1024]{1,0:T(8,128)(2,1)}, bf16[1024,1024]{1,0:T(8,128)(2,1)}, u32[]{:S(2)}, u32[]{:S(2)}) collective-permute-start(bf16[1024,1024]{1,0:T(8,128)(2,1)} %up_grad.2), channel_id=1, source_target_pairs={{0,2},{2,0},{1,3},{3,1},{4,6},{6,4},{5,7},{7,5},{8,10},{10,8},{9,1... | collective-permute-start | bytes 6291464 | tf_op jit(solution)/shard_map/ppermute | solution.py:1096
  222.1 16.3 %collective-permute-start.31 = (bf16[832,1024]{1,0:T(8,128)(2,1)}, bf16[832,1024]{1,0:T(8,128)(2,1)S(1)}, u32[]{:S(2)}, u32[]{:S(2)}) collective-permute-start(bf16[832,1024]{1,0:T(8,128)(2,1)} %get-tuple-element.360.mine_ref.refs_2_.refs_1_), channel_id=1, source_target_pairs={{0,1},{1,0},{2,3},{3,2},{4,5},{5,4},{6,7},{7,6},{8,9},{9,8},{10,11... | collective-permute-start | bytes 5111816 | tf_op jit(solution)/shard_map/ppermute | solution.py:1093
  222.3 42.3 %collective-permute-start.34 = (bf16[832,1024]{1,0:T(8,128)(2,1)}, bf16[832,1024]{1,0:T(8,128)(2,1)}, u32[]{:S(2)}, u32[]{:S(2)}) collective-permute-start(bf16[832,1024]{1,0:T(8,128)(2,1)} %get-tuple-element.357.mine_ref), channel_id=1, source_target_pairs={{0,1},{1,0},{2,3},{3,2},{4,5},{5,4},{6,7},{7,6},{8,9},{9,8},{10,11... | collective-permute-start | bytes 5111816 | tf_op jit(solution)/shard_map/ppermute | solution.py:1093
  244.7 20.0 %collective-permute-start.33 = (bf16[832,512]{1,0:T(8,128)(2,1)}, bf16[832,512]{1,0:T(8,128)(2,1)S(1)}, u32[]{:S(2)}, u32[]{:S(2)}) collective-permute-start(bf16[832,512]{1,0:T(8,128)(2,1)} %slice.86), channel_id=1, source_target_pairs={{0,1},{1,0},{2,3},{3,2},{4,5},{5,4},{6,7},{7,6},{8,9},{9,8},{10,11... | collective-permute-start | bytes 2555912 | tf_op jit(solution)/shard_map/ppermute | solution.py:1093
  244.7 26.6 %collective-permute-start.36 = (bf16[512,1024]{1,0:T(8,128)(2,1)}, bf16[512,1024]{1,0:T(8,128)(2,1)}, u32[]{:S(2)}, u32[]{:S(2)}) collective-permute-start(bf16[512,1024]{1,0:T(8,128)(2,1)} %get-tuple-element.524), channel_id=1, source_target_pairs={{0,4},{4,0},{8,12},{12,8},{16,20},{20,16},{24,28},{28,24},{1,5},{5... | collective-permute-start | bytes 3145736 | tf_op jit(solution)/shard_map/ppermute | solution.py:1099
  247.1 17.6 %collective-permute-start.35 = (f32[2,2,64,256]{3,2,0,1:T(8,128)}, f32[2,2,64,256]{3,2,0,1:T(8,128)}, u32[]{:S(2)}, u32[]{:S(2)}) collective-permute-start(f32[2,2,64,256]{3,2,0,1:T(8,128)} %get-tuple-element.537), channel_id=1, source_target_pairs={{0,1},{1,0},{2,3},{3,2},{4,5},{5,4},{6,7},{7,6},{8,9},{9,8},{10,11... | collective-permute-start | bytes 786440 | tf_op jit(solution)/shard_map/ppermute | solution.py:1093
  254.7 48.0 %collective-permute-start.32 = (bf16[1024,1024]{1,0:T(8,128)(2,1)}, bf16[1024,1024]{1,0:T(8,128)(2,1)S(1)}, u32[]{:S(2)}, u32[]{:S(2)}) collective-permute-start(bf16[1024,1024]{1,0:T(8,128)(2,1)} %down_grad.2), channel_id=1, source_target_pairs={{0,2},{2,0},{1,3},{3,1},{4,6},{6,4},{5,7},{7,5},{8,10},{10,8},{9,1... | collective-permute-start | bytes 6291464 | tf_op jit(solution)/shard_map/ppermute | solution.py:1096
  273.0 13.9 %collective-permute-start.37 = (bf16[256,1024]{1,0:T(8,128)(2,1)S(1)}, bf16[256,1024]{1,0:T(8,128)(2,1)S(1)}, u32[]{:S(2)}, u32[]{:S(2)}) collective-permute-start(bf16[256,1024]{1,0:T(8,128)(2,1)S(1)} %dynamic-slice_convert_fusion.1), channel_id=1, source_target_pairs={{0,8},{4,12},{8,0},{12,4},{16,24},{20,28},{24,16},{28,20},{1,9},{5... | collective-permute-start | bytes 1572872 | tf_op jit(solution)/shard_map/ppermute | solution.py:1099
  305.3 30.2 %collective-permute-start.38 = (bf16[512,1024]{1,0:T(8,128)(2,1)}, bf16[512,1024]{1,0:T(8,128)(2,1)}, u32[]{:S(2)}, u32[]{:S(2)}) collective-permute-start(bf16[512,1024]{1,0:T(8,128)(2,1)} %get-tuple-element.523), channel_id=1, source_target_pairs={{0,4},{4,0},{8,12},{12,8},{16,20},{20,16},{24,28},{28,24},{1,5},{5... | collective-permute-start | bytes 3145736 | tf_op jit(solution)/shard_map/ppermute | solution.py:1099
  305.8 36.6 %collective-permute-start.39 = (bf16[832,1024]{1,0:T(8,128)(2,1)}, bf16[832,1024]{1,0:T(8,128)(2,1)}, u32[]{:S(2)}, u32[]{:S(2)}) collective-permute-start(bf16[832,1024]{1,0:T(8,128)(2,1)} %get-tuple-element.444.refs_6_.refs_5_), channel_id=1, source_target_pairs={{0,1},{1,0},{2,3},{3,2},{4,5},{5,4},{6,7},{7,6},{8,9},{9,8},{10,11... | collective-permute-start | bytes 5111816 | tf_op jit(solution)/shard_map/ppermute | solution.py:1093
  305.8 56.2 %collective-permute-start.44 = (bf16[3072,256]{1,0:T(8,128)(2,1)}, bf16[3072,256]{1,0:T(8,128)(2,1)}, u32[]{:S(2)}, u32[]{:S(2)}) collective-permute-start(bf16[3072,256]{1,0:T(8,128)(2,1)} %qkv_grad.2), channel_id=1, source_target_pairs={{0,2},{2,0},{1,3},{3,1},{4,6},{6,4},{5,7},{7,5},{8,10},{10,8},{9,1... | collective-permute-start | bytes 4718600 | tf_op jit(solution)/shard_map/ppermute | solution.py:1096
  307.3 33.4 %collective-permute-start.40 = (bf16[832,512]{1,0:T(8,128)(2,1)}, bf16[832,512]{1,0:T(8,128)(2,1)}, u32[]{:S(2)}, u32[]{:S(2)}) collective-permute-start(bf16[832,512]{1,0:T(8,128)(2,1)} %slice.92), channel_id=1, source_target_pairs={{0,1},{1,0},{2,3},{3,2},{4,5},{5,4},{6,7},{7,6},{8,9},{9,8},{10,11... | collective-permute-start | bytes 2555912 | tf_op jit(solution)/shard_map/ppermute | solution.py:1093
  307.7 32.2 %collective-permute-start.41 = (bf16[256,1024]{1,0:T(8,128)(2,1)S(1)}, bf16[256,1024]{1,0:T(8,128)(2,1)S(1)}, u32[]{:S(2)}, u32[]{:S(2)}) collective-permute-start(bf16[256,1024]{1,0:T(8,128)(2,1)S(1)} %add_convert_fusion.9), channel_id=1, source_target_pairs={{0,16},{4,20},{8,24},{12,28},{16,0},{20,4},{24,8},{28,12},{1,17},{... | collective-permute-start | bytes 1572872 | tf_op jit(solution)/shard_map/ppermute | solution.py:1099
  335.5 38.8 %collective-permute-start.45 = (bf16[1024,256]{1,0:T(8,128)(2,1)}, bf16[1024,256]{1,0:T(8,128)(2,1)S(1)}, u32[]{:S(2)}, u32[]{:S(2)}) collective-permute-start(bf16[1024,256]{1,0:T(8,128)(2,1)} %query_grad.2), channel_id=1, source_target_pairs={{0,2},{2,0},{1,3},{3,1},{4,6},{6,4},{5,7},{7,5},{8,10},{10,8},{9,1... | collective-permute-start | bytes 1572872 | tf_op jit(solution)/shard_map/ppermute | solution.py:1096
  339.8 32.9 %collective-permute-start.46 = (bf16[2,64,256]{2,1,0:T(8,128)(2,1)S(1)}, bf16[2,64,256]{2,1,0:T(8,128)(2,1)S(1)}, u32[]{:S(2)}, u32[]{:S(2)}) collective-permute-start(bf16[2,64,256]{2,1,0:T(8,128)(2,1)S(1)} %maximum_select_fusion.12), channel_id=1, source_target_pairs={{0,2},{2,0},{1,3},{3,1},{4,6},{6,4},{5,7},{7,5},{8,10},{10,8},{9,1... | collective-permute-start | bytes 196616 | tf_op jit(solution)/shard_map/ppermute | solution.py:1096
  340.7 24.5 %collective-permute-start.43 = (bf16[256,1024]{1,0:T(8,128)(2,1)S(1)}, bf16[256,1024]{1,0:T(8,128)(2,1)S(1)}, u32[]{:S(2)}, u32[]{:S(2)}) collective-permute-start(bf16[256,1024]{1,0:T(8,128)(2,1)S(1)} %add_convert_fusion.8), channel_id=1, source_target_pairs={{0,8},{4,12},{8,0},{12,4},{16,24},{20,28},{24,16},{28,20},{1,9},{5... | collective-permute-start | bytes 1572872 | tf_op jit(solution)/shard_map/ppermute | solution.py:1099
  354.8 13.5 %collective-permute-start.42 = (bf16[256,1024]{1,0:T(8,128)(2,1)S(1)}, bf16[256,1024]{1,0:T(8,128)(2,1)S(1)}, u32[]{:S(2)}, u32[]{:S(2)}) collective-permute-start(bf16[256,1024]{1,0:T(8,128)(2,1)S(1)} %dynamic-slice_convert_fusion), channel_id=1, source_target_pairs={{0,8},{4,12},{8,0},{12,4},{16,24},{20,28},{24,16},{28,20},{1,9},{5... | collective-permute-start | bytes 1572872 | tf_op jit(solution)/shard_map/ppermute | solution.py:1099
  362.0 34.5 %collective-permute-start.47 = (bf16[832,1024]{1,0:T(8,128)(2,1)}, bf16[832,1024]{1,0:T(8,128)(2,1)}, u32[]{:S(2)}, u32[]{:S(2)}) collective-permute-start(bf16[832,1024]{1,0:T(8,128)(2,1)} %first_back.2), channel_id=1, source_target_pairs={{0,1},{1,0},{2,3},{3,2},{4,5},{5,4},{6,7},{7,6},{8,9},{9,8},{10,11... | collective-permute-start | bytes 5111816 | tf_op jit(solution)/shard_map/ppermute | solution.py:1093
  365.2 29.6 %collective-permute-start.48 = (bf16[512,1024]{1,0:T(8,128)(2,1)S(1)}, bf16[512,1024]{1,0:T(8,128)(2,1)}, u32[]{:S(2)}, u32[]{:S(2)}) collective-permute-start(bf16[512,1024]{1,0:T(8,128)(2,1)S(1)} %outputs_grad.2), channel_id=1, source_target_pairs={{0,2},{2,0},{1,3},{3,1},{4,6},{6,4},{5,7},{7,5},{8,10},{10,8},{9,1... | collective-permute-start | bytes 3145736 | tf_op jit(solution)/shard_map/ppermute | solution.py:1096
  368.4 26.4 %collective-permute-start.57 = (bf16[256,1024]{1,0:T(8,128)(2,1)S(1)}, bf16[256,1024]{1,0:T(8,128)(2,1)}, u32[]{:S(2)}, u32[]{:S(2)}) collective-permute-start(bf16[256,1024]{1,0:T(8,128)(2,1)S(1)} %add_convert_fusion.7), channel_id=1, source_target_pairs={{0,16},{4,20},{8,24},{12,28},{16,0},{20,4},{24,8},{28,12},{1,17},{... | collective-permute-start | bytes 1572872 | tf_op jit(solution)/shard_map/ppermute | solution.py:1099
  372.7 31.2 %collective-permute-start.59 = (bf16[512,1024]{1,0:T(8,128)(2,1)}, bf16[512,1024]{1,0:T(8,128)(2,1)}, u32[]{:S(2)}, u32[]{:S(2)}) collective-permute-start(bf16[512,1024]{1,0:T(8,128)(2,1)} %maximum_select_fusion.4), channel_id=1, source_target_pairs={{0,4},{4,0},{8,12},{12,8},{16,20},{20,16},{24,28},{28,24},{1,5},{5... | collective-permute-start | bytes 3145736 | tf_op jit(solution)/shard_map/ppermute | solution.py:1099
  375.5 29.9 %collective-permute-start.51 = (bf16[1536,256]{1,0:T(8,128)(2,1)S(1)}, bf16[1536,256]{1,0:T(8,128)(2,1)S(1)}, u32[]{:S(2)}, u32[]{:S(2)}) collective-permute-start(bf16[1536,256]{1,0:T(8,128)(2,1)S(1)} %get-tuple-element.532), channel_id=1, source_target_pairs={{0,8},{4,12},{8,0},{12,4},{16,24},{20,28},{24,16},{28,20},{1,9},{5... | collective-permute-start | bytes 2359304 | tf_op jit(solution)/shard_map/ppermute | solution.py:1099
  394.8 67.6 %collective-permute-start.29 = (bf16[832,1024]{1,0:T(8,128)(2,1)}, bf16[832,1024]{1,0:T(8,128)(2,1)S(1)}, u32[]{:S(2)}, u32[]{:S(2)}) collective-permute-start(bf16[832,1024]{1,0:T(8,128)(2,1)} %get-tuple-element.335), channel_id=1, source_target_pairs={{0,1},{1,0},{2,3},{3,2},{4,5},{5,4},{6,7},{7,6},{8,9},{9,8},{10,11... | collective-permute-start | bytes 5111816 | tf_op jit(solution)/shard_map/ppermute | solution.py:1093
  394.9 20.4 %collective-permute-start.52 = (bf16[1536,256]{1,0:T(8,128)(2,1)S(1)}, bf16[1536,256]{1,0:T(8,128)(2,1)S(1)}, u32[]{:S(2)}, u32[]{:S(2)}) collective-permute-start(bf16[1536,256]{1,0:T(8,128)(2,1)S(1)} %copy-done.109), channel_id=1, source_target_pairs={{0,4},{4,0},{8,12},{12,8},{16,20},{20,16},{24,28},{28,24},{1,5},{5... | collective-permute-start | bytes 2359304 | tf_op jit(solution)/shard_map/ppermute | solution.py:1099
  403.9 31.2 %collective-permute-start.56 = (f32[64,1024]{1,0:T(8,128)S(1)}, f32[64,1024]{1,0:T(8,128)S(1)}, u32[]{:S(2)}, u32[]{:S(2)}) collective-permute-start(f32[64,1024]{1,0:T(8,128)S(1)} %get-tuple-element.535), channel_id=1, source_target_pairs={{0,2},{2,0},{1,3},{3,1},{4,6},{6,4},{5,7},{7,5},{8,10},{10,8},{9,1... | collective-permute-start | bytes 786440 | tf_op jit(solution)/shard_map/ppermute | solution.py:1096
  405.7 29.2 %collective-permute-start.58 = (bf16[768,256]{1,0:T(8,128)(2,1)S(1)}, bf16[768,256]{1,0:T(8,128)(2,1)S(1)}, u32[]{:S(2)}, u32[]{:S(2)}) collective-permute-start(bf16[768,256]{1,0:T(8,128)(2,1)S(1)} %dynamic-slice_convert_fusion.2), channel_id=1, source_target_pairs={{0,4},{4,0},{8,12},{12,8},{16,20},{20,16},{24,28},{28,24},{1,5},{5... | collective-permute-start | bytes 1179656 | tf_op jit(solution)/shard_map/ppermute | solution.py:1099
  422.3 14.9 %collective-permute-start.55 = (bf16[256,1024]{1,0:T(8,128)(2,1)S(1)}, bf16[256,1024]{1,0:T(8,128)(2,1)S(1)}, u32[]{:S(2)}, u32[]{:S(2)}) collective-permute-start(bf16[256,1024]{1,0:T(8,128)(2,1)S(1)} %get-tuple-element.530), channel_id=1, source_target_pairs={{0,4},{4,0},{8,12},{12,8},{16,20},{20,16},{24,28},{28,24},{1,5},{5... | collective-permute-start | bytes 1572872 | tf_op jit(solution)/shard_map/ppermute | solution.py:1099
  433.0 32.4 %collective-permute-start.62 = (bf16[256,1024]{1,0:T(8,128)(2,1)S(1)}, bf16[256,1024]{1,0:T(8,128)(2,1)S(1)}, u32[]{:S(2)}, u32[]{:S(2)}) collective-permute-start(bf16[256,1024]{1,0:T(8,128)(2,1)S(1)} %add_convert_fusion.4), channel_id=1, source_target_pairs={{0,8},{4,12},{8,0},{12,4},{16,24},{20,28},{24,16},{28,20},{1,9},{5... | collective-permute-start | bytes 1572872 | tf_op jit(solution)/shard_map/ppermute | solution.py:1099
  434.9 27.2 %collective-permute-start.54 = (bf16[768,256]{1,0:T(8,128)(2,1)S(1)}, bf16[768,256]{1,0:T(8,128)(2,1)S(1)}, u32[]{:S(2)}, u32[]{:S(2)}) collective-permute-start(bf16[768,256]{1,0:T(8,128)(2,1)S(1)} %dynamic-slice_convert_fusion.3), channel_id=1, source_target_pairs={{0,8},{4,12},{8,0},{12,4},{16,24},{20,28},{24,16},{28,20},{1,9},{5... | collective-permute-start | bytes 1179656 | tf_op jit(solution)/shard_map/ppermute | solution.py:1099
  435.2 27.2 %collective-permute-start.53 = (f32[8,1024]{1,0:T(8,128)S(1)}, f32[8,1024]{1,0:T(8,128)S(1)}, u32[]{:S(2)}, u32[]{:S(2)}) collective-permute-start(f32[8,1024]{1,0:T(8,128)S(1)} %add.251), channel_id=1, source_target_pairs={{0,8},{4,12},{8,0},{12,4},{16,24},{20,28},{24,16},{28,20},{1,9},{5... | collective-permute-start | bytes 98312 | tf_op jit(solution)/shard_map/ppermute | solution.py:1099
  437.2 28.8 %collective-permute-start.61 = (bf16[768,256]{1,0:T(8,128)(2,1)S(1)}, bf16[768,256]{1,0:T(8,128)(2,1)S(1)}, u32[]{:S(2)}, u32[]{:S(2)}) collective-permute-start(bf16[768,256]{1,0:T(8,128)(2,1)S(1)} %add_convert_fusion.13), channel_id=1, source_target_pairs={{0,16},{4,20},{8,24},{12,28},{16,0},{20,4},{24,8},{28,12},{1,17},{... | collective-permute-start | bytes 1179656 | tf_op jit(solution)/shard_map/ppermute | solution.py:1099
  462.4 27.5 %collective-permute-start.64 = (bf16[768,256]{1,0:T(8,128)(2,1)S(1)}, bf16[768,256]{1,0:T(8,128)(2,1)S(1)}, u32[]{:S(2)}, u32[]{:S(2)}) collective-permute-start(bf16[768,256]{1,0:T(8,128)(2,1)S(1)} %add_convert_fusion.12), channel_id=1, source_target_pairs={{0,16},{4,20},{8,24},{12,28},{16,0},{20,4},{24,8},{28,12},{1,17},{... | collective-permute-start | bytes 1179656 | tf_op jit(solution)/shard_map/ppermute | solution.py:1099
  462.4 26.9 %collective-permute-start.65 = (f32[8,1024]{1,0:T(8,128)S(1)}, f32[8,1024]{1,0:T(8,128)S(1)}, u32[]{:S(2)}, u32[]{:S(2)}) collective-permute-start(f32[8,1024]{1,0:T(8,128)S(1)} %add.262), channel_id=1, source_target_pairs={{0,16},{4,20},{8,24},{12,28},{16,0},{20,4},{24,8},{28,12},{1,17},{... | collective-permute-start | bytes 98312 | tf_op jit(solution)/shard_map/ppermute | solution.py:1099
  465.4 12.5 %collective-permute-start.66 = (bf16[128,1024]{1,0:T(8,128)(2,1)S(1)}, bf16[128,1024]{1,0:T(8,128)(2,1)S(1)}, u32[]{:S(2)}, u32[]{:S(2)}) collective-permute-start(bf16[128,1024]{1,0:T(8,128)(2,1)S(1)} %dynamic-slice_convert_fusion.5), channel_id=1, source_target_pairs={{0,8},{4,12},{8,0},{12,4},{16,24},{20,28},{24,16},{28,20},{1,9},{5... | collective-permute-start | bytes 786440 | tf_op jit(solution)/shard_map/ppermute | solution.py:1099
  466.0 36.2 %collective-permute-start.71 = (bf16[512,1024]{1,0:T(8,128)(2,1)S(1)}, bf16[512,1024]{1,0:T(8,128)(2,1)S(1)}, u32[]{:S(2)}, u32[]{:S(2)}) collective-permute-start(bf16[512,1024]{1,0:T(8,128)(2,1)S(1)} %maximum_select_fusion.5), channel_id=1, source_target_pairs={{0,4},{4,0},{8,12},{12,8},{16,20},{20,16},{24,28},{28,24},{1,5},{5... | collective-permute-start | bytes 3145736 | tf_op jit(solution)/shard_map/ppermute | solution.py:1099
  466.7 33.0 %collective-permute-start.69 = (bf16[768,256]{1,0:T(8,128)(2,1)S(1)}, bf16[768,256]{1,0:T(8,128)(2,1)S(1)}, u32[]{:S(2)}, u32[]{:S(2)}) collective-permute-start(bf16[768,256]{1,0:T(8,128)(2,1)S(1)} %add_convert_fusion.11), channel_id=1, source_target_pairs={{0,4},{4,0},{8,12},{12,8},{16,20},{20,16},{24,28},{28,24},{1,5},{5... | collective-permute-start | bytes 1179656 | tf_op jit(solution)/shard_map/ppermute | solution.py:1099
  478.0 23.8 %collective-permute-start.68 = (bf16[128,1024]{1,0:T(8,128)(2,1)S(1)}, bf16[128,1024]{1,0:T(8,128)(2,1)S(1)}, u32[]{:S(2)}, u32[]{:S(2)}) collective-permute-start(bf16[128,1024]{1,0:T(8,128)(2,1)S(1)} %add_convert_fusion.15), channel_id=1, source_target_pairs={{0,16},{4,20},{8,24},{12,28},{16,0},{20,4},{24,8},{28,12},{1,17},{... | collective-permute-start | bytes 786440 | tf_op jit(solution)/shard_map/ppermute | solution.py:1099
  489.4 25.7 %collective-permute-start.67 = (f32[8,1024]{1,0:T(8,128)S(1)}, f32[8,1024]{1,0:T(8,128)S(1)}, u32[]{:S(2)}, u32[]{:S(2)}) collective-permute-start(f32[8,1024]{1,0:T(8,128)S(1)} %add.269), channel_id=1, source_target_pairs={{0,4},{4,0},{8,12},{12,8},{16,20},{20,16},{24,28},{28,24},{1,5},{5... | collective-permute-start | bytes 98312 | tf_op jit(solution)/shard_map/ppermute | solution.py:1099
  489.9 26.3 %collective-permute-start.63 = (bf16[64,1024]{1,0:T(8,128)(2,1)S(1)}, bf16[64,1024]{1,0:T(8,128)(2,1)S(1)}, u32[]{:S(2)}, u32[]{:S(2)}) collective-permute-start(bf16[64,1024]{1,0:T(8,128)(2,1)S(1)} %add_convert_fusion.16), channel_id=1, source_target_pairs={{0,2},{2,0},{1,3},{3,1},{4,6},{6,4},{5,7},{7,5},{8,10},{10,8},{9,1... | collective-permute-start | bytes 393224 | tf_op jit(solution)/shard_map/ppermute | solution.py:1096
  499.7 12.1 %collective-permute-start.72 = (bf16[768,256]{1,0:T(8,128)(2,1)S(1)}, bf16[768,256]{1,0:T(8,128)(2,1)S(1)}, u32[]{:S(2)}, u32[]{:S(2)}) collective-permute-start(bf16[768,256]{1,0:T(8,128)(2,1)S(1)} %add_convert_fusion.10), channel_id=1, source_target_pairs={{0,8},{4,12},{8,0},{12,4},{16,24},{20,28},{24,16},{28,20},{1,9},{5... | collective-permute-start | bytes 1179656 | tf_op jit(solution)/shard_map/ppermute | solution.py:1099
  501.8 31.8 %collective-permute-start.74 = (bf16[1536,256]{1,0:T(8,128)(2,1)S(1)}, bf16[1536,256]{1,0:T(8,128)(2,1)S(1)}, u32[]{:S(2)}, u32[]{:S(2)}) collective-permute-start(bf16[1536,256]{1,0:T(8,128)(2,1)S(1)} %maximum_select_fusion.7), channel_id=1, source_target_pairs={{0,8},{4,12},{8,0},{12,4},{16,24},{20,28},{24,16},{28,20},{1,9},{5... | collective-permute-start | bytes 2359304 | tf_op jit(solution)/shard_map/ppermute | solution.py:1099
  502.2 29.6 %collective-permute-start.70 = (bf16[128,1024]{1,0:T(8,128)(2,1)S(1)}, bf16[128,1024]{1,0:T(8,128)(2,1)}, u32[]{:S(2)}, u32[]{:S(2)}) collective-permute-start(bf16[128,1024]{1,0:T(8,128)(2,1)S(1)} %add_convert_fusion.14), channel_id=1, source_target_pairs={{0,8},{4,12},{8,0},{12,4},{16,24},{20,28},{24,16},{28,20},{1,9},{5... | collective-permute-start | bytes 786440 | tf_op jit(solution)/shard_map/ppermute | solution.py:1099
  512.1 21.9 %collective-permute-start.75 = (bf16[1536,256]{1,0:T(8,128)(2,1)S(1)}, bf16[1536,256]{1,0:T(8,128)(2,1)}, u32[]{:S(2)}, u32[]{:S(2)}) collective-permute-start(bf16[1536,256]{1,0:T(8,128)(2,1)S(1)} %maximum_select_fusion.8), channel_id=1, source_target_pairs={{0,4},{4,0},{8,12},{12,8},{16,20},{20,16},{24,28},{28,24},{1,5},{5... | collective-permute-start | bytes 2359304 | tf_op jit(solution)/shard_map/ppermute | solution.py:1099
  533.0 11.5 %collective-permute-start.73 = (bf16[256,1024]{1,0:T(8,128)(2,1)S(1)}, bf16[256,1024]{1,0:T(8,128)(2,1)S(1)}, u32[]{:S(2)}, u32[]{:S(2)}) collective-permute-start(bf16[256,1024]{1,0:T(8,128)(2,1)S(1)} %maximum_select_fusion.9), channel_id=1, source_target_pairs={{0,4},{4,0},{8,12},{12,8},{16,20},{20,16},{24,28},{28,24},{1,5},{5... | collective-permute-start | bytes 1572872 | tf_op jit(solution)/shard_map/ppermute | solution.py:1099
  (141 other events, 1087.2 us)

commit v15 on v14

--- a/solution.py
+++ b/solution.py
@@ -1429,9 +1429,9 @@
     cross_in.far()
     store["out_fly"] = over_core(out_o)
     text_rows.then(over_core)
+    norms.then(lambda v: along_wide(v, Z_FAR))
     outs.second()
     qkv.far()
-    norms.then(lambda v: along_wide(v, Z_FAR))
     order("x2", "out_fly")
     out_rows = lower(store["x2"] + out_m + store["out_fly"].astype(FULL))
     down.along()

time: 551 us -> 543 us (0.985)
  starting transfers between devices: 62.3 us -> 56 us
    ppermute x34, starting transfers between devices: 42.9 us -> 36.9 us  [along_wide(): return lax.ppermute(v, 'wide', pairs)]
    convert_element_type x17 -> x15, other arithmetic: 14.7 us -> 9.93 us  [lower(): return values_in.astype(jnp.bfloat16)]
where the time goes in v15:
time: 543 us; the launch traced here: 539 us
  Pallas kernels  269 us (50%)
  waiting for transfers between devices  121 us (22%)
  starting transfers between devices  56 us (10%)
  local copies, waits for them, and re-layouts  49 us (9%)
  other arithmetic  40.6 us (7%)
    ppermute x34, waiting for transfers between devices, along_wide(): return lax.ppermute(v, 'wide', pairs)  101 us
    pallas_call x4, Pallas kernels, feed(): pl.pallas_call(functools.partial(feed_kernel, parts=parts, carried=len(be...  51.6 us
    pallas_call x3, Pallas kernels, self_back(): pl.pallas_call(functools.partial(self_back_kernel, span=span, floor=floor...  39.7 us
    ppermute x34, starting transfers between devices, along_wide(): return lax.ppermute(v, 'wide', pairs)  36.9 us
    pallas_call x3, Pallas kernels, self_forward(): pl.pallas_call(functools.partial(self_forward_kernel, span=span, floor=fl...  30.8 us
    unnamed x259, local copies, waits for them, and re-layouts  25.8 us
    pallas_call x1, Pallas kernels, middle_back(): pl.pallas_call(middle_back_kernel, grid_spec=pltpu.PrefetchScalarGridSpec...  23 us
    pallas_call x1, Pallas kernels, middle_forward(): pl.pallas_call(middle_forward_kernel, grid_spec=pltpu.PrefetchScalarGridS...  20.7 us
  transfers between devices with their start and end apart: 76, of which 20 were waited for; matrix products, arithmetic and copies ran while one was open for 11% of the time, Pallas kernels for 47%

profile of v15, /device:TPU:0, one launch (start us, length us, event | category | flops | bytes accessed | tf_op | source)
XLA Modules:
  0.0 538.8 jit_solution(3414945026938944426)
XLA Ops:
  1.2 2.2 constant_dynamic-slice_fusion.15
  3.4 2.6 collective-permute-start.1
  10.9 6.2 %first_project.1 = (bf16[1664,1024]{1,0:T(8,128)(2,1)S(1)}, bf16[1664,256]{1,0:T(8,128)(2,1)S(1)}, bf16[1664,256]{1,0:T(8,128)(2,1)S(1)}, bf16[1664,256]{1,0:T(8,128)(2,1)S(1)}) custom-call(s32[3]{0:T(128)S(1)} %add_add_fusion.place_ref, bf16[832,1024]{1,0:T(8,128)(2,1)S(1)} %copy-done.53, bf16[832,1024]{1,0:T(8,128)(2,1)} %collective-permute-done.other_ref, ...), custom_call_target="tpu_custom_call" | custom-call | flops 1610000000 | bytes 1000 | tf_op jit(solution)/shard_map/first_project/pallas_call | solution.py:393
  19.9 4.4 collective-permute-done.1.weight_ref.refs_10_
  24.3 1.8 constant_dynamic-slice_fusion.12
  27.8 1.8 collective-permute-start.2
  29.9 14.1 %self_forward.3 = (bf16[1664,256]{1,0:T(8,128)(2,1)}, f32[2,8,1664]{2,1,0:T(8,128)}) custom-call(s32[1]{0:T(128)} %dynamic_slice.129.limit_ref, bf16[1664,256]{1,0:T(8,128)(2,1)} %copy-done.61, bf16[1664,256]{1,0:T(8,128)(2,1)} %copy-done.63, bf16[1664,256]{1,0:T(8,128)(2,1)} %copy-done.65), custom_call_target="tpu_custom_call" | custom-call | flops 4701199872 | bytes 1000 | tf_op jit(solution)/shard_map/self_forward/pallas_call | solution.py:525
  43.9 12.7 %project.2 = (bf16[1664,128]{1,0:T(8,128)(2,1)S(1)}, bf16[1664,128]{1,0:T(8,128)(2,1)S(1)}, bf16[1664,128]{1,0:T(8,128)(2,1)S(1)}) custom-call(s32[3]{0:T(128)S(1)} %add_add_fusion.place_ref, bf16[1664,1024]{1,0:T(8,128)(2,1)S(1)} %get-tuple-element.267.h_ref, bf16[3,1024,128]{2,1,0:T(8,128)(2,1)S(1)} %collective-permute-done.1.weight_ref.refs_10_), custom_call_target="tpu_custom_call" | custom-call | flops 1288000000 | bytes 1000 | tf_op jit(solution)/shard_map/project/pallas_call | solution.py:423
  58.2 1.8 collective-permute-start.8
  67.0 8.3 %self_forward.4 = (bf16[1664,128]{1,0:T(8,128)(2,1)}, f32[1,8,1664]{2,1,0:T(8,128)}) custom-call(s32[1]{0:T(128)} %dynamic_slice.129.limit_ref, bf16[1664,128]{1,0:T(8,128)(2,1)} %copy-done.68, bf16[1664,128]{1,0:T(8,128)(2,1)} %copy-done.70, bf16[1664,128]{1,0:T(8,128)(2,1)} %copy-done.72), custom_call_target="tpu_custom_call" | custom-call | flops 2350599936 | bytes 1000 | tf_op jit(solution)/shard_map/self_forward/pallas_call | solution.py:525
  75.4 5.2 collective-permute-done.7.weight_ref.refs_11_
  84.3 2.7 project.3
  89.9 8.4 %self_forward.5 = (bf16[1664,128]{1,0:T(8,128)(2,1)}, f32[1,8,1664]{2,1,0:T(8,128)}) custom-call(s32[1]{0:T(128)} %dynamic_slice.129.limit_ref, bf16[1664,128]{1,0:T(8,128)(2,1)} %copy-done.74, bf16[1664,128]{1,0:T(8,128)(2,1)} %copy-done.76, bf16[1664,128]{1,0:T(8,128)(2,1)} %copy-done.78), custom_call_target="tpu_custom_call" | custom-call | flops 2350599936 | bytes 1000 | tf_op jit(solution)/shard_map/self_forward/pallas_call | solution.py:525
  105.6 20.7 %middle_forward.1 = (f32[832,1024]{1,0:T(8,128)}, f32[832,1024]{1,0:T(8,128)}, bf16[832,1024]{1,0:T(8,128)(2,1)}, bf16[832,1024]{1,0:T(8,128)(2,1)}, bf16[832,10...) custom-call(s32[3]{0:T(128)} %copy-done.85, bf16[832,1024]{1,0:T(8,128)(2,1)} %frame_ref.3, ...), custom_call_target="tpu_custom_call" | custom-call | flops 7084000256 | bytes 1000 | tf_op jit(solution)/shard_map/middle_forward/pallas_call | solution.py:677
  128.4 12.1 %feed.4 = (bf16[1664,1024]{1,0:T(8,128)(2,1)}, bf16[1664,1024]{1,0:T(8,128)(2,1)}, f32[832,1024]{1,0:T(8,128)}, f32[832,1024]{1,0:T(8,128)}) custom-call(s32[3]{0:T(128)} %copy-done.85, bf16[832,1024]{1,0:T(8,128)(2,1)} %get-tuple-element.310.h_ref.mine_ref, bf16[832,1024]{1,0:T(8,128)(2,1)} %copy-done, bf16[1024,1024]{1,0:T(8,128)(2,1)} %refs_0_.1, ...), custom_call_target="tpu_custom_call" | custom-call | flops 4185999872 | bytes 1000 | tf_op jit(solution)/shard_map/feed/pallas_call | solution.py:756
  142.2 12.1 %feed.5 = (bf16[1664,1024]{1,0:T(8,128)(2,1)}, bf16[1664,1024]{1,0:T(8,128)(2,1)}, f32[832,1024]{1,0:T(8,128)}, f32[832,1024]{1,0:T(8,128)}) custom-call(s32[3]{0:T(128)} %copy-done.85, bf16[832,1024]{1,0:T(8,128)(2,1)} %copy-done.16, bf16[832,1024]{1,0:T(8,128)(2,1)} %copy-done.13, ...), custom_call_target="tpu_custom_call", output_to_operand_aliasing={{0}: (5, {}), {1}: (6, {})} | custom-call | flops 4185999872 | bytes 1000 | tf_op jit(solution)/shard_map/feed/pallas_call | solution.py:756
  155.3 13.6 %feed.6 = (bf16[1664,1024]{1,0:T(8,128)(2,1)}, bf16[1664,1024]{1,0:T(8,128)(2,1)}, bf16[832,1024]{1,0:T(8,128)(2,1)}, bf16[832,1024]{1,0:T(8,128)(2,1)}) custom-call(s32[3]{0:T(128)} %copy-done.85, bf16[832,1024]{1,0:T(8,128)(2,1)} %copy-done.16, bf16[832,1024]{1,0:T(8,128)(2,1)} %copy-done.13, bf16[1024,512]{1,0:T(8,128)(2,1)} %copy-done.106, ...), custom_call_target="tpu_custom_call" | custom-call | flops 4185999872 | bytes 1000 | tf_op jit(solution)/shard_map/feed/pallas_call | solution.py:756
  168.9 13.7 %feed.7 = (bf16[1664,1024]{1,0:T(8,128)(2,1)}, bf16[1664,1024]{1,0:T(8,128)(2,1)}, f32[832,1024]{1,0:T(8,128)}, f32[832,1024]{1,0:T(8,128)}) custom-call(s32[3]{0:T(128)} %copy-done.85, bf16[832,1024]{1,0:T(8,128)(2,1)} %get-tuple-element.310.h_ref.mine_ref, bf16[832,1024]{1,0:T(8,128)(2,1)} %copy-done, ...), custom_call_target="tpu_custom_call", output_to_operand_aliasing={{0}: (9, {}), {1}: (10, {})} | custom-call | flops 4185999872 | bytes 1000 | tf_op jit(solution)/shard_map/feed/pallas_call | solution.py:756
  182.7 7.4 %up_grad.2 = bf16[1024,1024]{1,0:T(8,128)(2,1)} custom-call(bf16[832,1024]{1,0:T(8,128)(2,1)S(1)} %copy-done.3, bf16[832,1024]{1,0:T(8,128)(2,1)S(1)} %copy-done.17, bf16[1664,1024]{1,0:T(8,128)(2,1)} %get-tuple-element.332.du_ref), custom_call_target="tpu_custom_call" | custom-call | flops 241500000 | bytes 1000 | tf_op jit(solution)/shard_map/up_grad/pallas_call | solution.py:786
  190.6 7.2 %down_grad.2 = bf16[1024,1024]{1,0:T(8,128)(2,1)} custom-call(bf16[1664,1024]{1,0:T(8,128)(2,1)} %get-tuple-element.333.g_ref, bf16[832,1024]{1,0:T(8,128)(2,1)S(1)} %copy-done.1, bf16[832,1024]{1,0:T(8,128)(2,1)S(1)} %copy-done.14), custom_call_target="tpu_custom_call" | custom-call | flops 1127000064 | bytes 1000 | tf_op jit(solution)/shard_map/down_grad/pallas_call | solution.py:809
  199.1 23.0 %middle_back.1 = (f32[832,1024]{1,0:T(8,128)}, bf16[832,1024]{1,0:T(8,128)(2,1)}, bf16[832,1024]{1,0:T(8,128)(2,1)}, bf16[832,1024]{1,0:T(8,128)(2,1)}, f32[4,64...) custom-call(s32[3]{0:T(128)} %copy-done.85, f32[832,1024]{1,0:T(8,128)} %get-tuple-element.337.ym_ref, ...), custom_call_target="tpu_custom_call" | custom-call | flops 827862016 | bytes 1000 | tf_op jit(solution)/shard_map/middle_back/pallas_call | solution.py:992
  224.1 6.4 %up_grad.3 = bf16[1024,1024]{1,0:T(8,128)(2,1)S(1)} custom-call(bf16[832,1024]{1,0:T(8,128)(2,1)S(1)} %copy-done.3, bf16[832,1024]{1,0:T(8,128)(2,1)S(1)} %copy-done.18, bf16[1664,1024]{1,0:T(8,128)(2,1)} %get-tuple-element.343.du_ref), custom_call_target="tpu_custom_call" | custom-call | flops 241500000 | bytes 1000 | tf_op jit(solution)/shard_map/up_grad/pallas_call | solution.py:786
  230.5 7.9 %collective-permute-done.30 = bf16[1024,1024]{1,0:T(8,128)(2,1)} collective-permute-done((bf16[1024,1024]{1,0:T(8,128)(2,1)}, bf16[1024,1024]{1,0:T(8,128)(2,1)}, u32[]{:S(2)}, u32[]{:S(2)}) %collective-permute-start.30) | collective-permute-done | bytes 2097184 | tf_op jit(solution)/shard_map/ppermute | solution.py:1096
  239.6 4.1 add_convert_fusion.2
  249.8 4.0 pull.1
  255.2 9.4 %self_back.3 = (bf16[1664,128]{1,0:T(8,128)(2,1)S(1)}, bf16[1664,128]{1,0:T(8,128)(2,1)S(1)}, bf16[1664,128]{1,0:T(8,128)(2,1)S(1)}) custom-call(s32[1]{0:T(128)} %dynamic_slice.129.limit_ref, bf16[1664,128]{1,0:T(8,128)(2,1)S(1)} %copy-done.69, bf16[1664,128]{1,0:T(8,128)(2,1)S(1)} %copy-done.71, bf16[1664,128]{1,0:T(8,128)(2,1)S(1)} %copy-done.73, ...), custom_call_target="tpu_custom_call" | custom-call | flops 338100000 | bytes 1000 | tf_op jit(solution)/shard_map/self_back/pallas_call | solution.py:606
  264.7 5.6 %query_grad.2 = bf16[1024,256]{1,0:T(8,128)(2,1)} custom-call(s32[3]{0:T(128)S(1)} %copy-done.86, bf16[832,1024]{1,0:T(8,128)(2,1)} %get-tuple-element.356.mine_ref, bf16[832,1024]{1,0:T(8,128)(2,1)} %collective-permute-done.34.other_ref, bf16[832,1024]{1,0:T(8,128)(2,1)} %get-tuple-element.421.dm_ref, bf16[832,512]{1,0:T(8,128)(2,1)S(1)} %collective-permute-done.33.do_ref), custom_call_target="tpu_custom_call" | custom-call | flops 138138000 | bytes 1000 | tf_op jit(solution)/shard_map/query_grad/pallas_call | solution.py:875
  273.0 1.7 collective-permute-start.37
  274.9 9.8 %self_back.4 = (bf16[1664,128]{1,0:T(8,128)(2,1)S(1)}, bf16[1664,128]{1,0:T(8,128)(2,1)S(1)}, bf16[1664,128]{1,0:T(8,128)(2,1)S(1)}) custom-call(s32[1]{0:T(128)} %dynamic_slice.129.limit_ref, bf16[1664,128]{1,0:T(8,128)(2,1)S(1)} %copy-done.75, bf16[1664,128]{1,0:T(8,128)(2,1)S(1)} %copy-done.77, bf16[1664,128]{1,0:T(8,128)(2,1)S(1)} %copy-done.79, ...), custom_call_target="tpu_custom_call" | custom-call | flops 338100000 | bytes 1000 | tf_op jit(solution)/shard_map/self_back/pallas_call | solution.py:606
  284.8 2.2 collective-permute-done.37
  287.1 6.2 %down_grad.3 = bf16[1024,1024]{1,0:T(8,128)(2,1)S(1)} custom-call(bf16[1664,1024]{1,0:T(8,128)(2,1)} %get-tuple-element.381.g_ref, bf16[832,1024]{1,0:T(8,128)(2,1)S(1)} %copy-done.2, bf16[832,1024]{1,0:T(8,128)(2,1)S(1)} %copy-done.15), custom_call_target="tpu_custom_call" | custom-call | flops 1127000064 | bytes 1000 | tf_op jit(solution)/shard_map/down_grad/pallas_call | solution.py:809
  293.4 7.3 %qkv_grad.2 = bf16[3072,256]{1,0:T(8,128)(2,1)} custom-call(s32[3]{0:T(128)S(1)} %copy-done.86, bf16[1664,1024]{1,0:T(8,128)(2,1)} %copy-done.8, bf16[1664,128]{1,0:T(8,128)(2,1)S(1)} %get-tuple-element.364.refs_0_.refs_3_, bf16[1664,128]{1,0:T(8,128)(2,1)S(1)} %get-tuple-element.365.refs_1_.refs_4_, ...), custom_call_target="tpu_custom_call" | custom-call | flops 1127000064 | bytes 1000 | tf_op jit(solution)/shard_map/qkv_grad/pallas_call | solution.py:846
  300.7 2.0 collective-permute-done.32
  302.7 2.6 convert_add_fusion.1
  307.7 2.7 collective-permute-start.42
  315.0 20.5 %self_back.5 = (bf16[1664,256]{1,0:T(8,128)(2,1)S(1)}, bf16[1664,256]{1,0:T(8,128)(2,1)S(1)}, bf16[1664,256]{1,0:T(8,128)(2,1)S(1)}) custom-call(s32[1]{0:T(128)} %dynamic_slice.129.limit_ref, bf16[1664,256]{1,0:T(8,128)(2,1)S(1)} %copy-done.62, bf16[1664,256]{1,0:T(8,128)(2,1)S(1)} %copy-done.64, bf16[1664,256]{1,0:T(8,128)(2,1)S(1)} %copy-done.66, ...), custom_call_target="tpu_custom_call" | custom-call | flops 676200000 | bytes 1000 | tf_op jit(solution)/shard_map/self_back/pallas_call | solution.py:606
  337.0 1.7 convert_add_fusion
  342.4 5.2 outputs_grad.2
  347.6 5.8 %first_back.2 = bf16[832,1024]{1,0:T(8,128)(2,1)} custom-call(s32[3]{0:T(128)S(1)} %add_add_fusion.1.place_ref, bf16[1664,256]{1,0:T(8,128)(2,1)S(1)} %get-tuple-element.430.refs_0_, bf16[1664,256]{1,0:T(8,128)(2,1)S(1)} %get-tuple-element.409.refs_1_, bf16[1664,256]{1,0:T(8,128)(2,1)S(1)} %get-tuple-element.410.refs_2_, bf16[1664,128]{1,0:T(8,128)(2,1)S(1)} %copy-done.23, ...), custom_call_target="tpu_custom_call" | custom-call | flops 172270000 | bytes 1000 | tf_op jit(solution)/shard_map/first_back/pallas_call | solution.py:1026
  356.0 6.0 %qkv_grad.3 = bf16[3072,256]{1,0:T(8,128)(2,1)S(1)} custom-call(s32[3]{0:T(128)S(1)} %copy-done.86, bf16[1664,1024]{1,0:T(8,128)(2,1)} %copy-done.8, bf16[1664,256]{1,0:T(8,128)(2,1)S(1)} %get-tuple-element.430.refs_0_, bf16[1664,256]{1,0:T(8,128)(2,1)S(1)} %get-tuple-element.409.refs_1_, bf16[1664,256]{1,0:T(8,128)(2,1)S(1)} %get-tuple-element.410.refs_2_), custom_call_target="tpu_custom_call" | custom-call | flops 1127000064 | bytes 1000 | tf_op jit(solution)/shard_map/qkv_grad/pallas_call | solution.py:846
  362.0 3.2 convert_add_fusion.6
  368.8 3.9 query_grad.3
  377.8 4.9 first_back.3.ym_ref
  383.1 11.6 %collective-permute-done.57 = bf16[256,1024]{1,0:T(8,128)(2,1)} collective-permute-done((bf16[256,1024]{1,0:T(8,128)(2,1)S(1)}, bf16[256,1024]{1,0:T(8,128)(2,1)}, u32[]{:S(2)}, u32[]{:S(2)}) %collective-permute-start.57) | collective-permute-done | bytes 524320 | tf_op jit(solution)/shard_map/ppermute | solution.py:1099
  396.3 6.0 %frames_back.1 = (bf16[832,1024]{1,0:T(8,128)(2,1)}, f32[8,1024]{1,0:T(8,128)S(1)}) custom-call(s32[3]{0:T(128)S(1)} %copy-done.86, f32[832,1024]{1,0:T(8,128)S(1)} %first_back.3.ym_ref, bf16[832,1024]{1,0:T(8,128)(2,1)} %collective-permute-done.49.yr_ref, f32[832,1024]{1,0:T(8,128)S(1)} %copy-done.42, bf16[832,1024]{1,0:T(8,128)(2,1)S(1)} %copy-done.54, ...), custom_call_target="tpu_custom_call" | custom-call | flops 207046000 | bytes 1000 | tf_op jit(solution)/shard_map/frames_back/pallas_call | solution.py:1061
  406.2 8.9 %collective-permute-done.43 = bf16[1536,256]{1,0:T(8,128)(2,1)S(1)} collective-permute-done((bf16[1536,256]{1,0:T(8,128)(2,1)S(1)}, bf16[1536,256]{1,0:T(8,128)(2,1)S(1)}, u32[]{:S(2)}, u32[]{:S(2)}) %collective-permute-start.43) | collective-permute-done | bytes 786464 | tf_op jit(solution)/shard_map/ppermute | solution.py:1099
  415.5 5.2 outputs_grad.3
  423.8 5.2 fusion
  429.5 3.4 collective-permute-done.54
  432.9 2.0 collective-permute-start.62
  435.1 2.1 collective-permute-start.52
  437.2 15.5 %collective-permute-done.55 = f32[8,1024]{1,0:T(8,128)S(1)} collective-permute-done((f32[8,1024]{1,0:T(8,128)S(1)}, f32[8,1024]{1,0:T(8,128)S(1)}, u32[]{:S(2)}, u32[]{:S(2)}) %collective-permute-start.55) | collective-permute-done | bytes 32800 | tf_op jit(solution)/shard_map/ppermute | solution.py:1099
  454.0 5.1 collective-permute-done.52
  460.1 2.0 collective-permute-start.64
  462.8 19.2 %collective-permute-done.61 = bf16[768,256]{1,0:T(8,128)(2,1)S(1)} collective-permute-done((bf16[768,256]{1,0:T(8,128)(2,1)S(1)}, bf16[768,256]{1,0:T(8,128)(2,1)S(1)}, u32[]{:S(2)}, u32[]{:S(2)}) %collective-permute-start.61) | collective-permute-done | bytes 393248 | tf_op jit(solution)/shard_map/ppermute | solution.py:1099
  485.0 7.6 %collective-permute-done.64 = bf16[768,256]{1,0:T(8,128)(2,1)S(1)} collective-permute-done((bf16[768,256]{1,0:T(8,128)(2,1)S(1)}, bf16[768,256]{1,0:T(8,128)(2,1)S(1)}, u32[]{:S(2)}, u32[]{:S(2)}) %collective-permute-start.64) | collective-permute-done | bytes 393248 | tf_op jit(solution)/shard_map/ppermute | solution.py:1099
  492.8 8.4 %collective-permute-done.69 = bf16[768,256]{1,0:T(8,128)(2,1)S(1)} collective-permute-done((bf16[768,256]{1,0:T(8,128)(2,1)S(1)}, bf16[768,256]{1,0:T(8,128)(2,1)S(1)}, u32[]{:S(2)}, u32[]{:S(2)}) %collective-permute-start.69) | collective-permute-done | bytes 393248 | tf_op jit(solution)/shard_map/ppermute | solution.py:1099
  501.6 2.1 collective-permute-start.74
  503.8 3.0 fusion.1
  506.8 6.2 %collective-permute-done.72 = bf16[768,256]{1,0:T(8,128)(2,1)S(1)} collective-permute-done((bf16[768,256]{1,0:T(8,128)(2,1)S(1)}, bf16[768,256]{1,0:T(8,128)(2,1)S(1)}, u32[]{:S(2)}, u32[]{:S(2)}) %collective-permute-start.72) | collective-permute-done | bytes 393248 | tf_op jit(solution)/shard_map/ppermute | solution.py:1099
  514.0 2.3 add_convert_fusion
  518.3 6.1 %collective-permute-done.70 = bf16[128,1024]{1,0:T(8,128)(2,1)} collective-permute-done((bf16[128,1024]{1,0:T(8,128)(2,1)S(1)}, bf16[128,1024]{1,0:T(8,128)(2,1)}, u32[]{:S(2)}, u32[]{:S(2)}) %collective-permute-start.70) | collective-permute-done | bytes 262176 | tf_op jit(solution)/shard_map/ppermute | solution.py:1099
  526.5 4.4 collective-permute-done.75
  533.4 3.4 fusion.3
  (472 shorter events, 101.7 us)
Async XLA Ops:
  3.4 20.9 %collective-permute-start.1 = (bf16[3,1024,128]{2,1,0:T(8,128)(2,1)}, bf16[3,1024,128]{2,1,0:T(8,128)(2,1)S(1)}, u32[]{:S(2)}, u32[]{:S(2)}) collective-permute-start(bf16[3,1024,128]{2,1,0:T(8,128)(2,1)} %constant_dynamic-slice_fusion.15), channel_id=1, source_target_pairs={{0,2},{2,0},{1,3},{3,1},{4,6},{6,4},{5,7},{7,5},{8,10},{10,8},{9,1... | collective-permute-start | bytes 2359304 | tf_op jit(solution)/shard_map/ppermute | solution.py:1096
  24.3 37.4 %collective-permute-start.5 = (bf16[1024,256]{1,0:T(8,128)(2,1)}, bf16[1024,256]{1,0:T(8,128)(2,1)S(1)}, u32[]{:S(2)}, u32[]{:S(2)}) collective-permute-start(bf16[1024,256]{1,0:T(8,128)(2,1)} %refs_0_.2), channel_id=1, source_target_pairs={{0,1},{1,0},{2,3},{3,2},{4,5},{5,4},{6,7},{7,6},{8,9},{9,8},{10,11... | collective-permute-start | bytes 1572872 | tf_op jit(solution)/shard_map/ppermute | solution.py:1093
  26.1 35.5 %collective-permute-start.4 = (bf16[256,1024]{1,0:T(8,128)(2,1)S(1)}, bf16[256,1024]{1,0:T(8,128)(2,1)}, u32[]{:S(2)}, u32[]{:S(2)}) collective-permute-start(bf16[256,1024]{1,0:T(8,128)(2,1)S(1)} %copy-done.55), channel_id=1, source_target_pairs={{0,1},{1,0},{2,3},{3,2},{4,5},{5,4},{6,7},{7,6},{8,9},{9,8},{10,11... | collective-permute-start | bytes 1572872 | tf_op jit(solution)/shard_map/ppermute | solution.py:1093
  27.5 34.2 %collective-permute-start.6 = (bf16[256,1024]{1,0:T(8,128)(2,1)}, bf16[256,1024]{1,0:T(8,128)(2,1)S(1)}, u32[]{:S(2)}, u32[]{:S(2)}) collective-permute-start(bf16[256,1024]{1,0:T(8,128)(2,1)} %refs_6_.1), channel_id=1, source_target_pairs={{0,1},{1,0},{2,3},{3,2},{4,5},{5,4},{6,7},{7,6},{8,9},{9,8},{10,11... | collective-permute-start | bytes 1572872 | tf_op jit(solution)/shard_map/ppermute | solution.py:1093
  27.8 32.3 %collective-permute-start.2 = (bf16[256,1024]{1,0:T(8,128)(2,1)S(1)}, bf16[256,1024]{1,0:T(8,128)(2,1)}, u32[]{:S(2)}, u32[]{:S(2)}) collective-permute-start(bf16[256,1024]{1,0:T(8,128)(2,1)S(1)} %pad_maximum_fusion.1), channel_id=1, source_target_pairs={{0,2},{2,0},{1,3},{3,1},{4,6},{6,4},{5,7},{7,5},{8,10},{10,8},{9,1... | collective-permute-start | bytes 1572872 | tf_op jit(solution)/shard_map/ppermute | solution.py:1096
  29.6 28.6 %collective-permute-start.3 = (bf16[1024,128]{1,0:T(8,128)(2,1)}, bf16[1024,128]{1,0:T(8,128)(2,1)S(1)}, u32[]{:S(2)}, u32[]{:S(2)}) collective-permute-start(bf16[1024,128]{1,0:T(8,128)(2,1)} %constant_dynamic-slice_fusion.12), channel_id=1, source_target_pairs={{0,2},{2,0},{1,3},{3,1},{4,6},{6,4},{5,7},{7,5},{8,10},{10,8},{9,1... | collective-permute-start | bytes 786440 | tf_op jit(solution)/shard_map/ppermute | solution.py:1096
  58.2 17.1 %collective-permute-start.8 = (bf16[2,64,256]{2,1,0:T(8,128)(2,1)S(1)}, bf16[2,64,256]{2,1,0:T(8,128)(2,1)S(1)}, u32[]{:S(2)}, u32[]{:S(2)}) collective-permute-start(bf16[2,64,256]{2,1,0:T(8,128)(2,1)S(1)} %get-tuple-element.547), channel_id=1, source_target_pairs={{0,2},{2,0},{1,3},{3,1},{4,6},{6,4},{5,7},{7,5},{8,10},{10,8},{9,1... | collective-permute-start | bytes 196616 | tf_op jit(solution)/shard_map/ppermute | solution.py:1096
  60.0 20.5 %collective-permute-start.7 = (bf16[3,1024,128]{2,1,0:T(8,128)(2,1)S(1)}, bf16[3,1024,128]{2,1,0:T(8,128)(2,1)S(1)}, u32[]{:S(2)}, u32[]{:S(2)}) collective-permute-start(bf16[3,1024,128]{2,1,0:T(8,128)(2,1)S(1)} %collective-permute-done.1.weight_ref.refs_10_), channel_id=1, source_target_pairs={{0,8},{4,12},{8,0},{12,4},{16,24},{20,28},{24,16},{28,20},{1,9},{5... | collective-permute-start | bytes 2359304 | tf_op jit(solution)/shard_map/ppermute | solution.py:1099
  62.6 19.5 %collective-permute-start.9 = (bf16[832,256]{1,0:T(8,128)(2,1)}, bf16[832,256]{1,0:T(8,128)(2,1)}, u32[]{:S(2)}, u32[]{:S(2)}) collective-permute-start(bf16[832,256]{1,0:T(8,128)(2,1)} %constant_dynamic-slice_fusion.11), channel_id=1, source_target_pairs={{0,1},{1,0},{2,3},{3,2},{4,5},{5,4},{6,7},{7,6},{8,9},{9,8},{10,11... | collective-permute-start | bytes 1277960 | tf_op jit(solution)/shard_map/ppermute | solution.py:1093
  63.8 35.2 %collective-permute-start.13 = (bf16[1024,512]{1,0:T(8,128)(2,1)}, bf16[1024,512]{1,0:T(8,128)(2,1)S(1)}, u32[]{:S(2)}, u32[]{:S(2)}) collective-permute-start(bf16[1024,512]{1,0:T(8,128)(2,1)} %constant_dynamic-slice_fusion.10), channel_id=1, source_target_pairs={{0,2},{2,0},{1,3},{3,1},{4,6},{6,4},{5,7},{7,5},{8,10},{10,8},{9,1... | collective-permute-start | bytes 3145736 | tf_op jit(solution)/shard_map/ppermute | solution.py:1096
  65.4 23.9 %collective-permute-start.10 = (bf16[128,1024]{1,0:T(8,128)(2,1)S(1)}, bf16[128,1024]{1,0:T(8,128)(2,1)S(1)}, u32[]{:S(2)}, u32[]{:S(2)}) collective-permute-start(bf16[128,1024]{1,0:T(8,128)(2,1)S(1)} %get-tuple-element.539.refs_7_.refs_0_), channel_id=1, source_target_pairs={{0,8},{4,12},{8,0},{12,4},{16,24},{20,28},{24,16},{28,20},{1,9},{5... | collective-permute-start | bytes 786440 | tf_op jit(solution)/shard_map/ppermute | solution.py:1099
  75.3 26.5 %collective-permute-start.17 = (bf16[128,1024]{1,0:T(8,128)(2,1)S(1)}, bf16[128,1024]{1,0:T(8,128)(2,1)}, u32[]{:S(2)}, u32[]{:S(2)}) collective-permute-start(bf16[128,1024]{1,0:T(8,128)(2,1)S(1)} %get-tuple-element.539.refs_7_.refs_0_), channel_id=1, source_target_pairs={{0,1},{1,0},{2,3},{3,2},{4,5},{5,4},{6,7},{7,6},{8,9},{9,8},{10,11... | collective-permute-start | bytes 786440 | tf_op jit(solution)/shard_map/ppermute | solution.py:1093
  82.1 16.2 %collective-permute-start.11 = (bf16[1024,128]{1,0:T(8,128)(2,1)S(1)}, bf16[1024,128]{1,0:T(8,128)(2,1)S(1)}, u32[]{:S(2)}, u32[]{:S(2)}) collective-permute-start(bf16[1024,128]{1,0:T(8,128)(2,1)S(1)} %copy-done.115), channel_id=1, source_target_pairs={{0,4},{4,0},{8,12},{12,8},{16,20},{20,16},{24,28},{28,24},{1,5},{5... | collective-permute-start | bytes 786440 | tf_op jit(solution)/shard_map/ppermute | solution.py:1099
  100.3 26.0 %collective-permute-start.23 = (bf16[1024,512]{1,0:T(8,128)(2,1)S(1)}, bf16[1024,512]{1,0:T(8,128)(2,1)}, u32[]{:S(2)}, u32[]{:S(2)}) collective-permute-start(bf16[1024,512]{1,0:T(8,128)(2,1)S(1)} %collective-permute-done.13.refs_0_), channel_id=1, source_target_pairs={{0,4},{4,0},{8,12},{12,8},{16,20},{20,16},{24,28},{28,24},{1,5},{5... | collective-permute-start | bytes 3145736 | tf_op jit(solution)/shard_map/ppermute | solution.py:1099
  101.8 25.5 %collective-permute-start.24 = (bf16[512,1024]{1,0:T(8,128)(2,1)}, bf16[512,1024]{1,0:T(8,128)(2,1)}, u32[]{:S(2)}, u32[]{:S(2)}) collective-permute-start(bf16[512,1024]{1,0:T(8,128)(2,1)} %constant_dynamic-slice_fusion.9), channel_id=1, source_target_pairs={{0,2},{2,0},{1,3},{3,1},{4,6},{6,4},{5,7},{7,5},{8,10},{10,8},{9,1... | collective-permute-start | bytes 3145736 | tf_op jit(solution)/shard_map/ppermute | solution.py:1096
  127.4 13.2 %collective-permute-start.25 = (bf16[832,1024]{1,0:T(8,128)(2,1)}, bf16[832,1024]{1,0:T(8,128)(2,1)S(1)}, u32[]{:S(2)}, u32[]{:S(2)}) collective-permute-start(bf16[832,1024]{1,0:T(8,128)(2,1)} %get-tuple-element.310.h_ref.mine_ref), channel_id=1, source_target_pairs={{0,1},{1,0},{2,3},{3,2},{4,5},{5,4},{6,7},{7,6},{8,9},{9,8},{10,11... | collective-permute-start | bytes 5111816 | tf_op jit(solution)/shard_map/ppermute | solution.py:1093
  127.4 13.2 %collective-permute-start.26 = (bf16[832,1024]{1,0:T(8,128)(2,1)S(1)}, bf16[832,1024]{1,0:T(8,128)(2,1)S(1)}, u32[]{:S(2)}, u32[]{:S(2)}) collective-permute-start(bf16[832,1024]{1,0:T(8,128)(2,1)S(1)} %broadcast_select_fusion.d_ref.mine_ref), channel_id=1, source_target_pairs={{0,1},{1,0},{2,3},{3,2},{4,5},{5,4},{6,7},{7,6},{8,9},{9,8},{10,11... | collective-permute-start | bytes 5111816 | tf_op jit(solution)/shard_map/ppermute | solution.py:1093
  127.9 26.5 %collective-permute-start.27 = (bf16[512,1024]{1,0:T(8,128)(2,1)}, bf16[512,1024]{1,0:T(8,128)(2,1)S(1)}, u32[]{:S(2)}, u32[]{:S(2)}) collective-permute-start(bf16[512,1024]{1,0:T(8,128)(2,1)} %collective-permute-done.24.refs_2_), channel_id=1, source_target_pairs={{0,4},{4,0},{8,12},{12,8},{16,20},{20,16},{24,28},{28,24},{1,5},{5... | collective-permute-start | bytes 3145736 | tf_op jit(solution)/shard_map/ppermute | solution.py:1099
  168.9 28.9 %collective-permute-start.28 = (bf16[832,1024]{1,0:T(8,128)(2,1)}, bf16[832,1024]{1,0:T(8,128)(2,1)S(1)}, u32[]{:S(2)}, u32[]{:S(2)}) collective-permute-start(bf16[832,1024]{1,0:T(8,128)(2,1)} %get-tuple-element.322), channel_id=1, source_target_pairs={{0,1},{1,0},{2,3},{3,2},{4,5},{5,4},{6,7},{7,6},{8,9},{9,8},{10,11... | collective-permute-start | bytes 5111816 | tf_op jit(solution)/shard_map/ppermute | solution.py:1093
  190.0 48.3 %collective-permute-start.30 = (bf16[1024,1024]{1,0:T(8,128)(2,1)}, bf16[1024,1024]{1,0:T(8,128)(2,1)}, u32[]{:S(2)}, u32[]{:S(2)}) collective-permute-start(bf16[1024,1024]{1,0:T(8,128)(2,1)} %up_grad.2), channel_id=1, source_target_pairs={{0,2},{2,0},{1,3},{3,1},{4,6},{6,4},{5,7},{7,5},{8,10},{10,8},{9,1... | collective-permute-start | bytes 6291464 | tf_op jit(solution)/shard_map/ppermute | solution.py:1096
  222.1 16.3 %collective-permute-start.31 = (bf16[832,1024]{1,0:T(8,128)(2,1)}, bf16[832,1024]{1,0:T(8,128)(2,1)S(1)}, u32[]{:S(2)}, u32[]{:S(2)}) collective-permute-start(bf16[832,1024]{1,0:T(8,128)(2,1)} %get-tuple-element.359.mine_ref.refs_2_.refs_1_), channel_id=1, source_target_pairs={{0,1},{1,0},{2,3},{3,2},{4,5},{5,4},{6,7},{7,6},{8,9},{9,8},{10,11... | collective-permute-start | bytes 5111816 | tf_op jit(solution)/shard_map/ppermute | solution.py:1093
  222.3 42.3 %collective-permute-start.34 = (bf16[832,1024]{1,0:T(8,128)(2,1)}, bf16[832,1024]{1,0:T(8,128)(2,1)}, u32[]{:S(2)}, u32[]{:S(2)}) collective-permute-start(bf16[832,1024]{1,0:T(8,128)(2,1)} %get-tuple-element.356.mine_ref), channel_id=1, source_target_pairs={{0,1},{1,0},{2,3},{3,2},{4,5},{5,4},{6,7},{7,6},{8,9},{9,8},{10,11... | collective-permute-start | bytes 5111816 | tf_op jit(solution)/shard_map/ppermute | solution.py:1093
  244.7 20.0 %collective-permute-start.33 = (bf16[832,512]{1,0:T(8,128)(2,1)}, bf16[832,512]{1,0:T(8,128)(2,1)S(1)}, u32[]{:S(2)}, u32[]{:S(2)}) collective-permute-start(bf16[832,512]{1,0:T(8,128)(2,1)} %slice.86), channel_id=1, source_target_pairs={{0,1},{1,0},{2,3},{3,2},{4,5},{5,4},{6,7},{7,6},{8,9},{9,8},{10,11... | collective-permute-start | bytes 2555912 | tf_op jit(solution)/shard_map/ppermute | solution.py:1093
  244.7 26.6 %collective-permute-start.36 = (bf16[512,1024]{1,0:T(8,128)(2,1)}, bf16[512,1024]{1,0:T(8,128)(2,1)}, u32[]{:S(2)}, u32[]{:S(2)}) collective-permute-start(bf16[512,1024]{1,0:T(8,128)(2,1)} %get-tuple-element.524), channel_id=1, source_target_pairs={{0,4},{4,0},{8,12},{12,8},{16,20},{20,16},{24,28},{28,24},{1,5},{5... | collective-permute-start | bytes 3145736 | tf_op jit(solution)/shard_map/ppermute | solution.py:1099
  247.1 17.6 %collective-permute-start.35 = (f32[2,2,64,256]{3,2,0,1:T(8,128)}, f32[2,2,64,256]{3,2,0,1:T(8,128)}, u32[]{:S(2)}, u32[]{:S(2)}) collective-permute-start(f32[2,2,64,256]{3,2,0,1:T(8,128)} %get-tuple-element.537), channel_id=1, source_target_pairs={{0,1},{1,0},{2,3},{3,2},{4,5},{5,4},{6,7},{7,6},{8,9},{9,8},{10,11... | collective-permute-start | bytes 786440 | tf_op jit(solution)/shard_map/ppermute | solution.py:1093
  254.7 48.0 %collective-permute-start.32 = (bf16[1024,1024]{1,0:T(8,128)(2,1)}, bf16[1024,1024]{1,0:T(8,128)(2,1)S(1)}, u32[]{:S(2)}, u32[]{:S(2)}) collective-permute-start(bf16[1024,1024]{1,0:T(8,128)(2,1)} %down_grad.2), channel_id=1, source_target_pairs={{0,2},{2,0},{1,3},{3,1},{4,6},{6,4},{5,7},{7,5},{8,10},{10,8},{9,1... | collective-permute-start | bytes 6291464 | tf_op jit(solution)/shard_map/ppermute | solution.py:1096
  273.0 13.9 %collective-permute-start.37 = (bf16[256,1024]{1,0:T(8,128)(2,1)S(1)}, bf16[256,1024]{1,0:T(8,128)(2,1)S(1)}, u32[]{:S(2)}, u32[]{:S(2)}) collective-permute-start(bf16[256,1024]{1,0:T(8,128)(2,1)S(1)} %dynamic-slice_convert_fusion.1), channel_id=1, source_target_pairs={{0,8},{4,12},{8,0},{12,4},{16,24},{20,28},{24,16},{28,20},{1,9},{5... | collective-permute-start | bytes 1572872 | tf_op jit(solution)/shard_map/ppermute | solution.py:1099
  305.3 30.2 %collective-permute-start.39 = (bf16[512,1024]{1,0:T(8,128)(2,1)}, bf16[512,1024]{1,0:T(8,128)(2,1)}, u32[]{:S(2)}, u32[]{:S(2)}) collective-permute-start(bf16[512,1024]{1,0:T(8,128)(2,1)} %get-tuple-element.523), channel_id=1, source_target_pairs={{0,4},{4,0},{8,12},{12,8},{16,20},{20,16},{24,28},{28,24},{1,5},{5... | collective-permute-start | bytes 3145736 | tf_op jit(solution)/shard_map/ppermute | solution.py:1099
  305.8 36.6 %collective-permute-start.40 = (bf16[832,1024]{1,0:T(8,128)(2,1)}, bf16[832,1024]{1,0:T(8,128)(2,1)}, u32[]{:S(2)}, u32[]{:S(2)}) collective-permute-start(bf16[832,1024]{1,0:T(8,128)(2,1)} %get-tuple-element.444.refs_6_.refs_5_), channel_id=1, source_target_pairs={{0,1},{1,0},{2,3},{3,2},{4,5},{5,4},{6,7},{7,6},{8,9},{9,8},{10,11... | collective-permute-start | bytes 5111816 | tf_op jit(solution)/shard_map/ppermute | solution.py:1093
  305.8 56.2 %collective-permute-start.38 = (bf16[3072,256]{1,0:T(8,128)(2,1)}, bf16[3072,256]{1,0:T(8,128)(2,1)}, u32[]{:S(2)}, u32[]{:S(2)}) collective-permute-start(bf16[3072,256]{1,0:T(8,128)(2,1)} %qkv_grad.2), channel_id=1, source_target_pairs={{0,2},{2,0},{1,3},{3,1},{4,6},{6,4},{5,7},{7,5},{8,10},{10,8},{9,1... | collective-permute-start | bytes 4718600 | tf_op jit(solution)/shard_map/ppermute | solution.py:1096
  307.3 33.4 %collective-permute-start.41 = (bf16[832,512]{1,0:T(8,128)(2,1)}, bf16[832,512]{1,0:T(8,128)(2,1)}, u32[]{:S(2)}, u32[]{:S(2)}) collective-permute-start(bf16[832,512]{1,0:T(8,128)(2,1)} %slice.92), channel_id=1, source_target_pairs={{0,1},{1,0},{2,3},{3,2},{4,5},{5,4},{6,7},{7,6},{8,9},{9,8},{10,11... | collective-permute-start | bytes 2555912 | tf_op jit(solution)/shard_map/ppermute | solution.py:1093
  307.7 32.2 %collective-permute-start.42 = (bf16[256,1024]{1,0:T(8,128)(2,1)S(1)}, bf16[256,1024]{1,0:T(8,128)(2,1)S(1)}, u32[]{:S(2)}, u32[]{:S(2)}) collective-permute-start(bf16[256,1024]{1,0:T(8,128)(2,1)S(1)} %add_convert_fusion.9), channel_id=1, source_target_pairs={{0,16},{4,20},{8,24},{12,28},{16,0},{20,4},{24,8},{28,12},{1,17},{... | collective-permute-start | bytes 1572872 | tf_op jit(solution)/shard_map/ppermute | solution.py:1099
  335.5 38.7 %collective-permute-start.46 = (bf16[1024,256]{1,0:T(8,128)(2,1)}, bf16[1024,256]{1,0:T(8,128)(2,1)S(1)}, u32[]{:S(2)}, u32[]{:S(2)}) collective-permute-start(bf16[1024,256]{1,0:T(8,128)(2,1)} %query_grad.2), channel_id=1, source_target_pairs={{0,2},{2,0},{1,3},{3,1},{4,6},{6,4},{5,7},{7,5},{8,10},{10,8},{9,1... | collective-permute-start | bytes 1572872 | tf_op jit(solution)/shard_map/ppermute | solution.py:1096
  339.8 32.8 %collective-permute-start.47 = (bf16[2,64,256]{2,1,0:T(8,128)(2,1)S(1)}, bf16[2,64,256]{2,1,0:T(8,128)(2,1)S(1)}, u32[]{:S(2)}, u32[]{:S(2)}) collective-permute-start(bf16[2,64,256]{2,1,0:T(8,128)(2,1)S(1)} %maximum_select_fusion.12), channel_id=1, source_target_pairs={{0,2},{2,0},{1,3},{3,1},{4,6},{6,4},{5,7},{7,5},{8,10},{10,8},{9,1... | collective-permute-start | bytes 196616 | tf_op jit(solution)/shard_map/ppermute | solution.py:1096
  340.7 24.5 %collective-permute-start.44 = (bf16[256,1024]{1,0:T(8,128)(2,1)S(1)}, bf16[256,1024]{1,0:T(8,128)(2,1)S(1)}, u32[]{:S(2)}, u32[]{:S(2)}) collective-permute-start(bf16[256,1024]{1,0:T(8,128)(2,1)S(1)} %add_convert_fusion.8), channel_id=1, source_target_pairs={{0,8},{4,12},{8,0},{12,4},{16,24},{20,28},{24,16},{28,20},{1,9},{5... | collective-permute-start | bytes 1572872 | tf_op jit(solution)/shard_map/ppermute | solution.py:1099
  354.8 13.4 %collective-permute-start.45 = (bf16[256,1024]{1,0:T(8,128)(2,1)S(1)}, bf16[256,1024]{1,0:T(8,128)(2,1)S(1)}, u32[]{:S(2)}, u32[]{:S(2)}) collective-permute-start(bf16[256,1024]{1,0:T(8,128)(2,1)S(1)} %dynamic-slice_convert_fusion), channel_id=1, source_target_pairs={{0,8},{4,12},{8,0},{12,4},{16,24},{20,28},{24,16},{28,20},{1,9},{5... | collective-permute-start | bytes 1572872 | tf_op jit(solution)/shard_map/ppermute | solution.py:1099
  362.0 34.4 %collective-permute-start.49 = (bf16[832,1024]{1,0:T(8,128)(2,1)}, bf16[832,1024]{1,0:T(8,128)(2,1)}, u32[]{:S(2)}, u32[]{:S(2)}) collective-permute-start(bf16[832,1024]{1,0:T(8,128)(2,1)} %first_back.2), channel_id=1, source_target_pairs={{0,1},{1,0},{2,3},{3,2},{4,5},{5,4},{6,7},{7,6},{8,9},{9,8},{10,11... | collective-permute-start | bytes 5111816 | tf_op jit(solution)/shard_map/ppermute | solution.py:1093
  365.2 29.6 %collective-permute-start.50 = (bf16[512,1024]{1,0:T(8,128)(2,1)S(1)}, bf16[512,1024]{1,0:T(8,128)(2,1)}, u32[]{:S(2)}, u32[]{:S(2)}) collective-permute-start(bf16[512,1024]{1,0:T(8,128)(2,1)S(1)} %outputs_grad.2), channel_id=1, source_target_pairs={{0,2},{2,0},{1,3},{3,1},{4,6},{6,4},{5,7},{7,5},{8,10},{10,8},{9,1... | collective-permute-start | bytes 3145736 | tf_op jit(solution)/shard_map/ppermute | solution.py:1096
  368.3 26.4 %collective-permute-start.57 = (bf16[256,1024]{1,0:T(8,128)(2,1)S(1)}, bf16[256,1024]{1,0:T(8,128)(2,1)}, u32[]{:S(2)}, u32[]{:S(2)}) collective-permute-start(bf16[256,1024]{1,0:T(8,128)(2,1)S(1)} %add_convert_fusion.7), channel_id=1, source_target_pairs={{0,16},{4,20},{8,24},{12,28},{16,0},{20,4},{24,8},{28,12},{1,17},{... | collective-permute-start | bytes 1572872 | tf_op jit(solution)/shard_map/ppermute | solution.py:1099
  372.6 31.2 %collective-permute-start.59 = (bf16[512,1024]{1,0:T(8,128)(2,1)}, bf16[512,1024]{1,0:T(8,128)(2,1)}, u32[]{:S(2)}, u32[]{:S(2)}) collective-permute-start(bf16[512,1024]{1,0:T(8,128)(2,1)} %maximum_select_fusion.4), channel_id=1, source_target_pairs={{0,4},{4,0},{8,12},{12,8},{16,20},{20,16},{24,28},{28,24},{1,5},{5... | collective-permute-start | bytes 3145736 | tf_op jit(solution)/shard_map/ppermute | solution.py:1099
  375.4 29.9 %collective-permute-start.48 = (bf16[1536,256]{1,0:T(8,128)(2,1)S(1)}, bf16[1536,256]{1,0:T(8,128)(2,1)S(1)}, u32[]{:S(2)}, u32[]{:S(2)}) collective-permute-start(bf16[1536,256]{1,0:T(8,128)(2,1)S(1)} %get-tuple-element.533), channel_id=1, source_target_pairs={{0,8},{4,12},{8,0},{12,4},{16,24},{20,28},{24,16},{28,20},{1,9},{5... | collective-permute-start | bytes 2359304 | tf_op jit(solution)/shard_map/ppermute | solution.py:1099
  394.7 65.4 %collective-permute-start.29 = (bf16[832,1024]{1,0:T(8,128)(2,1)}, bf16[832,1024]{1,0:T(8,128)(2,1)S(1)}, u32[]{:S(2)}, u32[]{:S(2)}) collective-permute-start(bf16[832,1024]{1,0:T(8,128)(2,1)} %get-tuple-element.335), channel_id=1, source_target_pairs={{0,1},{1,0},{2,3},{3,2},{4,5},{5,4},{6,7},{7,6},{8,9},{9,8},{10,11... | collective-permute-start | bytes 5111816 | tf_op jit(solution)/shard_map/ppermute | solution.py:1093
  394.8 20.4 %collective-permute-start.43 = (bf16[1536,256]{1,0:T(8,128)(2,1)S(1)}, bf16[1536,256]{1,0:T(8,128)(2,1)S(1)}, u32[]{:S(2)}, u32[]{:S(2)}) collective-permute-start(bf16[1536,256]{1,0:T(8,128)(2,1)S(1)} %copy-done.109), channel_id=1, source_target_pairs={{0,4},{4,0},{8,12},{12,8},{16,20},{20,16},{24,28},{28,24},{1,5},{5... | collective-permute-start | bytes 2359304 | tf_op jit(solution)/shard_map/ppermute | solution.py:1099
  403.8 31.2 %collective-permute-start.56 = (f32[64,1024]{1,0:T(8,128)S(1)}, f32[64,1024]{1,0:T(8,128)S(1)}, u32[]{:S(2)}, u32[]{:S(2)}) collective-permute-start(f32[64,1024]{1,0:T(8,128)S(1)} %get-tuple-element.535), channel_id=1, source_target_pairs={{0,2},{2,0},{1,3},{3,1},{4,6},{6,4},{5,7},{7,5},{8,10},{10,8},{9,1... | collective-permute-start | bytes 786440 | tf_op jit(solution)/shard_map/ppermute | solution.py:1096
  405.6 29.3 %collective-permute-start.58 = (bf16[768,256]{1,0:T(8,128)(2,1)S(1)}, bf16[768,256]{1,0:T(8,128)(2,1)S(1)}, u32[]{:S(2)}, u32[]{:S(2)}) collective-permute-start(bf16[768,256]{1,0:T(8,128)(2,1)S(1)} %dynamic-slice_convert_fusion.2), channel_id=1, source_target_pairs={{0,4},{4,0},{8,12},{12,8},{16,20},{20,16},{24,28},{28,24},{1,5},{5... | collective-permute-start | bytes 1179656 | tf_op jit(solution)/shard_map/ppermute | solution.py:1099
  422.2 31.5 %collective-permute-start.53 = (bf16[256,1024]{1,0:T(8,128)(2,1)S(1)}, bf16[256,1024]{1,0:T(8,128)(2,1)S(1)}, u32[]{:S(2)}, u32[]{:S(2)}) collective-permute-start(bf16[256,1024]{1,0:T(8,128)(2,1)S(1)} %get-tuple-element.531), channel_id=1, source_target_pairs={{0,4},{4,0},{8,12},{12,8},{16,20},{20,16},{24,28},{28,24},{1,5},{5... | collective-permute-start | bytes 1572872 | tf_op jit(solution)/shard_map/ppermute | solution.py:1099
  432.9 29.3 %collective-permute-start.62 = (bf16[256,1024]{1,0:T(8,128)(2,1)S(1)}, bf16[256,1024]{1,0:T(8,128)(2,1)S(1)}, u32[]{:S(2)}, u32[]{:S(2)}) collective-permute-start(bf16[256,1024]{1,0:T(8,128)(2,1)S(1)} %add_convert_fusion.4), channel_id=1, source_target_pairs={{0,8},{4,12},{8,0},{12,4},{16,24},{20,28},{24,16},{28,20},{1,9},{5... | collective-permute-start | bytes 1572872 | tf_op jit(solution)/shard_map/ppermute | solution.py:1099
  434.9 17.8 %collective-permute-start.55 = (f32[8,1024]{1,0:T(8,128)S(1)}, f32[8,1024]{1,0:T(8,128)S(1)}, u32[]{:S(2)}, u32[]{:S(2)}) collective-permute-start(f32[8,1024]{1,0:T(8,128)S(1)} %add.254), channel_id=1, source_target_pairs={{0,8},{4,12},{8,0},{12,4},{16,24},{20,28},{24,16},{28,20},{1,9},{5... | collective-permute-start | bytes 98312 | tf_op jit(solution)/shard_map/ppermute | solution.py:1099
  435.1 24.0 %collective-permute-start.52 = (bf16[768,256]{1,0:T(8,128)(2,1)S(1)}, bf16[768,256]{1,0:T(8,128)(2,1)S(1)}, u32[]{:S(2)}, u32[]{:S(2)}) collective-permute-start(bf16[768,256]{1,0:T(8,128)(2,1)S(1)} %dynamic-slice_convert_fusion.3), channel_id=1, source_target_pairs={{0,8},{4,12},{8,0},{12,4},{16,24},{20,28},{24,16},{28,20},{1,9},{5... | collective-permute-start | bytes 1179656 | tf_op jit(solution)/shard_map/ppermute | solution.py:1099
  452.6 29.3 %collective-permute-start.61 = (bf16[768,256]{1,0:T(8,128)(2,1)S(1)}, bf16[768,256]{1,0:T(8,128)(2,1)S(1)}, u32[]{:S(2)}, u32[]{:S(2)}) collective-permute-start(bf16[768,256]{1,0:T(8,128)(2,1)S(1)} %add_convert_fusion.13), channel_id=1, source_target_pairs={{0,16},{4,20},{8,24},{12,28},{16,0},{20,4},{24,8},{28,12},{1,17},{... | collective-permute-start | bytes 1179656 | tf_op jit(solution)/shard_map/ppermute | solution.py:1099
  453.7 28.9 %collective-permute-start.60 = (f32[64,1024]{1,0:T(8,128)S(1)}, f32[64,1024]{1,0:T(8,128)S(1)}, u32[]{:S(2)}, u32[]{:S(2)}) collective-permute-start(f32[64,1024]{1,0:T(8,128)S(1)} %add.259), channel_id=1, source_target_pairs={{0,1},{1,0},{2,3},{3,2},{4,5},{5,4},{6,7},{7,6},{8,9},{9,8},{10,11... | collective-permute-start | bytes 786440 | tf_op jit(solution)/shard_map/ppermute | solution.py:1093
  459.1 25.3 %collective-permute-start.65 = (f32[8,1024]{1,0:T(8,128)S(1)}, f32[8,1024]{1,0:T(8,128)S(1)}, u32[]{:S(2)}, u32[]{:S(2)}) collective-permute-start(f32[8,1024]{1,0:T(8,128)S(1)} %add.260), channel_id=1, source_target_pairs={{0,16},{4,20},{8,24},{12,28},{16,0},{20,4},{24,8},{28,12},{1,17},{... | collective-permute-start | bytes 98312 | tf_op jit(solution)/shard_map/ppermute | solution.py:1099
  460.1 32.5 %collective-permute-start.64 = (bf16[768,256]{1,0:T(8,128)(2,1)S(1)}, bf16[768,256]{1,0:T(8,128)(2,1)S(1)}, u32[]{:S(2)}, u32[]{:S(2)}) collective-permute-start(bf16[768,256]{1,0:T(8,128)(2,1)S(1)} %add_convert_fusion.12), channel_id=1, source_target_pairs={{0,16},{4,20},{8,24},{12,28},{16,0},{20,4},{24,8},{28,12},{1,17},{... | collective-permute-start | bytes 1179656 | tf_op jit(solution)/shard_map/ppermute | solution.py:1099
  462.2 22.0 %collective-permute-start.66 = (bf16[128,1024]{1,0:T(8,128)(2,1)S(1)}, bf16[128,1024]{1,0:T(8,128)(2,1)S(1)}, u32[]{:S(2)}, u32[]{:S(2)}) collective-permute-start(bf16[128,1024]{1,0:T(8,128)(2,1)S(1)} %dynamic-slice_convert_fusion.5), channel_id=1, source_target_pairs={{0,8},{4,12},{8,0},{12,4},{16,24},{20,28},{24,16},{28,20},{1,9},{5... | collective-permute-start | bytes 786440 | tf_op jit(solution)/shard_map/ppermute | solution.py:1099
  482.0 21.8 %collective-permute-start.71 = (bf16[512,1024]{1,0:T(8,128)(2,1)S(1)}, bf16[512,1024]{1,0:T(8,128)(2,1)S(1)}, u32[]{:S(2)}, u32[]{:S(2)}) collective-permute-start(bf16[512,1024]{1,0:T(8,128)(2,1)S(1)} %maximum_select_fusion.5), channel_id=1, source_target_pairs={{0,4},{4,0},{8,12},{12,8},{16,20},{20,16},{24,28},{28,24},{1,5},{5... | collective-permute-start | bytes 3145736 | tf_op jit(solution)/shard_map/ppermute | solution.py:1099
  482.6 18.6 %collective-permute-start.69 = (bf16[768,256]{1,0:T(8,128)(2,1)S(1)}, bf16[768,256]{1,0:T(8,128)(2,1)S(1)}, u32[]{:S(2)}, u32[]{:S(2)}) collective-permute-start(bf16[768,256]{1,0:T(8,128)(2,1)S(1)} %add_convert_fusion.11), channel_id=1, source_target_pairs={{0,4},{4,0},{8,12},{12,8},{16,20},{20,16},{24,28},{28,24},{1,5},{5... | collective-permute-start | bytes 1179656 | tf_op jit(solution)/shard_map/ppermute | solution.py:1099
  484.3 17.3 %collective-permute-start.68 = (bf16[128,1024]{1,0:T(8,128)(2,1)S(1)}, bf16[128,1024]{1,0:T(8,128)(2,1)S(1)}, u32[]{:S(2)}, u32[]{:S(2)}) collective-permute-start(bf16[128,1024]{1,0:T(8,128)(2,1)S(1)} %add_convert_fusion.15), channel_id=1, source_target_pairs={{0,16},{4,20},{8,24},{12,28},{16,0},{20,4},{24,8},{28,12},{1,17},{... | collective-permute-start | bytes 786440 | tf_op jit(solution)/shard_map/ppermute | solution.py:1099
  484.4 32.0 %collective-permute-start.67 = (f32[8,1024]{1,0:T(8,128)S(1)}, f32[8,1024]{1,0:T(8,128)S(1)}, u32[]{:S(2)}, u32[]{:S(2)}) collective-permute-start(f32[8,1024]{1,0:T(8,128)S(1)} %add.269), channel_id=1, source_target_pairs={{0,4},{4,0},{8,12},{12,8},{16,20},{20,16},{24,28},{28,24},{1,5},{5... | collective-permute-start | bytes 98312 | tf_op jit(solution)/shard_map/ppermute | solution.py:1099
  492.6 24.9 %collective-permute-start.63 = (bf16[64,1024]{1,0:T(8,128)(2,1)S(1)}, bf16[64,1024]{1,0:T(8,128)(2,1)S(1)}, u32[]{:S(2)}, u32[]{:S(2)}) collective-permute-start(bf16[64,1024]{1,0:T(8,128)(2,1)S(1)} %add_convert_fusion.16), channel_id=1, source_target_pairs={{0,2},{2,0},{1,3},{3,1},{4,6},{6,4},{5,7},{7,5},{8,10},{10,8},{9,1... | collective-permute-start | bytes 393224 | tf_op jit(solution)/shard_map/ppermute | solution.py:1096
  501.2 11.8 %collective-permute-start.72 = (bf16[768,256]{1,0:T(8,128)(2,1)S(1)}, bf16[768,256]{1,0:T(8,128)(2,1)S(1)}, u32[]{:S(2)}, u32[]{:S(2)}) collective-permute-start(bf16[768,256]{1,0:T(8,128)(2,1)S(1)} %add_convert_fusion.10), channel_id=1, source_target_pairs={{0,8},{4,12},{8,0},{12,4},{16,24},{20,28},{24,16},{28,20},{1,9},{5... | collective-permute-start | bytes 1179656 | tf_op jit(solution)/shard_map/ppermute | solution.py:1099
  501.6 24.6 %collective-permute-start.74 = (bf16[1536,256]{1,0:T(8,128)(2,1)S(1)}, bf16[1536,256]{1,0:T(8,128)(2,1)S(1)}, u32[]{:S(2)}, u32[]{:S(2)}) collective-permute-start(bf16[1536,256]{1,0:T(8,128)(2,1)S(1)} %maximum_select_fusion.7), channel_id=1, source_target_pairs={{0,8},{4,12},{8,0},{12,4},{16,24},{20,28},{24,16},{28,20},{1,9},{5... | collective-permute-start | bytes 2359304 | tf_op jit(solution)/shard_map/ppermute | solution.py:1099
  503.7 20.6 %collective-permute-start.70 = (bf16[128,1024]{1,0:T(8,128)(2,1)S(1)}, bf16[128,1024]{1,0:T(8,128)(2,1)}, u32[]{:S(2)}, u32[]{:S(2)}) collective-permute-start(bf16[128,1024]{1,0:T(8,128)(2,1)S(1)} %add_convert_fusion.14), channel_id=1, source_target_pairs={{0,8},{4,12},{8,0},{12,4},{16,24},{20,28},{24,16},{28,20},{1,9},{5... | collective-permute-start | bytes 786440 | tf_op jit(solution)/shard_map/ppermute | solution.py:1099
  513.4 17.5 %collective-permute-start.75 = (bf16[1536,256]{1,0:T(8,128)(2,1)S(1)}, bf16[1536,256]{1,0:T(8,128)(2,1)}, u32[]{:S(2)}, u32[]{:S(2)}) collective-permute-start(bf16[1536,256]{1,0:T(8,128)(2,1)S(1)} %maximum_select_fusion.8), channel_id=1, source_target_pairs={{0,4},{4,0},{8,12},{12,8},{16,20},{20,16},{24,28},{28,24},{1,5},{5... | collective-permute-start | bytes 2359304 | tf_op jit(solution)/shard_map/ppermute | solution.py:1099
  525.5 11.2 %collective-permute-start.73 = (bf16[256,1024]{1,0:T(8,128)(2,1)S(1)}, bf16[256,1024]{1,0:T(8,128)(2,1)S(1)}, u32[]{:S(2)}, u32[]{:S(2)}) collective-permute-start(bf16[256,1024]{1,0:T(8,128)(2,1)S(1)} %maximum_select_fusion.9), channel_id=1, source_target_pairs={{0,4},{4,0},{8,12},{12,8},{16,20},{20,16},{24,28},{28,24},{1,5},{5... | collective-permute-start | bytes 1572872 | tf_op jit(solution)/shard_map/ppermute | solution.py:1099
  (141 other events, 1095.5 us)
